TPU v7x, 32 devices: a whole 2x2x4 slice. The times are simulated.
32 devices in a mesh: rep: 2 (over y), sec: 4 (over x, core), tp: 4 (over z).
Axes of the slice: x: 2, y: 2, z: 4, core: 2. Of those that a mesh axis runs over, the one named last changes fastest.
Arguments:
- resid: bfloat16 [96, 5120], P(('rep', 'tp'), 'sec'), parts along dimension 0, may hold values from -6 to 6
- query: bfloat16 [96, 5120], P(('rep', 'tp'), 'sec'), parts along dimension 0, may hold values from -120 to 120
- new_kv: bfloat16 [96, 2048], P(('rep', 'tp'), 'sec'), parts along dimension 0, may hold values from -4 to 4
- key_cache: bfloat16 [96, 224, 1024], P(('rep', 'sec', 'tp')), parts along dimension 0, may hold values from -4 to 4
- cached_value_rows: bfloat16 [96, 224, 1024], P(('rep', 'sec', 'tp')), parts along dimension 0, may hold values from -6 to 6
- cache_len: int32 [96], P(('rep', 'sec', 'tp')), parts along dimension 0, may hold values from 1 to 224, as said below
- assign: int32 [96], P('rep'), parts along dimension 0, may hold values from 0 to 11, as said below
- out_weight: bfloat16 [5120, 5120], P('tp', 'sec'), may hold values from -0.078125 to 0.078125
- norm_gain: bfloat16 [5120], P('sec'), may hold values from 0.099609375 to 1.8984375
- gate_weight: bfloat16 [5120, 16384], P('sec', 'tp'), may hold values from -0.078125 to 0.078125
- up_weight: bfloat16 [5120, 16384], P('sec', 'tp'), may hold values from -0.078125 to 0.078125
- down_weight: bfloat16 [16384, 5120], P('tp', 'sec'), may hold values from -0.046875 to 0.046875
Outputs:
- layer_out: bfloat16 [96, 5120], P(('rep', 'tp'), 'sec'), parts along dimension 0
There are 2 independent parts, one for each index of `rep`. A program takes and returns all parts, laid end to end along the dimension named above; an argument that names none is the same for every part. Nothing has to cross between parts.
Inputs may be any that keep to these rules, and one draw needn't show every extreme that they name: `assign`: each block of 12 consecutive requests names every slot 0 to 11 exactly once. `cache_len`: some cache slot has all 224 positions valid.
All inputs are finite; a program needn't handle non-finite values.
Results may differ from a plain program's by a relative error of at most 0.025.
Values may be sent and summed in bfloat16 or wider, within the bound.
No kernel may reach another device: no remote copies, remote signals or barrier semaphores. Data moves between devices by JAX's collectives and lax.ppermute only.
A program may use at most 64 MiB of HBM per device.

v0:
```python
import math

import jax
import jax.numpy as jnp
from jax import lax
from jax.sharding import PartitionSpec as P

D = 5120
QUERY_HEADS = 40
KEY_VALUE_HEADS = 8
HEAD_WIDTH = 128
CACHE_SLOTS = 224


def attend_slots(query_rows, key_value_pairs, stored_keys, stored_values, lengths):
    cache_slots = query_rows.shape[0]
    group_query = QUERY_HEADS // KEY_VALUE_HEADS
    query_head_rows = query_rows.reshape(cache_slots, KEY_VALUE_HEADS, group_query, HEAD_WIDTH)
    paired_heads = key_value_pairs.reshape(cache_slots, KEY_VALUE_HEADS, 2, HEAD_WIDTH)
    fresh_keys = paired_heads[:, :, 0]
    fresh_values = paired_heads[:, :, 1]
    earlier_keys = stored_keys.reshape(cache_slots, CACHE_SLOTS, KEY_VALUE_HEADS, HEAD_WIDTH)
    earlier_values = stored_values.reshape(cache_slots, CACHE_SLOTS, KEY_VALUE_HEADS, HEAD_WIDTH)
    scaling = 1.0 / math.sqrt(HEAD_WIDTH)
    past_scores = (
        jnp.einsum(
            "rkgd,rlkd->rkgl", query_head_rows, earlier_keys, preferred_element_type=jnp.float32
        )
        * scaling
    )
    fresh_scores = (
        jnp.einsum("rkgd,rkd->rkg", query_head_rows, fresh_keys, preferred_element_type=jnp.float32)
        * scaling
    )
    valid = lax.broadcasted_iota(jnp.int32, (cache_slots, CACHE_SLOTS), 1) < lengths[:, None]
    past_scores = jnp.where(valid[:, None, None, :], past_scores, -1e30)
    highest = jnp.maximum(jnp.max(past_scores, axis=-1), fresh_scores)
    past_exp = jnp.exp(past_scores - highest[..., None])
    fresh_exp = jnp.exp(fresh_scores - highest)
    denominator = jnp.sum(past_exp, axis=-1) + fresh_exp
    past_weights = (past_exp / denominator[..., None]).astype(jnp.bfloat16)
    fresh_weights = (fresh_exp / denominator).astype(jnp.bfloat16)
    mixed = jnp.einsum(
        "rkgl,rlkd->rkgd", past_weights, earlier_values, preferred_element_type=jnp.float32
    )
    mixed = (
        mixed
        + fresh_weights.astype(jnp.float32)[..., None]
        * fresh_values.astype(jnp.float32)[:, :, None, :]
    )
    return mixed.reshape(cache_slots, QUERY_HEADS * HEAD_WIDTH).astype(jnp.bfloat16)


def gated_units(values, width):
    return (jax.nn.silu(values[:, :width]) * values[:, width:]).astype(jnp.bfloat16)


def local(
    resid,
    query,
    new_kv,
    key_cache,
    cached_value_rows,
    cache_len,
    assign,
    out_weight,
    norm_gain,
    gate_weight,
    up_weight,
    down_weight,
):
    group = query.shape[0]
    per_device = key_cache.shape[0]
    tp_index = lax.axis_index("tp")
    sec_index = lax.axis_index("sec")
    tp_count = lax.axis_size("tp")
    local_slots = lax.dynamic_slice_in_dim(assign, tp_index * group, group)
    full_query, full_pairs = (
        lax.all_gather(query, "sec", axis=1, tiled=True),
        lax.all_gather(new_kv, "sec", axis=1, tiled=True),
    )
    wanted = sec_index * per_device + lax.iota(jnp.int32, per_device)
    picker = (local_slots[None, :] == wanted[:, None]).astype(jnp.bfloat16)
    my_query = jnp.dot(picker, full_query, preferred_element_type=jnp.float32).astype(jnp.bfloat16)
    my_pairs = jnp.dot(picker, full_pairs, preferred_element_type=jnp.float32).astype(jnp.bfloat16)
    attended = attend_slots(my_query, my_pairs, key_cache, cached_value_rows, cache_len)
    request_ids = lax.iota(jnp.int32, group * tp_count)
    slot_block = lax.all_gather(attended, "sec", axis=0, tiled=True)
    received = lax.all_to_all(slot_block, "tp", split_axis=1, concat_axis=0, tiled=True)
    position = request_ids // group * group + assign
    ordered = jnp.take(received, position, axis=0)
    block = ordered
    attn_out = lax.psum_scatter(
        jnp.dot(block, out_weight, preferred_element_type=jnp.float32).astype(jnp.bfloat16),
        "tp",
        scatter_dimension=0,
        tiled=True,
    ).astype(jnp.float32)
    stream = resid.astype(jnp.float32) + attn_out
    squares = lax.psum(jnp.sum(stream * stream, axis=1), "sec")
    inverse = lax.rsqrt(squares / D + 1e-06)
    normed = (stream * inverse[:, None] * norm_gain.astype(jnp.float32)[None, :]).astype(
        jnp.bfloat16
    )
    piece = lax.all_gather(normed, "tp", axis=0, tiled=True)
    gate_part = jnp.dot(piece, gate_weight, preferred_element_type=jnp.float32)
    up_part = jnp.dot(piece, up_weight, preferred_element_type=jnp.float32)
    projected = jnp.concatenate([gate_part, up_part], axis=1)
    width = gate_weight.shape[1]
    share = lax.psum_scatter(
        projected.astype(jnp.bfloat16), "sec", scatter_dimension=0, tiled=True
    ).astype(jnp.float32)
    hidden = lax.all_gather(gated_units(share, width), "sec", axis=0, tiled=True)
    block = hidden
    ff_out = lax.psum_scatter(
        jnp.dot(block, down_weight, preferred_element_type=jnp.float32).astype(jnp.bfloat16),
        "tp",
        scatter_dimension=0,
        tiled=True,
    ).astype(jnp.float32)
    return (stream + ff_out).astype(jnp.bfloat16)


def solution(mesh):
    return jax.shard_map(
        local,
        mesh=mesh,
        in_specs=(
            P(("rep", "tp"), "sec"),
            P(("rep", "tp"), "sec"),
            P(("rep", "tp"), "sec"),
            P(("rep", "sec", "tp"), None, None),
            P(("rep", "sec", "tp"), None, None),
            P(("rep", "sec", "tp")),
            P("rep"),
            P("tp", "sec"),
            P("sec"),
            P("sec", "tp"),
            P("sec", "tp"),
            P("tp", "sec"),
        ),
        out_specs=P(("rep", "tp"), "sec"),
        check_vma=False,
    )
```

profile of v0, /device:TPU:0, one launch (start us, length us, event | category | flops | bytes accessed | tf_op | source)
XLA Modules:
  0.0 157.2 jit_solution(10076195548950512645)
XLA Ops:
  0.0 0.0 copy-start
  0.0 0.9 iota_compare_fusion
  0.9 6.5 %all_gather.16 = bf16[12,2048]{1,0:T(8,128)(2,1)S(1)} all-gather(bf16[12,512]{1,0:T(8,128)(2,1)} %param.14), channel_id=1, replica_groups=mesh['rep'=2,'sec'=4,'tp'=4] {'sec'}, dimensions={1}, use_global_device_ids=true | all-gather | bytes 61440 | tf_op jit(solution)/shard_map/all_gather | solution.py:80
  7.4 0.7 dynamic_slice.3
  8.2 0.2 convolution_convert_fusion.5
  8.4 6.0 %all_gather.15 = bf16[12,5120]{1,0:T(8,128)(2,1)S(1)} all-gather(bf16[12,1280]{1,0:T(8,128)(2,1)} %param.13), channel_id=1, replica_groups=mesh['rep'=2,'sec'=4,'tp'=4] {'sec'}, dimensions={1}, use_global_device_ids=true | all-gather | bytes 153600 | tf_op jit(solution)/shard_map/all_gather | solution.py:79
  14.4 0.2 convolution_convert_fusion
  14.6 0.1 reshape.47
  14.7 0.0 copy-start.7
  14.7 0.1 fusion.30
  14.8 2.3 %fusion.43 = (f32[3,8,5]{2,1,0:T(8,128)S(1)}, f32[3,8,5,224]{3,2,1,0:T(8,128)S(1)}) fusion(bf16[3,8,5,128]{3,2,1,0:T(8,128)(2,1)S(1)} %reshape.47, pred[3,224]{1,0:T(4,128)(4,1)S(1)} %iota_compare_fusion, bf16[3,224,1024]{2,1,0:T(8,128)(2,1)} %param.15), kind=kOutput, calls=%fused_computation.63 | convolution fusion | flops 6961800 | bytes 1515648 | tf_op jit(solution)/shard_map/rkgd,rlkd->rkgl/dot_general | solution.py:26
  17.2 0.2 fusion.22
  17.4 0.0 copy-done.7
  17.4 0.0 copy-start.8
  17.4 0.5 fusion.18
  18.0 5.5 %all-gather = bf16[4,3,5120]{2,1,0:T(4,128)(2,1)S(1)} all-gather(bf16[1,3,5120]{2,1,0:T(4,128)(2,1)S(1)} %reshape.61), channel_id=1, replica_groups=mesh['rep'=2,'sec'=4,'tp'=4] {'sec'}, dimensions={0}, use_global_device_ids=true | all-gather | bytes 153600 | tf_op jit(solution)/shard_map/all_gather | solution.py:88
  23.5 0.8 all_to_all.14
  24.3 1.6 copy.23
  25.8 5.1 %all-to-all-start = ((bf16[12,4,1280]{2,0,1:T(8,128)(2,1)}), bf16[12,4,1280]{2,0,1:T(8,128)(2,1)S(1)}, u32[]{:S(2)}, u32[]{:S(2)}) async-start(bf16[12,4,1280]{2,0,1:T(8,128)(2,1)} %copy.23), calls=%async_computation | async-start | bytes 327680 | tf_op jit(solution)/shard_map/all_to_all | solution.py:89
  30.9 0.0 copy-done.8
  31.0 6.8 %all-to-all-done = bf16[12,4,1280]{2,0,1:T(8,128)(2,1)S(1)} async-done(((bf16[12,4,1280]{2,0,1:T(8,128)(2,1)}), bf16[12,4,1280]{2,0,1:T(8,128)(2,1)S(1)}, u32[]{:S(2)}, u32[]{:S(2)}) %all-to-all-start) | async-done | bytes 122912 | tf_op jit(solution)/shard_map/all_to_all | solution.py:89
  37.8 0.7 copy-done.1
  38.4 0.9 all_to_all.17
  39.4 0.7 gather_fusion
  40.1 0.0 copy-done
  40.1 0.0 copy-start.6
  40.1 0.0 copy-start.4
  40.1 0.7 convolution_convert_fusion.4
  40.8 13.9 %fusion = bf16[16,1280]{1,0:T(8,128)(2,1)S(1)} fusion(bf16[48,1280]{1,0:T(8,128)(2,1)S(1)} %convolution_convert_fusion.4), kind=kCustom, calls=%all-reduce-scatter | all-reduce-scatter fusion | flops 81921 | bytes 164352
  54.7 1.4 collective-permute-start
  56.2 0.0 copy-done.6
  56.2 0.6 dynamic-slice.8
  57.4 0.4 collective-permute-done
  57.8 0.2 concatenate.5
  58.0 0.0 copy-start.2
  58.0 0.9 multiply_reduce_fusion
  59.0 0.0 copy-done.4
  59.0 5.7 %psum.7 = f32[12]{0:T(128)S(1)} all-reduce(f32[12]{0:T(128)S(1)} %multiply_reduce_fusion), channel_id=1, replica_groups=mesh['rep'=2,'sec'=4,'tp'=4] {'sec'}, use_global_device_ids=true, to_apply=%region_4.5 | all-reduce | flops 12 | bytes 96 | tf_op jit(solution)/shard_map/psum | solution.py:100
  64.7 0.9 fusion.29
  65.5 0.0 copy-done.2
  65.5 14.3 %all-gather.1 = bf16[4,12,1280]{2,1,0:T(8,128)(2,1)} all-gather(bf16[1,12,1280]{2,1,0:T(8,128)(2,1)S(1)} %fusion.29), channel_id=1, replica_groups=mesh['rep'=2,'sec'=4,'tp'=4] {'tp'}, dimensions={0}, use_global_device_ids=true | all-gather | bytes 153600 | tf_op jit(solution)/shard_map/all_gather | solution.py:105
  79.8 0.9 reshape.64
  80.8 5.9 %convolution_convert_fusion.1 = bf16[48,4096]{1,0:T(8,128)(2,1)S(1)} fusion(bf16[48,1280]{1,0:T(8,128)(2,1)S(1)} %reshape.64, bf16[1280,4096]{1,0:T(8,128)(2,1)} %param.22), kind=kOutput, calls=%fused_computation.2 | convolution fusion | flops 503513088 | bytes 11001856 | tf_op jit(solution)/shard_map/dot_general | solution.py:107
  86.7 5.9 %convolution_convert_fusion.2 = bf16[48,4096]{1,0:T(8,128)(2,1)S(1)} fusion(bf16[48,1280]{1,0:T(8,128)(2,1)S(1)} %reshape.64, bf16[1280,4096]{1,0:T(8,128)(2,1)} %param.21), kind=kOutput, calls=%fused_computation.3 | convolution fusion | flops 503513088 | bytes 11001856 | tf_op jit(solution)/shard_map/dot_general | solution.py:106
  92.6 0.0 copy-start.5
  92.6 0.9 pad_maximum_fusion
  93.6 15.0 %fusion.1 = bf16[16,8192]{1,0:T(8,128)(2,1)S(1)} fusion(bf16[48,8192]{1,0:T(8,128)(2,1)} %pad_maximum_fusion), kind=kCustom, calls=%all-reduce-scatter.1 | all-reduce-scatter fusion | flops 524289 | bytes 1049088
  108.6 0.8 slice.23
  109.3 2.0 %collective-permute-start.1 = (bf16[12,8192]{1,0:T(8,128)(2,1)}, bf16[12,8192]{1,0:T(8,128)(2,1)}, u32[]{:S(2)}, u32[]{:S(2)}) collective-permute-start(bf16[12,8192]{1,0:T(8,128)(2,1)} %slice.23), channel_id=1, source_target_pairs={{0,4},{4,8},{8,12},{1,5},{5,9},{9,13},{2,6},{6,10},{10,14},{3,7},{... | collective-permute-start | bytes 589832
  111.3 0.0 copy-done.5
  111.3 0.6 dynamic-slice.12
  112.6 0.0 collective-permute-done.1
  112.6 5.6 %concatenate.6 = bf16[28,8192]{1,0:T(8,128)(2,1)} concatenate(bf16[12,8192]{1,0:T(8,128)(2,1)} %collective-permute-done.1, bf16[16,8192]{1,0:T(8,128)(2,1)S(1)} %fusion.1), dimensions={0} | concatenate | bytes 917504
  118.2 1.1 dynamic-slice_convert_fusion
  119.3 0.1 fusion.23
  119.4 11.4 %all-gather.2 = bf16[4,12,4096]{2,1,0:T(8,128)(2,1)} all-gather(bf16[1,12,4096]{2,1,0:T(8,128)(2,1)S(1)} %fusion.23), channel_id=1, replica_groups=mesh['rep'=2,'sec'=4,'tp'=4] {'sec'}, dimensions={0}, use_global_device_ids=true | all-gather | bytes 491520 | tf_op jit(solution)/shard_map/all_gather | solution.py:113
  130.7 1.9 %reshape.66 = bf16[48,4096]{1,0:T(8,128)(2,1)} reshape(bf16[4,12,4096]{2,1,0:T(8,128)(2,1)} %all-gather.2) | data formatting | bytes 786432
  132.6 6.0 %convolution_convert_fusion.3 = bf16[48,1280]{1,0:T(8,128)(2,1)S(1)} fusion(bf16[48,4096]{1,0:T(8,128)(2,1)} %reshape.66, bf16[4096,1280]{1,0:T(8,128)(2,1)} %param.23), kind=kOutput, calls=%fused_computation.4 | convolution fusion | flops 503377920 | bytes 11001856 | tf_op jit(solution)/shard_map/dot_general | solution.py:116
  138.7 13.6 %fusion.2 = bf16[16,1280]{1,0:T(8,128)(2,1)S(1)} fusion(bf16[48,1280]{1,0:T(8,128)(2,1)S(1)} %convolution_convert_fusion.3), kind=kCustom, calls=%all-reduce-scatter.2 | all-reduce-scatter fusion | flops 81921 | bytes 164352
  152.3 1.7 %collective-permute-start.2 = (bf16[12,1280]{1,0:T(8,128)(2,1)S(1)}, bf16[12,1280]{1,0:T(8,128)(2,1)S(1)}, u32[]{:S(2)}, u32[]{:S(2)}) collective-permute-start(bf16[12,1280]{1,0:T(8,128)(2,1)S(1)} %slice.24), channel_id=1, source_target_pairs={{0,1},{1,2},{2,3},{4,5},{5,6},{6,7},{8,9},{9,10},{10,11},{12,13},{... | collective-permute-start | bytes 92168
  154.0 1.7 %collective-permute-done.2 = bf16[12,1280]{1,0:T(8,128)(2,1)S(1)} collective-permute-done((bf16[12,1280]{1,0:T(8,128)(2,1)S(1)}, bf16[12,1280]{1,0:T(8,128)(2,1)S(1)}, u32[]{:S(2)}, u32[]{:S(2)}) %collective-permute-start.2) | collective-permute-done | bytes 30752
  155.6 0.2 concatenate.7
  155.8 0.0 copy-done.3
  155.8 1.4 add_convert_fusion
  (15 shorter events, 0.2 us)
Async XLA Ops:
  0.0 40.1 %copy-start = (bf16[1280,1280]{1,0:T(8,128)(2,1)S(1)}, bf16[1280,1280]{1,0:T(8,128)(2,1)}, u32[]{:S(2)}) copy-start(bf16[1280,1280]{1,0:T(8,128)(2,1)} %param.19) | copy-start | bytes 9830404
  14.7 2.7 %copy-start.7 = (bf16[3,224,1024]{2,1,0:T(8,128)(2,1)S(1)}, bf16[3,224,1024]{2,1,0:T(8,128)(2,1)}, u32[]{:S(2)}) copy-start(bf16[3,224,1024]{2,1,0:T(8,128)(2,1)} %param.16) | copy-start | bytes 4128772
  17.4 13.5 %copy-start.8 = (s32[48]{0:T(128)S(1)}, s32[48]{0:T(128)}, u32[]{:S(2)}) copy-start(s32[48]{0:T(128)} %param.18) | copy-start | bytes 580
  25.8 11.9 %all-to-all-start = ((bf16[12,4,1280]{2,0,1:T(8,128)(2,1)}), bf16[12,4,1280]{2,0,1:T(8,128)(2,1)S(1)}, u32[]{:S(2)}, u32[]{:S(2)}) async-start(bf16[12,4,1280]{2,0,1:T(8,128)(2,1)} %copy.23), calls=%async_computation | async-start | bytes 327680 | tf_op jit(solution)/shard_map/all_to_all | solution.py:89
  37.8 0.7 copy-start.1
  40.1 16.1 %copy-start.6 = (u32[32]{0:T(128)S(1)}, u32[32]{0:T(128)}, u32[]{:S(2)}) copy-start(u32[32]{0:T(128)} %constant.63) | copy-start | bytes 388
  40.1 18.9 %copy-start.4 = (bf16[1280]{0:T(1024)(128)(2,1)S(1)}, bf16[1280]{0:T(1024)(128)(2,1)}, u32[]{:S(2)}) copy-start(bf16[1280]{0:T(1024)(128)(2,1)} %param.20) | copy-start | bytes 7684
  54.7 3.1 %collective-permute-start = (bf16[12,1280]{1,0:T(8,128)(2,1)S(1)}, bf16[12,1280]{1,0:T(8,128)(2,1)S(1)}, u32[]{:S(2)}, u32[]{:S(2)}) collective-permute-start(bf16[12,1280]{1,0:T(8,128)(2,1)S(1)} %slice.22), channel_id=1, source_target_pairs={{0,1},{1,2},{2,3},{4,5},{5,6},{6,7},{8,9},{9,10},{10,11},{12,13},{... | collective-permute-start | bytes 92168
  58.0 7.5 %copy-start.2 = (bf16[28,1280]{1,0:T(8,128)(2,1)}, bf16[28,1280]{1,0:T(8,128)(2,1)S(1)}, u32[]{:S(2)}) copy-start(bf16[28,1280]{1,0:T(8,128)(2,1)S(1)} %concatenate.5) | copy-start | bytes 215044
  92.6 18.7 %copy-start.5 = (u32[32]{0:T(128)S(1)}, u32[32]{0:T(128)}, u32[]{:S(2)}) copy-start(u32[32]{0:T(128)} %constant.67) | copy-start | bytes 388
  109.3 3.2 %collective-permute-start.1 = (bf16[12,8192]{1,0:T(8,128)(2,1)}, bf16[12,8192]{1,0:T(8,128)(2,1)}, u32[]{:S(2)}, u32[]{:S(2)}) collective-permute-start(bf16[12,8192]{1,0:T(8,128)(2,1)} %slice.23), channel_id=1, source_target_pairs={{0,4},{4,8},{8,12},{1,5},{5,9},{9,13},{2,6},{6,10},{10,14},{3,7},{... | collective-permute-start | bytes 589832
  132.6 23.2 %copy-start.3 = (bf16[28,1280]{1,0:T(8,128)(2,1)S(1)}, bf16[28,1280]{1,0:T(8,128)(2,1)}, u32[]{:S(2)}) copy-start(bf16[28,1280]{1,0:T(8,128)(2,1)} %copy-done.2) | copy-start | bytes 215044
  152.3 3.4 %collective-permute-start.2 = (bf16[12,1280]{1,0:T(8,128)(2,1)S(1)}, bf16[12,1280]{1,0:T(8,128)(2,1)S(1)}, u32[]{:S(2)}, u32[]{:S(2)}) collective-permute-start(bf16[12,1280]{1,0:T(8,128)(2,1)S(1)} %slice.24), channel_id=1, source_target_pairs={{0,1},{1,2},{2,3},{4,5},{5,6},{6,7},{8,9},{9,10},{10,11},{12,13},{... | collective-permute-start | bytes 92168
where the time goes:
time: 158 us; the launch traced here: 157 us
  blocking collectives  91.8 us (58%)
  matrix products  22 us (14%)
  local copies, waits for them, and re-layouts  16.3 us (10%)
  starting transfers between devices  10.2 us (6%)
  waiting for transfers between devices  8.89 us (6%)
  other arithmetic  6.47 us (4%)
  between operations  1.6 us (1%)
    unnamed x3, blocking collectives  42.4 us
    all_gather x1, blocking collectives, local(): piece = lax.all_gather(normed, 'tp', axis=0, tiled=True)  14.3 us
    unnamed x30, local copies, waits for them, and re-layouts  11.5 us
    all_gather x1, blocking collectives, local(): lax.all_gather(gated_units(share, width), 'sec', axis=0, tiled=True)  11.4 us
    all_to_all x1, waiting for transfers between devices, local(): lax.all_to_all(slot_block, 'tp', split_axis=1, concat_axis=0, tiled=True)  6.83 us
    all_gather x1, blocking collectives, local(): lax.all_gather(new_kv, 'sec', axis=1, tiled=True)  6.55 us
    dot_general x1, matrix products, local(): jnp.dot(block, down_weight, preferred_element_type=jnp.float32)  6.02 us
    all_gather x1, blocking collectives, local(): lax.all_gather(query, 'sec', axis=1, tiled=True)  5.98 us
  transfers between devices with their start and end apart: 4, of which 3 were waited for; matrix products, arithmetic and copies ran while one was open for 1% of the time, Pallas kernels for 0%

commit v1 on v0

--- a/solution.py
+++ b/solution.py
@@ -55,6 +55,14 @@
     return (jax.nn.silu(values[:, :width]) * values[:, width:]).astype(jnp.bfloat16)
 
 
+def received(blocks, axis):
+    count = lax.axis_size(axis)
+    result = [blocks[0]]
+    for step in range(1, count):
+        result.append(lax.ppermute(blocks[step], axis, [(i, i ^ step) for i in range(count)]))
+    return result
+
+
 def local(
     resid,
     query,
@@ -74,50 +82,62 @@
     tp_index = lax.axis_index("tp")
     sec_index = lax.axis_index("sec")
     tp_count = lax.axis_size("tp")
+    sec_count = lax.axis_size("sec")
     local_slots = lax.dynamic_slice_in_dim(assign, tp_index * group, group)
-    full_query, full_pairs = (
-        lax.all_gather(query, "sec", axis=1, tiled=True),
-        lax.all_gather(new_kv, "sec", axis=1, tiled=True),
-    )
-    wanted = sec_index * per_device + lax.iota(jnp.int32, per_device)
-    picker = (local_slots[None, :] == wanted[:, None]).astype(jnp.bfloat16)
-    my_query = jnp.dot(picker, full_query, preferred_element_type=jnp.float32).astype(jnp.bfloat16)
-    my_pairs = jnp.dot(picker, full_pairs, preferred_element_type=jnp.float32).astype(jnp.bfloat16)
+    resid_f32 = resid.astype(jnp.float32)
+    features = resid.shape[1]
+    width = gate_weight.shape[1]
+    rows = group * tp_count // sec_count
+
+    tokens = jnp.concatenate([query, new_kv], axis=1)
+    blocks = []
+    for step in range(sec_count):
+        wanted = (sec_index ^ step) * per_device + lax.iota(jnp.int32, per_device)
+        picker = (local_slots[None, :] == wanted[:, None]).astype(jnp.bfloat16)
+        blocks.append(jnp.dot(picker, tokens, preferred_element_type=jnp.float32).astype(jnp.bfloat16))
+    pieces = jnp.stack(received(blocks, "sec"))
+    pieces = jnp.take(pieces, sec_index ^ lax.iota(jnp.int32, sec_count), axis=0)
+    my_query = pieces[:, :, : query.shape[1]].transpose(1, 0, 2).reshape(per_device, -1)
+    my_pairs = pieces[:, :, query.shape[1] :].transpose(1, 0, 2).reshape(per_device, -1)
     attended = attend_slots(my_query, my_pairs, key_cache, cached_value_rows, cache_len)
-    request_ids = lax.iota(jnp.int32, group * tp_count)
-    slot_block = lax.all_gather(attended, "sec", axis=0, tiled=True)
-    received = lax.all_to_all(slot_block, "tp", split_axis=1, concat_axis=0, tiled=True)
-    position = request_ids // group * group + assign
-    ordered = jnp.take(received, position, axis=0)
-    block = ordered
-    attn_out = lax.psum_scatter(
-        jnp.dot(block, out_weight, preferred_element_type=jnp.float32).astype(jnp.bfloat16),
-        "tp",
-        scatter_dimension=0,
-        tiled=True,
-    ).astype(jnp.float32)
-    stream = resid.astype(jnp.float32) + attn_out
-    squares = lax.psum(jnp.sum(stream * stream, axis=1), "sec")
-    inverse = lax.rsqrt(squares / D + 1e-06)
-    normed = (stream * inverse[:, None] * norm_gain.astype(jnp.float32)[None, :]).astype(
-        jnp.bfloat16
-    )
-    piece = lax.all_gather(normed, "tp", axis=0, tiled=True)
+
+    head_block = out_weight.shape[0]
+    blocks = [
+        lax.dynamic_slice_in_dim(attended, (tp_index ^ step) * head_block, head_block, 1)
+        for step in range(tp_count)
+    ]
+    mine = jnp.stack(received(blocks, "tp"))
+    everyone = jnp.stack(received([mine] * sec_count, "sec"))
+    everyone = jnp.take(everyone, sec_index ^ lax.iota(jnp.int32, sec_count), axis=0)
+    everyone = everyone.transpose(1, 0, 2, 3).reshape(tp_count, group, head_block)
+    parts = jnp.dot(everyone.reshape(tp_count * group, head_block), out_weight, preferred_element_type=jnp.float32)
+    parts = parts.astype(jnp.bfloat16).reshape(tp_count, group, features)
+    shares = received([parts[step] for step in range(tp_count)], "tp")
+    attn_out = sum(share.astype(jnp.float32) for share in shares)
+    attn_out = jnp.take(attn_out, local_slots, axis=0)
+    stream = resid_f32 + attn_out
+
+    scaled = (stream * norm_gain.astype(jnp.float32)[None, :]).astype(jnp.bfloat16)
+    squares = jnp.broadcast_to(jnp.sum(stream * stream, axis=1, keepdims=True), (group, 128))
+    piece = jnp.concatenate(received([scaled] * tp_count, "tp"), axis=0)
+    square_parts = jnp.concatenate(received([squares] * tp_count, "tp"), axis=0)
+    square_parts = square_parts.reshape(sec_count, rows, 128)
     gate_part = jnp.dot(piece, gate_weight, preferred_element_type=jnp.float32)
     up_part = jnp.dot(piece, up_weight, preferred_element_type=jnp.float32)
-    projected = jnp.concatenate([gate_part, up_part], axis=1)
-    width = gate_weight.shape[1]
-    share = lax.psum_scatter(
-        projected.astype(jnp.bfloat16), "sec", scatter_dimension=0, tiled=True
-    ).astype(jnp.float32)
-    hidden = lax.all_gather(gated_units(share, width), "sec", axis=0, tiled=True)
-    block = hidden
-    ff_out = lax.psum_scatter(
-        jnp.dot(block, down_weight, preferred_element_type=jnp.float32).astype(jnp.bfloat16),
-        "tp",
-        scatter_dimension=0,
-        tiled=True,
-    ).astype(jnp.float32)
+    projected = jnp.concatenate([gate_part, up_part], axis=1).astype(jnp.bfloat16)
+    projected = projected.reshape(sec_count, rows, 2 * width)
+    blocks = [lax.dynamic_index_in_dim(projected, sec_index ^ step, 0, False) for step in range(sec_count)]
+    share = sum(block.astype(jnp.float32) for block in received(blocks, "sec"))
+    blocks = [lax.dynamic_index_in_dim(square_parts, sec_index ^ step, 0, False) for step in range(sec_count)]
+    total = sum(received(blocks, "sec"))
+    inverse = lax.rsqrt(total[:, :1] / D + 1e-06)
+    hidden = gated_units(share * inverse, width)
+    hidden = jnp.stack(received([hidden] * sec_count, "sec"))
+    hidden = jnp.take(hidden, sec_index ^ lax.iota(jnp.int32, sec_count), axis=0).reshape(-1, width)
+    parts = jnp.dot(hidden, down_weight, preferred_element_type=jnp.float32).astype(jnp.bfloat16)
+    parts = parts.reshape(tp_count, group, features)
+    shares = received([parts[step] for step in range(tp_count)], "tp")
+    ff_out = sum(share.astype(jnp.float32) for share in shares)
     return (stream + ff_out).astype(jnp.bfloat16)
 
 

time: 158 us -> 121 us (0.77)
  blocking collectives: 91.8 us -> 0 us
  waiting for transfers between devices: 8.89 us -> 36.1 us
  starting transfers between devices: 10.2 us -> 32.3 us
  matrix products: 22 us -> 26 us
  local copies, waits for them, and re-layouts: 16.3 us -> 18.4 us
    all_gather x5 -> x0, blocking collectives: 43.7 us -> none  [the longest x1 14.3 us: local(): piece = lax.all_gather(normed, 'tp', axis=0, tiled=True)]
    unnamed x3 -> x0, blocking collectives: 42.4 us -> none
    ppermute x0 -> x30, waiting for transfers between devices: none -> 36.1 us  [received(): lax.ppermute(blocks[step], axis, [(i, i ^ step) for i in range(count)])]
    ppermute x0 -> x30, starting transfers between devices: none -> 32.3 us  [received(): lax.ppermute(blocks[step], axis, [(i, i ^ step) for i in range(count)])]
    unnamed x30 -> x22, local copies, waits for them, and re-layouts: 11.5 us -> 3.01 us
    all_to_all x1 -> x0, waiting for transfers between devices: 6.83 us -> none  [local(): lax.all_to_all(slot_block, 'tp', split_axis=1, concat_axis=0, tiled=True)]
    gather x1 -> x5, local copies, waits for them, and re-layouts: 0.68 us -> 6.96 us  [the longest x2 4.43 us: local(): jnp.take(hidden, sec_index ^ lax.iota(jnp.int32, sec_count), axis=0)]
    psum x1 -> x0, blocking collectives: 5.67 us -> none  [local(): squares = lax.psum(jnp.sum(stream * stream, axis=1), 'sec')]
  transfers between devices with their start and end apart: 4 -> 30, of which waited for: 3 -> 16; matrix products, arithmetic and copies ran while one was open for 1% -> 3% of each run, Pallas kernels for 0% -> 0%
where the time goes in v1:
time: 121 us
  waiting for transfers between devices  36.1 us (30%)
  starting transfers between devices  32.3 us (27%)
  matrix products  26 us (21%)
  local copies, waits for them, and re-layouts  18.4 us (15%)
  other arithmetic  7.29 us (6%)
    ppermute x30, waiting for transfers between devices, received(): lax.ppermute(blocks[step], axis, [(i, i ^ step) for i in range(count)])  36.1 us
    ppermute x30, starting transfers between devices, received(): lax.ppermute(blocks[step], axis, [(i, i ^ step) for i in range(count)])  32.3 us
    dot_general x1, matrix products, local(): up_part = jnp.dot(piece, up_weight, preferred_element_type=jnp.float32)  6.68 us
    dot_general x1, matrix products, local(): gate_part = jnp.dot(piece, gate_weight, preferred_element_type=jnp.float32)  6.66 us
    dot_general x1, matrix products, local(): jnp.dot(hidden, down_weight, preferred_element_type=jnp.float32)  6.11 us
    concatenate x3, local copies, waits for them, and re-layouts, local(): jnp.concatenate([gate_part, up_part], axis=1).astype(jnp.bfloat16)  4.85 us
    gather x2, local copies, waits for them, and re-layouts, local(): jnp.take(hidden, sec_index ^ lax.iota(jnp.int32, sec_count), axis=0)  4.43 us
    unnamed x22, local copies, waits for them, and re-layouts  3.01 us
  transfers between devices with their start and end apart: 30, of which 16 were waited for; matrix products, arithmetic and copies ran while one was open for 3% of the time, Pallas kernels for 0%

profile of v1, /device:TPU:0, one launch (start us, length us, event | category | flops | bytes accessed | tf_op | source)
XLA Modules:
  0.0 120.5 jit_solution(15713749985708890675)
XLA Ops:
  0.0 0.9 constant_dynamic-update-slice_fusion.1
  0.9 0.8 compare_and_fusion.1
  1.7 0.7 constant_dynamic-update-slice_fusion
  2.7 0.5 collective-permute-start
  3.3 2.5 %collective-permute-start.1 = (bf16[3,1792]{1,0:T(4,128)(2,1)S(1)}, bf16[3,1792]{1,0:T(4,128)(2,1)S(1)}, u32[]{:S(2)}, u32[]{:S(2)}) collective-permute-start(bf16[3,1792]{1,0:T(4,128)(2,1)S(1)} %convolution_convert_fusion.5), channel_id=1, source_target_pairs={{0,8},{4,12},{8,0},{12,4},{1,9},{5,13},{9,1},{13,5},{2,10},{6,14},... | collective-permute-start | bytes 32264 | tf_op jit(solution)/shard_map/ppermute | solution.py:62
  6.2 0.7 iota_compare_fusion
  7.2 0.4 collective-permute-done.1
  7.6 1.7 %collective-permute-done.2 = bf16[3,1792]{1,0:T(4,128)(2,1)S(1)} collective-permute-done((bf16[3,1792]{1,0:T(4,128)(2,1)S(1)}, bf16[3,1792]{1,0:T(4,128)(2,1)S(1)}, u32[]{:S(2)}, u32[]{:S(2)}) %collective-permute-start.2) | collective-permute-done | bytes 10784 | tf_op jit(solution)/shard_map/ppermute | solution.py:62
  9.3 0.6 gather_fusion
  10.3 2.3 %fusion.54 = (f32[3,8,5]{2,1,0:T(8,128)S(1)}, f32[3,8,5,224]{3,2,1,0:T(8,128)S(1)}) fusion(bf16[3,8,5,128]{3,2,1,0:T(8,128)(2,1)S(1)} %reshape_reshape.9, pred[3,224]{1,0:T(4,128)(4,1)S(1)} %iota_compare_fusion, bf16[3,224,1024]{2,1,0:T(8,128)(2,1)} %param.15), kind=kOutput, calls=%fused_computation.112 | convolution fusion | flops 6961800 | bytes 1515648 | tf_op jit(solution)/shard_map/rkgd,rlkd->rkgl/dot_general | solution.py:26
  12.8 1.9 %fusion.16 = bf16[3,8,5,128]{3,2,1,0:T(8,128)(2,1)S(1)} fusion(f32[3,8,5,224]{3,2,1,0:T(8,128)S(1)} %get-tuple-element.29, f32[3,8,5]{2,1,0:T(8,128)S(1)} %get-tuple-element.23, f32[3,8,5]{2,1,0:T(8,128)S(1)} %multiply_maximum_fusion, f32[3,8,128]{2,1,0:T(8,128)S(1)} %bitcast.103, f32[3,8,5]{2,1,0:T(8,128)S(1)} %get-tuple-element.22, ...), kind=kOutput, calls=%fused_computation.22 | convolution fusion | flops 7008000 | bytes 1528224 | tf_op jit(solution)/shard_map/rkgl,rlkd->rkgd/dot_general | solution.py:43
  14.7 3.7 %collective-permute-start.5 = (bf16[3,1280]{1,0:T(4,128)(2,1)S(1)}, bf16[3,1280]{1,0:T(4,128)(2,1)S(1)}, u32[]{:S(2)}, u32[]{:S(2)}) collective-permute-start(bf16[3,1280]{1,0:T(4,128)(2,1)S(1)} %get-tuple-element.19), channel_id=1, source_target_pairs={{0,3},{1,2},{2,1},{3,0},{4,7},{5,6},{6,5},{7,4},{8,11},{9,10},{10,... | collective-permute-start | bytes 23048 | tf_op jit(solution)/shard_map/ppermute | solution.py:62
  18.4 0.8 collective-permute-start.3
  19.2 1.1 collective-permute-done.5
  20.3 2.7 %collective-permute-done.4 = bf16[3,1280]{1,0:T(4,128)(2,1)S(1)} collective-permute-done((bf16[3,1280]{1,0:T(4,128)(2,1)S(1)}, bf16[3,1280]{1,0:T(4,128)(2,1)S(1)}, u32[]{:S(2)}, u32[]{:S(2)}) %collective-permute-start.4) | collective-permute-done | bytes 7712 | tf_op jit(solution)/shard_map/ppermute | solution.py:62
  23.0 0.6 collective-permute-start.7
  23.6 1.6 %collective-permute-start.8 = (bf16[4,3,1280]{2,1,0:T(4,128)(2,1)S(1)}, bf16[4,3,1280]{2,1,0:T(4,128)(2,1)S(1)}, u32[]{:S(2)}, u32[]{:S(2)}) collective-permute-start(bf16[4,3,1280]{2,1,0:T(4,128)(2,1)S(1)} %pad_maximum_fusion.4), channel_id=1, source_target_pairs={{0,12},{4,8},{8,4},{12,0},{1,13},{5,9},{9,5},{13,1},{2,14},{6,10},... | collective-permute-start | bytes 92168 | tf_op jit(solution)/shard_map/ppermute | solution.py:62
  25.3 2.2 %collective-permute-done.7 = bf16[4,3,1280]{2,1,0:T(4,128)(2,1)S(1)} collective-permute-done((bf16[4,3,1280]{2,1,0:T(4,128)(2,1)S(1)}, bf16[4,3,1280]{2,1,0:T(4,128)(2,1)S(1)}, u32[]{:S(2)}, u32[]{:S(2)}) %collective-permute-start.7) | collective-permute-done | bytes 30752 | tf_op jit(solution)/shard_map/ppermute | solution.py:62
  27.7 1.3 %gather_fusion.1 = bf16[4,4,3,1280]{3,2,1,0:T(4,128)(2,1)} fusion(bf16[4,4,3,1280]{3,2,1,0:T(4,128)(2,1)S(1)} %pad_maximum_fusion.1, s32[1024]{0:T(1024)S(1)} %pad_clamp_fusion.1), kind=kCustom, calls=%fused_computation.1 | custom fusion | bytes 245776 | tf_op jit(solution)/shard_map/jit(_take)/gather | solution.py:111
  29.0 1.1 select_bitcast_fusion
  30.1 0.8 reshape_reshape.11
  30.9 1.6 %convolution_convert_fusion.3 = bf16[48,1280]{1,0:T(8,128)(2,1)S(1)} fusion(bf16[48,1280]{1,0:T(8,128)(2,1)} %reshape_reshape.11, bf16[1280,1280]{1,0:T(8,128)(2,1)S(1)} %copy-done), kind=kOutput, calls=%fused_computation.7 | convolution fusion | flops 157347840 | bytes 3522560 | tf_op jit(solution)/shard_map/dot_general | solution.py:113
  32.6 3.5 %collective-permute-start.11 = (bf16[12,1280]{1,0:T(8,128)(2,1)S(1)}, bf16[12,1280]{1,0:T(8,128)(2,1)S(1)}, u32[]{:S(2)}, u32[]{:S(2)}) collective-permute-start(bf16[12,1280]{1,0:T(8,128)(2,1)S(1)} %get-tuple-element.16), channel_id=1, source_target_pairs={{0,3},{1,2},{2,1},{3,0},{4,7},{5,6},{6,5},{7,4},{8,11},{9,10},{10,... | collective-permute-start | bytes 92168 | tf_op jit(solution)/shard_map/ppermute | solution.py:62
  36.1 0.5 collective-permute-done.9
  36.6 2.5 %collective-permute-done.11 = bf16[12,1280]{1,0:T(8,128)(2,1)S(1)} collective-permute-done((bf16[12,1280]{1,0:T(8,128)(2,1)S(1)}, bf16[12,1280]{1,0:T(8,128)(2,1)S(1)}, u32[]{:S(2)}, u32[]{:S(2)}) %collective-permute-start.11) | collective-permute-done | bytes 30752 | tf_op jit(solution)/shard_map/ppermute | solution.py:62
  39.1 1.9 %collective-permute-done.10 = bf16[12,1280]{1,0:T(8,128)(2,1)S(1)} collective-permute-done((bf16[12,1280]{1,0:T(8,128)(2,1)S(1)}, bf16[12,1280]{1,0:T(8,128)(2,1)S(1)}, u32[]{:S(2)}, u32[]{:S(2)}) %collective-permute-start.10) | collective-permute-done | bytes 30752 | tf_op jit(solution)/shard_map/ppermute | solution.py:62
  41.0 0.6 gather_fusion.2
  41.9 1.7 %collective-permute-start.20 = (f32[12,128]{1,0:T(8,128)S(1)}, f32[12,128]{1,0:T(8,128)S(1)}, u32[]{:S(2)}, u32[]{:S(2)}) collective-permute-start(f32[12,128]{1,0:T(8,128)S(1)} %broadcast_in_dim.91), channel_id=1, source_target_pairs={{0,3},{1,2},{2,1},{3,0},{4,7},{5,6},{6,5},{7,4},{8,11},{9,10},{10,... | collective-permute-start | bytes 18440 | tf_op jit(solution)/shard_map/ppermute | solution.py:62
  43.5 2.7 %collective-permute-start.18 = (f32[12,128]{1,0:T(8,128)S(1)}, f32[12,128]{1,0:T(8,128)S(1)}, u32[]{:S(2)}, u32[]{:S(2)}) collective-permute-start(f32[12,128]{1,0:T(8,128)S(1)} %broadcast_in_dim.91), channel_id=1, source_target_pairs={{0,1},{1,0},{2,3},{3,2},{4,5},{5,4},{6,7},{7,6},{8,9},{9,8},{10,11... | collective-permute-start | bytes 18440 | tf_op jit(solution)/shard_map/ppermute | solution.py:62
  46.3 1.7 %collective-permute-start.14 = (bf16[12,1280]{1,0:T(8,128)(2,1)S(1)}, bf16[12,1280]{1,0:T(8,128)(2,1)S(1)}, u32[]{:S(2)}, u32[]{:S(2)}) collective-permute-start(bf16[12,1280]{1,0:T(8,128)(2,1)S(1)} %get-tuple-element.11), channel_id=1, source_target_pairs={{0,3},{1,2},{2,1},{3,0},{4,7},{5,6},{6,5},{7,4},{8,11},{9,10},{10,... | collective-permute-start | bytes 92168 | tf_op jit(solution)/shard_map/ppermute | solution.py:62
  47.9 2.7 %collective-permute-start.12 = (bf16[12,1280]{1,0:T(8,128)(2,1)S(1)}, bf16[12,1280]{1,0:T(8,128)(2,1)S(1)}, u32[]{:S(2)}, u32[]{:S(2)}) collective-permute-start(bf16[12,1280]{1,0:T(8,128)(2,1)S(1)} %get-tuple-element.11), channel_id=1, source_target_pairs={{0,1},{1,0},{2,3},{3,2},{4,5},{5,4},{6,7},{7,6},{8,9},{9,8},{10,11... | collective-permute-start | bytes 92168 | tf_op jit(solution)/shard_map/ppermute | solution.py:62
  50.7 0.6 pad_maximum_fusion.5
  51.3 0.7 reshape.104
  52.1 1.0 collective-permute-done.13
  53.1 6.7 %convolution_convert_fusion = bf16[48,4096]{1,0:T(8,128)(2,1)} fusion(bf16[1280,4096]{1,0:T(8,128)(2,1)} %param.22, bf16[12,1280]{1,0:T(8,128)(2,1)S(1)} %collective-permute-done.14, bf16[12,1280]{1,0:T(8,128)(2,1)S(1)} %collective-permute-done.13, bf16[12,1280]{1,0:T(8,128)(2,1)S(1)} %collective-permute-done.12, bf16[12,1280]{1,0:T(8,128)(2,1)S(1)} %get-tuple-element.11), kind=kOutput, calls=%fused_computation.4 | convolution fusion | flops 504004608 | bytes 11001856 | tf_op jit(solution)/shard_map/dot_general | solution.py:126
  59.8 1.9 %concatenate.21 = bf16[4,12,4096]{2,1,0:T(8,128)(2,1)} reshape(bf16[48,4096]{1,0:T(8,128)(2,1)} %convolution_convert_fusion) | data formatting | bytes 786432 | tf_op jit(solution)/shard_map/concatenate | solution.py:127
  61.6 6.7 %convolution_convert_fusion.1 = bf16[48,4096]{1,0:T(8,128)(2,1)} fusion(bf16[1280,4096]{1,0:T(8,128)(2,1)} %param.21, bf16[12,1280]{1,0:T(8,128)(2,1)S(1)} %collective-permute-done.14, bf16[12,1280]{1,0:T(8,128)(2,1)S(1)} %collective-permute-done.13, bf16[12,1280]{1,0:T(8,128)(2,1)S(1)} %collective-permute-done.12, bf16[12,1280]{1,0:T(8,128)(2,1)S(1)} %get-tuple-element.11), kind=kOutput, calls=%fused_computation.5 | convolution fusion | flops 504004608 | bytes 11001856 | tf_op jit(solution)/shard_map/dot_general | solution.py:125
  68.3 1.9 %concatenate.20 = bf16[4,12,4096]{2,1,0:T(8,128)(2,1)} reshape(bf16[48,4096]{1,0:T(8,128)(2,1)} %convolution_convert_fusion.1) | data formatting | bytes 786432 | tf_op jit(solution)/shard_map/concatenate | solution.py:127
  70.2 1.1 constant_dynamic-update-slice_fusion.3
  71.3 1.1 constant_dynamic-update-slice_fusion.2
  72.4 1.0 copy-done.1
  73.3 0.9 dynamic-slice_bitcast_fusion.2
  74.2 1.2 collective-permute-start.17
  75.4 1.0 collective-permute-start.16
  76.4 0.4 collective-permute-start.23
  76.8 1.0 collective-permute-start.22
  77.7 10.5 %collective-permute-done.23 = f32[12,128]{1,0:T(8,128)S(1)} collective-permute-done((f32[12,128]{1,0:T(8,128)S(1)}, f32[12,128]{1,0:T(8,128)S(1)}, u32[]{:S(2)}, u32[]{:S(2)}) %collective-permute-start.23) | collective-permute-done | bytes 6176 | tf_op jit(solution)/shard_map/ppermute | solution.py:62
  88.2 0.9 collective-permute-start.21
  89.2 0.7 collective-permute-done.21
  90.0 1.3 %fusion.21 = f32[12,8192]{1,0:T(8,128)S(1)} fusion(bf16[12,8192]{1,0:T(8,128)(2,1)} %collective-permute-done.17, bf16[12,8192]{1,0:T(8,128)(2,1)} %collective-permute-done.16, bf16[12,8192]{1,0:T(8,128)(2,1)} %collective-permute-done.15, f32[12]{0:T(128)S(1)} %fusion.33, bf16[4,12,8192]{2,1,0:T(8,128)(2,1)} %copy-done.1, s32[]{:T(128)S(6)} %select_n.96), kind=kLoop, calls=%fused_computation.27 | loop fusion | flops 786432 | bytes 1179700 | tf_op jit(solution)/shard_map/mul | solution.py:134
  91.5 1.1 collective-permute-start.25
  92.7 1.0 collective-permute-start.26
  93.8 4.1 %collective-permute-done.25 = bf16[12,4096]{1,0:T(8,128)(2,1)S(1)} collective-permute-done((bf16[12,4096]{1,0:T(8,128)(2,1)S(1)}, bf16[12,4096]{1,0:T(8,128)(2,1)S(1)}, u32[]{:S(2)}, u32[]{:S(2)}) %collective-permute-start.25) | collective-permute-done | bytes 98336 | tf_op jit(solution)/shard_map/ppermute | solution.py:62
  97.9 1.7 %collective-permute-done.26 = bf16[12,4096]{1,0:T(8,128)(2,1)S(1)} collective-permute-done((bf16[12,4096]{1,0:T(8,128)(2,1)S(1)}, bf16[12,4096]{1,0:T(8,128)(2,1)S(1)}, u32[]{:S(2)}, u32[]{:S(2)}) %collective-permute-start.26) | collective-permute-done | bytes 98336 | tf_op jit(solution)/shard_map/ppermute | solution.py:62
  99.5 0.9 pad_maximum_fusion
  100.4 2.5 %gather_fusion.3 = bf16[4,12,4096]{2,1,0:T(8,128)(2,1)} fusion(bf16[4,12,4096]{2,1,0:T(8,128)(2,1)} %pad_maximum_fusion, s32[1024]{0:T(1024)} %copy-done.4), kind=kCustom, calls=%fused_computation.3 | custom fusion | bytes 786448 | tf_op jit(solution)/shard_map/jit(_take)/gather | solution.py:136
  103.0 1.9 %gather.22 = bf16[48,4096]{1,0:T(8,128)(2,1)} reshape(bf16[4,12,4096]{2,1,0:T(8,128)(2,1)} %gather_fusion.3) | data formatting | bytes 786432 | tf_op jit(solution)/shard_map/jit(_take)/gather | solution.py:136
  104.9 6.1 %convolution_convert_fusion.2 = bf16[48,1280]{1,0:T(8,128)(2,1)S(1)} fusion(bf16[4096,1280]{1,0:T(8,128)(2,1)} %param.23, bf16[48,4096]{1,0:T(8,128)(2,1)} %gather.22, pred[48]{0:T(512)(128)(4,1)S(1)} %broadcast_in_dim.89), kind=kOutput, calls=%fused_computation.6 | convolution fusion | flops 503574528 | bytes 11001904 | tf_op jit(solution)/shard_map/dot_general | solution.py:137
  111.0 1.6 %collective-permute-start.27 = (bf16[12,1280]{1,0:T(8,128)(2,1)S(1)}, bf16[12,1280]{1,0:T(8,128)(2,1)S(1)}, u32[]{:S(2)}, u32[]{:S(2)}) collective-permute-start(bf16[12,1280]{1,0:T(8,128)(2,1)S(1)} %get-tuple-element.12), channel_id=1, source_target_pairs={{0,1},{1,0},{2,3},{3,2},{4,5},{5,4},{6,7},{7,6},{8,9},{9,8},{10,11... | collective-permute-start | bytes 92168 | tf_op jit(solution)/shard_map/ppermute | solution.py:62
  112.7 1.7 %collective-permute-start.29 = (bf16[12,1280]{1,0:T(8,128)(2,1)S(1)}, bf16[12,1280]{1,0:T(8,128)(2,1)S(1)}, u32[]{:S(2)}, u32[]{:S(2)}) collective-permute-start(bf16[12,1280]{1,0:T(8,128)(2,1)S(1)} %get-tuple-element.13), channel_id=1, source_target_pairs={{0,3},{1,2},{2,1},{3,0},{4,7},{5,6},{6,5},{7,4},{8,11},{9,10},{10,... | collective-permute-start | bytes 92168 | tf_op jit(solution)/shard_map/ppermute | solution.py:62
  114.6 0.5 collective-permute-done.27
  115.1 3.5 %collective-permute-done.29 = bf16[12,1280]{1,0:T(8,128)(2,1)S(1)} collective-permute-done((bf16[12,1280]{1,0:T(8,128)(2,1)S(1)}, bf16[12,1280]{1,0:T(8,128)(2,1)S(1)}, u32[]{:S(2)}, u32[]{:S(2)}) %collective-permute-start.29) | collective-permute-done | bytes 30752 | tf_op jit(solution)/shard_map/ppermute | solution.py:62
  118.6 1.2 %collective-permute-done.28 = bf16[12,1280]{1,0:T(8,128)(2,1)S(1)} collective-permute-done((bf16[12,1280]{1,0:T(8,128)(2,1)S(1)}, bf16[12,1280]{1,0:T(8,128)(2,1)S(1)}, u32[]{:S(2)}, u32[]{:S(2)}) %collective-permute-start.28) | collective-permute-done | bytes 30752 | tf_op jit(solution)/shard_map/ppermute | solution.py:62
  119.8 0.7 add_convert_fusion
  (87 shorter events, 3.3 us)
Async XLA Ops:
  0.0 30.9 %copy-start = (bf16[1280,1280]{1,0:T(8,128)(2,1)S(1)}, bf16[1280,1280]{1,0:T(8,128)(2,1)}, u32[]{:S(2)}) copy-start(bf16[1280,1280]{1,0:T(8,128)(2,1)} %param.19) | copy-start | bytes 9830404
  1.7 39.8 %copy-start.5 = (pred[12]{0:T(512)(128)(4,1)}, pred[12]{0:T(512)(128)(4,1)S(1)}, u32[]{:S(2)}) copy-start(pred[12]{0:T(512)(128)(4,1)S(1)} %get-tuple-element.5) | copy-start | bytes 40
  2.7 4.6 %collective-permute-start = (bf16[3,1792]{1,0:T(4,128)(2,1)S(1)}, bf16[3,1792]{1,0:T(4,128)(2,1)S(1)}, u32[]{:S(2)}, u32[]{:S(2)}) collective-permute-start(bf16[3,1792]{1,0:T(4,128)(2,1)S(1)} %convolution_convert_fusion.6), channel_id=1, source_target_pairs={{0,4},{4,0},{8,12},{12,8},{1,5},{5,1},{9,13},{13,9},{2,6},{6,2},{1... | collective-permute-start | bytes 32264 | tf_op jit(solution)/shard_map/ppermute | solution.py:62
  3.3 4.2 %collective-permute-start.1 = (bf16[3,1792]{1,0:T(4,128)(2,1)S(1)}, bf16[3,1792]{1,0:T(4,128)(2,1)S(1)}, u32[]{:S(2)}, u32[]{:S(2)}) collective-permute-start(bf16[3,1792]{1,0:T(4,128)(2,1)S(1)} %convolution_convert_fusion.5), channel_id=1, source_target_pairs={{0,8},{4,12},{8,0},{12,4},{1,9},{5,13},{9,1},{13,5},{2,10},{6,14},... | collective-permute-start | bytes 32264 | tf_op jit(solution)/shard_map/ppermute | solution.py:62
  6.1 3.2 %collective-permute-start.2 = (bf16[3,1792]{1,0:T(4,128)(2,1)S(1)}, bf16[3,1792]{1,0:T(4,128)(2,1)S(1)}, u32[]{:S(2)}, u32[]{:S(2)}) collective-permute-start(bf16[3,1792]{1,0:T(4,128)(2,1)S(1)} %convolution_convert_fusion.4), channel_id=1, source_target_pairs={{0,12},{4,8},{8,4},{12,0},{1,13},{5,9},{9,5},{13,1},{2,14},{6,10},... | collective-permute-start | bytes 32264 | tf_op jit(solution)/shard_map/ppermute | solution.py:62
  7.0 23.1 %copy-start.4 = (s32[1024]{0:T(1024)}, s32[1024]{0:T(1024)S(1)}, u32[]{:S(2)}) copy-start(s32[1024]{0:T(1024)S(1)} %pad_clamp_fusion.1) | copy-start | bytes 12292
  7.2 22.9 %copy-start.8 = (pred[4]{0:T(512)(128)(4,1)}, pred[4]{0:T(512)(128)(4,1)S(1)}, u32[]{:S(2)}) copy-start(pred[4]{0:T(512)(128)(4,1)S(1)} %compare_and_fusion) | copy-start | bytes 16
  14.7 21.4 %copy-start.7 = (bf16[1280]{0:T(1024)(128)(2,1)S(1)}, bf16[1280]{0:T(1024)(128)(2,1)}, u32[]{:S(2)}) copy-start(bf16[1280]{0:T(1024)(128)(2,1)} %param.20) | copy-start | bytes 7684
  14.7 5.5 %collective-permute-start.5 = (bf16[3,1280]{1,0:T(4,128)(2,1)S(1)}, bf16[3,1280]{1,0:T(4,128)(2,1)S(1)}, u32[]{:S(2)}, u32[]{:S(2)}) collective-permute-start(bf16[3,1280]{1,0:T(4,128)(2,1)S(1)} %get-tuple-element.19), channel_id=1, source_target_pairs={{0,3},{1,2},{2,1},{3,0},{4,7},{5,6},{6,5},{7,4},{8,11},{9,10},{10,... | collective-permute-start | bytes 23048 | tf_op jit(solution)/shard_map/ppermute | solution.py:62
  18.4 4.6 %collective-permute-start.4 = (bf16[3,1280]{1,0:T(4,128)(2,1)S(1)}, bf16[3,1280]{1,0:T(4,128)(2,1)S(1)}, u32[]{:S(2)}, u32[]{:S(2)}) collective-permute-start(bf16[3,1280]{1,0:T(4,128)(2,1)S(1)} %get-tuple-element.20), channel_id=1, source_target_pairs={{0,2},{1,3},{2,0},{3,1},{4,6},{5,7},{6,4},{7,5},{8,10},{9,11},{10,... | collective-permute-start | bytes 23048 | tf_op jit(solution)/shard_map/ppermute | solution.py:62
  18.4 23.2 %copy-start.2 = (bf16[12,1280]{1,0:T(8,128)(2,1)S(1)}, bf16[12,1280]{1,0:T(8,128)(2,1)}, u32[]{:S(2)}) copy-start(bf16[12,1280]{1,0:T(8,128)(2,1)} %param.12) | copy-start | bytes 92164
  18.4 4.6 %collective-permute-start.3 = (bf16[3,1280]{1,0:T(4,128)(2,1)S(1)}, bf16[3,1280]{1,0:T(4,128)(2,1)S(1)}, u32[]{:S(2)}, u32[]{:S(2)}) collective-permute-start(bf16[3,1280]{1,0:T(4,128)(2,1)S(1)} %get-tuple-element.21), channel_id=1, source_target_pairs={{0,1},{1,0},{2,3},{3,2},{4,5},{5,4},{6,7},{7,6},{8,9},{9,8},{10,11... | collective-permute-start | bytes 23048 | tf_op jit(solution)/shard_map/ppermute | solution.py:62
  23.0 4.5 %collective-permute-start.7 = (bf16[4,3,1280]{2,1,0:T(4,128)(2,1)S(1)}, bf16[4,3,1280]{2,1,0:T(4,128)(2,1)S(1)}, u32[]{:S(2)}, u32[]{:S(2)}) collective-permute-start(bf16[4,3,1280]{2,1,0:T(4,128)(2,1)S(1)} %pad_maximum_fusion.4), channel_id=1, source_target_pairs={{0,8},{4,12},{8,0},{12,4},{1,9},{5,13},{9,1},{13,5},{2,10},{6,14},... | collective-permute-start | bytes 92168 | tf_op jit(solution)/shard_map/ppermute | solution.py:62
  23.6 3.9 %collective-permute-start.6 = (bf16[4,3,1280]{2,1,0:T(4,128)(2,1)S(1)}, bf16[4,3,1280]{2,1,0:T(4,128)(2,1)S(1)}, u32[]{:S(2)}, u32[]{:S(2)}) collective-permute-start(bf16[4,3,1280]{2,1,0:T(4,128)(2,1)S(1)} %pad_maximum_fusion.4), channel_id=1, source_target_pairs={{0,4},{4,0},{8,12},{12,8},{1,5},{5,1},{9,13},{13,9},{2,6},{6,2},{1... | collective-permute-start | bytes 92168 | tf_op jit(solution)/shard_map/ppermute | solution.py:62
  23.6 3.9 %collective-permute-start.8 = (bf16[4,3,1280]{2,1,0:T(4,128)(2,1)S(1)}, bf16[4,3,1280]{2,1,0:T(4,128)(2,1)S(1)}, u32[]{:S(2)}, u32[]{:S(2)}) collective-permute-start(bf16[4,3,1280]{2,1,0:T(4,128)(2,1)S(1)} %pad_maximum_fusion.4), channel_id=1, source_target_pairs={{0,12},{4,8},{8,4},{12,0},{1,13},{5,9},{9,5},{13,1},{2,14},{6,10},... | collective-permute-start | bytes 92168 | tf_op jit(solution)/shard_map/ppermute | solution.py:62
  32.5 4.1 %collective-permute-start.9 = (bf16[12,1280]{1,0:T(8,128)(2,1)S(1)}, bf16[12,1280]{1,0:T(8,128)(2,1)S(1)}, u32[]{:S(2)}, u32[]{:S(2)}) collective-permute-start(bf16[12,1280]{1,0:T(8,128)(2,1)S(1)} %get-tuple-element.15), channel_id=1, source_target_pairs={{0,1},{1,0},{2,3},{3,2},{4,5},{5,4},{6,7},{7,6},{8,9},{9,8},{10,11... | collective-permute-start | bytes 92168 | tf_op jit(solution)/shard_map/ppermute | solution.py:62
  32.6 6.5 %collective-permute-start.11 = (bf16[12,1280]{1,0:T(8,128)(2,1)S(1)}, bf16[12,1280]{1,0:T(8,128)(2,1)S(1)}, u32[]{:S(2)}, u32[]{:S(2)}) collective-permute-start(bf16[12,1280]{1,0:T(8,128)(2,1)S(1)} %get-tuple-element.16), channel_id=1, source_target_pairs={{0,3},{1,2},{2,1},{3,0},{4,7},{5,6},{6,5},{7,4},{8,11},{9,10},{10,... | collective-permute-start | bytes 92168 | tf_op jit(solution)/shard_map/ppermute | solution.py:62
  36.1 4.9 %collective-permute-start.10 = (bf16[12,1280]{1,0:T(8,128)(2,1)S(1)}, bf16[12,1280]{1,0:T(8,128)(2,1)S(1)}, u32[]{:S(2)}, u32[]{:S(2)}) collective-permute-start(bf16[12,1280]{1,0:T(8,128)(2,1)S(1)} %get-tuple-element.17), channel_id=1, source_target_pairs={{0,2},{1,3},{2,0},{3,1},{4,6},{5,7},{6,4},{7,5},{8,10},{9,11},{10,... | collective-permute-start | bytes 92168 | tf_op jit(solution)/shard_map/ppermute | solution.py:62
  41.9 6.1 %collective-permute-start.20 = (f32[12,128]{1,0:T(8,128)S(1)}, f32[12,128]{1,0:T(8,128)S(1)}, u32[]{:S(2)}, u32[]{:S(2)}) collective-permute-start(f32[12,128]{1,0:T(8,128)S(1)} %broadcast_in_dim.91), channel_id=1, source_target_pairs={{0,3},{1,2},{2,1},{3,0},{4,7},{5,6},{6,5},{7,4},{8,11},{9,10},{10,... | collective-permute-start | bytes 18440 | tf_op jit(solution)/shard_map/ppermute | solution.py:62
  43.5 7.1 %collective-permute-start.19 = (f32[12,128]{1,0:T(8,128)S(1)}, f32[12,128]{1,0:T(8,128)S(1)}, u32[]{:S(2)}, u32[]{:S(2)}) collective-permute-start(f32[12,128]{1,0:T(8,128)S(1)} %broadcast_in_dim.91), channel_id=1, source_target_pairs={{0,2},{1,3},{2,0},{3,1},{4,6},{5,7},{6,4},{7,5},{8,10},{9,11},{10,... | collective-permute-start | bytes 18440 | tf_op jit(solution)/shard_map/ppermute | solution.py:62
  43.5 7.1 %collective-permute-start.18 = (f32[12,128]{1,0:T(8,128)S(1)}, f32[12,128]{1,0:T(8,128)S(1)}, u32[]{:S(2)}, u32[]{:S(2)}) collective-permute-start(f32[12,128]{1,0:T(8,128)S(1)} %broadcast_in_dim.91), channel_id=1, source_target_pairs={{0,1},{1,0},{2,3},{3,2},{4,5},{5,4},{6,7},{7,6},{8,9},{9,8},{10,11... | collective-permute-start | bytes 18440 | tf_op jit(solution)/shard_map/ppermute | solution.py:62
  46.3 5.8 %collective-permute-start.14 = (bf16[12,1280]{1,0:T(8,128)(2,1)S(1)}, bf16[12,1280]{1,0:T(8,128)(2,1)S(1)}, u32[]{:S(2)}, u32[]{:S(2)}) collective-permute-start(bf16[12,1280]{1,0:T(8,128)(2,1)S(1)} %get-tuple-element.11), channel_id=1, source_target_pairs={{0,3},{1,2},{2,1},{3,0},{4,7},{5,6},{6,5},{7,4},{8,11},{9,10},{10,... | collective-permute-start | bytes 92168 | tf_op jit(solution)/shard_map/ppermute | solution.py:62
  47.9 5.1 %collective-permute-start.13 = (bf16[12,1280]{1,0:T(8,128)(2,1)S(1)}, bf16[12,1280]{1,0:T(8,128)(2,1)S(1)}, u32[]{:S(2)}, u32[]{:S(2)}) collective-permute-start(bf16[12,1280]{1,0:T(8,128)(2,1)S(1)} %get-tuple-element.11), channel_id=1, source_target_pairs={{0,2},{1,3},{2,0},{3,1},{4,6},{5,7},{6,4},{7,5},{8,10},{9,11},{10,... | collective-permute-start | bytes 92168 | tf_op jit(solution)/shard_map/ppermute | solution.py:62
  47.9 5.1 %collective-permute-start.12 = (bf16[12,1280]{1,0:T(8,128)(2,1)S(1)}, bf16[12,1280]{1,0:T(8,128)(2,1)S(1)}, u32[]{:S(2)}, u32[]{:S(2)}) collective-permute-start(bf16[12,1280]{1,0:T(8,128)(2,1)S(1)} %get-tuple-element.11), channel_id=1, source_target_pairs={{0,1},{1,0},{2,3},{3,2},{4,5},{5,4},{6,7},{7,6},{8,9},{9,8},{10,11... | collective-permute-start | bytes 92168 | tf_op jit(solution)/shard_map/ppermute | solution.py:62
  68.3 20.8 %copy-start.9 = (pred[4]{0:T(512)(128)(4,1)S(1)}, pred[4]{0:T(512)(128)(4,1)}, u32[]{:S(2)}) copy-start(pred[4]{0:T(512)(128)(4,1)} %copy-done.8) | copy-start | bytes 16
  72.4 1.0 copy-start.1
  74.2 15.8 %collective-permute-start.15 = (bf16[12,8192]{1,0:T(8,128)(2,1)}, bf16[12,8192]{1,0:T(8,128)(2,1)}, u32[]{:S(2)}, u32[]{:S(2)}) collective-permute-start(bf16[12,8192]{1,0:T(8,128)(2,1)} %get-tuple-element.7), channel_id=1, source_target_pairs={{0,4},{4,0},{8,12},{12,8},{1,5},{5,1},{9,13},{13,9},{2,6},{6,2},{1... | collective-permute-start | bytes 589832 | tf_op jit(solution)/shard_map/ppermute | solution.py:62
  74.2 15.8 %collective-permute-start.17 = (bf16[12,8192]{1,0:T(8,128)(2,1)}, bf16[12,8192]{1,0:T(8,128)(2,1)}, u32[]{:S(2)}, u32[]{:S(2)}) collective-permute-start(bf16[12,8192]{1,0:T(8,128)(2,1)} %get-tuple-element.8), channel_id=1, source_target_pairs={{0,12},{4,8},{8,4},{12,0},{1,13},{5,9},{9,5},{13,1},{2,14},{6,10},... | collective-permute-start | bytes 589832 | tf_op jit(solution)/shard_map/ppermute | solution.py:62
  75.4 14.6 %collective-permute-start.16 = (bf16[12,8192]{1,0:T(8,128)(2,1)}, bf16[12,8192]{1,0:T(8,128)(2,1)}, u32[]{:S(2)}, u32[]{:S(2)}) collective-permute-start(bf16[12,8192]{1,0:T(8,128)(2,1)} %get-tuple-element.9), channel_id=1, source_target_pairs={{0,8},{4,12},{8,0},{12,4},{1,9},{5,13},{9,1},{13,5},{2,10},{6,14},... | collective-permute-start | bytes 589832 | tf_op jit(solution)/shard_map/ppermute | solution.py:62
  76.4 11.8 %collective-permute-start.23 = (f32[12,128]{1,0:T(8,128)S(1)}, f32[12,128]{1,0:T(8,128)S(1)}, u32[]{:S(2)}, u32[]{:S(2)}) collective-permute-start(f32[12,128]{1,0:T(8,128)S(1)} %get-tuple-element.25), channel_id=1, source_target_pairs={{0,12},{4,8},{8,4},{12,0},{1,13},{5,9},{9,5},{13,1},{2,14},{6,10},... | collective-permute-start | bytes 18440 | tf_op jit(solution)/shard_map/ppermute | solution.py:62
  76.8 12.5 %collective-permute-start.22 = (f32[12,128]{1,0:T(8,128)S(1)}, f32[12,128]{1,0:T(8,128)S(1)}, u32[]{:S(2)}, u32[]{:S(2)}) collective-permute-start(f32[12,128]{1,0:T(8,128)S(1)} %get-tuple-element.26), channel_id=1, source_target_pairs={{0,8},{4,12},{8,0},{12,4},{1,9},{5,13},{9,1},{13,5},{2,10},{6,14},... | collective-permute-start | bytes 18440 | tf_op jit(solution)/shard_map/ppermute | solution.py:62
  88.2 1.7 %collective-permute-start.21 = (f32[12,128]{1,0:T(8,128)S(1)}, f32[12,128]{1,0:T(8,128)S(1)}, u32[]{:S(2)}, u32[]{:S(2)}) collective-permute-start(f32[12,128]{1,0:T(8,128)S(1)} %get-tuple-element.27), channel_id=1, source_target_pairs={{0,4},{4,0},{8,12},{12,8},{1,5},{5,1},{9,13},{13,9},{2,6},{6,2},{1... | collective-permute-start | bytes 18440 | tf_op jit(solution)/shard_map/ppermute | solution.py:62
  91.5 6.4 %collective-permute-start.25 = (bf16[12,4096]{1,0:T(8,128)(2,1)S(1)}, bf16[12,4096]{1,0:T(8,128)(2,1)S(1)}, u32[]{:S(2)}, u32[]{:S(2)}) collective-permute-start(bf16[12,4096]{1,0:T(8,128)(2,1)S(1)} %fusion.24), channel_id=1, source_target_pairs={{0,8},{4,12},{8,0},{12,4},{1,9},{5,13},{9,1},{13,5},{2,10},{6,14},... | collective-permute-start | bytes 294920 | tf_op jit(solution)/shard_map/ppermute | solution.py:62
  92.6 5.3 %collective-permute-start.24 = (bf16[12,4096]{1,0:T(8,128)(2,1)S(1)}, bf16[12,4096]{1,0:T(8,128)(2,1)S(1)}, u32[]{:S(2)}, u32[]{:S(2)}) collective-permute-start(bf16[12,4096]{1,0:T(8,128)(2,1)S(1)} %fusion.24), channel_id=1, source_target_pairs={{0,4},{4,0},{8,12},{12,8},{1,5},{5,1},{9,13},{13,9},{2,6},{6,2},{1... | collective-permute-start | bytes 294920 | tf_op jit(solution)/shard_map/ppermute | solution.py:62
  92.7 6.9 %collective-permute-start.26 = (bf16[12,4096]{1,0:T(8,128)(2,1)S(1)}, bf16[12,4096]{1,0:T(8,128)(2,1)S(1)}, u32[]{:S(2)}, u32[]{:S(2)}) collective-permute-start(bf16[12,4096]{1,0:T(8,128)(2,1)S(1)} %fusion.24), channel_id=1, source_target_pairs={{0,12},{4,8},{8,4},{12,0},{1,13},{5,9},{9,5},{13,1},{2,14},{6,10},... | collective-permute-start | bytes 294920 | tf_op jit(solution)/shard_map/ppermute | solution.py:62
  104.9 15.0 %copy-start.3 = (bf16[12,1280]{1,0:T(8,128)(2,1)S(1)}, bf16[12,1280]{1,0:T(8,128)(2,1)}, u32[]{:S(2)}) copy-start(bf16[12,1280]{1,0:T(8,128)(2,1)} %param.12) | copy-start | bytes 92164
  104.9 15.0 %copy-start.6 = (pred[12]{0:T(512)(128)(4,1)S(1)}, pred[12]{0:T(512)(128)(4,1)}, u32[]{:S(2)}) copy-start(pred[12]{0:T(512)(128)(4,1)} %copy-done.5) | copy-start | bytes 40
  111.0 4.1 %collective-permute-start.27 = (bf16[12,1280]{1,0:T(8,128)(2,1)S(1)}, bf16[12,1280]{1,0:T(8,128)(2,1)S(1)}, u32[]{:S(2)}, u32[]{:S(2)}) collective-permute-start(bf16[12,1280]{1,0:T(8,128)(2,1)S(1)} %get-tuple-element.12), channel_id=1, source_target_pairs={{0,1},{1,0},{2,3},{3,2},{4,5},{5,4},{6,7},{7,6},{8,9},{9,8},{10,11... | collective-permute-start | bytes 92168 | tf_op jit(solution)/shard_map/ppermute | solution.py:62
  112.7 5.9 %collective-permute-start.29 = (bf16[12,1280]{1,0:T(8,128)(2,1)S(1)}, bf16[12,1280]{1,0:T(8,128)(2,1)S(1)}, u32[]{:S(2)}, u32[]{:S(2)}) collective-permute-start(bf16[12,1280]{1,0:T(8,128)(2,1)S(1)} %get-tuple-element.13), channel_id=1, source_target_pairs={{0,3},{1,2},{2,1},{3,0},{4,7},{5,6},{6,5},{7,4},{8,11},{9,10},{10,... | collective-permute-start | bytes 92168 | tf_op jit(solution)/shard_map/ppermute | solution.py:62
  114.3 5.5 %collective-permute-start.28 = (bf16[12,1280]{1,0:T(8,128)(2,1)S(1)}, bf16[12,1280]{1,0:T(8,128)(2,1)S(1)}, u32[]{:S(2)}, u32[]{:S(2)}) collective-permute-start(bf16[12,1280]{1,0:T(8,128)(2,1)S(1)} %get-tuple-element.14), channel_id=1, source_target_pairs={{0,2},{1,3},{2,0},{3,1},{4,6},{5,7},{6,4},{7,5},{8,10},{9,11},{10,... | collective-permute-start | bytes 92168 | tf_op jit(solution)/shard_map/ppermute | solution.py:62

commit v2 on v1

--- a/solution.py
+++ b/solution.py
@@ -1,8 +1,11 @@
+import functools
 import math
 
 import jax
 import jax.numpy as jnp
 from jax import lax
+from jax.experimental import pallas as pl
+from jax.experimental.pallas import tpu as pltpu
 from jax.sharding import PartitionSpec as P
 
 D = 5120
@@ -141,9 +144,373 @@
     return (stream + ff_out).astype(jnp.bfloat16)
 
 
+MIB = 1024 * 1024
+
+
+def call(kernel, outs, operands, scratch=(), smem=(), resident=(), flops=0, moved=0, limit=8):
+    specs = []
+    placed = []
+    for place, operand in enumerate(operands):
+        space = pltpu.SMEM if place in smem else pltpu.VMEM
+        specs.append(pl.BlockSpec(memory_space=space))
+        placed.append(in_vmem(operand) if place in resident else operand)
+    return pl.pallas_call(
+        kernel,
+        out_shape=[jax.ShapeDtypeStruct(shape, dtype) for shape, dtype in outs],
+        in_specs=specs,
+        out_specs=[pl.BlockSpec(memory_space=pltpu.VMEM) for _ in outs],
+        scratch_shapes=list(scratch),
+        compiler_params=pltpu.CompilerParams(vmem_limit_bytes=limit * MIB),
+        cost_estimate=pl.CostEstimate(flops=flops, bytes_accessed=moved, transcendentals=0),
+    )(*placed)
+
+
+def in_vmem(operand):
+    return pltpu.with_memory_space_constraint(operand, pltpu.VMEM)
+
+
+def swap(value, axis, step):
+    count = lax.axis_size(axis)
+    return lax.ppermute(value, axis, [(i, i ^ step) for i in range(count)])
+
+
+def pick_kernel(per_device, group, heads, query_a, pairs_a, query_b, pairs_b, assign, keep, send, rows):
+    sec, tp = lax.axis_index("sec"), lax.axis_index("tp")
+    odd = (sec & 1) == 1
+    slots = jnp.zeros((1, group), jnp.int32)
+    for index in range(assign.shape[1] // group):
+        slots = jnp.where(tp == index, assign[:, index * group : (index + 1) * group], slots)
+    line = lax.broadcasted_iota(jnp.int32, (16, group), 0)
+    wanted = jnp.where(line < 8, sec * per_device + line, (sec ^ 2) * per_device + line - 8)
+    inside = (line & 7) < per_device
+    picker = jnp.where(inside & (jnp.broadcast_to(slots, (16, group)) == wanted), 1.0, 0.0).astype(jnp.bfloat16)
+
+    def picked(ref):
+        return jnp.dot(picker, ref[...], preferred_element_type=jnp.float32)
+
+    mine_q, mine_p, other_q, other_p = picked(query_a), picked(pairs_a), picked(query_b), picked(pairs_b)
+    both = (
+        (jnp.where(odd, other_q, mine_q), jnp.where(odd, other_p, mine_p)),
+        (jnp.where(odd, mine_q, other_q), jnp.where(odd, mine_p, other_p)),
+    )
+    rows[...] = jnp.zeros_like(rows)
+    width = HEAD_WIDTH
+    for side in range(2):
+        for place, (queries, pairs) in enumerate(both):
+            for j in range(per_device):
+                base = j * 32 + place * 16
+                line = side * 8 + j
+                for h in range(heads):
+                    rows[side, base + h : base + h + 1, :] = queries[line : line + 1, h * width : (h + 1) * width]
+                for h in range(pairs.shape[1] // width):
+                    at = base + heads + h
+                    rows[side, at : at + 1, :] = pairs[line : line + 1, h * width : (h + 1) * width]
+    keep[...] = rows[0].astype(jnp.bfloat16)
+    send[...] = rows[1].astype(jnp.bfloat16)
+
+
+def attend_kernel(per_device, heads, lengths, mine, other, keys, values, keep, send, total):
+    sec, tp = lax.axis_index("sec"), lax.axis_index("tp")
+    high = (sec >> 1) == 1
+    share = heads // 2
+    first, second = mine[...], other[...]
+    halves = (jnp.where(high, second, first), jnp.where(high, first, second))
+    slots = keys.shape[1]
+    width = HEAD_WIDTH
+    scaling = 1.0 / math.sqrt(width)
+    line = lax.broadcasted_iota(jnp.int32, (16, width), 0)
+    upper = line < share
+    place = lax.broadcasted_iota(jnp.int32, (16, slots), 1)
+    total[...] = jnp.zeros_like(total)
+    for j in range(per_device):
+        valid = place < lengths[j]
+        for b in range(4):
+            base = j * 32 + (b & 1) * 16
+            block = halves[b >> 1][base : base + 16]
+            wide = block.astype(jnp.float32)
+            zero = jnp.zeros_like(wide)
+            left = jnp.where(upper, wide, zero).astype(jnp.bfloat16)
+            right = jnp.where(upper, zero, wide).astype(jnp.bfloat16)
+            both = jnp.concatenate([left, right], axis=1)
+            columns = slice(b * 2 * width, (b + 1) * 2 * width)
+            past = lax.dot_general(
+                both, keys[j, :, columns], (((1,), (1,)), ((), ())), preferred_element_type=jnp.float32
+            )
+            past = jnp.where(valid, past * scaling, -1e30)
+            new_key = jnp.where(upper, wide[heads : heads + 1], wide[heads + 2 : heads + 3])
+            new_value = jnp.where(upper, wide[heads + 1 : heads + 2], wide[heads + 3 : heads + 4])
+            fresh = jnp.sum(wide * new_key, axis=1, keepdims=True) * scaling
+            highest = jnp.maximum(jnp.max(past, axis=1, keepdims=True), fresh)
+            past_exp = jnp.exp(past - highest)
+            fresh_exp = jnp.exp(fresh - highest)
+            inverse = 1.0 / (jnp.sum(past_exp, axis=1, keepdims=True) + fresh_exp)
+            weights = (past_exp * inverse).astype(jnp.bfloat16)
+            fresh_weight = (fresh_exp * inverse).astype(jnp.bfloat16).astype(jnp.float32)
+            mixed = jnp.dot(weights, values[j, :, columns], preferred_element_type=jnp.float32)
+            mixed = jnp.where(upper, mixed[:, :width], mixed[:, width:]) + fresh_weight * new_value
+            side = (b & 1) ^ (tp & 1)
+            for h in range(heads):
+                total[side, b >> 1, j : j + 1, h * width : (h + 1) * width] = mixed[h : h + 1]
+    keep[...] = total[0, :, 0:4].astype(jnp.bfloat16)
+    send[...] = total[1, :, 0:4].astype(jnp.bfloat16)
+
+
+def forward_kernel(mine, other, send):
+    away = (lax.axis_index("tp") >> 1) ^ 1
+    send[0] = mine[away]
+    send[1] = other[away]
+
+
+def gather_kernel(mine, other, far, out, rows):
+    here = lax.axis_index("tp") >> 1
+    rows[0:4] = mine[here].astype(jnp.float32)
+    rows[4:8] = other[here].astype(jnp.float32)
+    rows[8:12] = far[0].astype(jnp.float32)
+    rows[12:16] = far[1].astype(jnp.float32)
+    out[...] = rows[...].astype(jnp.bfloat16)
+
+
+def group_order(group, shape, axis):
+    place = lax.broadcasted_iota(jnp.int32, shape, axis)
+    number = jnp.zeros(shape, jnp.int32)
+    for limit in range(1, 4):
+        number = number + jnp.where(place >= limit * group, 1, 0)
+    return (((number & 1) << 1) | (number >> 1)) * group + place - number * group
+
+
+def project_kernel(per_device, group, first, second, third, fourth, assign, weight, keep, send, product):
+    sec, tp = lax.axis_index("sec"), lax.axis_index("tp")
+    count = assign.shape[1]
+    lines = jnp.concatenate([first[...], second[...], third[...], fourth[...]], axis=0)
+    line = lax.broadcasted_iota(jnp.int32, (64, count), 0)
+    request = lax.broadcasted_iota(jnp.int32, (64, count), 1)
+    number = jnp.zeros((64, count), jnp.int32)
+    for limit in range(1, 4):
+        number = number + jnp.where(request >= limit * group, 1, 0)
+    slot = (sec ^ (line >> 4)) * per_device + (line & 3)
+    match = (number == (tp ^ ((line >> 2) & 3))) & (jnp.broadcast_to(assign[...], (64, count)) == slot)
+    match = jnp.where(match & ((line & 3) < per_device), 1.0, 0.0).astype(jnp.bfloat16)
+    order = group_order(group, (count, count), 1) == lax.broadcasted_iota(jnp.int32, (count, count), 0)
+    order = jnp.where(order, 1.0, 0.0).astype(jnp.bfloat16)
+    match = jnp.dot(match, order, preferred_element_type=jnp.float32).astype(jnp.bfloat16)
+    ordered = lax.dot_general(match, lines, (((0,), (0,)), ((), ())), preferred_element_type=jnp.float32)
+    ordered = ordered.astype(jnp.bfloat16)
+    product[...] = jnp.dot(ordered, weight[...], preferred_element_type=jnp.float32)
+    half = count // 2
+    odd = tp & 1
+    keep[...] = product[pl.ds(pl.multiple_of(odd * half, 8), half), :]
+    send[...] = product[pl.ds(pl.multiple_of((1 - odd) * half, 8), half), :].astype(jnp.bfloat16)
+
+
+def add_resid_kernel(mine, other, resid, keep, send):
+    tp = lax.axis_index("tp")
+    group = resid.shape[0]
+    line = lax.broadcasted_iota(jnp.int32, (2 * group, group), 0)
+    match = line == lax.broadcasted_iota(jnp.int32, (2 * group, group), 1) + (tp >> 1) * group
+    match = jnp.where(match, 1.0, 0.0).astype(jnp.bfloat16)
+    total = mine[...] + other[...].astype(jnp.float32)
+    total = total + jnp.dot(match, resid[...], preferred_element_type=jnp.float32)
+    keep[...] = total
+    send[...] = total.astype(jnp.bfloat16)
+
+
+def stream_kernel(mine, other, stream, send):
+    total = mine[...] + other[...].astype(jnp.float32)
+    stream[...] = total
+    send[...] = total.astype(jnp.bfloat16)
+
+
+def gate_up_kernel(chunk, mine, other, gain, gate, up, keep, send, lines):
+    sec, tp = lax.axis_index("sec"), lax.axis_index("tp")
+    half = mine.shape[0]
+    mine_at = (tp ^ sec) & 1
+    lines[mine_at] = mine[...].astype(jnp.float32)
+    lines[1 - mine_at] = other[...].astype(jnp.float32)
+    stream = jnp.concatenate([lines[0], lines[1]], axis=0)
+    squares = jnp.sum(stream * stream, axis=1, keepdims=True)
+    features = (stream * gain[...].astype(jnp.float32)).astype(jnp.bfloat16)
+    width = gate.shape[1] // 2
+    for part in range(2):
+        for kind, weight in enumerate((gate, up)):
+            for start in range(0, width, chunk):
+                column = part * width + start
+                product = jnp.dot(features, weight[:, column : column + chunk], preferred_element_type=jnp.float32)
+                at = kind * width + start
+                keep[part, :, at : at + chunk] = product[:half]
+                send[part, :, at : at + chunk] = product[half:].astype(jnp.bfloat16)
+        keep[part, :, 2 * width :] = jnp.broadcast_to(squares[:half], (half, 128))
+        send[part, :, 2 * width :] = two_terms(squares[half:])
+
+
+def two_terms(column):
+    shape = (column.shape[0], 128)
+    column = jnp.broadcast_to(column, shape)
+    coarse = column.astype(jnp.bfloat16).astype(jnp.float32)
+    lane = lax.broadcasted_iota(jnp.int32, shape, 1)
+    return jnp.where(lane < 64, coarse, column - coarse).astype(jnp.bfloat16)
+
+
+def one_column(terms):
+    return terms[:, 0:1].astype(jnp.float32) + terms[:, 64:65].astype(jnp.float32)
+
+
+def pair_sum_kernel(mine, other, keep, send):
+    here = lax.axis_index("sec") >> 1
+    width = mine.shape[2] - 128
+    for target, part in ((send, 1 - here), (keep, here)):
+        total = mine[part, :, :width] + other[part, :, :width].astype(jnp.float32)
+        target[:, :width] = total.astype(target.dtype)
+    squares = mine[0, :, width:] + one_column(other[0, :, width:])
+    keep[:, width:] = squares
+    send[:, width:] = two_terms(squares[:, 0:1])
+
+
+def hidden_kernel(features, mine, other, hidden):
+    width = (mine.shape[1] - 128) // 2
+    squares = mine[:, 2 * width : 2 * width + 1] + one_column(other[:, 2 * width :])
+    inverse = lax.rsqrt(squares / features + 1e-06)
+    gate = (mine[:, :width] + other[:, :width].astype(jnp.float32)) * inverse
+    up = (mine[:, width : 2 * width] + other[:, width : 2 * width].astype(jnp.float32)) * inverse
+    hidden[...] = (gate / (1.0 + jnp.exp(-gate)) * up).astype(jnp.bfloat16)
+
+
+def down_first_kernel(mine, other, weight, out):
+    here = lax.axis_index("sec") >> 1
+    lines = jnp.concatenate([mine[...].astype(jnp.float32), other[...].astype(jnp.float32)], axis=0)
+    lines = lines.astype(jnp.bfloat16)
+    depth = lines.shape[1]
+    rows = weight[pl.ds(pl.multiple_of(here * depth, depth), depth), :]
+    out[...] = jnp.dot(lines, rows, preferred_element_type=jnp.float32)
+
+
+def down_second_kernel(mine, other, before, weight, keep, send, product):
+    sec, tp = lax.axis_index("sec"), lax.axis_index("tp")
+    away = 1 - (sec >> 1)
+    lines = jnp.concatenate([mine[...].astype(jnp.float32), other[...].astype(jnp.float32)], axis=0)
+    lines = lines.astype(jnp.bfloat16)
+    depth = lines.shape[1]
+    rows = weight[pl.ds(pl.multiple_of(away * depth, depth), depth), :]
+    product[...] = before[...] + jnp.dot(lines, rows, preferred_element_type=jnp.float32)
+    half = product.shape[0] // 2
+    at = (sec ^ tp) & 1
+    keep[...] = product[pl.ds(pl.multiple_of(at * half, 8), half), :]
+    send[...] = product[pl.ds(pl.multiple_of((1 - at) * half, 8), half), :].astype(jnp.bfloat16)
+
+
+def share_kernel(mine, other, stream, keep, send):
+    high = (lax.axis_index("tp") >> 1) == 1
+    group = keep.shape[0]
+    total = mine[...] + other[...].astype(jnp.float32)
+    lower, upper = total[:group], total[group:]
+    send[...] = jnp.where(high, lower, upper).astype(jnp.bfloat16)
+    total = total + stream[...]
+    keep[...] = jnp.where(high, total[group:], total[:group])
+
+
+def finish_kernel(mine, other, out):
+    out[...] = (mine[...] + other[...].astype(jnp.float32)).astype(jnp.bfloat16)
+
+
+def local_pairs(
+    resid,
+    query,
+    new_kv,
+    key_cache,
+    cached_value_rows,
+    cache_len,
+    assign,
+    out_weight,
+    norm_gain,
+    gate_weight,
+    up_weight,
+    down_weight,
+):
+    f32, bf16 = jnp.float32, jnp.bfloat16
+    group, features = resid.shape
+    per_device = key_cache.shape[0]
+    heads = query.shape[1] // HEAD_WIDTH
+    head_block = out_weight.shape[0]
+    width = gate_weight.shape[1]
+    half = 2 * group
+    assign = assign.reshape(1, -1)
+    gain = norm_gain.reshape(1, -1)
+
+    query_b, pairs_b = swap(query, "sec", 1), swap(new_kv, "sec", 1)
+    lines = 32 * per_device
+    mine, away = call(
+        functools.partial(pick_kernel, per_device, group, heads),
+        [((lines, HEAD_WIDTH), bf16)] * 2,
+        (query, new_kv, query_b, pairs_b, assign),
+        [pltpu.VMEM((2, lines, HEAD_WIDTH), f32)],
+    )
+    other = swap(away, "sec", 2)
+    mine, away = call(
+        functools.partial(attend_kernel, per_device, heads),
+        [((2, 4, head_block), bf16)] * 2,
+        (cache_len, mine, other, key_cache, cached_value_rows),
+        [pltpu.VMEM((2, 2, 8, head_block), f32)],
+        smem=(0,),
+        resident=(3, 4),
+    )
+
+    other = swap(away, "tp", 1)
+    (away,) = call(forward_kernel, [((2, 4, head_block), bf16)], (mine, other))
+    far = swap(away, "tp", 2)
+    (block,) = call(
+        gather_kernel, [((16, head_block), bf16)], (mine, other, far), [pltpu.VMEM((16, head_block), f32)]
+    )
+    blocks = [block] + [swap(block, "sec", step) for step in range(1, 4)]
+    mine, away = call(
+        functools.partial(project_kernel, per_device, group),
+        [((half, features), f32), ((half, features), bf16)],
+        (*blocks, assign, out_weight),
+        [pltpu.VMEM((2 * half, features), f32)],
+        resident=(5,),
+    )
+    other = swap(away, "tp", 1)
+    mine, away = call(
+        add_resid_kernel, [((half, features), f32), ((half, features), bf16)], (mine, other, resid)
+    )
+    other = swap(away, "tp", 2)
+    stream, mine = call(stream_kernel, [((half, features), f32), ((half, features), bf16)], (mine, other))
+    other = swap(mine, "tp", 1)
+
+    wide = (2, half, width + 128)
+    mine, away = call(
+        functools.partial(gate_up_kernel, min(512, width // 2)),
+        [(wide, f32), (wide, bf16)],
+        (mine, other, gain, gate_weight, up_weight),
+        [pltpu.VMEM((2, half, features), f32)],
+        resident=(3, 4),
+    )
+    other = swap(away, "sec", 1)
+    mine, away = call(pair_sum_kernel, [(wide[1:], f32), (wide[1:], bf16)], (mine, other))
+    other = swap(away, "sec", 2)
+    (hidden,) = call(
+        functools.partial(hidden_kernel, features * lax.axis_size("sec")), [((half, width // 2), bf16)], (mine, other)
+    )
+    across = swap(hidden, "sec", 2)
+    beside = swap(hidden, "sec", 1)
+    corner = swap(across, "sec", 1)
+    (before,) = call(down_first_kernel, [((2 * half, features), f32)], (hidden, beside, down_weight), resident=(2,))
+    mine, away = call(
+        down_second_kernel,
+        [((half, features), f32), ((half, features), bf16)],
+        (across, corner, before, down_weight),
+        [pltpu.VMEM((2 * half, features), f32)],
+        resident=(3,),
+    )
+    other = swap(away, "tp", 1)
+    mine, away = call(share_kernel, [((group, features), f32), ((group, features), bf16)], (mine, other, stream))
+    other = swap(away, "tp", 2)
+    (out,) = call(finish_kernel, [((group, features), bf16)], (mine, other))
+    return out
+
+
 def solution(mesh):
+    small = mesh.shape["sec"] == 4 and mesh.shape["tp"] == 4
     return jax.shard_map(
-        local,
+        local_pairs if small else local,
         mesh=mesh,
         in_specs=(
             P(("rep", "tp"), "sec"),

time: 121 us -> 88 us (0.73)
  matrix products: 26 us -> 0 us
  Pallas kernels: 0 us -> 13.4 us
  starting transfers between devices: 32.3 us -> 24.5 us
  other arithmetic: 7.29 us -> 0.01 us
  waiting for transfers between devices: 36.1 us -> 31.2 us
    dot_general x11 -> x0, matrix products: 26 us -> none  [the longest x1 6.68 us: local(): up_part = jnp.dot(piece, up_weight, preferred_element_type=jnp.float32)]
    unnamed x22 -> x28, local copies, waits for them, and re-layouts: 3.01 us -> 17.4 us
    pallas_call x0 -> x14, Pallas kernels: none -> 13.4 us  [call(): pl.pallas_call(kernel, out_shape=[jax.ShapeDtypeStruct(shape, dtype) for...]
    ppermute x30 -> x18, starting transfers between devices: 32.3 us -> 24.5 us  [swap(): return lax.ppermute(value, axis, [(i, i ^ step) for i in range(count)])]
    gather x5 -> x0, local copies, waits for them, and re-layouts: 6.96 us -> none  [the longest x2 4.43 us: local(): jnp.take(hidden, sec_index ^ lax.iota(jnp.int32, sec_count), axis=0)]
    concatenate x4 -> x0, local copies, waits for them, and re-layouts: 5.57 us -> none  [the longest x3 4.85 us: local(): jnp.concatenate([gate_part, up_part], axis=1).astype(jnp.bfloat16)]
    ppermute x30 -> x18, waiting for transfers between devices: 36.1 us -> 31.2 us  [swap(): return lax.ppermute(value, axis, [(i, i ^ step) for i in range(count)])]
    mul x2 -> x0, other arithmetic: 1.36 us -> none  [the longest x1 1.34 us: local(): hidden = gated_units(share * inverse, width)]
  transfers between devices with their start and end apart: 30 -> 18, of which waited for: 16 -> 15; matrix products, arithmetic and copies ran while one was open for 3% -> 1% of each run, Pallas kernels for 0% -> 1%
where the time goes in v2:
time: 88 us; the launch traced here: 87.6 us
  waiting for transfers between devices  31.2 us (35%)
  starting transfers between devices  24.5 us (28%)
  local copies, waits for them, and re-layouts  18.3 us (21%)
  Pallas kernels  13.4 us (15%)
    ppermute x18, waiting for transfers between devices, swap(): return lax.ppermute(value, axis, [(i, i ^ step) for i in range(count)])  31.2 us
    ppermute x18, starting transfers between devices, swap(): return lax.ppermute(value, axis, [(i, i ^ step) for i in range(count)])  24.5 us
    unnamed x28, local copies, waits for them, and re-layouts  17.4 us
    pallas_call x14, Pallas kernels, call(): pl.pallas_call(kernel, out_shape=[jax.ShapeDtypeStruct(shape, dtype) for...  13.4 us
  transfers between devices with their start and end apart: 18, of which 15 were waited for; matrix products, arithmetic and copies ran while one was open for 1% of the time, Pallas kernels for 1%

profile of v2, /device:TPU:0, one launch (start us, length us, event | category | flops | bytes accessed | tf_op | source)
XLA Modules:
  0.0 87.6 jit_solution(2926455859629949471)
XLA Ops:
  0.0 0.5 collective-permute-start
  0.5 0.1 collective-permute-start.1
  0.5 1.3 %collective-permute-done.1.pairs_b = bf16[12,512]{1,0:T(8,128)(2,1)S(1)} collective-permute-done((bf16[12,512]{1,0:T(8,128)(2,1)}, bf16[12,512]{1,0:T(8,128)(2,1)S(1)}, u32[]{:S(2)}, u32[]{:S(2)}) %collective-permute-start.1) | collective-permute-done | bytes 12320 | tf_op jit(solution)/shard_map/ppermute | solution.py:174
  1.8 0.0 collective-permute-done.query_b
  1.9 0.0 copy-start.5
  1.9 0.8 copy-done.5
  2.6 0.0 copy-start.7
  2.6 0.7 copy-done.7
  3.4 0.0 copy-start.8
  3.4 0.7 copy-done.8
  4.0 0.5 shard_map.118
  4.5 2.7 %collective-permute-start.2 = (bf16[96,128]{1,0:T(8,128)(2,1)S(1)}, bf16[96,128]{1,0:T(8,128)(2,1)S(1)}, u32[]{:S(2)}, u32[]{:S(2)}) collective-permute-start(bf16[96,128]{1,0:T(8,128)(2,1)S(1)} %get-tuple-element.24), channel_id=1, source_target_pairs={{0,8},{4,12},{8,0},{12,4},{1,9},{5,13},{9,1},{13,5},{2,10},{6,14},... | collective-permute-start | bytes 73736 | tf_op jit(solution)/shard_map/ppermute | solution.py:174
  7.2 1.8 %collective-permute-done.2.other = bf16[96,128]{1,0:T(8,128)(2,1)S(1)} collective-permute-done((bf16[96,128]{1,0:T(8,128)(2,1)S(1)}, bf16[96,128]{1,0:T(8,128)(2,1)S(1)}, u32[]{:S(2)}, u32[]{:S(2)}) %collective-permute-start.2) | collective-permute-done | bytes 24608 | tf_op jit(solution)/shard_map/ppermute | solution.py:174
  9.0 1.3 %copy-done.3 = bf16[3,224,1024]{2,1,0:T(8,128)(2,1)S(1)} copy-done((bf16[3,224,1024]{2,1,0:T(8,128)(2,1)S(1)}, bf16[3,224,1024]{2,1,0:T(8,128)(2,1)}, u32[]{:S(2)}) %copy-start.3) | copy-done | bytes 1376280
  10.4 1.3 %copy-done.4 = bf16[3,224,1024]{2,1,0:T(8,128)(2,1)S(1)} copy-done((bf16[3,224,1024]{2,1,0:T(8,128)(2,1)S(1)}, bf16[3,224,1024]{2,1,0:T(8,128)(2,1)}, u32[]{:S(2)}) %copy-start.4) | copy-done | bytes 1376280
  11.7 0.7 copy-done.10
  12.3 4.8 %shard_map.119 = (bf16[2,4,1280]{2,1,0:T(4,128)(2,1)S(1)}, bf16[2,4,1280]{2,1,0:T(4,128)(2,1)S(1)}) custom-call(s32[3]{0:T(128)S(1)} %copy-done.10, bf16[96,128]{1,0:T(8,128)(2,1)S(1)} %get-tuple-element.23.mine, bf16[96,128]{1,0:T(8,128)(2,1)S(1)} %collective-permute-done.2.other, bf16[3,224,1024]{2,1,0:T(8,128)(2,1)S(1)} %copy-done.3, ...), custom_call_target="tpu_custom_call" | custom-call | tf_op jit(solution)/shard_map/pallas_call | solution.py:157
  17.2 2.2 %collective-permute-start.3 = (bf16[2,4,1280]{2,1,0:T(4,128)(2,1)S(1)}, bf16[2,4,1280]{2,1,0:T(4,128)(2,1)S(1)}, u32[]{:S(2)}, u32[]{:S(2)}) collective-permute-start(bf16[2,4,1280]{2,1,0:T(4,128)(2,1)S(1)} %get-tuple-element.26), channel_id=1, source_target_pairs={{0,1},{1,0},{2,3},{3,2},{4,5},{5,4},{6,7},{7,6},{8,9},{9,8},{10,11... | collective-permute-start | bytes 61448 | tf_op jit(solution)/shard_map/ppermute | solution.py:174
  19.4 1.8 %collective-permute-done.3.other = bf16[2,4,1280]{2,1,0:T(4,128)(2,1)S(1)} collective-permute-done((bf16[2,4,1280]{2,1,0:T(4,128)(2,1)S(1)}, bf16[2,4,1280]{2,1,0:T(4,128)(2,1)S(1)}, u32[]{:S(2)}, u32[]{:S(2)}) %collective-permute-start.3) | collective-permute-done | bytes 20512 | tf_op jit(solution)/shard_map/ppermute | solution.py:174
  21.1 3.0 %collective-permute-start.4 = (bf16[2,4,1280]{2,1,0:T(4,128)(2,1)S(1)}, bf16[2,4,1280]{2,1,0:T(4,128)(2,1)S(1)}, u32[]{:S(2)}, u32[]{:S(2)}) collective-permute-start(bf16[2,4,1280]{2,1,0:T(4,128)(2,1)S(1)} %shard_map.120), channel_id=1, source_target_pairs={{0,2},{1,3},{2,0},{3,1},{4,6},{5,7},{6,4},{7,5},{8,10},{9,11},{10,... | collective-permute-start | bytes 61448 | tf_op jit(solution)/shard_map/ppermute | solution.py:174
  24.2 1.8 %collective-permute-done.4.far = bf16[2,4,1280]{2,1,0:T(4,128)(2,1)S(1)} collective-permute-done((bf16[2,4,1280]{2,1,0:T(4,128)(2,1)S(1)}, bf16[2,4,1280]{2,1,0:T(4,128)(2,1)S(1)}, u32[]{:S(2)}, u32[]{:S(2)}) %collective-permute-start.4) | collective-permute-done | bytes 20512 | tf_op jit(solution)/shard_map/ppermute | solution.py:174
  25.9 0.1 collective-permute-start.7
  26.0 1.9 %collective-permute-start.6 = (bf16[16,1280]{1,0:T(8,128)(2,1)S(1)}, bf16[16,1280]{1,0:T(8,128)(2,1)S(1)}, u32[]{:S(2)}, u32[]{:S(2)}) collective-permute-start(bf16[16,1280]{1,0:T(8,128)(2,1)S(1)} %shard_map.121.first), channel_id=1, source_target_pairs={{0,8},{4,12},{8,0},{12,4},{1,9},{5,13},{9,1},{13,5},{2,10},{6,14},... | collective-permute-start | bytes 122888 | tf_op jit(solution)/shard_map/ppermute | solution.py:174
  27.9 0.0 collective-permute-start.5
  28.0 1.6 %collective-permute-done.7.fourth = bf16[16,1280]{1,0:T(8,128)(2,1)S(1)} collective-permute-done((bf16[16,1280]{1,0:T(8,128)(2,1)S(1)}, bf16[16,1280]{1,0:T(8,128)(2,1)S(1)}, u32[]{:S(2)}, u32[]{:S(2)}) %collective-permute-start.7) | collective-permute-done | bytes 40992 | tf_op jit(solution)/shard_map/ppermute | solution.py:174
  29.6 0.7 collective-permute-done.6.third
  30.3 0.0 collective-permute-done.5.second
  30.3 1.9 %copy-done.2 = bf16[1280,1280]{1,0:T(8,128)(2,1)S(1)} copy-done((bf16[1280,1280]{1,0:T(8,128)(2,1)S(1)}, bf16[1280,1280]{1,0:T(8,128)(2,1)}, u32[]{:S(2)}) %copy-start.2) | copy-done | bytes 3276824
  32.2 0.7 copy-done.9
  32.9 0.9 %shard_map.122 = (f32[24,1280]{1,0:T(8,128)S(1)}, bf16[24,1280]{1,0:T(8,128)(2,1)S(1)}) custom-call(bf16[16,1280]{1,0:T(8,128)(2,1)S(1)} %shard_map.121.first, bf16[16,1280]{1,0:T(8,128)(2,1)S(1)} %collective-permute-done.5.second, bf16[16,1280]{1,0:T(8,128)(2,1)S(1)} %collective-permute-done.6.third, bf16[16,1280]{1,0:T(8,128)(2,1)S(1)} %collective-permute-done.7.fourth, ...), custom_call_target="tpu_custom_call" | custom-call | tf_op jit(solution)/shard_map/pallas_call | solution.py:157
  33.9 2.1 %collective-permute-start.8 = (bf16[24,1280]{1,0:T(8,128)(2,1)S(1)}, bf16[24,1280]{1,0:T(8,128)(2,1)S(1)}, u32[]{:S(2)}, u32[]{:S(2)}) collective-permute-start(bf16[24,1280]{1,0:T(8,128)(2,1)S(1)} %get-tuple-element.28), channel_id=1, source_target_pairs={{0,1},{1,0},{2,3},{3,2},{4,5},{5,4},{6,7},{7,6},{8,9},{9,8},{10,11... | collective-permute-start | bytes 184328 | tf_op jit(solution)/shard_map/ppermute | solution.py:174
  35.9 2.4 %collective-permute-done.8.other = bf16[24,1280]{1,0:T(8,128)(2,1)S(1)} collective-permute-done((bf16[24,1280]{1,0:T(8,128)(2,1)S(1)}, bf16[24,1280]{1,0:T(8,128)(2,1)S(1)}, u32[]{:S(2)}, u32[]{:S(2)}) %collective-permute-start.8) | collective-permute-done | bytes 61472 | tf_op jit(solution)/shard_map/ppermute | solution.py:174
  38.3 0.8 copy-done.6
  39.1 0.2 shard_map.123
  39.2 2.9 %collective-permute-start.9 = (bf16[24,1280]{1,0:T(8,128)(2,1)S(1)}, bf16[24,1280]{1,0:T(8,128)(2,1)S(1)}, u32[]{:S(2)}, u32[]{:S(2)}) collective-permute-start(bf16[24,1280]{1,0:T(8,128)(2,1)S(1)} %get-tuple-element.30), channel_id=1, source_target_pairs={{0,2},{1,3},{2,0},{3,1},{4,6},{5,7},{6,4},{7,5},{8,10},{9,11},{10,... | collective-permute-start | bytes 184328 | tf_op jit(solution)/shard_map/ppermute | solution.py:174
  42.1 2.3 %collective-permute-done.9.other = bf16[24,1280]{1,0:T(8,128)(2,1)S(1)} collective-permute-done((bf16[24,1280]{1,0:T(8,128)(2,1)S(1)}, bf16[24,1280]{1,0:T(8,128)(2,1)S(1)}, u32[]{:S(2)}, u32[]{:S(2)}) %collective-permute-start.9) | collective-permute-done | bytes 61472 | tf_op jit(solution)/shard_map/ppermute | solution.py:174
  44.5 1.8 %collective-permute-start.10 = (bf16[24,1280]{1,0:T(8,128)(2,1)S(1)}, bf16[24,1280]{1,0:T(8,128)(2,1)S(1)}, u32[]{:S(2)}, u32[]{:S(2)}) collective-permute-start(bf16[24,1280]{1,0:T(8,128)(2,1)S(1)} %get-tuple-element.31.mine), channel_id=1, source_target_pairs={{0,1},{1,0},{2,3},{3,2},{4,5},{5,4},{6,7},{7,6},{8,9},{9,8},{10,11... | collective-permute-start | bytes 184328 | tf_op jit(solution)/shard_map/ppermute | solution.py:174
  46.3 0.8 reshape.7.gain
  47.2 1.6 %collective-permute-done.10.other = bf16[24,1280]{1,0:T(8,128)(2,1)S(1)} collective-permute-done((bf16[24,1280]{1,0:T(8,128)(2,1)S(1)}, bf16[24,1280]{1,0:T(8,128)(2,1)S(1)}, u32[]{:S(2)}, u32[]{:S(2)}) %collective-permute-start.10) | collective-permute-done | bytes 61472 | tf_op jit(solution)/shard_map/ppermute | solution.py:174
  48.8 4.6 %copy-done = bf16[1280,4096]{1,0:T(8,128)(2,1)S(1)} copy-done((bf16[1280,4096]{1,0:T(8,128)(2,1)S(1)}, bf16[1280,4096]{1,0:T(8,128)(2,1)}, u32[]{:S(2)}) %copy-start) | copy-done | bytes 10485784
  53.4 4.0 %copy-done.1 = bf16[1280,4096]{1,0:T(8,128)(2,1)S(1)} copy-done((bf16[1280,4096]{1,0:T(8,128)(2,1)S(1)}, bf16[1280,4096]{1,0:T(8,128)(2,1)}, u32[]{:S(2)}) %copy-start.1) | copy-done | bytes 10485784
  57.4 3.8 %shard_map.125 = (f32[2,24,4224]{2,1,0:T(8,128)S(1)}, bf16[2,24,4224]{2,1,0:T(8,128)(2,1)S(1)}) custom-call(bf16[24,1280]{1,0:T(8,128)(2,1)S(1)} %get-tuple-element.31.mine, bf16[24,1280]{1,0:T(8,128)(2,1)S(1)} %collective-permute-done.10.other, bf16[1,1280]{1,0:T(2,128)(2,1)S(1)} %reshape.7.gain, bf16[1280,4096]{1,0:T(8,128)(2,1)S(1)} %copy-done, ...), custom_call_target="tpu_custom_call" | custom-call | tf_op jit(solution)/shard_map/pallas_call | solution.py:157
  61.1 0.1 collective-permute-start.11
  61.2 1.7 %collective-permute-done.11.other = bf16[2,24,4224]{2,1,0:T(8,128)(2,1)S(1)} collective-permute-done((bf16[2,24,4224]{2,1,0:T(8,128)(2,1)S(1)}, bf16[2,24,4224]{2,1,0:T(8,128)(2,1)S(1)}, u32[]{:S(2)}, u32[]{:S(2)}) %collective-permute-start.11) | collective-permute-done | bytes 405536 | tf_op jit(solution)/shard_map/ppermute | solution.py:174
  62.9 0.2 shard_map.126
  63.1 1.4 %collective-permute-start.12 = (bf16[24,4224]{1,0:T(8,128)(2,1)S(1)}, bf16[24,4224]{1,0:T(8,128)(2,1)S(1)}, u32[]{:S(2)}, u32[]{:S(2)}) collective-permute-start(bf16[24,4224]{1,0:T(8,128)(2,1)S(1)} %get-tuple-element.35), channel_id=1, source_target_pairs={{0,8},{4,12},{8,0},{12,4},{1,9},{5,13},{9,1},{13,5},{2,10},{6,14},... | collective-permute-start | bytes 608264 | tf_op jit(solution)/shard_map/ppermute | solution.py:174
  64.6 5.7 %collective-permute-done.12.other = bf16[24,4224]{1,0:T(8,128)(2,1)S(1)} collective-permute-done((bf16[24,4224]{1,0:T(8,128)(2,1)S(1)}, bf16[24,4224]{1,0:T(8,128)(2,1)S(1)}, u32[]{:S(2)}, u32[]{:S(2)}) %collective-permute-start.12) | collective-permute-done | bytes 202784 | tf_op jit(solution)/shard_map/ppermute | solution.py:174
  70.3 0.2 shard_map.127.mine
  70.5 1.5 %collective-permute-start.13 = (bf16[24,2048]{1,0:T(8,128)(2,1)S(1)}, bf16[24,2048]{1,0:T(8,128)(2,1)S(1)}, u32[]{:S(2)}, u32[]{:S(2)}) collective-permute-start(bf16[24,2048]{1,0:T(8,128)(2,1)S(1)} %shard_map.127.mine), channel_id=1, source_target_pairs={{0,8},{4,12},{8,0},{12,4},{1,9},{5,13},{9,1},{13,5},{2,10},{6,14},... | collective-permute-start | bytes 294920 | tf_op jit(solution)/shard_map/ppermute | solution.py:174
  72.0 0.0 collective-permute-start.15
  72.0 3.2 %collective-permute-done.13.mine = bf16[24,2048]{1,0:T(8,128)(2,1)S(1)} collective-permute-done((bf16[24,2048]{1,0:T(8,128)(2,1)S(1)}, bf16[24,2048]{1,0:T(8,128)(2,1)S(1)}, u32[]{:S(2)}, u32[]{:S(2)}) %collective-permute-start.13) | collective-permute-done | bytes 98336 | tf_op jit(solution)/shard_map/ppermute | solution.py:174
  75.2 0.0 collective-permute-start.14
  75.2 0.0 collective-permute-done.15.other
  75.2 0.0 slice-done
  75.2 0.0 slice-done.1
  75.2 0.0 slice-done.2
  75.2 1.0 %shard_map.128.before = f32[48,1280]{1,0:T(8,128)S(1)} custom-call(bf16[24,2048]{1,0:T(8,128)(2,1)S(1)} %shard_map.127.mine, bf16[24,2048]{1,0:T(8,128)(2,1)S(1)} %collective-permute-done.15.other, bf16[4096,1280]{1,0:T(8,128)(2,1)S(1)} %bitcast.2), custom_call_target="tpu_custom_call" | custom-call | tf_op jit(solution)/shard_map/pallas_call | solution.py:157
  76.2 0.2 collective-permute-done.14.other
  76.5 1.0 %shard_map.129 = (f32[24,1280]{1,0:T(8,128)S(1)}, bf16[24,1280]{1,0:T(8,128)(2,1)S(1)}) custom-call(bf16[24,2048]{1,0:T(8,128)(2,1)S(1)} %collective-permute-done.13.mine, bf16[24,2048]{1,0:T(8,128)(2,1)S(1)} %collective-permute-done.14.other, f32[48,1280]{1,0:T(8,128)S(1)} %shard_map.128.before, bf16[4096,1280]{1,0:T(8,128)(2,1)S(1)} %bitcast.2), custom_call_target="tpu_custom_call" | custom-call | tf_op jit(solution)/shard_map/pallas_call | solution.py:157
  77.5 1.2 %collective-permute-start.16 = (bf16[24,1280]{1,0:T(8,128)(2,1)S(1)}, bf16[24,1280]{1,0:T(8,128)(2,1)S(1)}, u32[]{:S(2)}, u32[]{:S(2)}) collective-permute-start(bf16[24,1280]{1,0:T(8,128)(2,1)S(1)} %get-tuple-element.37), channel_id=1, source_target_pairs={{0,1},{1,0},{2,3},{3,2},{4,5},{5,4},{6,7},{7,6},{8,9},{9,8},{10,11... | collective-permute-start | bytes 184328 | tf_op jit(solution)/shard_map/ppermute | solution.py:174
  78.7 3.1 %collective-permute-done.16.other = bf16[24,1280]{1,0:T(8,128)(2,1)S(1)} collective-permute-done((bf16[24,1280]{1,0:T(8,128)(2,1)S(1)}, bf16[24,1280]{1,0:T(8,128)(2,1)S(1)}, u32[]{:S(2)}, u32[]{:S(2)}) %collective-permute-start.16) | collective-permute-done | bytes 61472 | tf_op jit(solution)/shard_map/ppermute | solution.py:174
  81.9 3.1 %collective-permute-start.17 = (bf16[12,1280]{1,0:T(8,128)(2,1)S(1)}, bf16[12,1280]{1,0:T(8,128)(2,1)S(1)}, u32[]{:S(2)}, u32[]{:S(2)}) collective-permute-start(bf16[12,1280]{1,0:T(8,128)(2,1)S(1)} %get-tuple-element.40), channel_id=1, source_target_pairs={{0,2},{1,3},{2,0},{3,1},{4,6},{5,7},{6,4},{7,5},{8,10},{9,11},{10,... | collective-permute-start | bytes 92168 | tf_op jit(solution)/shard_map/ppermute | solution.py:174
  84.9 2.0 %collective-permute-done.17.other = bf16[12,1280]{1,0:T(8,128)(2,1)S(1)} collective-permute-done((bf16[12,1280]{1,0:T(8,128)(2,1)S(1)}, bf16[12,1280]{1,0:T(8,128)(2,1)S(1)}, u32[]{:S(2)}, u32[]{:S(2)}) %collective-permute-start.17) | collective-permute-done | bytes 30752 | tf_op jit(solution)/shard_map/ppermute | solution.py:174
  86.9 0.6 shard_map.131
  (16 shorter events, 0.1 us)
Async XLA Ops:
  0.0 1.9 %collective-permute-start = (bf16[12,1280]{1,0:T(8,128)(2,1)}, bf16[12,1280]{1,0:T(8,128)(2,1)S(1)}, u32[]{:S(2)}, u32[]{:S(2)}) collective-permute-start(bf16[12,1280]{1,0:T(8,128)(2,1)} %query_a.1), channel_id=1, source_target_pairs={{0,4},{4,0},{8,12},{12,8},{1,5},{5,1},{9,13},{13,9},{2,6},{6,2},{1... | collective-permute-start | bytes 92168 | tf_op jit(solution)/shard_map/ppermute | solution.py:174
  0.5 1.4 %collective-permute-start.1 = (bf16[12,512]{1,0:T(8,128)(2,1)}, bf16[12,512]{1,0:T(8,128)(2,1)S(1)}, u32[]{:S(2)}, u32[]{:S(2)}) collective-permute-start(bf16[12,512]{1,0:T(8,128)(2,1)} %pairs_a.1), channel_id=1, source_target_pairs={{0,4},{4,0},{8,12},{12,8},{1,5},{5,1},{9,13},{13,9},{2,6},{6,2},{1... | collective-permute-start | bytes 36872 | tf_op jit(solution)/shard_map/ppermute | solution.py:174
  1.9 0.8 copy-start.5
  2.6 0.7 copy-start.7
  3.4 0.7 copy-start.8
  4.5 4.5 %collective-permute-start.2 = (bf16[96,128]{1,0:T(8,128)(2,1)S(1)}, bf16[96,128]{1,0:T(8,128)(2,1)S(1)}, u32[]{:S(2)}, u32[]{:S(2)}) collective-permute-start(bf16[96,128]{1,0:T(8,128)(2,1)S(1)} %get-tuple-element.24), channel_id=1, source_target_pairs={{0,8},{4,12},{8,0},{12,4},{1,9},{5,13},{9,1},{13,5},{2,10},{6,14},... | collective-permute-start | bytes 73736 | tf_op jit(solution)/shard_map/ppermute | solution.py:174
  9.0 1.3 %copy-start.3 = (bf16[3,224,1024]{2,1,0:T(8,128)(2,1)S(1)}, bf16[3,224,1024]{2,1,0:T(8,128)(2,1)}, u32[]{:S(2)}) copy-start(bf16[3,224,1024]{2,1,0:T(8,128)(2,1)} %keys.1) | copy-start | bytes 4128772
  10.4 1.3 %copy-start.4 = (bf16[3,224,1024]{2,1,0:T(8,128)(2,1)S(1)}, bf16[3,224,1024]{2,1,0:T(8,128)(2,1)}, u32[]{:S(2)}) copy-start(bf16[3,224,1024]{2,1,0:T(8,128)(2,1)} %values.1) | copy-start | bytes 4128772
  11.7 0.7 copy-start.10
  17.2 3.9 %collective-permute-start.3 = (bf16[2,4,1280]{2,1,0:T(4,128)(2,1)S(1)}, bf16[2,4,1280]{2,1,0:T(4,128)(2,1)S(1)}, u32[]{:S(2)}, u32[]{:S(2)}) collective-permute-start(bf16[2,4,1280]{2,1,0:T(4,128)(2,1)S(1)} %get-tuple-element.26), channel_id=1, source_target_pairs={{0,1},{1,0},{2,3},{3,2},{4,5},{5,4},{6,7},{7,6},{8,9},{9,8},{10,11... | collective-permute-start | bytes 61448 | tf_op jit(solution)/shard_map/ppermute | solution.py:174
  21.1 4.8 %collective-permute-start.4 = (bf16[2,4,1280]{2,1,0:T(4,128)(2,1)S(1)}, bf16[2,4,1280]{2,1,0:T(4,128)(2,1)S(1)}, u32[]{:S(2)}, u32[]{:S(2)}) collective-permute-start(bf16[2,4,1280]{2,1,0:T(4,128)(2,1)S(1)} %shard_map.120), channel_id=1, source_target_pairs={{0,2},{1,3},{2,0},{3,1},{4,6},{5,7},{6,4},{7,5},{8,10},{9,11},{10,... | collective-permute-start | bytes 61448 | tf_op jit(solution)/shard_map/ppermute | solution.py:174
  25.9 3.6 %collective-permute-start.7 = (bf16[16,1280]{1,0:T(8,128)(2,1)S(1)}, bf16[16,1280]{1,0:T(8,128)(2,1)S(1)}, u32[]{:S(2)}, u32[]{:S(2)}) collective-permute-start(bf16[16,1280]{1,0:T(8,128)(2,1)S(1)} %shard_map.121.first), channel_id=1, source_target_pairs={{0,12},{4,8},{8,4},{12,0},{1,13},{5,9},{9,5},{13,1},{2,14},{6,10},... | collective-permute-start | bytes 122888 | tf_op jit(solution)/shard_map/ppermute | solution.py:174
  26.0 4.3 %collective-permute-start.6 = (bf16[16,1280]{1,0:T(8,128)(2,1)S(1)}, bf16[16,1280]{1,0:T(8,128)(2,1)S(1)}, u32[]{:S(2)}, u32[]{:S(2)}) collective-permute-start(bf16[16,1280]{1,0:T(8,128)(2,1)S(1)} %shard_map.121.first), channel_id=1, source_target_pairs={{0,8},{4,12},{8,0},{12,4},{1,9},{5,13},{9,1},{13,5},{2,10},{6,14},... | collective-permute-start | bytes 122888 | tf_op jit(solution)/shard_map/ppermute | solution.py:174
  27.9 2.4 %collective-permute-start.5 = (bf16[16,1280]{1,0:T(8,128)(2,1)S(1)}, bf16[16,1280]{1,0:T(8,128)(2,1)S(1)}, u32[]{:S(2)}, u32[]{:S(2)}) collective-permute-start(bf16[16,1280]{1,0:T(8,128)(2,1)S(1)} %shard_map.121.first), channel_id=1, source_target_pairs={{0,4},{4,0},{8,12},{12,8},{1,5},{5,1},{9,13},{13,9},{2,6},{6,2},{1... | collective-permute-start | bytes 122888 | tf_op jit(solution)/shard_map/ppermute | solution.py:174
  30.3 1.9 %copy-start.2 = (bf16[1280,1280]{1,0:T(8,128)(2,1)S(1)}, bf16[1280,1280]{1,0:T(8,128)(2,1)}, u32[]{:S(2)}) copy-start(bf16[1280,1280]{1,0:T(8,128)(2,1)} %weight.3) | copy-start | bytes 9830404
  32.2 0.7 copy-start.9
  33.9 4.5 %collective-permute-start.8 = (bf16[24,1280]{1,0:T(8,128)(2,1)S(1)}, bf16[24,1280]{1,0:T(8,128)(2,1)S(1)}, u32[]{:S(2)}, u32[]{:S(2)}) collective-permute-start(bf16[24,1280]{1,0:T(8,128)(2,1)S(1)} %get-tuple-element.28), channel_id=1, source_target_pairs={{0,1},{1,0},{2,3},{3,2},{4,5},{5,4},{6,7},{7,6},{8,9},{9,8},{10,11... | collective-permute-start | bytes 184328 | tf_op jit(solution)/shard_map/ppermute | solution.py:174
  38.3 0.8 copy-start.6
  39.2 5.2 %collective-permute-start.9 = (bf16[24,1280]{1,0:T(8,128)(2,1)S(1)}, bf16[24,1280]{1,0:T(8,128)(2,1)S(1)}, u32[]{:S(2)}, u32[]{:S(2)}) collective-permute-start(bf16[24,1280]{1,0:T(8,128)(2,1)S(1)} %get-tuple-element.30), channel_id=1, source_target_pairs={{0,2},{1,3},{2,0},{3,1},{4,6},{5,7},{6,4},{7,5},{8,10},{9,11},{10,... | collective-permute-start | bytes 184328 | tf_op jit(solution)/shard_map/ppermute | solution.py:174
  44.5 4.3 %collective-permute-start.10 = (bf16[24,1280]{1,0:T(8,128)(2,1)S(1)}, bf16[24,1280]{1,0:T(8,128)(2,1)S(1)}, u32[]{:S(2)}, u32[]{:S(2)}) collective-permute-start(bf16[24,1280]{1,0:T(8,128)(2,1)S(1)} %get-tuple-element.31.mine), channel_id=1, source_target_pairs={{0,1},{1,0},{2,3},{3,2},{4,5},{5,4},{6,7},{7,6},{8,9},{9,8},{10,11... | collective-permute-start | bytes 184328 | tf_op jit(solution)/shard_map/ppermute | solution.py:174
  46.3 28.8 %slice-start = ((s8[10485760]{0:T(1024)(128)(4,1)}), s8[4194304]{0:T(1024)(128)(4,1)S(1)}, s32[]{:S(2)}) async-start(s8[10485760]{0:T(1024)(128)(4,1)} %bitcast.1), calls=%async_computation | async-start | bytes 8388608
  47.2 28.0 %slice-start.1 = ((s8[10485760]{0:T(1024)(128)(4,1)}), s8[4194304]{0:T(1024)(128)(4,1)S(1)}, s32[]{:S(2)}) async-start(s8[10485760]{0:T(1024)(128)(4,1)} %bitcast.1), calls=%async_computation.1 | async-start | bytes 8388608
  47.2 28.0 %slice-start.2 = ((s8[10485760]{0:T(1024)(128)(4,1)}), s8[2097152]{0:T(1024)(128)(4,1)S(1)}, s32[]{:S(2)}) async-start(s8[10485760]{0:T(1024)(128)(4,1)} %bitcast.1), calls=%async_computation.2 | async-start | bytes 4194304
  48.8 4.6 %copy-start = (bf16[1280,4096]{1,0:T(8,128)(2,1)S(1)}, bf16[1280,4096]{1,0:T(8,128)(2,1)}, u32[]{:S(2)}) copy-start(bf16[1280,4096]{1,0:T(8,128)(2,1)} %gate.1) | copy-start | bytes 31457284
  53.4 4.0 %copy-start.1 = (bf16[1280,4096]{1,0:T(8,128)(2,1)S(1)}, bf16[1280,4096]{1,0:T(8,128)(2,1)}, u32[]{:S(2)}) copy-start(bf16[1280,4096]{1,0:T(8,128)(2,1)} %up.1) | copy-start | bytes 31457284
  61.1 1.8 %collective-permute-start.11 = (bf16[2,24,4224]{2,1,0:T(8,128)(2,1)S(1)}, bf16[2,24,4224]{2,1,0:T(8,128)(2,1)S(1)}, u32[]{:S(2)}, u32[]{:S(2)}) collective-permute-start(bf16[2,24,4224]{2,1,0:T(8,128)(2,1)S(1)} %get-tuple-element.33), channel_id=1, source_target_pairs={{0,4},{4,0},{8,12},{12,8},{1,5},{5,1},{9,13},{13,9},{2,6},{6,2},{1... | collective-permute-start | bytes 1216520 | tf_op jit(solution)/shard_map/ppermute | solution.py:174
  63.1 7.1 %collective-permute-start.12 = (bf16[24,4224]{1,0:T(8,128)(2,1)S(1)}, bf16[24,4224]{1,0:T(8,128)(2,1)S(1)}, u32[]{:S(2)}, u32[]{:S(2)}) collective-permute-start(bf16[24,4224]{1,0:T(8,128)(2,1)S(1)} %get-tuple-element.35), channel_id=1, source_target_pairs={{0,8},{4,12},{8,0},{12,4},{1,9},{5,13},{9,1},{13,5},{2,10},{6,14},... | collective-permute-start | bytes 608264 | tf_op jit(solution)/shard_map/ppermute | solution.py:174
  70.5 4.7 %collective-permute-start.13 = (bf16[24,2048]{1,0:T(8,128)(2,1)S(1)}, bf16[24,2048]{1,0:T(8,128)(2,1)S(1)}, u32[]{:S(2)}, u32[]{:S(2)}) collective-permute-start(bf16[24,2048]{1,0:T(8,128)(2,1)S(1)} %shard_map.127.mine), channel_id=1, source_target_pairs={{0,8},{4,12},{8,0},{12,4},{1,9},{5,13},{9,1},{13,5},{2,10},{6,14},... | collective-permute-start | bytes 294920 | tf_op jit(solution)/shard_map/ppermute | solution.py:174
  72.0 3.2 %collective-permute-start.15 = (bf16[24,2048]{1,0:T(8,128)(2,1)S(1)}, bf16[24,2048]{1,0:T(8,128)(2,1)S(1)}, u32[]{:S(2)}, u32[]{:S(2)}) collective-permute-start(bf16[24,2048]{1,0:T(8,128)(2,1)S(1)} %shard_map.127.mine), channel_id=1, source_target_pairs={{0,4},{4,0},{8,12},{12,8},{1,5},{5,1},{9,13},{13,9},{2,6},{6,2},{1... | collective-permute-start | bytes 294920 | tf_op jit(solution)/shard_map/ppermute | solution.py:174
  75.2 1.3 %collective-permute-start.14 = (bf16[24,2048]{1,0:T(8,128)(2,1)S(1)}, bf16[24,2048]{1,0:T(8,128)(2,1)S(1)}, u32[]{:S(2)}, u32[]{:S(2)}) collective-permute-start(bf16[24,2048]{1,0:T(8,128)(2,1)S(1)} %collective-permute-done.13.mine), channel_id=1, source_target_pairs={{0,4},{4,0},{8,12},{12,8},{1,5},{5,1},{9,13},{13,9},{2,6},{6,2},{1... | collective-permute-start | bytes 294920 | tf_op jit(solution)/shard_map/ppermute | solution.py:174
  77.5 4.3 %collective-permute-start.16 = (bf16[24,1280]{1,0:T(8,128)(2,1)S(1)}, bf16[24,1280]{1,0:T(8,128)(2,1)S(1)}, u32[]{:S(2)}, u32[]{:S(2)}) collective-permute-start(bf16[24,1280]{1,0:T(8,128)(2,1)S(1)} %get-tuple-element.37), channel_id=1, source_target_pairs={{0,1},{1,0},{2,3},{3,2},{4,5},{5,4},{6,7},{7,6},{8,9},{9,8},{10,11... | collective-permute-start | bytes 184328 | tf_op jit(solution)/shard_map/ppermute | solution.py:174
  81.9 5.1 %collective-permute-start.17 = (bf16[12,1280]{1,0:T(8,128)(2,1)S(1)}, bf16[12,1280]{1,0:T(8,128)(2,1)S(1)}, u32[]{:S(2)}, u32[]{:S(2)}) collective-permute-start(bf16[12,1280]{1,0:T(8,128)(2,1)S(1)} %get-tuple-element.40), channel_id=1, source_target_pairs={{0,2},{1,3},{2,0},{3,1},{4,6},{5,7},{6,4},{7,5},{8,10},{9,11},{10,... | collective-permute-start | bytes 92168 | tf_op jit(solution)/shard_map/ppermute | solution.py:174

commit v3 on v2

--- a/solution.py
+++ b/solution.py
@@ -147,7 +147,7 @@
 MIB = 1024 * 1024
 
 
-def call(kernel, outs, operands, scratch=(), smem=(), resident=(), flops=0, moved=0, limit=8):
+def call(kernel, outs, operands, scratch=(), smem=(), resident=(), micros=4, limit=8):
     specs = []
     placed = []
     for place, operand in enumerate(operands):
@@ -161,7 +161,7 @@
         out_specs=[pl.BlockSpec(memory_space=pltpu.VMEM) for _ in outs],
         scratch_shapes=list(scratch),
         compiler_params=pltpu.CompilerParams(vmem_limit_bytes=limit * MIB),
-        cost_estimate=pl.CostEstimate(flops=flops, bytes_accessed=moved, transcendentals=0),
+        cost_estimate=pl.CostEstimate(flops=micros * 10**9, bytes_accessed=0, transcendentals=0),
     )(*placed)
 
 

time: 88 us -> 72.9 us (0.83)
  local copies, waits for them, and re-layouts: 18.3 us -> 2.22 us
  starting transfers between devices: 24.5 us -> 25.6 us
    unnamed x28 -> x38, local copies, waits for them, and re-layouts: 17.4 us -> 2.22 us
    ppermute x18, starting transfers between devices: 24.5 us -> 25.6 us  [swap(): return lax.ppermute(value, axis, [(i, i ^ step) for i in range(count)])]
  transfers between devices with their start and end apart: 18 -> 18, of which waited for: 15 -> 15; matrix products, arithmetic and copies ran while one was open for 1% -> 0% of each run, Pallas kernels for 1% -> 1%
where the time goes in v3:
time: 72.9 us; the launch traced here: 72.7 us
  waiting for transfers between devices  31.2 us (43%)
  starting transfers between devices  25.6 us (35%)
  Pallas kernels  13.4 us (18%)
  local copies, waits for them, and re-layouts  2.22 us (3%)
    ppermute x18, waiting for transfers between devices, swap(): return lax.ppermute(value, axis, [(i, i ^ step) for i in range(count)])  31.2 us
    ppermute x18, starting transfers between devices, swap(): return lax.ppermute(value, axis, [(i, i ^ step) for i in range(count)])  25.6 us
    pallas_call x14, Pallas kernels, call(): pl.pallas_call(kernel, out_shape=[jax.ShapeDtypeStruct(shape, dtype) for...  13.4 us
    unnamed x38, local copies, waits for them, and re-layouts  2.22 us
  transfers between devices with their start and end apart: 18, of which 15 were waited for; matrix products, arithmetic and copies ran while one was open for 0% of the time, Pallas kernels for 1%

profile of v3, /device:TPU:0, one launch (start us, length us, event | category | flops | bytes accessed | tf_op | source)
XLA Modules:
  0.0 72.7 jit_solution(10595184602722221498)
XLA Ops:
  0.0 0.5 collective-permute-start
  0.5 0.1 collective-permute-start.1
  0.5 1.3 %collective-permute-done.1.pairs_b = bf16[12,512]{1,0:T(8,128)(2,1)S(1)} collective-permute-done((bf16[12,512]{1,0:T(8,128)(2,1)}, bf16[12,512]{1,0:T(8,128)(2,1)S(1)}, u32[]{:S(2)}, u32[]{:S(2)}) %collective-permute-start.1) | collective-permute-done | bytes 12320 | tf_op jit(solution)/shard_map/ppermute | solution.py:174
  1.9 0.0 collective-permute-done.query_b
  1.9 0.8 %copy-done.3 = bf16[12,1280]{1,0:T(8,128)(2,1)S(1)} copy-done((bf16[12,1280]{1,0:T(8,128)(2,1)S(1)}, bf16[12,1280]{1,0:T(8,128)(2,1)}, u32[]{:S(2)}) %copy-start.3) | copy-done | bytes 30744
  2.6 0.7 copy-done.5
  3.4 0.7 copy-done.7
  4.0 0.5 shard_map.118
  4.5 2.7 %collective-permute-start.2 = (bf16[96,128]{1,0:T(8,128)(2,1)S(1)}, bf16[96,128]{1,0:T(8,128)(2,1)S(1)}, u32[]{:S(2)}, u32[]{:S(2)}) collective-permute-start(bf16[96,128]{1,0:T(8,128)(2,1)S(1)} %get-tuple-element.24), channel_id=1, source_target_pairs={{0,8},{4,12},{8,0},{12,4},{1,9},{5,13},{9,1},{13,5},{2,10},{6,14},... | collective-permute-start | bytes 73736 | tf_op jit(solution)/shard_map/ppermute | solution.py:174
  7.2 1.8 %collective-permute-done.2.other = bf16[96,128]{1,0:T(8,128)(2,1)S(1)} collective-permute-done((bf16[96,128]{1,0:T(8,128)(2,1)S(1)}, bf16[96,128]{1,0:T(8,128)(2,1)S(1)}, u32[]{:S(2)}, u32[]{:S(2)}) %collective-permute-start.2) | collective-permute-done | bytes 24608 | tf_op jit(solution)/shard_map/ppermute | solution.py:174
  9.0 0.0 copy-done.2
  9.0 0.0 copy-done.1
  9.0 0.0 copy-done.6
  9.0 4.8 %shard_map.119 = (bf16[2,4,1280]{2,1,0:T(4,128)(2,1)S(1)}, bf16[2,4,1280]{2,1,0:T(4,128)(2,1)S(1)}) custom-call(s32[3]{0:T(128)S(1)} %copy-done.6, bf16[96,128]{1,0:T(8,128)(2,1)S(1)} %get-tuple-element.23.mine, bf16[96,128]{1,0:T(8,128)(2,1)S(1)} %collective-permute-done.2.other, bf16[3,224,1024]{2,1,0:T(8,128)(2,1)S(1)} %copy-done.1, ...), custom_call_target="tpu_custom_call" | custom-call | flops 4000000000 | tf_op jit(solution)/shard_map/pallas_call | solution.py:157
  13.9 2.2 %collective-permute-start.3 = (bf16[2,4,1280]{2,1,0:T(4,128)(2,1)S(1)}, bf16[2,4,1280]{2,1,0:T(4,128)(2,1)S(1)}, u32[]{:S(2)}, u32[]{:S(2)}) collective-permute-start(bf16[2,4,1280]{2,1,0:T(4,128)(2,1)S(1)} %get-tuple-element.26), channel_id=1, source_target_pairs={{0,1},{1,0},{2,3},{3,2},{4,5},{5,4},{6,7},{7,6},{8,9},{9,8},{10,11... | collective-permute-start | bytes 61448 | tf_op jit(solution)/shard_map/ppermute | solution.py:174
  16.0 1.8 %collective-permute-done.3.other = bf16[2,4,1280]{2,1,0:T(4,128)(2,1)S(1)} collective-permute-done((bf16[2,4,1280]{2,1,0:T(4,128)(2,1)S(1)}, bf16[2,4,1280]{2,1,0:T(4,128)(2,1)S(1)}, u32[]{:S(2)}, u32[]{:S(2)}) %collective-permute-start.3) | collective-permute-done | bytes 20512 | tf_op jit(solution)/shard_map/ppermute | solution.py:174
  17.8 3.1 %collective-permute-start.4 = (bf16[2,4,1280]{2,1,0:T(4,128)(2,1)S(1)}, bf16[2,4,1280]{2,1,0:T(4,128)(2,1)S(1)}, u32[]{:S(2)}, u32[]{:S(2)}) collective-permute-start(bf16[2,4,1280]{2,1,0:T(4,128)(2,1)S(1)} %shard_map.120), channel_id=1, source_target_pairs={{0,2},{1,3},{2,0},{3,1},{4,6},{5,7},{6,4},{7,5},{8,10},{9,11},{10,... | collective-permute-start | bytes 61448 | tf_op jit(solution)/shard_map/ppermute | solution.py:174
  20.9 1.8 %collective-permute-done.4.far = bf16[2,4,1280]{2,1,0:T(4,128)(2,1)S(1)} collective-permute-done((bf16[2,4,1280]{2,1,0:T(4,128)(2,1)S(1)}, bf16[2,4,1280]{2,1,0:T(4,128)(2,1)S(1)}, u32[]{:S(2)}, u32[]{:S(2)}) %collective-permute-start.4) | collective-permute-done | bytes 20512 | tf_op jit(solution)/shard_map/ppermute | solution.py:174
  22.7 0.0 copy-start.4
  22.7 0.1 collective-permute-start.7
  22.8 1.9 %collective-permute-start.6 = (bf16[16,1280]{1,0:T(8,128)(2,1)S(1)}, bf16[16,1280]{1,0:T(8,128)(2,1)S(1)}, u32[]{:S(2)}, u32[]{:S(2)}) collective-permute-start(bf16[16,1280]{1,0:T(8,128)(2,1)S(1)} %shard_map.121.first), channel_id=1, source_target_pairs={{0,8},{4,12},{8,0},{12,4},{1,9},{5,13},{9,1},{13,5},{2,10},{6,14},... | collective-permute-start | bytes 122888 | tf_op jit(solution)/shard_map/ppermute | solution.py:174
  24.7 0.0 collective-permute-start.5
  24.7 1.6 %collective-permute-done.7.fourth = bf16[16,1280]{1,0:T(8,128)(2,1)S(1)} collective-permute-done((bf16[16,1280]{1,0:T(8,128)(2,1)S(1)}, bf16[16,1280]{1,0:T(8,128)(2,1)S(1)}, u32[]{:S(2)}, u32[]{:S(2)}) %collective-permute-start.7) | collective-permute-done | bytes 40992 | tf_op jit(solution)/shard_map/ppermute | solution.py:174
  26.3 0.7 %collective-permute-done.6.third = bf16[16,1280]{1,0:T(8,128)(2,1)S(1)} collective-permute-done((bf16[16,1280]{1,0:T(8,128)(2,1)S(1)}, bf16[16,1280]{1,0:T(8,128)(2,1)S(1)}, u32[]{:S(2)}, u32[]{:S(2)}) %collective-permute-start.6) | collective-permute-done | bytes 40992 | tf_op jit(solution)/shard_map/ppermute | solution.py:174
  27.1 0.0 collective-permute-done.5.second
  27.1 0.0 copy-done
  27.1 0.0 copy-done.8
  27.1 0.9 %shard_map.122 = (f32[24,1280]{1,0:T(8,128)S(1)}, bf16[24,1280]{1,0:T(8,128)(2,1)S(1)}) custom-call(bf16[16,1280]{1,0:T(8,128)(2,1)S(1)} %shard_map.121.first, bf16[16,1280]{1,0:T(8,128)(2,1)S(1)} %collective-permute-done.5.second, bf16[16,1280]{1,0:T(8,128)(2,1)S(1)} %collective-permute-done.6.third, bf16[16,1280]{1,0:T(8,128)(2,1)S(1)} %collective-permute-done.7.fourth, ...), custom_call_target="tpu_custom_call" | custom-call | flops 4000000000 | tf_op jit(solution)/shard_map/pallas_call | solution.py:157
  28.0 2.0 %collective-permute-start.8 = (bf16[24,1280]{1,0:T(8,128)(2,1)S(1)}, bf16[24,1280]{1,0:T(8,128)(2,1)S(1)}, u32[]{:S(2)}, u32[]{:S(2)}) collective-permute-start(bf16[24,1280]{1,0:T(8,128)(2,1)S(1)} %get-tuple-element.28), channel_id=1, source_target_pairs={{0,1},{1,0},{2,3},{3,2},{4,5},{5,4},{6,7},{7,6},{8,9},{9,8},{10,11... | collective-permute-start | bytes 184328 | tf_op jit(solution)/shard_map/ppermute | solution.py:174
  30.1 2.4 %collective-permute-done.8.other = bf16[24,1280]{1,0:T(8,128)(2,1)S(1)} collective-permute-done((bf16[24,1280]{1,0:T(8,128)(2,1)S(1)}, bf16[24,1280]{1,0:T(8,128)(2,1)S(1)}, u32[]{:S(2)}, u32[]{:S(2)}) %collective-permute-start.8) | collective-permute-done | bytes 61472 | tf_op jit(solution)/shard_map/ppermute | solution.py:174
  32.5 0.0 copy-done.4
  32.5 0.0 slice-start.4
  32.5 0.2 shard_map.123
  32.7 0.0 copy-start.9
  32.7 2.9 %collective-permute-start.9 = (bf16[24,1280]{1,0:T(8,128)(2,1)S(1)}, bf16[24,1280]{1,0:T(8,128)(2,1)S(1)}, u32[]{:S(2)}, u32[]{:S(2)}) collective-permute-start(bf16[24,1280]{1,0:T(8,128)(2,1)S(1)} %get-tuple-element.30), channel_id=1, source_target_pairs={{0,2},{1,3},{2,0},{3,1},{4,6},{5,7},{6,4},{7,5},{8,10},{9,11},{10,... | collective-permute-start | bytes 184328 | tf_op jit(solution)/shard_map/ppermute | solution.py:174
  35.6 2.3 %collective-permute-done.9.other = bf16[24,1280]{1,0:T(8,128)(2,1)S(1)} collective-permute-done((bf16[24,1280]{1,0:T(8,128)(2,1)S(1)}, bf16[24,1280]{1,0:T(8,128)(2,1)S(1)}, u32[]{:S(2)}, u32[]{:S(2)}) %collective-permute-start.9) | collective-permute-done | bytes 61472 | tf_op jit(solution)/shard_map/ppermute | solution.py:174
  38.0 1.8 %collective-permute-start.10 = (bf16[24,1280]{1,0:T(8,128)(2,1)S(1)}, bf16[24,1280]{1,0:T(8,128)(2,1)S(1)}, u32[]{:S(2)}, u32[]{:S(2)}) collective-permute-start(bf16[24,1280]{1,0:T(8,128)(2,1)S(1)} %get-tuple-element.31.mine), channel_id=1, source_target_pairs={{0,1},{1,0},{2,3},{3,2},{4,5},{5,4},{6,7},{7,6},{8,9},{9,8},{10,11... | collective-permute-start | bytes 184328 | tf_op jit(solution)/shard_map/ppermute | solution.py:174
  39.8 0.0 copy-done.9
  39.8 2.5 %collective-permute-done.10.other = bf16[24,1280]{1,0:T(8,128)(2,1)S(1)} collective-permute-done((bf16[24,1280]{1,0:T(8,128)(2,1)S(1)}, bf16[24,1280]{1,0:T(8,128)(2,1)S(1)}, u32[]{:S(2)}, u32[]{:S(2)}) %collective-permute-start.10) | collective-permute-done | bytes 61472 | tf_op jit(solution)/shard_map/ppermute | solution.py:174
  42.3 0.0 slice-done.4
  42.3 0.0 slice-done.2
  42.3 0.0 slice-done.5
  42.3 3.8 %shard_map.125 = (f32[2,24,4224]{2,1,0:T(8,128)S(1)}, bf16[2,24,4224]{2,1,0:T(8,128)(2,1)S(1)}) custom-call(bf16[24,1280]{1,0:T(8,128)(2,1)S(1)} %get-tuple-element.31.mine, bf16[24,1280]{1,0:T(8,128)(2,1)S(1)} %collective-permute-done.10.other, bf16[1,1280]{1,0:T(2,128)(2,1)S(1)} %reshape.7.gain, bf16[1280,4096]{1,0:T(8,128)(2,1)S(1)} %bitcast.2, ...), custom_call_target="tpu_custom_call" | custom-call | flops 4000000000 | tf_op jit(solution)/shard_map/pallas_call | solution.py:157
  46.1 0.1 collective-permute-start.11
  46.2 1.7 %collective-permute-done.11.other = bf16[2,24,4224]{2,1,0:T(8,128)(2,1)S(1)} collective-permute-done((bf16[2,24,4224]{2,1,0:T(8,128)(2,1)S(1)}, bf16[2,24,4224]{2,1,0:T(8,128)(2,1)S(1)}, u32[]{:S(2)}, u32[]{:S(2)}) %collective-permute-start.11) | collective-permute-done | bytes 405536 | tf_op jit(solution)/shard_map/ppermute | solution.py:174
  47.9 0.2 shard_map.126
  48.1 1.6 %collective-permute-start.12 = (bf16[24,4224]{1,0:T(8,128)(2,1)S(1)}, bf16[24,4224]{1,0:T(8,128)(2,1)S(1)}, u32[]{:S(2)}, u32[]{:S(2)}) collective-permute-start(bf16[24,4224]{1,0:T(8,128)(2,1)S(1)} %get-tuple-element.35), channel_id=1, source_target_pairs={{0,8},{4,12},{8,0},{12,4},{1,9},{5,13},{9,1},{13,5},{2,10},{6,14},... | collective-permute-start | bytes 608264 | tf_op jit(solution)/shard_map/ppermute | solution.py:174
  49.7 5.5 %collective-permute-done.12.other = bf16[24,4224]{1,0:T(8,128)(2,1)S(1)} collective-permute-done((bf16[24,4224]{1,0:T(8,128)(2,1)S(1)}, bf16[24,4224]{1,0:T(8,128)(2,1)S(1)}, u32[]{:S(2)}, u32[]{:S(2)}) %collective-permute-start.12) | collective-permute-done | bytes 202784 | tf_op jit(solution)/shard_map/ppermute | solution.py:174
  55.2 0.2 shard_map.127.mine
  55.4 1.7 %collective-permute-start.13 = (bf16[24,2048]{1,0:T(8,128)(2,1)S(1)}, bf16[24,2048]{1,0:T(8,128)(2,1)S(1)}, u32[]{:S(2)}, u32[]{:S(2)}) collective-permute-start(bf16[24,2048]{1,0:T(8,128)(2,1)S(1)} %shard_map.127.mine), channel_id=1, source_target_pairs={{0,8},{4,12},{8,0},{12,4},{1,9},{5,13},{9,1},{13,5},{2,10},{6,14},... | collective-permute-start | bytes 294920 | tf_op jit(solution)/shard_map/ppermute | solution.py:174
  57.1 0.0 collective-permute-start.15
  57.1 3.0 %collective-permute-done.13.mine = bf16[24,2048]{1,0:T(8,128)(2,1)S(1)} collective-permute-done((bf16[24,2048]{1,0:T(8,128)(2,1)S(1)}, bf16[24,2048]{1,0:T(8,128)(2,1)S(1)}, u32[]{:S(2)}, u32[]{:S(2)}) %collective-permute-start.13) | collective-permute-done | bytes 98336 | tf_op jit(solution)/shard_map/ppermute | solution.py:174
  60.1 0.0 collective-permute-start.14
  60.1 0.0 collective-permute-done.15.other
  60.1 0.0 slice-done.7
  60.1 0.0 slice-done.8
  60.2 1.0 %shard_map.128.before = f32[48,1280]{1,0:T(8,128)S(1)} custom-call(bf16[24,2048]{1,0:T(8,128)(2,1)S(1)} %shard_map.127.mine, bf16[24,2048]{1,0:T(8,128)(2,1)S(1)} %collective-permute-done.15.other, bf16[4096,1280]{1,0:T(8,128)(2,1)S(1)} %bitcast.6), custom_call_target="tpu_custom_call" | custom-call | flops 4000000000 | tf_op jit(solution)/shard_map/pallas_call | solution.py:157
  61.2 0.2 collective-permute-done.14.other
  61.4 1.0 %shard_map.129 = (f32[24,1280]{1,0:T(8,128)S(1)}, bf16[24,1280]{1,0:T(8,128)(2,1)S(1)}) custom-call(bf16[24,2048]{1,0:T(8,128)(2,1)S(1)} %collective-permute-done.13.mine, bf16[24,2048]{1,0:T(8,128)(2,1)S(1)} %collective-permute-done.14.other, f32[48,1280]{1,0:T(8,128)S(1)} %shard_map.128.before, bf16[4096,1280]{1,0:T(8,128)(2,1)S(1)} %bitcast.6), custom_call_target="tpu_custom_call" | custom-call | flops 4000000000 | tf_op jit(solution)/shard_map/pallas_call | solution.py:157
  62.5 1.8 %collective-permute-start.16 = (bf16[24,1280]{1,0:T(8,128)(2,1)S(1)}, bf16[24,1280]{1,0:T(8,128)(2,1)S(1)}, u32[]{:S(2)}, u32[]{:S(2)}) collective-permute-start(bf16[24,1280]{1,0:T(8,128)(2,1)S(1)} %get-tuple-element.37), channel_id=1, source_target_pairs={{0,1},{1,0},{2,3},{3,2},{4,5},{5,4},{6,7},{7,6},{8,9},{9,8},{10,11... | collective-permute-start | bytes 184328 | tf_op jit(solution)/shard_map/ppermute | solution.py:174
  64.3 2.5 %collective-permute-done.16.other = bf16[24,1280]{1,0:T(8,128)(2,1)S(1)} collective-permute-done((bf16[24,1280]{1,0:T(8,128)(2,1)S(1)}, bf16[24,1280]{1,0:T(8,128)(2,1)S(1)}, u32[]{:S(2)}, u32[]{:S(2)}) %collective-permute-start.16) | collective-permute-done | bytes 61472 | tf_op jit(solution)/shard_map/ppermute | solution.py:174
  66.8 3.2 %collective-permute-start.17 = (bf16[12,1280]{1,0:T(8,128)(2,1)S(1)}, bf16[12,1280]{1,0:T(8,128)(2,1)S(1)}, u32[]{:S(2)}, u32[]{:S(2)}) collective-permute-start(bf16[12,1280]{1,0:T(8,128)(2,1)S(1)} %get-tuple-element.40), channel_id=1, source_target_pairs={{0,2},{1,3},{2,0},{3,1},{4,6},{5,7},{6,4},{7,5},{8,10},{9,11},{10,... | collective-permute-start | bytes 92168 | tf_op jit(solution)/shard_map/ppermute | solution.py:174
  70.0 2.1 %collective-permute-done.17.other = bf16[12,1280]{1,0:T(8,128)(2,1)S(1)} collective-permute-done((bf16[12,1280]{1,0:T(8,128)(2,1)S(1)}, bf16[12,1280]{1,0:T(8,128)(2,1)S(1)}, u32[]{:S(2)}, u32[]{:S(2)}) %collective-permute-start.17) | collective-permute-done | bytes 30752 | tf_op jit(solution)/shard_map/ppermute | solution.py:174
  72.1 0.6 shard_map.131
  (28 shorter events, 0.1 us)
Async XLA Ops:
  0.0 9.0 %copy-start.2 = (bf16[3,224,1024]{2,1,0:T(8,128)(2,1)S(1)}, bf16[3,224,1024]{2,1,0:T(8,128)(2,1)}, u32[]{:S(2)}) copy-start(bf16[3,224,1024]{2,1,0:T(8,128)(2,1)} %values.1) | copy-start | bytes 4128772
  0.0 9.0 %copy-start.1 = (bf16[3,224,1024]{2,1,0:T(8,128)(2,1)S(1)}, bf16[3,224,1024]{2,1,0:T(8,128)(2,1)}, u32[]{:S(2)}) copy-start(bf16[3,224,1024]{2,1,0:T(8,128)(2,1)} %keys.1) | copy-start | bytes 4128772
  0.0 1.9 %collective-permute-start = (bf16[12,1280]{1,0:T(8,128)(2,1)}, bf16[12,1280]{1,0:T(8,128)(2,1)S(1)}, u32[]{:S(2)}, u32[]{:S(2)}) collective-permute-start(bf16[12,1280]{1,0:T(8,128)(2,1)} %query_a.1), channel_id=1, source_target_pairs={{0,4},{4,0},{8,12},{12,8},{1,5},{5,1},{9,13},{13,9},{2,6},{6,2},{1... | collective-permute-start | bytes 92168 | tf_op jit(solution)/shard_map/ppermute | solution.py:174
  0.5 1.4 %collective-permute-start.1 = (bf16[12,512]{1,0:T(8,128)(2,1)}, bf16[12,512]{1,0:T(8,128)(2,1)S(1)}, u32[]{:S(2)}, u32[]{:S(2)}) collective-permute-start(bf16[12,512]{1,0:T(8,128)(2,1)} %pairs_a.1), channel_id=1, source_target_pairs={{0,4},{4,0},{8,12},{12,8},{1,5},{5,1},{9,13},{13,9},{2,6},{6,2},{1... | collective-permute-start | bytes 36872 | tf_op jit(solution)/shard_map/ppermute | solution.py:174
  1.9 0.8 %copy-start.3 = (bf16[12,1280]{1,0:T(8,128)(2,1)S(1)}, bf16[12,1280]{1,0:T(8,128)(2,1)}, u32[]{:S(2)}) copy-start(bf16[12,1280]{1,0:T(8,128)(2,1)} %query_a.1) | copy-start | bytes 92164
  2.6 0.7 copy-start.5
  3.4 0.7 copy-start.7
  4.0 5.0 %copy-start.6 = (s32[3]{0:T(128)S(1)}, s32[3]{0:T(128)}, u32[]{:S(2)}) copy-start(s32[3]{0:T(128)} %lengths.1) | copy-start | bytes 40
  4.5 4.5 %collective-permute-start.2 = (bf16[96,128]{1,0:T(8,128)(2,1)S(1)}, bf16[96,128]{1,0:T(8,128)(2,1)S(1)}, u32[]{:S(2)}, u32[]{:S(2)}) collective-permute-start(bf16[96,128]{1,0:T(8,128)(2,1)S(1)} %get-tuple-element.24), channel_id=1, source_target_pairs={{0,8},{4,12},{8,0},{12,4},{1,9},{5,13},{9,1},{13,5},{2,10},{6,14},... | collective-permute-start | bytes 73736 | tf_op jit(solution)/shard_map/ppermute | solution.py:174
  13.9 3.9 %collective-permute-start.3 = (bf16[2,4,1280]{2,1,0:T(4,128)(2,1)S(1)}, bf16[2,4,1280]{2,1,0:T(4,128)(2,1)S(1)}, u32[]{:S(2)}, u32[]{:S(2)}) collective-permute-start(bf16[2,4,1280]{2,1,0:T(4,128)(2,1)S(1)} %get-tuple-element.26), channel_id=1, source_target_pairs={{0,1},{1,0},{2,3},{3,2},{4,5},{5,4},{6,7},{7,6},{8,9},{9,8},{10,11... | collective-permute-start | bytes 61448 | tf_op jit(solution)/shard_map/ppermute | solution.py:174
  17.8 9.3 %copy-start = (bf16[1280,1280]{1,0:T(8,128)(2,1)S(1)}, bf16[1280,1280]{1,0:T(8,128)(2,1)}, u32[]{:S(2)}) copy-start(bf16[1280,1280]{1,0:T(8,128)(2,1)} %weight.3) | copy-start | bytes 9830404
  17.8 9.3 %copy-start.8 = (s32[48]{0:T(128)S(1)}, s32[48]{0:T(128)}, u32[]{:S(2)}) copy-start(s32[48]{0:T(128)} %param.18) | copy-start | bytes 580
  17.8 4.9 %collective-permute-start.4 = (bf16[2,4,1280]{2,1,0:T(4,128)(2,1)S(1)}, bf16[2,4,1280]{2,1,0:T(4,128)(2,1)S(1)}, u32[]{:S(2)}, u32[]{:S(2)}) collective-permute-start(bf16[2,4,1280]{2,1,0:T(4,128)(2,1)S(1)} %shard_map.120), channel_id=1, source_target_pairs={{0,2},{1,3},{2,0},{3,1},{4,6},{5,7},{6,4},{7,5},{8,10},{9,11},{10,... | collective-permute-start | bytes 61448 | tf_op jit(solution)/shard_map/ppermute | solution.py:174
  22.7 9.8 %copy-start.4 = (bf16[12,1280]{1,0:T(8,128)(2,1)S(1)}, bf16[12,1280]{1,0:T(8,128)(2,1)}, u32[]{:S(2)}) copy-start(bf16[12,1280]{1,0:T(8,128)(2,1)} %resid.1) | copy-start | bytes 92164
  22.7 3.6 %collective-permute-start.7 = (bf16[16,1280]{1,0:T(8,128)(2,1)S(1)}, bf16[16,1280]{1,0:T(8,128)(2,1)S(1)}, u32[]{:S(2)}, u32[]{:S(2)}) collective-permute-start(bf16[16,1280]{1,0:T(8,128)(2,1)S(1)} %shard_map.121.first), channel_id=1, source_target_pairs={{0,12},{4,8},{8,4},{12,0},{1,13},{5,9},{9,5},{13,1},{2,14},{6,10},... | collective-permute-start | bytes 122888 | tf_op jit(solution)/shard_map/ppermute | solution.py:174
  22.8 4.3 %collective-permute-start.6 = (bf16[16,1280]{1,0:T(8,128)(2,1)S(1)}, bf16[16,1280]{1,0:T(8,128)(2,1)S(1)}, u32[]{:S(2)}, u32[]{:S(2)}) collective-permute-start(bf16[16,1280]{1,0:T(8,128)(2,1)S(1)} %shard_map.121.first), channel_id=1, source_target_pairs={{0,8},{4,12},{8,0},{12,4},{1,9},{5,13},{9,1},{13,5},{2,10},{6,14},... | collective-permute-start | bytes 122888 | tf_op jit(solution)/shard_map/ppermute | solution.py:174
  24.7 2.4 %collective-permute-start.5 = (bf16[16,1280]{1,0:T(8,128)(2,1)S(1)}, bf16[16,1280]{1,0:T(8,128)(2,1)S(1)}, u32[]{:S(2)}, u32[]{:S(2)}) collective-permute-start(bf16[16,1280]{1,0:T(8,128)(2,1)S(1)} %shard_map.121.first), channel_id=1, source_target_pairs={{0,4},{4,0},{8,12},{12,8},{1,5},{5,1},{9,13},{13,9},{2,6},{6,2},{1... | collective-permute-start | bytes 122888 | tf_op jit(solution)/shard_map/ppermute | solution.py:174
  28.0 4.5 %collective-permute-start.8 = (bf16[24,1280]{1,0:T(8,128)(2,1)S(1)}, bf16[24,1280]{1,0:T(8,128)(2,1)S(1)}, u32[]{:S(2)}, u32[]{:S(2)}) collective-permute-start(bf16[24,1280]{1,0:T(8,128)(2,1)S(1)} %get-tuple-element.28), channel_id=1, source_target_pairs={{0,1},{1,0},{2,3},{3,2},{4,5},{5,4},{6,7},{7,6},{8,9},{9,8},{10,11... | collective-permute-start | bytes 184328 | tf_op jit(solution)/shard_map/ppermute | solution.py:174
  32.5 9.7 %slice-start = ((s8[10485760]{0:T(1024)(128)(4,1)}), s8[4194304]{0:T(1024)(128)(4,1)S(1)}, s32[]{:S(2)}) async-start(s8[10485760]{0:T(1024)(128)(4,1)} %bitcast.1), calls=%async_computation | async-start | bytes 8388608
  32.5 9.7 %slice-start.1 = ((s8[10485760]{0:T(1024)(128)(4,1)}), s8[4194304]{0:T(1024)(128)(4,1)S(1)}, s32[]{:S(2)}) async-start(s8[10485760]{0:T(1024)(128)(4,1)} %bitcast.1), calls=%async_computation.1 | async-start | bytes 8388608
  32.5 9.7 %slice-start.3 = ((s8[10485760]{0:T(1024)(128)(4,1)}), s8[4194304]{0:T(1024)(128)(4,1)S(1)}, s32[]{:S(2)}) async-start(s8[10485760]{0:T(1024)(128)(4,1)} %bitcast.3), calls=%async_computation.3 | async-start | bytes 8388608
  32.5 9.7 %slice-start.4 = ((s8[10485760]{0:T(1024)(128)(4,1)}), s8[4194304]{0:T(1024)(128)(4,1)S(1)}, s32[]{:S(2)}) async-start(s8[10485760]{0:T(1024)(128)(4,1)} %bitcast.3), calls=%async_computation.4 | async-start | bytes 8388608
  32.7 7.1 %copy-start.9 = (bf16[1280]{0:T(1024)(128)(2,1)S(1)}, bf16[1280]{0:T(1024)(128)(2,1)}, u32[]{:S(2)}) copy-start(bf16[1280]{0:T(1024)(128)(2,1)} %param.20) | copy-start | bytes 7684
  32.7 5.2 %collective-permute-start.9 = (bf16[24,1280]{1,0:T(8,128)(2,1)S(1)}, bf16[24,1280]{1,0:T(8,128)(2,1)S(1)}, u32[]{:S(2)}, u32[]{:S(2)}) collective-permute-start(bf16[24,1280]{1,0:T(8,128)(2,1)S(1)} %get-tuple-element.30), channel_id=1, source_target_pairs={{0,2},{1,3},{2,0},{3,1},{4,6},{5,7},{6,4},{7,5},{8,10},{9,11},{10,... | collective-permute-start | bytes 184328 | tf_op jit(solution)/shard_map/ppermute | solution.py:174
  37.9 4.3 %slice-start.2 = ((s8[10485760]{0:T(1024)(128)(4,1)}), s8[2097152]{0:T(1024)(128)(4,1)S(1)}, s32[]{:S(2)}) async-start(s8[10485760]{0:T(1024)(128)(4,1)} %bitcast.1), calls=%async_computation.2 | async-start | bytes 4194304
  37.9 4.3 %slice-start.5 = ((s8[10485760]{0:T(1024)(128)(4,1)}), s8[2097152]{0:T(1024)(128)(4,1)S(1)}, s32[]{:S(2)}) async-start(s8[10485760]{0:T(1024)(128)(4,1)} %bitcast.3), calls=%async_computation.5 | async-start | bytes 4194304
  38.0 4.3 %collective-permute-start.10 = (bf16[24,1280]{1,0:T(8,128)(2,1)S(1)}, bf16[24,1280]{1,0:T(8,128)(2,1)S(1)}, u32[]{:S(2)}, u32[]{:S(2)}) collective-permute-start(bf16[24,1280]{1,0:T(8,128)(2,1)S(1)} %get-tuple-element.31.mine), channel_id=1, source_target_pairs={{0,1},{1,0},{2,3},{3,2},{4,5},{5,4},{6,7},{7,6},{8,9},{9,8},{10,11... | collective-permute-start | bytes 184328 | tf_op jit(solution)/shard_map/ppermute | solution.py:174
  46.1 1.8 %collective-permute-start.11 = (bf16[2,24,4224]{2,1,0:T(8,128)(2,1)S(1)}, bf16[2,24,4224]{2,1,0:T(8,128)(2,1)S(1)}, u32[]{:S(2)}, u32[]{:S(2)}) collective-permute-start(bf16[2,24,4224]{2,1,0:T(8,128)(2,1)S(1)} %get-tuple-element.33), channel_id=1, source_target_pairs={{0,4},{4,0},{8,12},{12,8},{1,5},{5,1},{9,13},{13,9},{2,6},{6,2},{1... | collective-permute-start | bytes 1216520 | tf_op jit(solution)/shard_map/ppermute | solution.py:174
  47.9 12.2 %slice-start.6 = ((s8[10485760]{0:T(1024)(128)(4,1)}), s8[4194304]{0:T(1024)(128)(4,1)S(1)}, s32[]{:S(2)}) async-start(s8[10485760]{0:T(1024)(128)(4,1)} %bitcast.5), calls=%async_computation.6 | async-start | bytes 8388608
  47.9 12.2 %slice-start.7 = ((s8[10485760]{0:T(1024)(128)(4,1)}), s8[4194304]{0:T(1024)(128)(4,1)S(1)}, s32[]{:S(2)}) async-start(s8[10485760]{0:T(1024)(128)(4,1)} %bitcast.5), calls=%async_computation.7 | async-start | bytes 8388608
  48.1 7.1 %collective-permute-start.12 = (bf16[24,4224]{1,0:T(8,128)(2,1)S(1)}, bf16[24,4224]{1,0:T(8,128)(2,1)S(1)}, u32[]{:S(2)}, u32[]{:S(2)}) collective-permute-start(bf16[24,4224]{1,0:T(8,128)(2,1)S(1)} %get-tuple-element.35), channel_id=1, source_target_pairs={{0,8},{4,12},{8,0},{12,4},{1,9},{5,13},{9,1},{13,5},{2,10},{6,14},... | collective-permute-start | bytes 608264 | tf_op jit(solution)/shard_map/ppermute | solution.py:174
  55.2 4.9 %slice-start.8 = ((s8[10485760]{0:T(1024)(128)(4,1)}), s8[2097152]{0:T(1024)(128)(4,1)S(1)}, s32[]{:S(2)}) async-start(s8[10485760]{0:T(1024)(128)(4,1)} %bitcast.5), calls=%async_computation.8 | async-start | bytes 4194304
  55.4 4.7 %collective-permute-start.13 = (bf16[24,2048]{1,0:T(8,128)(2,1)S(1)}, bf16[24,2048]{1,0:T(8,128)(2,1)S(1)}, u32[]{:S(2)}, u32[]{:S(2)}) collective-permute-start(bf16[24,2048]{1,0:T(8,128)(2,1)S(1)} %shard_map.127.mine), channel_id=1, source_target_pairs={{0,8},{4,12},{8,0},{12,4},{1,9},{5,13},{9,1},{13,5},{2,10},{6,14},... | collective-permute-start | bytes 294920 | tf_op jit(solution)/shard_map/ppermute | solution.py:174
  57.1 3.0 %collective-permute-start.15 = (bf16[24,2048]{1,0:T(8,128)(2,1)S(1)}, bf16[24,2048]{1,0:T(8,128)(2,1)S(1)}, u32[]{:S(2)}, u32[]{:S(2)}) collective-permute-start(bf16[24,2048]{1,0:T(8,128)(2,1)S(1)} %shard_map.127.mine), channel_id=1, source_target_pairs={{0,4},{4,0},{8,12},{12,8},{1,5},{5,1},{9,13},{13,9},{2,6},{6,2},{1... | collective-permute-start | bytes 294920 | tf_op jit(solution)/shard_map/ppermute | solution.py:174
  60.1 1.3 %collective-permute-start.14 = (bf16[24,2048]{1,0:T(8,128)(2,1)S(1)}, bf16[24,2048]{1,0:T(8,128)(2,1)S(1)}, u32[]{:S(2)}, u32[]{:S(2)}) collective-permute-start(bf16[24,2048]{1,0:T(8,128)(2,1)S(1)} %collective-permute-done.13.mine), channel_id=1, source_target_pairs={{0,4},{4,0},{8,12},{12,8},{1,5},{5,1},{9,13},{13,9},{2,6},{6,2},{1... | collective-permute-start | bytes 294920 | tf_op jit(solution)/shard_map/ppermute | solution.py:174
  62.5 4.3 %collective-permute-start.16 = (bf16[24,1280]{1,0:T(8,128)(2,1)S(1)}, bf16[24,1280]{1,0:T(8,128)(2,1)S(1)}, u32[]{:S(2)}, u32[]{:S(2)}) collective-permute-start(bf16[24,1280]{1,0:T(8,128)(2,1)S(1)} %get-tuple-element.37), channel_id=1, source_target_pairs={{0,1},{1,0},{2,3},{3,2},{4,5},{5,4},{6,7},{7,6},{8,9},{9,8},{10,11... | collective-permute-start | bytes 184328 | tf_op jit(solution)/shard_map/ppermute | solution.py:174
  66.8 5.3 %collective-permute-start.17 = (bf16[12,1280]{1,0:T(8,128)(2,1)S(1)}, bf16[12,1280]{1,0:T(8,128)(2,1)S(1)}, u32[]{:S(2)}, u32[]{:S(2)}) collective-permute-start(bf16[12,1280]{1,0:T(8,128)(2,1)S(1)} %get-tuple-element.40), channel_id=1, source_target_pairs={{0,2},{1,3},{2,0},{3,1},{4,6},{5,7},{6,4},{7,5},{8,10},{9,11},{10,... | collective-permute-start | bytes 92168 | tf_op jit(solution)/shard_map/ppermute | solution.py:174

commit v4 on v1

--- a/solution.py
+++ b/solution.py
@@ -1,8 +1,11 @@
+import functools
 import math
 
 import jax
 import jax.numpy as jnp
 from jax import lax
+from jax.experimental import pallas as pl
+from jax.experimental.pallas import tpu as pltpu
 from jax.sharding import PartitionSpec as P
 
 D = 5120
@@ -141,9 +144,424 @@
     return (stream + ff_out).astype(jnp.bfloat16)
 
 
+MIB = 1024 * 1024
+
+
+def call(kernel, outs, operands, scratch=(), smem=(), resident=(), remote=(), micros=4, limit=8):
+    specs = []
+    placed = []
+    for place, operand in enumerate(operands):
+        space = pltpu.SMEM if place in smem else pltpu.HBM if place in remote else pltpu.VMEM
+        specs.append(pl.BlockSpec(memory_space=space))
+        if place in resident or place in remote:
+            operand = constrained(operand, space)
+        placed.append(operand)
+    return pl.pallas_call(
+        kernel,
+        out_shape=[jax.ShapeDtypeStruct(shape, dtype) for shape, dtype in outs],
+        in_specs=specs,
+        out_specs=[pl.BlockSpec(memory_space=pltpu.VMEM) for _ in outs],
+        scratch_shapes=list(scratch),
+        compiler_params=pltpu.CompilerParams(vmem_limit_bytes=limit * MIB),
+        cost_estimate=pl.CostEstimate(flops=micros * 10**9, bytes_accessed=0, transcendentals=0),
+    )(*placed)
+
+
+def constrained(operand, space):
+    return pltpu.with_memory_space_constraint(operand, space)
+
+
+def swap(value, axis, step):
+    if isinstance(axis, tuple):
+        count = lax.axis_size(axis[1])
+        total = lax.axis_size(axis[0]) * count
+        step = step[0] * count + step[1]
+    else:
+        total = lax.axis_size(axis)
+    return lax.ppermute(value, axis, [(i, i ^ step) for i in range(total)])
+
+
+def slot_picker(per_device, group, assign):
+    sec, tp = lax.axis_index("sec"), lax.axis_index("tp")
+    slots = jnp.zeros((1, group), jnp.int32)
+    for index in range(assign.shape[1] // group):
+        slots = jnp.where(tp == index, assign[:, index * group : (index + 1) * group], slots)
+    line = lax.broadcasted_iota(jnp.int32, (16, group), 0)
+    wanted = jnp.where(line < 8, sec * per_device + line, (sec ^ 3) * per_device + line - 8)
+    inside = (line & 7) < per_device
+    return jnp.where(inside & (jnp.broadcast_to(slots, (16, group)) == wanted), 1.0, 0.0).astype(jnp.bfloat16)
+
+
+def split_heads(per_device, picker, query, pairs, rows):
+    queries = jnp.dot(picker, query[...], preferred_element_type=jnp.float32)
+    others = jnp.dot(picker, pairs[...], preferred_element_type=jnp.float32)
+    width = HEAD_WIDTH
+    heads = query.shape[1] // width
+    rows[...] = jnp.zeros_like(rows)
+    for side in range(2):
+        for j in range(per_device):
+            line = side * 8 + j
+            for h in range(heads):
+                rows[side, j * 16 + h : j * 16 + h + 1, :] = queries[line : line + 1, h * width : (h + 1) * width]
+            for h in range(pairs.shape[1] // width):
+                at = j * 16 + heads + h
+                rows[side, at : at + 1, :] = others[line : line + 1, h * width : (h + 1) * width]
+
+
+def pick_own_kernel(per_device, group, query, pairs, assign, out, query_here, pairs_here, assign_here, rows, sems):
+    copies = [
+        pltpu.make_async_copy(source, target, sems.at[index])
+        for index, (source, target) in enumerate(
+            ((query, query_here), (pairs, pairs_here), (assign, assign_here))
+        )
+    ]
+    for copy in copies:
+        copy.start()
+    for copy in copies:
+        copy.wait()
+    split_heads(per_device, slot_picker(per_device, group, assign_here), query_here, pairs_here, rows)
+    out[...] = rows[...].astype(jnp.bfloat16)
+
+
+def pick_other_kernel(per_device, group, own, query, pairs, assign, keep, send, rows):
+    split_heads(per_device, slot_picker(per_device, group, assign), query, pairs, rows)
+    here = lax.axis_index("sec") & 1
+    keep[here] = own[0]
+    keep[1 - here] = rows[0].astype(jnp.bfloat16)
+    send[here] = own[1]
+    send[1 - here] = rows[1].astype(jnp.bfloat16)
+
+
+def attend_kernel(flip, per_device, heads, lengths, mine, other, keys, values, out, total):
+    sec, tp = lax.axis_index("sec"), lax.axis_index("tp")
+    chip = sec >> 1
+    parity = (tp & 1) ^ flip
+    share = heads // 2
+    slots = keys.shape[1]
+    width = HEAD_WIDTH
+    scaling = 1.0 / math.sqrt(width)
+    line = lax.broadcasted_iota(jnp.int32, (16, width), 0)
+    upper = line < share
+    place = lax.broadcasted_iota(jnp.int32, (16, slots), 1)
+    near, far = mine[parity].astype(jnp.float32), other[parity].astype(jnp.float32)
+    sources = (jnp.where(chip == 0, near, far), jnp.where(chip == 0, far, near))
+    work = [(i, j) for i in range(2) for j in range(per_device)]
+    past, fresh, new_values, columns = [], [], [], []
+    for i, j in work:
+        wide = sources[i][j * 16 : (j + 1) * 16]
+        zero = jnp.zeros_like(wide)
+        both = jnp.concatenate([jnp.where(upper, wide, zero), jnp.where(upper, zero, wide)], axis=1)
+        column = pl.ds(pl.multiple_of((2 * i + parity) * 2 * width, 2 * width), 2 * width)
+        columns.append(column)
+        scores = lax.dot_general(
+            both.astype(jnp.bfloat16),
+            keys[j, :, column],
+            (((1,), (1,)), ((), ())),
+            preferred_element_type=jnp.float32,
+        )
+        past.append(jnp.where(place < lengths[j], scores * scaling, -1e30))
+        new_key = jnp.where(upper, wide[heads : heads + 1], wide[heads + 2 : heads + 3])
+        new_values.append(jnp.where(upper, wide[heads + 1 : heads + 2], wide[heads + 3 : heads + 4]))
+        fresh.append(wide * new_key)
+    past = jnp.concatenate(past, axis=0)
+    fresh = jnp.sum(jnp.concatenate(fresh, axis=0), axis=1, keepdims=True) * scaling
+    highest = jnp.maximum(jnp.max(past, axis=1, keepdims=True), fresh)
+    past_exp = jnp.exp(past - highest)
+    fresh_exp = jnp.exp(fresh - highest)
+    inverse = 1.0 / (jnp.sum(past_exp, axis=1, keepdims=True) + fresh_exp)
+    weights = (past_exp * inverse).astype(jnp.bfloat16)
+    fresh_weight = (fresh_exp * inverse).astype(jnp.bfloat16).astype(jnp.float32)
+    total[...] = jnp.zeros_like(total)
+    for index, (i, j) in enumerate(work):
+        lines = slice(index * 16, (index + 1) * 16)
+        mixed = jnp.dot(weights[lines], values[j, :, columns[index]], preferred_element_type=jnp.float32)
+        mixed = jnp.where(upper, mixed[:, :width], mixed[:, width:]) + fresh_weight[lines] * new_values[index]
+        for h in range(heads):
+            total[i, j : j + 1, h * width : (h + 1) * width] = mixed[h : h + 1]
+    out[...] = total[:, 0:4].astype(jnp.bfloat16)
+
+
+def forward_kernel(mine, other, send):
+    away = (lax.axis_index("tp") >> 1) ^ 1
+    send[0] = mine[away]
+    send[1] = other[away]
+
+
+def gather_kernel(mine, other, far, out, rows):
+    here = lax.axis_index("tp") >> 1
+    rows[0:4] = mine[here].astype(jnp.float32)
+    rows[4:8] = other[here].astype(jnp.float32)
+    rows[8:12] = far[0].astype(jnp.float32)
+    rows[12:16] = far[1].astype(jnp.float32)
+    out[...] = rows[...].astype(jnp.bfloat16)
+
+
+def project_kernel(per_device, group, own, beside, across, corner, assign, resid, weight, keep, send):
+    sec, tp = lax.axis_index("sec"), lax.axis_index("tp")
+    count = assign.shape[1]
+    lines = jnp.concatenate([own[...], beside[...], across[...], corner[...]], axis=0)
+    line = lax.broadcasted_iota(jnp.int32, (64, count), 0)
+    request = lax.broadcasted_iota(jnp.int32, (64, count), 1)
+    number = jnp.zeros((64, count), jnp.int32)
+    for limit in range(1, 4):
+        number = number + jnp.where(request >= limit * group, 1, 0)
+    block, place = line >> 4, (line >> 2) & 3
+    from_sec = sec ^ block ^ (block >> 1) ^ ((place ^ (place >> 1)) & 1)
+    slot = from_sec * per_device + (line & 3)
+    match = (number == (tp ^ place)) & (jnp.broadcast_to(assign[...], (64, count)) == slot)
+    match = jnp.where(match & ((line & 3) < per_device), 1.0, 0.0).astype(jnp.bfloat16)
+    ordered = lax.dot_general(match, lines, (((0,), (0,)), ((), ())), preferred_element_type=jnp.float32)
+    total = jnp.dot(ordered.astype(jnp.bfloat16), weight[...], preferred_element_type=jnp.float32)
+    line = lax.broadcasted_iota(jnp.int32, (count, group), 0)
+    match = line == lax.broadcasted_iota(jnp.int32, (count, group), 1) + tp * group
+    match = jnp.where(match, 1.0, 0.0).astype(jnp.bfloat16)
+    total = total + jnp.dot(match, resid[...], preferred_element_type=jnp.float32)
+    keep[...] = total
+    send[...] = total.astype(jnp.bfloat16)
+
+
+def add_kernel(mine, other, keep, send):
+    total = mine[...] + other[...].astype(jnp.float32)
+    keep[...] = total
+    send[...] = total.astype(jnp.bfloat16)
+
+
+def row_half():
+    sec = lax.axis_index("sec")
+    return (sec ^ (sec >> 1)) & 1
+
+
+def products(features, gate, up, part, chunk, keep, send):
+    half = keep.shape[0]
+    width = gate.shape[1] // 2
+    for kind, weight in enumerate((gate, up)):
+        for start in range(0, width, chunk):
+            column = pl.ds(pl.multiple_of(part * width + start, chunk), chunk)
+            product = jnp.dot(features, weight[:, column], preferred_element_type=jnp.float32)
+            at = kind * width + start
+            keep[:, at : at + chunk] = product[:half]
+            send[:, at : at + chunk] = product[half:].astype(jnp.bfloat16)
+
+
+def gate_up_first_kernel(chunk, mine, other, gain, gate, up, keep, send, features, stream, halves, groups):
+    sec, tp = lax.axis_index("sec"), lax.axis_index("tp")
+    half = mine.shape[0] // 2
+    total = mine[...] + other[...].astype(jnp.float32)
+    group = stream.shape[0]
+    for index in range(mine.shape[0] // group):
+        groups[index, 0:group] = total[index * group : (index + 1) * group]
+    stream[...] = groups[tp, 0:group]
+    halves[0] = total[:half]
+    halves[1] = total[half:]
+    first = row_half()
+    total = jnp.concatenate([halves[first], halves[1 - first]], axis=0)
+    squares = jnp.sum(total * total, axis=1, keepdims=True)
+    scaled = (total * gain[...].astype(jnp.float32)).astype(jnp.bfloat16)
+    features[...] = scaled
+    products(scaled, gate, up, 1 - (sec >> 1), chunk, keep, send)
+    width = gate.shape[1]
+    keep[:, width:] = jnp.broadcast_to(squares[:half], (half, 128))
+    send[:, width:] = two_terms(squares[half:])
+
+
+def gate_up_second_kernel(chunk, features, gate, up, keep, send):
+    products(features[...], gate, up, lax.axis_index("sec") >> 1, chunk, keep, send)
+
+
+def two_terms(column):
+    shape = (column.shape[0], 128)
+    column = jnp.broadcast_to(column, shape)
+    coarse = column.astype(jnp.bfloat16).astype(jnp.float32)
+    lane = lax.broadcasted_iota(jnp.int32, shape, 1)
+    return jnp.where(lane < 64, coarse, column - coarse).astype(jnp.bfloat16)
+
+
+def one_column(terms):
+    return terms[:, 0:1].astype(jnp.float32) + terms[:, 64:65].astype(jnp.float32)
+
+
+def pair_sum_kernel(mine, other, send, squares):
+    width = mine.shape[1] - 128
+    total = mine[:, :width] + other[:, :width].astype(jnp.float32)
+    send[:, :width] = total.astype(jnp.bfloat16)
+    both = mine[:, width:] + one_column(other[:, width:])
+    squares[...] = both
+    send[:, width:] = two_terms(both[:, 0:1])
+
+
+def hidden_kernel(features, mine, beside, across, squares, hidden):
+    width = mine.shape[1] // 2
+    total = squares[:, 0:1] + one_column(across[:, 2 * width :])
+    inverse = lax.rsqrt(total / features + 1e-06)
+
+    def summed(columns):
+        here = mine[:, columns] + beside[:, columns].astype(jnp.float32)
+        return (here + across[:, columns].astype(jnp.float32)) * inverse
+
+    gate, up = summed(slice(0, width)), summed(slice(width, 2 * width))
+    hidden[...] = (gate / (1.0 + jnp.exp(-gate)) * up).astype(jnp.bfloat16)
+
+
+def down_lines(mine, other):
+    lines = jnp.concatenate([mine[...].astype(jnp.float32), other[...].astype(jnp.float32)], axis=0)
+    return lines.astype(jnp.bfloat16)
+
+
+def down_first_kernel(mine, other, weight, out):
+    here = lax.axis_index("sec") >> 1
+    depth = mine.shape[1]
+    rows = weight[pl.ds(pl.multiple_of(here * depth, depth), depth), :]
+    out[...] = jnp.dot(down_lines(mine, other), rows, preferred_element_type=jnp.float32)
+
+
+def down_second_kernel(mine, other, before, weight, keep, first, second, third, groups):
+    tp = lax.axis_index("tp")
+    away = 1 - (lax.axis_index("sec") >> 1)
+    depth = mine.shape[1]
+    rows = weight[pl.ds(pl.multiple_of(away * depth, depth), depth), :]
+    product = before[...] + jnp.dot(down_lines(mine, other), rows, preferred_element_type=jnp.float32)
+    group = keep.shape[0]
+    for index in range(product.shape[0] // group):
+        groups[index, 0:group] = product[index * group : (index + 1) * group]
+    here = tp ^ (2 * row_half())
+    keep[...] = groups[here, 0:group]
+    for step, target in enumerate((first, second, third)):
+        target[...] = groups[here ^ (step + 1), 0:group].astype(jnp.bfloat16)
+
+
+def finish_kernel(stream, mine, first, second, third, out):
+    total = stream[...] + mine[...]
+    for other in (first, second, third):
+        total = total + other[...].astype(jnp.float32)
+    out[...] = total.astype(jnp.bfloat16)
+
+
+def local_pairs(
+    resid,
+    query,
+    new_kv,
+    key_cache,
+    cached_value_rows,
+    cache_len,
+    assign,
+    out_weight,
+    norm_gain,
+    gate_weight,
+    up_weight,
+    down_weight,
+):
+    f32, bf16 = jnp.float32, jnp.bfloat16
+    group, features = resid.shape
+    per_device = key_cache.shape[0]
+    heads = query.shape[1] // HEAD_WIDTH
+    head_block = out_weight.shape[0]
+    width = gate_weight.shape[1]
+    half = 2 * group
+    assign = assign.reshape(1, -1)
+    gain = norm_gain.reshape(1, -1)
+
+    query_b, pairs_b = swap(query, "sec", 1), swap(new_kv, "sec", 1)
+    block = (2, 16 * per_device, HEAD_WIDTH)
+    (own,) = call(
+        functools.partial(pick_own_kernel, per_device, group),
+        [(block, bf16)],
+        (query, new_kv, assign),
+        [
+            pltpu.VMEM(query.shape, bf16),
+            pltpu.VMEM(new_kv.shape, bf16),
+            pltpu.VMEM(assign.shape, jnp.int32),
+            pltpu.VMEM(block, f32),
+            pltpu.SemaphoreType.DMA((3,)),
+        ],
+        remote=(0, 1, 2),
+    )
+    mine, away = call(
+        functools.partial(pick_other_kernel, per_device, group),
+        [(block, bf16)] * 2,
+        (own, query_b, pairs_b, assign),
+        [pltpu.VMEM(block, f32)],
+    )
+    other = swap(away, "sec", 3)
+    sent, kept = [
+        call(
+            functools.partial(attend_kernel, flip, per_device, heads),
+            [((2, 4, head_block), bf16)],
+            (cache_len, mine, other, key_cache, cached_value_rows),
+            [pltpu.VMEM((2, 8, head_block), f32)],
+            smem=(0,),
+            resident=(3, 4),
+        )[0]
+        for flip in (1, 0)
+    ]
+
+    other = swap(sent, ("sec", "tp"), (1, 1))
+    (away,) = call(forward_kernel, [((2, 4, head_block), bf16)], (kept, other))
+    far = swap(away, ("sec", "tp"), (1, 2))
+    (own,) = call(
+        gather_kernel, [((16, head_block), bf16)], (kept, other, far), [pltpu.VMEM((16, head_block), f32)]
+    )
+    across = swap(own, "sec", 3)
+    beside = swap(own, "sec", 1)
+    corner = swap(across, "sec", 1)
+    pair = [((2 * half, features), f32), ((2 * half, features), bf16)]
+    mine, away = call(
+        functools.partial(project_kernel, per_device, group),
+        pair,
+        (own, beside, across, corner, assign, resid, out_weight),
+        resident=(6,),
+    )
+    mine, away = call(add_kernel, pair, (mine, swap(away, "tp", 1)))
+    other = swap(away, "tp", 2)
+
+    chunk = min(512, width // 2)
+    mine, away, lines, stream = call(
+        functools.partial(gate_up_first_kernel, chunk),
+        [
+            ((half, width + 128), f32),
+            ((half, width + 128), bf16),
+            ((2 * half, features), bf16),
+            ((group, features), f32),
+        ],
+        (mine, other, gain, gate_weight, up_weight),
+        [pltpu.VMEM((2, half, features), f32), pltpu.VMEM((4, 16, features), f32)],
+        resident=(3, 4),
+    )
+    away, squares = call(
+        pair_sum_kernel, [((half, width + 128), bf16), ((half, 128), f32)], (mine, swap(away, "sec", 1))
+    )
+    across = swap(away, "sec", 3)
+    mine, away = call(
+        functools.partial(gate_up_second_kernel, chunk),
+        [((half, width), f32), ((half, width), bf16)],
+        (lines, gate_weight, up_weight),
+        resident=(1, 2),
+    )
+    beside = swap(away, "sec", 1)
+    (hidden,) = call(
+        functools.partial(hidden_kernel, features * lax.axis_size("sec")),
+        [((half, width // 2), bf16)],
+        (mine, beside, across, squares),
+    )
+    across = swap(hidden, "sec", 3)
+    beside = swap(hidden, "sec", 1)
+    corner = swap(across, "sec", 1)
+    (before,) = call(down_first_kernel, [((2 * half, features), f32)], (hidden, beside, down_weight), resident=(2,))
+    mine, *parts = call(
+        down_second_kernel,
+        [((group, features), f32)] + [((group, features), bf16)] * 3,
+        (across, corner, before, down_weight),
+        [pltpu.VMEM((4, 16, features), f32)],
+        resident=(3,),
+    )
+    parts = [swap(part, "tp", step + 1) for step, part in enumerate(parts)]
+    (out,) = call(finish_kernel, [((group, features), bf16)], (stream, mine, *parts))
+    return out
+
+
 def solution(mesh):
+    small = mesh.shape["sec"] == 4 and mesh.shape["tp"] == 4
     return jax.shard_map(
-        local,
+        local_pairs if small else local,
         mesh=mesh,
         in_specs=(
             P(("rep", "tp"), "sec"),

time: 121 us -> 64.6 us (0.53)
  matrix products: 26 us -> 0 us
  local copies, waits for them, and re-layouts: 18.4 us -> 0.08 us
  Pallas kernels: 0 us -> 11.9 us
  starting transfers between devices: 32.3 us -> 23.4 us
  waiting for transfers between devices: 36.1 us -> 28.8 us
  other arithmetic: 7.29 us -> 0.01 us
    dot_general x11 -> x0, matrix products: 26 us -> none  [the longest x1 6.68 us: local(): up_part = jnp.dot(piece, up_weight, preferred_element_type=jnp.float32)]
    pallas_call x0 -> x15, Pallas kernels: none -> 11.9 us  [call(): pl.pallas_call(kernel, out_shape=[jax.ShapeDtypeStruct(shape, dtype) for...]
    ppermute x30 -> x19, starting transfers between devices: 32.3 us -> 23.4 us  [swap(): return lax.ppermute(value, axis, [(i, i ^ step) for i in range(total)])]
    ppermute x30 -> x19, waiting for transfers between devices: 36.1 us -> 28.8 us  [swap(): return lax.ppermute(value, axis, [(i, i ^ step) for i in range(total)])]
    gather x5 -> x0, local copies, waits for them, and re-layouts: 6.96 us -> none  [the longest x2 4.43 us: local(): jnp.take(hidden, sec_index ^ lax.iota(jnp.int32, sec_count), axis=0)]
    concatenate x4 -> x0, local copies, waits for them, and re-layouts: 5.57 us -> none  [the longest x3 4.85 us: local(): jnp.concatenate([gate_part, up_part], axis=1).astype(jnp.bfloat16)]
    unnamed x22 -> x32, local copies, waits for them, and re-layouts: 3.01 us -> 0.08 us
    mul x2 -> x0, other arithmetic: 1.36 us -> none  [the longest x1 1.34 us: local(): hidden = gated_units(share * inverse, width)]
  transfers between devices with their start and end apart: 30 -> 19, of which waited for: 16 -> 15; matrix products, arithmetic and copies ran while one was open for 3% -> 0% of each run, Pallas kernels for 0% -> 8%
where the time goes in v4:
time: 64.6 us; the launch traced here: 64.4 us
  waiting for transfers between devices  28.8 us (45%)
  starting transfers between devices  23.4 us (36%)
  Pallas kernels  11.9 us (18%)
    ppermute x19, waiting for transfers between devices, swap(): return lax.ppermute(value, axis, [(i, i ^ step) for i in range(total)])  28.8 us
    ppermute x19, starting transfers between devices, swap(): return lax.ppermute(value, axis, [(i, i ^ step) for i in range(total)])  23.4 us
    pallas_call x15, Pallas kernels, call(): pl.pallas_call(kernel, out_shape=[jax.ShapeDtypeStruct(shape, dtype) for...  11.9 us
  transfers between devices with their start and end apart: 19, of which 15 were waited for; matrix products, arithmetic and copies ran while one was open for 0% of the time, Pallas kernels for 8%

profile of v4, /device:TPU:0, one launch (start us, length us, event | category | flops | bytes accessed | tf_op | source)
XLA Modules:
  0.0 64.4 jit_solution(7350681679876757577)
XLA Ops:
  0.0 0.5 collective-permute-start.1
  0.5 0.1 collective-permute-start
  0.5 1.2 %shard_map.118.own = bf16[2,48,128]{2,1,0:T(8,128)(2,1)S(1)} custom-call(bf16[12,1280]{1,0:T(8,128)(2,1)} %query.1, bf16[12,512]{1,0:T(8,128)(2,1)} %pairs.1, s32[1,48]{1,0:T(1,128)} %bitcast.7), custom_call_target="tpu_custom_call" | custom-call | flops 4000000000 | tf_op jit(solution)/shard_map/pallas_call | solution.py:159
  1.8 0.0 copy-start.1
  1.8 0.0 copy-start.2
  1.8 0.0 copy-start.4
  1.8 0.0 collective-permute-done.1.pairs
  1.8 0.1 collective-permute-done.query
  1.9 0.0 copy-done.5
  1.9 0.4 shard_map.119
  2.3 2.7 %collective-permute-start.2 = (bf16[2,48,128]{2,1,0:T(8,128)(2,1)S(1)}, bf16[2,48,128]{2,1,0:T(8,128)(2,1)S(1)}, u32[]{:S(2)}, u32[]{:S(2)}) collective-permute-start(bf16[2,48,128]{2,1,0:T(8,128)(2,1)S(1)} %get-tuple-element.24), channel_id=1, source_target_pairs={{0,12},{4,8},{8,4},{12,0},{1,13},{5,9},{9,5},{13,1},{2,14},{6,10},... | collective-permute-start | bytes 73736 | tf_op jit(solution)/shard_map/ppermute | solution.py:181
  5.0 1.5 %collective-permute-done.2.other = bf16[2,48,128]{2,1,0:T(8,128)(2,1)S(1)} collective-permute-done((bf16[2,48,128]{2,1,0:T(8,128)(2,1)S(1)}, bf16[2,48,128]{2,1,0:T(8,128)(2,1)S(1)}, u32[]{:S(2)}, u32[]{:S(2)}) %collective-permute-start.2) | collective-permute-done | bytes 24608 | tf_op jit(solution)/shard_map/ppermute | solution.py:181
  6.5 0.0 copy-done.1
  6.5 0.0 copy-done.2
  6.5 0.0 copy-done.4
  6.5 1.1 %shard_map.121 = bf16[2,4,1280]{2,1,0:T(4,128)(2,1)S(1)} custom-call(s32[3]{0:T(128)S(1)} %copy-done.4, bf16[2,48,128]{2,1,0:T(8,128)(2,1)S(1)} %get-tuple-element.23.mine, bf16[2,48,128]{2,1,0:T(8,128)(2,1)S(1)} %collective-permute-done.2.other, bf16[3,224,1024]{2,1,0:T(8,128)(2,1)S(1)} %copy-done.1, bf16[3,224,1024]{2,1,0:T(8,128)(2,1)S(1)} %copy-done.2), custom_call_target="tpu_custom_call" | custom-call | flops 4000000000 | tf_op jit(solution)/shard_map/pallas_call | solution.py:159
  7.7 1.9 %collective-permute-start.3 = (bf16[2,4,1280]{2,1,0:T(4,128)(2,1)S(1)}, bf16[2,4,1280]{2,1,0:T(4,128)(2,1)S(1)}, u32[]{:S(2)}, u32[]{:S(2)}) collective-permute-start(bf16[2,4,1280]{2,1,0:T(4,128)(2,1)S(1)} %shard_map.121), channel_id=1, source_target_pairs={{0,5},{1,4},{2,7},{3,6},{4,1},{5,0},{6,3},{7,2},{8,13},{9,12},{10,... | collective-permute-start | bytes 61448 | tf_op jit(solution)/shard_map/ppermute | solution.py:181
  9.6 1.1 %shard_map.120.mine = bf16[2,4,1280]{2,1,0:T(4,128)(2,1)S(1)} custom-call(s32[3]{0:T(128)S(1)} %copy-done.4, bf16[2,48,128]{2,1,0:T(8,128)(2,1)S(1)} %get-tuple-element.23.mine, bf16[2,48,128]{2,1,0:T(8,128)(2,1)S(1)} %collective-permute-done.2.other, bf16[3,224,1024]{2,1,0:T(8,128)(2,1)S(1)} %copy-done.1, bf16[3,224,1024]{2,1,0:T(8,128)(2,1)S(1)} %copy-done.2), custom_call_target="tpu_custom_call" | custom-call | flops 4000000000 | tf_op jit(solution)/shard_map/pallas_call | solution.py:159
  10.7 0.3 collective-permute-done.3.other
  11.0 2.8 %collective-permute-start.4 = (bf16[2,4,1280]{2,1,0:T(4,128)(2,1)S(1)}, bf16[2,4,1280]{2,1,0:T(4,128)(2,1)S(1)}, u32[]{:S(2)}, u32[]{:S(2)}) collective-permute-start(bf16[2,4,1280]{2,1,0:T(4,128)(2,1)S(1)} %shard_map.122), channel_id=1, source_target_pairs={{0,6},{1,7},{2,4},{3,5},{4,2},{5,3},{6,0},{7,1},{8,14},{9,15},{10,... | collective-permute-start | bytes 61448 | tf_op jit(solution)/shard_map/ppermute | solution.py:181
  13.8 1.5 %collective-permute-done.4.far = bf16[2,4,1280]{2,1,0:T(4,128)(2,1)S(1)} collective-permute-done((bf16[2,4,1280]{2,1,0:T(4,128)(2,1)S(1)}, bf16[2,4,1280]{2,1,0:T(4,128)(2,1)S(1)}, u32[]{:S(2)}, u32[]{:S(2)}) %collective-permute-start.4) | collective-permute-done | bytes 20512 | tf_op jit(solution)/shard_map/ppermute | solution.py:181
  15.4 1.6 %collective-permute-start.6 = (bf16[16,1280]{1,0:T(8,128)(2,1)S(1)}, bf16[16,1280]{1,0:T(8,128)(2,1)S(1)}, u32[]{:S(2)}, u32[]{:S(2)}) collective-permute-start(bf16[16,1280]{1,0:T(8,128)(2,1)S(1)} %shard_map.123.own), channel_id=1, source_target_pairs={{0,12},{4,8},{8,4},{12,0},{1,13},{5,9},{9,5},{13,1},{2,14},{6,10},... | collective-permute-start | bytes 122888 | tf_op jit(solution)/shard_map/ppermute | solution.py:181
  16.9 0.4 collective-permute-start.5
  17.3 1.5 %collective-permute-done.6.across = bf16[16,1280]{1,0:T(8,128)(2,1)S(1)} collective-permute-done((bf16[16,1280]{1,0:T(8,128)(2,1)S(1)}, bf16[16,1280]{1,0:T(8,128)(2,1)S(1)}, u32[]{:S(2)}, u32[]{:S(2)}) %collective-permute-start.6) | collective-permute-done | bytes 40992 | tf_op jit(solution)/shard_map/ppermute | solution.py:181
  18.9 0.4 collective-permute-start.7
  19.2 0.0 collective-permute-done.5.beside
  19.2 0.9 %collective-permute-done.7.corner = bf16[16,1280]{1,0:T(8,128)(2,1)S(1)} collective-permute-done((bf16[16,1280]{1,0:T(8,128)(2,1)S(1)}, bf16[16,1280]{1,0:T(8,128)(2,1)S(1)}, u32[]{:S(2)}, u32[]{:S(2)}) %collective-permute-start.7) | collective-permute-done | bytes 40992 | tf_op jit(solution)/shard_map/ppermute | solution.py:181
  20.1 0.0 copy-done
  20.1 0.0 slice-start.3
  20.1 0.0 slice-start.4
  20.1 0.8 %shard_map.124 = (f32[48,1280]{1,0:T(8,128)S(1)}, bf16[48,1280]{1,0:T(8,128)(2,1)S(1)}) custom-call(bf16[16,1280]{1,0:T(8,128)(2,1)S(1)} %shard_map.123.own, bf16[16,1280]{1,0:T(8,128)(2,1)S(1)} %collective-permute-done.5.beside, bf16[16,1280]{1,0:T(8,128)(2,1)S(1)} %collective-permute-done.6.across, bf16[16,1280]{1,0:T(8,128)(2,1)S(1)} %collective-permute-done.7.corner, ...), custom_call_target="tpu_custom_call" | custom-call | flops 4000000000 | tf_op jit(solution)/shard_map/pallas_call | solution.py:159
  21.0 0.0 copy-start.6
  21.0 2.1 %collective-permute-start.8 = (bf16[48,1280]{1,0:T(8,128)(2,1)S(1)}, bf16[48,1280]{1,0:T(8,128)(2,1)S(1)}, u32[]{:S(2)}, u32[]{:S(2)}) collective-permute-start(bf16[48,1280]{1,0:T(8,128)(2,1)S(1)} %get-tuple-element.26), channel_id=1, source_target_pairs={{0,1},{1,0},{2,3},{3,2},{4,5},{5,4},{6,7},{7,6},{8,9},{9,8},{10,11... | collective-permute-start | bytes 368648 | tf_op jit(solution)/shard_map/ppermute | solution.py:181
  23.1 3.6 %collective-permute-done.8.other = bf16[48,1280]{1,0:T(8,128)(2,1)S(1)} collective-permute-done((bf16[48,1280]{1,0:T(8,128)(2,1)S(1)}, bf16[48,1280]{1,0:T(8,128)(2,1)S(1)}, u32[]{:S(2)}, u32[]{:S(2)}) %collective-permute-start.8) | collective-permute-done | bytes 122912 | tf_op jit(solution)/shard_map/ppermute | solution.py:181
  26.7 3.1 %collective-permute-start.9 = (bf16[48,1280]{1,0:T(8,128)(2,1)S(1)}, bf16[48,1280]{1,0:T(8,128)(2,1)S(1)}, u32[]{:S(2)}, u32[]{:S(2)}) collective-permute-start(bf16[48,1280]{1,0:T(8,128)(2,1)S(1)} %get-tuple-element.28), channel_id=1, source_target_pairs={{0,2},{1,3},{2,0},{3,1},{4,6},{5,7},{6,4},{7,5},{8,10},{9,11},{10,... | collective-permute-start | bytes 368648 | tf_op jit(solution)/shard_map/ppermute | solution.py:181
  29.9 5.8 %collective-permute-done.9.other = bf16[48,1280]{1,0:T(8,128)(2,1)S(1)} collective-permute-done((bf16[48,1280]{1,0:T(8,128)(2,1)S(1)}, bf16[48,1280]{1,0:T(8,128)(2,1)S(1)}, u32[]{:S(2)}, u32[]{:S(2)}) %collective-permute-start.9) | collective-permute-done | bytes 122912 | tf_op jit(solution)/shard_map/ppermute | solution.py:181
  35.6 0.0 slice-done
  35.6 0.0 slice-done.3
  35.7 2.0 %shard_map.126 = (f32[24,4224]{1,0:T(8,128)S(1)}, bf16[24,4224]{1,0:T(8,128)(2,1)S(1)}, bf16[48,1280]{1,0:T(8,128)(2,1)S(1)}, f32[12,1280]{1,0:T(8,128)S(1)}) custom-call(f32[48,1280]{1,0:T(8,128)S(1)} %get-tuple-element.27.mine, bf16[48,1280]{1,0:T(8,128)(2,1)S(1)} %collective-permute-done.9.other, bf16[1,1280]{1,0:T(2,128)(2,1)S(1)} %reshape.7.gain, ...), custom_call_target="tpu_custom_call" | custom-call | flops 4000000000 | tf_op jit(solution)/shard_map/pallas_call | solution.py:159
  37.7 0.1 collective-permute-start.11
  37.7 1.4 %collective-permute-done.11.other = bf16[24,4224]{1,0:T(8,128)(2,1)S(1)} collective-permute-done((bf16[24,4224]{1,0:T(8,128)(2,1)S(1)}, bf16[24,4224]{1,0:T(8,128)(2,1)S(1)}, u32[]{:S(2)}, u32[]{:S(2)}) %collective-permute-start.11) | collective-permute-done | bytes 202784 | tf_op jit(solution)/shard_map/ppermute | solution.py:181
  39.2 0.2 shard_map.128
  39.4 1.2 %collective-permute-start.12 = (bf16[24,4224]{1,0:T(8,128)(2,1)S(1)}, bf16[24,4224]{1,0:T(8,128)(2,1)S(1)}, u32[]{:S(2)}, u32[]{:S(2)}) collective-permute-start(bf16[24,4224]{1,0:T(8,128)(2,1)S(1)} %get-tuple-element.35), channel_id=1, source_target_pairs={{0,12},{4,8},{8,4},{12,0},{1,13},{5,9},{9,5},{13,1},{2,14},{6,10},... | collective-permute-start | bytes 608264 | tf_op jit(solution)/shard_map/ppermute | solution.py:181
  40.6 1.9 %shard_map.127 = (f32[24,4096]{1,0:T(8,128)S(1)}, bf16[24,4096]{1,0:T(8,128)(2,1)S(1)}) custom-call(bf16[48,1280]{1,0:T(8,128)(2,1)S(1)} %get-tuple-element.30.features, bf16[1280,4096]{1,0:T(8,128)(2,1)S(1)} %bitcast.2, bf16[1280,4096]{1,0:T(8,128)(2,1)S(1)} %bitcast.4), custom_call_target="tpu_custom_call" | custom-call | flops 4000000000 | tf_op jit(solution)/shard_map/pallas_call | solution.py:159
  42.6 0.4 collective-permute-start.10
  43.0 1.1 %collective-permute-done.10.beside = bf16[24,4096]{1,0:T(8,128)(2,1)S(1)} collective-permute-done((bf16[24,4096]{1,0:T(8,128)(2,1)S(1)}, bf16[24,4096]{1,0:T(8,128)(2,1)S(1)}, u32[]{:S(2)}, u32[]{:S(2)}) %collective-permute-start.10) | collective-permute-done | bytes 196640 | tf_op jit(solution)/shard_map/ppermute | solution.py:181
  44.0 2.4 %collective-permute-done.12.across = bf16[24,4224]{1,0:T(8,128)(2,1)S(1)} collective-permute-done((bf16[24,4224]{1,0:T(8,128)(2,1)S(1)}, bf16[24,4224]{1,0:T(8,128)(2,1)S(1)}, u32[]{:S(2)}, u32[]{:S(2)}) %collective-permute-start.12) | collective-permute-done | bytes 202784 | tf_op jit(solution)/shard_map/ppermute | solution.py:181
  46.4 0.2 shard_map.129.mine
  46.6 1.3 %collective-permute-start.13 = (bf16[24,2048]{1,0:T(8,128)(2,1)S(1)}, bf16[24,2048]{1,0:T(8,128)(2,1)S(1)}, u32[]{:S(2)}, u32[]{:S(2)}) collective-permute-start(bf16[24,2048]{1,0:T(8,128)(2,1)S(1)} %shard_map.129.mine), channel_id=1, source_target_pairs={{0,12},{4,8},{8,4},{12,0},{1,13},{5,9},{9,5},{13,1},{2,14},{6,10},... | collective-permute-start | bytes 294920 | tf_op jit(solution)/shard_map/ppermute | solution.py:181
  47.9 0.4 collective-permute-start.15
  48.3 3.2 %collective-permute-done.13.mine = bf16[24,2048]{1,0:T(8,128)(2,1)S(1)} collective-permute-done((bf16[24,2048]{1,0:T(8,128)(2,1)S(1)}, bf16[24,2048]{1,0:T(8,128)(2,1)S(1)}, u32[]{:S(2)}, u32[]{:S(2)}) %collective-permute-start.13) | collective-permute-done | bytes 98336 | tf_op jit(solution)/shard_map/ppermute | solution.py:181
  51.5 0.1 collective-permute-start.14
  51.6 0.0 collective-permute-done.15.other
  51.6 0.0 slice-done.6
  51.6 1.0 %shard_map.130.before = f32[48,1280]{1,0:T(8,128)S(1)} custom-call(bf16[24,2048]{1,0:T(8,128)(2,1)S(1)} %shard_map.129.mine, bf16[24,2048]{1,0:T(8,128)(2,1)S(1)} %collective-permute-done.15.other, bf16[4096,1280]{1,0:T(8,128)(2,1)S(1)} %bitcast.6), custom_call_target="tpu_custom_call" | custom-call | flops 4000000000 | tf_op jit(solution)/shard_map/pallas_call | solution.py:159
  52.7 0.1 collective-permute-done.14.other
  52.8 1.0 %shard_map.131 = (f32[12,1280]{1,0:T(8,128)S(1)}, bf16[12,1280]{1,0:T(8,128)(2,1)S(1)}, bf16[12,1280]{1,0:T(8,128)(2,1)S(1)}, bf16[12,1280]{1,0:T(8,128)(2,1)S(1)}) custom-call(bf16[24,2048]{1,0:T(8,128)(2,1)S(1)} %collective-permute-done.13.mine, bf16[24,2048]{1,0:T(8,128)(2,1)S(1)} %collective-permute-done.14.other, f32[48,1280]{1,0:T(8,128)S(1)} %shard_map.130.before, ...), custom_call_target="tpu_custom_call" | custom-call | flops 4000000000 | tf_op jit(solution)/shard_map/pallas_call | solution.py:159
  53.8 0.7 %collective-permute-start.16 = (bf16[12,1280]{1,0:T(8,128)(2,1)S(1)}, bf16[12,1280]{1,0:T(8,128)(2,1)S(1)}, u32[]{:S(2)}, u32[]{:S(2)}) collective-permute-start(bf16[12,1280]{1,0:T(8,128)(2,1)S(1)} %get-tuple-element.38), channel_id=1, source_target_pairs={{0,1},{1,0},{2,3},{3,2},{4,5},{5,4},{6,7},{7,6},{8,9},{9,8},{10,11... | collective-permute-start | bytes 92168 | tf_op jit(solution)/shard_map/ppermute | solution.py:181
  54.6 3.4 %collective-permute-start.17 = (bf16[12,1280]{1,0:T(8,128)(2,1)S(1)}, bf16[12,1280]{1,0:T(8,128)(2,1)S(1)}, u32[]{:S(2)}, u32[]{:S(2)}) collective-permute-start(bf16[12,1280]{1,0:T(8,128)(2,1)S(1)} %get-tuple-element.39), channel_id=1, source_target_pairs={{0,2},{1,3},{2,0},{3,1},{4,6},{5,7},{6,4},{7,5},{8,10},{9,11},{10,... | collective-permute-start | bytes 92168 | tf_op jit(solution)/shard_map/ppermute | solution.py:181
  58.0 0.3 collective-permute-start.18
  58.3 0.0 collective-permute-done.16.first
  58.3 2.6 %collective-permute-done.17.second = bf16[12,1280]{1,0:T(8,128)(2,1)S(1)} collective-permute-done((bf16[12,1280]{1,0:T(8,128)(2,1)S(1)}, bf16[12,1280]{1,0:T(8,128)(2,1)S(1)}, u32[]{:S(2)}, u32[]{:S(2)}) %collective-permute-start.17) | collective-permute-done | bytes 30752 | tf_op jit(solution)/shard_map/ppermute | solution.py:181
  60.8 2.9 %collective-permute-done.18.third = bf16[12,1280]{1,0:T(8,128)(2,1)S(1)} collective-permute-done((bf16[12,1280]{1,0:T(8,128)(2,1)S(1)}, bf16[12,1280]{1,0:T(8,128)(2,1)S(1)}, u32[]{:S(2)}, u32[]{:S(2)}) %collective-permute-start.18) | collective-permute-done | bytes 30752 | tf_op jit(solution)/shard_map/ppermute | solution.py:181
  63.8 0.6 %shard_map.132 = bf16[12,1280]{1,0:T(8,128)(2,1)} custom-call(f32[12,1280]{1,0:T(8,128)S(1)} %get-tuple-element.29.stream, f32[12,1280]{1,0:T(8,128)S(1)} %get-tuple-element.37.mine, bf16[12,1280]{1,0:T(8,128)(2,1)S(1)} %collective-permute-done.16.first, bf16[12,1280]{1,0:T(8,128)(2,1)S(1)} %collective-permute-done.17.second, ...), custom_call_target="tpu_custom_call" | custom-call | flops 4000000000 | tf_op jit(solution)/shard_map/pallas_call | solution.py:159
  (25 shorter events, 0.1 us)
Async XLA Ops:
  0.0 1.9 %copy-start.5 = (s32[48]{0:T(128)S(1)}, s32[48]{0:T(128)}, u32[]{:S(2)}) copy-start(s32[48]{0:T(128)} %param.18) | copy-start | bytes 580
  0.0 1.8 %collective-permute-start.1 = (bf16[12,512]{1,0:T(8,128)(2,1)}, bf16[12,512]{1,0:T(8,128)(2,1)S(1)}, u32[]{:S(2)}, u32[]{:S(2)}) collective-permute-start(bf16[12,512]{1,0:T(8,128)(2,1)} %pairs.1), channel_id=1, source_target_pairs={{0,4},{4,0},{8,12},{12,8},{1,5},{5,1},{9,13},{13,9},{2,6},{6,2},{1... | collective-permute-start | bytes 36872 | tf_op jit(solution)/shard_map/ppermute | solution.py:181
  0.5 1.4 %collective-permute-start = (bf16[12,1280]{1,0:T(8,128)(2,1)}, bf16[12,1280]{1,0:T(8,128)(2,1)S(1)}, u32[]{:S(2)}, u32[]{:S(2)}) collective-permute-start(bf16[12,1280]{1,0:T(8,128)(2,1)} %query.1), channel_id=1, source_target_pairs={{0,4},{4,0},{8,12},{12,8},{1,5},{5,1},{9,13},{13,9},{2,6},{6,2},{1... | collective-permute-start | bytes 92168 | tf_op jit(solution)/shard_map/ppermute | solution.py:181
  1.8 4.7 %copy-start.1 = (bf16[3,224,1024]{2,1,0:T(8,128)(2,1)S(1)}, bf16[3,224,1024]{2,1,0:T(8,128)(2,1)}, u32[]{:S(2)}) copy-start(bf16[3,224,1024]{2,1,0:T(8,128)(2,1)} %keys.3) | copy-start | bytes 4128772
  1.8 4.7 %copy-start.2 = (bf16[3,224,1024]{2,1,0:T(8,128)(2,1)S(1)}, bf16[3,224,1024]{2,1,0:T(8,128)(2,1)}, u32[]{:S(2)}) copy-start(bf16[3,224,1024]{2,1,0:T(8,128)(2,1)} %values.3) | copy-start | bytes 4128772
  1.8 4.7 %copy-start.4 = (s32[3]{0:T(128)S(1)}, s32[3]{0:T(128)}, u32[]{:S(2)}) copy-start(s32[3]{0:T(128)} %lengths.3) | copy-start | bytes 40
  2.3 4.2 %collective-permute-start.2 = (bf16[2,48,128]{2,1,0:T(8,128)(2,1)S(1)}, bf16[2,48,128]{2,1,0:T(8,128)(2,1)S(1)}, u32[]{:S(2)}, u32[]{:S(2)}) collective-permute-start(bf16[2,48,128]{2,1,0:T(8,128)(2,1)S(1)} %get-tuple-element.24), channel_id=1, source_target_pairs={{0,12},{4,8},{8,4},{12,0},{1,13},{5,9},{9,5},{13,1},{2,14},{6,10},... | collective-permute-start | bytes 73736 | tf_op jit(solution)/shard_map/ppermute | solution.py:181
  7.7 3.4 %collective-permute-start.3 = (bf16[2,4,1280]{2,1,0:T(4,128)(2,1)S(1)}, bf16[2,4,1280]{2,1,0:T(4,128)(2,1)S(1)}, u32[]{:S(2)}, u32[]{:S(2)}) collective-permute-start(bf16[2,4,1280]{2,1,0:T(4,128)(2,1)S(1)} %shard_map.121), channel_id=1, source_target_pairs={{0,5},{1,4},{2,7},{3,6},{4,1},{5,0},{6,3},{7,2},{8,13},{9,12},{10,... | collective-permute-start | bytes 61448 | tf_op jit(solution)/shard_map/ppermute | solution.py:181
  11.0 9.1 %copy-start = (bf16[1280,1280]{1,0:T(8,128)(2,1)S(1)}, bf16[1280,1280]{1,0:T(8,128)(2,1)}, u32[]{:S(2)}) copy-start(bf16[1280,1280]{1,0:T(8,128)(2,1)} %weight.3) | copy-start | bytes 9830404
  11.0 9.1 %copy-start.3 = (bf16[12,1280]{1,0:T(8,128)(2,1)S(1)}, bf16[12,1280]{1,0:T(8,128)(2,1)}, u32[]{:S(2)}) copy-start(bf16[12,1280]{1,0:T(8,128)(2,1)} %resid.1) | copy-start | bytes 92164
  11.0 4.3 %collective-permute-start.4 = (bf16[2,4,1280]{2,1,0:T(4,128)(2,1)S(1)}, bf16[2,4,1280]{2,1,0:T(4,128)(2,1)S(1)}, u32[]{:S(2)}, u32[]{:S(2)}) collective-permute-start(bf16[2,4,1280]{2,1,0:T(4,128)(2,1)S(1)} %shard_map.122), channel_id=1, source_target_pairs={{0,6},{1,7},{2,4},{3,5},{4,2},{5,3},{6,0},{7,1},{8,14},{9,15},{10,... | collective-permute-start | bytes 61448 | tf_op jit(solution)/shard_map/ppermute | solution.py:181
  15.4 3.5 %collective-permute-start.6 = (bf16[16,1280]{1,0:T(8,128)(2,1)S(1)}, bf16[16,1280]{1,0:T(8,128)(2,1)S(1)}, u32[]{:S(2)}, u32[]{:S(2)}) collective-permute-start(bf16[16,1280]{1,0:T(8,128)(2,1)S(1)} %shard_map.123.own), channel_id=1, source_target_pairs={{0,12},{4,8},{8,4},{12,0},{1,13},{5,9},{9,5},{13,1},{2,14},{6,10},... | collective-permute-start | bytes 122888 | tf_op jit(solution)/shard_map/ppermute | solution.py:181
  16.9 2.3 %collective-permute-start.5 = (bf16[16,1280]{1,0:T(8,128)(2,1)S(1)}, bf16[16,1280]{1,0:T(8,128)(2,1)S(1)}, u32[]{:S(2)}, u32[]{:S(2)}) collective-permute-start(bf16[16,1280]{1,0:T(8,128)(2,1)S(1)} %shard_map.123.own), channel_id=1, source_target_pairs={{0,4},{4,0},{8,12},{12,8},{1,5},{5,1},{9,13},{13,9},{2,6},{6,2},{1... | collective-permute-start | bytes 122888 | tf_op jit(solution)/shard_map/ppermute | solution.py:181
  18.9 1.2 %collective-permute-start.7 = (bf16[16,1280]{1,0:T(8,128)(2,1)S(1)}, bf16[16,1280]{1,0:T(8,128)(2,1)S(1)}, u32[]{:S(2)}, u32[]{:S(2)}) collective-permute-start(bf16[16,1280]{1,0:T(8,128)(2,1)S(1)} %collective-permute-done.6.across), channel_id=1, source_target_pairs={{0,4},{4,0},{8,12},{12,8},{1,5},{5,1},{9,13},{13,9},{2,6},{6,2},{1... | collective-permute-start | bytes 122888 | tf_op jit(solution)/shard_map/ppermute | solution.py:181
  20.1 15.5 %slice-start = ((s8[10485760]{0:T(1024)(128)(4,1)}), s8[4194304]{0:T(1024)(128)(4,1)S(1)}, s32[]{:S(2)}) async-start(s8[10485760]{0:T(1024)(128)(4,1)} %bitcast.1), calls=%async_computation | async-start | bytes 8388608
  20.1 15.5 %slice-start.1 = ((s8[10485760]{0:T(1024)(128)(4,1)}), s8[4194304]{0:T(1024)(128)(4,1)S(1)}, s32[]{:S(2)}) async-start(s8[10485760]{0:T(1024)(128)(4,1)} %bitcast.1), calls=%async_computation.1 | async-start | bytes 8388608
  20.1 15.5 %slice-start.3 = ((s8[10485760]{0:T(1024)(128)(4,1)}), s8[4194304]{0:T(1024)(128)(4,1)S(1)}, s32[]{:S(2)}) async-start(s8[10485760]{0:T(1024)(128)(4,1)} %bitcast.3), calls=%async_computation.3 | async-start | bytes 8388608
  20.1 15.5 %slice-start.4 = ((s8[10485760]{0:T(1024)(128)(4,1)}), s8[4194304]{0:T(1024)(128)(4,1)S(1)}, s32[]{:S(2)}) async-start(s8[10485760]{0:T(1024)(128)(4,1)} %bitcast.3), calls=%async_computation.4 | async-start | bytes 8388608
  21.0 8.9 %copy-start.6 = (bf16[1280]{0:T(1024)(128)(2,1)S(1)}, bf16[1280]{0:T(1024)(128)(2,1)}, u32[]{:S(2)}) copy-start(bf16[1280]{0:T(1024)(128)(2,1)} %param.20) | copy-start | bytes 7684
  21.0 5.7 %collective-permute-start.8 = (bf16[48,1280]{1,0:T(8,128)(2,1)S(1)}, bf16[48,1280]{1,0:T(8,128)(2,1)S(1)}, u32[]{:S(2)}, u32[]{:S(2)}) collective-permute-start(bf16[48,1280]{1,0:T(8,128)(2,1)S(1)} %get-tuple-element.26), channel_id=1, source_target_pairs={{0,1},{1,0},{2,3},{3,2},{4,5},{5,4},{6,7},{7,6},{8,9},{9,8},{10,11... | collective-permute-start | bytes 368648 | tf_op jit(solution)/shard_map/ppermute | solution.py:181
  26.7 9.0 %slice-start.2 = ((s8[10485760]{0:T(1024)(128)(4,1)}), s8[2097152]{0:T(1024)(128)(4,1)S(1)}, s32[]{:S(2)}) async-start(s8[10485760]{0:T(1024)(128)(4,1)} %bitcast.1), calls=%async_computation.2 | async-start | bytes 4194304
  26.7 9.0 %slice-start.5 = ((s8[10485760]{0:T(1024)(128)(4,1)}), s8[2097152]{0:T(1024)(128)(4,1)S(1)}, s32[]{:S(2)}) async-start(s8[10485760]{0:T(1024)(128)(4,1)} %bitcast.3), calls=%async_computation.5 | async-start | bytes 4194304
  26.7 8.9 %collective-permute-start.9 = (bf16[48,1280]{1,0:T(8,128)(2,1)S(1)}, bf16[48,1280]{1,0:T(8,128)(2,1)S(1)}, u32[]{:S(2)}, u32[]{:S(2)}) collective-permute-start(bf16[48,1280]{1,0:T(8,128)(2,1)S(1)} %get-tuple-element.28), channel_id=1, source_target_pairs={{0,2},{1,3},{2,0},{3,1},{4,6},{5,7},{6,4},{7,5},{8,10},{9,11},{10,... | collective-permute-start | bytes 368648 | tf_op jit(solution)/shard_map/ppermute | solution.py:181
  37.7 1.5 %collective-permute-start.11 = (bf16[24,4224]{1,0:T(8,128)(2,1)S(1)}, bf16[24,4224]{1,0:T(8,128)(2,1)S(1)}, u32[]{:S(2)}, u32[]{:S(2)}) collective-permute-start(bf16[24,4224]{1,0:T(8,128)(2,1)S(1)} %get-tuple-element.34), channel_id=1, source_target_pairs={{0,4},{4,0},{8,12},{12,8},{1,5},{5,1},{9,13},{13,9},{2,6},{6,2},{1... | collective-permute-start | bytes 608264 | tf_op jit(solution)/shard_map/ppermute | solution.py:181
  39.4 7.0 %collective-permute-start.12 = (bf16[24,4224]{1,0:T(8,128)(2,1)S(1)}, bf16[24,4224]{1,0:T(8,128)(2,1)S(1)}, u32[]{:S(2)}, u32[]{:S(2)}) collective-permute-start(bf16[24,4224]{1,0:T(8,128)(2,1)S(1)} %get-tuple-element.35), channel_id=1, source_target_pairs={{0,12},{4,8},{8,4},{12,0},{1,13},{5,9},{9,5},{13,1},{2,14},{6,10},... | collective-permute-start | bytes 608264 | tf_op jit(solution)/shard_map/ppermute | solution.py:181
  40.6 11.0 %slice-start.6 = ((s8[10485760]{0:T(1024)(128)(4,1)}), s8[4194304]{0:T(1024)(128)(4,1)S(1)}, s32[]{:S(2)}) async-start(s8[10485760]{0:T(1024)(128)(4,1)} %bitcast.5), calls=%async_computation.6 | async-start | bytes 8388608
  40.6 11.0 %slice-start.7 = ((s8[10485760]{0:T(1024)(128)(4,1)}), s8[4194304]{0:T(1024)(128)(4,1)S(1)}, s32[]{:S(2)}) async-start(s8[10485760]{0:T(1024)(128)(4,1)} %bitcast.5), calls=%async_computation.7 | async-start | bytes 8388608
  42.6 1.5 %collective-permute-start.10 = (bf16[24,4096]{1,0:T(8,128)(2,1)S(1)}, bf16[24,4096]{1,0:T(8,128)(2,1)S(1)}, u32[]{:S(2)}, u32[]{:S(2)}) collective-permute-start(bf16[24,4096]{1,0:T(8,128)(2,1)S(1)} %get-tuple-element.32), channel_id=1, source_target_pairs={{0,4},{4,0},{8,12},{12,8},{1,5},{5,1},{9,13},{13,9},{2,6},{6,2},{1... | collective-permute-start | bytes 589832 | tf_op jit(solution)/shard_map/ppermute | solution.py:181
  46.4 5.2 %slice-start.8 = ((s8[10485760]{0:T(1024)(128)(4,1)}), s8[2097152]{0:T(1024)(128)(4,1)S(1)}, s32[]{:S(2)}) async-start(s8[10485760]{0:T(1024)(128)(4,1)} %bitcast.5), calls=%async_computation.8 | async-start | bytes 4194304
  46.6 4.8 %collective-permute-start.13 = (bf16[24,2048]{1,0:T(8,128)(2,1)S(1)}, bf16[24,2048]{1,0:T(8,128)(2,1)S(1)}, u32[]{:S(2)}, u32[]{:S(2)}) collective-permute-start(bf16[24,2048]{1,0:T(8,128)(2,1)S(1)} %shard_map.129.mine), channel_id=1, source_target_pairs={{0,12},{4,8},{8,4},{12,0},{1,13},{5,9},{9,5},{13,1},{2,14},{6,10},... | collective-permute-start | bytes 294920 | tf_op jit(solution)/shard_map/ppermute | solution.py:181
  47.9 3.7 %collective-permute-start.15 = (bf16[24,2048]{1,0:T(8,128)(2,1)S(1)}, bf16[24,2048]{1,0:T(8,128)(2,1)S(1)}, u32[]{:S(2)}, u32[]{:S(2)}) collective-permute-start(bf16[24,2048]{1,0:T(8,128)(2,1)S(1)} %shard_map.129.mine), channel_id=1, source_target_pairs={{0,4},{4,0},{8,12},{12,8},{1,5},{5,1},{9,13},{13,9},{2,6},{6,2},{1... | collective-permute-start | bytes 294920 | tf_op jit(solution)/shard_map/ppermute | solution.py:181
  51.5 1.3 %collective-permute-start.14 = (bf16[24,2048]{1,0:T(8,128)(2,1)S(1)}, bf16[24,2048]{1,0:T(8,128)(2,1)S(1)}, u32[]{:S(2)}, u32[]{:S(2)}) collective-permute-start(bf16[24,2048]{1,0:T(8,128)(2,1)S(1)} %collective-permute-done.13.mine), channel_id=1, source_target_pairs={{0,4},{4,0},{8,12},{12,8},{1,5},{5,1},{9,13},{13,9},{2,6},{6,2},{1... | collective-permute-start | bytes 294920 | tf_op jit(solution)/shard_map/ppermute | solution.py:181
  53.8 4.5 %collective-permute-start.16 = (bf16[12,1280]{1,0:T(8,128)(2,1)S(1)}, bf16[12,1280]{1,0:T(8,128)(2,1)S(1)}, u32[]{:S(2)}, u32[]{:S(2)}) collective-permute-start(bf16[12,1280]{1,0:T(8,128)(2,1)S(1)} %get-tuple-element.38), channel_id=1, source_target_pairs={{0,1},{1,0},{2,3},{3,2},{4,5},{5,4},{6,7},{7,6},{8,9},{9,8},{10,11... | collective-permute-start | bytes 92168 | tf_op jit(solution)/shard_map/ppermute | solution.py:181
  54.6 6.3 %collective-permute-start.17 = (bf16[12,1280]{1,0:T(8,128)(2,1)S(1)}, bf16[12,1280]{1,0:T(8,128)(2,1)S(1)}, u32[]{:S(2)}, u32[]{:S(2)}) collective-permute-start(bf16[12,1280]{1,0:T(8,128)(2,1)S(1)} %get-tuple-element.39), channel_id=1, source_target_pairs={{0,2},{1,3},{2,0},{3,1},{4,6},{5,7},{6,4},{7,5},{8,10},{9,11},{10,... | collective-permute-start | bytes 92168 | tf_op jit(solution)/shard_map/ppermute | solution.py:181
  58.0 5.8 %collective-permute-start.18 = (bf16[12,1280]{1,0:T(8,128)(2,1)S(1)}, bf16[12,1280]{1,0:T(8,128)(2,1)S(1)}, u32[]{:S(2)}, u32[]{:S(2)}) collective-permute-start(bf16[12,1280]{1,0:T(8,128)(2,1)S(1)} %get-tuple-element.40), channel_id=1, source_target_pairs={{0,3},{1,2},{2,1},{3,0},{4,7},{5,6},{6,5},{7,4},{8,11},{9,10},{10,... | collective-permute-start | bytes 92168 | tf_op jit(solution)/shard_map/ppermute | solution.py:181

commit v5 on v4

--- a/solution.py
+++ b/solution.py
@@ -232,10 +232,7 @@
     send[1 - here] = rows[1].astype(jnp.bfloat16)
 
 
-def attend_kernel(flip, per_device, heads, lengths, mine, other, keys, values, out, total):
-    sec, tp = lax.axis_index("sec"), lax.axis_index("tp")
-    chip = sec >> 1
-    parity = (tp & 1) ^ flip
+def attend_blocks(per_device, heads, lengths, chip, source, keys, values, target, first):
     share = heads // 2
     slots = keys.shape[1]
     width = HEAD_WIDTH
@@ -243,15 +240,13 @@
     line = lax.broadcasted_iota(jnp.int32, (16, width), 0)
     upper = line < share
     place = lax.broadcasted_iota(jnp.int32, (16, slots), 1)
-    near, far = mine[parity].astype(jnp.float32), other[parity].astype(jnp.float32)
-    sources = (jnp.where(chip == 0, near, far), jnp.where(chip == 0, far, near))
     work = [(i, j) for i in range(2) for j in range(per_device)]
     past, fresh, new_values, columns = [], [], [], []
     for i, j in work:
-        wide = sources[i][j * 16 : (j + 1) * 16]
+        wide = source[i, j * 16 : (j + 1) * 16].astype(jnp.float32)
         zero = jnp.zeros_like(wide)
         both = jnp.concatenate([jnp.where(upper, wide, zero), jnp.where(upper, zero, wide)], axis=1)
-        column = pl.ds(pl.multiple_of((2 * i + parity) * 2 * width, 2 * width), 2 * width)
+        column = pl.ds(pl.multiple_of((2 * chip + i) * 2 * width, 2 * width), 2 * width)
         columns.append(column)
         scores = lax.dot_general(
             both.astype(jnp.bfloat16),
@@ -271,32 +266,37 @@
     inverse = 1.0 / (jnp.sum(past_exp, axis=1, keepdims=True) + fresh_exp)
     weights = (past_exp * inverse).astype(jnp.bfloat16)
     fresh_weight = (fresh_exp * inverse).astype(jnp.bfloat16).astype(jnp.float32)
-    total[...] = jnp.zeros_like(total)
     for index, (i, j) in enumerate(work):
         lines = slice(index * 16, (index + 1) * 16)
         mixed = jnp.dot(weights[lines], values[j, :, columns[index]], preferred_element_type=jnp.float32)
         mixed = jnp.where(upper, mixed[:, :width], mixed[:, width:]) + fresh_weight[lines] * new_values[index]
         for h in range(heads):
-            total[i, j : j + 1, h * width : (h + 1) * width] = mixed[h : h + 1]
-    out[...] = total[:, 0:4].astype(jnp.bfloat16)
-
-
-def forward_kernel(mine, other, send):
-    away = (lax.axis_index("tp") >> 1) ^ 1
-    send[0] = mine[away]
-    send[1] = other[away]
-
-
-def gather_kernel(mine, other, far, out, rows):
-    here = lax.axis_index("tp") >> 1
-    rows[0:4] = mine[here].astype(jnp.float32)
-    rows[4:8] = other[here].astype(jnp.float32)
-    rows[8:12] = far[0].astype(jnp.float32)
-    rows[12:16] = far[1].astype(jnp.float32)
+            target[first + i, j : j + 1, h * width : (h + 1) * width] = mixed[h : h + 1]
+
+
+def attend_near_kernel(per_device, heads, lengths, source, keys, values, out):
+    out[...] = jnp.zeros_like(out)
+    attend_blocks(per_device, heads, lengths, lax.axis_index("sec") >> 1, source, keys, values, out, 0)
+
+
+def attend_far_kernel(per_device, heads, lengths, source, near, keys, values, own, first, second, third, total):
+    chip = lax.axis_index("sec") >> 1
+    tp = lax.axis_index("tp")
+    total[...] = jnp.zeros_like(total)
+    total[2 * chip] = near[0]
+    total[2 * chip + 1] = near[1]
+    attend_blocks(per_device, heads, lengths, 1 - chip, source, keys, values, total, 2 * (1 - chip))
+    for step, target in enumerate((own, first, second, third)):
+        target[...] = total[tp ^ step, 0:4].astype(jnp.bfloat16)
+
+
+def gather_kernel(own, first, second, third, out, rows):
+    for step, part in enumerate((own, first, second, third)):
+        rows[4 * step : 4 * step + 4] = part[...].astype(jnp.float32)
     out[...] = rows[...].astype(jnp.bfloat16)
 
 
-def project_kernel(per_device, group, own, beside, across, corner, assign, resid, weight, keep, send):
+def project_kernel(per_device, group, own, beside, across, corner, assign, resid, weight, *outs):
     sec, tp = lax.axis_index("sec"), lax.axis_index("tp")
     count = assign.shape[1]
     lines = jnp.concatenate([own[...], beside[...], across[...], corner[...]], axis=0)
@@ -306,7 +306,7 @@
     for limit in range(1, 4):
         number = number + jnp.where(request >= limit * group, 1, 0)
     block, place = line >> 4, (line >> 2) & 3
-    from_sec = sec ^ block ^ (block >> 1) ^ ((place ^ (place >> 1)) & 1)
+    from_sec = sec ^ block ^ (block >> 1) ^ jnp.where(place > 0, 1, 0)
     slot = from_sec * per_device + (line & 3)
     match = (number == (tp ^ place)) & (jnp.broadcast_to(assign[...], (64, count)) == slot)
     match = jnp.where(match & ((line & 3) < per_device), 1.0, 0.0).astype(jnp.bfloat16)
@@ -316,8 +316,11 @@
     match = line == lax.broadcasted_iota(jnp.int32, (count, group), 1) + tp * group
     match = jnp.where(match, 1.0, 0.0).astype(jnp.bfloat16)
     total = total + jnp.dot(match, resid[...], preferred_element_type=jnp.float32)
-    keep[...] = total
-    send[...] = total.astype(jnp.bfloat16)
+    half = count // 2
+    for index in range(2):
+        rows = total[index * half : (index + 1) * half]
+        outs[2 * index][...] = rows
+        outs[2 * index + 1][...] = rows.astype(jnp.bfloat16)
 
 
 def add_kernel(mine, other, keep, send):
@@ -343,16 +346,18 @@
             send[:, at : at + chunk] = product[half:].astype(jnp.bfloat16)
 
 
-def gate_up_first_kernel(chunk, mine, other, gain, gate, up, keep, send, features, stream, halves, groups):
+def gate_up_first_kernel(
+    chunk, mine_a, other_a, mine_b, other_b, gain, gate, up, keep, send, features, stream, halves, groups
+):
     sec, tp = lax.axis_index("sec"), lax.axis_index("tp")
-    half = mine.shape[0] // 2
-    total = mine[...] + other[...].astype(jnp.float32)
+    half = mine_a.shape[0]
     group = stream.shape[0]
-    for index in range(mine.shape[0] // group):
-        groups[index, 0:group] = total[index * group : (index + 1) * group]
+    halves[0] = mine_a[...] + other_a[...].astype(jnp.float32)
+    halves[1] = mine_b[...] + other_b[...].astype(jnp.float32)
+    for index in range(2 * half // group):
+        at = index * group % half
+        groups[index, 0:group] = halves[index * group // half, at : at + group]
     stream[...] = groups[tp, 0:group]
-    halves[0] = total[:half]
-    halves[1] = total[half:]
     first = row_half()
     total = jnp.concatenate([halves[first], halves[1 - first]], axis=0)
     squares = jnp.sum(total * total, axis=1, keepdims=True)
@@ -482,36 +487,38 @@
         [pltpu.VMEM(block, f32)],
     )
     other = swap(away, "sec", 3)
-    sent, kept = [
-        call(
-            functools.partial(attend_kernel, flip, per_device, heads),
-            [((2, 4, head_block), bf16)],
-            (cache_len, mine, other, key_cache, cached_value_rows),
-            [pltpu.VMEM((2, 8, head_block), f32)],
-            smem=(0,),
-            resident=(3, 4),
-        )[0]
-        for flip in (1, 0)
-    ]
-
-    other = swap(sent, ("sec", "tp"), (1, 1))
-    (away,) = call(forward_kernel, [((2, 4, head_block), bf16)], (kept, other))
-    far = swap(away, ("sec", "tp"), (1, 2))
-    (own,) = call(
-        gather_kernel, [((16, head_block), bf16)], (kept, other, far), [pltpu.VMEM((16, head_block), f32)]
-    )
+    caches = (key_cache, cached_value_rows)
+    (near,) = call(
+        functools.partial(attend_near_kernel, per_device, heads),
+        [((2, 4, head_block), f32)],
+        (cache_len, mine, *caches),
+        smem=(0,),
+        resident=(2, 3),
+    )
+    own, *parts = call(
+        functools.partial(attend_far_kernel, per_device, heads),
+        [((4, head_block), bf16)] * 4,
+        (cache_len, other, near, *caches),
+        [pltpu.VMEM((4, 4, head_block), f32)],
+        smem=(0,),
+        resident=(3, 4),
+    )
+
+    parts = [swap(part, ("sec", "tp"), (1, step + 1)) for step, part in enumerate(parts)]
+    (own,) = call(gather_kernel, [((16, head_block), bf16)], (own, *parts), [pltpu.VMEM((16, head_block), f32)])
     across = swap(own, "sec", 3)
     beside = swap(own, "sec", 1)
     corner = swap(across, "sec", 1)
-    pair = [((2 * half, features), f32), ((2 * half, features), bf16)]
-    mine, away = call(
+    pair = [((half, features), f32), ((half, features), bf16)]
+    mine_a, away_a, mine_b, away_b = call(
         functools.partial(project_kernel, per_device, group),
-        pair,
+        pair * 2,
         (own, beside, across, corner, assign, resid, out_weight),
         resident=(6,),
     )
-    mine, away = call(add_kernel, pair, (mine, swap(away, "tp", 1)))
-    other = swap(away, "tp", 2)
+    mine_a, away_a = call(add_kernel, pair, (mine_a, swap(away_a, "tp", 1)))
+    mine_b, away_b = call(add_kernel, pair, (mine_b, swap(away_b, "tp", 2)))
+    other_a, other_b = swap(away_a, "tp", 2), swap(away_b, "tp", 1)
 
     chunk = min(512, width // 2)
     mine, away, lines, stream = call(
@@ -522,9 +529,9 @@
             ((2 * half, features), bf16),
             ((group, features), f32),
         ],
-        (mine, other, gain, gate_weight, up_weight),
+        (mine_a, other_a, mine_b, other_b, gain, gate_weight, up_weight),
         [pltpu.VMEM((2, half, features), f32), pltpu.VMEM((4, 16, features), f32)],
-        resident=(3, 4),
+        resident=(5, 6),
     )
     away, squares = call(
         pair_sum_kernel, [((half, width + 128), bf16), ((half, 128), f32)], (mine, swap(away, "sec", 1))

time: 64.6 us -> 61.3 us (0.949)
  starting transfers between devices: 23.4 us -> 19.5 us
  local copies, waits for them, and re-layouts: 0.08 us -> 1.71 us
  waiting for transfers between devices: 28.8 us -> 27.8 us
    ppermute x19 -> x22, starting transfers between devices: 23.4 us -> 19.5 us  [swap(): return lax.ppermute(value, axis, [(i, i ^ step) for i in range(total)])]
    unnamed x32, local copies, waits for them, and re-layouts: 0.08 us -> 1.71 us
    ppermute x19 -> x22, waiting for transfers between devices: 28.8 us -> 27.8 us  [swap(): return lax.ppermute(value, axis, [(i, i ^ step) for i in range(total)])]
  transfers between devices with their start and end apart: 19 -> 22, of which waited for: 15 -> 17; matrix products, arithmetic and copies ran while one was open for 0% -> 0% of each run, Pallas kernels for 8% -> 9%
where the time goes in v5:
time: 61.3 us; the launch traced here: 61.2 us
  waiting for transfers between devices  27.8 us (45%)
  starting transfers between devices  19.5 us (32%)
  Pallas kernels  11.9 us (19%)
  local copies, waits for them, and re-layouts  1.71 us (3%)
    ppermute x22, waiting for transfers between devices, swap(): return lax.ppermute(value, axis, [(i, i ^ step) for i in range(total)])  27.8 us
    ppermute x22, starting transfers between devices, swap(): return lax.ppermute(value, axis, [(i, i ^ step) for i in range(total)])  19.5 us
    pallas_call x15, Pallas kernels, call(): pl.pallas_call(kernel, out_shape=[jax.ShapeDtypeStruct(shape, dtype) for...  11.9 us
    unnamed x32, local copies, waits for them, and re-layouts  1.71 us
  transfers between devices with their start and end apart: 22, of which 17 were waited for; matrix products, arithmetic and copies ran while one was open for 0% of the time, Pallas kernels for 9%

profile of v5, /device:TPU:0, one launch (start us, length us, event | category | flops | bytes accessed | tf_op | source)
XLA Modules:
  0.0 61.2 jit_solution(5447788361872113263)
XLA Ops:
  0.0 0.5 collective-permute-start.1
  0.5 0.1 collective-permute-start
  0.5 1.2 %shard_map.118.own = bf16[2,48,128]{2,1,0:T(8,128)(2,1)S(1)} custom-call(bf16[12,1280]{1,0:T(8,128)(2,1)} %query.1, bf16[12,512]{1,0:T(8,128)(2,1)} %pairs.1, s32[1,48]{1,0:T(1,128)} %bitcast.7), custom_call_target="tpu_custom_call" | custom-call | flops 4000000000 | tf_op jit(solution)/shard_map/pallas_call | solution.py:159
  1.8 0.0 copy-start.1
  1.8 0.0 copy-start.2
  1.8 0.0 copy-start.4
  1.8 0.0 collective-permute-done.1.pairs
  1.8 0.1 collective-permute-done.query
  1.9 0.4 shard_map.119
  2.3 2.7 %collective-permute-start.2 = (bf16[2,48,128]{2,1,0:T(8,128)(2,1)S(1)}, bf16[2,48,128]{2,1,0:T(8,128)(2,1)S(1)}, u32[]{:S(2)}, u32[]{:S(2)}) collective-permute-start(bf16[2,48,128]{2,1,0:T(8,128)(2,1)S(1)} %get-tuple-element.31), channel_id=1, source_target_pairs={{0,12},{4,8},{8,4},{12,0},{1,13},{5,9},{9,5},{13,1},{2,14},{6,10},... | collective-permute-start | bytes 73736 | tf_op jit(solution)/shard_map/ppermute | solution.py:181
  5.0 1.1 %shard_map.120.near = f32[2,4,1280]{2,1,0:T(4,128)S(1)} custom-call(s32[3]{0:T(128)S(1)} %copy-done.4, bf16[2,48,128]{2,1,0:T(8,128)(2,1)S(1)} %get-tuple-element.32.source, bf16[3,224,1024]{2,1,0:T(8,128)(2,1)S(1)} %copy-done.1, bf16[3,224,1024]{2,1,0:T(8,128)(2,1)S(1)} %copy-done.2), custom_call_target="tpu_custom_call" | custom-call | flops 4000000000 | tf_op jit(solution)/shard_map/pallas_call | solution.py:159
  6.1 0.4 collective-permute-done.2.source
  6.5 1.2 %shard_map.121 = (bf16[4,1280]{1,0:T(4,128)(2,1)S(1)}, bf16[4,1280]{1,0:T(4,128)(2,1)S(1)}, bf16[4,1280]{1,0:T(4,128)(2,1)S(1)}, bf16[4,1280]{1,0:T(4,128)(2,1)S(1)}) custom-call(s32[3]{0:T(128)S(1)} %copy-done.4, bf16[2,48,128]{2,1,0:T(8,128)(2,1)S(1)} %collective-permute-done.2.source, f32[2,4,1280]{2,1,0:T(4,128)S(1)} %shard_map.120.near, ...), custom_call_target="tpu_custom_call" | custom-call | flops 4000000000 | tf_op jit(solution)/shard_map/pallas_call | solution.py:159
  7.7 0.0 copy-start
  7.7 0.0 copy-start.3
  7.7 1.9 %collective-permute-start.3 = (bf16[4,1280]{1,0:T(4,128)(2,1)S(1)}, bf16[4,1280]{1,0:T(4,128)(2,1)S(1)}, u32[]{:S(2)}, u32[]{:S(2)}) collective-permute-start(bf16[4,1280]{1,0:T(4,128)(2,1)S(1)} %get-tuple-element.34), channel_id=1, source_target_pairs={{0,5},{1,4},{2,7},{3,6},{4,1},{5,0},{6,3},{7,2},{8,13},{9,12},{10,... | collective-permute-start | bytes 30728 | tf_op jit(solution)/shard_map/ppermute | solution.py:181
  9.6 2.6 %collective-permute-start.4 = (bf16[4,1280]{1,0:T(4,128)(2,1)S(1)}, bf16[4,1280]{1,0:T(4,128)(2,1)S(1)}, u32[]{:S(2)}, u32[]{:S(2)}) collective-permute-start(bf16[4,1280]{1,0:T(4,128)(2,1)S(1)} %get-tuple-element.35), channel_id=1, source_target_pairs={{0,6},{1,7},{2,4},{3,5},{4,2},{5,3},{6,0},{7,1},{8,14},{9,15},{10,... | collective-permute-start | bytes 30728 | tf_op jit(solution)/shard_map/ppermute | solution.py:181
  12.2 0.0 collective-permute-start.5
  12.2 0.0 collective-permute-done.3.first
  12.2 1.4 %collective-permute-done.4.second = bf16[4,1280]{1,0:T(4,128)(2,1)S(1)} collective-permute-done((bf16[4,1280]{1,0:T(4,128)(2,1)S(1)}, bf16[4,1280]{1,0:T(4,128)(2,1)S(1)}, u32[]{:S(2)}, u32[]{:S(2)}) %collective-permute-start.4) | collective-permute-done | bytes 10272 | tf_op jit(solution)/shard_map/ppermute | solution.py:181
  13.6 3.5 %collective-permute-done.5.third = bf16[4,1280]{1,0:T(4,128)(2,1)S(1)} collective-permute-done((bf16[4,1280]{1,0:T(4,128)(2,1)S(1)}, bf16[4,1280]{1,0:T(4,128)(2,1)S(1)}, u32[]{:S(2)}, u32[]{:S(2)}) %collective-permute-start.5) | collective-permute-done | bytes 10272 | tf_op jit(solution)/shard_map/ppermute | solution.py:181
  17.1 1.3 %collective-permute-start.7 = (bf16[16,1280]{1,0:T(8,128)(2,1)S(1)}, bf16[16,1280]{1,0:T(8,128)(2,1)S(1)}, u32[]{:S(2)}, u32[]{:S(2)}) collective-permute-start(bf16[16,1280]{1,0:T(8,128)(2,1)S(1)} %shard_map.122.own), channel_id=1, source_target_pairs={{0,12},{4,8},{8,4},{12,0},{1,13},{5,9},{9,5},{13,1},{2,14},{6,10},... | collective-permute-start | bytes 122888 | tf_op jit(solution)/shard_map/ppermute | solution.py:181
  18.4 0.4 collective-permute-start.6
  18.8 2.0 %collective-permute-done.7.across = bf16[16,1280]{1,0:T(8,128)(2,1)S(1)} collective-permute-done((bf16[16,1280]{1,0:T(8,128)(2,1)S(1)}, bf16[16,1280]{1,0:T(8,128)(2,1)S(1)}, u32[]{:S(2)}, u32[]{:S(2)}) %collective-permute-start.7) | collective-permute-done | bytes 40992 | tf_op jit(solution)/shard_map/ppermute | solution.py:181
  20.8 0.1 collective-permute-start.8
  20.9 0.0 collective-permute-done.6.beside
  20.9 1.1 %collective-permute-done.8.corner = bf16[16,1280]{1,0:T(8,128)(2,1)S(1)} collective-permute-done((bf16[16,1280]{1,0:T(8,128)(2,1)S(1)}, bf16[16,1280]{1,0:T(8,128)(2,1)S(1)}, u32[]{:S(2)}, u32[]{:S(2)}) %collective-permute-start.8) | collective-permute-done | bytes 40992 | tf_op jit(solution)/shard_map/ppermute | solution.py:181
  22.0 0.8 %shard_map.123 = (f32[24,1280]{1,0:T(8,128)S(1)}, bf16[24,1280]{1,0:T(8,128)(2,1)S(1)}, f32[24,1280]{1,0:T(8,128)S(1)}, bf16[24,1280]{1,0:T(8,128)(2,1)S(1)}) custom-call(bf16[16,1280]{1,0:T(8,128)(2,1)S(1)} %shard_map.122.own, bf16[16,1280]{1,0:T(8,128)(2,1)S(1)} %collective-permute-done.6.beside, bf16[16,1280]{1,0:T(8,128)(2,1)S(1)} %collective-permute-done.7.across, ...), custom_call_target="tpu_custom_call" | custom-call | flops 4000000000 | tf_op jit(solution)/shard_map/pallas_call | solution.py:159
  22.8 0.1 collective-permute-start.9
  22.9 0.6 collective-permute-start.11
  23.5 4.7 %collective-permute-done.9.other = bf16[24,1280]{1,0:T(8,128)(2,1)S(1)} collective-permute-done((bf16[24,1280]{1,0:T(8,128)(2,1)S(1)}, bf16[24,1280]{1,0:T(8,128)(2,1)S(1)}, u32[]{:S(2)}, u32[]{:S(2)}) %collective-permute-start.9) | collective-permute-done | bytes 61472 | tf_op jit(solution)/shard_map/ppermute | solution.py:181
  28.2 0.0 copy-start.6
  28.2 0.1 collective-permute-start.10
  28.3 0.5 collective-permute-done.11.other
  28.8 1.4 %collective-permute-start.12 = (bf16[24,1280]{1,0:T(8,128)(2,1)S(1)}, bf16[24,1280]{1,0:T(8,128)(2,1)S(1)}, u32[]{:S(2)}, u32[]{:S(2)}) collective-permute-start(bf16[24,1280]{1,0:T(8,128)(2,1)S(1)} %get-tuple-element.44), channel_id=1, source_target_pairs={{0,1},{1,0},{2,3},{3,2},{4,5},{5,4},{6,7},{7,6},{8,9},{9,8},{10,11... | collective-permute-start | bytes 184328 | tf_op jit(solution)/shard_map/ppermute | solution.py:181
  30.1 3.4 %collective-permute-done.10.other_a = bf16[24,1280]{1,0:T(8,128)(2,1)S(1)} collective-permute-done((bf16[24,1280]{1,0:T(8,128)(2,1)S(1)}, bf16[24,1280]{1,0:T(8,128)(2,1)S(1)}, u32[]{:S(2)}, u32[]{:S(2)}) %collective-permute-start.10) | collective-permute-done | bytes 61472 | tf_op jit(solution)/shard_map/ppermute | solution.py:181
  33.5 0.2 collective-permute-done.12.other_b
  33.7 0.3 slice-done.4
  34.0 0.7 %slice-done.2 = s8[2097152]{0:T(1024)(128)(4,1)S(1)} async-done(((s8[10485760]{0:T(1024)(128)(4,1)}), s8[2097152]{0:T(1024)(128)(4,1)S(1)}, s32[]{:S(2)}) %slice-start.2) | async-done | bytes 2097176
  34.8 0.6 slice-done.5
  35.4 2.0 %shard_map.126 = (f32[24,4224]{1,0:T(8,128)S(1)}, bf16[24,4224]{1,0:T(8,128)(2,1)S(1)}, bf16[48,1280]{1,0:T(8,128)(2,1)S(1)}, f32[12,1280]{1,0:T(8,128)S(1)}) custom-call(f32[24,1280]{1,0:T(8,128)S(1)} %get-tuple-element.39.mine_a, bf16[24,1280]{1,0:T(8,128)(2,1)S(1)} %collective-permute-done.10.other_a, f32[24,1280]{1,0:T(8,128)S(1)} %get-tuple-element.43.mine_b, ...), custom_call_target="tpu_custom_call" | custom-call | flops 4000000000 | tf_op jit(solution)/shard_map/pallas_call | solution.py:159
  37.4 0.1 collective-permute-start.14
  37.4 1.4 %collective-permute-done.14.other = bf16[24,4224]{1,0:T(8,128)(2,1)S(1)} collective-permute-done((bf16[24,4224]{1,0:T(8,128)(2,1)S(1)}, bf16[24,4224]{1,0:T(8,128)(2,1)S(1)}, u32[]{:S(2)}, u32[]{:S(2)}) %collective-permute-start.14) | collective-permute-done | bytes 202784 | tf_op jit(solution)/shard_map/ppermute | solution.py:181
  38.9 0.2 shard_map.128
  39.1 1.2 %collective-permute-start.15 = (bf16[24,4224]{1,0:T(8,128)(2,1)S(1)}, bf16[24,4224]{1,0:T(8,128)(2,1)S(1)}, u32[]{:S(2)}, u32[]{:S(2)}) collective-permute-start(bf16[24,4224]{1,0:T(8,128)(2,1)S(1)} %get-tuple-element.51), channel_id=1, source_target_pairs={{0,12},{4,8},{8,4},{12,0},{1,13},{5,9},{9,5},{13,1},{2,14},{6,10},... | collective-permute-start | bytes 608264 | tf_op jit(solution)/shard_map/ppermute | solution.py:181
  40.3 1.9 %shard_map.127 = (f32[24,4096]{1,0:T(8,128)S(1)}, bf16[24,4096]{1,0:T(8,128)(2,1)S(1)}) custom-call(bf16[48,1280]{1,0:T(8,128)(2,1)S(1)} %get-tuple-element.46.features, bf16[1280,4096]{1,0:T(8,128)(2,1)S(1)} %bitcast.2, bf16[1280,4096]{1,0:T(8,128)(2,1)S(1)} %bitcast.4), custom_call_target="tpu_custom_call" | custom-call | flops 4000000000 | tf_op jit(solution)/shard_map/pallas_call | solution.py:159
  42.2 0.4 collective-permute-start.13
  42.7 1.1 %collective-permute-done.13.beside = bf16[24,4096]{1,0:T(8,128)(2,1)S(1)} collective-permute-done((bf16[24,4096]{1,0:T(8,128)(2,1)S(1)}, bf16[24,4096]{1,0:T(8,128)(2,1)S(1)}, u32[]{:S(2)}, u32[]{:S(2)}) %collective-permute-start.13) | collective-permute-done | bytes 196640 | tf_op jit(solution)/shard_map/ppermute | solution.py:181
  43.7 2.4 %collective-permute-done.15.across = bf16[24,4224]{1,0:T(8,128)(2,1)S(1)} collective-permute-done((bf16[24,4224]{1,0:T(8,128)(2,1)S(1)}, bf16[24,4224]{1,0:T(8,128)(2,1)S(1)}, u32[]{:S(2)}, u32[]{:S(2)}) %collective-permute-start.15) | collective-permute-done | bytes 202784 | tf_op jit(solution)/shard_map/ppermute | solution.py:181
  46.1 0.2 shard_map.129.mine
  46.3 1.3 %collective-permute-start.16 = (bf16[24,2048]{1,0:T(8,128)(2,1)S(1)}, bf16[24,2048]{1,0:T(8,128)(2,1)S(1)}, u32[]{:S(2)}, u32[]{:S(2)}) collective-permute-start(bf16[24,2048]{1,0:T(8,128)(2,1)S(1)} %shard_map.129.mine), channel_id=1, source_target_pairs={{0,12},{4,8},{8,4},{12,0},{1,13},{5,9},{9,5},{13,1},{2,14},{6,10},... | collective-permute-start | bytes 294920 | tf_op jit(solution)/shard_map/ppermute | solution.py:181
  47.6 0.4 collective-permute-start.18
  48.0 3.2 %collective-permute-done.16.mine = bf16[24,2048]{1,0:T(8,128)(2,1)S(1)} collective-permute-done((bf16[24,2048]{1,0:T(8,128)(2,1)S(1)}, bf16[24,2048]{1,0:T(8,128)(2,1)S(1)}, u32[]{:S(2)}, u32[]{:S(2)}) %collective-permute-start.16) | collective-permute-done | bytes 98336 | tf_op jit(solution)/shard_map/ppermute | solution.py:181
  51.2 0.1 collective-permute-start.17
  51.3 1.0 %shard_map.130.before = f32[48,1280]{1,0:T(8,128)S(1)} custom-call(bf16[24,2048]{1,0:T(8,128)(2,1)S(1)} %shard_map.129.mine, bf16[24,2048]{1,0:T(8,128)(2,1)S(1)} %collective-permute-done.18.other, bf16[4096,1280]{1,0:T(8,128)(2,1)S(1)} %bitcast.6), custom_call_target="tpu_custom_call" | custom-call | flops 4000000000 | tf_op jit(solution)/shard_map/pallas_call | solution.py:159
  52.4 0.1 collective-permute-done.17.other
  52.5 1.0 %shard_map.131 = (f32[12,1280]{1,0:T(8,128)S(1)}, bf16[12,1280]{1,0:T(8,128)(2,1)S(1)}, bf16[12,1280]{1,0:T(8,128)(2,1)S(1)}, bf16[12,1280]{1,0:T(8,128)(2,1)S(1)}) custom-call(bf16[24,2048]{1,0:T(8,128)(2,1)S(1)} %collective-permute-done.16.mine, bf16[24,2048]{1,0:T(8,128)(2,1)S(1)} %collective-permute-done.17.other, f32[48,1280]{1,0:T(8,128)S(1)} %shard_map.130.before, ...), custom_call_target="tpu_custom_call" | custom-call | flops 4000000000 | tf_op jit(solution)/shard_map/pallas_call | solution.py:159
  53.5 0.1 collective-permute-start.19
  53.6 0.3 collective-permute-start.20
  53.9 4.0 %collective-permute-start.21 = (bf16[12,1280]{1,0:T(8,128)(2,1)S(1)}, bf16[12,1280]{1,0:T(8,128)(2,1)S(1)}, u32[]{:S(2)}, u32[]{:S(2)}) collective-permute-start(bf16[12,1280]{1,0:T(8,128)(2,1)S(1)} %get-tuple-element.56), channel_id=1, source_target_pairs={{0,3},{1,2},{2,1},{3,0},{4,7},{5,6},{6,5},{7,4},{8,11},{9,10},{10,... | collective-permute-start | bytes 92168 | tf_op jit(solution)/shard_map/ppermute | solution.py:181
  58.0 0.1 collective-permute-done.19.first
  58.0 2.5 %collective-permute-done.20.second = bf16[12,1280]{1,0:T(8,128)(2,1)S(1)} collective-permute-done((bf16[12,1280]{1,0:T(8,128)(2,1)S(1)}, bf16[12,1280]{1,0:T(8,128)(2,1)S(1)}, u32[]{:S(2)}, u32[]{:S(2)}) %collective-permute-start.20) | collective-permute-done | bytes 30752 | tf_op jit(solution)/shard_map/ppermute | solution.py:181
  60.5 0.0 collective-permute-done.21.third
  60.5 0.6 %shard_map.132 = bf16[12,1280]{1,0:T(8,128)(2,1)} custom-call(f32[12,1280]{1,0:T(8,128)S(1)} %get-tuple-element.45.stream, f32[12,1280]{1,0:T(8,128)S(1)} %get-tuple-element.53.mine, bf16[12,1280]{1,0:T(8,128)(2,1)S(1)} %collective-permute-done.19.first, bf16[12,1280]{1,0:T(8,128)(2,1)S(1)} %collective-permute-done.20.second, ...), custom_call_target="tpu_custom_call" | custom-call | flops 4000000000 | tf_op jit(solution)/shard_map/pallas_call | solution.py:159
  (31 shorter events, 0.1 us)
Async XLA Ops:
  0.0 1.9 %copy-start.5 = (s32[48]{0:T(128)S(1)}, s32[48]{0:T(128)}, u32[]{:S(2)}) copy-start(s32[48]{0:T(128)} %param.18) | copy-start | bytes 580
  0.0 1.8 %collective-permute-start.1 = (bf16[12,512]{1,0:T(8,128)(2,1)}, bf16[12,512]{1,0:T(8,128)(2,1)S(1)}, u32[]{:S(2)}, u32[]{:S(2)}) collective-permute-start(bf16[12,512]{1,0:T(8,128)(2,1)} %pairs.1), channel_id=1, source_target_pairs={{0,4},{4,0},{8,12},{12,8},{1,5},{5,1},{9,13},{13,9},{2,6},{6,2},{1... | collective-permute-start | bytes 36872 | tf_op jit(solution)/shard_map/ppermute | solution.py:181
  0.5 1.4 %collective-permute-start = (bf16[12,1280]{1,0:T(8,128)(2,1)}, bf16[12,1280]{1,0:T(8,128)(2,1)S(1)}, u32[]{:S(2)}, u32[]{:S(2)}) collective-permute-start(bf16[12,1280]{1,0:T(8,128)(2,1)} %query.1), channel_id=1, source_target_pairs={{0,4},{4,0},{8,12},{12,8},{1,5},{5,1},{9,13},{13,9},{2,6},{6,2},{1... | collective-permute-start | bytes 92168 | tf_op jit(solution)/shard_map/ppermute | solution.py:181
  1.8 3.2 %copy-start.1 = (bf16[3,224,1024]{2,1,0:T(8,128)(2,1)S(1)}, bf16[3,224,1024]{2,1,0:T(8,128)(2,1)}, u32[]{:S(2)}) copy-start(bf16[3,224,1024]{2,1,0:T(8,128)(2,1)} %keys.3) | copy-start | bytes 4128772
  1.8 3.2 %copy-start.2 = (bf16[3,224,1024]{2,1,0:T(8,128)(2,1)S(1)}, bf16[3,224,1024]{2,1,0:T(8,128)(2,1)}, u32[]{:S(2)}) copy-start(bf16[3,224,1024]{2,1,0:T(8,128)(2,1)} %values.3) | copy-start | bytes 4128772
  1.8 3.2 %copy-start.4 = (s32[3]{0:T(128)S(1)}, s32[3]{0:T(128)}, u32[]{:S(2)}) copy-start(s32[3]{0:T(128)} %lengths.3) | copy-start | bytes 40
  2.3 4.2 %collective-permute-start.2 = (bf16[2,48,128]{2,1,0:T(8,128)(2,1)S(1)}, bf16[2,48,128]{2,1,0:T(8,128)(2,1)S(1)}, u32[]{:S(2)}, u32[]{:S(2)}) collective-permute-start(bf16[2,48,128]{2,1,0:T(8,128)(2,1)S(1)} %get-tuple-element.31), channel_id=1, source_target_pairs={{0,12},{4,8},{8,4},{12,0},{1,13},{5,9},{9,5},{13,1},{2,14},{6,10},... | collective-permute-start | bytes 73736 | tf_op jit(solution)/shard_map/ppermute | solution.py:181
  7.7 14.3 %copy-start = (bf16[1280,1280]{1,0:T(8,128)(2,1)S(1)}, bf16[1280,1280]{1,0:T(8,128)(2,1)}, u32[]{:S(2)}) copy-start(bf16[1280,1280]{1,0:T(8,128)(2,1)} %weight.3) | copy-start | bytes 9830404
  7.7 14.3 %copy-start.3 = (bf16[12,1280]{1,0:T(8,128)(2,1)S(1)}, bf16[12,1280]{1,0:T(8,128)(2,1)}, u32[]{:S(2)}) copy-start(bf16[12,1280]{1,0:T(8,128)(2,1)} %resid.1) | copy-start | bytes 92164
  7.7 4.5 %collective-permute-start.3 = (bf16[4,1280]{1,0:T(4,128)(2,1)S(1)}, bf16[4,1280]{1,0:T(4,128)(2,1)S(1)}, u32[]{:S(2)}, u32[]{:S(2)}) collective-permute-start(bf16[4,1280]{1,0:T(4,128)(2,1)S(1)} %get-tuple-element.34), channel_id=1, source_target_pairs={{0,5},{1,4},{2,7},{3,6},{4,1},{5,0},{6,3},{7,2},{8,13},{9,12},{10,... | collective-permute-start | bytes 30728 | tf_op jit(solution)/shard_map/ppermute | solution.py:181
  9.6 4.0 %collective-permute-start.4 = (bf16[4,1280]{1,0:T(4,128)(2,1)S(1)}, bf16[4,1280]{1,0:T(4,128)(2,1)S(1)}, u32[]{:S(2)}, u32[]{:S(2)}) collective-permute-start(bf16[4,1280]{1,0:T(4,128)(2,1)S(1)} %get-tuple-element.35), channel_id=1, source_target_pairs={{0,6},{1,7},{2,4},{3,5},{4,2},{5,3},{6,0},{7,1},{8,14},{9,15},{10,... | collective-permute-start | bytes 30728 | tf_op jit(solution)/shard_map/ppermute | solution.py:181
  12.2 4.9 %collective-permute-start.5 = (bf16[4,1280]{1,0:T(4,128)(2,1)S(1)}, bf16[4,1280]{1,0:T(4,128)(2,1)S(1)}, u32[]{:S(2)}, u32[]{:S(2)}) collective-permute-start(bf16[4,1280]{1,0:T(4,128)(2,1)S(1)} %get-tuple-element.36), channel_id=1, source_target_pairs={{0,7},{1,6},{2,5},{3,4},{4,3},{5,2},{6,1},{7,0},{8,15},{9,14},{10,... | collective-permute-start | bytes 30728 | tf_op jit(solution)/shard_map/ppermute | solution.py:181
  17.1 3.6 %collective-permute-start.7 = (bf16[16,1280]{1,0:T(8,128)(2,1)S(1)}, bf16[16,1280]{1,0:T(8,128)(2,1)S(1)}, u32[]{:S(2)}, u32[]{:S(2)}) collective-permute-start(bf16[16,1280]{1,0:T(8,128)(2,1)S(1)} %shard_map.122.own), channel_id=1, source_target_pairs={{0,12},{4,8},{8,4},{12,0},{1,13},{5,9},{9,5},{13,1},{2,14},{6,10},... | collective-permute-start | bytes 122888 | tf_op jit(solution)/shard_map/ppermute | solution.py:181
  18.4 2.5 %collective-permute-start.6 = (bf16[16,1280]{1,0:T(8,128)(2,1)S(1)}, bf16[16,1280]{1,0:T(8,128)(2,1)S(1)}, u32[]{:S(2)}, u32[]{:S(2)}) collective-permute-start(bf16[16,1280]{1,0:T(8,128)(2,1)S(1)} %shard_map.122.own), channel_id=1, source_target_pairs={{0,4},{4,0},{8,12},{12,8},{1,5},{5,1},{9,13},{13,9},{2,6},{6,2},{1... | collective-permute-start | bytes 122888 | tf_op jit(solution)/shard_map/ppermute | solution.py:181
  20.8 1.2 %collective-permute-start.8 = (bf16[16,1280]{1,0:T(8,128)(2,1)S(1)}, bf16[16,1280]{1,0:T(8,128)(2,1)S(1)}, u32[]{:S(2)}, u32[]{:S(2)}) collective-permute-start(bf16[16,1280]{1,0:T(8,128)(2,1)S(1)} %collective-permute-done.7.across), channel_id=1, source_target_pairs={{0,4},{4,0},{8,12},{12,8},{1,5},{5,1},{9,13},{13,9},{2,6},{6,2},{1... | collective-permute-start | bytes 122888 | tf_op jit(solution)/shard_map/ppermute | solution.py:181
  22.8 5.3 %collective-permute-start.9 = (bf16[24,1280]{1,0:T(8,128)(2,1)S(1)}, bf16[24,1280]{1,0:T(8,128)(2,1)S(1)}, u32[]{:S(2)}, u32[]{:S(2)}) collective-permute-start(bf16[24,1280]{1,0:T(8,128)(2,1)S(1)} %get-tuple-element.38), channel_id=1, source_target_pairs={{0,1},{1,0},{2,3},{3,2},{4,5},{5,4},{6,7},{7,6},{8,9},{9,8},{10,11... | collective-permute-start | bytes 184328 | tf_op jit(solution)/shard_map/ppermute | solution.py:181
  22.9 5.8 %collective-permute-start.11 = (bf16[24,1280]{1,0:T(8,128)(2,1)S(1)}, bf16[24,1280]{1,0:T(8,128)(2,1)S(1)}, u32[]{:S(2)}, u32[]{:S(2)}) collective-permute-start(bf16[24,1280]{1,0:T(8,128)(2,1)S(1)} %get-tuple-element.42), channel_id=1, source_target_pairs={{0,2},{1,3},{2,0},{3,1},{4,6},{5,7},{6,4},{7,5},{8,10},{9,11},{10,... | collective-permute-start | bytes 184328 | tf_op jit(solution)/shard_map/ppermute | solution.py:181
  28.2 5.6 %slice-start = ((s8[10485760]{0:T(1024)(128)(4,1)}), s8[4194304]{0:T(1024)(128)(4,1)S(1)}, s32[]{:S(2)}) async-start(s8[10485760]{0:T(1024)(128)(4,1)} %bitcast.1), calls=%async_computation | async-start | bytes 8388608
  28.2 5.6 %slice-start.1 = ((s8[10485760]{0:T(1024)(128)(4,1)}), s8[4194304]{0:T(1024)(128)(4,1)S(1)}, s32[]{:S(2)}) async-start(s8[10485760]{0:T(1024)(128)(4,1)} %bitcast.1), calls=%async_computation.1 | async-start | bytes 8388608
  28.2 5.6 %slice-start.3 = ((s8[10485760]{0:T(1024)(128)(4,1)}), s8[4194304]{0:T(1024)(128)(4,1)S(1)}, s32[]{:S(2)}) async-start(s8[10485760]{0:T(1024)(128)(4,1)} %bitcast.3), calls=%async_computation.3 | async-start | bytes 8388608
  28.2 5.9 %slice-start.4 = ((s8[10485760]{0:T(1024)(128)(4,1)}), s8[4194304]{0:T(1024)(128)(4,1)S(1)}, s32[]{:S(2)}) async-start(s8[10485760]{0:T(1024)(128)(4,1)} %bitcast.3), calls=%async_computation.4 | async-start | bytes 8388608
  28.2 1.9 %copy-start.6 = (bf16[1280]{0:T(1024)(128)(2,1)S(1)}, bf16[1280]{0:T(1024)(128)(2,1)}, u32[]{:S(2)}) copy-start(bf16[1280]{0:T(1024)(128)(2,1)} %param.20) | copy-start | bytes 7684
  28.2 5.3 %collective-permute-start.10 = (bf16[24,1280]{1,0:T(8,128)(2,1)S(1)}, bf16[24,1280]{1,0:T(8,128)(2,1)S(1)}, u32[]{:S(2)}, u32[]{:S(2)}) collective-permute-start(bf16[24,1280]{1,0:T(8,128)(2,1)S(1)} %get-tuple-element.40), channel_id=1, source_target_pairs={{0,2},{1,3},{2,0},{3,1},{4,6},{5,7},{6,4},{7,5},{8,10},{9,11},{10,... | collective-permute-start | bytes 184328 | tf_op jit(solution)/shard_map/ppermute | solution.py:181
  28.7 6.0 %slice-start.2 = ((s8[10485760]{0:T(1024)(128)(4,1)}), s8[2097152]{0:T(1024)(128)(4,1)S(1)}, s32[]{:S(2)}) async-start(s8[10485760]{0:T(1024)(128)(4,1)} %bitcast.1), calls=%async_computation.2 | async-start | bytes 4194304
  28.7 6.6 %slice-start.5 = ((s8[10485760]{0:T(1024)(128)(4,1)}), s8[2097152]{0:T(1024)(128)(4,1)S(1)}, s32[]{:S(2)}) async-start(s8[10485760]{0:T(1024)(128)(4,1)} %bitcast.3), calls=%async_computation.5 | async-start | bytes 4194304
  28.8 4.9 %collective-permute-start.12 = (bf16[24,1280]{1,0:T(8,128)(2,1)S(1)}, bf16[24,1280]{1,0:T(8,128)(2,1)S(1)}, u32[]{:S(2)}, u32[]{:S(2)}) collective-permute-start(bf16[24,1280]{1,0:T(8,128)(2,1)S(1)} %get-tuple-element.44), channel_id=1, source_target_pairs={{0,1},{1,0},{2,3},{3,2},{4,5},{5,4},{6,7},{7,6},{8,9},{9,8},{10,11... | collective-permute-start | bytes 184328 | tf_op jit(solution)/shard_map/ppermute | solution.py:181
  37.4 1.5 %collective-permute-start.14 = (bf16[24,4224]{1,0:T(8,128)(2,1)S(1)}, bf16[24,4224]{1,0:T(8,128)(2,1)S(1)}, u32[]{:S(2)}, u32[]{:S(2)}) collective-permute-start(bf16[24,4224]{1,0:T(8,128)(2,1)S(1)} %get-tuple-element.50), channel_id=1, source_target_pairs={{0,4},{4,0},{8,12},{12,8},{1,5},{5,1},{9,13},{13,9},{2,6},{6,2},{1... | collective-permute-start | bytes 608264 | tf_op jit(solution)/shard_map/ppermute | solution.py:181
  39.1 7.0 %collective-permute-start.15 = (bf16[24,4224]{1,0:T(8,128)(2,1)S(1)}, bf16[24,4224]{1,0:T(8,128)(2,1)S(1)}, u32[]{:S(2)}, u32[]{:S(2)}) collective-permute-start(bf16[24,4224]{1,0:T(8,128)(2,1)S(1)} %get-tuple-element.51), channel_id=1, source_target_pairs={{0,12},{4,8},{8,4},{12,0},{1,13},{5,9},{9,5},{13,1},{2,14},{6,10},... | collective-permute-start | bytes 608264 | tf_op jit(solution)/shard_map/ppermute | solution.py:181
  40.3 11.0 %slice-start.6 = ((s8[10485760]{0:T(1024)(128)(4,1)}), s8[4194304]{0:T(1024)(128)(4,1)S(1)}, s32[]{:S(2)}) async-start(s8[10485760]{0:T(1024)(128)(4,1)} %bitcast.5), calls=%async_computation.6 | async-start | bytes 8388608
  40.3 11.0 %slice-start.7 = ((s8[10485760]{0:T(1024)(128)(4,1)}), s8[4194304]{0:T(1024)(128)(4,1)S(1)}, s32[]{:S(2)}) async-start(s8[10485760]{0:T(1024)(128)(4,1)} %bitcast.5), calls=%async_computation.7 | async-start | bytes 8388608
  42.2 1.5 %collective-permute-start.13 = (bf16[24,4096]{1,0:T(8,128)(2,1)S(1)}, bf16[24,4096]{1,0:T(8,128)(2,1)S(1)}, u32[]{:S(2)}, u32[]{:S(2)}) collective-permute-start(bf16[24,4096]{1,0:T(8,128)(2,1)S(1)} %get-tuple-element.48), channel_id=1, source_target_pairs={{0,4},{4,0},{8,12},{12,8},{1,5},{5,1},{9,13},{13,9},{2,6},{6,2},{1... | collective-permute-start | bytes 589832 | tf_op jit(solution)/shard_map/ppermute | solution.py:181
  46.1 5.2 %slice-start.8 = ((s8[10485760]{0:T(1024)(128)(4,1)}), s8[2097152]{0:T(1024)(128)(4,1)S(1)}, s32[]{:S(2)}) async-start(s8[10485760]{0:T(1024)(128)(4,1)} %bitcast.5), calls=%async_computation.8 | async-start | bytes 4194304
  46.3 4.8 %collective-permute-start.16 = (bf16[24,2048]{1,0:T(8,128)(2,1)S(1)}, bf16[24,2048]{1,0:T(8,128)(2,1)S(1)}, u32[]{:S(2)}, u32[]{:S(2)}) collective-permute-start(bf16[24,2048]{1,0:T(8,128)(2,1)S(1)} %shard_map.129.mine), channel_id=1, source_target_pairs={{0,12},{4,8},{8,4},{12,0},{1,13},{5,9},{9,5},{13,1},{2,14},{6,10},... | collective-permute-start | bytes 294920 | tf_op jit(solution)/shard_map/ppermute | solution.py:181
  47.6 3.7 %collective-permute-start.18 = (bf16[24,2048]{1,0:T(8,128)(2,1)S(1)}, bf16[24,2048]{1,0:T(8,128)(2,1)S(1)}, u32[]{:S(2)}, u32[]{:S(2)}) collective-permute-start(bf16[24,2048]{1,0:T(8,128)(2,1)S(1)} %shard_map.129.mine), channel_id=1, source_target_pairs={{0,4},{4,0},{8,12},{12,8},{1,5},{5,1},{9,13},{13,9},{2,6},{6,2},{1... | collective-permute-start | bytes 294920 | tf_op jit(solution)/shard_map/ppermute | solution.py:181
  51.2 1.3 %collective-permute-start.17 = (bf16[24,2048]{1,0:T(8,128)(2,1)S(1)}, bf16[24,2048]{1,0:T(8,128)(2,1)S(1)}, u32[]{:S(2)}, u32[]{:S(2)}) collective-permute-start(bf16[24,2048]{1,0:T(8,128)(2,1)S(1)} %collective-permute-done.16.mine), channel_id=1, source_target_pairs={{0,4},{4,0},{8,12},{12,8},{1,5},{5,1},{9,13},{13,9},{2,6},{6,2},{1... | collective-permute-start | bytes 294920 | tf_op jit(solution)/shard_map/ppermute | solution.py:181
  53.5 4.5 %collective-permute-start.19 = (bf16[12,1280]{1,0:T(8,128)(2,1)S(1)}, bf16[12,1280]{1,0:T(8,128)(2,1)S(1)}, u32[]{:S(2)}, u32[]{:S(2)}) collective-permute-start(bf16[12,1280]{1,0:T(8,128)(2,1)S(1)} %get-tuple-element.54), channel_id=1, source_target_pairs={{0,1},{1,0},{2,3},{3,2},{4,5},{5,4},{6,7},{7,6},{8,9},{9,8},{10,11... | collective-permute-start | bytes 92168 | tf_op jit(solution)/shard_map/ppermute | solution.py:181
  53.6 6.9 %collective-permute-start.20 = (bf16[12,1280]{1,0:T(8,128)(2,1)S(1)}, bf16[12,1280]{1,0:T(8,128)(2,1)S(1)}, u32[]{:S(2)}, u32[]{:S(2)}) collective-permute-start(bf16[12,1280]{1,0:T(8,128)(2,1)S(1)} %get-tuple-element.55), channel_id=1, source_target_pairs={{0,2},{1,3},{2,0},{3,1},{4,6},{5,7},{6,4},{7,5},{8,10},{9,11},{10,... | collective-permute-start | bytes 92168 | tf_op jit(solution)/shard_map/ppermute | solution.py:181
  53.9 6.6 %collective-permute-start.21 = (bf16[12,1280]{1,0:T(8,128)(2,1)S(1)}, bf16[12,1280]{1,0:T(8,128)(2,1)S(1)}, u32[]{:S(2)}, u32[]{:S(2)}) collective-permute-start(bf16[12,1280]{1,0:T(8,128)(2,1)S(1)} %get-tuple-element.56), channel_id=1, source_target_pairs={{0,3},{1,2},{2,1},{3,0},{4,7},{5,6},{6,5},{7,4},{8,11},{9,10},{10,... | collective-permute-start | bytes 92168 | tf_op jit(solution)/shard_map/ppermute | solution.py:181

commit v6 on v5

--- a/solution.py
+++ b/solution.py
@@ -147,7 +147,7 @@
 MIB = 1024 * 1024
 
 
-def call(kernel, outs, operands, scratch=(), smem=(), resident=(), remote=(), micros=4, limit=8):
+def call(kernel, outs, operands, scratch=(), smem=(), resident=(), remote=(), micros=2, limit=8):
     specs = []
     placed = []
     for place, operand in enumerate(operands):
@@ -290,7 +290,7 @@
         target[...] = total[tp ^ step, 0:4].astype(jnp.bfloat16)
 
 
-def gather_kernel(own, first, second, third, out, rows):
+def gather_kernel(third, second, first, own, out, rows):
     for step, part in enumerate((own, first, second, third)):
         rows[4 * step : 4 * step + 4] = part[...].astype(jnp.float32)
     out[...] = rows[...].astype(jnp.bfloat16)
@@ -434,7 +434,7 @@
         target[...] = groups[here ^ (step + 1), 0:group].astype(jnp.bfloat16)
 
 
-def finish_kernel(stream, mine, first, second, third, out):
+def finish_kernel(third, second, first, stream, mine, out):
     total = stream[...] + mine[...]
     for other in (first, second, third):
         total = total + other[...].astype(jnp.float32)
@@ -504,8 +504,8 @@
         resident=(3, 4),
     )
 
-    parts = [swap(part, ("sec", "tp"), (1, step + 1)) for step, part in enumerate(parts)]
-    (own,) = call(gather_kernel, [((16, head_block), bf16)], (own, *parts), [pltpu.VMEM((16, head_block), f32)])
+    parts = [swap(parts[step - 1], ("sec", "tp"), (1, step)) for step in (3, 2, 1)]
+    (own,) = call(gather_kernel, [((16, head_block), bf16)], (*parts, own), [pltpu.VMEM((16, head_block), f32)])
     across = swap(own, "sec", 3)
     beside = swap(own, "sec", 1)
     corner = swap(across, "sec", 1)
@@ -560,8 +560,8 @@
         [pltpu.VMEM((4, 16, features), f32)],
         resident=(3,),
     )
-    parts = [swap(part, "tp", step + 1) for step, part in enumerate(parts)]
-    (out,) = call(finish_kernel, [((group, features), bf16)], (stream, mine, *parts))
+    parts = [swap(parts[step - 1], "tp", step) for step in (3, 2, 1)]
+    (out,) = call(finish_kernel, [((group, features), bf16)], (*parts, stream, mine))
     return out
 
 

time: 61.3 us -> 60.3 us (0.984)
  waiting for transfers between devices: 27.8 us -> 24.5 us
  starting transfers between devices: 19.5 us -> 22.5 us
  local copies, waits for them, and re-layouts: 1.71 us -> 0.73 us
    ppermute x22, waiting for transfers between devices: 27.8 us -> 24.5 us  [swap(): return lax.ppermute(value, axis, [(i, i ^ step) for i in range(total)])]
    ppermute x22, starting transfers between devices: 19.5 us -> 22.5 us  [swap(): return lax.ppermute(value, axis, [(i, i ^ step) for i in range(total)])]
    unnamed x32 -> x34, local copies, waits for them, and re-layouts: 1.71 us -> 0.73 us
  transfers between devices with their start and end apart: 22 -> 22, of which waited for: 17 -> 15; matrix products, arithmetic and copies ran while one was open for 0% -> 0% of each run, Pallas kernels for 9% -> 9%
where the time goes in v6:
time: 60.3 us; the launch traced here: 60.1 us
  waiting for transfers between devices  24.5 us (41%)
  starting transfers between devices  22.5 us (37%)
  Pallas kernels  12.1 us (20%)
  local copies, waits for them, and re-layouts  0.73 us (1%)
    ppermute x22, waiting for transfers between devices, swap(): return lax.ppermute(value, axis, [(i, i ^ step) for i in range(total)])  24.5 us
    ppermute x22, starting transfers between devices, swap(): return lax.ppermute(value, axis, [(i, i ^ step) for i in range(total)])  22.5 us
    pallas_call x15, Pallas kernels, call(): pl.pallas_call(kernel, out_shape=[jax.ShapeDtypeStruct(shape, dtype) for...  12.1 us
  transfers between devices with their start and end apart: 22, of which 15 were waited for; matrix products, arithmetic and copies ran while one was open for 0% of the time, Pallas kernels for 9%

profile of v6, /device:TPU:0, one launch (start us, length us, event | category | flops | bytes accessed | tf_op | source)
XLA Modules:
  0.0 60.1 jit_solution(4706013070321003943)
XLA Ops:
  0.0 0.5 collective-permute-start.1
  0.5 0.1 collective-permute-start
  0.6 1.5 %shard_map.118.own = bf16[2,48,128]{2,1,0:T(8,128)(2,1)S(1)} custom-call(bf16[12,1280]{1,0:T(8,128)(2,1)} %query.1, bf16[12,512]{1,0:T(8,128)(2,1)} %pairs.1, s32[1,48]{1,0:T(1,128)} %bitcast.7), custom_call_target="tpu_custom_call" | custom-call | flops 2000000000 | tf_op jit(solution)/shard_map/pallas_call | solution.py:159
  2.1 0.0 collective-permute-done.1.pairs
  2.1 0.0 collective-permute-done.query
  2.1 0.0 copy-start.5
  2.1 0.6 %copy-done.5 = s32[48]{0:T(128)S(1)} copy-done((s32[48]{0:T(128)S(1)}, s32[48]{0:T(128)}, u32[]{:S(2)}) %copy-start.5) | copy-done | bytes 216
  2.8 0.4 shard_map.119
  3.2 2.5 %collective-permute-start.2 = (bf16[2,48,128]{2,1,0:T(8,128)(2,1)S(1)}, bf16[2,48,128]{2,1,0:T(8,128)(2,1)S(1)}, u32[]{:S(2)}, u32[]{:S(2)}) collective-permute-start(bf16[2,48,128]{2,1,0:T(8,128)(2,1)S(1)} %get-tuple-element.31), channel_id=1, source_target_pairs={{0,12},{4,8},{8,4},{12,0},{1,13},{5,9},{9,5},{13,1},{2,14},{6,10},... | collective-permute-start | bytes 73736 | tf_op jit(solution)/shard_map/ppermute | solution.py:181
  5.7 0.0 copy-done.1
  5.7 0.0 copy-start.3
  5.7 0.0 copy-start.6
  5.8 1.1 %shard_map.120.near = f32[2,4,1280]{2,1,0:T(4,128)S(1)} custom-call(s32[3]{0:T(128)S(1)} %copy-done.4, bf16[2,48,128]{2,1,0:T(8,128)(2,1)S(1)} %get-tuple-element.32.source, bf16[3,224,1024]{2,1,0:T(8,128)(2,1)S(1)} %copy-done.1, bf16[3,224,1024]{2,1,0:T(8,128)(2,1)S(1)} %copy-done.2), custom_call_target="tpu_custom_call" | custom-call | flops 2000000000 | tf_op jit(solution)/shard_map/pallas_call | solution.py:159
  6.9 0.4 collective-permute-done.2.source
  7.2 1.2 %shard_map.121 = (bf16[4,1280]{1,0:T(4,128)(2,1)S(1)}, bf16[4,1280]{1,0:T(4,128)(2,1)S(1)}, bf16[4,1280]{1,0:T(4,128)(2,1)S(1)}, bf16[4,1280]{1,0:T(4,128)(2,1)S(1)}) custom-call(s32[3]{0:T(128)S(1)} %copy-done.4, bf16[2,48,128]{2,1,0:T(8,128)(2,1)S(1)} %collective-permute-done.2.source, f32[2,4,1280]{2,1,0:T(4,128)S(1)} %shard_map.120.near, ...), custom_call_target="tpu_custom_call" | custom-call | flops 2000000000 | tf_op jit(solution)/shard_map/pallas_call | solution.py:159
  8.4 4.3 %collective-permute-start.3 = (bf16[4,1280]{1,0:T(4,128)(2,1)S(1)}, bf16[4,1280]{1,0:T(4,128)(2,1)S(1)}, u32[]{:S(2)}, u32[]{:S(2)}) collective-permute-start(bf16[4,1280]{1,0:T(4,128)(2,1)S(1)} %get-tuple-element.33), channel_id=1, source_target_pairs={{0,7},{1,6},{2,5},{3,4},{4,3},{5,2},{6,1},{7,0},{8,15},{9,14},{10,... | collective-permute-start | bytes 30728 | tf_op jit(solution)/shard_map/ppermute | solution.py:181
  12.7 0.0 collective-permute-start.4
  12.7 0.7 %collective-permute-start.5 = (bf16[4,1280]{1,0:T(4,128)(2,1)S(1)}, bf16[4,1280]{1,0:T(4,128)(2,1)S(1)}, u32[]{:S(2)}, u32[]{:S(2)}) collective-permute-start(bf16[4,1280]{1,0:T(4,128)(2,1)S(1)} %get-tuple-element.35), channel_id=1, source_target_pairs={{0,5},{1,4},{2,7},{3,6},{4,1},{5,0},{6,3},{7,2},{8,13},{9,12},{10,... | collective-permute-start | bytes 30728 | tf_op jit(solution)/shard_map/ppermute | solution.py:181
  13.4 0.7 %collective-permute-done.3.third = bf16[4,1280]{1,0:T(4,128)(2,1)S(1)} collective-permute-done((bf16[4,1280]{1,0:T(4,128)(2,1)S(1)}, bf16[4,1280]{1,0:T(4,128)(2,1)S(1)}, u32[]{:S(2)}, u32[]{:S(2)}) %collective-permute-start.3) | collective-permute-done | bytes 10272 | tf_op jit(solution)/shard_map/ppermute | solution.py:181
  14.1 2.6 %collective-permute-done.4.second = bf16[4,1280]{1,0:T(4,128)(2,1)S(1)} collective-permute-done((bf16[4,1280]{1,0:T(4,128)(2,1)S(1)}, bf16[4,1280]{1,0:T(4,128)(2,1)S(1)}, u32[]{:S(2)}, u32[]{:S(2)}) %collective-permute-start.4) | collective-permute-done | bytes 10272 | tf_op jit(solution)/shard_map/ppermute | solution.py:181
  16.7 0.0 collective-permute-done.5.first
  16.7 0.0 copy-start.7
  16.7 0.0 slice-start.1
  16.8 0.0 slice-start.4
  16.8 1.6 %collective-permute-start.7 = (bf16[16,1280]{1,0:T(8,128)(2,1)S(1)}, bf16[16,1280]{1,0:T(8,128)(2,1)S(1)}, u32[]{:S(2)}, u32[]{:S(2)}) collective-permute-start(bf16[16,1280]{1,0:T(8,128)(2,1)S(1)} %shard_map.122.own), channel_id=1, source_target_pairs={{0,12},{4,8},{8,4},{12,0},{1,13},{5,9},{9,5},{13,1},{2,14},{6,10},... | collective-permute-start | bytes 122888 | tf_op jit(solution)/shard_map/ppermute | solution.py:181
  18.4 0.1 collective-permute-start.6
  18.4 1.8 %collective-permute-done.7.across = bf16[16,1280]{1,0:T(8,128)(2,1)S(1)} collective-permute-done((bf16[16,1280]{1,0:T(8,128)(2,1)S(1)}, bf16[16,1280]{1,0:T(8,128)(2,1)S(1)}, u32[]{:S(2)}, u32[]{:S(2)}) %collective-permute-start.7) | collective-permute-done | bytes 40992 | tf_op jit(solution)/shard_map/ppermute | solution.py:181
  20.3 0.4 collective-permute-start.8
  20.7 0.0 collective-permute-done.6.beside
  20.7 0.9 %collective-permute-done.8.corner = bf16[16,1280]{1,0:T(8,128)(2,1)S(1)} collective-permute-done((bf16[16,1280]{1,0:T(8,128)(2,1)S(1)}, bf16[16,1280]{1,0:T(8,128)(2,1)S(1)}, u32[]{:S(2)}, u32[]{:S(2)}) %collective-permute-start.8) | collective-permute-done | bytes 40992 | tf_op jit(solution)/shard_map/ppermute | solution.py:181
  21.6 0.8 %shard_map.123 = (f32[24,1280]{1,0:T(8,128)S(1)}, bf16[24,1280]{1,0:T(8,128)(2,1)S(1)}, f32[24,1280]{1,0:T(8,128)S(1)}, bf16[24,1280]{1,0:T(8,128)(2,1)S(1)}) custom-call(bf16[16,1280]{1,0:T(8,128)(2,1)S(1)} %shard_map.122.own, bf16[16,1280]{1,0:T(8,128)(2,1)S(1)} %collective-permute-done.6.beside, bf16[16,1280]{1,0:T(8,128)(2,1)S(1)} %collective-permute-done.7.across, ...), custom_call_target="tpu_custom_call" | custom-call | flops 2000000000 | tf_op jit(solution)/shard_map/pallas_call | solution.py:159
  22.4 0.1 collective-permute-start.9
  22.5 2.2 %collective-permute-start.11 = (bf16[24,1280]{1,0:T(8,128)(2,1)S(1)}, bf16[24,1280]{1,0:T(8,128)(2,1)S(1)}, u32[]{:S(2)}, u32[]{:S(2)}) collective-permute-start(bf16[24,1280]{1,0:T(8,128)(2,1)S(1)} %get-tuple-element.42), channel_id=1, source_target_pairs={{0,2},{1,3},{2,0},{3,1},{4,6},{5,7},{6,4},{7,5},{8,10},{9,11},{10,... | collective-permute-start | bytes 184328 | tf_op jit(solution)/shard_map/ppermute | solution.py:181
  24.7 3.3 %collective-permute-done.9.other = bf16[24,1280]{1,0:T(8,128)(2,1)S(1)} collective-permute-done((bf16[24,1280]{1,0:T(8,128)(2,1)S(1)}, bf16[24,1280]{1,0:T(8,128)(2,1)S(1)}, u32[]{:S(2)}, u32[]{:S(2)}) %collective-permute-start.9) | collective-permute-done | bytes 61472 | tf_op jit(solution)/shard_map/ppermute | solution.py:181
  28.0 1.4 %collective-permute-start.10 = (bf16[24,1280]{1,0:T(8,128)(2,1)S(1)}, bf16[24,1280]{1,0:T(8,128)(2,1)S(1)}, u32[]{:S(2)}, u32[]{:S(2)}) collective-permute-start(bf16[24,1280]{1,0:T(8,128)(2,1)S(1)} %get-tuple-element.40), channel_id=1, source_target_pairs={{0,2},{1,3},{2,0},{3,1},{4,6},{5,7},{6,4},{7,5},{8,10},{9,11},{10,... | collective-permute-start | bytes 184328 | tf_op jit(solution)/shard_map/ppermute | solution.py:181
  29.5 0.0 collective-permute-done.11.other
  29.5 0.6 %collective-permute-start.12 = (bf16[24,1280]{1,0:T(8,128)(2,1)S(1)}, bf16[24,1280]{1,0:T(8,128)(2,1)S(1)}, u32[]{:S(2)}, u32[]{:S(2)}) collective-permute-start(bf16[24,1280]{1,0:T(8,128)(2,1)S(1)} %get-tuple-element.44), channel_id=1, source_target_pairs={{0,1},{1,0},{2,3},{3,2},{4,5},{5,4},{6,7},{7,6},{8,9},{9,8},{10,11... | collective-permute-start | bytes 184328 | tf_op jit(solution)/shard_map/ppermute | solution.py:181
  30.1 3.1 %collective-permute-done.10.other_a = bf16[24,1280]{1,0:T(8,128)(2,1)S(1)} collective-permute-done((bf16[24,1280]{1,0:T(8,128)(2,1)S(1)}, bf16[24,1280]{1,0:T(8,128)(2,1)S(1)}, u32[]{:S(2)}, u32[]{:S(2)}) %collective-permute-start.10) | collective-permute-done | bytes 61472 | tf_op jit(solution)/shard_map/ppermute | solution.py:181
  33.2 0.7 %collective-permute-done.12.other_b = bf16[24,1280]{1,0:T(8,128)(2,1)S(1)} collective-permute-done((bf16[24,1280]{1,0:T(8,128)(2,1)S(1)}, bf16[24,1280]{1,0:T(8,128)(2,1)S(1)}, u32[]{:S(2)}, u32[]{:S(2)}) %collective-permute-start.12) | collective-permute-done | bytes 61472 | tf_op jit(solution)/shard_map/ppermute | solution.py:181
  33.9 2.0 %shard_map.126 = (f32[24,4224]{1,0:T(8,128)S(1)}, bf16[24,4224]{1,0:T(8,128)(2,1)S(1)}, bf16[48,1280]{1,0:T(8,128)(2,1)S(1)}, f32[12,1280]{1,0:T(8,128)S(1)}) custom-call(f32[24,1280]{1,0:T(8,128)S(1)} %get-tuple-element.39.mine_a, bf16[24,1280]{1,0:T(8,128)(2,1)S(1)} %collective-permute-done.10.other_a, f32[24,1280]{1,0:T(8,128)S(1)} %get-tuple-element.43.mine_b, ...), custom_call_target="tpu_custom_call" | custom-call | flops 2000000000 | tf_op jit(solution)/shard_map/pallas_call | solution.py:159
  35.9 0.1 collective-permute-start.14
  36.0 1.4 %collective-permute-done.14.other = bf16[24,4224]{1,0:T(8,128)(2,1)S(1)} collective-permute-done((bf16[24,4224]{1,0:T(8,128)(2,1)S(1)}, bf16[24,4224]{1,0:T(8,128)(2,1)S(1)}, u32[]{:S(2)}, u32[]{:S(2)}) %collective-permute-start.14) | collective-permute-done | bytes 202784 | tf_op jit(solution)/shard_map/ppermute | solution.py:181
  37.4 0.2 shard_map.128
  37.7 1.2 %collective-permute-start.15 = (bf16[24,4224]{1,0:T(8,128)(2,1)S(1)}, bf16[24,4224]{1,0:T(8,128)(2,1)S(1)}, u32[]{:S(2)}, u32[]{:S(2)}) collective-permute-start(bf16[24,4224]{1,0:T(8,128)(2,1)S(1)} %get-tuple-element.50), channel_id=1, source_target_pairs={{0,12},{4,8},{8,4},{12,0},{1,13},{5,9},{9,5},{13,1},{2,14},{6,10},... | collective-permute-start | bytes 608264 | tf_op jit(solution)/shard_map/ppermute | solution.py:181
  38.9 1.9 %shard_map.127 = (f32[24,4096]{1,0:T(8,128)S(1)}, bf16[24,4096]{1,0:T(8,128)(2,1)S(1)}) custom-call(bf16[48,1280]{1,0:T(8,128)(2,1)S(1)} %get-tuple-element.45.features, bf16[1280,4096]{1,0:T(8,128)(2,1)S(1)} %bitcast.2, bf16[1280,4096]{1,0:T(8,128)(2,1)S(1)} %bitcast.4), custom_call_target="tpu_custom_call" | custom-call | flops 2000000000 | tf_op jit(solution)/shard_map/pallas_call | solution.py:159
  40.8 0.4 collective-permute-start.13
  41.3 1.1 %collective-permute-done.13.beside = bf16[24,4096]{1,0:T(8,128)(2,1)S(1)} collective-permute-done((bf16[24,4096]{1,0:T(8,128)(2,1)S(1)}, bf16[24,4096]{1,0:T(8,128)(2,1)S(1)}, u32[]{:S(2)}, u32[]{:S(2)}) %collective-permute-start.13) | collective-permute-done | bytes 196640 | tf_op jit(solution)/shard_map/ppermute | solution.py:181
  42.3 2.4 %collective-permute-done.15.across = bf16[24,4224]{1,0:T(8,128)(2,1)S(1)} collective-permute-done((bf16[24,4224]{1,0:T(8,128)(2,1)S(1)}, bf16[24,4224]{1,0:T(8,128)(2,1)S(1)}, u32[]{:S(2)}, u32[]{:S(2)}) %collective-permute-start.15) | collective-permute-done | bytes 202784 | tf_op jit(solution)/shard_map/ppermute | solution.py:181
  44.7 0.2 shard_map.129.mine
  44.9 1.3 %collective-permute-start.16 = (bf16[24,2048]{1,0:T(8,128)(2,1)S(1)}, bf16[24,2048]{1,0:T(8,128)(2,1)S(1)}, u32[]{:S(2)}, u32[]{:S(2)}) collective-permute-start(bf16[24,2048]{1,0:T(8,128)(2,1)S(1)} %shard_map.129.mine), channel_id=1, source_target_pairs={{0,12},{4,8},{8,4},{12,0},{1,13},{5,9},{9,5},{13,1},{2,14},{6,10},... | collective-permute-start | bytes 294920 | tf_op jit(solution)/shard_map/ppermute | solution.py:181
  46.2 0.4 collective-permute-start.18
  46.6 3.2 %collective-permute-done.16.mine = bf16[24,2048]{1,0:T(8,128)(2,1)S(1)} collective-permute-done((bf16[24,2048]{1,0:T(8,128)(2,1)S(1)}, bf16[24,2048]{1,0:T(8,128)(2,1)S(1)}, u32[]{:S(2)}, u32[]{:S(2)}) %collective-permute-start.16) | collective-permute-done | bytes 98336 | tf_op jit(solution)/shard_map/ppermute | solution.py:181
  49.7 0.1 collective-permute-start.17
  49.9 0.0 collective-permute-done.18.other
  49.9 1.0 %shard_map.130.before = f32[48,1280]{1,0:T(8,128)S(1)} custom-call(bf16[24,2048]{1,0:T(8,128)(2,1)S(1)} %shard_map.129.mine, bf16[24,2048]{1,0:T(8,128)(2,1)S(1)} %collective-permute-done.18.other, bf16[4096,1280]{1,0:T(8,128)(2,1)S(1)} %bitcast.6), custom_call_target="tpu_custom_call" | custom-call | flops 2000000000 | tf_op jit(solution)/shard_map/pallas_call | solution.py:159
  50.9 0.1 collective-permute-done.17.other
  51.0 1.0 %shard_map.131 = (f32[12,1280]{1,0:T(8,128)S(1)}, bf16[12,1280]{1,0:T(8,128)(2,1)S(1)}, bf16[12,1280]{1,0:T(8,128)(2,1)S(1)}, bf16[12,1280]{1,0:T(8,128)(2,1)S(1)}) custom-call(bf16[24,2048]{1,0:T(8,128)(2,1)S(1)} %collective-permute-done.16.mine, bf16[24,2048]{1,0:T(8,128)(2,1)S(1)} %collective-permute-done.17.other, f32[48,1280]{1,0:T(8,128)S(1)} %shard_map.130.before, ...), custom_call_target="tpu_custom_call" | custom-call | flops 2000000000 | tf_op jit(solution)/shard_map/pallas_call | solution.py:159
  52.1 2.5 %collective-permute-start.19 = (bf16[12,1280]{1,0:T(8,128)(2,1)S(1)}, bf16[12,1280]{1,0:T(8,128)(2,1)S(1)}, u32[]{:S(2)}, u32[]{:S(2)}) collective-permute-start(bf16[12,1280]{1,0:T(8,128)(2,1)S(1)} %get-tuple-element.52), channel_id=1, source_target_pairs={{0,3},{1,2},{2,1},{3,0},{4,7},{5,6},{6,5},{7,4},{8,11},{9,10},{10,... | collective-permute-start | bytes 92168 | tf_op jit(solution)/shard_map/ppermute | solution.py:181
  54.6 0.0 collective-permute-start.20
  54.6 2.0 %collective-permute-start.21 = (bf16[12,1280]{1,0:T(8,128)(2,1)S(1)}, bf16[12,1280]{1,0:T(8,128)(2,1)S(1)}, u32[]{:S(2)}, u32[]{:S(2)}) collective-permute-start(bf16[12,1280]{1,0:T(8,128)(2,1)S(1)} %get-tuple-element.54), channel_id=1, source_target_pairs={{0,1},{1,0},{2,3},{3,2},{4,5},{5,4},{6,7},{7,6},{8,9},{9,8},{10,11... | collective-permute-start | bytes 92168 | tf_op jit(solution)/shard_map/ppermute | solution.py:181
  56.5 1.6 %collective-permute-done.19.third = bf16[12,1280]{1,0:T(8,128)(2,1)S(1)} collective-permute-done((bf16[12,1280]{1,0:T(8,128)(2,1)S(1)}, bf16[12,1280]{1,0:T(8,128)(2,1)S(1)}, u32[]{:S(2)}, u32[]{:S(2)}) %collective-permute-start.19) | collective-permute-done | bytes 30752 | tf_op jit(solution)/shard_map/ppermute | solution.py:181
  58.2 1.3 %collective-permute-done.20.second = bf16[12,1280]{1,0:T(8,128)(2,1)S(1)} collective-permute-done((bf16[12,1280]{1,0:T(8,128)(2,1)S(1)}, bf16[12,1280]{1,0:T(8,128)(2,1)S(1)}, u32[]{:S(2)}, u32[]{:S(2)}) %collective-permute-start.20) | collective-permute-done | bytes 30752 | tf_op jit(solution)/shard_map/ppermute | solution.py:181
  59.5 0.0 collective-permute-done.21.first
  59.5 0.6 %shard_map.132 = bf16[12,1280]{1,0:T(8,128)(2,1)} custom-call(bf16[12,1280]{1,0:T(8,128)(2,1)S(1)} %collective-permute-done.19.third, bf16[12,1280]{1,0:T(8,128)(2,1)S(1)} %collective-permute-done.20.second, bf16[12,1280]{1,0:T(8,128)(2,1)S(1)} %collective-permute-done.21.first, f32[12,1280]{1,0:T(8,128)S(1)} %get-tuple-element.55.stream, ...), custom_call_target="tpu_custom_call" | custom-call | flops 2000000000 | tf_op jit(solution)/shard_map/pallas_call | solution.py:159
  (33 shorter events, 0.1 us)
Async XLA Ops:
  0.0 5.7 %copy-start.4 = (s32[3]{0:T(128)S(1)}, s32[3]{0:T(128)}, u32[]{:S(2)}) copy-start(s32[3]{0:T(128)} %lengths.3) | copy-start | bytes 40
  0.0 5.7 %copy-start.2 = (bf16[3,224,1024]{2,1,0:T(8,128)(2,1)S(1)}, bf16[3,224,1024]{2,1,0:T(8,128)(2,1)}, u32[]{:S(2)}) copy-start(bf16[3,224,1024]{2,1,0:T(8,128)(2,1)} %values.3) | copy-start | bytes 4128772
  0.0 5.7 %copy-start.1 = (bf16[3,224,1024]{2,1,0:T(8,128)(2,1)S(1)}, bf16[3,224,1024]{2,1,0:T(8,128)(2,1)}, u32[]{:S(2)}) copy-start(bf16[3,224,1024]{2,1,0:T(8,128)(2,1)} %keys.3) | copy-start | bytes 4128772
  0.0 2.1 %collective-permute-start.1 = (bf16[12,512]{1,0:T(8,128)(2,1)}, bf16[12,512]{1,0:T(8,128)(2,1)S(1)}, u32[]{:S(2)}, u32[]{:S(2)}) collective-permute-start(bf16[12,512]{1,0:T(8,128)(2,1)} %pairs.1), channel_id=1, source_target_pairs={{0,4},{4,0},{8,12},{12,8},{1,5},{5,1},{9,13},{13,9},{2,6},{6,2},{1... | collective-permute-start | bytes 36872 | tf_op jit(solution)/shard_map/ppermute | solution.py:181
  0.5 1.6 %collective-permute-start = (bf16[12,1280]{1,0:T(8,128)(2,1)}, bf16[12,1280]{1,0:T(8,128)(2,1)S(1)}, u32[]{:S(2)}, u32[]{:S(2)}) collective-permute-start(bf16[12,1280]{1,0:T(8,128)(2,1)} %query.1), channel_id=1, source_target_pairs={{0,4},{4,0},{8,12},{12,8},{1,5},{5,1},{9,13},{13,9},{2,6},{6,2},{1... | collective-permute-start | bytes 92168 | tf_op jit(solution)/shard_map/ppermute | solution.py:181
  2.1 0.7 %copy-start.5 = (s32[48]{0:T(128)S(1)}, s32[48]{0:T(128)}, u32[]{:S(2)}) copy-start(s32[48]{0:T(128)} %param.18) | copy-start | bytes 580
  3.2 4.0 %collective-permute-start.2 = (bf16[2,48,128]{2,1,0:T(8,128)(2,1)S(1)}, bf16[2,48,128]{2,1,0:T(8,128)(2,1)S(1)}, u32[]{:S(2)}, u32[]{:S(2)}) collective-permute-start(bf16[2,48,128]{2,1,0:T(8,128)(2,1)S(1)} %get-tuple-element.31), channel_id=1, source_target_pairs={{0,12},{4,8},{8,4},{12,0},{1,13},{5,9},{9,5},{13,1},{2,14},{6,10},... | collective-permute-start | bytes 73736 | tf_op jit(solution)/shard_map/ppermute | solution.py:181
  5.7 15.9 %copy-start = (bf16[1280,1280]{1,0:T(8,128)(2,1)S(1)}, bf16[1280,1280]{1,0:T(8,128)(2,1)}, u32[]{:S(2)}) copy-start(bf16[1280,1280]{1,0:T(8,128)(2,1)} %weight.3) | copy-start | bytes 9830404
  5.7 15.8 %copy-start.3 = (bf16[12,1280]{1,0:T(8,128)(2,1)S(1)}, bf16[12,1280]{1,0:T(8,128)(2,1)}, u32[]{:S(2)}) copy-start(bf16[12,1280]{1,0:T(8,128)(2,1)} %resid.1) | copy-start | bytes 92164
  5.7 15.8 %copy-start.6 = (s32[48]{0:T(128)S(1)}, s32[48]{0:T(128)}, u32[]{:S(2)}) copy-start(s32[48]{0:T(128)} %param.18) | copy-start | bytes 580
  8.4 5.7 %collective-permute-start.3 = (bf16[4,1280]{1,0:T(4,128)(2,1)S(1)}, bf16[4,1280]{1,0:T(4,128)(2,1)S(1)}, u32[]{:S(2)}, u32[]{:S(2)}) collective-permute-start(bf16[4,1280]{1,0:T(4,128)(2,1)S(1)} %get-tuple-element.33), channel_id=1, source_target_pairs={{0,7},{1,6},{2,5},{3,4},{4,3},{5,2},{6,1},{7,0},{8,15},{9,14},{10,... | collective-permute-start | bytes 30728 | tf_op jit(solution)/shard_map/ppermute | solution.py:181
  12.7 4.0 %collective-permute-start.4 = (bf16[4,1280]{1,0:T(4,128)(2,1)S(1)}, bf16[4,1280]{1,0:T(4,128)(2,1)S(1)}, u32[]{:S(2)}, u32[]{:S(2)}) collective-permute-start(bf16[4,1280]{1,0:T(4,128)(2,1)S(1)} %get-tuple-element.34), channel_id=1, source_target_pairs={{0,6},{1,7},{2,4},{3,5},{4,2},{5,3},{6,0},{7,1},{8,14},{9,15},{10,... | collective-permute-start | bytes 30728 | tf_op jit(solution)/shard_map/ppermute | solution.py:181
  12.7 4.0 %collective-permute-start.5 = (bf16[4,1280]{1,0:T(4,128)(2,1)S(1)}, bf16[4,1280]{1,0:T(4,128)(2,1)S(1)}, u32[]{:S(2)}, u32[]{:S(2)}) collective-permute-start(bf16[4,1280]{1,0:T(4,128)(2,1)S(1)} %get-tuple-element.35), channel_id=1, source_target_pairs={{0,5},{1,4},{2,7},{3,6},{4,1},{5,0},{6,3},{7,2},{8,13},{9,12},{10,... | collective-permute-start | bytes 30728 | tf_op jit(solution)/shard_map/ppermute | solution.py:181
  16.7 17.2 %slice-start = ((s8[10485760]{0:T(1024)(128)(4,1)}), s8[4194304]{0:T(1024)(128)(4,1)S(1)}, s32[]{:S(2)}) async-start(s8[10485760]{0:T(1024)(128)(4,1)} %bitcast.1), calls=%async_computation | async-start | bytes 8388608
  16.7 17.2 %slice-start.3 = ((s8[10485760]{0:T(1024)(128)(4,1)}), s8[4194304]{0:T(1024)(128)(4,1)S(1)}, s32[]{:S(2)}) async-start(s8[10485760]{0:T(1024)(128)(4,1)} %bitcast.3), calls=%async_computation.3 | async-start | bytes 8388608
  16.7 13.4 %copy-start.7 = (bf16[1280]{0:T(1024)(128)(2,1)S(1)}, bf16[1280]{0:T(1024)(128)(2,1)}, u32[]{:S(2)}) copy-start(bf16[1280]{0:T(1024)(128)(2,1)} %param.20) | copy-start | bytes 7684
  16.7 17.1 %slice-start.1 = ((s8[10485760]{0:T(1024)(128)(4,1)}), s8[4194304]{0:T(1024)(128)(4,1)S(1)}, s32[]{:S(2)}) async-start(s8[10485760]{0:T(1024)(128)(4,1)} %bitcast.1), calls=%async_computation.1 | async-start | bytes 8388608
  16.8 17.1 %slice-start.4 = ((s8[10485760]{0:T(1024)(128)(4,1)}), s8[4194304]{0:T(1024)(128)(4,1)S(1)}, s32[]{:S(2)}) async-start(s8[10485760]{0:T(1024)(128)(4,1)} %bitcast.3), calls=%async_computation.4 | async-start | bytes 8388608
  16.8 3.5 %collective-permute-start.7 = (bf16[16,1280]{1,0:T(8,128)(2,1)S(1)}, bf16[16,1280]{1,0:T(8,128)(2,1)S(1)}, u32[]{:S(2)}, u32[]{:S(2)}) collective-permute-start(bf16[16,1280]{1,0:T(8,128)(2,1)S(1)} %shard_map.122.own), channel_id=1, source_target_pairs={{0,12},{4,8},{8,4},{12,0},{1,13},{5,9},{9,5},{13,1},{2,14},{6,10},... | collective-permute-start | bytes 122888 | tf_op jit(solution)/shard_map/ppermute | solution.py:181
  18.4 2.3 %collective-permute-start.6 = (bf16[16,1280]{1,0:T(8,128)(2,1)S(1)}, bf16[16,1280]{1,0:T(8,128)(2,1)S(1)}, u32[]{:S(2)}, u32[]{:S(2)}) collective-permute-start(bf16[16,1280]{1,0:T(8,128)(2,1)S(1)} %shard_map.122.own), channel_id=1, source_target_pairs={{0,4},{4,0},{8,12},{12,8},{1,5},{5,1},{9,13},{13,9},{2,6},{6,2},{1... | collective-permute-start | bytes 122888 | tf_op jit(solution)/shard_map/ppermute | solution.py:181
  20.3 1.3 %collective-permute-start.8 = (bf16[16,1280]{1,0:T(8,128)(2,1)S(1)}, bf16[16,1280]{1,0:T(8,128)(2,1)S(1)}, u32[]{:S(2)}, u32[]{:S(2)}) collective-permute-start(bf16[16,1280]{1,0:T(8,128)(2,1)S(1)} %collective-permute-done.7.across), channel_id=1, source_target_pairs={{0,4},{4,0},{8,12},{12,8},{1,5},{5,1},{9,13},{13,9},{2,6},{6,2},{1... | collective-permute-start | bytes 122888 | tf_op jit(solution)/shard_map/ppermute | solution.py:181
  22.4 5.6 %collective-permute-start.9 = (bf16[24,1280]{1,0:T(8,128)(2,1)S(1)}, bf16[24,1280]{1,0:T(8,128)(2,1)S(1)}, u32[]{:S(2)}, u32[]{:S(2)}) collective-permute-start(bf16[24,1280]{1,0:T(8,128)(2,1)S(1)} %get-tuple-element.38), channel_id=1, source_target_pairs={{0,1},{1,0},{2,3},{3,2},{4,5},{5,4},{6,7},{7,6},{8,9},{9,8},{10,11... | collective-permute-start | bytes 184328 | tf_op jit(solution)/shard_map/ppermute | solution.py:181
  22.5 7.0 %collective-permute-start.11 = (bf16[24,1280]{1,0:T(8,128)(2,1)S(1)}, bf16[24,1280]{1,0:T(8,128)(2,1)S(1)}, u32[]{:S(2)}, u32[]{:S(2)}) collective-permute-start(bf16[24,1280]{1,0:T(8,128)(2,1)S(1)} %get-tuple-element.42), channel_id=1, source_target_pairs={{0,2},{1,3},{2,0},{3,1},{4,6},{5,7},{6,4},{7,5},{8,10},{9,11},{10,... | collective-permute-start | bytes 184328 | tf_op jit(solution)/shard_map/ppermute | solution.py:181
  28.0 5.9 %slice-start.2 = ((s8[10485760]{0:T(1024)(128)(4,1)}), s8[2097152]{0:T(1024)(128)(4,1)S(1)}, s32[]{:S(2)}) async-start(s8[10485760]{0:T(1024)(128)(4,1)} %bitcast.1), calls=%async_computation.2 | async-start | bytes 4194304
  28.0 5.9 %slice-start.5 = ((s8[10485760]{0:T(1024)(128)(4,1)}), s8[2097152]{0:T(1024)(128)(4,1)S(1)}, s32[]{:S(2)}) async-start(s8[10485760]{0:T(1024)(128)(4,1)} %bitcast.3), calls=%async_computation.5 | async-start | bytes 4194304
  28.0 5.2 %collective-permute-start.10 = (bf16[24,1280]{1,0:T(8,128)(2,1)S(1)}, bf16[24,1280]{1,0:T(8,128)(2,1)S(1)}, u32[]{:S(2)}, u32[]{:S(2)}) collective-permute-start(bf16[24,1280]{1,0:T(8,128)(2,1)S(1)} %get-tuple-element.40), channel_id=1, source_target_pairs={{0,2},{1,3},{2,0},{3,1},{4,6},{5,7},{6,4},{7,5},{8,10},{9,11},{10,... | collective-permute-start | bytes 184328 | tf_op jit(solution)/shard_map/ppermute | solution.py:181
  29.5 4.4 %collective-permute-start.12 = (bf16[24,1280]{1,0:T(8,128)(2,1)S(1)}, bf16[24,1280]{1,0:T(8,128)(2,1)S(1)}, u32[]{:S(2)}, u32[]{:S(2)}) collective-permute-start(bf16[24,1280]{1,0:T(8,128)(2,1)S(1)} %get-tuple-element.44), channel_id=1, source_target_pairs={{0,1},{1,0},{2,3},{3,2},{4,5},{5,4},{6,7},{7,6},{8,9},{9,8},{10,11... | collective-permute-start | bytes 184328 | tf_op jit(solution)/shard_map/ppermute | solution.py:181
  35.9 1.5 %collective-permute-start.14 = (bf16[24,4224]{1,0:T(8,128)(2,1)S(1)}, bf16[24,4224]{1,0:T(8,128)(2,1)S(1)}, u32[]{:S(2)}, u32[]{:S(2)}) collective-permute-start(bf16[24,4224]{1,0:T(8,128)(2,1)S(1)} %get-tuple-element.49), channel_id=1, source_target_pairs={{0,4},{4,0},{8,12},{12,8},{1,5},{5,1},{9,13},{13,9},{2,6},{6,2},{1... | collective-permute-start | bytes 608264 | tf_op jit(solution)/shard_map/ppermute | solution.py:181
  37.7 7.0 %collective-permute-start.15 = (bf16[24,4224]{1,0:T(8,128)(2,1)S(1)}, bf16[24,4224]{1,0:T(8,128)(2,1)S(1)}, u32[]{:S(2)}, u32[]{:S(2)}) collective-permute-start(bf16[24,4224]{1,0:T(8,128)(2,1)S(1)} %get-tuple-element.50), channel_id=1, source_target_pairs={{0,12},{4,8},{8,4},{12,0},{1,13},{5,9},{9,5},{13,1},{2,14},{6,10},... | collective-permute-start | bytes 608264 | tf_op jit(solution)/shard_map/ppermute | solution.py:181
  38.9 11.0 %slice-start.6 = ((s8[10485760]{0:T(1024)(128)(4,1)}), s8[4194304]{0:T(1024)(128)(4,1)S(1)}, s32[]{:S(2)}) async-start(s8[10485760]{0:T(1024)(128)(4,1)} %bitcast.5), calls=%async_computation.6 | async-start | bytes 8388608
  38.9 11.0 %slice-start.7 = ((s8[10485760]{0:T(1024)(128)(4,1)}), s8[4194304]{0:T(1024)(128)(4,1)S(1)}, s32[]{:S(2)}) async-start(s8[10485760]{0:T(1024)(128)(4,1)} %bitcast.5), calls=%async_computation.7 | async-start | bytes 8388608
  38.9 11.0 %slice-start.8 = ((s8[10485760]{0:T(1024)(128)(4,1)}), s8[2097152]{0:T(1024)(128)(4,1)S(1)}, s32[]{:S(2)}) async-start(s8[10485760]{0:T(1024)(128)(4,1)} %bitcast.5), calls=%async_computation.8 | async-start | bytes 4194304
  40.8 1.5 %collective-permute-start.13 = (bf16[24,4096]{1,0:T(8,128)(2,1)S(1)}, bf16[24,4096]{1,0:T(8,128)(2,1)S(1)}, u32[]{:S(2)}, u32[]{:S(2)}) collective-permute-start(bf16[24,4096]{1,0:T(8,128)(2,1)S(1)} %get-tuple-element.47), channel_id=1, source_target_pairs={{0,4},{4,0},{8,12},{12,8},{1,5},{5,1},{9,13},{13,9},{2,6},{6,2},{1... | collective-permute-start | bytes 589832 | tf_op jit(solution)/shard_map/ppermute | solution.py:181
  44.9 4.8 %collective-permute-start.16 = (bf16[24,2048]{1,0:T(8,128)(2,1)S(1)}, bf16[24,2048]{1,0:T(8,128)(2,1)S(1)}, u32[]{:S(2)}, u32[]{:S(2)}) collective-permute-start(bf16[24,2048]{1,0:T(8,128)(2,1)S(1)} %shard_map.129.mine), channel_id=1, source_target_pairs={{0,12},{4,8},{8,4},{12,0},{1,13},{5,9},{9,5},{13,1},{2,14},{6,10},... | collective-permute-start | bytes 294920 | tf_op jit(solution)/shard_map/ppermute | solution.py:181
  46.2 3.7 %collective-permute-start.18 = (bf16[24,2048]{1,0:T(8,128)(2,1)S(1)}, bf16[24,2048]{1,0:T(8,128)(2,1)S(1)}, u32[]{:S(2)}, u32[]{:S(2)}) collective-permute-start(bf16[24,2048]{1,0:T(8,128)(2,1)S(1)} %shard_map.129.mine), channel_id=1, source_target_pairs={{0,4},{4,0},{8,12},{12,8},{1,5},{5,1},{9,13},{13,9},{2,6},{6,2},{1... | collective-permute-start | bytes 294920 | tf_op jit(solution)/shard_map/ppermute | solution.py:181
  49.7 1.3 %collective-permute-start.17 = (bf16[24,2048]{1,0:T(8,128)(2,1)S(1)}, bf16[24,2048]{1,0:T(8,128)(2,1)S(1)}, u32[]{:S(2)}, u32[]{:S(2)}) collective-permute-start(bf16[24,2048]{1,0:T(8,128)(2,1)S(1)} %collective-permute-done.16.mine), channel_id=1, source_target_pairs={{0,4},{4,0},{8,12},{12,8},{1,5},{5,1},{9,13},{13,9},{2,6},{6,2},{1... | collective-permute-start | bytes 294920 | tf_op jit(solution)/shard_map/ppermute | solution.py:181
  52.1 6.1 %collective-permute-start.19 = (bf16[12,1280]{1,0:T(8,128)(2,1)S(1)}, bf16[12,1280]{1,0:T(8,128)(2,1)S(1)}, u32[]{:S(2)}, u32[]{:S(2)}) collective-permute-start(bf16[12,1280]{1,0:T(8,128)(2,1)S(1)} %get-tuple-element.52), channel_id=1, source_target_pairs={{0,3},{1,2},{2,1},{3,0},{4,7},{5,6},{6,5},{7,4},{8,11},{9,10},{10,... | collective-permute-start | bytes 92168 | tf_op jit(solution)/shard_map/ppermute | solution.py:181
  54.6 4.9 %collective-permute-start.20 = (bf16[12,1280]{1,0:T(8,128)(2,1)S(1)}, bf16[12,1280]{1,0:T(8,128)(2,1)S(1)}, u32[]{:S(2)}, u32[]{:S(2)}) collective-permute-start(bf16[12,1280]{1,0:T(8,128)(2,1)S(1)} %get-tuple-element.53), channel_id=1, source_target_pairs={{0,2},{1,3},{2,0},{3,1},{4,6},{5,7},{6,4},{7,5},{8,10},{9,11},{10,... | collective-permute-start | bytes 92168 | tf_op jit(solution)/shard_map/ppermute | solution.py:181
  54.6 4.9 %collective-permute-start.21 = (bf16[12,1280]{1,0:T(8,128)(2,1)S(1)}, bf16[12,1280]{1,0:T(8,128)(2,1)S(1)}, u32[]{:S(2)}, u32[]{:S(2)}) collective-permute-start(bf16[12,1280]{1,0:T(8,128)(2,1)S(1)} %get-tuple-element.54), channel_id=1, source_target_pairs={{0,1},{1,0},{2,3},{3,2},{4,5},{5,4},{6,7},{7,6},{8,9},{9,8},{10,11... | collective-permute-start | bytes 92168 | tf_op jit(solution)/shard_map/ppermute | solution.py:181

commit v7 on v6

--- a/solution.py
+++ b/solution.py
@@ -147,11 +147,12 @@
 MIB = 1024 * 1024
 
 
-def call(kernel, outs, operands, scratch=(), smem=(), resident=(), remote=(), micros=2, limit=8):
+def call(kernel, outs, operands, scratch=(), smem=(), resident=(), remote=(), free=(), micros=2, limit=8):
     specs = []
     placed = []
     for place, operand in enumerate(operands):
         space = pltpu.SMEM if place in smem else pltpu.HBM if place in remote else pltpu.VMEM
+        space = pl.ANY if place in free else space
         specs.append(pl.BlockSpec(memory_space=space))
         if place in resident or place in remote:
             operand = constrained(operand, space)
@@ -167,6 +168,15 @@
     )(*placed)
 
 
+def copy_kernel(value, earlier, out):
+    out[...] = value[...]
+
+
+def after(value, earlier):
+    (value,) = call(copy_kernel, [(value.shape, value.dtype)], (value, earlier), free=(1,))
+    return value
+
+
 def constrained(operand, space):
     return pltpu.with_memory_space_constraint(operand, space)
 
@@ -181,11 +191,17 @@
     return lax.ppermute(value, axis, [(i, i ^ step) for i in range(total)])
 
 
-def slot_picker(per_device, group, assign):
-    sec, tp = lax.axis_index("sec"), lax.axis_index("tp")
+def group_slots(group, assign):
+    tp = lax.axis_index("tp")
     slots = jnp.zeros((1, group), jnp.int32)
     for index in range(assign.shape[1] // group):
         slots = jnp.where(tp == index, assign[:, index * group : (index + 1) * group], slots)
+    return slots
+
+
+def slot_picker(per_device, slots):
+    sec = lax.axis_index("sec")
+    group = slots.shape[1]
     line = lax.broadcasted_iota(jnp.int32, (16, group), 0)
     wanted = jnp.where(line < 8, sec * per_device + line, (sec ^ 3) * per_device + line - 8)
     inside = (line & 7) < per_device
@@ -208,7 +224,9 @@
                 rows[side, at : at + 1, :] = others[line : line + 1, h * width : (h + 1) * width]
 
 
-def pick_own_kernel(per_device, group, query, pairs, assign, out, query_here, pairs_here, assign_here, rows, sems):
+def pick_own_kernel(
+    per_device, group, query, pairs, assign, out, picker, query_here, pairs_here, assign_here, rows, sems
+):
     copies = [
         pltpu.make_async_copy(source, target, sems.at[index])
         for index, (source, target) in enumerate(
@@ -219,12 +237,13 @@
         copy.start()
     for copy in copies:
         copy.wait()
-    split_heads(per_device, slot_picker(per_device, group, assign_here), query_here, pairs_here, rows)
+    picker[...] = slot_picker(per_device, group_slots(group, assign_here))
+    split_heads(per_device, picker[...], query_here, pairs_here, rows)
     out[...] = rows[...].astype(jnp.bfloat16)
 
 
-def pick_other_kernel(per_device, group, own, query, pairs, assign, keep, send, rows):
-    split_heads(per_device, slot_picker(per_device, group, assign), query, pairs, rows)
+def pick_other_kernel(per_device, own, picker, query, pairs, keep, send, rows):
+    split_heads(per_device, picker[...], query, pairs, rows)
     here = lax.axis_index("sec") & 1
     keep[here] = own[0]
     keep[1 - here] = rows[0].astype(jnp.bfloat16)
@@ -296,31 +315,28 @@
     out[...] = rows[...].astype(jnp.bfloat16)
 
 
-def project_kernel(per_device, group, own, beside, across, corner, assign, resid, weight, *outs):
+def project_kernel(far, per_device, first, second, assign, resid, weight, keep, send):
     sec, tp = lax.axis_index("sec"), lax.axis_index("tp")
-    count = assign.shape[1]
-    lines = jnp.concatenate([own[...], beside[...], across[...], corner[...]], axis=0)
-    line = lax.broadcasted_iota(jnp.int32, (64, count), 0)
-    request = lax.broadcasted_iota(jnp.int32, (64, count), 1)
-    number = jnp.zeros((64, count), jnp.int32)
-    for limit in range(1, 4):
-        number = number + jnp.where(request >= limit * group, 1, 0)
-    block, place = line >> 4, (line >> 2) & 3
-    from_sec = sec ^ block ^ (block >> 1) ^ jnp.where(place > 0, 1, 0)
-    slot = from_sec * per_device + (line & 3)
-    match = (number == (tp ^ place)) & (jnp.broadcast_to(assign[...], (64, count)) == slot)
-    match = jnp.where(match & ((line & 3) < per_device), 1.0, 0.0).astype(jnp.bfloat16)
-    ordered = lax.dot_general(match, lines, (((0,), (0,)), ((), ())), preferred_element_type=jnp.float32)
-    total = jnp.dot(ordered.astype(jnp.bfloat16), weight[...], preferred_element_type=jnp.float32)
-    line = lax.broadcasted_iota(jnp.int32, (count, group), 0)
-    match = line == lax.broadcasted_iota(jnp.int32, (count, group), 1) + tp * group
+    base = sec ^ (3 * far)
+    share = 2 * per_device
+    count = keep.shape[0]
+    lines = jnp.concatenate([first[...], second[...]], axis=0)
+    shape = (count, lines.shape[0])
+    line = lax.broadcasted_iota(jnp.int32, shape, 1)
+    place, index = (line >> 2) & 3, line & 3
+    from_sec = base ^ (line >> 4) ^ jnp.where(place > 0, 1, 0)
+    row = (tp ^ place) * share + (from_sec & 1) * per_device + index
+    match = (lax.broadcasted_iota(jnp.int32, shape, 0) == row) & (index < per_device)
     match = jnp.where(match, 1.0, 0.0).astype(jnp.bfloat16)
+    ordered = jnp.dot(match, lines, preferred_element_type=jnp.float32).astype(jnp.bfloat16)
+    total = jnp.dot(ordered, weight[...], preferred_element_type=jnp.float32)
+    group = resid.shape[0]
+    slots = jnp.broadcast_to(group_slots(group, assign), (count, group)) - share * (base >> 1)
+    match = lax.broadcasted_iota(jnp.int32, (count, group), 0) == slots + tp * share
+    match = jnp.where(match & (slots >= 0) & (slots < share), 1.0, 0.0).astype(jnp.bfloat16)
     total = total + jnp.dot(match, resid[...], preferred_element_type=jnp.float32)
-    half = count // 2
-    for index in range(2):
-        rows = total[index * half : (index + 1) * half]
-        outs[2 * index][...] = rows
-        outs[2 * index + 1][...] = rows.astype(jnp.bfloat16)
+    keep[...] = total
+    send[...] = total.astype(jnp.bfloat16)
 
 
 def add_kernel(mine, other, keep, send):
@@ -346,18 +362,24 @@
             send[:, at : at + chunk] = product[half:].astype(jnp.bfloat16)
 
 
+def to_groups(first, second, groups):
+    share = first.shape[0] // groups.shape[0]
+    for index in range(groups.shape[0]):
+        lines = slice(index * share, (index + 1) * share)
+        groups[index, 0:share] = first[lines]
+        groups[index, share : 2 * share] = second[lines]
+
+
 def gate_up_first_kernel(
-    chunk, mine_a, other_a, mine_b, other_b, gain, gate, up, keep, send, features, stream, halves, groups
+    chunk, near, near_other, far, far_other, gain, gate, up, keep, send, features, stream, halves, groups
 ):
     sec, tp = lax.axis_index("sec"), lax.axis_index("tp")
-    half = mine_a.shape[0]
-    group = stream.shape[0]
-    halves[0] = mine_a[...] + other_a[...].astype(jnp.float32)
-    halves[1] = mine_b[...] + other_b[...].astype(jnp.float32)
-    for index in range(2 * half // group):
-        at = index * group % half
-        groups[index, 0:group] = halves[index * group // half, at : at + group]
-    stream[...] = groups[tp, 0:group]
+    chip = sec >> 1
+    half = near.shape[0]
+    halves[chip] = near[...] + near_other[...].astype(jnp.float32)
+    halves[1 - chip] = far[...] + far_other[...].astype(jnp.float32)
+    to_groups(halves[0], halves[1], groups)
+    stream[...] = groups[tp, 0 : stream.shape[0]]
     first = row_half()
     total = jnp.concatenate([halves[first], halves[1 - first]], axis=0)
     squares = jnp.sum(total * total, axis=1, keepdims=True)
@@ -426,19 +448,29 @@
     rows = weight[pl.ds(pl.multiple_of(away * depth, depth), depth), :]
     product = before[...] + jnp.dot(down_lines(mine, other), rows, preferred_element_type=jnp.float32)
     group = keep.shape[0]
-    for index in range(product.shape[0] // group):
-        groups[index, 0:group] = product[index * group : (index + 1) * group]
-    here = tp ^ (2 * row_half())
-    keep[...] = groups[here, 0:group]
+    half = product.shape[0] // 2
+    swapped = row_half() == 1
+    lower, upper = product[:half], product[half:]
+    to_groups(jnp.where(swapped, upper, lower), jnp.where(swapped, lower, upper), groups)
+    keep[...] = groups[tp, 0:group]
     for step, target in enumerate((first, second, third)):
-        target[...] = groups[here ^ (step + 1), 0:group].astype(jnp.bfloat16)
-
-
-def finish_kernel(third, second, first, stream, mine, out):
+        target[...] = groups[tp ^ (step + 1), 0:group].astype(jnp.bfloat16)
+
+
+def finish_kernel(third, second, first, stream, mine, assign, out):
     total = stream[...] + mine[...]
     for other in (first, second, third):
         total = total + other[...].astype(jnp.float32)
-    out[...] = total.astype(jnp.bfloat16)
+    group = out.shape[0]
+    slots = jnp.broadcast_to(group_slots(group, assign), (group, group))
+    match = jnp.where(lax.broadcasted_iota(jnp.int32, (group, group), 0) == slots, 1.0, 0.0).astype(jnp.bfloat16)
+    coarse = total.astype(jnp.bfloat16)
+    fine = (total - coarse.astype(jnp.float32)).astype(jnp.bfloat16)
+    ordered = [
+        lax.dot_general(match, term, (((0,), (0,)), ((), ())), preferred_element_type=jnp.float32)
+        for term in (coarse, fine)
+    ]
+    out[...] = (ordered[0] + ordered[1]).astype(jnp.bfloat16)
 
 
 def local_pairs(
@@ -467,9 +499,9 @@
 
     query_b, pairs_b = swap(query, "sec", 1), swap(new_kv, "sec", 1)
     block = (2, 16 * per_device, HEAD_WIDTH)
-    (own,) = call(
+    own, picker = call(
         functools.partial(pick_own_kernel, per_device, group),
-        [(block, bf16)],
+        [(block, bf16), ((16, group), bf16)],
         (query, new_kv, assign),
         [
             pltpu.VMEM(query.shape, bf16),
@@ -481,9 +513,9 @@
         remote=(0, 1, 2),
     )
     mine, away = call(
-        functools.partial(pick_other_kernel, per_device, group),
+        functools.partial(pick_other_kernel, per_device),
         [(block, bf16)] * 2,
-        (own, query_b, pairs_b, assign),
+        (own, picker, query_b, pairs_b),
         [pltpu.VMEM(block, f32)],
     )
     other = swap(away, "sec", 3)
@@ -508,17 +540,22 @@
     (own,) = call(gather_kernel, [((16, head_block), bf16)], (*parts, own), [pltpu.VMEM((16, head_block), f32)])
     across = swap(own, "sec", 3)
     beside = swap(own, "sec", 1)
-    corner = swap(across, "sec", 1)
+
     pair = [((half, features), f32), ((half, features), bf16)]
-    mine_a, away_a, mine_b, away_b = call(
-        functools.partial(project_kernel, per_device, group),
-        pair * 2,
-        (own, beside, across, corner, assign, resid, out_weight),
-        resident=(6,),
-    )
-    mine_a, away_a = call(add_kernel, pair, (mine_a, swap(away_a, "tp", 1)))
-    mine_b, away_b = call(add_kernel, pair, (mine_b, swap(away_b, "tp", 2)))
-    other_a, other_b = swap(away_a, "tp", 2), swap(away_b, "tp", 1)
+
+    def project(far, *lines):
+        return call(
+            functools.partial(project_kernel, far, per_device), pair, (*lines, assign, resid, out_weight), resident=(4,)
+        )
+
+    def tp_sum(mine, away):
+        mine, away = call(add_kernel, pair, (mine, swap(away, "tp", 1)))
+        return mine, swap(away, "tp", 2)
+
+    near = project(0, own, beside)
+    corner = swap(after(across, near[1]), "sec", 1)
+    far = project(1, across, corner)
+    sums = tp_sum(*near) + tp_sum(*far)
 
     chunk = min(512, width // 2)
     mine, away, lines, stream = call(
@@ -529,7 +566,7 @@
             ((2 * half, features), bf16),
             ((group, features), f32),
         ],
-        (mine_a, other_a, mine_b, other_b, gain, gate_weight, up_weight),
+        (*sums, gain, gate_weight, up_weight),
         [pltpu.VMEM((2, half, features), f32), pltpu.VMEM((4, 16, features), f32)],
         resident=(5, 6),
     )
@@ -561,7 +598,7 @@
         resident=(3,),
     )
     parts = [swap(parts[step - 1], "tp", step) for step in (3, 2, 1)]
-    (out,) = call(finish_kernel, [((group, features), bf16)], (*parts, stream, mine))
+    (out,) = call(finish_kernel, [((group, features), bf16)], (*parts, stream, mine, assign))
     return out
 
 

time: 60.3 us -> 59.7 us (0.990)
  Pallas kernels: 12.1 us -> 13.3 us
  waiting for transfers between devices: 24.5 us -> 23.5 us
  local copies, waits for them, and re-layouts: 0.73 us -> 0.08 us
    pallas_call x15 -> x17, Pallas kernels: 12.1 us -> 13.3 us  [call(): pl.pallas_call(kernel, out_shape=[jax.ShapeDtypeStruct(shape, dtype) for...]
    ppermute x22, waiting for transfers between devices: 24.5 us -> 23.5 us  [swap(): return lax.ppermute(value, axis, [(i, i ^ step) for i in range(total)])]
    unnamed x34 -> x32, local copies, waits for them, and re-layouts: 0.73 us -> 0.08 us
  transfers between devices with their start and end apart: 22 -> 22, of which waited for: 15 -> 16; matrix products, arithmetic and copies ran while one was open for 0% -> 0% of each run, Pallas kernels for 9% -> 12%
where the time goes in v7:
time: 59.7 us; the launch traced here: 59.5 us
  waiting for transfers between devices  23.5 us (39%)
  starting transfers between devices  22.5 us (38%)
  Pallas kernels  13.3 us (22%)
    ppermute x22, waiting for transfers between devices, swap(): return lax.ppermute(value, axis, [(i, i ^ step) for i in range(total)])  23.5 us
    ppermute x22, starting transfers between devices, swap(): return lax.ppermute(value, axis, [(i, i ^ step) for i in range(total)])  22.5 us
    pallas_call x17, Pallas kernels, call(): pl.pallas_call(kernel, out_shape=[jax.ShapeDtypeStruct(shape, dtype) for...  13.3 us
  transfers between devices with their start and end apart: 22, of which 16 were waited for; matrix products, arithmetic and copies ran while one was open for 0% of the time, Pallas kernels for 12%

profile of v7, /device:TPU:0, one launch (start us, length us, event | category | flops | bytes accessed | tf_op | source)
XLA Modules:
  0.0 59.5 jit_solution(8779890080073908410)
XLA Ops:
  0.0 0.5 collective-permute-start.1
  0.5 0.1 collective-permute-start
  0.6 1.5 %shard_map.118 = (bf16[2,48,128]{2,1,0:T(8,128)(2,1)S(1)}, bf16[16,12]{1,0:T(8,128)(2,1)S(1)}) custom-call(bf16[12,1280]{1,0:T(8,128)(2,1)} %query.1, bf16[12,512]{1,0:T(8,128)(2,1)} %pairs.1, s32[1,48]{1,0:T(1,128)} %bitcast.7), custom_call_target="tpu_custom_call" | custom-call | flops 2000000000 | tf_op jit(solution)/shard_map/pallas_call | solution.py:160
  2.1 0.0 collective-permute-done.1.pairs
  2.1 0.0 collective-permute-done.query
  2.1 0.1 shard_map.119
  2.3 2.5 %collective-permute-start.2 = (bf16[2,48,128]{2,1,0:T(8,128)(2,1)S(1)}, bf16[2,48,128]{2,1,0:T(8,128)(2,1)S(1)}, u32[]{:S(2)}, u32[]{:S(2)}) collective-permute-start(bf16[2,48,128]{2,1,0:T(8,128)(2,1)S(1)} %get-tuple-element.35), channel_id=1, source_target_pairs={{0,12},{4,8},{8,4},{12,0},{1,13},{5,9},{9,5},{13,1},{2,14},{6,10},... | collective-permute-start | bytes 73736 | tf_op jit(solution)/shard_map/ppermute | solution.py:191
  4.8 0.0 copy-done.4
  4.8 0.0 copy-done.1
  4.8 0.0 copy-start.3
  4.8 0.0 copy-start.5
  4.8 1.1 %shard_map.120.near = f32[2,4,1280]{2,1,0:T(4,128)S(1)} custom-call(s32[3]{0:T(128)S(1)} %copy-done.4, bf16[2,48,128]{2,1,0:T(8,128)(2,1)S(1)} %get-tuple-element.36.source, bf16[3,224,1024]{2,1,0:T(8,128)(2,1)S(1)} %copy-done.1, bf16[3,224,1024]{2,1,0:T(8,128)(2,1)S(1)} %copy-done.2), custom_call_target="tpu_custom_call" | custom-call | flops 2000000000 | tf_op jit(solution)/shard_map/pallas_call | solution.py:160
  6.0 0.4 collective-permute-done.2.source
  6.3 1.2 %shard_map.121 = (bf16[4,1280]{1,0:T(4,128)(2,1)S(1)}, bf16[4,1280]{1,0:T(4,128)(2,1)S(1)}, bf16[4,1280]{1,0:T(4,128)(2,1)S(1)}, bf16[4,1280]{1,0:T(4,128)(2,1)S(1)}) custom-call(s32[3]{0:T(128)S(1)} %copy-done.4, bf16[2,48,128]{2,1,0:T(8,128)(2,1)S(1)} %collective-permute-done.2.source, f32[2,4,1280]{2,1,0:T(4,128)S(1)} %shard_map.120.near, ...), custom_call_target="tpu_custom_call" | custom-call | flops 2000000000 | tf_op jit(solution)/shard_map/pallas_call | solution.py:160
  7.5 4.3 %collective-permute-start.3 = (bf16[4,1280]{1,0:T(4,128)(2,1)S(1)}, bf16[4,1280]{1,0:T(4,128)(2,1)S(1)}, u32[]{:S(2)}, u32[]{:S(2)}) collective-permute-start(bf16[4,1280]{1,0:T(4,128)(2,1)S(1)} %get-tuple-element.37), channel_id=1, source_target_pairs={{0,7},{1,6},{2,5},{3,4},{4,3},{5,2},{6,1},{7,0},{8,15},{9,14},{10,... | collective-permute-start | bytes 30728 | tf_op jit(solution)/shard_map/ppermute | solution.py:191
  11.8 0.0 collective-permute-start.4
  11.8 0.7 %collective-permute-start.5 = (bf16[4,1280]{1,0:T(4,128)(2,1)S(1)}, bf16[4,1280]{1,0:T(4,128)(2,1)S(1)}, u32[]{:S(2)}, u32[]{:S(2)}) collective-permute-start(bf16[4,1280]{1,0:T(4,128)(2,1)S(1)} %get-tuple-element.39), channel_id=1, source_target_pairs={{0,5},{1,4},{2,7},{3,6},{4,1},{5,0},{6,3},{7,2},{8,13},{9,12},{10,... | collective-permute-start | bytes 30728 | tf_op jit(solution)/shard_map/ppermute | solution.py:191
  12.5 0.7 %collective-permute-done.3.third = bf16[4,1280]{1,0:T(4,128)(2,1)S(1)} collective-permute-done((bf16[4,1280]{1,0:T(4,128)(2,1)S(1)}, bf16[4,1280]{1,0:T(4,128)(2,1)S(1)}, u32[]{:S(2)}, u32[]{:S(2)}) %collective-permute-start.3) | collective-permute-done | bytes 10272 | tf_op jit(solution)/shard_map/ppermute | solution.py:191
  13.2 2.6 %collective-permute-done.4.second = bf16[4,1280]{1,0:T(4,128)(2,1)S(1)} collective-permute-done((bf16[4,1280]{1,0:T(4,128)(2,1)S(1)}, bf16[4,1280]{1,0:T(4,128)(2,1)S(1)}, u32[]{:S(2)}, u32[]{:S(2)}) %collective-permute-start.4) | collective-permute-done | bytes 10272 | tf_op jit(solution)/shard_map/ppermute | solution.py:191
  15.8 0.0 collective-permute-done.5.first
  15.8 0.5 collective-permute-start.6
  16.3 1.2 %collective-permute-start.9 = (bf16[16,1280]{1,0:T(8,128)(2,1)S(1)}, bf16[16,1280]{1,0:T(8,128)(2,1)S(1)}, u32[]{:S(2)}, u32[]{:S(2)}) collective-permute-start(bf16[16,1280]{1,0:T(8,128)(2,1)S(1)} %shard_map.122.first), channel_id=1, source_target_pairs={{0,12},{4,8},{8,4},{12,0},{1,13},{5,9},{9,5},{13,1},{2,14},{6,10},... | collective-permute-start | bytes 122888 | tf_op jit(solution)/shard_map/ppermute | solution.py:191
  17.5 0.0 collective-permute-done.6.second
  17.5 0.9 %shard_map.123 = (f32[24,1280]{1,0:T(8,128)S(1)}, bf16[24,1280]{1,0:T(8,128)(2,1)S(1)}) custom-call(bf16[16,1280]{1,0:T(8,128)(2,1)S(1)} %shard_map.122.first, bf16[16,1280]{1,0:T(8,128)(2,1)S(1)} %collective-permute-done.6.second, s32[1,48]{1,0:T(1,128)S(1)} %bitcast.8, bf16[12,1280]{1,0:T(8,128)(2,1)S(1)} %copy-done.3, bf16[1280,1280]{1,0:T(8,128)(2,1)S(1)} %copy-done), custom_call_target="tpu_custom_call" | custom-call | flops 2000000000 | tf_op jit(solution)/shard_map/pallas_call | solution.py:160
  18.4 1.5 %collective-permute-done.9.value.first = bf16[16,1280]{1,0:T(8,128)(2,1)S(1)} collective-permute-done((bf16[16,1280]{1,0:T(8,128)(2,1)S(1)}, bf16[16,1280]{1,0:T(8,128)(2,1)S(1)}, u32[]{:S(2)}, u32[]{:S(2)}) %collective-permute-start.9) | collective-permute-done | bytes 40992 | tf_op jit(solution)/shard_map/ppermute | solution.py:191
  19.9 0.0 copy-start.6
  19.9 0.0 slice-start.1
  19.9 0.0 slice-start.4
  20.0 0.2 collective-permute-start.10
  20.1 0.0 collective-permute-start.7
  20.1 1.1 %collective-permute-done.10.second = bf16[16,1280]{1,0:T(8,128)(2,1)S(1)} collective-permute-done((bf16[16,1280]{1,0:T(8,128)(2,1)S(1)}, bf16[16,1280]{1,0:T(8,128)(2,1)S(1)}, u32[]{:S(2)}, u32[]{:S(2)}) %collective-permute-start.10) | collective-permute-done | bytes 40992 | tf_op jit(solution)/shard_map/ppermute | solution.py:191
  21.2 0.9 %shard_map.126 = (f32[24,1280]{1,0:T(8,128)S(1)}, bf16[24,1280]{1,0:T(8,128)(2,1)S(1)}) custom-call(bf16[16,1280]{1,0:T(8,128)(2,1)S(1)} %collective-permute-done.9.value.first, bf16[16,1280]{1,0:T(8,128)(2,1)S(1)} %collective-permute-done.10.second, s32[1,48]{1,0:T(1,128)S(1)} %bitcast.9, bf16[12,1280]{1,0:T(8,128)(2,1)S(1)} %copy-done.3, ...), custom_call_target="tpu_custom_call" | custom-call | flops 2000000000 | tf_op jit(solution)/shard_map/pallas_call | solution.py:160
  22.1 1.0 %collective-permute-start.11 = (bf16[24,1280]{1,0:T(8,128)(2,1)S(1)}, bf16[24,1280]{1,0:T(8,128)(2,1)S(1)}, u32[]{:S(2)}, u32[]{:S(2)}) collective-permute-start(bf16[24,1280]{1,0:T(8,128)(2,1)S(1)} %get-tuple-element.46), channel_id=1, source_target_pairs={{0,1},{1,0},{2,3},{3,2},{4,5},{5,4},{6,7},{7,6},{8,9},{9,8},{10,11... | collective-permute-start | bytes 184328 | tf_op jit(solution)/shard_map/ppermute | solution.py:191
  23.1 1.3 %collective-permute-done.7.other = bf16[24,1280]{1,0:T(8,128)(2,1)S(1)} collective-permute-done((bf16[24,1280]{1,0:T(8,128)(2,1)S(1)}, bf16[24,1280]{1,0:T(8,128)(2,1)S(1)}, u32[]{:S(2)}, u32[]{:S(2)}) %collective-permute-start.7) | collective-permute-done | bytes 61472 | tf_op jit(solution)/shard_map/ppermute | solution.py:191
  24.5 1.8 %collective-permute-start.8 = (bf16[24,1280]{1,0:T(8,128)(2,1)S(1)}, bf16[24,1280]{1,0:T(8,128)(2,1)S(1)}, u32[]{:S(2)}, u32[]{:S(2)}) collective-permute-start(bf16[24,1280]{1,0:T(8,128)(2,1)S(1)} %get-tuple-element.44), channel_id=1, source_target_pairs={{0,2},{1,3},{2,0},{3,1},{4,6},{5,7},{6,4},{7,5},{8,10},{9,11},{10,... | collective-permute-start | bytes 184328 | tf_op jit(solution)/shard_map/ppermute | solution.py:191
  26.3 0.1 collective-permute-done.11.other
  26.4 1.7 %collective-permute-start.12 = (bf16[24,1280]{1,0:T(8,128)(2,1)S(1)}, bf16[24,1280]{1,0:T(8,128)(2,1)S(1)}, u32[]{:S(2)}, u32[]{:S(2)}) collective-permute-start(bf16[24,1280]{1,0:T(8,128)(2,1)S(1)} %get-tuple-element.48), channel_id=1, source_target_pairs={{0,2},{1,3},{2,0},{3,1},{4,6},{5,7},{6,4},{7,5},{8,10},{9,11},{10,... | collective-permute-start | bytes 184328 | tf_op jit(solution)/shard_map/ppermute | solution.py:191
  28.2 3.3 %collective-permute-done.8.near_other = bf16[24,1280]{1,0:T(8,128)(2,1)S(1)} collective-permute-done((bf16[24,1280]{1,0:T(8,128)(2,1)S(1)}, bf16[24,1280]{1,0:T(8,128)(2,1)S(1)}, u32[]{:S(2)}, u32[]{:S(2)}) %collective-permute-start.8) | collective-permute-done | bytes 61472 | tf_op jit(solution)/shard_map/ppermute | solution.py:191
  31.4 1.4 %collective-permute-done.12.far_other = bf16[24,1280]{1,0:T(8,128)(2,1)S(1)} collective-permute-done((bf16[24,1280]{1,0:T(8,128)(2,1)S(1)}, bf16[24,1280]{1,0:T(8,128)(2,1)S(1)}, u32[]{:S(2)}, u32[]{:S(2)}) %collective-permute-start.12) | collective-permute-done | bytes 61472 | tf_op jit(solution)/shard_map/ppermute | solution.py:191
  32.9 2.0 %shard_map.128 = (f32[24,4224]{1,0:T(8,128)S(1)}, bf16[24,4224]{1,0:T(8,128)(2,1)S(1)}, bf16[48,1280]{1,0:T(8,128)(2,1)S(1)}, f32[12,1280]{1,0:T(8,128)S(1)}) custom-call(f32[24,1280]{1,0:T(8,128)S(1)} %get-tuple-element.43.near, bf16[24,1280]{1,0:T(8,128)(2,1)S(1)} %collective-permute-done.8.near_other, f32[24,1280]{1,0:T(8,128)S(1)} %get-tuple-element.47.far, ...), custom_call_target="tpu_custom_call" | custom-call | flops 2000000000 | tf_op jit(solution)/shard_map/pallas_call | solution.py:160
  34.9 0.1 collective-permute-start.14
  35.0 1.4 %collective-permute-done.14.other = bf16[24,4224]{1,0:T(8,128)(2,1)S(1)} collective-permute-done((bf16[24,4224]{1,0:T(8,128)(2,1)S(1)}, bf16[24,4224]{1,0:T(8,128)(2,1)S(1)}, u32[]{:S(2)}, u32[]{:S(2)}) %collective-permute-start.14) | collective-permute-done | bytes 202784 | tf_op jit(solution)/shard_map/ppermute | solution.py:191
  36.4 0.2 shard_map.130
  36.6 1.2 %collective-permute-start.15 = (bf16[24,4224]{1,0:T(8,128)(2,1)S(1)}, bf16[24,4224]{1,0:T(8,128)(2,1)S(1)}, u32[]{:S(2)}, u32[]{:S(2)}) collective-permute-start(bf16[24,4224]{1,0:T(8,128)(2,1)S(1)} %get-tuple-element.54), channel_id=1, source_target_pairs={{0,12},{4,8},{8,4},{12,0},{1,13},{5,9},{9,5},{13,1},{2,14},{6,10},... | collective-permute-start | bytes 608264 | tf_op jit(solution)/shard_map/ppermute | solution.py:191
  37.9 1.9 %shard_map.129 = (f32[24,4096]{1,0:T(8,128)S(1)}, bf16[24,4096]{1,0:T(8,128)(2,1)S(1)}) custom-call(bf16[48,1280]{1,0:T(8,128)(2,1)S(1)} %get-tuple-element.49.features, bf16[1280,4096]{1,0:T(8,128)(2,1)S(1)} %bitcast.2, bf16[1280,4096]{1,0:T(8,128)(2,1)S(1)} %bitcast.4), custom_call_target="tpu_custom_call" | custom-call | flops 2000000000 | tf_op jit(solution)/shard_map/pallas_call | solution.py:160
  39.8 0.4 collective-permute-start.13
  40.2 1.1 %collective-permute-done.13.beside = bf16[24,4096]{1,0:T(8,128)(2,1)S(1)} collective-permute-done((bf16[24,4096]{1,0:T(8,128)(2,1)S(1)}, bf16[24,4096]{1,0:T(8,128)(2,1)S(1)}, u32[]{:S(2)}, u32[]{:S(2)}) %collective-permute-start.13) | collective-permute-done | bytes 196640 | tf_op jit(solution)/shard_map/ppermute | solution.py:191
  41.3 2.4 %collective-permute-done.15.across = bf16[24,4224]{1,0:T(8,128)(2,1)S(1)} collective-permute-done((bf16[24,4224]{1,0:T(8,128)(2,1)S(1)}, bf16[24,4224]{1,0:T(8,128)(2,1)S(1)}, u32[]{:S(2)}, u32[]{:S(2)}) %collective-permute-start.15) | collective-permute-done | bytes 202784 | tf_op jit(solution)/shard_map/ppermute | solution.py:191
  43.6 0.2 shard_map.131.mine
  43.9 1.3 %collective-permute-start.16 = (bf16[24,2048]{1,0:T(8,128)(2,1)S(1)}, bf16[24,2048]{1,0:T(8,128)(2,1)S(1)}, u32[]{:S(2)}, u32[]{:S(2)}) collective-permute-start(bf16[24,2048]{1,0:T(8,128)(2,1)S(1)} %shard_map.131.mine), channel_id=1, source_target_pairs={{0,12},{4,8},{8,4},{12,0},{1,13},{5,9},{9,5},{13,1},{2,14},{6,10},... | collective-permute-start | bytes 294920 | tf_op jit(solution)/shard_map/ppermute | solution.py:191
  45.2 0.4 collective-permute-start.18
  45.5 3.2 %collective-permute-done.16.mine = bf16[24,2048]{1,0:T(8,128)(2,1)S(1)} collective-permute-done((bf16[24,2048]{1,0:T(8,128)(2,1)S(1)}, bf16[24,2048]{1,0:T(8,128)(2,1)S(1)}, u32[]{:S(2)}, u32[]{:S(2)}) %collective-permute-start.16) | collective-permute-done | bytes 98336 | tf_op jit(solution)/shard_map/ppermute | solution.py:191
  48.7 0.1 collective-permute-start.17
  48.8 0.0 collective-permute-done.18.other
  48.9 1.0 %shard_map.132.before = f32[48,1280]{1,0:T(8,128)S(1)} custom-call(bf16[24,2048]{1,0:T(8,128)(2,1)S(1)} %shard_map.131.mine, bf16[24,2048]{1,0:T(8,128)(2,1)S(1)} %collective-permute-done.18.other, bf16[4096,1280]{1,0:T(8,128)(2,1)S(1)} %bitcast.6), custom_call_target="tpu_custom_call" | custom-call | flops 2000000000 | tf_op jit(solution)/shard_map/pallas_call | solution.py:160
  49.9 0.1 collective-permute-done.17.other
  50.0 1.1 %shard_map.133 = (f32[12,1280]{1,0:T(8,128)S(1)}, bf16[12,1280]{1,0:T(8,128)(2,1)S(1)}, bf16[12,1280]{1,0:T(8,128)(2,1)S(1)}, bf16[12,1280]{1,0:T(8,128)(2,1)S(1)}) custom-call(bf16[24,2048]{1,0:T(8,128)(2,1)S(1)} %collective-permute-done.16.mine, bf16[24,2048]{1,0:T(8,128)(2,1)S(1)} %collective-permute-done.17.other, f32[48,1280]{1,0:T(8,128)S(1)} %shard_map.132.before, ...), custom_call_target="tpu_custom_call" | custom-call | flops 2000000000 | tf_op jit(solution)/shard_map/pallas_call | solution.py:160
  51.1 1.7 %collective-permute-start.19 = (bf16[12,1280]{1,0:T(8,128)(2,1)S(1)}, bf16[12,1280]{1,0:T(8,128)(2,1)S(1)}, u32[]{:S(2)}, u32[]{:S(2)}) collective-permute-start(bf16[12,1280]{1,0:T(8,128)(2,1)S(1)} %get-tuple-element.56), channel_id=1, source_target_pairs={{0,3},{1,2},{2,1},{3,0},{4,7},{5,6},{6,5},{7,4},{8,11},{9,10},{10,... | collective-permute-start | bytes 92168 | tf_op jit(solution)/shard_map/ppermute | solution.py:191
  52.8 0.0 collective-permute-start.20
  52.8 2.7 %collective-permute-start.21 = (bf16[12,1280]{1,0:T(8,128)(2,1)S(1)}, bf16[12,1280]{1,0:T(8,128)(2,1)S(1)}, u32[]{:S(2)}, u32[]{:S(2)}) collective-permute-start(bf16[12,1280]{1,0:T(8,128)(2,1)S(1)} %get-tuple-element.58), channel_id=1, source_target_pairs={{0,1},{1,0},{2,3},{3,2},{4,5},{5,4},{6,7},{7,6},{8,9},{9,8},{10,11... | collective-permute-start | bytes 92168 | tf_op jit(solution)/shard_map/ppermute | solution.py:191
  55.5 1.7 %collective-permute-done.19.third = bf16[12,1280]{1,0:T(8,128)(2,1)S(1)} collective-permute-done((bf16[12,1280]{1,0:T(8,128)(2,1)S(1)}, bf16[12,1280]{1,0:T(8,128)(2,1)S(1)}, u32[]{:S(2)}, u32[]{:S(2)}) %collective-permute-start.19) | collective-permute-done | bytes 30752 | tf_op jit(solution)/shard_map/ppermute | solution.py:191
  57.2 1.2 %collective-permute-done.20.second = bf16[12,1280]{1,0:T(8,128)(2,1)S(1)} collective-permute-done((bf16[12,1280]{1,0:T(8,128)(2,1)S(1)}, bf16[12,1280]{1,0:T(8,128)(2,1)S(1)}, u32[]{:S(2)}, u32[]{:S(2)}) %collective-permute-start.20) | collective-permute-done | bytes 30752 | tf_op jit(solution)/shard_map/ppermute | solution.py:191
  58.4 0.0 collective-permute-done.21.first
  58.4 1.1 %shard_map.134 = bf16[12,1280]{1,0:T(8,128)(2,1)} custom-call(bf16[12,1280]{1,0:T(8,128)(2,1)S(1)} %collective-permute-done.19.third, bf16[12,1280]{1,0:T(8,128)(2,1)S(1)} %collective-permute-done.20.second, bf16[12,1280]{1,0:T(8,128)(2,1)S(1)} %collective-permute-done.21.first, f32[12,1280]{1,0:T(8,128)S(1)} %get-tuple-element.59.stream, ...), custom_call_target="tpu_custom_call" | custom-call | flops 2000000000 | tf_op jit(solution)/shard_map/pallas_call | solution.py:160
  (33 shorter events, 0.1 us)
Async XLA Ops:
  0.0 4.8 %copy-start.4 = (s32[3]{0:T(128)S(1)}, s32[3]{0:T(128)}, u32[]{:S(2)}) copy-start(s32[3]{0:T(128)} %lengths.3) | copy-start | bytes 40
  0.0 4.8 %copy-start.2 = (bf16[3,224,1024]{2,1,0:T(8,128)(2,1)S(1)}, bf16[3,224,1024]{2,1,0:T(8,128)(2,1)}, u32[]{:S(2)}) copy-start(bf16[3,224,1024]{2,1,0:T(8,128)(2,1)} %values.3) | copy-start | bytes 4128772
  0.0 4.8 %copy-start.1 = (bf16[3,224,1024]{2,1,0:T(8,128)(2,1)S(1)}, bf16[3,224,1024]{2,1,0:T(8,128)(2,1)}, u32[]{:S(2)}) copy-start(bf16[3,224,1024]{2,1,0:T(8,128)(2,1)} %keys.3) | copy-start | bytes 4128772
  0.0 2.1 %collective-permute-start.1 = (bf16[12,512]{1,0:T(8,128)(2,1)}, bf16[12,512]{1,0:T(8,128)(2,1)S(1)}, u32[]{:S(2)}, u32[]{:S(2)}) collective-permute-start(bf16[12,512]{1,0:T(8,128)(2,1)} %pairs.1), channel_id=1, source_target_pairs={{0,4},{4,0},{8,12},{12,8},{1,5},{5,1},{9,13},{13,9},{2,6},{6,2},{1... | collective-permute-start | bytes 36872 | tf_op jit(solution)/shard_map/ppermute | solution.py:191
  0.5 1.6 %collective-permute-start = (bf16[12,1280]{1,0:T(8,128)(2,1)}, bf16[12,1280]{1,0:T(8,128)(2,1)S(1)}, u32[]{:S(2)}, u32[]{:S(2)}) collective-permute-start(bf16[12,1280]{1,0:T(8,128)(2,1)} %query.1), channel_id=1, source_target_pairs={{0,4},{4,0},{8,12},{12,8},{1,5},{5,1},{9,13},{13,9},{2,6},{6,2},{1... | collective-permute-start | bytes 92168 | tf_op jit(solution)/shard_map/ppermute | solution.py:191
  2.3 4.1 %collective-permute-start.2 = (bf16[2,48,128]{2,1,0:T(8,128)(2,1)S(1)}, bf16[2,48,128]{2,1,0:T(8,128)(2,1)S(1)}, u32[]{:S(2)}, u32[]{:S(2)}) collective-permute-start(bf16[2,48,128]{2,1,0:T(8,128)(2,1)S(1)} %get-tuple-element.35), channel_id=1, source_target_pairs={{0,12},{4,8},{8,4},{12,0},{1,13},{5,9},{9,5},{13,1},{2,14},{6,10},... | collective-permute-start | bytes 73736 | tf_op jit(solution)/shard_map/ppermute | solution.py:191
  4.8 12.7 %copy-start = (bf16[1280,1280]{1,0:T(8,128)(2,1)S(1)}, bf16[1280,1280]{1,0:T(8,128)(2,1)}, u32[]{:S(2)}) copy-start(bf16[1280,1280]{1,0:T(8,128)(2,1)} %weight.5) | copy-start | bytes 9830404
  4.8 12.7 %copy-start.3 = (bf16[12,1280]{1,0:T(8,128)(2,1)S(1)}, bf16[12,1280]{1,0:T(8,128)(2,1)}, u32[]{:S(2)}) copy-start(bf16[12,1280]{1,0:T(8,128)(2,1)} %resid.3) | copy-start | bytes 92164
  4.8 12.7 %copy-start.5 = (s32[48]{0:T(128)S(1)}, s32[48]{0:T(128)}, u32[]{:S(2)}) copy-start(s32[48]{0:T(128)} %param.18) | copy-start | bytes 580
  7.5 5.7 %collective-permute-start.3 = (bf16[4,1280]{1,0:T(4,128)(2,1)S(1)}, bf16[4,1280]{1,0:T(4,128)(2,1)S(1)}, u32[]{:S(2)}, u32[]{:S(2)}) collective-permute-start(bf16[4,1280]{1,0:T(4,128)(2,1)S(1)} %get-tuple-element.37), channel_id=1, source_target_pairs={{0,7},{1,6},{2,5},{3,4},{4,3},{5,2},{6,1},{7,0},{8,15},{9,14},{10,... | collective-permute-start | bytes 30728 | tf_op jit(solution)/shard_map/ppermute | solution.py:191
  11.8 4.0 %collective-permute-start.4 = (bf16[4,1280]{1,0:T(4,128)(2,1)S(1)}, bf16[4,1280]{1,0:T(4,128)(2,1)S(1)}, u32[]{:S(2)}, u32[]{:S(2)}) collective-permute-start(bf16[4,1280]{1,0:T(4,128)(2,1)S(1)} %get-tuple-element.38), channel_id=1, source_target_pairs={{0,6},{1,7},{2,4},{3,5},{4,2},{5,3},{6,0},{7,1},{8,14},{9,15},{10,... | collective-permute-start | bytes 30728 | tf_op jit(solution)/shard_map/ppermute | solution.py:191
  11.8 4.0 %collective-permute-start.5 = (bf16[4,1280]{1,0:T(4,128)(2,1)S(1)}, bf16[4,1280]{1,0:T(4,128)(2,1)S(1)}, u32[]{:S(2)}, u32[]{:S(2)}) collective-permute-start(bf16[4,1280]{1,0:T(4,128)(2,1)S(1)} %get-tuple-element.39), channel_id=1, source_target_pairs={{0,5},{1,4},{2,7},{3,6},{4,1},{5,0},{6,3},{7,2},{8,13},{9,12},{10,... | collective-permute-start | bytes 30728 | tf_op jit(solution)/shard_map/ppermute | solution.py:191
  15.8 1.7 %collective-permute-start.6 = (bf16[16,1280]{1,0:T(8,128)(2,1)S(1)}, bf16[16,1280]{1,0:T(8,128)(2,1)S(1)}, u32[]{:S(2)}, u32[]{:S(2)}) collective-permute-start(bf16[16,1280]{1,0:T(8,128)(2,1)S(1)} %shard_map.122.first), channel_id=1, source_target_pairs={{0,4},{4,0},{8,12},{12,8},{1,5},{5,1},{9,13},{13,9},{2,6},{6,2},{1... | collective-permute-start | bytes 122888 | tf_op jit(solution)/shard_map/ppermute | solution.py:191
  16.3 3.6 %collective-permute-start.9 = (bf16[16,1280]{1,0:T(8,128)(2,1)S(1)}, bf16[16,1280]{1,0:T(8,128)(2,1)S(1)}, u32[]{:S(2)}, u32[]{:S(2)}) collective-permute-start(bf16[16,1280]{1,0:T(8,128)(2,1)S(1)} %shard_map.122.first), channel_id=1, source_target_pairs={{0,12},{4,8},{8,4},{12,0},{1,13},{5,9},{9,5},{13,1},{2,14},{6,10},... | collective-permute-start | bytes 122888 | tf_op jit(solution)/shard_map/ppermute | solution.py:191
  19.9 12.9 %slice-start = ((s8[10485760]{0:T(1024)(128)(4,1)}), s8[4194304]{0:T(1024)(128)(4,1)S(1)}, s32[]{:S(2)}) async-start(s8[10485760]{0:T(1024)(128)(4,1)} %bitcast.1), calls=%async_computation | async-start | bytes 8388608
  19.9 12.9 %slice-start.3 = ((s8[10485760]{0:T(1024)(128)(4,1)}), s8[4194304]{0:T(1024)(128)(4,1)S(1)}, s32[]{:S(2)}) async-start(s8[10485760]{0:T(1024)(128)(4,1)} %bitcast.3), calls=%async_computation.3 | async-start | bytes 8388608
  19.9 8.2 %copy-start.6 = (bf16[1280]{0:T(1024)(128)(2,1)S(1)}, bf16[1280]{0:T(1024)(128)(2,1)}, u32[]{:S(2)}) copy-start(bf16[1280]{0:T(1024)(128)(2,1)} %param.20) | copy-start | bytes 7684
  19.9 12.9 %slice-start.1 = ((s8[10485760]{0:T(1024)(128)(4,1)}), s8[4194304]{0:T(1024)(128)(4,1)S(1)}, s32[]{:S(2)}) async-start(s8[10485760]{0:T(1024)(128)(4,1)} %bitcast.1), calls=%async_computation.1 | async-start | bytes 8388608
  19.9 12.9 %slice-start.4 = ((s8[10485760]{0:T(1024)(128)(4,1)}), s8[4194304]{0:T(1024)(128)(4,1)S(1)}, s32[]{:S(2)}) async-start(s8[10485760]{0:T(1024)(128)(4,1)} %bitcast.3), calls=%async_computation.4 | async-start | bytes 8388608
  20.0 1.3 %collective-permute-start.10 = (bf16[16,1280]{1,0:T(8,128)(2,1)S(1)}, bf16[16,1280]{1,0:T(8,128)(2,1)S(1)}, u32[]{:S(2)}, u32[]{:S(2)}) collective-permute-start(bf16[16,1280]{1,0:T(8,128)(2,1)S(1)} %shard_map.125), channel_id=1, source_target_pairs={{0,4},{4,0},{8,12},{12,8},{1,5},{5,1},{9,13},{13,9},{2,6},{6,2},{1... | collective-permute-start | bytes 122888 | tf_op jit(solution)/shard_map/ppermute | solution.py:191
  20.1 4.3 %collective-permute-start.7 = (bf16[24,1280]{1,0:T(8,128)(2,1)S(1)}, bf16[24,1280]{1,0:T(8,128)(2,1)S(1)}, u32[]{:S(2)}, u32[]{:S(2)}) collective-permute-start(bf16[24,1280]{1,0:T(8,128)(2,1)S(1)} %get-tuple-element.42.earlier), channel_id=1, source_target_pairs={{0,1},{1,0},{2,3},{3,2},{4,5},{5,4},{6,7},{7,6},{8,9},{9,8},{10,11... | collective-permute-start | bytes 184328 | tf_op jit(solution)/shard_map/ppermute | solution.py:191
  22.1 4.3 %collective-permute-start.11 = (bf16[24,1280]{1,0:T(8,128)(2,1)S(1)}, bf16[24,1280]{1,0:T(8,128)(2,1)S(1)}, u32[]{:S(2)}, u32[]{:S(2)}) collective-permute-start(bf16[24,1280]{1,0:T(8,128)(2,1)S(1)} %get-tuple-element.46), channel_id=1, source_target_pairs={{0,1},{1,0},{2,3},{3,2},{4,5},{5,4},{6,7},{7,6},{8,9},{9,8},{10,11... | collective-permute-start | bytes 184328 | tf_op jit(solution)/shard_map/ppermute | solution.py:191
  24.4 8.4 %slice-start.2 = ((s8[10485760]{0:T(1024)(128)(4,1)}), s8[2097152]{0:T(1024)(128)(4,1)S(1)}, s32[]{:S(2)}) async-start(s8[10485760]{0:T(1024)(128)(4,1)} %bitcast.1), calls=%async_computation.2 | async-start | bytes 4194304
  24.4 8.4 %slice-start.5 = ((s8[10485760]{0:T(1024)(128)(4,1)}), s8[2097152]{0:T(1024)(128)(4,1)S(1)}, s32[]{:S(2)}) async-start(s8[10485760]{0:T(1024)(128)(4,1)} %bitcast.3), calls=%async_computation.5 | async-start | bytes 4194304
  24.5 6.9 %collective-permute-start.8 = (bf16[24,1280]{1,0:T(8,128)(2,1)S(1)}, bf16[24,1280]{1,0:T(8,128)(2,1)S(1)}, u32[]{:S(2)}, u32[]{:S(2)}) collective-permute-start(bf16[24,1280]{1,0:T(8,128)(2,1)S(1)} %get-tuple-element.44), channel_id=1, source_target_pairs={{0,2},{1,3},{2,0},{3,1},{4,6},{5,7},{6,4},{7,5},{8,10},{9,11},{10,... | collective-permute-start | bytes 184328 | tf_op jit(solution)/shard_map/ppermute | solution.py:191
  26.4 6.4 %collective-permute-start.12 = (bf16[24,1280]{1,0:T(8,128)(2,1)S(1)}, bf16[24,1280]{1,0:T(8,128)(2,1)S(1)}, u32[]{:S(2)}, u32[]{:S(2)}) collective-permute-start(bf16[24,1280]{1,0:T(8,128)(2,1)S(1)} %get-tuple-element.48), channel_id=1, source_target_pairs={{0,2},{1,3},{2,0},{3,1},{4,6},{5,7},{6,4},{7,5},{8,10},{9,11},{10,... | collective-permute-start | bytes 184328 | tf_op jit(solution)/shard_map/ppermute | solution.py:191
  34.9 1.5 %collective-permute-start.14 = (bf16[24,4224]{1,0:T(8,128)(2,1)S(1)}, bf16[24,4224]{1,0:T(8,128)(2,1)S(1)}, u32[]{:S(2)}, u32[]{:S(2)}) collective-permute-start(bf16[24,4224]{1,0:T(8,128)(2,1)S(1)} %get-tuple-element.53), channel_id=1, source_target_pairs={{0,4},{4,0},{8,12},{12,8},{1,5},{5,1},{9,13},{13,9},{2,6},{6,2},{1... | collective-permute-start | bytes 608264 | tf_op jit(solution)/shard_map/ppermute | solution.py:191
  36.6 7.0 %collective-permute-start.15 = (bf16[24,4224]{1,0:T(8,128)(2,1)S(1)}, bf16[24,4224]{1,0:T(8,128)(2,1)S(1)}, u32[]{:S(2)}, u32[]{:S(2)}) collective-permute-start(bf16[24,4224]{1,0:T(8,128)(2,1)S(1)} %get-tuple-element.54), channel_id=1, source_target_pairs={{0,12},{4,8},{8,4},{12,0},{1,13},{5,9},{9,5},{13,1},{2,14},{6,10},... | collective-permute-start | bytes 608264 | tf_op jit(solution)/shard_map/ppermute | solution.py:191
  37.9 11.0 %slice-start.6 = ((s8[10485760]{0:T(1024)(128)(4,1)}), s8[4194304]{0:T(1024)(128)(4,1)S(1)}, s32[]{:S(2)}) async-start(s8[10485760]{0:T(1024)(128)(4,1)} %bitcast.5), calls=%async_computation.6 | async-start | bytes 8388608
  37.9 11.0 %slice-start.7 = ((s8[10485760]{0:T(1024)(128)(4,1)}), s8[4194304]{0:T(1024)(128)(4,1)S(1)}, s32[]{:S(2)}) async-start(s8[10485760]{0:T(1024)(128)(4,1)} %bitcast.5), calls=%async_computation.7 | async-start | bytes 8388608
  37.9 11.0 %slice-start.8 = ((s8[10485760]{0:T(1024)(128)(4,1)}), s8[2097152]{0:T(1024)(128)(4,1)S(1)}, s32[]{:S(2)}) async-start(s8[10485760]{0:T(1024)(128)(4,1)} %bitcast.5), calls=%async_computation.8 | async-start | bytes 4194304
  39.8 1.5 %collective-permute-start.13 = (bf16[24,4096]{1,0:T(8,128)(2,1)S(1)}, bf16[24,4096]{1,0:T(8,128)(2,1)S(1)}, u32[]{:S(2)}, u32[]{:S(2)}) collective-permute-start(bf16[24,4096]{1,0:T(8,128)(2,1)S(1)} %get-tuple-element.51), channel_id=1, source_target_pairs={{0,4},{4,0},{8,12},{12,8},{1,5},{5,1},{9,13},{13,9},{2,6},{6,2},{1... | collective-permute-start | bytes 589832 | tf_op jit(solution)/shard_map/ppermute | solution.py:191
  43.9 4.8 %collective-permute-start.16 = (bf16[24,2048]{1,0:T(8,128)(2,1)S(1)}, bf16[24,2048]{1,0:T(8,128)(2,1)S(1)}, u32[]{:S(2)}, u32[]{:S(2)}) collective-permute-start(bf16[24,2048]{1,0:T(8,128)(2,1)S(1)} %shard_map.131.mine), channel_id=1, source_target_pairs={{0,12},{4,8},{8,4},{12,0},{1,13},{5,9},{9,5},{13,1},{2,14},{6,10},... | collective-permute-start | bytes 294920 | tf_op jit(solution)/shard_map/ppermute | solution.py:191
  45.2 3.7 %collective-permute-start.18 = (bf16[24,2048]{1,0:T(8,128)(2,1)S(1)}, bf16[24,2048]{1,0:T(8,128)(2,1)S(1)}, u32[]{:S(2)}, u32[]{:S(2)}) collective-permute-start(bf16[24,2048]{1,0:T(8,128)(2,1)S(1)} %shard_map.131.mine), channel_id=1, source_target_pairs={{0,4},{4,0},{8,12},{12,8},{1,5},{5,1},{9,13},{13,9},{2,6},{6,2},{1... | collective-permute-start | bytes 294920 | tf_op jit(solution)/shard_map/ppermute | solution.py:191
  48.7 1.3 %collective-permute-start.17 = (bf16[24,2048]{1,0:T(8,128)(2,1)S(1)}, bf16[24,2048]{1,0:T(8,128)(2,1)S(1)}, u32[]{:S(2)}, u32[]{:S(2)}) collective-permute-start(bf16[24,2048]{1,0:T(8,128)(2,1)S(1)} %collective-permute-done.16.mine), channel_id=1, source_target_pairs={{0,4},{4,0},{8,12},{12,8},{1,5},{5,1},{9,13},{13,9},{2,6},{6,2},{1... | collective-permute-start | bytes 294920 | tf_op jit(solution)/shard_map/ppermute | solution.py:191
  51.1 6.2 %collective-permute-start.19 = (bf16[12,1280]{1,0:T(8,128)(2,1)S(1)}, bf16[12,1280]{1,0:T(8,128)(2,1)S(1)}, u32[]{:S(2)}, u32[]{:S(2)}) collective-permute-start(bf16[12,1280]{1,0:T(8,128)(2,1)S(1)} %get-tuple-element.56), channel_id=1, source_target_pairs={{0,3},{1,2},{2,1},{3,0},{4,7},{5,6},{6,5},{7,4},{8,11},{9,10},{10,... | collective-permute-start | bytes 92168 | tf_op jit(solution)/shard_map/ppermute | solution.py:191
  52.8 5.7 %collective-permute-start.20 = (bf16[12,1280]{1,0:T(8,128)(2,1)S(1)}, bf16[12,1280]{1,0:T(8,128)(2,1)S(1)}, u32[]{:S(2)}, u32[]{:S(2)}) collective-permute-start(bf16[12,1280]{1,0:T(8,128)(2,1)S(1)} %get-tuple-element.57), channel_id=1, source_target_pairs={{0,2},{1,3},{2,0},{3,1},{4,6},{5,7},{6,4},{7,5},{8,10},{9,11},{10,... | collective-permute-start | bytes 92168 | tf_op jit(solution)/shard_map/ppermute | solution.py:191
  52.8 5.7 %collective-permute-start.21 = (bf16[12,1280]{1,0:T(8,128)(2,1)S(1)}, bf16[12,1280]{1,0:T(8,128)(2,1)S(1)}, u32[]{:S(2)}, u32[]{:S(2)}) collective-permute-start(bf16[12,1280]{1,0:T(8,128)(2,1)S(1)} %get-tuple-element.58), channel_id=1, source_target_pairs={{0,1},{1,0},{2,3},{3,2},{4,5},{5,4},{6,7},{7,6},{8,9},{9,8},{10,11... | collective-permute-start | bytes 92168 | tf_op jit(solution)/shard_map/ppermute | solution.py:191

commit v8 on v7

--- a/solution.py
+++ b/solution.py
@@ -173,7 +173,7 @@
 
 
 def after(value, earlier):
-    (value,) = call(copy_kernel, [(value.shape, value.dtype)], (value, earlier), free=(1,))
+    (value,) = call(copy_kernel, [(value.shape, value.dtype)], (value, earlier), free=(1,), micros=0)
     return value
 
 
@@ -293,7 +293,15 @@
             target[first + i, j : j + 1, h * width : (h + 1) * width] = mixed[h : h + 1]
 
 
-def attend_near_kernel(per_device, heads, lengths, source, keys, values, out):
+def attend_near_kernel(per_device, heads, lengths, source, keys, values, assign, out, order):
+    shape = order.shape
+    slots = jnp.broadcast_to(group_slots(shape[0], assign), shape)
+    line = lax.broadcasted_iota(jnp.int32, shape, 0)
+    match = jnp.where(line == slots, 1.0, 0.0).astype(jnp.bfloat16)
+    same = jnp.where(line == lax.broadcasted_iota(jnp.int32, shape, 1), 1.0, 0.0).astype(jnp.bfloat16)
+    order[...] = lax.dot_general(
+        match, same, (((0,), (0,)), ((), ())), preferred_element_type=jnp.float32
+    ).astype(jnp.bfloat16)
     out[...] = jnp.zeros_like(out)
     attend_blocks(per_device, heads, lengths, lax.axis_index("sec") >> 1, source, keys, values, out, 0)
 
@@ -350,14 +358,13 @@
     return (sec ^ (sec >> 1)) & 1
 
 
-def products(features, gate, up, part, chunk, keep, send):
+def products(features, gate, up, unit, units, chunk, keep, send):
     half = keep.shape[0]
-    width = gate.shape[1] // 2
     for kind, weight in enumerate((gate, up)):
-        for start in range(0, width, chunk):
-            column = pl.ds(pl.multiple_of(part * width + start, chunk), chunk)
+        for start in range(0, units, chunk):
+            column = pl.ds(pl.multiple_of(unit + start, chunk), chunk)
             product = jnp.dot(features, weight[:, column], preferred_element_type=jnp.float32)
-            at = kind * width + start
+            at = kind * units + start
             keep[:, at : at + chunk] = product[:half]
             send[:, at : at + chunk] = product[half:].astype(jnp.bfloat16)
 
@@ -385,14 +392,18 @@
     squares = jnp.sum(total * total, axis=1, keepdims=True)
     scaled = (total * gain[...].astype(jnp.float32)).astype(jnp.bfloat16)
     features[...] = scaled
-    products(scaled, gate, up, 1 - (sec >> 1), chunk, keep, send)
-    width = gate.shape[1]
-    keep[:, width:] = jnp.broadcast_to(squares[:half], (half, 128))
-    send[:, width:] = two_terms(squares[half:])
-
-
-def gate_up_second_kernel(chunk, features, gate, up, keep, send):
-    products(features[...], gate, up, lax.axis_index("sec") >> 1, chunk, keep, send)
+    units = (keep.shape[1] - 128) // 2
+    products(scaled, gate, up, (1 - (sec >> 1)) * (gate.shape[1] // 2), units, chunk, keep, send)
+    keep[:, 2 * units :] = jnp.broadcast_to(squares[:half], (half, 128))
+    send[:, 2 * units :] = two_terms(squares[half:])
+
+
+def gate_up_more_kernel(chunk, part, features, gate, up, earlier, keep, send):
+    units = keep.shape[1] // 2
+    width = gate.shape[1] // 2
+    away = 1 - (lax.axis_index("sec") >> 1)
+    first = away * width + width - units if part else (1 - away) * width
+    products(features[...], gate, up, first, units, chunk, keep, send)
 
 
 def two_terms(column):
@@ -416,37 +427,46 @@
     send[:, width:] = two_terms(both[:, 0:1])
 
 
-def hidden_kernel(features, mine, beside, across, squares, hidden):
+def add_send_kernel(mine, other, earlier, send):
+    send[...] = (mine[...] + other[...].astype(jnp.float32)).astype(jnp.bfloat16)
+
+
+def scale_kernel(features, squares, first, second, scale):
+    width = first.shape[1] - 128
+    total = squares[:, 0:1] + one_column(first[:, width:])
+    scale[...] = jnp.broadcast_to(lax.rsqrt(total / features + 1e-06), scale.shape)
+
+
+def hidden_kernel(mine, beside, first, second, scale, hidden):
     width = mine.shape[1] // 2
-    total = squares[:, 0:1] + one_column(across[:, 2 * width :])
-    inverse = lax.rsqrt(total / features + 1e-06)
-
-    def summed(columns):
-        here = mine[:, columns] + beside[:, columns].astype(jnp.float32)
-        return (here + across[:, columns].astype(jnp.float32)) * inverse
-
-    gate, up = summed(slice(0, width)), summed(slice(width, 2 * width))
-    hidden[...] = (gate / (1.0 + jnp.exp(-gate)) * up).astype(jnp.bfloat16)
-
-
-def down_lines(mine, other):
+    units = width // 2
+    factor = scale[:, 0:1]
+    for index, across in enumerate((first, second)):
+
+        def summed(kind):
+            here = slice(kind * width + index * units, kind * width + (index + 1) * units)
+            there = across[:, kind * units : (kind + 1) * units].astype(jnp.float32)
+            return (mine[:, here] + beside[:, here].astype(jnp.float32) + there) * factor
+
+        gate, up = summed(0), summed(1)
+        hidden[:, index * units : (index + 1) * units] = (gate / (1.0 + jnp.exp(-gate)) * up).astype(jnp.bfloat16)
+
+
+def down_product(away, mine, other, weight):
+    here = (lax.axis_index("sec") >> 1) ^ away
     lines = jnp.concatenate([mine[...].astype(jnp.float32), other[...].astype(jnp.float32)], axis=0)
-    return lines.astype(jnp.bfloat16)
+    depth = lines.shape[1]
+    rows = weight[pl.ds(pl.multiple_of(here * depth, depth), depth), :]
+    return jnp.dot(lines.astype(jnp.bfloat16), rows, preferred_element_type=jnp.float32)
 
 
 def down_first_kernel(mine, other, weight, out):
-    here = lax.axis_index("sec") >> 1
-    depth = mine.shape[1]
-    rows = weight[pl.ds(pl.multiple_of(here * depth, depth), depth), :]
-    out[...] = jnp.dot(down_lines(mine, other), rows, preferred_element_type=jnp.float32)
+    out[...] = down_product(0, mine, other, weight)
 
 
 def down_second_kernel(mine, other, before, weight, keep, first, second, third, groups):
     tp = lax.axis_index("tp")
-    away = 1 - (lax.axis_index("sec") >> 1)
-    depth = mine.shape[1]
-    rows = weight[pl.ds(pl.multiple_of(away * depth, depth), depth), :]
-    product = before[...] + jnp.dot(down_lines(mine, other), rows, preferred_element_type=jnp.float32)
+    product = before[...] + down_product(1, mine, other, weight)
     group = keep.shape[0]
     half = product.shape[0] // 2
     swapped = row_half() == 1
@@ -457,19 +477,13 @@
         target[...] = groups[tp ^ (step + 1), 0:group].astype(jnp.bfloat16)
 
 
-def finish_kernel(third, second, first, stream, mine, assign, out):
+def finish_kernel(third, second, first, stream, mine, order, out):
     total = stream[...] + mine[...]
     for other in (first, second, third):
         total = total + other[...].astype(jnp.float32)
-    group = out.shape[0]
-    slots = jnp.broadcast_to(group_slots(group, assign), (group, group))
-    match = jnp.where(lax.broadcasted_iota(jnp.int32, (group, group), 0) == slots, 1.0, 0.0).astype(jnp.bfloat16)
     coarse = total.astype(jnp.bfloat16)
     fine = (total - coarse.astype(jnp.float32)).astype(jnp.bfloat16)
-    ordered = [
-        lax.dot_general(match, term, (((0,), (0,)), ((), ())), preferred_element_type=jnp.float32)
-        for term in (coarse, fine)
-    ]
+    ordered = [jnp.dot(order[...], term, preferred_element_type=jnp.float32) for term in (coarse, fine)]
     out[...] = (ordered[0] + ordered[1]).astype(jnp.bfloat16)
 
 
@@ -520,10 +534,10 @@
     )
     other = swap(away, "sec", 3)
     caches = (key_cache, cached_value_rows)
-    (near,) = call(
+    near, order = call(
         functools.partial(attend_near_kernel, per_device, heads),
-        [((2, 4, head_block), f32)],
-        (cache_len, mine, *caches),
+        [((2, 4, head_block), f32), ((group, group), bf16)],
+        (cache_len, mine, *caches, assign),
         smem=(0,),
         resident=(2, 3),
     )
@@ -545,7 +559,7 @@
 
     def project(far, *lines):
         return call(
-            functools.partial(project_kernel, far, per_device), pair, (*lines, assign, resid, out_weight), resident=(4,)
+            functools.partial(project_kernel, far, per_device), pair, (*lines, assign, resid, out_weight), resident=(4,), micros=0 if far else 2
         )
 
     def tp_sum(mine, away):
@@ -557,39 +571,61 @@
     far = project(1, across, corner)
     sums = tp_sum(*near) + tp_sum(*far)
 
-    chunk = min(512, width // 2)
+    units = width // 4
+    chunk = min(512, units)
+    weights = (gate_weight, up_weight)
     mine, away, lines, stream = call(
         functools.partial(gate_up_first_kernel, chunk),
         [
-            ((half, width + 128), f32),
-            ((half, width + 128), bf16),
+            ((half, 2 * units + 128), f32),
+            ((half, 2 * units + 128), bf16),
             ((2 * half, features), bf16),
             ((group, features), f32),
         ],
-        (*sums, gain, gate_weight, up_weight),
+        (*sums, gain, *weights),
         [pltpu.VMEM((2, half, features), f32), pltpu.VMEM((4, 16, features), f32)],
         resident=(5, 6),
-    )
+        micros=2,
+    )
+    beside = swap(away, "sec", 1)
+    mine_b, away_b = call(
+        functools.partial(gate_up_more_kernel, chunk, 1),
+        [((half, 2 * units), f32), ((half, 2 * units), bf16)],
+        (lines, *weights, away),
+        resident=(1, 2),
+        free=(3,),
+        micros=0,
+    )
+    beside_b = swap(away_b, "sec", 1)
     away, squares = call(
-        pair_sum_kernel, [((half, width + 128), bf16), ((half, 128), f32)], (mine, swap(away, "sec", 1))
-    )
-    across = swap(away, "sec", 3)
+        pair_sum_kernel, [((half, 2 * units + 128), bf16), ((half, 128), f32)], (mine, beside), micros=0
+    )
+    across = [swap(away, "sec", 3)]
+    (away,) = call(add_send_kernel, [((half, 2 * units), bf16)], (mine_b, beside_b, away), free=(2,), micros=0)
+    across += [swap(away, "sec", 3)]
     mine, away = call(
-        functools.partial(gate_up_second_kernel, chunk),
-        [((half, width), f32), ((half, width), bf16)],
-        (lines, gate_weight, up_weight),
+        functools.partial(gate_up_more_kernel, chunk, 0),
+        [((half, 4 * units), f32), ((half, 4 * units), bf16)],
+        (lines, *weights, away),
         resident=(1, 2),
+        free=(3,),
+        micros=0,
     )
     beside = swap(away, "sec", 1)
-    (hidden,) = call(
-        functools.partial(hidden_kernel, features * lax.axis_size("sec")),
-        [((half, width // 2), bf16)],
-        (mine, beside, across, squares),
-    )
+    (scale,) = call(
+        functools.partial(scale_kernel, features * lax.axis_size("sec")),
+        [((half, 128), f32)],
+        (squares, *across),
+        free=(2,),
+        micros=4,
+    )
+    (hidden,) = call(hidden_kernel, [((half, 2 * units), bf16)], (mine, beside, *across, scale), micros=0)
     across = swap(hidden, "sec", 3)
     beside = swap(hidden, "sec", 1)
     corner = swap(across, "sec", 1)
-    (before,) = call(down_first_kernel, [((2 * half, features), f32)], (hidden, beside, down_weight), resident=(2,))
+    (before,) = call(
+        down_first_kernel, [((2 * half, features), f32)], (hidden, beside, down_weight), resident=(2,), micros=2
+    )
     mine, *parts = call(
         down_second_kernel,
         [((group, features), f32)] + [((group, features), bf16)] * 3,
@@ -598,7 +634,7 @@
         resident=(3,),
     )
     parts = [swap(parts[step - 1], "tp", step) for step in (3, 2, 1)]
-    (out,) = call(finish_kernel, [((group, features), bf16)], (*parts, stream, mine, assign))
+    (out,) = call(finish_kernel, [((group, features), bf16)], (*parts, stream, mine, order))
     return out
 
 

time: 59.7 us -> 58.2 us (0.975)
  waiting for transfers between devices: 23.5 us -> 20.1 us
  starting transfers between devices: 22.5 us -> 24.1 us
    ppermute x22 -> x24, waiting for transfers between devices: 23.5 us -> 20.1 us  [swap(): return lax.ppermute(value, axis, [(i, i ^ step) for i in range(total)])]
    ppermute x22 -> x24, starting transfers between devices: 22.5 us -> 24.1 us  [swap(): return lax.ppermute(value, axis, [(i, i ^ step) for i in range(total)])]
    pallas_call x17 -> x20, Pallas kernels: 13.3 us -> 13.5 us  [call(): pl.pallas_call(kernel, out_shape=[jax.ShapeDtypeStruct(shape, dtype) for...]
  transfers between devices with their start and end apart: 22 -> 24, of which waited for: 16 -> 14; matrix products, arithmetic and copies ran while one was open for 0% -> 0% of each run, Pallas kernels for 12% -> 16%
where the time goes in v8:
time: 58.2 us; the launch traced here: 58.1 us
  starting transfers between devices  24.1 us (41%)
  waiting for transfers between devices  20.1 us (35%)
  Pallas kernels  13.5 us (23%)
    ppermute x24, starting transfers between devices, swap(): return lax.ppermute(value, axis, [(i, i ^ step) for i in range(total)])  24.1 us
    ppermute x24, waiting for transfers between devices, swap(): return lax.ppermute(value, axis, [(i, i ^ step) for i in range(total)])  20.1 us
    pallas_call x20, Pallas kernels, call(): pl.pallas_call(kernel, out_shape=[jax.ShapeDtypeStruct(shape, dtype) for...  13.5 us
  transfers between devices with their start and end apart: 24, of which 14 were waited for; matrix products, arithmetic and copies ran while one was open for 0% of the time, Pallas kernels for 16%

profile of v8, /device:TPU:0, one launch (start us, length us, event | category | flops | bytes accessed | tf_op | source)
XLA Modules:
  0.0 58.1 jit_solution(8160343881523152754)
XLA Ops:
  0.0 0.5 collective-permute-start
  0.5 0.1 collective-permute-start.1
  0.6 1.5 %shard_map.118 = (bf16[2,48,128]{2,1,0:T(8,128)(2,1)S(1)}, bf16[16,12]{1,0:T(8,128)(2,1)S(1)}) custom-call(bf16[12,1280]{1,0:T(8,128)(2,1)} %query.1, bf16[12,512]{1,0:T(8,128)(2,1)} %pairs.1, s32[1,48]{1,0:T(1,128)} %bitcast.7), custom_call_target="tpu_custom_call" | custom-call | flops 2000000000 | tf_op jit(solution)/shard_map/pallas_call | solution.py:160
  2.1 0.0 collective-permute-done.1.pairs
  2.1 0.0 collective-permute-done.query
  2.1 0.1 shard_map.119
  2.3 2.5 %collective-permute-start.2 = (bf16[2,48,128]{2,1,0:T(8,128)(2,1)S(1)}, bf16[2,48,128]{2,1,0:T(8,128)(2,1)S(1)}, u32[]{:S(2)}, u32[]{:S(2)}) collective-permute-start(bf16[2,48,128]{2,1,0:T(8,128)(2,1)S(1)} %get-tuple-element.39), channel_id=1, source_target_pairs={{0,12},{4,8},{8,4},{12,0},{1,13},{5,9},{9,5},{13,1},{2,14},{6,10},... | collective-permute-start | bytes 73736 | tf_op jit(solution)/shard_map/ppermute | solution.py:191
  4.8 0.0 copy-start
  4.8 0.0 copy-start.1
  4.8 1.5 %shard_map.120 = (f32[2,4,1280]{2,1,0:T(4,128)S(1)}, bf16[12,12]{1,0:T(8,128)(2,1)S(1)}) custom-call(s32[3]{0:T(128)S(1)} %copy-done.5, bf16[2,48,128]{2,1,0:T(8,128)(2,1)S(1)} %get-tuple-element.40.source, bf16[3,224,1024]{2,1,0:T(8,128)(2,1)S(1)} %copy-done.3, bf16[3,224,1024]{2,1,0:T(8,128)(2,1)S(1)} %copy-done.4, s32[1,48]{1,0:T(1,128)S(1)} %bitcast.8), custom_call_target="tpu_custom_call" | custom-call | flops 2000000000 | tf_op jit(solution)/shard_map/pallas_call | solution.py:160
  6.3 0.1 collective-permute-done.2.source
  6.4 1.2 %shard_map.121 = (bf16[4,1280]{1,0:T(4,128)(2,1)S(1)}, bf16[4,1280]{1,0:T(4,128)(2,1)S(1)}, bf16[4,1280]{1,0:T(4,128)(2,1)S(1)}, bf16[4,1280]{1,0:T(4,128)(2,1)S(1)}) custom-call(s32[3]{0:T(128)S(1)} %copy-done.5, bf16[2,48,128]{2,1,0:T(8,128)(2,1)S(1)} %collective-permute-done.2.source, f32[2,4,1280]{2,1,0:T(4,128)S(1)} %get-tuple-element.41.near, ...), custom_call_target="tpu_custom_call" | custom-call | flops 2000000000 | tf_op jit(solution)/shard_map/pallas_call | solution.py:160
  7.5 4.3 %collective-permute-start.3 = (bf16[4,1280]{1,0:T(4,128)(2,1)S(1)}, bf16[4,1280]{1,0:T(4,128)(2,1)S(1)}, u32[]{:S(2)}, u32[]{:S(2)}) collective-permute-start(bf16[4,1280]{1,0:T(4,128)(2,1)S(1)} %get-tuple-element.42), channel_id=1, source_target_pairs={{0,7},{1,6},{2,5},{3,4},{4,3},{5,2},{6,1},{7,0},{8,15},{9,14},{10,... | collective-permute-start | bytes 30728 | tf_op jit(solution)/shard_map/ppermute | solution.py:191
  11.8 0.0 collective-permute-start.4
  11.8 0.7 %collective-permute-start.5 = (bf16[4,1280]{1,0:T(4,128)(2,1)S(1)}, bf16[4,1280]{1,0:T(4,128)(2,1)S(1)}, u32[]{:S(2)}, u32[]{:S(2)}) collective-permute-start(bf16[4,1280]{1,0:T(4,128)(2,1)S(1)} %get-tuple-element.44), channel_id=1, source_target_pairs={{0,5},{1,4},{2,7},{3,6},{4,1},{5,0},{6,3},{7,2},{8,13},{9,12},{10,... | collective-permute-start | bytes 30728 | tf_op jit(solution)/shard_map/ppermute | solution.py:191
  12.5 0.7 %collective-permute-done.3.third = bf16[4,1280]{1,0:T(4,128)(2,1)S(1)} collective-permute-done((bf16[4,1280]{1,0:T(4,128)(2,1)S(1)}, bf16[4,1280]{1,0:T(4,128)(2,1)S(1)}, u32[]{:S(2)}, u32[]{:S(2)}) %collective-permute-start.3) | collective-permute-done | bytes 10272 | tf_op jit(solution)/shard_map/ppermute | solution.py:191
  13.2 2.6 %collective-permute-done.4.second = bf16[4,1280]{1,0:T(4,128)(2,1)S(1)} collective-permute-done((bf16[4,1280]{1,0:T(4,128)(2,1)S(1)}, bf16[4,1280]{1,0:T(4,128)(2,1)S(1)}, u32[]{:S(2)}, u32[]{:S(2)}) %collective-permute-start.4) | collective-permute-done | bytes 10272 | tf_op jit(solution)/shard_map/ppermute | solution.py:191
  15.8 0.0 collective-permute-done.5.first
  15.8 0.0 slice-start.4
  15.9 0.5 collective-permute-start.6
  16.3 1.2 %collective-permute-start.9 = (bf16[16,1280]{1,0:T(8,128)(2,1)S(1)}, bf16[16,1280]{1,0:T(8,128)(2,1)S(1)}, u32[]{:S(2)}, u32[]{:S(2)}) collective-permute-start(bf16[16,1280]{1,0:T(8,128)(2,1)S(1)} %shard_map.122.first), channel_id=1, source_target_pairs={{0,12},{4,8},{8,4},{12,0},{1,13},{5,9},{9,5},{13,1},{2,14},{6,10},... | collective-permute-start | bytes 122888 | tf_op jit(solution)/shard_map/ppermute | solution.py:191
  17.5 0.0 collective-permute-done.6.second
  17.6 0.0 slice-start
  17.6 0.9 %shard_map.123 = (f32[24,1280]{1,0:T(8,128)S(1)}, bf16[24,1280]{1,0:T(8,128)(2,1)S(1)}) custom-call(bf16[16,1280]{1,0:T(8,128)(2,1)S(1)} %shard_map.122.first, bf16[16,1280]{1,0:T(8,128)(2,1)S(1)} %collective-permute-done.6.second, s32[1,48]{1,0:T(1,128)S(1)} %bitcast.9, bf16[12,1280]{1,0:T(8,128)(2,1)S(1)} %copy-done.1, bf16[1280,1280]{1,0:T(8,128)(2,1)S(1)} %copy-done), custom_call_target="tpu_custom_call" | custom-call | flops 2000000000 | tf_op jit(solution)/shard_map/pallas_call | solution.py:160
  18.5 0.1 collective-permute-start.7
  18.5 1.4 %collective-permute-done.9.value.first = bf16[16,1280]{1,0:T(8,128)(2,1)S(1)} collective-permute-done((bf16[16,1280]{1,0:T(8,128)(2,1)S(1)}, bf16[16,1280]{1,0:T(8,128)(2,1)S(1)}, u32[]{:S(2)}, u32[]{:S(2)}) %collective-permute-start.9) | collective-permute-done | bytes 40992 | tf_op jit(solution)/shard_map/ppermute | solution.py:191
  20.0 0.1 collective-permute-start.10
  20.1 1.1 %collective-permute-done.10.second = bf16[16,1280]{1,0:T(8,128)(2,1)S(1)} collective-permute-done((bf16[16,1280]{1,0:T(8,128)(2,1)S(1)}, bf16[16,1280]{1,0:T(8,128)(2,1)S(1)}, u32[]{:S(2)}, u32[]{:S(2)}) %collective-permute-start.10) | collective-permute-done | bytes 40992 | tf_op jit(solution)/shard_map/ppermute | solution.py:191
  21.2 0.9 %shard_map.126 = (f32[24,1280]{1,0:T(8,128)S(1)}, bf16[24,1280]{1,0:T(8,128)(2,1)S(1)}) custom-call(bf16[16,1280]{1,0:T(8,128)(2,1)S(1)} %collective-permute-done.9.value.first, bf16[16,1280]{1,0:T(8,128)(2,1)S(1)} %collective-permute-done.10.second, s32[1,48]{1,0:T(1,128)S(1)} %bitcast.10, bf16[12,1280]{1,0:T(8,128)(2,1)S(1)} %copy-done.1, ...), custom_call_target="tpu_custom_call" | custom-call | tf_op jit(solution)/shard_map/pallas_call | solution.py:160
  22.1 0.7 %collective-permute-start.11 = (bf16[24,1280]{1,0:T(8,128)(2,1)S(1)}, bf16[24,1280]{1,0:T(8,128)(2,1)S(1)}, u32[]{:S(2)}, u32[]{:S(2)}) collective-permute-start(bf16[24,1280]{1,0:T(8,128)(2,1)S(1)} %get-tuple-element.51), channel_id=1, source_target_pairs={{0,1},{1,0},{2,3},{3,2},{4,5},{5,4},{6,7},{7,6},{8,9},{9,8},{10,11... | collective-permute-start | bytes 184328 | tf_op jit(solution)/shard_map/ppermute | solution.py:191
  22.8 0.1 collective-permute-done.7.other
  22.9 2.0 %collective-permute-start.8 = (bf16[24,1280]{1,0:T(8,128)(2,1)S(1)}, bf16[24,1280]{1,0:T(8,128)(2,1)S(1)}, u32[]{:S(2)}, u32[]{:S(2)}) collective-permute-start(bf16[24,1280]{1,0:T(8,128)(2,1)S(1)} %get-tuple-element.49), channel_id=1, source_target_pairs={{0,2},{1,3},{2,0},{3,1},{4,6},{5,7},{6,4},{7,5},{8,10},{9,11},{10,... | collective-permute-start | bytes 184328 | tf_op jit(solution)/shard_map/ppermute | solution.py:191
  24.9 1.4 %collective-permute-done.11.other = bf16[24,1280]{1,0:T(8,128)(2,1)S(1)} collective-permute-done((bf16[24,1280]{1,0:T(8,128)(2,1)S(1)}, bf16[24,1280]{1,0:T(8,128)(2,1)S(1)}, u32[]{:S(2)}, u32[]{:S(2)}) %collective-permute-start.11) | collective-permute-done | bytes 61472 | tf_op jit(solution)/shard_map/ppermute | solution.py:191
  26.4 2.1 %collective-permute-start.12 = (bf16[24,1280]{1,0:T(8,128)(2,1)S(1)}, bf16[24,1280]{1,0:T(8,128)(2,1)S(1)}, u32[]{:S(2)}, u32[]{:S(2)}) collective-permute-start(bf16[24,1280]{1,0:T(8,128)(2,1)S(1)} %get-tuple-element.53), channel_id=1, source_target_pairs={{0,2},{1,3},{2,0},{3,1},{4,6},{5,7},{6,4},{7,5},{8,10},{9,11},{10,... | collective-permute-start | bytes 184328 | tf_op jit(solution)/shard_map/ppermute | solution.py:191
  28.5 1.6 %collective-permute-done.8.near_other = bf16[24,1280]{1,0:T(8,128)(2,1)S(1)} collective-permute-done((bf16[24,1280]{1,0:T(8,128)(2,1)S(1)}, bf16[24,1280]{1,0:T(8,128)(2,1)S(1)}, u32[]{:S(2)}, u32[]{:S(2)}) %collective-permute-start.8) | collective-permute-done | bytes 61472 | tf_op jit(solution)/shard_map/ppermute | solution.py:191
  30.1 2.1 %collective-permute-done.12.far_other = bf16[24,1280]{1,0:T(8,128)(2,1)S(1)} collective-permute-done((bf16[24,1280]{1,0:T(8,128)(2,1)S(1)}, bf16[24,1280]{1,0:T(8,128)(2,1)S(1)}, u32[]{:S(2)}, u32[]{:S(2)}) %collective-permute-start.12) | collective-permute-done | bytes 61472 | tf_op jit(solution)/shard_map/ppermute | solution.py:191
  32.3 1.1 %shard_map.128 = (f32[24,2176]{1,0:T(8,128)S(1)}, bf16[24,2176]{1,0:T(8,128)(2,1)S(1)}, bf16[48,1280]{1,0:T(8,128)(2,1)S(1)}, f32[12,1280]{1,0:T(8,128)S(1)}) custom-call(f32[24,1280]{1,0:T(8,128)S(1)} %get-tuple-element.48.near, bf16[24,1280]{1,0:T(8,128)(2,1)S(1)} %collective-permute-done.8.near_other, f32[24,1280]{1,0:T(8,128)S(1)} %get-tuple-element.52.far, ...), custom_call_target="tpu_custom_call" | custom-call | flops 2000000000 | tf_op jit(solution)/shard_map/pallas_call | solution.py:160
  33.4 0.1 collective-permute-start.14
  33.4 1.0 %shard_map.129 = (f32[24,2048]{1,0:T(8,128)S(1)}, bf16[24,2048]{1,0:T(8,128)(2,1)S(1)}) custom-call(bf16[48,1280]{1,0:T(8,128)(2,1)S(1)} %get-tuple-element.54.features, bf16[1280,4096]{1,0:T(8,128)(2,1)S(1)} %bitcast.2, bf16[1280,4096]{1,0:T(8,128)(2,1)S(1)} %bitcast.4, bf16[24,2176]{1,0:T(8,128)(2,1)S(1)} %get-tuple-element.55.earlier), custom_call_target="tpu_custom_call" | custom-call | tf_op jit(solution)/shard_map/pallas_call | solution.py:160
  34.5 0.5 collective-permute-start.13
  35.0 0.0 collective-permute-done.14.other
  35.0 0.2 shard_map.130
  35.2 1.1 %collective-permute-start.16 = (bf16[24,2176]{1,0:T(8,128)(2,1)S(1)}, bf16[24,2176]{1,0:T(8,128)(2,1)S(1)}, u32[]{:S(2)}, u32[]{:S(2)}) collective-permute-start(bf16[24,2176]{1,0:T(8,128)(2,1)S(1)} %get-tuple-element.59.earlier), channel_id=1, source_target_pairs={{0,12},{4,8},{8,4},{12,0},{1,13},{5,9},{9,5},{13,1},{2,14},{6,10},... | collective-permute-start | bytes 313352 | tf_op jit(solution)/shard_map/ppermute | solution.py:191
  36.3 0.0 collective-permute-done.13.other
  36.4 1.1 %collective-permute-start.17 = (bf16[24,2048]{1,0:T(8,128)(2,1)S(1)}, bf16[24,2048]{1,0:T(8,128)(2,1)S(1)}, u32[]{:S(2)}, u32[]{:S(2)}) collective-permute-start(bf16[24,2048]{1,0:T(8,128)(2,1)S(1)} %shard_map.131.earlier), channel_id=1, source_target_pairs={{0,12},{4,8},{8,4},{12,0},{1,13},{5,9},{9,5},{13,1},{2,14},{6,10},... | collective-permute-start | bytes 294920 | tf_op jit(solution)/shard_map/ppermute | solution.py:191
  37.5 1.9 %shard_map.132 = (f32[24,4096]{1,0:T(8,128)S(1)}, bf16[24,4096]{1,0:T(8,128)(2,1)S(1)}) custom-call(bf16[48,1280]{1,0:T(8,128)(2,1)S(1)} %get-tuple-element.54.features, bf16[1280,4096]{1,0:T(8,128)(2,1)S(1)} %bitcast.2, bf16[1280,4096]{1,0:T(8,128)(2,1)S(1)} %bitcast.4, bf16[24,2048]{1,0:T(8,128)(2,1)S(1)} %shard_map.131.earlier), custom_call_target="tpu_custom_call" | custom-call | tf_op jit(solution)/shard_map/pallas_call | solution.py:160
  39.4 0.2 collective-permute-start.15
  39.6 2.7 %collective-permute-done.17.second = bf16[24,2048]{1,0:T(8,128)(2,1)S(1)} collective-permute-done((bf16[24,2048]{1,0:T(8,128)(2,1)S(1)}, bf16[24,2048]{1,0:T(8,128)(2,1)S(1)}, u32[]{:S(2)}, u32[]{:S(2)}) %collective-permute-start.17) | collective-permute-done | bytes 98336 | tf_op jit(solution)/shard_map/ppermute | solution.py:191
  42.3 0.1 shard_map.133.scale
  42.5 0.2 shard_map.134.mine
  42.7 1.3 %collective-permute-start.18 = (bf16[24,2048]{1,0:T(8,128)(2,1)S(1)}, bf16[24,2048]{1,0:T(8,128)(2,1)S(1)}, u32[]{:S(2)}, u32[]{:S(2)}) collective-permute-start(bf16[24,2048]{1,0:T(8,128)(2,1)S(1)} %shard_map.134.mine), channel_id=1, source_target_pairs={{0,12},{4,8},{8,4},{12,0},{1,13},{5,9},{9,5},{13,1},{2,14},{6,10},... | collective-permute-start | bytes 294920 | tf_op jit(solution)/shard_map/ppermute | solution.py:191
  43.9 0.4 collective-permute-start.20
  44.3 3.2 %collective-permute-done.18.mine = bf16[24,2048]{1,0:T(8,128)(2,1)S(1)} collective-permute-done((bf16[24,2048]{1,0:T(8,128)(2,1)S(1)}, bf16[24,2048]{1,0:T(8,128)(2,1)S(1)}, u32[]{:S(2)}, u32[]{:S(2)}) %collective-permute-start.18) | collective-permute-done | bytes 98336 | tf_op jit(solution)/shard_map/ppermute | solution.py:191
  47.5 0.1 collective-permute-start.19
  47.6 0.0 collective-permute-done.20.other
  47.7 1.0 %shard_map.135.before = f32[48,1280]{1,0:T(8,128)S(1)} custom-call(bf16[24,2048]{1,0:T(8,128)(2,1)S(1)} %shard_map.134.mine, bf16[24,2048]{1,0:T(8,128)(2,1)S(1)} %collective-permute-done.20.other, bf16[4096,1280]{1,0:T(8,128)(2,1)S(1)} %bitcast.6), custom_call_target="tpu_custom_call" | custom-call | flops 2000000000 | tf_op jit(solution)/shard_map/pallas_call | solution.py:160
  48.7 0.1 collective-permute-done.19.other
  48.8 1.1 %shard_map.136 = (f32[12,1280]{1,0:T(8,128)S(1)}, bf16[12,1280]{1,0:T(8,128)(2,1)S(1)}, bf16[12,1280]{1,0:T(8,128)(2,1)S(1)}, bf16[12,1280]{1,0:T(8,128)(2,1)S(1)}) custom-call(bf16[24,2048]{1,0:T(8,128)(2,1)S(1)} %collective-permute-done.18.mine, bf16[24,2048]{1,0:T(8,128)(2,1)S(1)} %collective-permute-done.19.other, f32[48,1280]{1,0:T(8,128)S(1)} %shard_map.135.before, ...), custom_call_target="tpu_custom_call" | custom-call | flops 2000000000 | tf_op jit(solution)/shard_map/pallas_call | solution.py:160
  49.9 1.6 %collective-permute-start.21 = (bf16[12,1280]{1,0:T(8,128)(2,1)S(1)}, bf16[12,1280]{1,0:T(8,128)(2,1)S(1)}, u32[]{:S(2)}, u32[]{:S(2)}) collective-permute-start(bf16[12,1280]{1,0:T(8,128)(2,1)S(1)} %get-tuple-element.63), channel_id=1, source_target_pairs={{0,3},{1,2},{2,1},{3,0},{4,7},{5,6},{6,5},{7,4},{8,11},{9,10},{10,... | collective-permute-start | bytes 92168 | tf_op jit(solution)/shard_map/ppermute | solution.py:191
  51.5 0.1 collective-permute-start.22
  51.5 2.8 %collective-permute-start.23 = (bf16[12,1280]{1,0:T(8,128)(2,1)S(1)}, bf16[12,1280]{1,0:T(8,128)(2,1)S(1)}, u32[]{:S(2)}, u32[]{:S(2)}) collective-permute-start(bf16[12,1280]{1,0:T(8,128)(2,1)S(1)} %get-tuple-element.65), channel_id=1, source_target_pairs={{0,1},{1,0},{2,3},{3,2},{4,5},{5,4},{6,7},{7,6},{8,9},{9,8},{10,11... | collective-permute-start | bytes 92168 | tf_op jit(solution)/shard_map/ppermute | solution.py:191
  54.3 1.7 %collective-permute-done.21.third = bf16[12,1280]{1,0:T(8,128)(2,1)S(1)} collective-permute-done((bf16[12,1280]{1,0:T(8,128)(2,1)S(1)}, bf16[12,1280]{1,0:T(8,128)(2,1)S(1)}, u32[]{:S(2)}, u32[]{:S(2)}) %collective-permute-start.21) | collective-permute-done | bytes 30752 | tf_op jit(solution)/shard_map/ppermute | solution.py:191
  56.1 1.2 %collective-permute-done.22.second = bf16[12,1280]{1,0:T(8,128)(2,1)S(1)} collective-permute-done((bf16[12,1280]{1,0:T(8,128)(2,1)S(1)}, bf16[12,1280]{1,0:T(8,128)(2,1)S(1)}, u32[]{:S(2)}, u32[]{:S(2)}) %collective-permute-start.22) | collective-permute-done | bytes 30752 | tf_op jit(solution)/shard_map/ppermute | solution.py:191
  57.3 0.8 %shard_map.137 = bf16[12,1280]{1,0:T(8,128)(2,1)} custom-call(bf16[12,1280]{1,0:T(8,128)(2,1)S(1)} %collective-permute-done.21.third, bf16[12,1280]{1,0:T(8,128)(2,1)S(1)} %collective-permute-done.22.second, bf16[12,1280]{1,0:T(8,128)(2,1)S(1)} %collective-permute-done.23.first, f32[12,1280]{1,0:T(8,128)S(1)} %get-tuple-element.66.stream, ...), custom_call_target="tpu_custom_call" | custom-call | flops 2000000000 | tf_op jit(solution)/shard_map/pallas_call | solution.py:160
  (40 shorter events, 0.1 us)
Async XLA Ops:
  0.0 4.8 %copy-start.2 = (s32[48]{0:T(128)S(1)}, s32[48]{0:T(128)}, u32[]{:S(2)}) copy-start(s32[48]{0:T(128)} %param.18) | copy-start | bytes 580
  0.0 4.8 %copy-start.5 = (s32[3]{0:T(128)S(1)}, s32[3]{0:T(128)}, u32[]{:S(2)}) copy-start(s32[3]{0:T(128)} %lengths.3) | copy-start | bytes 40
  0.0 4.8 %copy-start.3 = (bf16[3,224,1024]{2,1,0:T(8,128)(2,1)S(1)}, bf16[3,224,1024]{2,1,0:T(8,128)(2,1)}, u32[]{:S(2)}) copy-start(bf16[3,224,1024]{2,1,0:T(8,128)(2,1)} %keys.3) | copy-start | bytes 4128772
  0.0 4.8 %copy-start.4 = (bf16[3,224,1024]{2,1,0:T(8,128)(2,1)S(1)}, bf16[3,224,1024]{2,1,0:T(8,128)(2,1)}, u32[]{:S(2)}) copy-start(bf16[3,224,1024]{2,1,0:T(8,128)(2,1)} %values.3) | copy-start | bytes 4128772
  0.0 2.1 %collective-permute-start = (bf16[12,1280]{1,0:T(8,128)(2,1)}, bf16[12,1280]{1,0:T(8,128)(2,1)S(1)}, u32[]{:S(2)}, u32[]{:S(2)}) collective-permute-start(bf16[12,1280]{1,0:T(8,128)(2,1)} %query.1), channel_id=1, source_target_pairs={{0,4},{4,0},{8,12},{12,8},{1,5},{5,1},{9,13},{13,9},{2,6},{6,2},{1... | collective-permute-start | bytes 92168 | tf_op jit(solution)/shard_map/ppermute | solution.py:191
  0.5 1.6 %collective-permute-start.1 = (bf16[12,512]{1,0:T(8,128)(2,1)}, bf16[12,512]{1,0:T(8,128)(2,1)S(1)}, u32[]{:S(2)}, u32[]{:S(2)}) collective-permute-start(bf16[12,512]{1,0:T(8,128)(2,1)} %pairs.1), channel_id=1, source_target_pairs={{0,4},{4,0},{8,12},{12,8},{1,5},{5,1},{9,13},{13,9},{2,6},{6,2},{1... | collective-permute-start | bytes 36872 | tf_op jit(solution)/shard_map/ppermute | solution.py:191
  2.3 4.1 %collective-permute-start.2 = (bf16[2,48,128]{2,1,0:T(8,128)(2,1)S(1)}, bf16[2,48,128]{2,1,0:T(8,128)(2,1)S(1)}, u32[]{:S(2)}, u32[]{:S(2)}) collective-permute-start(bf16[2,48,128]{2,1,0:T(8,128)(2,1)S(1)} %get-tuple-element.39), channel_id=1, source_target_pairs={{0,12},{4,8},{8,4},{12,0},{1,13},{5,9},{9,5},{13,1},{2,14},{6,10},... | collective-permute-start | bytes 73736 | tf_op jit(solution)/shard_map/ppermute | solution.py:191
  4.8 12.8 %copy-start = (bf16[1280,1280]{1,0:T(8,128)(2,1)S(1)}, bf16[1280,1280]{1,0:T(8,128)(2,1)}, u32[]{:S(2)}) copy-start(bf16[1280,1280]{1,0:T(8,128)(2,1)} %weight.5) | copy-start | bytes 9830404
  4.8 12.8 %copy-start.1 = (bf16[12,1280]{1,0:T(8,128)(2,1)S(1)}, bf16[12,1280]{1,0:T(8,128)(2,1)}, u32[]{:S(2)}) copy-start(bf16[12,1280]{1,0:T(8,128)(2,1)} %resid.3) | copy-start | bytes 92164
  7.5 5.7 %collective-permute-start.3 = (bf16[4,1280]{1,0:T(4,128)(2,1)S(1)}, bf16[4,1280]{1,0:T(4,128)(2,1)S(1)}, u32[]{:S(2)}, u32[]{:S(2)}) collective-permute-start(bf16[4,1280]{1,0:T(4,128)(2,1)S(1)} %get-tuple-element.42), channel_id=1, source_target_pairs={{0,7},{1,6},{2,5},{3,4},{4,3},{5,2},{6,1},{7,0},{8,15},{9,14},{10,... | collective-permute-start | bytes 30728 | tf_op jit(solution)/shard_map/ppermute | solution.py:191
  11.8 4.0 %collective-permute-start.4 = (bf16[4,1280]{1,0:T(4,128)(2,1)S(1)}, bf16[4,1280]{1,0:T(4,128)(2,1)S(1)}, u32[]{:S(2)}, u32[]{:S(2)}) collective-permute-start(bf16[4,1280]{1,0:T(4,128)(2,1)S(1)} %get-tuple-element.43), channel_id=1, source_target_pairs={{0,6},{1,7},{2,4},{3,5},{4,2},{5,3},{6,0},{7,1},{8,14},{9,15},{10,... | collective-permute-start | bytes 30728 | tf_op jit(solution)/shard_map/ppermute | solution.py:191
  11.8 4.0 %collective-permute-start.5 = (bf16[4,1280]{1,0:T(4,128)(2,1)S(1)}, bf16[4,1280]{1,0:T(4,128)(2,1)S(1)}, u32[]{:S(2)}, u32[]{:S(2)}) collective-permute-start(bf16[4,1280]{1,0:T(4,128)(2,1)S(1)} %get-tuple-element.44), channel_id=1, source_target_pairs={{0,5},{1,4},{2,7},{3,6},{4,1},{5,0},{6,3},{7,2},{8,13},{9,12},{10,... | collective-permute-start | bytes 30728 | tf_op jit(solution)/shard_map/ppermute | solution.py:191
  15.8 16.4 %slice-start.3 = ((s8[10485760]{0:T(1024)(128)(4,1)}), s8[4194304]{0:T(1024)(128)(4,1)S(1)}, s32[]{:S(2)}) async-start(s8[10485760]{0:T(1024)(128)(4,1)} %bitcast.3), calls=%async_computation.3 | async-start | bytes 8388608
  15.8 16.4 %slice-start.4 = ((s8[10485760]{0:T(1024)(128)(4,1)}), s8[4194304]{0:T(1024)(128)(4,1)S(1)}, s32[]{:S(2)}) async-start(s8[10485760]{0:T(1024)(128)(4,1)} %bitcast.3), calls=%async_computation.4 | async-start | bytes 8388608
  15.9 1.7 %collective-permute-start.6 = (bf16[16,1280]{1,0:T(8,128)(2,1)S(1)}, bf16[16,1280]{1,0:T(8,128)(2,1)S(1)}, u32[]{:S(2)}, u32[]{:S(2)}) collective-permute-start(bf16[16,1280]{1,0:T(8,128)(2,1)S(1)} %shard_map.122.first), channel_id=1, source_target_pairs={{0,4},{4,0},{8,12},{12,8},{1,5},{5,1},{9,13},{13,9},{2,6},{6,2},{1... | collective-permute-start | bytes 122888 | tf_op jit(solution)/shard_map/ppermute | solution.py:191
  16.3 3.6 %collective-permute-start.9 = (bf16[16,1280]{1,0:T(8,128)(2,1)S(1)}, bf16[16,1280]{1,0:T(8,128)(2,1)S(1)}, u32[]{:S(2)}, u32[]{:S(2)}) collective-permute-start(bf16[16,1280]{1,0:T(8,128)(2,1)S(1)} %shard_map.122.first), channel_id=1, source_target_pairs={{0,12},{4,8},{8,4},{12,0},{1,13},{5,9},{9,5},{13,1},{2,14},{6,10},... | collective-permute-start | bytes 122888 | tf_op jit(solution)/shard_map/ppermute | solution.py:191
  17.6 14.7 %slice-start = ((s8[10485760]{0:T(1024)(128)(4,1)}), s8[4194304]{0:T(1024)(128)(4,1)S(1)}, s32[]{:S(2)}) async-start(s8[10485760]{0:T(1024)(128)(4,1)} %bitcast.1), calls=%async_computation | async-start | bytes 8388608
  18.5 10.0 %copy-start.6 = (bf16[1280]{0:T(1024)(128)(2,1)S(1)}, bf16[1280]{0:T(1024)(128)(2,1)}, u32[]{:S(2)}) copy-start(bf16[1280]{0:T(1024)(128)(2,1)} %param.20) | copy-start | bytes 7684
  18.5 4.4 %collective-permute-start.7 = (bf16[24,1280]{1,0:T(8,128)(2,1)S(1)}, bf16[24,1280]{1,0:T(8,128)(2,1)S(1)}, u32[]{:S(2)}, u32[]{:S(2)}) collective-permute-start(bf16[24,1280]{1,0:T(8,128)(2,1)S(1)} %get-tuple-element.47.earlier), channel_id=1, source_target_pairs={{0,1},{1,0},{2,3},{3,2},{4,5},{5,4},{6,7},{7,6},{8,9},{9,8},{10,11... | collective-permute-start | bytes 184328 | tf_op jit(solution)/shard_map/ppermute | solution.py:191
  20.0 12.3 %slice-start.1 = ((s8[10485760]{0:T(1024)(128)(4,1)}), s8[4194304]{0:T(1024)(128)(4,1)S(1)}, s32[]{:S(2)}) async-start(s8[10485760]{0:T(1024)(128)(4,1)} %bitcast.1), calls=%async_computation.1 | async-start | bytes 8388608
  20.0 1.2 %collective-permute-start.10 = (bf16[16,1280]{1,0:T(8,128)(2,1)S(1)}, bf16[16,1280]{1,0:T(8,128)(2,1)S(1)}, u32[]{:S(2)}, u32[]{:S(2)}) collective-permute-start(bf16[16,1280]{1,0:T(8,128)(2,1)S(1)} %shard_map.125), channel_id=1, source_target_pairs={{0,4},{4,0},{8,12},{12,8},{1,5},{5,1},{9,13},{13,9},{2,6},{6,2},{1... | collective-permute-start | bytes 122888 | tf_op jit(solution)/shard_map/ppermute | solution.py:191
  22.1 4.3 %collective-permute-start.11 = (bf16[24,1280]{1,0:T(8,128)(2,1)S(1)}, bf16[24,1280]{1,0:T(8,128)(2,1)S(1)}, u32[]{:S(2)}, u32[]{:S(2)}) collective-permute-start(bf16[24,1280]{1,0:T(8,128)(2,1)S(1)} %get-tuple-element.51), channel_id=1, source_target_pairs={{0,1},{1,0},{2,3},{3,2},{4,5},{5,4},{6,7},{7,6},{8,9},{9,8},{10,11... | collective-permute-start | bytes 184328 | tf_op jit(solution)/shard_map/ppermute | solution.py:191
  22.9 9.4 %slice-start.2 = ((s8[10485760]{0:T(1024)(128)(4,1)}), s8[2097152]{0:T(1024)(128)(4,1)S(1)}, s32[]{:S(2)}) async-start(s8[10485760]{0:T(1024)(128)(4,1)} %bitcast.1), calls=%async_computation.2 | async-start | bytes 4194304
  22.9 9.4 %slice-start.5 = ((s8[10485760]{0:T(1024)(128)(4,1)}), s8[2097152]{0:T(1024)(128)(4,1)S(1)}, s32[]{:S(2)}) async-start(s8[10485760]{0:T(1024)(128)(4,1)} %bitcast.3), calls=%async_computation.5 | async-start | bytes 4194304
  22.9 7.2 %collective-permute-start.8 = (bf16[24,1280]{1,0:T(8,128)(2,1)S(1)}, bf16[24,1280]{1,0:T(8,128)(2,1)S(1)}, u32[]{:S(2)}, u32[]{:S(2)}) collective-permute-start(bf16[24,1280]{1,0:T(8,128)(2,1)S(1)} %get-tuple-element.49), channel_id=1, source_target_pairs={{0,2},{1,3},{2,0},{3,1},{4,6},{5,7},{6,4},{7,5},{8,10},{9,11},{10,... | collective-permute-start | bytes 184328 | tf_op jit(solution)/shard_map/ppermute | solution.py:191
  26.4 5.8 %collective-permute-start.12 = (bf16[24,1280]{1,0:T(8,128)(2,1)S(1)}, bf16[24,1280]{1,0:T(8,128)(2,1)S(1)}, u32[]{:S(2)}, u32[]{:S(2)}) collective-permute-start(bf16[24,1280]{1,0:T(8,128)(2,1)S(1)} %get-tuple-element.53), channel_id=1, source_target_pairs={{0,2},{1,3},{2,0},{3,1},{4,6},{5,7},{6,4},{7,5},{8,10},{9,11},{10,... | collective-permute-start | bytes 184328 | tf_op jit(solution)/shard_map/ppermute | solution.py:191
  33.4 1.6 %collective-permute-start.14 = (bf16[24,2176]{1,0:T(8,128)(2,1)S(1)}, bf16[24,2176]{1,0:T(8,128)(2,1)S(1)}, u32[]{:S(2)}, u32[]{:S(2)}) collective-permute-start(bf16[24,2176]{1,0:T(8,128)(2,1)S(1)} %get-tuple-element.55.earlier), channel_id=1, source_target_pairs={{0,4},{4,0},{8,12},{12,8},{1,5},{5,1},{9,13},{13,9},{2,6},{6,2},{1... | collective-permute-start | bytes 313352 | tf_op jit(solution)/shard_map/ppermute | solution.py:191
  34.5 1.9 %collective-permute-start.13 = (bf16[24,2048]{1,0:T(8,128)(2,1)S(1)}, bf16[24,2048]{1,0:T(8,128)(2,1)S(1)}, u32[]{:S(2)}, u32[]{:S(2)}) collective-permute-start(bf16[24,2048]{1,0:T(8,128)(2,1)S(1)} %get-tuple-element.57), channel_id=1, source_target_pairs={{0,4},{4,0},{8,12},{12,8},{1,5},{5,1},{9,13},{13,9},{2,6},{6,2},{1... | collective-permute-start | bytes 294920 | tf_op jit(solution)/shard_map/ppermute | solution.py:191
  35.2 7.1 %collective-permute-start.16 = (bf16[24,2176]{1,0:T(8,128)(2,1)S(1)}, bf16[24,2176]{1,0:T(8,128)(2,1)S(1)}, u32[]{:S(2)}, u32[]{:S(2)}) collective-permute-start(bf16[24,2176]{1,0:T(8,128)(2,1)S(1)} %get-tuple-element.59.earlier), channel_id=1, source_target_pairs={{0,12},{4,8},{8,4},{12,0},{1,13},{5,9},{9,5},{13,1},{2,14},{6,10},... | collective-permute-start | bytes 313352 | tf_op jit(solution)/shard_map/ppermute | solution.py:191
  36.4 6.0 %collective-permute-start.17 = (bf16[24,2048]{1,0:T(8,128)(2,1)S(1)}, bf16[24,2048]{1,0:T(8,128)(2,1)S(1)}, u32[]{:S(2)}, u32[]{:S(2)}) collective-permute-start(bf16[24,2048]{1,0:T(8,128)(2,1)S(1)} %shard_map.131.earlier), channel_id=1, source_target_pairs={{0,12},{4,8},{8,4},{12,0},{1,13},{5,9},{9,5},{13,1},{2,14},{6,10},... | collective-permute-start | bytes 294920 | tf_op jit(solution)/shard_map/ppermute | solution.py:191
  37.5 10.2 %slice-start.6 = ((s8[10485760]{0:T(1024)(128)(4,1)}), s8[4194304]{0:T(1024)(128)(4,1)S(1)}, s32[]{:S(2)}) async-start(s8[10485760]{0:T(1024)(128)(4,1)} %bitcast.5), calls=%async_computation.6 | async-start | bytes 8388608
  37.5 10.2 %slice-start.7 = ((s8[10485760]{0:T(1024)(128)(4,1)}), s8[4194304]{0:T(1024)(128)(4,1)S(1)}, s32[]{:S(2)}) async-start(s8[10485760]{0:T(1024)(128)(4,1)} %bitcast.5), calls=%async_computation.7 | async-start | bytes 8388608
  39.4 3.1 %collective-permute-start.15 = (bf16[24,4096]{1,0:T(8,128)(2,1)S(1)}, bf16[24,4096]{1,0:T(8,128)(2,1)S(1)}, u32[]{:S(2)}, u32[]{:S(2)}) collective-permute-start(bf16[24,4096]{1,0:T(8,128)(2,1)S(1)} %get-tuple-element.61), channel_id=1, source_target_pairs={{0,4},{4,0},{8,12},{12,8},{1,5},{5,1},{9,13},{13,9},{2,6},{6,2},{1... | collective-permute-start | bytes 589832 | tf_op jit(solution)/shard_map/ppermute | solution.py:191
  42.3 5.3 %slice-start.8 = ((s8[10485760]{0:T(1024)(128)(4,1)}), s8[2097152]{0:T(1024)(128)(4,1)S(1)}, s32[]{:S(2)}) async-start(s8[10485760]{0:T(1024)(128)(4,1)} %bitcast.5), calls=%async_computation.8 | async-start | bytes 4194304
  42.7 4.9 %collective-permute-start.18 = (bf16[24,2048]{1,0:T(8,128)(2,1)S(1)}, bf16[24,2048]{1,0:T(8,128)(2,1)S(1)}, u32[]{:S(2)}, u32[]{:S(2)}) collective-permute-start(bf16[24,2048]{1,0:T(8,128)(2,1)S(1)} %shard_map.134.mine), channel_id=1, source_target_pairs={{0,12},{4,8},{8,4},{12,0},{1,13},{5,9},{9,5},{13,1},{2,14},{6,10},... | collective-permute-start | bytes 294920 | tf_op jit(solution)/shard_map/ppermute | solution.py:191
  43.9 3.7 %collective-permute-start.20 = (bf16[24,2048]{1,0:T(8,128)(2,1)S(1)}, bf16[24,2048]{1,0:T(8,128)(2,1)S(1)}, u32[]{:S(2)}, u32[]{:S(2)}) collective-permute-start(bf16[24,2048]{1,0:T(8,128)(2,1)S(1)} %shard_map.134.mine), channel_id=1, source_target_pairs={{0,4},{4,0},{8,12},{12,8},{1,5},{5,1},{9,13},{13,9},{2,6},{6,2},{1... | collective-permute-start | bytes 294920 | tf_op jit(solution)/shard_map/ppermute | solution.py:191
  47.5 1.3 %collective-permute-start.19 = (bf16[24,2048]{1,0:T(8,128)(2,1)S(1)}, bf16[24,2048]{1,0:T(8,128)(2,1)S(1)}, u32[]{:S(2)}, u32[]{:S(2)}) collective-permute-start(bf16[24,2048]{1,0:T(8,128)(2,1)S(1)} %collective-permute-done.18.mine), channel_id=1, source_target_pairs={{0,4},{4,0},{8,12},{12,8},{1,5},{5,1},{9,13},{13,9},{2,6},{6,2},{1... | collective-permute-start | bytes 294920 | tf_op jit(solution)/shard_map/ppermute | solution.py:191
  49.9 6.2 %collective-permute-start.21 = (bf16[12,1280]{1,0:T(8,128)(2,1)S(1)}, bf16[12,1280]{1,0:T(8,128)(2,1)S(1)}, u32[]{:S(2)}, u32[]{:S(2)}) collective-permute-start(bf16[12,1280]{1,0:T(8,128)(2,1)S(1)} %get-tuple-element.63), channel_id=1, source_target_pairs={{0,3},{1,2},{2,1},{3,0},{4,7},{5,6},{6,5},{7,4},{8,11},{9,10},{10,... | collective-permute-start | bytes 92168 | tf_op jit(solution)/shard_map/ppermute | solution.py:191
  51.5 5.8 %collective-permute-start.22 = (bf16[12,1280]{1,0:T(8,128)(2,1)S(1)}, bf16[12,1280]{1,0:T(8,128)(2,1)S(1)}, u32[]{:S(2)}, u32[]{:S(2)}) collective-permute-start(bf16[12,1280]{1,0:T(8,128)(2,1)S(1)} %get-tuple-element.64), channel_id=1, source_target_pairs={{0,2},{1,3},{2,0},{3,1},{4,6},{5,7},{6,4},{7,5},{8,10},{9,11},{10,... | collective-permute-start | bytes 92168 | tf_op jit(solution)/shard_map/ppermute | solution.py:191
  51.5 5.7 %collective-permute-start.23 = (bf16[12,1280]{1,0:T(8,128)(2,1)S(1)}, bf16[12,1280]{1,0:T(8,128)(2,1)S(1)}, u32[]{:S(2)}, u32[]{:S(2)}) collective-permute-start(bf16[12,1280]{1,0:T(8,128)(2,1)S(1)} %get-tuple-element.65), channel_id=1, source_target_pairs={{0,1},{1,0},{2,3},{3,2},{4,5},{5,4},{6,7},{7,6},{8,9},{9,8},{10,11... | collective-permute-start | bytes 92168 | tf_op jit(solution)/shard_map/ppermute | solution.py:191

commit v9 on v8

--- a/solution.py
+++ b/solution.py
@@ -147,7 +147,7 @@
 MIB = 1024 * 1024
 
 
-def call(kernel, outs, operands, scratch=(), smem=(), resident=(), remote=(), free=(), micros=2, limit=8):
+def call(kernel, outs, operands, scratch=(), smem=(), resident=(), remote=(), free=(), nanos=2000, limit=8):
     specs = []
     placed = []
     for place, operand in enumerate(operands):
@@ -164,7 +164,7 @@
         out_specs=[pl.BlockSpec(memory_space=pltpu.VMEM) for _ in outs],
         scratch_shapes=list(scratch),
         compiler_params=pltpu.CompilerParams(vmem_limit_bytes=limit * MIB),
-        cost_estimate=pl.CostEstimate(flops=micros * 10**9, bytes_accessed=0, transcendentals=0),
+        cost_estimate=pl.CostEstimate(flops=nanos * 10**6, bytes_accessed=0, transcendentals=0),
     )(*placed)
 
 
@@ -173,7 +173,7 @@
 
 
 def after(value, earlier):
-    (value,) = call(copy_kernel, [(value.shape, value.dtype)], (value, earlier), free=(1,), micros=0)
+    (value,) = call(copy_kernel, [(value.shape, value.dtype)], (value, earlier), free=(1,), nanos=0)
     return value
 
 
@@ -235,9 +235,10 @@
     ]
     for copy in copies:
         copy.start()
-    for copy in copies:
-        copy.wait()
+    copies[2].wait()
     picker[...] = slot_picker(per_device, group_slots(group, assign_here))
+    copies[0].wait()
+    copies[1].wait()
     split_heads(per_device, picker[...], query_here, pairs_here, rows)
     out[...] = rows[...].astype(jnp.bfloat16)
 
@@ -362,7 +363,7 @@
     half = keep.shape[0]
     for kind, weight in enumerate((gate, up)):
         for start in range(0, units, chunk):
-            column = pl.ds(pl.multiple_of(unit + start, chunk), chunk)
+            column = slice(unit + start, unit + start + chunk)
             product = jnp.dot(features, weight[:, column], preferred_element_type=jnp.float32)
             at = kind * units + start
             keep[:, at : at + chunk] = product[:half]
@@ -393,17 +394,13 @@
     scaled = (total * gain[...].astype(jnp.float32)).astype(jnp.bfloat16)
     features[...] = scaled
     units = (keep.shape[1] - 128) // 2
-    products(scaled, gate, up, (1 - (sec >> 1)) * (gate.shape[1] // 2), units, chunk, keep, send)
+    products(scaled, gate, up, 0, units, chunk, keep, send)
     keep[:, 2 * units :] = jnp.broadcast_to(squares[:half], (half, 128))
     send[:, 2 * units :] = two_terms(squares[half:])
 
 
-def gate_up_more_kernel(chunk, part, features, gate, up, earlier, keep, send):
-    units = keep.shape[1] // 2
-    width = gate.shape[1] // 2
-    away = 1 - (lax.axis_index("sec") >> 1)
-    first = away * width + width - units if part else (1 - away) * width
-    products(features[...], gate, up, first, units, chunk, keep, send)
+def gate_up_more_kernel(chunk, unit, features, gate, up, earlier, keep, send):
+    products(features[...], gate, up, unit, keep.shape[1] // 2, chunk, keep, send)
 
 
 def two_terms(column):
@@ -418,45 +415,47 @@
     return terms[:, 0:1].astype(jnp.float32) + terms[:, 64:65].astype(jnp.float32)
 
 
-def pair_sum_kernel(mine, other, send, squares):
+def pair_sum_first_kernel(mine, other, keep, send):
     width = mine.shape[1] - 128
     total = mine[:, :width] + other[:, :width].astype(jnp.float32)
+    both = mine[:, width:] + one_column(other[:, width:])
+    keep[:, :width] = total
+    keep[:, width:] = both
     send[:, :width] = total.astype(jnp.bfloat16)
-    both = mine[:, width:] + one_column(other[:, width:])
-    squares[...] = both
     send[:, width:] = two_terms(both[:, 0:1])
 
 
-def add_send_kernel(mine, other, earlier, send):
-    send[...] = (mine[...] + other[...].astype(jnp.float32)).astype(jnp.bfloat16)
-
-
-def scale_kernel(features, squares, first, second, scale):
-    width = first.shape[1] - 128
-    total = squares[:, 0:1] + one_column(first[:, width:])
-    scale[...] = jnp.broadcast_to(lax.rsqrt(total / features + 1e-06), scale.shape)
-
-
-def hidden_kernel(mine, beside, first, second, scale, hidden):
-    width = mine.shape[1] // 2
-    units = width // 2
-    factor = scale[:, 0:1]
-    for index, across in enumerate((first, second)):
-
-        def summed(kind):
-            here = slice(kind * width + index * units, kind * width + (index + 1) * units)
-            there = across[:, kind * units : (kind + 1) * units].astype(jnp.float32)
-            return (mine[:, here] + beside[:, here].astype(jnp.float32) + there) * factor
-
-        gate, up = summed(0), summed(1)
-        hidden[:, index * units : (index + 1) * units] = (gate / (1.0 + jnp.exp(-gate)) * up).astype(jnp.bfloat16)
-
-
-def down_product(away, mine, other, weight):
-    here = (lax.axis_index("sec") >> 1) ^ away
+def pair_sum_kernel(mine, other, earlier, keep, send):
+    total = mine[...] + other[...].astype(jnp.float32)
+    width = total.shape[1]
+    keep[...] = total
+    send[:, :width] = total.astype(jnp.bfloat16)
+    if send.shape[1] > width:
+        send[:, width:] = jnp.zeros_like(send[:, width:])
+
+
+def gated(mine, other, factor, hidden):
+    width = hidden.shape[1]
+    gate = (mine[:, :width] + other[:, :width].astype(jnp.float32)) * factor
+    up = (mine[:, width : 2 * width] + other[:, width : 2 * width].astype(jnp.float32)) * factor
+    hidden[...] = (gate / (1.0 + jnp.exp(-gate)) * up).astype(jnp.bfloat16)
+
+
+def hidden_first_kernel(features, mine, other, earlier, hidden, scale):
+    width = mine.shape[1] - 128
+    total = mine[:, width : width + 1] + one_column(other[:, width:])
+    factor = lax.rsqrt(total / features + 1e-06)
+    scale[...] = jnp.broadcast_to(factor, scale.shape)
+    gated(mine, other, factor, hidden)
+
+
+def hidden_kernel(mine, other, scale, hidden):
+    gated(mine, other, scale[:, 0:1], hidden)
+
+
+def down_product(unit, mine, other, weight):
     lines = jnp.concatenate([mine[...].astype(jnp.float32), other[...].astype(jnp.float32)], axis=0)
-    depth = lines.shape[1]
-    rows = weight[pl.ds(pl.multiple_of(here * depth, depth), depth), :]
+    rows = weight[unit : unit + lines.shape[1], :]
     return jnp.dot(lines.astype(jnp.bfloat16), rows, preferred_element_type=jnp.float32)
 
 
@@ -464,9 +463,13 @@
     out[...] = down_product(0, mine, other, weight)
 
 
-def down_second_kernel(mine, other, before, weight, keep, first, second, third, groups):
+def down_more_kernel(unit, before, mine, other, weight, out):
+    out[...] = before[...] + down_product(unit, mine, other, weight)
+
+
+def down_last_kernel(unit, before, mine, other, weight, keep, first, second, third, groups):
     tp = lax.axis_index("tp")
-    product = before[...] + down_product(1, mine, other, weight)
+    product = before[...] + down_product(unit, mine, other, weight)
     group = keep.shape[0]
     half = product.shape[0] // 2
     swapped = row_half() == 1
@@ -559,7 +562,7 @@
 
     def project(far, *lines):
         return call(
-            functools.partial(project_kernel, far, per_device), pair, (*lines, assign, resid, out_weight), resident=(4,), micros=0 if far else 2
+            functools.partial(project_kernel, far, per_device), pair, (*lines, assign, resid, out_weight), resident=(4,), nanos=0 if far else 2000
         )
 
     def tp_sum(mine, away):
@@ -571,68 +574,80 @@
     far = project(1, across, corner)
     sums = tp_sum(*near) + tp_sum(*far)
 
-    units = width // 4
+    count = 4
+    units = width // count
     chunk = min(512, units)
     weights = (gate_weight, up_weight)
-    mine, away, lines, stream = call(
+    wide = [((half, 2 * units + 128), f32), ((half, 2 * units + 128), bf16)]
+    plain = [((half, 2 * units), f32), ((half, 2 * units), bf16)]
+    *product, lines, stream = call(
         functools.partial(gate_up_first_kernel, chunk),
-        [
-            ((half, 2 * units + 128), f32),
-            ((half, 2 * units + 128), bf16),
-            ((2 * half, features), bf16),
-            ((group, features), f32),
-        ],
+        wide + [((2 * half, features), bf16), ((group, features), f32)],
         (*sums, gain, *weights),
         [pltpu.VMEM((2, half, features), f32), pltpu.VMEM((4, 16, features), f32)],
         resident=(5, 6),
-        micros=2,
-    )
-    beside = swap(away, "sec", 1)
-    mine_b, away_b = call(
-        functools.partial(gate_up_more_kernel, chunk, 1),
-        [((half, 2 * units), f32), ((half, 2 * units), bf16)],
-        (lines, *weights, away),
-        resident=(1, 2),
-        free=(3,),
-        micros=0,
-    )
-    beside_b = swap(away_b, "sec", 1)
-    away, squares = call(
-        pair_sum_kernel, [((half, 2 * units + 128), bf16), ((half, 128), f32)], (mine, beside), micros=0
-    )
-    across = [swap(away, "sec", 3)]
-    (away,) = call(add_send_kernel, [((half, 2 * units), bf16)], (mine_b, beside_b, away), free=(2,), micros=0)
-    across += [swap(away, "sec", 3)]
-    mine, away = call(
-        functools.partial(gate_up_more_kernel, chunk, 0),
-        [((half, 4 * units), f32), ((half, 4 * units), bf16)],
-        (lines, *weights, away),
-        resident=(1, 2),
-        free=(3,),
-        micros=0,
-    )
-    beside = swap(away, "sec", 1)
-    (scale,) = call(
-        functools.partial(scale_kernel, features * lax.axis_size("sec")),
-        [((half, 128), f32)],
-        (squares, *across),
-        free=(2,),
-        micros=4,
-    )
-    (hidden,) = call(hidden_kernel, [((half, 2 * units), bf16)], (mine, beside, *across, scale), micros=0)
-    across = swap(hidden, "sec", 3)
-    beside = swap(hidden, "sec", 1)
-    corner = swap(across, "sec", 1)
-    (before,) = call(
-        down_first_kernel, [((2 * half, features), f32)], (hidden, beside, down_weight), resident=(2,), micros=2
-    )
-    mine, *parts = call(
-        down_second_kernel,
-        [((group, features), f32)] + [((group, features), bf16)] * 3,
-        (across, corner, before, down_weight),
-        [pltpu.VMEM((4, 16, features), f32)],
-        resident=(3,),
-    )
+        nanos=2000,
+    )
+    products_made = [product]
+
+    def more_products(index, earlier):
+        return call(
+            functools.partial(gate_up_more_kernel, chunk, index * units),
+            plain,
+            (lines, *weights, earlier),
+            resident=(1, 2),
+            free=(3,),
+            nanos=0,
+        )
+
+    def pair_sum(index, earlier):
+        mine, away = products_made[index]
+        other = swap(away, "sec", 1)
+        if index == 0:
+            return call(pair_sum_first_kernel, wide, (mine, other), nanos=0)
+        outs = [plain[0], wide[1]] if index in (1,) else plain
+        return call(pair_sum_kernel, outs, (mine, other, earlier), free=(2,), nanos=0)
+
+    products_made.append(more_products(1, product[1]))
+    chip_sums = [pair_sum(0, None)]
+    chip_sums.append(pair_sum(1, chip_sums[0][1]))
+    products_made.append(more_products(2, chip_sums[1][1]))
+    products_made.append(more_products(3, products_made[2][1]))
+    chip_sums.append(pair_sum(2, products_made[3][1]))
+    chip_sums.append(pair_sum(3, chip_sums[2][1]))
+    total = [((2 * half, features), f32)]
+    before = scale = None
+    for index, (mine, away) in enumerate(chip_sums):
+        other = swap(away, "sec", 3)
+        if index == 0:
+            hidden, scale = call(
+                functools.partial(hidden_first_kernel, features * lax.axis_size("sec")),
+                [((half, units), bf16), ((half, 128), f32)],
+                (mine, other, chip_sums[-1][1]),
+                free=(2,),
+                nanos=0,
+            )
+        else:
+            (hidden,) = call(hidden_kernel, [((half, units), bf16)], (mine, other, scale), nanos=1000)
+        beside = swap(hidden, "sec", 1)
+        if index == 0:
+            (before,) = call(down_first_kernel, total, (hidden, beside, down_weight), resident=(2,), nanos=1000)
+        elif index < count - 1:
+            (before,) = call(
+                functools.partial(down_more_kernel, index * units),
+                total,
+                (before, hidden, beside, down_weight),
+                resident=(3,),
+                nanos=1000,
+            )
+        else:
+            mine, *parts = call(
+                functools.partial(down_last_kernel, index * units),
+                [((group, features), f32)] + [((group, features), bf16)] * 3,
+                (before, hidden, beside, down_weight),
+                [pltpu.VMEM((4, 16, features), f32)],
+                resident=(3,),
+            )
     parts = [swap(parts[step - 1], "tp", step) for step in (3, 2, 1)]
     (out,) = call(finish_kernel, [((group, features), bf16)], (*parts, stream, mine, order))
     return out

time: 58.2 us -> 57.3 us (0.985)
  waiting for transfers between devices: 20.1 us -> 16.6 us
  starting transfers between devices: 24.1 us -> 26.1 us
    ppermute x24 -> x28, waiting for transfers between devices: 20.1 us -> 16.6 us  [swap(): return lax.ppermute(value, axis, [(i, i ^ step) for i in range(total)])]
    ppermute x24 -> x28, starting transfers between devices: 24.1 us -> 26.1 us  [swap(): return lax.ppermute(value, axis, [(i, i ^ step) for i in range(total)])]
    pallas_call x20 -> x27, Pallas kernels: 13.5 us -> 14 us  [call(): pl.pallas_call(kernel, out_shape=[jax.ShapeDtypeStruct(shape, dtype) for...]
  transfers between devices with their start and end apart: 24 -> 28, of which waited for: 14 -> 15; matrix products, arithmetic and copies ran while one was open for 0% -> 0% of each run, Pallas kernels for 16% -> 18%
where the time goes in v9:
time: 57.3 us; the launch traced here: 57.1 us
  starting transfers between devices  26.1 us (46%)
  waiting for transfers between devices  16.6 us (29%)
  Pallas kernels  14 us (24%)
    ppermute x28, starting transfers between devices, swap(): return lax.ppermute(value, axis, [(i, i ^ step) for i in range(total)])  26.1 us
    ppermute x28, waiting for transfers between devices, swap(): return lax.ppermute(value, axis, [(i, i ^ step) for i in range(total)])  16.6 us
    pallas_call x27, Pallas kernels, call(): pl.pallas_call(kernel, out_shape=[jax.ShapeDtypeStruct(shape, dtype) for...  14 us
  transfers between devices with their start and end apart: 28, of which 15 were waited for; matrix products, arithmetic and copies ran while one was open for 0% of the time, Pallas kernels for 18%

profile of v9, /device:TPU:0, one launch (start us, length us, event | category | flops | bytes accessed | tf_op | source)
XLA Modules:
  0.0 57.1 jit_solution(13027430493720813035)
XLA Ops:
  0.0 0.5 collective-permute-start
  0.5 0.1 collective-permute-start.1
  0.6 1.4 %shard_map.118 = (bf16[2,48,128]{2,1,0:T(8,128)(2,1)S(1)}, bf16[16,12]{1,0:T(8,128)(2,1)S(1)}) custom-call(bf16[12,1280]{1,0:T(8,128)(2,1)} %query.1, bf16[12,512]{1,0:T(8,128)(2,1)} %pairs.1, s32[1,48]{1,0:T(1,128)} %bitcast.7), custom_call_target="tpu_custom_call" | custom-call | flops 2000000000 | tf_op jit(solution)/shard_map/pallas_call | solution.py:160
  2.0 0.1 shard_map.119
  2.2 2.6 %collective-permute-start.2 = (bf16[2,48,128]{2,1,0:T(8,128)(2,1)S(1)}, bf16[2,48,128]{2,1,0:T(8,128)(2,1)S(1)}, u32[]{:S(2)}, u32[]{:S(2)}) collective-permute-start(bf16[2,48,128]{2,1,0:T(8,128)(2,1)S(1)} %get-tuple-element.49), channel_id=1, source_target_pairs={{0,12},{4,8},{8,4},{12,0},{1,13},{5,9},{9,5},{13,1},{2,14},{6,10},... | collective-permute-start | bytes 73736 | tf_op jit(solution)/shard_map/ppermute | solution.py:191
  4.8 1.5 %shard_map.120 = (f32[2,4,1280]{2,1,0:T(4,128)S(1)}, bf16[12,12]{1,0:T(8,128)(2,1)S(1)}) custom-call(s32[3]{0:T(128)S(1)} %copy-done.5, bf16[2,48,128]{2,1,0:T(8,128)(2,1)S(1)} %get-tuple-element.50.source, bf16[3,224,1024]{2,1,0:T(8,128)(2,1)S(1)} %copy-done.3, bf16[3,224,1024]{2,1,0:T(8,128)(2,1)S(1)} %copy-done.4, s32[1,48]{1,0:T(1,128)S(1)} %bitcast.8), custom_call_target="tpu_custom_call" | custom-call | flops 2000000000 | tf_op jit(solution)/shard_map/pallas_call | solution.py:160
  6.3 0.0 collective-permute-done.2.source
  6.3 1.2 %shard_map.121 = (bf16[4,1280]{1,0:T(4,128)(2,1)S(1)}, bf16[4,1280]{1,0:T(4,128)(2,1)S(1)}, bf16[4,1280]{1,0:T(4,128)(2,1)S(1)}, bf16[4,1280]{1,0:T(4,128)(2,1)S(1)}) custom-call(s32[3]{0:T(128)S(1)} %copy-done.5, bf16[2,48,128]{2,1,0:T(8,128)(2,1)S(1)} %collective-permute-done.2.source, f32[2,4,1280]{2,1,0:T(4,128)S(1)} %get-tuple-element.51.near, ...), custom_call_target="tpu_custom_call" | custom-call | flops 2000000000 | tf_op jit(solution)/shard_map/pallas_call | solution.py:160
  7.4 4.2 %collective-permute-start.3 = (bf16[4,1280]{1,0:T(4,128)(2,1)S(1)}, bf16[4,1280]{1,0:T(4,128)(2,1)S(1)}, u32[]{:S(2)}, u32[]{:S(2)}) collective-permute-start(bf16[4,1280]{1,0:T(4,128)(2,1)S(1)} %get-tuple-element.52), channel_id=1, source_target_pairs={{0,7},{1,6},{2,5},{3,4},{4,3},{5,2},{6,1},{7,0},{8,15},{9,14},{10,... | collective-permute-start | bytes 30728 | tf_op jit(solution)/shard_map/ppermute | solution.py:191
  11.6 0.7 %collective-permute-start.5 = (bf16[4,1280]{1,0:T(4,128)(2,1)S(1)}, bf16[4,1280]{1,0:T(4,128)(2,1)S(1)}, u32[]{:S(2)}, u32[]{:S(2)}) collective-permute-start(bf16[4,1280]{1,0:T(4,128)(2,1)S(1)} %get-tuple-element.54), channel_id=1, source_target_pairs={{0,5},{1,4},{2,7},{3,6},{4,1},{5,0},{6,3},{7,2},{8,13},{9,12},{10,... | collective-permute-start | bytes 30728 | tf_op jit(solution)/shard_map/ppermute | solution.py:191
  12.3 0.7 %collective-permute-done.3.third = bf16[4,1280]{1,0:T(4,128)(2,1)S(1)} collective-permute-done((bf16[4,1280]{1,0:T(4,128)(2,1)S(1)}, bf16[4,1280]{1,0:T(4,128)(2,1)S(1)}, u32[]{:S(2)}, u32[]{:S(2)}) %collective-permute-start.3) | collective-permute-done | bytes 10272 | tf_op jit(solution)/shard_map/ppermute | solution.py:191
  13.0 2.6 %collective-permute-done.4.second = bf16[4,1280]{1,0:T(4,128)(2,1)S(1)} collective-permute-done((bf16[4,1280]{1,0:T(4,128)(2,1)S(1)}, bf16[4,1280]{1,0:T(4,128)(2,1)S(1)}, u32[]{:S(2)}, u32[]{:S(2)}) %collective-permute-start.4) | collective-permute-done | bytes 10272 | tf_op jit(solution)/shard_map/ppermute | solution.py:191
  15.7 0.5 collective-permute-start.6
  16.2 1.2 %collective-permute-start.9 = (bf16[16,1280]{1,0:T(8,128)(2,1)S(1)}, bf16[16,1280]{1,0:T(8,128)(2,1)S(1)}, u32[]{:S(2)}, u32[]{:S(2)}) collective-permute-start(bf16[16,1280]{1,0:T(8,128)(2,1)S(1)} %shard_map.122.first), channel_id=1, source_target_pairs={{0,12},{4,8},{8,4},{12,0},{1,13},{5,9},{9,5},{13,1},{2,14},{6,10},... | collective-permute-start | bytes 122888 | tf_op jit(solution)/shard_map/ppermute | solution.py:191
  17.4 0.9 %shard_map.123 = (f32[24,1280]{1,0:T(8,128)S(1)}, bf16[24,1280]{1,0:T(8,128)(2,1)S(1)}) custom-call(bf16[16,1280]{1,0:T(8,128)(2,1)S(1)} %shard_map.122.first, bf16[16,1280]{1,0:T(8,128)(2,1)S(1)} %collective-permute-done.6.second, s32[1,48]{1,0:T(1,128)S(1)} %bitcast.9, bf16[12,1280]{1,0:T(8,128)(2,1)S(1)} %copy-done.1, bf16[1280,1280]{1,0:T(8,128)(2,1)S(1)} %copy-done), custom_call_target="tpu_custom_call" | custom-call | flops 2000000000 | tf_op jit(solution)/shard_map/pallas_call | solution.py:160
  18.3 0.1 collective-permute-start.7
  18.4 1.4 %collective-permute-done.9.value.first = bf16[16,1280]{1,0:T(8,128)(2,1)S(1)} collective-permute-done((bf16[16,1280]{1,0:T(8,128)(2,1)S(1)}, bf16[16,1280]{1,0:T(8,128)(2,1)S(1)}, u32[]{:S(2)}, u32[]{:S(2)}) %collective-permute-start.9) | collective-permute-done | bytes 40992 | tf_op jit(solution)/shard_map/ppermute | solution.py:191
  19.8 0.1 collective-permute-start.10
  19.9 1.1 %collective-permute-done.10.second = bf16[16,1280]{1,0:T(8,128)(2,1)S(1)} collective-permute-done((bf16[16,1280]{1,0:T(8,128)(2,1)S(1)}, bf16[16,1280]{1,0:T(8,128)(2,1)S(1)}, u32[]{:S(2)}, u32[]{:S(2)}) %collective-permute-start.10) | collective-permute-done | bytes 40992 | tf_op jit(solution)/shard_map/ppermute | solution.py:191
  21.0 0.9 %shard_map.126 = (f32[24,1280]{1,0:T(8,128)S(1)}, bf16[24,1280]{1,0:T(8,128)(2,1)S(1)}) custom-call(bf16[16,1280]{1,0:T(8,128)(2,1)S(1)} %collective-permute-done.9.value.first, bf16[16,1280]{1,0:T(8,128)(2,1)S(1)} %collective-permute-done.10.second, s32[1,48]{1,0:T(1,128)S(1)} %bitcast.10, bf16[12,1280]{1,0:T(8,128)(2,1)S(1)} %copy-done.1, ...), custom_call_target="tpu_custom_call" | custom-call | tf_op jit(solution)/shard_map/pallas_call | solution.py:160
  21.9 0.7 %collective-permute-start.11 = (bf16[24,1280]{1,0:T(8,128)(2,1)S(1)}, bf16[24,1280]{1,0:T(8,128)(2,1)S(1)}, u32[]{:S(2)}, u32[]{:S(2)}) collective-permute-start(bf16[24,1280]{1,0:T(8,128)(2,1)S(1)} %get-tuple-element.61), channel_id=1, source_target_pairs={{0,1},{1,0},{2,3},{3,2},{4,5},{5,4},{6,7},{7,6},{8,9},{9,8},{10,11... | collective-permute-start | bytes 184328 | tf_op jit(solution)/shard_map/ppermute | solution.py:191
  22.6 0.1 collective-permute-done.7.other
  22.7 2.0 %collective-permute-start.8 = (bf16[24,1280]{1,0:T(8,128)(2,1)S(1)}, bf16[24,1280]{1,0:T(8,128)(2,1)S(1)}, u32[]{:S(2)}, u32[]{:S(2)}) collective-permute-start(bf16[24,1280]{1,0:T(8,128)(2,1)S(1)} %get-tuple-element.59), channel_id=1, source_target_pairs={{0,2},{1,3},{2,0},{3,1},{4,6},{5,7},{6,4},{7,5},{8,10},{9,11},{10,... | collective-permute-start | bytes 184328 | tf_op jit(solution)/shard_map/ppermute | solution.py:191
  24.8 1.4 %collective-permute-done.11.other = bf16[24,1280]{1,0:T(8,128)(2,1)S(1)} collective-permute-done((bf16[24,1280]{1,0:T(8,128)(2,1)S(1)}, bf16[24,1280]{1,0:T(8,128)(2,1)S(1)}, u32[]{:S(2)}, u32[]{:S(2)}) %collective-permute-start.11) | collective-permute-done | bytes 61472 | tf_op jit(solution)/shard_map/ppermute | solution.py:191
  26.2 2.1 %collective-permute-start.12 = (bf16[24,1280]{1,0:T(8,128)(2,1)S(1)}, bf16[24,1280]{1,0:T(8,128)(2,1)S(1)}, u32[]{:S(2)}, u32[]{:S(2)}) collective-permute-start(bf16[24,1280]{1,0:T(8,128)(2,1)S(1)} %get-tuple-element.63), channel_id=1, source_target_pairs={{0,2},{1,3},{2,0},{3,1},{4,6},{5,7},{6,4},{7,5},{8,10},{9,11},{10,... | collective-permute-start | bytes 184328 | tf_op jit(solution)/shard_map/ppermute | solution.py:191
  28.3 1.6 %collective-permute-done.8.near_other = bf16[24,1280]{1,0:T(8,128)(2,1)S(1)} collective-permute-done((bf16[24,1280]{1,0:T(8,128)(2,1)S(1)}, bf16[24,1280]{1,0:T(8,128)(2,1)S(1)}, u32[]{:S(2)}, u32[]{:S(2)}) %collective-permute-start.8) | collective-permute-done | bytes 61472 | tf_op jit(solution)/shard_map/ppermute | solution.py:191
  29.9 2.1 %collective-permute-done.12.far_other = bf16[24,1280]{1,0:T(8,128)(2,1)S(1)} collective-permute-done((bf16[24,1280]{1,0:T(8,128)(2,1)S(1)}, bf16[24,1280]{1,0:T(8,128)(2,1)S(1)}, u32[]{:S(2)}, u32[]{:S(2)}) %collective-permute-start.12) | collective-permute-done | bytes 61472 | tf_op jit(solution)/shard_map/ppermute | solution.py:191
  32.1 1.1 %shard_map.128 = (f32[24,2176]{1,0:T(8,128)S(1)}, bf16[24,2176]{1,0:T(8,128)(2,1)S(1)}, bf16[48,1280]{1,0:T(8,128)(2,1)S(1)}, f32[12,1280]{1,0:T(8,128)S(1)}) custom-call(f32[24,1280]{1,0:T(8,128)S(1)} %get-tuple-element.58.near, bf16[24,1280]{1,0:T(8,128)(2,1)S(1)} %collective-permute-done.8.near_other, f32[24,1280]{1,0:T(8,128)S(1)} %get-tuple-element.62.far, ...), custom_call_target="tpu_custom_call" | custom-call | flops 2000000000 | tf_op jit(solution)/shard_map/pallas_call | solution.py:160
  33.2 0.1 collective-permute-start.13
  33.3 1.0 %shard_map.130 = (f32[24,2048]{1,0:T(8,128)S(1)}, bf16[24,2048]{1,0:T(8,128)(2,1)S(1)}) custom-call(bf16[48,1280]{1,0:T(8,128)(2,1)S(1)} %get-tuple-element.68.features, bf16[1280,4096]{1,0:T(8,128)(2,1)S(1)} %bitcast.2, bf16[1280,4096]{1,0:T(8,128)(2,1)S(1)} %bitcast.4, bf16[24,2176]{1,0:T(8,128)(2,1)S(1)} %get-tuple-element.65.earlier), custom_call_target="tpu_custom_call" | custom-call | tf_op jit(solution)/shard_map/pallas_call | solution.py:160
  34.3 0.5 collective-permute-start.15
  34.8 0.2 shard_map.129
  35.1 1.1 %collective-permute-start.14 = (bf16[24,2176]{1,0:T(8,128)(2,1)S(1)}, bf16[24,2176]{1,0:T(8,128)(2,1)S(1)}, u32[]{:S(2)}, u32[]{:S(2)}) collective-permute-start(bf16[24,2176]{1,0:T(8,128)(2,1)S(1)} %get-tuple-element.67.earlier), channel_id=1, source_target_pairs={{0,12},{4,8},{8,4},{12,0},{1,13},{5,9},{9,5},{13,1},{2,14},{6,10},... | collective-permute-start | bytes 313352 | tf_op jit(solution)/shard_map/ppermute | solution.py:191
  36.2 1.1 %collective-permute-start.19 = (bf16[24,2176]{1,0:T(8,128)(2,1)S(1)}, bf16[24,2176]{1,0:T(8,128)(2,1)S(1)}, u32[]{:S(2)}, u32[]{:S(2)}) collective-permute-start(bf16[24,2176]{1,0:T(8,128)(2,1)S(1)} %get-tuple-element.71.earlier), channel_id=1, source_target_pairs={{0,12},{4,8},{8,4},{12,0},{1,13},{5,9},{9,5},{13,1},{2,14},{6,10},... | collective-permute-start | bytes 313352 | tf_op jit(solution)/shard_map/ppermute | solution.py:191
  37.3 1.0 %shard_map.132 = (f32[24,2048]{1,0:T(8,128)S(1)}, bf16[24,2048]{1,0:T(8,128)(2,1)S(1)}) custom-call(bf16[48,1280]{1,0:T(8,128)(2,1)S(1)} %get-tuple-element.68.features, bf16[1280,4096]{1,0:T(8,128)(2,1)S(1)} %bitcast.2, bf16[1280,4096]{1,0:T(8,128)(2,1)S(1)} %bitcast.4, bf16[24,2176]{1,0:T(8,128)(2,1)S(1)} %get-tuple-element.71.earlier), custom_call_target="tpu_custom_call" | custom-call | tf_op jit(solution)/shard_map/pallas_call | solution.py:160
  38.3 0.0 slice-start.6
  38.4 0.2 collective-permute-start.17
  38.6 1.0 %shard_map.133 = (f32[24,2048]{1,0:T(8,128)S(1)}, bf16[24,2048]{1,0:T(8,128)(2,1)S(1)}) custom-call(bf16[48,1280]{1,0:T(8,128)(2,1)S(1)} %get-tuple-element.68.features, bf16[1280,4096]{1,0:T(8,128)(2,1)S(1)} %bitcast.2, bf16[1280,4096]{1,0:T(8,128)(2,1)S(1)} %bitcast.4, bf16[24,2048]{1,0:T(8,128)(2,1)S(1)} %get-tuple-element.72.earlier), custom_call_target="tpu_custom_call" | custom-call | tf_op jit(solution)/shard_map/pallas_call | solution.py:160
  39.6 0.4 collective-permute-start.16
  40.0 0.8 %collective-permute-start.21 = (bf16[24,2048]{1,0:T(8,128)(2,1)S(1)}, bf16[24,2048]{1,0:T(8,128)(2,1)S(1)}, u32[]{:S(2)}, u32[]{:S(2)}) collective-permute-start(bf16[24,2048]{1,0:T(8,128)(2,1)S(1)} %get-tuple-element.76.earlier), channel_id=1, source_target_pairs={{0,12},{4,8},{8,4},{12,0},{1,13},{5,9},{9,5},{13,1},{2,14},{6,10},... | collective-permute-start | bytes 294920 | tf_op jit(solution)/shard_map/ppermute | solution.py:191
  40.8 0.1 collective-permute-done.16.other
  41.0 1.1 %collective-permute-start.23 = (bf16[24,2048]{1,0:T(8,128)(2,1)S(1)}, bf16[24,2048]{1,0:T(8,128)(2,1)S(1)}, u32[]{:S(2)}, u32[]{:S(2)}) collective-permute-start(bf16[24,2048]{1,0:T(8,128)(2,1)S(1)} %get-tuple-element.77.earlier), channel_id=1, source_target_pairs={{0,12},{4,8},{8,4},{12,0},{1,13},{5,9},{9,5},{13,1},{2,14},{6,10},... | collective-permute-start | bytes 294920 | tf_op jit(solution)/shard_map/ppermute | solution.py:191
  42.1 0.2 shard_map.136
  42.3 0.2 collective-permute-start.18
  42.5 0.1 shard_map.138.mine
  42.7 0.4 collective-permute-start.20
  43.1 0.5 collective-permute-done.18.other
  43.6 0.6 shard_map.137.before
  44.2 0.6 shard_map.139.before
  44.8 0.2 collective-permute-done.21.other
  45.0 0.1 shard_map.140.mine
  45.1 0.7 %collective-permute-start.22 = (bf16[24,1024]{1,0:T(8,128)(2,1)S(1)}, bf16[24,1024]{1,0:T(8,128)(2,1)S(1)}, u32[]{:S(2)}, u32[]{:S(2)}) collective-permute-start(bf16[24,1024]{1,0:T(8,128)(2,1)S(1)} %shard_map.140.mine), channel_id=1, source_target_pairs={{0,4},{4,0},{8,12},{12,8},{1,5},{5,1},{9,13},{13,9},{2,6},{6,2},{1... | collective-permute-start | bytes 147464 | tf_op jit(solution)/shard_map/ppermute | solution.py:191
  45.8 1.3 %collective-permute-done.23.other = bf16[24,2048]{1,0:T(8,128)(2,1)S(1)} collective-permute-done((bf16[24,2048]{1,0:T(8,128)(2,1)S(1)}, bf16[24,2048]{1,0:T(8,128)(2,1)S(1)}, u32[]{:S(2)}, u32[]{:S(2)}) %collective-permute-start.23) | collective-permute-done | bytes 98336 | tf_op jit(solution)/shard_map/ppermute | solution.py:191
  47.1 0.1 shard_map.142.mine
  47.2 0.2 collective-permute-start.24
  47.4 0.6 shard_map.141.before
  47.9 0.5 collective-permute-done.24.other
  48.5 0.6 %shard_map.143 = (f32[12,1280]{1,0:T(8,128)S(1)}, bf16[12,1280]{1,0:T(8,128)(2,1)S(1)}, bf16[12,1280]{1,0:T(8,128)(2,1)S(1)}, bf16[12,1280]{1,0:T(8,128)(2,1)S(1)}) custom-call(f32[48,1280]{1,0:T(8,128)S(1)} %shard_map.141.before, bf16[24,1024]{1,0:T(8,128)(2,1)S(1)} %shard_map.142.mine, bf16[24,1024]{1,0:T(8,128)(2,1)S(1)} %collective-permute-done.24.other, ...), custom_call_target="tpu_custom_call" | custom-call | flops 2000000000 | tf_op jit(solution)/shard_map/pallas_call | solution.py:160
  49.1 1.3 %collective-permute-start.25 = (bf16[12,1280]{1,0:T(8,128)(2,1)S(1)}, bf16[12,1280]{1,0:T(8,128)(2,1)S(1)}, u32[]{:S(2)}, u32[]{:S(2)}) collective-permute-start(bf16[12,1280]{1,0:T(8,128)(2,1)S(1)} %get-tuple-element.83), channel_id=1, source_target_pairs={{0,3},{1,2},{2,1},{3,0},{4,7},{5,6},{6,5},{7,4},{8,11},{9,10},{10,... | collective-permute-start | bytes 92168 | tf_op jit(solution)/shard_map/ppermute | solution.py:191
  50.3 0.2 collective-permute-start.26
  50.6 2.9 %collective-permute-start.27 = (bf16[12,1280]{1,0:T(8,128)(2,1)S(1)}, bf16[12,1280]{1,0:T(8,128)(2,1)S(1)}, u32[]{:S(2)}, u32[]{:S(2)}) collective-permute-start(bf16[12,1280]{1,0:T(8,128)(2,1)S(1)} %get-tuple-element.85), channel_id=1, source_target_pairs={{0,1},{1,0},{2,3},{3,2},{4,5},{5,4},{6,7},{7,6},{8,9},{9,8},{10,11... | collective-permute-start | bytes 92168 | tf_op jit(solution)/shard_map/ppermute | solution.py:191
  53.5 1.6 %collective-permute-done.25.third = bf16[12,1280]{1,0:T(8,128)(2,1)S(1)} collective-permute-done((bf16[12,1280]{1,0:T(8,128)(2,1)S(1)}, bf16[12,1280]{1,0:T(8,128)(2,1)S(1)}, u32[]{:S(2)}, u32[]{:S(2)}) %collective-permute-start.25) | collective-permute-done | bytes 30752 | tf_op jit(solution)/shard_map/ppermute | solution.py:191
  55.1 1.2 %collective-permute-done.26.second = bf16[12,1280]{1,0:T(8,128)(2,1)S(1)} collective-permute-done((bf16[12,1280]{1,0:T(8,128)(2,1)S(1)}, bf16[12,1280]{1,0:T(8,128)(2,1)S(1)}, u32[]{:S(2)}, u32[]{:S(2)}) %collective-permute-start.26) | collective-permute-done | bytes 30752 | tf_op jit(solution)/shard_map/ppermute | solution.py:191
  56.3 0.8 %shard_map.144 = bf16[12,1280]{1,0:T(8,128)(2,1)} custom-call(bf16[12,1280]{1,0:T(8,128)(2,1)S(1)} %collective-permute-done.25.third, bf16[12,1280]{1,0:T(8,128)(2,1)S(1)} %collective-permute-done.26.second, bf16[12,1280]{1,0:T(8,128)(2,1)S(1)} %collective-permute-done.27.first, f32[12,1280]{1,0:T(8,128)S(1)} %get-tuple-element.86.stream, ...), custom_call_target="tpu_custom_call" | custom-call | flops 2000000000 | tf_op jit(solution)/shard_map/pallas_call | solution.py:160
  (55 shorter events, 0.3 us)
Async XLA Ops:
  0.0 4.8 %copy-start.2 = (s32[48]{0:T(128)S(1)}, s32[48]{0:T(128)}, u32[]{:S(2)}) copy-start(s32[48]{0:T(128)} %param.18) | copy-start | bytes 580
  0.0 4.8 %copy-start.3 = (bf16[3,224,1024]{2,1,0:T(8,128)(2,1)S(1)}, bf16[3,224,1024]{2,1,0:T(8,128)(2,1)}, u32[]{:S(2)}) copy-start(bf16[3,224,1024]{2,1,0:T(8,128)(2,1)} %keys.3) | copy-start | bytes 4128772
  0.0 4.8 %copy-start.4 = (bf16[3,224,1024]{2,1,0:T(8,128)(2,1)S(1)}, bf16[3,224,1024]{2,1,0:T(8,128)(2,1)}, u32[]{:S(2)}) copy-start(bf16[3,224,1024]{2,1,0:T(8,128)(2,1)} %values.3) | copy-start | bytes 4128772
  0.0 4.8 %copy-start.5 = (s32[3]{0:T(128)S(1)}, s32[3]{0:T(128)}, u32[]{:S(2)}) copy-start(s32[3]{0:T(128)} %lengths.3) | copy-start | bytes 40
  0.0 2.0 %collective-permute-start = (bf16[12,1280]{1,0:T(8,128)(2,1)}, bf16[12,1280]{1,0:T(8,128)(2,1)S(1)}, u32[]{:S(2)}, u32[]{:S(2)}) collective-permute-start(bf16[12,1280]{1,0:T(8,128)(2,1)} %query.1), channel_id=1, source_target_pairs={{0,4},{4,0},{8,12},{12,8},{1,5},{5,1},{9,13},{13,9},{2,6},{6,2},{1... | collective-permute-start | bytes 92168 | tf_op jit(solution)/shard_map/ppermute | solution.py:191
  0.5 1.5 %collective-permute-start.1 = (bf16[12,512]{1,0:T(8,128)(2,1)}, bf16[12,512]{1,0:T(8,128)(2,1)S(1)}, u32[]{:S(2)}, u32[]{:S(2)}) collective-permute-start(bf16[12,512]{1,0:T(8,128)(2,1)} %pairs.1), channel_id=1, source_target_pairs={{0,4},{4,0},{8,12},{12,8},{1,5},{5,1},{9,13},{13,9},{2,6},{6,2},{1... | collective-permute-start | bytes 36872 | tf_op jit(solution)/shard_map/ppermute | solution.py:191
  2.2 4.1 %collective-permute-start.2 = (bf16[2,48,128]{2,1,0:T(8,128)(2,1)S(1)}, bf16[2,48,128]{2,1,0:T(8,128)(2,1)S(1)}, u32[]{:S(2)}, u32[]{:S(2)}) collective-permute-start(bf16[2,48,128]{2,1,0:T(8,128)(2,1)S(1)} %get-tuple-element.49), channel_id=1, source_target_pairs={{0,12},{4,8},{8,4},{12,0},{1,13},{5,9},{9,5},{13,1},{2,14},{6,10},... | collective-permute-start | bytes 73736 | tf_op jit(solution)/shard_map/ppermute | solution.py:191
  4.8 12.6 %copy-start = (bf16[1280,1280]{1,0:T(8,128)(2,1)S(1)}, bf16[1280,1280]{1,0:T(8,128)(2,1)}, u32[]{:S(2)}) copy-start(bf16[1280,1280]{1,0:T(8,128)(2,1)} %weight.7) | copy-start | bytes 9830404
  4.8 12.6 %copy-start.1 = (bf16[12,1280]{1,0:T(8,128)(2,1)S(1)}, bf16[12,1280]{1,0:T(8,128)(2,1)}, u32[]{:S(2)}) copy-start(bf16[12,1280]{1,0:T(8,128)(2,1)} %resid.3) | copy-start | bytes 92164
  7.4 5.6 %collective-permute-start.3 = (bf16[4,1280]{1,0:T(4,128)(2,1)S(1)}, bf16[4,1280]{1,0:T(4,128)(2,1)S(1)}, u32[]{:S(2)}, u32[]{:S(2)}) collective-permute-start(bf16[4,1280]{1,0:T(4,128)(2,1)S(1)} %get-tuple-element.52), channel_id=1, source_target_pairs={{0,7},{1,6},{2,5},{3,4},{4,3},{5,2},{6,1},{7,0},{8,15},{9,14},{10,... | collective-permute-start | bytes 30728 | tf_op jit(solution)/shard_map/ppermute | solution.py:191
  11.6 4.0 %collective-permute-start.4 = (bf16[4,1280]{1,0:T(4,128)(2,1)S(1)}, bf16[4,1280]{1,0:T(4,128)(2,1)S(1)}, u32[]{:S(2)}, u32[]{:S(2)}) collective-permute-start(bf16[4,1280]{1,0:T(4,128)(2,1)S(1)} %get-tuple-element.53), channel_id=1, source_target_pairs={{0,6},{1,7},{2,4},{3,5},{4,2},{5,3},{6,0},{7,1},{8,14},{9,15},{10,... | collective-permute-start | bytes 30728 | tf_op jit(solution)/shard_map/ppermute | solution.py:191
  11.6 4.0 %collective-permute-start.5 = (bf16[4,1280]{1,0:T(4,128)(2,1)S(1)}, bf16[4,1280]{1,0:T(4,128)(2,1)S(1)}, u32[]{:S(2)}, u32[]{:S(2)}) collective-permute-start(bf16[4,1280]{1,0:T(4,128)(2,1)S(1)} %get-tuple-element.54), channel_id=1, source_target_pairs={{0,5},{1,4},{2,7},{3,6},{4,1},{5,0},{6,3},{7,2},{8,13},{9,12},{10,... | collective-permute-start | bytes 30728 | tf_op jit(solution)/shard_map/ppermute | solution.py:191
  15.6 16.4 %slice-start.3 = ((s8[10485760]{0:T(1024)(128)(4,1)}), s8[4194304]{0:T(1024)(128)(4,1)S(1)}, s32[]{:S(2)}) async-start(s8[10485760]{0:T(1024)(128)(4,1)} %bitcast.3), calls=%async_computation.3 | async-start | bytes 8388608
  15.7 16.4 %slice-start.4 = ((s8[10485760]{0:T(1024)(128)(4,1)}), s8[4194304]{0:T(1024)(128)(4,1)S(1)}, s32[]{:S(2)}) async-start(s8[10485760]{0:T(1024)(128)(4,1)} %bitcast.3), calls=%async_computation.4 | async-start | bytes 8388608
  15.7 1.7 %collective-permute-start.6 = (bf16[16,1280]{1,0:T(8,128)(2,1)S(1)}, bf16[16,1280]{1,0:T(8,128)(2,1)S(1)}, u32[]{:S(2)}, u32[]{:S(2)}) collective-permute-start(bf16[16,1280]{1,0:T(8,128)(2,1)S(1)} %shard_map.122.first), channel_id=1, source_target_pairs={{0,4},{4,0},{8,12},{12,8},{1,5},{5,1},{9,13},{13,9},{2,6},{6,2},{1... | collective-permute-start | bytes 122888 | tf_op jit(solution)/shard_map/ppermute | solution.py:191
  16.2 3.6 %collective-permute-start.9 = (bf16[16,1280]{1,0:T(8,128)(2,1)S(1)}, bf16[16,1280]{1,0:T(8,128)(2,1)S(1)}, u32[]{:S(2)}, u32[]{:S(2)}) collective-permute-start(bf16[16,1280]{1,0:T(8,128)(2,1)S(1)} %shard_map.122.first), channel_id=1, source_target_pairs={{0,12},{4,8},{8,4},{12,0},{1,13},{5,9},{9,5},{13,1},{2,14},{6,10},... | collective-permute-start | bytes 122888 | tf_op jit(solution)/shard_map/ppermute | solution.py:191
  17.4 14.7 %slice-start = ((s8[10485760]{0:T(1024)(128)(4,1)}), s8[4194304]{0:T(1024)(128)(4,1)S(1)}, s32[]{:S(2)}) async-start(s8[10485760]{0:T(1024)(128)(4,1)} %bitcast.1), calls=%async_computation | async-start | bytes 8388608
  18.3 10.0 %copy-start.6 = (bf16[1280]{0:T(1024)(128)(2,1)S(1)}, bf16[1280]{0:T(1024)(128)(2,1)}, u32[]{:S(2)}) copy-start(bf16[1280]{0:T(1024)(128)(2,1)} %param.20) | copy-start | bytes 7684
  18.3 4.4 %collective-permute-start.7 = (bf16[24,1280]{1,0:T(8,128)(2,1)S(1)}, bf16[24,1280]{1,0:T(8,128)(2,1)S(1)}, u32[]{:S(2)}, u32[]{:S(2)}) collective-permute-start(bf16[24,1280]{1,0:T(8,128)(2,1)S(1)} %get-tuple-element.57.earlier), channel_id=1, source_target_pairs={{0,1},{1,0},{2,3},{3,2},{4,5},{5,4},{6,7},{7,6},{8,9},{9,8},{10,11... | collective-permute-start | bytes 184328 | tf_op jit(solution)/shard_map/ppermute | solution.py:191
  19.8 12.3 %slice-start.1 = ((s8[10485760]{0:T(1024)(128)(4,1)}), s8[4194304]{0:T(1024)(128)(4,1)S(1)}, s32[]{:S(2)}) async-start(s8[10485760]{0:T(1024)(128)(4,1)} %bitcast.1), calls=%async_computation.1 | async-start | bytes 8388608
  19.8 1.2 %collective-permute-start.10 = (bf16[16,1280]{1,0:T(8,128)(2,1)S(1)}, bf16[16,1280]{1,0:T(8,128)(2,1)S(1)}, u32[]{:S(2)}, u32[]{:S(2)}) collective-permute-start(bf16[16,1280]{1,0:T(8,128)(2,1)S(1)} %shard_map.125), channel_id=1, source_target_pairs={{0,4},{4,0},{8,12},{12,8},{1,5},{5,1},{9,13},{13,9},{2,6},{6,2},{1... | collective-permute-start | bytes 122888 | tf_op jit(solution)/shard_map/ppermute | solution.py:191
  21.9 4.3 %collective-permute-start.11 = (bf16[24,1280]{1,0:T(8,128)(2,1)S(1)}, bf16[24,1280]{1,0:T(8,128)(2,1)S(1)}, u32[]{:S(2)}, u32[]{:S(2)}) collective-permute-start(bf16[24,1280]{1,0:T(8,128)(2,1)S(1)} %get-tuple-element.61), channel_id=1, source_target_pairs={{0,1},{1,0},{2,3},{3,2},{4,5},{5,4},{6,7},{7,6},{8,9},{9,8},{10,11... | collective-permute-start | bytes 184328 | tf_op jit(solution)/shard_map/ppermute | solution.py:191
  22.7 9.4 %slice-start.2 = ((s8[10485760]{0:T(1024)(128)(4,1)}), s8[2097152]{0:T(1024)(128)(4,1)S(1)}, s32[]{:S(2)}) async-start(s8[10485760]{0:T(1024)(128)(4,1)} %bitcast.1), calls=%async_computation.2 | async-start | bytes 4194304
  22.7 9.4 %slice-start.5 = ((s8[10485760]{0:T(1024)(128)(4,1)}), s8[2097152]{0:T(1024)(128)(4,1)S(1)}, s32[]{:S(2)}) async-start(s8[10485760]{0:T(1024)(128)(4,1)} %bitcast.3), calls=%async_computation.5 | async-start | bytes 4194304
  22.7 7.2 %collective-permute-start.8 = (bf16[24,1280]{1,0:T(8,128)(2,1)S(1)}, bf16[24,1280]{1,0:T(8,128)(2,1)S(1)}, u32[]{:S(2)}, u32[]{:S(2)}) collective-permute-start(bf16[24,1280]{1,0:T(8,128)(2,1)S(1)} %get-tuple-element.59), channel_id=1, source_target_pairs={{0,2},{1,3},{2,0},{3,1},{4,6},{5,7},{6,4},{7,5},{8,10},{9,11},{10,... | collective-permute-start | bytes 184328 | tf_op jit(solution)/shard_map/ppermute | solution.py:191
  26.2 5.8 %collective-permute-start.12 = (bf16[24,1280]{1,0:T(8,128)(2,1)S(1)}, bf16[24,1280]{1,0:T(8,128)(2,1)S(1)}, u32[]{:S(2)}, u32[]{:S(2)}) collective-permute-start(bf16[24,1280]{1,0:T(8,128)(2,1)S(1)} %get-tuple-element.63), channel_id=1, source_target_pairs={{0,2},{1,3},{2,0},{3,1},{4,6},{5,7},{6,4},{7,5},{8,10},{9,11},{10,... | collective-permute-start | bytes 184328 | tf_op jit(solution)/shard_map/ppermute | solution.py:191
  33.2 1.6 %collective-permute-start.13 = (bf16[24,2176]{1,0:T(8,128)(2,1)S(1)}, bf16[24,2176]{1,0:T(8,128)(2,1)S(1)}, u32[]{:S(2)}, u32[]{:S(2)}) collective-permute-start(bf16[24,2176]{1,0:T(8,128)(2,1)S(1)} %get-tuple-element.65.earlier), channel_id=1, source_target_pairs={{0,4},{4,0},{8,12},{12,8},{1,5},{5,1},{9,13},{13,9},{2,6},{6,2},{1... | collective-permute-start | bytes 313352 | tf_op jit(solution)/shard_map/ppermute | solution.py:191
  34.3 1.9 %collective-permute-start.15 = (bf16[24,2048]{1,0:T(8,128)(2,1)S(1)}, bf16[24,2048]{1,0:T(8,128)(2,1)S(1)}, u32[]{:S(2)}, u32[]{:S(2)}) collective-permute-start(bf16[24,2048]{1,0:T(8,128)(2,1)S(1)} %get-tuple-element.70), channel_id=1, source_target_pairs={{0,4},{4,0},{8,12},{12,8},{1,5},{5,1},{9,13},{13,9},{2,6},{6,2},{1... | collective-permute-start | bytes 294920 | tf_op jit(solution)/shard_map/ppermute | solution.py:191
  35.1 7.0 %collective-permute-start.14 = (bf16[24,2176]{1,0:T(8,128)(2,1)S(1)}, bf16[24,2176]{1,0:T(8,128)(2,1)S(1)}, u32[]{:S(2)}, u32[]{:S(2)}) collective-permute-start(bf16[24,2176]{1,0:T(8,128)(2,1)S(1)} %get-tuple-element.67.earlier), channel_id=1, source_target_pairs={{0,12},{4,8},{8,4},{12,0},{1,13},{5,9},{9,5},{13,1},{2,14},{6,10},... | collective-permute-start | bytes 313352 | tf_op jit(solution)/shard_map/ppermute | solution.py:191
  36.2 6.3 %collective-permute-start.19 = (bf16[24,2176]{1,0:T(8,128)(2,1)S(1)}, bf16[24,2176]{1,0:T(8,128)(2,1)S(1)}, u32[]{:S(2)}, u32[]{:S(2)}) collective-permute-start(bf16[24,2176]{1,0:T(8,128)(2,1)S(1)} %get-tuple-element.71.earlier), channel_id=1, source_target_pairs={{0,12},{4,8},{8,4},{12,0},{1,13},{5,9},{9,5},{13,1},{2,14},{6,10},... | collective-permute-start | bytes 313352 | tf_op jit(solution)/shard_map/ppermute | solution.py:191
  38.3 5.3 %slice-start.6 = ((s8[10485760]{0:T(1024)(128)(4,1)}), s8[4194304]{0:T(1024)(128)(4,1)S(1)}, s32[]{:S(2)}) async-start(s8[10485760]{0:T(1024)(128)(4,1)} %bitcast.5), calls=%async_computation.6 | async-start | bytes 8388608
  38.4 5.2 %slice-start.7 = ((s8[10485760]{0:T(1024)(128)(4,1)}), s8[4194304]{0:T(1024)(128)(4,1)S(1)}, s32[]{:S(2)}) async-start(s8[10485760]{0:T(1024)(128)(4,1)} %bitcast.5), calls=%async_computation.7 | async-start | bytes 8388608
  38.4 5.2 %slice-start.8 = ((s8[10485760]{0:T(1024)(128)(4,1)}), s8[2097152]{0:T(1024)(128)(4,1)S(1)}, s32[]{:S(2)}) async-start(s8[10485760]{0:T(1024)(128)(4,1)} %bitcast.5), calls=%async_computation.8 | async-start | bytes 4194304
  38.4 1.6 %collective-permute-start.17 = (bf16[24,2048]{1,0:T(8,128)(2,1)S(1)}, bf16[24,2048]{1,0:T(8,128)(2,1)S(1)}, u32[]{:S(2)}, u32[]{:S(2)}) collective-permute-start(bf16[24,2048]{1,0:T(8,128)(2,1)S(1)} %get-tuple-element.72.earlier), channel_id=1, source_target_pairs={{0,4},{4,0},{8,12},{12,8},{1,5},{5,1},{9,13},{13,9},{2,6},{6,2},{1... | collective-permute-start | bytes 294920 | tf_op jit(solution)/shard_map/ppermute | solution.py:191
  39.6 1.4 %collective-permute-start.16 = (bf16[24,2048]{1,0:T(8,128)(2,1)S(1)}, bf16[24,2048]{1,0:T(8,128)(2,1)S(1)}, u32[]{:S(2)}, u32[]{:S(2)}) collective-permute-start(bf16[24,2048]{1,0:T(8,128)(2,1)S(1)} %get-tuple-element.74.earlier), channel_id=1, source_target_pairs={{0,4},{4,0},{8,12},{12,8},{1,5},{5,1},{9,13},{13,9},{2,6},{6,2},{1... | collective-permute-start | bytes 294920 | tf_op jit(solution)/shard_map/ppermute | solution.py:191
  40.0 4.9 %collective-permute-start.21 = (bf16[24,2048]{1,0:T(8,128)(2,1)S(1)}, bf16[24,2048]{1,0:T(8,128)(2,1)S(1)}, u32[]{:S(2)}, u32[]{:S(2)}) collective-permute-start(bf16[24,2048]{1,0:T(8,128)(2,1)S(1)} %get-tuple-element.76.earlier), channel_id=1, source_target_pairs={{0,12},{4,8},{8,4},{12,0},{1,13},{5,9},{9,5},{13,1},{2,14},{6,10},... | collective-permute-start | bytes 294920 | tf_op jit(solution)/shard_map/ppermute | solution.py:191
  41.0 6.1 %collective-permute-start.23 = (bf16[24,2048]{1,0:T(8,128)(2,1)S(1)}, bf16[24,2048]{1,0:T(8,128)(2,1)S(1)}, u32[]{:S(2)}, u32[]{:S(2)}) collective-permute-start(bf16[24,2048]{1,0:T(8,128)(2,1)S(1)} %get-tuple-element.77.earlier), channel_id=1, source_target_pairs={{0,12},{4,8},{8,4},{12,0},{1,13},{5,9},{9,5},{13,1},{2,14},{6,10},... | collective-permute-start | bytes 294920 | tf_op jit(solution)/shard_map/ppermute | solution.py:191
  42.3 1.3 %collective-permute-start.18 = (bf16[24,1024]{1,0:T(8,128)(2,1)S(1)}, bf16[24,1024]{1,0:T(8,128)(2,1)S(1)}, u32[]{:S(2)}, u32[]{:S(2)}) collective-permute-start(bf16[24,1024]{1,0:T(8,128)(2,1)S(1)} %get-tuple-element.78.mine), channel_id=1, source_target_pairs={{0,4},{4,0},{8,12},{12,8},{1,5},{5,1},{9,13},{13,9},{2,6},{6,2},{1... | collective-permute-start | bytes 147464 | tf_op jit(solution)/shard_map/ppermute | solution.py:191
  42.7 1.5 %collective-permute-start.20 = (bf16[24,1024]{1,0:T(8,128)(2,1)S(1)}, bf16[24,1024]{1,0:T(8,128)(2,1)S(1)}, u32[]{:S(2)}, u32[]{:S(2)}) collective-permute-start(bf16[24,1024]{1,0:T(8,128)(2,1)S(1)} %shard_map.138.mine), channel_id=1, source_target_pairs={{0,4},{4,0},{8,12},{12,8},{1,5},{5,1},{9,13},{13,9},{2,6},{6,2},{1... | collective-permute-start | bytes 147464 | tf_op jit(solution)/shard_map/ppermute | solution.py:191
  45.1 2.3 %collective-permute-start.22 = (bf16[24,1024]{1,0:T(8,128)(2,1)S(1)}, bf16[24,1024]{1,0:T(8,128)(2,1)S(1)}, u32[]{:S(2)}, u32[]{:S(2)}) collective-permute-start(bf16[24,1024]{1,0:T(8,128)(2,1)S(1)} %shard_map.140.mine), channel_id=1, source_target_pairs={{0,4},{4,0},{8,12},{12,8},{1,5},{5,1},{9,13},{13,9},{2,6},{6,2},{1... | collective-permute-start | bytes 147464 | tf_op jit(solution)/shard_map/ppermute | solution.py:191
  47.2 1.3 %collective-permute-start.24 = (bf16[24,1024]{1,0:T(8,128)(2,1)S(1)}, bf16[24,1024]{1,0:T(8,128)(2,1)S(1)}, u32[]{:S(2)}, u32[]{:S(2)}) collective-permute-start(bf16[24,1024]{1,0:T(8,128)(2,1)S(1)} %shard_map.142.mine), channel_id=1, source_target_pairs={{0,4},{4,0},{8,12},{12,8},{1,5},{5,1},{9,13},{13,9},{2,6},{6,2},{1... | collective-permute-start | bytes 147464 | tf_op jit(solution)/shard_map/ppermute | solution.py:191
  49.1 6.0 %collective-permute-start.25 = (bf16[12,1280]{1,0:T(8,128)(2,1)S(1)}, bf16[12,1280]{1,0:T(8,128)(2,1)S(1)}, u32[]{:S(2)}, u32[]{:S(2)}) collective-permute-start(bf16[12,1280]{1,0:T(8,128)(2,1)S(1)} %get-tuple-element.83), channel_id=1, source_target_pairs={{0,3},{1,2},{2,1},{3,0},{4,7},{5,6},{6,5},{7,4},{8,11},{9,10},{10,... | collective-permute-start | bytes 92168 | tf_op jit(solution)/shard_map/ppermute | solution.py:191
  50.3 6.0 %collective-permute-start.26 = (bf16[12,1280]{1,0:T(8,128)(2,1)S(1)}, bf16[12,1280]{1,0:T(8,128)(2,1)S(1)}, u32[]{:S(2)}, u32[]{:S(2)}) collective-permute-start(bf16[12,1280]{1,0:T(8,128)(2,1)S(1)} %get-tuple-element.84), channel_id=1, source_target_pairs={{0,2},{1,3},{2,0},{3,1},{4,6},{5,7},{6,4},{7,5},{8,10},{9,11},{10,... | collective-permute-start | bytes 92168 | tf_op jit(solution)/shard_map/ppermute | solution.py:191
  50.6 5.7 %collective-permute-start.27 = (bf16[12,1280]{1,0:T(8,128)(2,1)S(1)}, bf16[12,1280]{1,0:T(8,128)(2,1)S(1)}, u32[]{:S(2)}, u32[]{:S(2)}) collective-permute-start(bf16[12,1280]{1,0:T(8,128)(2,1)S(1)} %get-tuple-element.85), channel_id=1, source_target_pairs={{0,1},{1,0},{2,3},{3,2},{4,5},{5,4},{6,7},{7,6},{8,9},{9,8},{10,11... | collective-permute-start | bytes 92168 | tf_op jit(solution)/shard_map/ppermute | solution.py:191

commit v10 on v9

--- a/solution.py
+++ b/solution.py
@@ -427,11 +427,8 @@
 
 def pair_sum_kernel(mine, other, earlier, keep, send):
     total = mine[...] + other[...].astype(jnp.float32)
-    width = total.shape[1]
     keep[...] = total
-    send[:, :width] = total.astype(jnp.bfloat16)
-    if send.shape[1] > width:
-        send[:, width:] = jnp.zeros_like(send[:, width:])
+    send[...] = total.astype(jnp.bfloat16)
 
 
 def gated(mine, other, factor, hidden):
@@ -449,7 +446,7 @@
     gated(mine, other, factor, hidden)
 
 
-def hidden_kernel(mine, other, scale, hidden):
+def hidden_kernel(mine, other, scale, earlier, hidden):
     gated(mine, other, scale[:, 0:1], hidden)
 
 
@@ -574,15 +571,18 @@
     far = project(1, across, corner)
     sums = tp_sum(*near) + tp_sum(*far)
 
-    count = 4
-    units = width // count
-    chunk = min(512, units)
+    sizes = [width * sixteenths // 16 for sixteenths in (5, 5, 3, 3)]
+    starts = [sum(sizes[:index]) for index in range(len(sizes))]
+    chunk = width // 16
     weights = (gate_weight, up_weight)
-    wide = [((half, 2 * units + 128), f32), ((half, 2 * units + 128), bf16)]
-    plain = [((half, 2 * units), f32), ((half, 2 * units), bf16)]
+
+    def sums_of(index, extra=0):
+        shape = (half, 2 * sizes[index] + extra)
+        return [(shape, f32), (shape, bf16)]
+
     *product, lines, stream = call(
         functools.partial(gate_up_first_kernel, chunk),
-        wide + [((2 * half, features), bf16), ((group, features), f32)],
+        sums_of(0, 128) + [((2 * half, features), bf16), ((group, features), f32)],
         (*sums, gain, *weights),
         [pltpu.VMEM((2, half, features), f32), pltpu.VMEM((4, 16, features), f32)],
         resident=(5, 6),
@@ -592,8 +592,8 @@
 
     def more_products(index, earlier):
         return call(
-            functools.partial(gate_up_more_kernel, chunk, index * units),
-            plain,
+            functools.partial(gate_up_more_kernel, chunk, starts[index]),
+            sums_of(index),
             (lines, *weights, earlier),
             resident=(1, 2),
             free=(3,),
@@ -604,9 +604,8 @@
         mine, away = products_made[index]
         other = swap(away, "sec", 1)
         if index == 0:
-            return call(pair_sum_first_kernel, wide, (mine, other), nanos=0)
-        outs = [plain[0], wide[1]] if index in (1,) else plain
-        return call(pair_sum_kernel, outs, (mine, other, earlier), free=(2,), nanos=0)
+            return call(pair_sum_first_kernel, sums_of(0, 128), (mine, other), nanos=0)
+        return call(pair_sum_kernel, sums_of(index), (mine, other, earlier), free=(2,), nanos=0)
 
     products_made.append(more_products(1, product[1]))
     chip_sums = [pair_sum(0, None)]
@@ -617,32 +616,38 @@
     chip_sums.append(pair_sum(3, chip_sums[2][1]))
     total = [((2 * half, features), f32)]
     before = scale = None
+    parts_done = []
     for index, (mine, away) in enumerate(chip_sums):
         other = swap(away, "sec", 3)
         if index == 0:
             hidden, scale = call(
                 functools.partial(hidden_first_kernel, features * lax.axis_size("sec")),
-                [((half, units), bf16), ((half, 128), f32)],
+                [((half, sizes[0]), bf16), ((half, 128), f32)],
                 (mine, other, chip_sums[-1][1]),
                 free=(2,),
                 nanos=0,
             )
         else:
-            (hidden,) = call(hidden_kernel, [((half, units), bf16)], (mine, other, scale), nanos=1000)
+            earlier = parts_done[max(index - 2, 0)] if index > 1 else hidden
+            (hidden,) = call(
+                hidden_kernel, [((half, sizes[index]), bf16)], (mine, other, scale, earlier), free=(3,), nanos=1000
+            )
         beside = swap(hidden, "sec", 1)
         if index == 0:
             (before,) = call(down_first_kernel, total, (hidden, beside, down_weight), resident=(2,), nanos=1000)
-        elif index < count - 1:
+            parts_done.append(before)
+        elif index < len(sizes) - 1:
             (before,) = call(
-                functools.partial(down_more_kernel, index * units),
+                functools.partial(down_more_kernel, starts[index]),
                 total,
                 (before, hidden, beside, down_weight),
                 resident=(3,),
                 nanos=1000,
             )
+            parts_done.append(before)
         else:
             mine, *parts = call(
-                functools.partial(down_last_kernel, index * units),
+                functools.partial(down_last_kernel, starts[index]),
                 [((group, features), f32)] + [((group, features), bf16)] * 3,
                 (before, hidden, beside, down_weight),
                 [pltpu.VMEM((4, 16, features), f32)],

time: 57.3 us -> 57 us (level)
  no operation moved by 1% of the time
where the time goes in v10:
time: 57 us; the launch traced here: 56.8 us
  starting transfers between devices  26.1 us (46%)
  waiting for transfers between devices  16.2 us (28%)
  Pallas kernels  14.1 us (25%)
    ppermute x28, starting transfers between devices, swap(): return lax.ppermute(value, axis, [(i, i ^ step) for i in range(total)])  26.1 us
    ppermute x28, waiting for transfers between devices, swap(): return lax.ppermute(value, axis, [(i, i ^ step) for i in range(total)])  16.2 us
    pallas_call x27, Pallas kernels, call(): pl.pallas_call(kernel, out_shape=[jax.ShapeDtypeStruct(shape, dtype) for...  14.1 us
  transfers between devices with their start and end apart: 28, of which 15 were waited for; matrix products, arithmetic and copies ran while one was open for 0% of the time, Pallas kernels for 18%

profile of v10, /device:TPU:0, one launch (start us, length us, event | category | flops | bytes accessed | tf_op | source)
XLA Modules:
  0.0 56.8 jit_solution(1974714512566705329)
XLA Ops:
  0.0 0.5 collective-permute-start
  0.5 0.1 collective-permute-start.1
  0.6 1.4 %shard_map.118 = (bf16[2,48,128]{2,1,0:T(8,128)(2,1)S(1)}, bf16[16,12]{1,0:T(8,128)(2,1)S(1)}) custom-call(bf16[12,1280]{1,0:T(8,128)(2,1)} %query.1, bf16[12,512]{1,0:T(8,128)(2,1)} %pairs.1, s32[1,48]{1,0:T(1,128)} %bitcast.7), custom_call_target="tpu_custom_call" | custom-call | flops 2000000000 | tf_op jit(solution)/shard_map/pallas_call | solution.py:160
  2.0 0.1 shard_map.119
  2.2 2.6 %collective-permute-start.2 = (bf16[2,48,128]{2,1,0:T(8,128)(2,1)S(1)}, bf16[2,48,128]{2,1,0:T(8,128)(2,1)S(1)}, u32[]{:S(2)}, u32[]{:S(2)}) collective-permute-start(bf16[2,48,128]{2,1,0:T(8,128)(2,1)S(1)} %get-tuple-element.49), channel_id=1, source_target_pairs={{0,12},{4,8},{8,4},{12,0},{1,13},{5,9},{9,5},{13,1},{2,14},{6,10},... | collective-permute-start | bytes 73736 | tf_op jit(solution)/shard_map/ppermute | solution.py:191
  4.8 1.5 %shard_map.120 = (f32[2,4,1280]{2,1,0:T(4,128)S(1)}, bf16[12,12]{1,0:T(8,128)(2,1)S(1)}) custom-call(s32[3]{0:T(128)S(1)} %copy-done.5, bf16[2,48,128]{2,1,0:T(8,128)(2,1)S(1)} %get-tuple-element.50.source, bf16[3,224,1024]{2,1,0:T(8,128)(2,1)S(1)} %copy-done.3, bf16[3,224,1024]{2,1,0:T(8,128)(2,1)S(1)} %copy-done.4, s32[1,48]{1,0:T(1,128)S(1)} %bitcast.8), custom_call_target="tpu_custom_call" | custom-call | flops 2000000000 | tf_op jit(solution)/shard_map/pallas_call | solution.py:160
  6.3 0.0 collective-permute-done.2.source
  6.3 1.2 %shard_map.121 = (bf16[4,1280]{1,0:T(4,128)(2,1)S(1)}, bf16[4,1280]{1,0:T(4,128)(2,1)S(1)}, bf16[4,1280]{1,0:T(4,128)(2,1)S(1)}, bf16[4,1280]{1,0:T(4,128)(2,1)S(1)}) custom-call(s32[3]{0:T(128)S(1)} %copy-done.5, bf16[2,48,128]{2,1,0:T(8,128)(2,1)S(1)} %collective-permute-done.2.source, f32[2,4,1280]{2,1,0:T(4,128)S(1)} %get-tuple-element.51.near, ...), custom_call_target="tpu_custom_call" | custom-call | flops 2000000000 | tf_op jit(solution)/shard_map/pallas_call | solution.py:160
  7.4 4.2 %collective-permute-start.3 = (bf16[4,1280]{1,0:T(4,128)(2,1)S(1)}, bf16[4,1280]{1,0:T(4,128)(2,1)S(1)}, u32[]{:S(2)}, u32[]{:S(2)}) collective-permute-start(bf16[4,1280]{1,0:T(4,128)(2,1)S(1)} %get-tuple-element.52), channel_id=1, source_target_pairs={{0,7},{1,6},{2,5},{3,4},{4,3},{5,2},{6,1},{7,0},{8,15},{9,14},{10,... | collective-permute-start | bytes 30728 | tf_op jit(solution)/shard_map/ppermute | solution.py:191
  11.6 0.7 %collective-permute-start.5 = (bf16[4,1280]{1,0:T(4,128)(2,1)S(1)}, bf16[4,1280]{1,0:T(4,128)(2,1)S(1)}, u32[]{:S(2)}, u32[]{:S(2)}) collective-permute-start(bf16[4,1280]{1,0:T(4,128)(2,1)S(1)} %get-tuple-element.54), channel_id=1, source_target_pairs={{0,5},{1,4},{2,7},{3,6},{4,1},{5,0},{6,3},{7,2},{8,13},{9,12},{10,... | collective-permute-start | bytes 30728 | tf_op jit(solution)/shard_map/ppermute | solution.py:191
  12.3 0.7 %collective-permute-done.3.third = bf16[4,1280]{1,0:T(4,128)(2,1)S(1)} collective-permute-done((bf16[4,1280]{1,0:T(4,128)(2,1)S(1)}, bf16[4,1280]{1,0:T(4,128)(2,1)S(1)}, u32[]{:S(2)}, u32[]{:S(2)}) %collective-permute-start.3) | collective-permute-done | bytes 10272 | tf_op jit(solution)/shard_map/ppermute | solution.py:191
  13.0 2.6 %collective-permute-done.4.second = bf16[4,1280]{1,0:T(4,128)(2,1)S(1)} collective-permute-done((bf16[4,1280]{1,0:T(4,128)(2,1)S(1)}, bf16[4,1280]{1,0:T(4,128)(2,1)S(1)}, u32[]{:S(2)}, u32[]{:S(2)}) %collective-permute-start.4) | collective-permute-done | bytes 10272 | tf_op jit(solution)/shard_map/ppermute | solution.py:191
  15.7 0.5 collective-permute-start.6
  16.2 1.2 %collective-permute-start.9 = (bf16[16,1280]{1,0:T(8,128)(2,1)S(1)}, bf16[16,1280]{1,0:T(8,128)(2,1)S(1)}, u32[]{:S(2)}, u32[]{:S(2)}) collective-permute-start(bf16[16,1280]{1,0:T(8,128)(2,1)S(1)} %shard_map.122.first), channel_id=1, source_target_pairs={{0,12},{4,8},{8,4},{12,0},{1,13},{5,9},{9,5},{13,1},{2,14},{6,10},... | collective-permute-start | bytes 122888 | tf_op jit(solution)/shard_map/ppermute | solution.py:191
  17.4 0.9 %shard_map.123 = (f32[24,1280]{1,0:T(8,128)S(1)}, bf16[24,1280]{1,0:T(8,128)(2,1)S(1)}) custom-call(bf16[16,1280]{1,0:T(8,128)(2,1)S(1)} %shard_map.122.first, bf16[16,1280]{1,0:T(8,128)(2,1)S(1)} %collective-permute-done.6.second, s32[1,48]{1,0:T(1,128)S(1)} %bitcast.9, bf16[12,1280]{1,0:T(8,128)(2,1)S(1)} %copy-done.1, bf16[1280,1280]{1,0:T(8,128)(2,1)S(1)} %copy-done), custom_call_target="tpu_custom_call" | custom-call | flops 2000000000 | tf_op jit(solution)/shard_map/pallas_call | solution.py:160
  18.3 0.1 collective-permute-start.7
  18.4 1.4 %collective-permute-done.9.value.first = bf16[16,1280]{1,0:T(8,128)(2,1)S(1)} collective-permute-done((bf16[16,1280]{1,0:T(8,128)(2,1)S(1)}, bf16[16,1280]{1,0:T(8,128)(2,1)S(1)}, u32[]{:S(2)}, u32[]{:S(2)}) %collective-permute-start.9) | collective-permute-done | bytes 40992 | tf_op jit(solution)/shard_map/ppermute | solution.py:191
  19.8 0.1 collective-permute-start.10
  19.9 1.1 %collective-permute-done.10.second = bf16[16,1280]{1,0:T(8,128)(2,1)S(1)} collective-permute-done((bf16[16,1280]{1,0:T(8,128)(2,1)S(1)}, bf16[16,1280]{1,0:T(8,128)(2,1)S(1)}, u32[]{:S(2)}, u32[]{:S(2)}) %collective-permute-start.10) | collective-permute-done | bytes 40992 | tf_op jit(solution)/shard_map/ppermute | solution.py:191
  21.0 0.9 %shard_map.126 = (f32[24,1280]{1,0:T(8,128)S(1)}, bf16[24,1280]{1,0:T(8,128)(2,1)S(1)}) custom-call(bf16[16,1280]{1,0:T(8,128)(2,1)S(1)} %collective-permute-done.9.value.first, bf16[16,1280]{1,0:T(8,128)(2,1)S(1)} %collective-permute-done.10.second, s32[1,48]{1,0:T(1,128)S(1)} %bitcast.10, bf16[12,1280]{1,0:T(8,128)(2,1)S(1)} %copy-done.1, ...), custom_call_target="tpu_custom_call" | custom-call | tf_op jit(solution)/shard_map/pallas_call | solution.py:160
  21.9 0.7 %collective-permute-start.11 = (bf16[24,1280]{1,0:T(8,128)(2,1)S(1)}, bf16[24,1280]{1,0:T(8,128)(2,1)S(1)}, u32[]{:S(2)}, u32[]{:S(2)}) collective-permute-start(bf16[24,1280]{1,0:T(8,128)(2,1)S(1)} %get-tuple-element.61), channel_id=1, source_target_pairs={{0,1},{1,0},{2,3},{3,2},{4,5},{5,4},{6,7},{7,6},{8,9},{9,8},{10,11... | collective-permute-start | bytes 184328 | tf_op jit(solution)/shard_map/ppermute | solution.py:191
  22.6 0.1 collective-permute-done.7.other
  22.7 2.0 %collective-permute-start.8 = (bf16[24,1280]{1,0:T(8,128)(2,1)S(1)}, bf16[24,1280]{1,0:T(8,128)(2,1)S(1)}, u32[]{:S(2)}, u32[]{:S(2)}) collective-permute-start(bf16[24,1280]{1,0:T(8,128)(2,1)S(1)} %get-tuple-element.59), channel_id=1, source_target_pairs={{0,2},{1,3},{2,0},{3,1},{4,6},{5,7},{6,4},{7,5},{8,10},{9,11},{10,... | collective-permute-start | bytes 184328 | tf_op jit(solution)/shard_map/ppermute | solution.py:191
  24.8 1.4 %collective-permute-done.11.other = bf16[24,1280]{1,0:T(8,128)(2,1)S(1)} collective-permute-done((bf16[24,1280]{1,0:T(8,128)(2,1)S(1)}, bf16[24,1280]{1,0:T(8,128)(2,1)S(1)}, u32[]{:S(2)}, u32[]{:S(2)}) %collective-permute-start.11) | collective-permute-done | bytes 61472 | tf_op jit(solution)/shard_map/ppermute | solution.py:191
  26.2 2.1 %collective-permute-start.12 = (bf16[24,1280]{1,0:T(8,128)(2,1)S(1)}, bf16[24,1280]{1,0:T(8,128)(2,1)S(1)}, u32[]{:S(2)}, u32[]{:S(2)}) collective-permute-start(bf16[24,1280]{1,0:T(8,128)(2,1)S(1)} %get-tuple-element.63), channel_id=1, source_target_pairs={{0,2},{1,3},{2,0},{3,1},{4,6},{5,7},{6,4},{7,5},{8,10},{9,11},{10,... | collective-permute-start | bytes 184328 | tf_op jit(solution)/shard_map/ppermute | solution.py:191
  28.3 1.6 %collective-permute-done.8.near_other = bf16[24,1280]{1,0:T(8,128)(2,1)S(1)} collective-permute-done((bf16[24,1280]{1,0:T(8,128)(2,1)S(1)}, bf16[24,1280]{1,0:T(8,128)(2,1)S(1)}, u32[]{:S(2)}, u32[]{:S(2)}) %collective-permute-start.8) | collective-permute-done | bytes 61472 | tf_op jit(solution)/shard_map/ppermute | solution.py:191
  29.9 2.1 %collective-permute-done.12.far_other = bf16[24,1280]{1,0:T(8,128)(2,1)S(1)} collective-permute-done((bf16[24,1280]{1,0:T(8,128)(2,1)S(1)}, bf16[24,1280]{1,0:T(8,128)(2,1)S(1)}, u32[]{:S(2)}, u32[]{:S(2)}) %collective-permute-start.12) | collective-permute-done | bytes 61472 | tf_op jit(solution)/shard_map/ppermute | solution.py:191
  32.1 1.3 %shard_map.128 = (f32[24,2688]{1,0:T(8,128)S(1)}, bf16[24,2688]{1,0:T(8,128)(2,1)S(1)}, bf16[48,1280]{1,0:T(8,128)(2,1)S(1)}, f32[12,1280]{1,0:T(8,128)S(1)}) custom-call(f32[24,1280]{1,0:T(8,128)S(1)} %get-tuple-element.58.near, bf16[24,1280]{1,0:T(8,128)(2,1)S(1)} %collective-permute-done.8.near_other, f32[24,1280]{1,0:T(8,128)S(1)} %get-tuple-element.62.far, ...), custom_call_target="tpu_custom_call" | custom-call | flops 2000000000 | tf_op jit(solution)/shard_map/pallas_call | solution.py:160
  33.4 0.1 collective-permute-start.13
  33.5 1.3 %shard_map.130 = (f32[24,2560]{1,0:T(8,128)S(1)}, bf16[24,2560]{1,0:T(8,128)(2,1)S(1)}) custom-call(bf16[48,1280]{1,0:T(8,128)(2,1)S(1)} %get-tuple-element.68.features, bf16[1280,4096]{1,0:T(8,128)(2,1)S(1)} %bitcast.2, bf16[1280,4096]{1,0:T(8,128)(2,1)S(1)} %bitcast.4, bf16[24,2688]{1,0:T(8,128)(2,1)S(1)} %get-tuple-element.65.earlier), custom_call_target="tpu_custom_call" | custom-call | tf_op jit(solution)/shard_map/pallas_call | solution.py:160
  34.8 0.5 collective-permute-start.15
  35.3 0.2 shard_map.129
  35.5 1.1 %collective-permute-start.14 = (bf16[24,2688]{1,0:T(8,128)(2,1)S(1)}, bf16[24,2688]{1,0:T(8,128)(2,1)S(1)}, u32[]{:S(2)}, u32[]{:S(2)}) collective-permute-start(bf16[24,2688]{1,0:T(8,128)(2,1)S(1)} %get-tuple-element.67.earlier), channel_id=1, source_target_pairs={{0,12},{4,8},{8,4},{12,0},{1,13},{5,9},{9,5},{13,1},{2,14},{6,10},... | collective-permute-start | bytes 387080 | tf_op jit(solution)/shard_map/ppermute | solution.py:191
  36.7 1.1 %collective-permute-start.19 = (bf16[24,2560]{1,0:T(8,128)(2,1)S(1)}, bf16[24,2560]{1,0:T(8,128)(2,1)S(1)}, u32[]{:S(2)}, u32[]{:S(2)}) collective-permute-start(bf16[24,2560]{1,0:T(8,128)(2,1)S(1)} %get-tuple-element.71.earlier), channel_id=1, source_target_pairs={{0,12},{4,8},{8,4},{12,0},{1,13},{5,9},{9,5},{13,1},{2,14},{6,10},... | collective-permute-start | bytes 368648 | tf_op jit(solution)/shard_map/ppermute | solution.py:191
  37.8 0.8 %shard_map.132 = (f32[24,1536]{1,0:T(8,128)S(1)}, bf16[24,1536]{1,0:T(8,128)(2,1)S(1)}) custom-call(bf16[48,1280]{1,0:T(8,128)(2,1)S(1)} %get-tuple-element.68.features, bf16[1280,4096]{1,0:T(8,128)(2,1)S(1)} %bitcast.2, bf16[1280,4096]{1,0:T(8,128)(2,1)S(1)} %bitcast.4, bf16[24,2560]{1,0:T(8,128)(2,1)S(1)} %get-tuple-element.71.earlier), custom_call_target="tpu_custom_call" | custom-call | tf_op jit(solution)/shard_map/pallas_call | solution.py:160
  38.6 0.0 slice-start.6
  38.7 0.2 collective-permute-start.17
  38.9 0.8 %shard_map.133 = (f32[24,1536]{1,0:T(8,128)S(1)}, bf16[24,1536]{1,0:T(8,128)(2,1)S(1)}) custom-call(bf16[48,1280]{1,0:T(8,128)(2,1)S(1)} %get-tuple-element.68.features, bf16[1280,4096]{1,0:T(8,128)(2,1)S(1)} %bitcast.2, bf16[1280,4096]{1,0:T(8,128)(2,1)S(1)} %bitcast.4, bf16[24,1536]{1,0:T(8,128)(2,1)S(1)} %get-tuple-element.72.earlier), custom_call_target="tpu_custom_call" | custom-call | tf_op jit(solution)/shard_map/pallas_call | solution.py:160
  39.7 0.4 collective-permute-start.16
  40.1 0.8 %collective-permute-start.21 = (bf16[24,1536]{1,0:T(8,128)(2,1)S(1)}, bf16[24,1536]{1,0:T(8,128)(2,1)S(1)}, u32[]{:S(2)}, u32[]{:S(2)}) collective-permute-start(bf16[24,1536]{1,0:T(8,128)(2,1)S(1)} %get-tuple-element.76.earlier), channel_id=1, source_target_pairs={{0,12},{4,8},{8,4},{12,0},{1,13},{5,9},{9,5},{13,1},{2,14},{6,10},... | collective-permute-start | bytes 221192 | tf_op jit(solution)/shard_map/ppermute | solution.py:191
  40.9 0.1 collective-permute-done.16.other
  41.0 1.1 %collective-permute-start.23 = (bf16[24,1536]{1,0:T(8,128)(2,1)S(1)}, bf16[24,1536]{1,0:T(8,128)(2,1)S(1)}, u32[]{:S(2)}, u32[]{:S(2)}) collective-permute-start(bf16[24,1536]{1,0:T(8,128)(2,1)S(1)} %get-tuple-element.77.earlier), channel_id=1, source_target_pairs={{0,12},{4,8},{8,4},{12,0},{1,13},{5,9},{9,5},{13,1},{2,14},{6,10},... | collective-permute-start | bytes 221192 | tf_op jit(solution)/shard_map/ppermute | solution.py:191
  42.1 0.2 shard_map.136
  42.3 0.2 collective-permute-start.18
  42.5 1.2 %collective-permute-done.19.other = bf16[24,2560]{1,0:T(8,128)(2,1)S(1)} collective-permute-done((bf16[24,2560]{1,0:T(8,128)(2,1)S(1)}, bf16[24,2560]{1,0:T(8,128)(2,1)S(1)}, u32[]{:S(2)}, u32[]{:S(2)}) %collective-permute-start.19) | collective-permute-done | bytes 122912 | tf_op jit(solution)/shard_map/ppermute | solution.py:191
  43.7 0.1 shard_map.138.mine
  43.9 0.6 %collective-permute-start.20 = (bf16[24,1280]{1,0:T(8,128)(2,1)S(1)}, bf16[24,1280]{1,0:T(8,128)(2,1)S(1)}, u32[]{:S(2)}, u32[]{:S(2)}) collective-permute-start(bf16[24,1280]{1,0:T(8,128)(2,1)S(1)} %shard_map.138.mine), channel_id=1, source_target_pairs={{0,4},{4,0},{8,12},{12,8},{1,5},{5,1},{9,13},{13,9},{2,6},{6,2},{1... | collective-permute-start | bytes 184328 | tf_op jit(solution)/shard_map/ppermute | solution.py:191
  44.5 0.7 %shard_map.137.before.earlier = f32[48,1280]{1,0:T(8,128)S(1)} custom-call(bf16[24,1280]{1,0:T(8,128)(2,1)S(1)} %get-tuple-element.78.mine.earlier, bf16[24,1280]{1,0:T(8,128)(2,1)S(1)} %collective-permute-done.18.other, bf16[4096,1280]{1,0:T(8,128)(2,1)S(1)} %bitcast.6), custom_call_target="tpu_custom_call" | custom-call | flops 1000000000 | tf_op jit(solution)/shard_map/pallas_call | solution.py:160
  45.2 0.2 collective-permute-done.21.other
  45.3 0.1 shard_map.140.mine
  45.4 0.6 %collective-permute-start.22 = (bf16[24,768]{1,0:T(8,128)(2,1)S(1)}, bf16[24,768]{1,0:T(8,128)(2,1)S(1)}, u32[]{:S(2)}, u32[]{:S(2)}) collective-permute-start(bf16[24,768]{1,0:T(8,128)(2,1)S(1)} %shard_map.140.mine), channel_id=1, source_target_pairs={{0,4},{4,0},{8,12},{12,8},{1,5},{5,1},{9,13},{13,9},{2,6},{6,2},{1... | collective-permute-start | bytes 110600 | tf_op jit(solution)/shard_map/ppermute | solution.py:191
  46.0 0.7 %shard_map.139.before.earlier = f32[48,1280]{1,0:T(8,128)S(1)} custom-call(f32[48,1280]{1,0:T(8,128)S(1)} %shard_map.137.before.earlier, bf16[24,1280]{1,0:T(8,128)(2,1)S(1)} %shard_map.138.mine, bf16[24,1280]{1,0:T(8,128)(2,1)S(1)} %collective-permute-done.20.other, bf16[4096,1280]{1,0:T(8,128)(2,1)S(1)} %bitcast.6), custom_call_target="tpu_custom_call" | custom-call | flops 1000000000 | tf_op jit(solution)/shard_map/pallas_call | solution.py:160
  46.7 0.2 collective-permute-done.23.other
  46.9 0.1 shard_map.142.mine
  47.0 0.2 collective-permute-start.24
  47.2 0.5 shard_map.141.before
  47.7 0.6 %collective-permute-done.24.other = bf16[24,768]{1,0:T(8,128)(2,1)S(1)} collective-permute-done((bf16[24,768]{1,0:T(8,128)(2,1)S(1)}, bf16[24,768]{1,0:T(8,128)(2,1)S(1)}, u32[]{:S(2)}, u32[]{:S(2)}) %collective-permute-start.24) | collective-permute-done | bytes 36896 | tf_op jit(solution)/shard_map/ppermute | solution.py:191
  48.3 0.5 shard_map.143
  48.8 1.6 %collective-permute-start.25 = (bf16[12,1280]{1,0:T(8,128)(2,1)S(1)}, bf16[12,1280]{1,0:T(8,128)(2,1)S(1)}, u32[]{:S(2)}, u32[]{:S(2)}) collective-permute-start(bf16[12,1280]{1,0:T(8,128)(2,1)S(1)} %get-tuple-element.83), channel_id=1, source_target_pairs={{0,3},{1,2},{2,1},{3,0},{4,7},{5,6},{6,5},{7,4},{8,11},{9,10},{10,... | collective-permute-start | bytes 92168 | tf_op jit(solution)/shard_map/ppermute | solution.py:191
  50.3 0.1 collective-permute-start.26
  50.4 2.8 %collective-permute-start.27 = (bf16[12,1280]{1,0:T(8,128)(2,1)S(1)}, bf16[12,1280]{1,0:T(8,128)(2,1)S(1)}, u32[]{:S(2)}, u32[]{:S(2)}) collective-permute-start(bf16[12,1280]{1,0:T(8,128)(2,1)S(1)} %get-tuple-element.85), channel_id=1, source_target_pairs={{0,1},{1,0},{2,3},{3,2},{4,5},{5,4},{6,7},{7,6},{8,9},{9,8},{10,11... | collective-permute-start | bytes 92168 | tf_op jit(solution)/shard_map/ppermute | solution.py:191
  53.2 1.6 %collective-permute-done.25.third = bf16[12,1280]{1,0:T(8,128)(2,1)S(1)} collective-permute-done((bf16[12,1280]{1,0:T(8,128)(2,1)S(1)}, bf16[12,1280]{1,0:T(8,128)(2,1)S(1)}, u32[]{:S(2)}, u32[]{:S(2)}) %collective-permute-start.25) | collective-permute-done | bytes 30752 | tf_op jit(solution)/shard_map/ppermute | solution.py:191
  54.8 1.2 %collective-permute-done.26.second = bf16[12,1280]{1,0:T(8,128)(2,1)S(1)} collective-permute-done((bf16[12,1280]{1,0:T(8,128)(2,1)S(1)}, bf16[12,1280]{1,0:T(8,128)(2,1)S(1)}, u32[]{:S(2)}, u32[]{:S(2)}) %collective-permute-start.26) | collective-permute-done | bytes 30752 | tf_op jit(solution)/shard_map/ppermute | solution.py:191
  56.0 0.8 %shard_map.144 = bf16[12,1280]{1,0:T(8,128)(2,1)} custom-call(bf16[12,1280]{1,0:T(8,128)(2,1)S(1)} %collective-permute-done.25.third, bf16[12,1280]{1,0:T(8,128)(2,1)S(1)} %collective-permute-done.26.second, bf16[12,1280]{1,0:T(8,128)(2,1)S(1)} %collective-permute-done.27.first, f32[12,1280]{1,0:T(8,128)S(1)} %get-tuple-element.86.stream, ...), custom_call_target="tpu_custom_call" | custom-call | flops 2000000000 | tf_op jit(solution)/shard_map/pallas_call | solution.py:160
  (55 shorter events, 0.2 us)
Async XLA Ops:
  0.0 4.8 %copy-start.2 = (s32[48]{0:T(128)S(1)}, s32[48]{0:T(128)}, u32[]{:S(2)}) copy-start(s32[48]{0:T(128)} %param.18) | copy-start | bytes 580
  0.0 4.8 %copy-start.3 = (bf16[3,224,1024]{2,1,0:T(8,128)(2,1)S(1)}, bf16[3,224,1024]{2,1,0:T(8,128)(2,1)}, u32[]{:S(2)}) copy-start(bf16[3,224,1024]{2,1,0:T(8,128)(2,1)} %keys.3) | copy-start | bytes 4128772
  0.0 4.8 %copy-start.4 = (bf16[3,224,1024]{2,1,0:T(8,128)(2,1)S(1)}, bf16[3,224,1024]{2,1,0:T(8,128)(2,1)}, u32[]{:S(2)}) copy-start(bf16[3,224,1024]{2,1,0:T(8,128)(2,1)} %values.3) | copy-start | bytes 4128772
  0.0 4.8 %copy-start.5 = (s32[3]{0:T(128)S(1)}, s32[3]{0:T(128)}, u32[]{:S(2)}) copy-start(s32[3]{0:T(128)} %lengths.3) | copy-start | bytes 40
  0.0 2.0 %collective-permute-start = (bf16[12,1280]{1,0:T(8,128)(2,1)}, bf16[12,1280]{1,0:T(8,128)(2,1)S(1)}, u32[]{:S(2)}, u32[]{:S(2)}) collective-permute-start(bf16[12,1280]{1,0:T(8,128)(2,1)} %query.1), channel_id=1, source_target_pairs={{0,4},{4,0},{8,12},{12,8},{1,5},{5,1},{9,13},{13,9},{2,6},{6,2},{1... | collective-permute-start | bytes 92168 | tf_op jit(solution)/shard_map/ppermute | solution.py:191
  0.5 1.5 %collective-permute-start.1 = (bf16[12,512]{1,0:T(8,128)(2,1)}, bf16[12,512]{1,0:T(8,128)(2,1)S(1)}, u32[]{:S(2)}, u32[]{:S(2)}) collective-permute-start(bf16[12,512]{1,0:T(8,128)(2,1)} %pairs.1), channel_id=1, source_target_pairs={{0,4},{4,0},{8,12},{12,8},{1,5},{5,1},{9,13},{13,9},{2,6},{6,2},{1... | collective-permute-start | bytes 36872 | tf_op jit(solution)/shard_map/ppermute | solution.py:191
  2.2 4.1 %collective-permute-start.2 = (bf16[2,48,128]{2,1,0:T(8,128)(2,1)S(1)}, bf16[2,48,128]{2,1,0:T(8,128)(2,1)S(1)}, u32[]{:S(2)}, u32[]{:S(2)}) collective-permute-start(bf16[2,48,128]{2,1,0:T(8,128)(2,1)S(1)} %get-tuple-element.49), channel_id=1, source_target_pairs={{0,12},{4,8},{8,4},{12,0},{1,13},{5,9},{9,5},{13,1},{2,14},{6,10},... | collective-permute-start | bytes 73736 | tf_op jit(solution)/shard_map/ppermute | solution.py:191
  4.8 12.6 %copy-start = (bf16[1280,1280]{1,0:T(8,128)(2,1)S(1)}, bf16[1280,1280]{1,0:T(8,128)(2,1)}, u32[]{:S(2)}) copy-start(bf16[1280,1280]{1,0:T(8,128)(2,1)} %weight.7) | copy-start | bytes 9830404
  4.8 12.6 %copy-start.1 = (bf16[12,1280]{1,0:T(8,128)(2,1)S(1)}, bf16[12,1280]{1,0:T(8,128)(2,1)}, u32[]{:S(2)}) copy-start(bf16[12,1280]{1,0:T(8,128)(2,1)} %resid.3) | copy-start | bytes 92164
  7.4 5.6 %collective-permute-start.3 = (bf16[4,1280]{1,0:T(4,128)(2,1)S(1)}, bf16[4,1280]{1,0:T(4,128)(2,1)S(1)}, u32[]{:S(2)}, u32[]{:S(2)}) collective-permute-start(bf16[4,1280]{1,0:T(4,128)(2,1)S(1)} %get-tuple-element.52), channel_id=1, source_target_pairs={{0,7},{1,6},{2,5},{3,4},{4,3},{5,2},{6,1},{7,0},{8,15},{9,14},{10,... | collective-permute-start | bytes 30728 | tf_op jit(solution)/shard_map/ppermute | solution.py:191
  11.6 4.0 %collective-permute-start.4 = (bf16[4,1280]{1,0:T(4,128)(2,1)S(1)}, bf16[4,1280]{1,0:T(4,128)(2,1)S(1)}, u32[]{:S(2)}, u32[]{:S(2)}) collective-permute-start(bf16[4,1280]{1,0:T(4,128)(2,1)S(1)} %get-tuple-element.53), channel_id=1, source_target_pairs={{0,6},{1,7},{2,4},{3,5},{4,2},{5,3},{6,0},{7,1},{8,14},{9,15},{10,... | collective-permute-start | bytes 30728 | tf_op jit(solution)/shard_map/ppermute | solution.py:191
  11.6 4.0 %collective-permute-start.5 = (bf16[4,1280]{1,0:T(4,128)(2,1)S(1)}, bf16[4,1280]{1,0:T(4,128)(2,1)S(1)}, u32[]{:S(2)}, u32[]{:S(2)}) collective-permute-start(bf16[4,1280]{1,0:T(4,128)(2,1)S(1)} %get-tuple-element.54), channel_id=1, source_target_pairs={{0,5},{1,4},{2,7},{3,6},{4,1},{5,0},{6,3},{7,2},{8,13},{9,12},{10,... | collective-permute-start | bytes 30728 | tf_op jit(solution)/shard_map/ppermute | solution.py:191
  15.6 16.4 %slice-start.3 = ((s8[10485760]{0:T(1024)(128)(4,1)}), s8[4194304]{0:T(1024)(128)(4,1)S(1)}, s32[]{:S(2)}) async-start(s8[10485760]{0:T(1024)(128)(4,1)} %bitcast.3), calls=%async_computation.3 | async-start | bytes 8388608
  15.7 16.4 %slice-start.4 = ((s8[10485760]{0:T(1024)(128)(4,1)}), s8[4194304]{0:T(1024)(128)(4,1)S(1)}, s32[]{:S(2)}) async-start(s8[10485760]{0:T(1024)(128)(4,1)} %bitcast.3), calls=%async_computation.4 | async-start | bytes 8388608
  15.7 1.7 %collective-permute-start.6 = (bf16[16,1280]{1,0:T(8,128)(2,1)S(1)}, bf16[16,1280]{1,0:T(8,128)(2,1)S(1)}, u32[]{:S(2)}, u32[]{:S(2)}) collective-permute-start(bf16[16,1280]{1,0:T(8,128)(2,1)S(1)} %shard_map.122.first), channel_id=1, source_target_pairs={{0,4},{4,0},{8,12},{12,8},{1,5},{5,1},{9,13},{13,9},{2,6},{6,2},{1... | collective-permute-start | bytes 122888 | tf_op jit(solution)/shard_map/ppermute | solution.py:191
  16.2 3.6 %collective-permute-start.9 = (bf16[16,1280]{1,0:T(8,128)(2,1)S(1)}, bf16[16,1280]{1,0:T(8,128)(2,1)S(1)}, u32[]{:S(2)}, u32[]{:S(2)}) collective-permute-start(bf16[16,1280]{1,0:T(8,128)(2,1)S(1)} %shard_map.122.first), channel_id=1, source_target_pairs={{0,12},{4,8},{8,4},{12,0},{1,13},{5,9},{9,5},{13,1},{2,14},{6,10},... | collective-permute-start | bytes 122888 | tf_op jit(solution)/shard_map/ppermute | solution.py:191
  17.4 14.7 %slice-start = ((s8[10485760]{0:T(1024)(128)(4,1)}), s8[4194304]{0:T(1024)(128)(4,1)S(1)}, s32[]{:S(2)}) async-start(s8[10485760]{0:T(1024)(128)(4,1)} %bitcast.1), calls=%async_computation | async-start | bytes 8388608
  18.3 10.0 %copy-start.6 = (bf16[1280]{0:T(1024)(128)(2,1)S(1)}, bf16[1280]{0:T(1024)(128)(2,1)}, u32[]{:S(2)}) copy-start(bf16[1280]{0:T(1024)(128)(2,1)} %param.20) | copy-start | bytes 7684
  18.3 4.4 %collective-permute-start.7 = (bf16[24,1280]{1,0:T(8,128)(2,1)S(1)}, bf16[24,1280]{1,0:T(8,128)(2,1)S(1)}, u32[]{:S(2)}, u32[]{:S(2)}) collective-permute-start(bf16[24,1280]{1,0:T(8,128)(2,1)S(1)} %get-tuple-element.57.earlier), channel_id=1, source_target_pairs={{0,1},{1,0},{2,3},{3,2},{4,5},{5,4},{6,7},{7,6},{8,9},{9,8},{10,11... | collective-permute-start | bytes 184328 | tf_op jit(solution)/shard_map/ppermute | solution.py:191
  19.8 12.3 %slice-start.1 = ((s8[10485760]{0:T(1024)(128)(4,1)}), s8[4194304]{0:T(1024)(128)(4,1)S(1)}, s32[]{:S(2)}) async-start(s8[10485760]{0:T(1024)(128)(4,1)} %bitcast.1), calls=%async_computation.1 | async-start | bytes 8388608
  19.8 1.2 %collective-permute-start.10 = (bf16[16,1280]{1,0:T(8,128)(2,1)S(1)}, bf16[16,1280]{1,0:T(8,128)(2,1)S(1)}, u32[]{:S(2)}, u32[]{:S(2)}) collective-permute-start(bf16[16,1280]{1,0:T(8,128)(2,1)S(1)} %shard_map.125), channel_id=1, source_target_pairs={{0,4},{4,0},{8,12},{12,8},{1,5},{5,1},{9,13},{13,9},{2,6},{6,2},{1... | collective-permute-start | bytes 122888 | tf_op jit(solution)/shard_map/ppermute | solution.py:191
  21.9 4.3 %collective-permute-start.11 = (bf16[24,1280]{1,0:T(8,128)(2,1)S(1)}, bf16[24,1280]{1,0:T(8,128)(2,1)S(1)}, u32[]{:S(2)}, u32[]{:S(2)}) collective-permute-start(bf16[24,1280]{1,0:T(8,128)(2,1)S(1)} %get-tuple-element.61), channel_id=1, source_target_pairs={{0,1},{1,0},{2,3},{3,2},{4,5},{5,4},{6,7},{7,6},{8,9},{9,8},{10,11... | collective-permute-start | bytes 184328 | tf_op jit(solution)/shard_map/ppermute | solution.py:191
  22.7 9.4 %slice-start.2 = ((s8[10485760]{0:T(1024)(128)(4,1)}), s8[2097152]{0:T(1024)(128)(4,1)S(1)}, s32[]{:S(2)}) async-start(s8[10485760]{0:T(1024)(128)(4,1)} %bitcast.1), calls=%async_computation.2 | async-start | bytes 4194304
  22.7 9.4 %slice-start.5 = ((s8[10485760]{0:T(1024)(128)(4,1)}), s8[2097152]{0:T(1024)(128)(4,1)S(1)}, s32[]{:S(2)}) async-start(s8[10485760]{0:T(1024)(128)(4,1)} %bitcast.3), calls=%async_computation.5 | async-start | bytes 4194304
  22.7 7.2 %collective-permute-start.8 = (bf16[24,1280]{1,0:T(8,128)(2,1)S(1)}, bf16[24,1280]{1,0:T(8,128)(2,1)S(1)}, u32[]{:S(2)}, u32[]{:S(2)}) collective-permute-start(bf16[24,1280]{1,0:T(8,128)(2,1)S(1)} %get-tuple-element.59), channel_id=1, source_target_pairs={{0,2},{1,3},{2,0},{3,1},{4,6},{5,7},{6,4},{7,5},{8,10},{9,11},{10,... | collective-permute-start | bytes 184328 | tf_op jit(solution)/shard_map/ppermute | solution.py:191
  26.2 5.8 %collective-permute-start.12 = (bf16[24,1280]{1,0:T(8,128)(2,1)S(1)}, bf16[24,1280]{1,0:T(8,128)(2,1)S(1)}, u32[]{:S(2)}, u32[]{:S(2)}) collective-permute-start(bf16[24,1280]{1,0:T(8,128)(2,1)S(1)} %get-tuple-element.63), channel_id=1, source_target_pairs={{0,2},{1,3},{2,0},{3,1},{4,6},{5,7},{6,4},{7,5},{8,10},{9,11},{10,... | collective-permute-start | bytes 184328 | tf_op jit(solution)/shard_map/ppermute | solution.py:191
  33.4 1.9 %collective-permute-start.13 = (bf16[24,2688]{1,0:T(8,128)(2,1)S(1)}, bf16[24,2688]{1,0:T(8,128)(2,1)S(1)}, u32[]{:S(2)}, u32[]{:S(2)}) collective-permute-start(bf16[24,2688]{1,0:T(8,128)(2,1)S(1)} %get-tuple-element.65.earlier), channel_id=1, source_target_pairs={{0,4},{4,0},{8,12},{12,8},{1,5},{5,1},{9,13},{13,9},{2,6},{6,2},{1... | collective-permute-start | bytes 387080 | tf_op jit(solution)/shard_map/ppermute | solution.py:191
  34.8 1.9 %collective-permute-start.15 = (bf16[24,2560]{1,0:T(8,128)(2,1)S(1)}, bf16[24,2560]{1,0:T(8,128)(2,1)S(1)}, u32[]{:S(2)}, u32[]{:S(2)}) collective-permute-start(bf16[24,2560]{1,0:T(8,128)(2,1)S(1)} %get-tuple-element.70), channel_id=1, source_target_pairs={{0,4},{4,0},{8,12},{12,8},{1,5},{5,1},{9,13},{13,9},{2,6},{6,2},{1... | collective-permute-start | bytes 368648 | tf_op jit(solution)/shard_map/ppermute | solution.py:191
  35.5 6.6 %collective-permute-start.14 = (bf16[24,2688]{1,0:T(8,128)(2,1)S(1)}, bf16[24,2688]{1,0:T(8,128)(2,1)S(1)}, u32[]{:S(2)}, u32[]{:S(2)}) collective-permute-start(bf16[24,2688]{1,0:T(8,128)(2,1)S(1)} %get-tuple-element.67.earlier), channel_id=1, source_target_pairs={{0,12},{4,8},{8,4},{12,0},{1,13},{5,9},{9,5},{13,1},{2,14},{6,10},... | collective-permute-start | bytes 387080 | tf_op jit(solution)/shard_map/ppermute | solution.py:191
  36.7 7.0 %collective-permute-start.19 = (bf16[24,2560]{1,0:T(8,128)(2,1)S(1)}, bf16[24,2560]{1,0:T(8,128)(2,1)S(1)}, u32[]{:S(2)}, u32[]{:S(2)}) collective-permute-start(bf16[24,2560]{1,0:T(8,128)(2,1)S(1)} %get-tuple-element.71.earlier), channel_id=1, source_target_pairs={{0,12},{4,8},{8,4},{12,0},{1,13},{5,9},{9,5},{13,1},{2,14},{6,10},... | collective-permute-start | bytes 368648 | tf_op jit(solution)/shard_map/ppermute | solution.py:191
  38.6 5.8 %slice-start.6 = ((s8[10485760]{0:T(1024)(128)(4,1)}), s8[4194304]{0:T(1024)(128)(4,1)S(1)}, s32[]{:S(2)}) async-start(s8[10485760]{0:T(1024)(128)(4,1)} %bitcast.5), calls=%async_computation.6 | async-start | bytes 8388608
  38.6 5.8 %slice-start.7 = ((s8[10485760]{0:T(1024)(128)(4,1)}), s8[4194304]{0:T(1024)(128)(4,1)S(1)}, s32[]{:S(2)}) async-start(s8[10485760]{0:T(1024)(128)(4,1)} %bitcast.5), calls=%async_computation.7 | async-start | bytes 8388608
  38.6 5.8 %slice-start.8 = ((s8[10485760]{0:T(1024)(128)(4,1)}), s8[2097152]{0:T(1024)(128)(4,1)S(1)}, s32[]{:S(2)}) async-start(s8[10485760]{0:T(1024)(128)(4,1)} %bitcast.5), calls=%async_computation.8 | async-start | bytes 4194304
  38.7 1.4 %collective-permute-start.17 = (bf16[24,1536]{1,0:T(8,128)(2,1)S(1)}, bf16[24,1536]{1,0:T(8,128)(2,1)S(1)}, u32[]{:S(2)}, u32[]{:S(2)}) collective-permute-start(bf16[24,1536]{1,0:T(8,128)(2,1)S(1)} %get-tuple-element.72.earlier), channel_id=1, source_target_pairs={{0,4},{4,0},{8,12},{12,8},{1,5},{5,1},{9,13},{13,9},{2,6},{6,2},{1... | collective-permute-start | bytes 221192 | tf_op jit(solution)/shard_map/ppermute | solution.py:191
  39.7 1.3 %collective-permute-start.16 = (bf16[24,1536]{1,0:T(8,128)(2,1)S(1)}, bf16[24,1536]{1,0:T(8,128)(2,1)S(1)}, u32[]{:S(2)}, u32[]{:S(2)}) collective-permute-start(bf16[24,1536]{1,0:T(8,128)(2,1)S(1)} %get-tuple-element.74.earlier), channel_id=1, source_target_pairs={{0,4},{4,0},{8,12},{12,8},{1,5},{5,1},{9,13},{13,9},{2,6},{6,2},{1... | collective-permute-start | bytes 221192 | tf_op jit(solution)/shard_map/ppermute | solution.py:191
  40.1 5.2 %collective-permute-start.21 = (bf16[24,1536]{1,0:T(8,128)(2,1)S(1)}, bf16[24,1536]{1,0:T(8,128)(2,1)S(1)}, u32[]{:S(2)}, u32[]{:S(2)}) collective-permute-start(bf16[24,1536]{1,0:T(8,128)(2,1)S(1)} %get-tuple-element.76.earlier), channel_id=1, source_target_pairs={{0,12},{4,8},{8,4},{12,0},{1,13},{5,9},{9,5},{13,1},{2,14},{6,10},... | collective-permute-start | bytes 221192 | tf_op jit(solution)/shard_map/ppermute | solution.py:191
  41.0 5.9 %collective-permute-start.23 = (bf16[24,1536]{1,0:T(8,128)(2,1)S(1)}, bf16[24,1536]{1,0:T(8,128)(2,1)S(1)}, u32[]{:S(2)}, u32[]{:S(2)}) collective-permute-start(bf16[24,1536]{1,0:T(8,128)(2,1)S(1)} %get-tuple-element.77.earlier), channel_id=1, source_target_pairs={{0,12},{4,8},{8,4},{12,0},{1,13},{5,9},{9,5},{13,1},{2,14},{6,10},... | collective-permute-start | bytes 221192 | tf_op jit(solution)/shard_map/ppermute | solution.py:191
  42.3 2.1 %collective-permute-start.18 = (bf16[24,1280]{1,0:T(8,128)(2,1)S(1)}, bf16[24,1280]{1,0:T(8,128)(2,1)S(1)}, u32[]{:S(2)}, u32[]{:S(2)}) collective-permute-start(bf16[24,1280]{1,0:T(8,128)(2,1)S(1)} %get-tuple-element.78.mine.earlier), channel_id=1, source_target_pairs={{0,4},{4,0},{8,12},{12,8},{1,5},{5,1},{9,13},{13,9},{2,6},{6,2},{1... | collective-permute-start | bytes 184328 | tf_op jit(solution)/shard_map/ppermute | solution.py:191
  43.9 2.1 %collective-permute-start.20 = (bf16[24,1280]{1,0:T(8,128)(2,1)S(1)}, bf16[24,1280]{1,0:T(8,128)(2,1)S(1)}, u32[]{:S(2)}, u32[]{:S(2)}) collective-permute-start(bf16[24,1280]{1,0:T(8,128)(2,1)S(1)} %shard_map.138.mine), channel_id=1, source_target_pairs={{0,4},{4,0},{8,12},{12,8},{1,5},{5,1},{9,13},{13,9},{2,6},{6,2},{1... | collective-permute-start | bytes 184328 | tf_op jit(solution)/shard_map/ppermute | solution.py:191
  45.4 1.8 %collective-permute-start.22 = (bf16[24,768]{1,0:T(8,128)(2,1)S(1)}, bf16[24,768]{1,0:T(8,128)(2,1)S(1)}, u32[]{:S(2)}, u32[]{:S(2)}) collective-permute-start(bf16[24,768]{1,0:T(8,128)(2,1)S(1)} %shard_map.140.mine), channel_id=1, source_target_pairs={{0,4},{4,0},{8,12},{12,8},{1,5},{5,1},{9,13},{13,9},{2,6},{6,2},{1... | collective-permute-start | bytes 110600 | tf_op jit(solution)/shard_map/ppermute | solution.py:191
  47.0 1.3 %collective-permute-start.24 = (bf16[24,768]{1,0:T(8,128)(2,1)S(1)}, bf16[24,768]{1,0:T(8,128)(2,1)S(1)}, u32[]{:S(2)}, u32[]{:S(2)}) collective-permute-start(bf16[24,768]{1,0:T(8,128)(2,1)S(1)} %shard_map.142.mine), channel_id=1, source_target_pairs={{0,4},{4,0},{8,12},{12,8},{1,5},{5,1},{9,13},{13,9},{2,6},{6,2},{1... | collective-permute-start | bytes 110600 | tf_op jit(solution)/shard_map/ppermute | solution.py:191
  48.8 6.0 %collective-permute-start.25 = (bf16[12,1280]{1,0:T(8,128)(2,1)S(1)}, bf16[12,1280]{1,0:T(8,128)(2,1)S(1)}, u32[]{:S(2)}, u32[]{:S(2)}) collective-permute-start(bf16[12,1280]{1,0:T(8,128)(2,1)S(1)} %get-tuple-element.83), channel_id=1, source_target_pairs={{0,3},{1,2},{2,1},{3,0},{4,7},{5,6},{6,5},{7,4},{8,11},{9,10},{10,... | collective-permute-start | bytes 92168 | tf_op jit(solution)/shard_map/ppermute | solution.py:191
  50.3 5.7 %collective-permute-start.26 = (bf16[12,1280]{1,0:T(8,128)(2,1)S(1)}, bf16[12,1280]{1,0:T(8,128)(2,1)S(1)}, u32[]{:S(2)}, u32[]{:S(2)}) collective-permute-start(bf16[12,1280]{1,0:T(8,128)(2,1)S(1)} %get-tuple-element.84), channel_id=1, source_target_pairs={{0,2},{1,3},{2,0},{3,1},{4,6},{5,7},{6,4},{7,5},{8,10},{9,11},{10,... | collective-permute-start | bytes 92168 | tf_op jit(solution)/shard_map/ppermute | solution.py:191
  50.4 5.6 %collective-permute-start.27 = (bf16[12,1280]{1,0:T(8,128)(2,1)S(1)}, bf16[12,1280]{1,0:T(8,128)(2,1)S(1)}, u32[]{:S(2)}, u32[]{:S(2)}) collective-permute-start(bf16[12,1280]{1,0:T(8,128)(2,1)S(1)} %get-tuple-element.85), channel_id=1, source_target_pairs={{0,1},{1,0},{2,3},{3,2},{4,5},{5,4},{6,7},{7,6},{8,9},{9,8},{10,11... | collective-permute-start | bytes 92168 | tf_op jit(solution)/shard_map/ppermute | solution.py:191

commit v11 on v10

--- a/solution.py
+++ b/solution.py
@@ -257,26 +257,32 @@
     slots = keys.shape[1]
     width = HEAD_WIDTH
     scaling = 1.0 / math.sqrt(width)
-    line = lax.broadcasted_iota(jnp.int32, (16, width), 0)
-    upper = line < share
-    place = lax.broadcasted_iota(jnp.int32, (16, slots), 1)
-    work = [(i, j) for i in range(2) for j in range(per_device)]
-    past, fresh, new_values, columns = [], [], [], []
-    for i, j in work:
-        wide = source[i, j * 16 : (j + 1) * 16].astype(jnp.float32)
+    line = lax.broadcasted_iota(jnp.int32, (32, width), 0)
+    kind = 2 * (line >> 4) + jnp.where((line & 15) < share, 0, 1)
+    upper = (lax.broadcasted_iota(jnp.int32, (16, width), 0)) < share
+    place = lax.broadcasted_iota(jnp.int32, (32, slots), 1)
+    columns = pl.ds(pl.multiple_of(chip * 4 * width, 4 * width), 4 * width)
+    past, fresh, new_values = [], [], []
+    for j in range(per_device):
+        blocks = [source[i, j * 16 : (j + 1) * 16].astype(jnp.float32) for i in range(2)]
+        wide = jnp.concatenate(blocks, axis=0)
         zero = jnp.zeros_like(wide)
-        both = jnp.concatenate([jnp.where(upper, wide, zero), jnp.where(upper, zero, wide)], axis=1)
-        column = pl.ds(pl.multiple_of((2 * chip + i) * 2 * width, 2 * width), 2 * width)
-        columns.append(column)
+        spread = jnp.concatenate([jnp.where(kind == c, wide, zero) for c in range(4)], axis=1)
         scores = lax.dot_general(
-            both.astype(jnp.bfloat16),
-            keys[j, :, column],
+            spread.astype(jnp.bfloat16),
+            keys[j, :, columns],
             (((1,), (1,)), ((), ())),
             preferred_element_type=jnp.float32,
         )
         past.append(jnp.where(place < lengths[j], scores * scaling, -1e30))
-        new_key = jnp.where(upper, wide[heads : heads + 1], wide[heads + 2 : heads + 3])
-        new_values.append(jnp.where(upper, wide[heads + 1 : heads + 2], wide[heads + 3 : heads + 4]))
+        new_key, new_value = [
+            jnp.concatenate(
+                [jnp.where(upper, block[heads + at : heads + at + 1], block[heads + at + 2 : heads + at + 3]) for block in blocks],
+                axis=0,
+            )
+            for at in range(2)
+        ]
+        new_values.append(new_value)
         fresh.append(wide * new_key)
     past = jnp.concatenate(past, axis=0)
     fresh = jnp.sum(jnp.concatenate(fresh, axis=0), axis=1, keepdims=True) * scaling
@@ -286,12 +292,15 @@
     inverse = 1.0 / (jnp.sum(past_exp, axis=1, keepdims=True) + fresh_exp)
     weights = (past_exp * inverse).astype(jnp.bfloat16)
     fresh_weight = (fresh_exp * inverse).astype(jnp.bfloat16).astype(jnp.float32)
-    for index, (i, j) in enumerate(work):
-        lines = slice(index * 16, (index + 1) * 16)
-        mixed = jnp.dot(weights[lines], values[j, :, columns[index]], preferred_element_type=jnp.float32)
-        mixed = jnp.where(upper, mixed[:, :width], mixed[:, width:]) + fresh_weight[lines] * new_values[index]
-        for h in range(heads):
-            target[first + i, j : j + 1, h * width : (h + 1) * width] = mixed[h : h + 1]
+    for j in range(per_device):
+        lines = slice(j * 32, (j + 1) * 32)
+        product = jnp.dot(weights[lines], values[j, :, columns], preferred_element_type=jnp.float32)
+        mixed = fresh_weight[lines] * new_values[j]
+        for c in range(4):
+            mixed = mixed + jnp.where(kind == c, product[:, c * width : (c + 1) * width], 0.0)
+        for i in range(2):
+            for h in range(heads):
+                target[first + i, j : j + 1, h * width : (h + 1) * width] = mixed[i * 16 + h : i * 16 + h + 1]
 
 
 def attend_near_kernel(per_device, heads, lengths, source, keys, values, assign, out, order):
@@ -324,28 +333,47 @@
     out[...] = rows[...].astype(jnp.bfloat16)
 
 
-def project_kernel(far, per_device, first, second, assign, resid, weight, keep, send):
+def slot_rows(far, per_device, count):
     sec, tp = lax.axis_index("sec"), lax.axis_index("tp")
-    base = sec ^ (3 * far)
     share = 2 * per_device
-    count = keep.shape[0]
-    lines = jnp.concatenate([first[...], second[...]], axis=0)
-    shape = (count, lines.shape[0])
+    shape = (count, 32)
     line = lax.broadcasted_iota(jnp.int32, shape, 1)
     place, index = (line >> 2) & 3, line & 3
-    from_sec = base ^ (line >> 4) ^ jnp.where(place > 0, 1, 0)
+    from_sec = sec ^ (3 * far) ^ (line >> 4) ^ jnp.where(place > 0, 1, 0)
     row = (tp ^ place) * share + (from_sec & 1) * per_device + index
     match = (lax.broadcasted_iota(jnp.int32, shape, 0) == row) & (index < per_device)
-    match = jnp.where(match, 1.0, 0.0).astype(jnp.bfloat16)
-    ordered = jnp.dot(match, lines, preferred_element_type=jnp.float32).astype(jnp.bfloat16)
-    total = jnp.dot(ordered, weight[...], preferred_element_type=jnp.float32)
+    return jnp.where(match, 1.0, 0.0).astype(jnp.bfloat16)
+
+
+def resid_rows(far, per_device, count, assign, resid):
+    sec, tp = lax.axis_index("sec"), lax.axis_index("tp")
+    share = 2 * per_device
     group = resid.shape[0]
-    slots = jnp.broadcast_to(group_slots(group, assign), (count, group)) - share * (base >> 1)
+    chip = (sec ^ (3 * far)) >> 1
+    slots = jnp.broadcast_to(group_slots(group, assign), (count, group)) - share * chip
     match = lax.broadcasted_iota(jnp.int32, (count, group), 0) == slots + tp * share
     match = jnp.where(match & (slots >= 0) & (slots < share), 1.0, 0.0).astype(jnp.bfloat16)
-    total = total + jnp.dot(match, resid[...], preferred_element_type=jnp.float32)
+    return jnp.dot(match, resid[...], preferred_element_type=jnp.float32)
+
+
+def project(match, first, second, resid, weight, keep, send):
+    lines = jnp.concatenate([first[...], second[...]], axis=0)
+    ordered = jnp.dot(match, lines, preferred_element_type=jnp.float32).astype(jnp.bfloat16)
+    total = resid + jnp.dot(ordered, weight[...], preferred_element_type=jnp.float32)
     keep[...] = total
     send[...] = total.astype(jnp.bfloat16)
+
+
+def project_near_kernel(per_device, first, second, assign, resid, weight, keep, send, far_match, far_resid):
+    count = keep.shape[0]
+    near = resid_rows(0, per_device, count, assign, resid)
+    project(slot_rows(0, per_device, count), first, second, near, weight, keep, send)
+    far_match[...] = slot_rows(1, per_device, count)
+    far_resid[...] = resid_rows(1, per_device, count, assign, resid)
+
+
+def project_far_kernel(first, second, match, resid, weight, keep, send):
+    project(match[...], first, second, resid[...], weight, keep, send)
 
 
 def add_kernel(mine, other, keep, send):
@@ -557,18 +585,18 @@
 
     pair = [((half, features), f32), ((half, features), bf16)]
 
-    def project(far, *lines):
-        return call(
-            functools.partial(project_kernel, far, per_device), pair, (*lines, assign, resid, out_weight), resident=(4,), nanos=0 if far else 2000
-        )
-
     def tp_sum(mine, away):
         mine, away = call(add_kernel, pair, (mine, swap(away, "tp", 1)))
         return mine, swap(away, "tp", 2)
 
-    near = project(0, own, beside)
+    *near, match, rows = call(
+        functools.partial(project_near_kernel, per_device),
+        pair + [((half, 32), bf16), ((half, features), f32)],
+        (own, beside, assign, resid, out_weight),
+        resident=(4,),
+    )
     corner = swap(after(across, near[1]), "sec", 1)
-    far = project(1, across, corner)
+    far = call(project_far_kernel, pair, (across, corner, match, rows, out_weight), resident=(4,), nanos=0)
     sums = tp_sum(*near) + tp_sum(*far)
 
     sizes = [width * sixteenths // 16 for sixteenths in (5, 5, 3, 3)]

time: 57 us -> 56.8 us (level)
  no operation moved by 1% of the time
where the time goes in v11:
time: 56.8 us; the launch traced here: 56.6 us
  starting transfers between devices  26.2 us (46%)
  waiting for transfers between devices  16.1 us (28%)
  Pallas kernels  14 us (25%)
    ppermute x28, starting transfers between devices, swap(): return lax.ppermute(value, axis, [(i, i ^ step) for i in range(total)])  26.2 us
    ppermute x28, waiting for transfers between devices, swap(): return lax.ppermute(value, axis, [(i, i ^ step) for i in range(total)])  16.1 us
    pallas_call x27, Pallas kernels, call(): pl.pallas_call(kernel, out_shape=[jax.ShapeDtypeStruct(shape, dtype) for...  14 us
  transfers between devices with their start and end apart: 28, of which 15 were waited for; matrix products, arithmetic and copies ran while one was open for 0% of the time, Pallas kernels for 18%

profile of v11, /device:TPU:0, one launch (start us, length us, event | category | flops | bytes accessed | tf_op | source)
XLA Modules:
  0.0 56.6 jit_solution(12569948370584856760)
XLA Ops:
  0.0 0.5 collective-permute-start
  0.5 0.1 collective-permute-start.1
  0.6 1.4 %shard_map.118 = (bf16[2,48,128]{2,1,0:T(8,128)(2,1)S(1)}, bf16[16,12]{1,0:T(8,128)(2,1)S(1)}) custom-call(bf16[12,1280]{1,0:T(8,128)(2,1)} %query.1, bf16[12,512]{1,0:T(8,128)(2,1)} %pairs.1, s32[1,48]{1,0:T(1,128)} %bitcast.7), custom_call_target="tpu_custom_call" | custom-call | flops 2000000000 | tf_op jit(solution)/shard_map/pallas_call | solution.py:160
  2.0 0.1 shard_map.119
  2.2 2.6 %collective-permute-start.2 = (bf16[2,48,128]{2,1,0:T(8,128)(2,1)S(1)}, bf16[2,48,128]{2,1,0:T(8,128)(2,1)S(1)}, u32[]{:S(2)}, u32[]{:S(2)}) collective-permute-start(bf16[2,48,128]{2,1,0:T(8,128)(2,1)S(1)} %get-tuple-element.51), channel_id=1, source_target_pairs={{0,12},{4,8},{8,4},{12,0},{1,13},{5,9},{9,5},{13,1},{2,14},{6,10},... | collective-permute-start | bytes 73736 | tf_op jit(solution)/shard_map/ppermute | solution.py:191
  4.8 1.5 %shard_map.120 = (f32[2,4,1280]{2,1,0:T(4,128)S(1)}, bf16[12,12]{1,0:T(8,128)(2,1)S(1)}) custom-call(s32[3]{0:T(128)S(1)} %copy-done.4, bf16[2,48,128]{2,1,0:T(8,128)(2,1)S(1)} %get-tuple-element.52.source, bf16[3,224,1024]{2,1,0:T(8,128)(2,1)S(1)} %copy-done.1, bf16[3,224,1024]{2,1,0:T(8,128)(2,1)S(1)} %copy-done.2, s32[1,48]{1,0:T(1,128)S(1)} %bitcast.8), custom_call_target="tpu_custom_call" | custom-call | flops 2000000000 | tf_op jit(solution)/shard_map/pallas_call | solution.py:160
  6.3 1.3 %shard_map.121 = (bf16[4,1280]{1,0:T(4,128)(2,1)S(1)}, bf16[4,1280]{1,0:T(4,128)(2,1)S(1)}, bf16[4,1280]{1,0:T(4,128)(2,1)S(1)}, bf16[4,1280]{1,0:T(4,128)(2,1)S(1)}) custom-call(s32[3]{0:T(128)S(1)} %copy-done.4, bf16[2,48,128]{2,1,0:T(8,128)(2,1)S(1)} %collective-permute-done.2.source, f32[2,4,1280]{2,1,0:T(4,128)S(1)} %get-tuple-element.53.near, ...), custom_call_target="tpu_custom_call" | custom-call | flops 2000000000 | tf_op jit(solution)/shard_map/pallas_call | solution.py:160
  7.6 4.2 %collective-permute-start.3 = (bf16[4,1280]{1,0:T(4,128)(2,1)S(1)}, bf16[4,1280]{1,0:T(4,128)(2,1)S(1)}, u32[]{:S(2)}, u32[]{:S(2)}) collective-permute-start(bf16[4,1280]{1,0:T(4,128)(2,1)S(1)} %get-tuple-element.54), channel_id=1, source_target_pairs={{0,7},{1,6},{2,5},{3,4},{4,3},{5,2},{6,1},{7,0},{8,15},{9,14},{10,... | collective-permute-start | bytes 30728 | tf_op jit(solution)/shard_map/ppermute | solution.py:191
  11.8 0.6 %collective-permute-start.5 = (bf16[4,1280]{1,0:T(4,128)(2,1)S(1)}, bf16[4,1280]{1,0:T(4,128)(2,1)S(1)}, u32[]{:S(2)}, u32[]{:S(2)}) collective-permute-start(bf16[4,1280]{1,0:T(4,128)(2,1)S(1)} %get-tuple-element.56), channel_id=1, source_target_pairs={{0,5},{1,4},{2,7},{3,6},{4,1},{5,0},{6,3},{7,2},{8,13},{9,12},{10,... | collective-permute-start | bytes 30728 | tf_op jit(solution)/shard_map/ppermute | solution.py:191
  12.4 0.7 %collective-permute-done.3.third = bf16[4,1280]{1,0:T(4,128)(2,1)S(1)} collective-permute-done((bf16[4,1280]{1,0:T(4,128)(2,1)S(1)}, bf16[4,1280]{1,0:T(4,128)(2,1)S(1)}, u32[]{:S(2)}, u32[]{:S(2)}) %collective-permute-start.3) | collective-permute-done | bytes 10272 | tf_op jit(solution)/shard_map/ppermute | solution.py:191
  13.2 2.6 %collective-permute-done.4.second = bf16[4,1280]{1,0:T(4,128)(2,1)S(1)} collective-permute-done((bf16[4,1280]{1,0:T(4,128)(2,1)S(1)}, bf16[4,1280]{1,0:T(4,128)(2,1)S(1)}, u32[]{:S(2)}, u32[]{:S(2)}) %collective-permute-start.4) | collective-permute-done | bytes 10272 | tf_op jit(solution)/shard_map/ppermute | solution.py:191
  15.8 0.0 slice-start.4
  15.9 0.4 collective-permute-start.6
  16.3 1.2 %collective-permute-start.9 = (bf16[16,1280]{1,0:T(8,128)(2,1)S(1)}, bf16[16,1280]{1,0:T(8,128)(2,1)S(1)}, u32[]{:S(2)}, u32[]{:S(2)}) collective-permute-start(bf16[16,1280]{1,0:T(8,128)(2,1)S(1)} %shard_map.122.first), channel_id=1, source_target_pairs={{0,12},{4,8},{8,4},{12,0},{1,13},{5,9},{9,5},{13,1},{2,14},{6,10},... | collective-permute-start | bytes 122888 | tf_op jit(solution)/shard_map/ppermute | solution.py:191
  17.5 0.8 %shard_map.123 = (f32[24,1280]{1,0:T(8,128)S(1)}, bf16[24,1280]{1,0:T(8,128)(2,1)S(1)}, bf16[24,32]{1,0:T(8,128)(2,1)S(1)}, f32[24,1280]{1,0:T(8,128)S(1)}) custom-call(bf16[16,1280]{1,0:T(8,128)(2,1)S(1)} %shard_map.122.first, bf16[16,1280]{1,0:T(8,128)(2,1)S(1)} %collective-permute-done.6.second, s32[1,48]{1,0:T(1,128)S(1)} %bitcast.9, ...), custom_call_target="tpu_custom_call" | custom-call | flops 2000000000 | tf_op jit(solution)/shard_map/pallas_call | solution.py:160
  18.3 0.1 collective-permute-start.7
  18.4 1.4 %collective-permute-done.9.value.first = bf16[16,1280]{1,0:T(8,128)(2,1)S(1)} collective-permute-done((bf16[16,1280]{1,0:T(8,128)(2,1)S(1)}, bf16[16,1280]{1,0:T(8,128)(2,1)S(1)}, u32[]{:S(2)}, u32[]{:S(2)}) %collective-permute-start.9) | collective-permute-done | bytes 40992 | tf_op jit(solution)/shard_map/ppermute | solution.py:191
  19.8 0.1 collective-permute-start.10
  20.0 1.1 %collective-permute-done.10.second = bf16[16,1280]{1,0:T(8,128)(2,1)S(1)} collective-permute-done((bf16[16,1280]{1,0:T(8,128)(2,1)S(1)}, bf16[16,1280]{1,0:T(8,128)(2,1)S(1)}, u32[]{:S(2)}, u32[]{:S(2)}) %collective-permute-start.10) | collective-permute-done | bytes 40992 | tf_op jit(solution)/shard_map/ppermute | solution.py:191
  21.0 0.7 %shard_map.126 = (f32[24,1280]{1,0:T(8,128)S(1)}, bf16[24,1280]{1,0:T(8,128)(2,1)S(1)}) custom-call(bf16[16,1280]{1,0:T(8,128)(2,1)S(1)} %collective-permute-done.9.value.first, bf16[16,1280]{1,0:T(8,128)(2,1)S(1)} %collective-permute-done.10.second, bf16[24,32]{1,0:T(8,128)(2,1)S(1)} %get-tuple-element.62.match, f32[24,1280]{1,0:T(8,128)S(1)} %get-tuple-element.63.resid, ...), custom_call_target="tpu_custom_call" | custom-call | tf_op jit(solution)/shard_map/pallas_call | solution.py:160
  21.7 0.7 %collective-permute-start.11 = (bf16[24,1280]{1,0:T(8,128)(2,1)S(1)}, bf16[24,1280]{1,0:T(8,128)(2,1)S(1)}, u32[]{:S(2)}, u32[]{:S(2)}) collective-permute-start(bf16[24,1280]{1,0:T(8,128)(2,1)S(1)} %get-tuple-element.65), channel_id=1, source_target_pairs={{0,1},{1,0},{2,3},{3,2},{4,5},{5,4},{6,7},{7,6},{8,9},{9,8},{10,11... | collective-permute-start | bytes 184328 | tf_op jit(solution)/shard_map/ppermute | solution.py:191
  22.4 0.4 collective-permute-done.7.other
  22.8 2.0 %collective-permute-start.8 = (bf16[24,1280]{1,0:T(8,128)(2,1)S(1)}, bf16[24,1280]{1,0:T(8,128)(2,1)S(1)}, u32[]{:S(2)}, u32[]{:S(2)}) collective-permute-start(bf16[24,1280]{1,0:T(8,128)(2,1)S(1)} %get-tuple-element.61), channel_id=1, source_target_pairs={{0,2},{1,3},{2,0},{3,1},{4,6},{5,7},{6,4},{7,5},{8,10},{9,11},{10,... | collective-permute-start | bytes 184328 | tf_op jit(solution)/shard_map/ppermute | solution.py:191
  24.8 1.2 %collective-permute-done.11.other = bf16[24,1280]{1,0:T(8,128)(2,1)S(1)} collective-permute-done((bf16[24,1280]{1,0:T(8,128)(2,1)S(1)}, bf16[24,1280]{1,0:T(8,128)(2,1)S(1)}, u32[]{:S(2)}, u32[]{:S(2)}) %collective-permute-start.11) | collective-permute-done | bytes 61472 | tf_op jit(solution)/shard_map/ppermute | solution.py:191
  26.0 2.2 %collective-permute-start.12 = (bf16[24,1280]{1,0:T(8,128)(2,1)S(1)}, bf16[24,1280]{1,0:T(8,128)(2,1)S(1)}, u32[]{:S(2)}, u32[]{:S(2)}) collective-permute-start(bf16[24,1280]{1,0:T(8,128)(2,1)S(1)} %get-tuple-element.67), channel_id=1, source_target_pairs={{0,2},{1,3},{2,0},{3,1},{4,6},{5,7},{6,4},{7,5},{8,10},{9,11},{10,... | collective-permute-start | bytes 184328 | tf_op jit(solution)/shard_map/ppermute | solution.py:191
  28.2 1.8 %collective-permute-done.8.near_other = bf16[24,1280]{1,0:T(8,128)(2,1)S(1)} collective-permute-done((bf16[24,1280]{1,0:T(8,128)(2,1)S(1)}, bf16[24,1280]{1,0:T(8,128)(2,1)S(1)}, u32[]{:S(2)}, u32[]{:S(2)}) %collective-permute-start.8) | collective-permute-done | bytes 61472 | tf_op jit(solution)/shard_map/ppermute | solution.py:191
  30.0 1.8 %collective-permute-done.12.far_other = bf16[24,1280]{1,0:T(8,128)(2,1)S(1)} collective-permute-done((bf16[24,1280]{1,0:T(8,128)(2,1)S(1)}, bf16[24,1280]{1,0:T(8,128)(2,1)S(1)}, u32[]{:S(2)}, u32[]{:S(2)}) %collective-permute-start.12) | collective-permute-done | bytes 61472 | tf_op jit(solution)/shard_map/ppermute | solution.py:191
  31.9 1.3 %shard_map.128 = (f32[24,2688]{1,0:T(8,128)S(1)}, bf16[24,2688]{1,0:T(8,128)(2,1)S(1)}, bf16[48,1280]{1,0:T(8,128)(2,1)S(1)}, f32[12,1280]{1,0:T(8,128)S(1)}) custom-call(f32[24,1280]{1,0:T(8,128)S(1)} %get-tuple-element.60.near, bf16[24,1280]{1,0:T(8,128)(2,1)S(1)} %collective-permute-done.8.near_other, f32[24,1280]{1,0:T(8,128)S(1)} %get-tuple-element.66.far, ...), custom_call_target="tpu_custom_call" | custom-call | flops 2000000000 | tf_op jit(solution)/shard_map/pallas_call | solution.py:160
  33.2 0.1 collective-permute-start.13
  33.3 1.3 %shard_map.130 = (f32[24,2560]{1,0:T(8,128)S(1)}, bf16[24,2560]{1,0:T(8,128)(2,1)S(1)}) custom-call(bf16[48,1280]{1,0:T(8,128)(2,1)S(1)} %get-tuple-element.72.features, bf16[1280,4096]{1,0:T(8,128)(2,1)S(1)} %bitcast.2, bf16[1280,4096]{1,0:T(8,128)(2,1)S(1)} %bitcast.4, bf16[24,2688]{1,0:T(8,128)(2,1)S(1)} %get-tuple-element.69.earlier), custom_call_target="tpu_custom_call" | custom-call | tf_op jit(solution)/shard_map/pallas_call | solution.py:160
  34.6 0.5 collective-permute-start.15
  35.1 0.2 shard_map.129
  35.4 1.2 %collective-permute-start.14 = (bf16[24,2688]{1,0:T(8,128)(2,1)S(1)}, bf16[24,2688]{1,0:T(8,128)(2,1)S(1)}, u32[]{:S(2)}, u32[]{:S(2)}) collective-permute-start(bf16[24,2688]{1,0:T(8,128)(2,1)S(1)} %get-tuple-element.71.earlier), channel_id=1, source_target_pairs={{0,12},{4,8},{8,4},{12,0},{1,13},{5,9},{9,5},{13,1},{2,14},{6,10},... | collective-permute-start | bytes 387080 | tf_op jit(solution)/shard_map/ppermute | solution.py:191
  36.6 1.1 %collective-permute-start.19 = (bf16[24,2560]{1,0:T(8,128)(2,1)S(1)}, bf16[24,2560]{1,0:T(8,128)(2,1)S(1)}, u32[]{:S(2)}, u32[]{:S(2)}) collective-permute-start(bf16[24,2560]{1,0:T(8,128)(2,1)S(1)} %get-tuple-element.75.earlier), channel_id=1, source_target_pairs={{0,12},{4,8},{8,4},{12,0},{1,13},{5,9},{9,5},{13,1},{2,14},{6,10},... | collective-permute-start | bytes 368648 | tf_op jit(solution)/shard_map/ppermute | solution.py:191
  37.8 0.8 %shard_map.132 = (f32[24,1536]{1,0:T(8,128)S(1)}, bf16[24,1536]{1,0:T(8,128)(2,1)S(1)}) custom-call(bf16[48,1280]{1,0:T(8,128)(2,1)S(1)} %get-tuple-element.72.features, bf16[1280,4096]{1,0:T(8,128)(2,1)S(1)} %bitcast.2, bf16[1280,4096]{1,0:T(8,128)(2,1)S(1)} %bitcast.4, bf16[24,2560]{1,0:T(8,128)(2,1)S(1)} %get-tuple-element.75.earlier), custom_call_target="tpu_custom_call" | custom-call | tf_op jit(solution)/shard_map/pallas_call | solution.py:160
  38.5 0.0 slice-start.6
  38.6 0.2 collective-permute-start.17
  38.8 0.8 %shard_map.133 = (f32[24,1536]{1,0:T(8,128)S(1)}, bf16[24,1536]{1,0:T(8,128)(2,1)S(1)}) custom-call(bf16[48,1280]{1,0:T(8,128)(2,1)S(1)} %get-tuple-element.72.features, bf16[1280,4096]{1,0:T(8,128)(2,1)S(1)} %bitcast.2, bf16[1280,4096]{1,0:T(8,128)(2,1)S(1)} %bitcast.4, bf16[24,1536]{1,0:T(8,128)(2,1)S(1)} %get-tuple-element.76.earlier), custom_call_target="tpu_custom_call" | custom-call | tf_op jit(solution)/shard_map/pallas_call | solution.py:160
  39.6 0.4 collective-permute-start.16
  40.0 0.8 %collective-permute-start.21 = (bf16[24,1536]{1,0:T(8,128)(2,1)S(1)}, bf16[24,1536]{1,0:T(8,128)(2,1)S(1)}, u32[]{:S(2)}, u32[]{:S(2)}) collective-permute-start(bf16[24,1536]{1,0:T(8,128)(2,1)S(1)} %get-tuple-element.80.earlier), channel_id=1, source_target_pairs={{0,12},{4,8},{8,4},{12,0},{1,13},{5,9},{9,5},{13,1},{2,14},{6,10},... | collective-permute-start | bytes 221192 | tf_op jit(solution)/shard_map/ppermute | solution.py:191
  40.8 0.1 collective-permute-done.16.other
  40.9 1.1 %collective-permute-start.23 = (bf16[24,1536]{1,0:T(8,128)(2,1)S(1)}, bf16[24,1536]{1,0:T(8,128)(2,1)S(1)}, u32[]{:S(2)}, u32[]{:S(2)}) collective-permute-start(bf16[24,1536]{1,0:T(8,128)(2,1)S(1)} %get-tuple-element.81.earlier), channel_id=1, source_target_pairs={{0,12},{4,8},{8,4},{12,0},{1,13},{5,9},{9,5},{13,1},{2,14},{6,10},... | collective-permute-start | bytes 221192 | tf_op jit(solution)/shard_map/ppermute | solution.py:191
  42.0 0.2 shard_map.136
  42.2 0.2 collective-permute-start.18
  42.5 1.1 %collective-permute-done.19.other = bf16[24,2560]{1,0:T(8,128)(2,1)S(1)} collective-permute-done((bf16[24,2560]{1,0:T(8,128)(2,1)S(1)}, bf16[24,2560]{1,0:T(8,128)(2,1)S(1)}, u32[]{:S(2)}, u32[]{:S(2)}) %collective-permute-start.19) | collective-permute-done | bytes 122912 | tf_op jit(solution)/shard_map/ppermute | solution.py:191
  43.5 0.1 shard_map.138.mine
  43.7 0.6 %collective-permute-start.20 = (bf16[24,1280]{1,0:T(8,128)(2,1)S(1)}, bf16[24,1280]{1,0:T(8,128)(2,1)S(1)}, u32[]{:S(2)}, u32[]{:S(2)}) collective-permute-start(bf16[24,1280]{1,0:T(8,128)(2,1)S(1)} %shard_map.138.mine), channel_id=1, source_target_pairs={{0,4},{4,0},{8,12},{12,8},{1,5},{5,1},{9,13},{13,9},{2,6},{6,2},{1... | collective-permute-start | bytes 184328 | tf_op jit(solution)/shard_map/ppermute | solution.py:191
  44.3 0.7 %shard_map.137.before.earlier = f32[48,1280]{1,0:T(8,128)S(1)} custom-call(bf16[24,1280]{1,0:T(8,128)(2,1)S(1)} %get-tuple-element.82.mine.earlier, bf16[24,1280]{1,0:T(8,128)(2,1)S(1)} %collective-permute-done.18.other, bf16[4096,1280]{1,0:T(8,128)(2,1)S(1)} %bitcast.6), custom_call_target="tpu_custom_call" | custom-call | flops 1000000000 | tf_op jit(solution)/shard_map/pallas_call | solution.py:160
  45.0 0.2 collective-permute-done.21.other
  45.1 0.1 shard_map.140.mine
  45.2 0.6 %collective-permute-start.22 = (bf16[24,768]{1,0:T(8,128)(2,1)S(1)}, bf16[24,768]{1,0:T(8,128)(2,1)S(1)}, u32[]{:S(2)}, u32[]{:S(2)}) collective-permute-start(bf16[24,768]{1,0:T(8,128)(2,1)S(1)} %shard_map.140.mine), channel_id=1, source_target_pairs={{0,4},{4,0},{8,12},{12,8},{1,5},{5,1},{9,13},{13,9},{2,6},{6,2},{1... | collective-permute-start | bytes 110600 | tf_op jit(solution)/shard_map/ppermute | solution.py:191
  45.8 0.7 %shard_map.139.before.earlier = f32[48,1280]{1,0:T(8,128)S(1)} custom-call(f32[48,1280]{1,0:T(8,128)S(1)} %shard_map.137.before.earlier, bf16[24,1280]{1,0:T(8,128)(2,1)S(1)} %shard_map.138.mine, bf16[24,1280]{1,0:T(8,128)(2,1)S(1)} %collective-permute-done.20.other, bf16[4096,1280]{1,0:T(8,128)(2,1)S(1)} %bitcast.6), custom_call_target="tpu_custom_call" | custom-call | flops 1000000000 | tf_op jit(solution)/shard_map/pallas_call | solution.py:160
  46.5 0.2 collective-permute-done.23.other
  46.7 0.1 shard_map.142.mine
  46.8 0.2 collective-permute-start.24
  47.0 0.5 shard_map.141.before
  47.5 0.6 %collective-permute-done.24.other = bf16[24,768]{1,0:T(8,128)(2,1)S(1)} collective-permute-done((bf16[24,768]{1,0:T(8,128)(2,1)S(1)}, bf16[24,768]{1,0:T(8,128)(2,1)S(1)}, u32[]{:S(2)}, u32[]{:S(2)}) %collective-permute-start.24) | collective-permute-done | bytes 36896 | tf_op jit(solution)/shard_map/ppermute | solution.py:191
  48.1 0.5 shard_map.143
  48.6 1.5 %collective-permute-start.25 = (bf16[12,1280]{1,0:T(8,128)(2,1)S(1)}, bf16[12,1280]{1,0:T(8,128)(2,1)S(1)}, u32[]{:S(2)}, u32[]{:S(2)}) collective-permute-start(bf16[12,1280]{1,0:T(8,128)(2,1)S(1)} %get-tuple-element.87), channel_id=1, source_target_pairs={{0,3},{1,2},{2,1},{3,0},{4,7},{5,6},{6,5},{7,4},{8,11},{9,10},{10,... | collective-permute-start | bytes 92168 | tf_op jit(solution)/shard_map/ppermute | solution.py:191
  50.1 0.1 collective-permute-start.26
  50.2 2.8 %collective-permute-start.27 = (bf16[12,1280]{1,0:T(8,128)(2,1)S(1)}, bf16[12,1280]{1,0:T(8,128)(2,1)S(1)}, u32[]{:S(2)}, u32[]{:S(2)}) collective-permute-start(bf16[12,1280]{1,0:T(8,128)(2,1)S(1)} %get-tuple-element.89), channel_id=1, source_target_pairs={{0,1},{1,0},{2,3},{3,2},{4,5},{5,4},{6,7},{7,6},{8,9},{9,8},{10,11... | collective-permute-start | bytes 92168 | tf_op jit(solution)/shard_map/ppermute | solution.py:191
  53.0 1.6 %collective-permute-done.25.third = bf16[12,1280]{1,0:T(8,128)(2,1)S(1)} collective-permute-done((bf16[12,1280]{1,0:T(8,128)(2,1)S(1)}, bf16[12,1280]{1,0:T(8,128)(2,1)S(1)}, u32[]{:S(2)}, u32[]{:S(2)}) %collective-permute-start.25) | collective-permute-done | bytes 30752 | tf_op jit(solution)/shard_map/ppermute | solution.py:191
  54.6 1.2 %collective-permute-done.26.second = bf16[12,1280]{1,0:T(8,128)(2,1)S(1)} collective-permute-done((bf16[12,1280]{1,0:T(8,128)(2,1)S(1)}, bf16[12,1280]{1,0:T(8,128)(2,1)S(1)}, u32[]{:S(2)}, u32[]{:S(2)}) %collective-permute-start.26) | collective-permute-done | bytes 30752 | tf_op jit(solution)/shard_map/ppermute | solution.py:191
  55.8 0.8 %shard_map.144 = bf16[12,1280]{1,0:T(8,128)(2,1)} custom-call(bf16[12,1280]{1,0:T(8,128)(2,1)S(1)} %collective-permute-done.25.third, bf16[12,1280]{1,0:T(8,128)(2,1)S(1)} %collective-permute-done.26.second, bf16[12,1280]{1,0:T(8,128)(2,1)S(1)} %collective-permute-done.27.first, f32[12,1280]{1,0:T(8,128)S(1)} %get-tuple-element.90.stream, ...), custom_call_target="tpu_custom_call" | custom-call | flops 2000000000 | tf_op jit(solution)/shard_map/pallas_call | solution.py:160
  (55 shorter events, 0.2 us)
Async XLA Ops:
  0.0 4.8 %copy-start.5 = (s32[48]{0:T(128)S(1)}, s32[48]{0:T(128)}, u32[]{:S(2)}) copy-start(s32[48]{0:T(128)} %param.18) | copy-start | bytes 580
  0.0 4.8 %copy-start.1 = (bf16[3,224,1024]{2,1,0:T(8,128)(2,1)S(1)}, bf16[3,224,1024]{2,1,0:T(8,128)(2,1)}, u32[]{:S(2)}) copy-start(bf16[3,224,1024]{2,1,0:T(8,128)(2,1)} %keys.3) | copy-start | bytes 4128772
  0.0 4.8 %copy-start.2 = (bf16[3,224,1024]{2,1,0:T(8,128)(2,1)S(1)}, bf16[3,224,1024]{2,1,0:T(8,128)(2,1)}, u32[]{:S(2)}) copy-start(bf16[3,224,1024]{2,1,0:T(8,128)(2,1)} %values.3) | copy-start | bytes 4128772
  0.0 4.8 %copy-start.4 = (s32[3]{0:T(128)S(1)}, s32[3]{0:T(128)}, u32[]{:S(2)}) copy-start(s32[3]{0:T(128)} %lengths.3) | copy-start | bytes 40
  0.0 2.0 %collective-permute-start = (bf16[12,1280]{1,0:T(8,128)(2,1)}, bf16[12,1280]{1,0:T(8,128)(2,1)S(1)}, u32[]{:S(2)}, u32[]{:S(2)}) collective-permute-start(bf16[12,1280]{1,0:T(8,128)(2,1)} %query.1), channel_id=1, source_target_pairs={{0,4},{4,0},{8,12},{12,8},{1,5},{5,1},{9,13},{13,9},{2,6},{6,2},{1... | collective-permute-start | bytes 92168 | tf_op jit(solution)/shard_map/ppermute | solution.py:191
  0.5 1.5 %collective-permute-start.1 = (bf16[12,512]{1,0:T(8,128)(2,1)}, bf16[12,512]{1,0:T(8,128)(2,1)S(1)}, u32[]{:S(2)}, u32[]{:S(2)}) collective-permute-start(bf16[12,512]{1,0:T(8,128)(2,1)} %pairs.1), channel_id=1, source_target_pairs={{0,4},{4,0},{8,12},{12,8},{1,5},{5,1},{9,13},{13,9},{2,6},{6,2},{1... | collective-permute-start | bytes 36872 | tf_op jit(solution)/shard_map/ppermute | solution.py:191
  2.2 4.1 %collective-permute-start.2 = (bf16[2,48,128]{2,1,0:T(8,128)(2,1)S(1)}, bf16[2,48,128]{2,1,0:T(8,128)(2,1)S(1)}, u32[]{:S(2)}, u32[]{:S(2)}) collective-permute-start(bf16[2,48,128]{2,1,0:T(8,128)(2,1)S(1)} %get-tuple-element.51), channel_id=1, source_target_pairs={{0,12},{4,8},{8,4},{12,0},{1,13},{5,9},{9,5},{13,1},{2,14},{6,10},... | collective-permute-start | bytes 73736 | tf_op jit(solution)/shard_map/ppermute | solution.py:191
  4.8 12.7 %copy-start = (bf16[1280,1280]{1,0:T(8,128)(2,1)S(1)}, bf16[1280,1280]{1,0:T(8,128)(2,1)}, u32[]{:S(2)}) copy-start(bf16[1280,1280]{1,0:T(8,128)(2,1)} %weight.7) | copy-start | bytes 9830404
  4.8 12.7 %copy-start.3 = (bf16[12,1280]{1,0:T(8,128)(2,1)S(1)}, bf16[12,1280]{1,0:T(8,128)(2,1)}, u32[]{:S(2)}) copy-start(bf16[12,1280]{1,0:T(8,128)(2,1)} %resid.1) | copy-start | bytes 92164
  7.6 5.5 %collective-permute-start.3 = (bf16[4,1280]{1,0:T(4,128)(2,1)S(1)}, bf16[4,1280]{1,0:T(4,128)(2,1)S(1)}, u32[]{:S(2)}, u32[]{:S(2)}) collective-permute-start(bf16[4,1280]{1,0:T(4,128)(2,1)S(1)} %get-tuple-element.54), channel_id=1, source_target_pairs={{0,7},{1,6},{2,5},{3,4},{4,3},{5,2},{6,1},{7,0},{8,15},{9,14},{10,... | collective-permute-start | bytes 30728 | tf_op jit(solution)/shard_map/ppermute | solution.py:191
  11.8 4.0 %collective-permute-start.4 = (bf16[4,1280]{1,0:T(4,128)(2,1)S(1)}, bf16[4,1280]{1,0:T(4,128)(2,1)S(1)}, u32[]{:S(2)}, u32[]{:S(2)}) collective-permute-start(bf16[4,1280]{1,0:T(4,128)(2,1)S(1)} %get-tuple-element.55), channel_id=1, source_target_pairs={{0,6},{1,7},{2,4},{3,5},{4,2},{5,3},{6,0},{7,1},{8,14},{9,15},{10,... | collective-permute-start | bytes 30728 | tf_op jit(solution)/shard_map/ppermute | solution.py:191
  11.8 4.0 %collective-permute-start.5 = (bf16[4,1280]{1,0:T(4,128)(2,1)S(1)}, bf16[4,1280]{1,0:T(4,128)(2,1)S(1)}, u32[]{:S(2)}, u32[]{:S(2)}) collective-permute-start(bf16[4,1280]{1,0:T(4,128)(2,1)S(1)} %get-tuple-element.56), channel_id=1, source_target_pairs={{0,5},{1,4},{2,7},{3,6},{4,1},{5,0},{6,3},{7,2},{8,13},{9,12},{10,... | collective-permute-start | bytes 30728 | tf_op jit(solution)/shard_map/ppermute | solution.py:191
  15.8 16.0 %slice-start.3 = ((s8[10485760]{0:T(1024)(128)(4,1)}), s8[4194304]{0:T(1024)(128)(4,1)S(1)}, s32[]{:S(2)}) async-start(s8[10485760]{0:T(1024)(128)(4,1)} %bitcast.3), calls=%async_computation.3 | async-start | bytes 8388608
  15.8 16.0 %slice-start.4 = ((s8[10485760]{0:T(1024)(128)(4,1)}), s8[4194304]{0:T(1024)(128)(4,1)S(1)}, s32[]{:S(2)}) async-start(s8[10485760]{0:T(1024)(128)(4,1)} %bitcast.3), calls=%async_computation.4 | async-start | bytes 8388608
  15.9 1.7 %collective-permute-start.6 = (bf16[16,1280]{1,0:T(8,128)(2,1)S(1)}, bf16[16,1280]{1,0:T(8,128)(2,1)S(1)}, u32[]{:S(2)}, u32[]{:S(2)}) collective-permute-start(bf16[16,1280]{1,0:T(8,128)(2,1)S(1)} %shard_map.122.first), channel_id=1, source_target_pairs={{0,4},{4,0},{8,12},{12,8},{1,5},{5,1},{9,13},{13,9},{2,6},{6,2},{1... | collective-permute-start | bytes 122888 | tf_op jit(solution)/shard_map/ppermute | solution.py:191
  16.3 3.5 %collective-permute-start.9 = (bf16[16,1280]{1,0:T(8,128)(2,1)S(1)}, bf16[16,1280]{1,0:T(8,128)(2,1)S(1)}, u32[]{:S(2)}, u32[]{:S(2)}) collective-permute-start(bf16[16,1280]{1,0:T(8,128)(2,1)S(1)} %shard_map.122.first), channel_id=1, source_target_pairs={{0,12},{4,8},{8,4},{12,0},{1,13},{5,9},{9,5},{13,1},{2,14},{6,10},... | collective-permute-start | bytes 122888 | tf_op jit(solution)/shard_map/ppermute | solution.py:191
  17.5 14.4 %slice-start = ((s8[10485760]{0:T(1024)(128)(4,1)}), s8[4194304]{0:T(1024)(128)(4,1)S(1)}, s32[]{:S(2)}) async-start(s8[10485760]{0:T(1024)(128)(4,1)} %bitcast.1), calls=%async_computation | async-start | bytes 8388608
  18.3 9.9 %copy-start.6 = (bf16[1280]{0:T(1024)(128)(2,1)S(1)}, bf16[1280]{0:T(1024)(128)(2,1)}, u32[]{:S(2)}) copy-start(bf16[1280]{0:T(1024)(128)(2,1)} %param.20) | copy-start | bytes 7684
  18.3 4.4 %collective-permute-start.7 = (bf16[24,1280]{1,0:T(8,128)(2,1)S(1)}, bf16[24,1280]{1,0:T(8,128)(2,1)S(1)}, u32[]{:S(2)}, u32[]{:S(2)}) collective-permute-start(bf16[24,1280]{1,0:T(8,128)(2,1)S(1)} %get-tuple-element.59.earlier), channel_id=1, source_target_pairs={{0,1},{1,0},{2,3},{3,2},{4,5},{5,4},{6,7},{7,6},{8,9},{9,8},{10,11... | collective-permute-start | bytes 184328 | tf_op jit(solution)/shard_map/ppermute | solution.py:191
  19.8 1.2 %collective-permute-start.10 = (bf16[16,1280]{1,0:T(8,128)(2,1)S(1)}, bf16[16,1280]{1,0:T(8,128)(2,1)S(1)}, u32[]{:S(2)}, u32[]{:S(2)}) collective-permute-start(bf16[16,1280]{1,0:T(8,128)(2,1)S(1)} %shard_map.125), channel_id=1, source_target_pairs={{0,4},{4,0},{8,12},{12,8},{1,5},{5,1},{9,13},{13,9},{2,6},{6,2},{1... | collective-permute-start | bytes 122888 | tf_op jit(solution)/shard_map/ppermute | solution.py:191
  21.0 10.8 %slice-start.1 = ((s8[10485760]{0:T(1024)(128)(4,1)}), s8[4194304]{0:T(1024)(128)(4,1)S(1)}, s32[]{:S(2)}) async-start(s8[10485760]{0:T(1024)(128)(4,1)} %bitcast.1), calls=%async_computation.1 | async-start | bytes 8388608
  21.7 4.3 %collective-permute-start.11 = (bf16[24,1280]{1,0:T(8,128)(2,1)S(1)}, bf16[24,1280]{1,0:T(8,128)(2,1)S(1)}, u32[]{:S(2)}, u32[]{:S(2)}) collective-permute-start(bf16[24,1280]{1,0:T(8,128)(2,1)S(1)} %get-tuple-element.65), channel_id=1, source_target_pairs={{0,1},{1,0},{2,3},{3,2},{4,5},{5,4},{6,7},{7,6},{8,9},{9,8},{10,11... | collective-permute-start | bytes 184328 | tf_op jit(solution)/shard_map/ppermute | solution.py:191
  22.8 9.1 %slice-start.2 = ((s8[10485760]{0:T(1024)(128)(4,1)}), s8[2097152]{0:T(1024)(128)(4,1)S(1)}, s32[]{:S(2)}) async-start(s8[10485760]{0:T(1024)(128)(4,1)} %bitcast.1), calls=%async_computation.2 | async-start | bytes 4194304
  22.8 9.1 %slice-start.5 = ((s8[10485760]{0:T(1024)(128)(4,1)}), s8[2097152]{0:T(1024)(128)(4,1)S(1)}, s32[]{:S(2)}) async-start(s8[10485760]{0:T(1024)(128)(4,1)} %bitcast.3), calls=%async_computation.5 | async-start | bytes 4194304
  22.8 7.2 %collective-permute-start.8 = (bf16[24,1280]{1,0:T(8,128)(2,1)S(1)}, bf16[24,1280]{1,0:T(8,128)(2,1)S(1)}, u32[]{:S(2)}, u32[]{:S(2)}) collective-permute-start(bf16[24,1280]{1,0:T(8,128)(2,1)S(1)} %get-tuple-element.61), channel_id=1, source_target_pairs={{0,2},{1,3},{2,0},{3,1},{4,6},{5,7},{6,4},{7,5},{8,10},{9,11},{10,... | collective-permute-start | bytes 184328 | tf_op jit(solution)/shard_map/ppermute | solution.py:191
  26.0 5.8 %collective-permute-start.12 = (bf16[24,1280]{1,0:T(8,128)(2,1)S(1)}, bf16[24,1280]{1,0:T(8,128)(2,1)S(1)}, u32[]{:S(2)}, u32[]{:S(2)}) collective-permute-start(bf16[24,1280]{1,0:T(8,128)(2,1)S(1)} %get-tuple-element.67), channel_id=1, source_target_pairs={{0,2},{1,3},{2,0},{3,1},{4,6},{5,7},{6,4},{7,5},{8,10},{9,11},{10,... | collective-permute-start | bytes 184328 | tf_op jit(solution)/shard_map/ppermute | solution.py:191
  33.2 1.9 %collective-permute-start.13 = (bf16[24,2688]{1,0:T(8,128)(2,1)S(1)}, bf16[24,2688]{1,0:T(8,128)(2,1)S(1)}, u32[]{:S(2)}, u32[]{:S(2)}) collective-permute-start(bf16[24,2688]{1,0:T(8,128)(2,1)S(1)} %get-tuple-element.69.earlier), channel_id=1, source_target_pairs={{0,4},{4,0},{8,12},{12,8},{1,5},{5,1},{9,13},{13,9},{2,6},{6,2},{1... | collective-permute-start | bytes 387080 | tf_op jit(solution)/shard_map/ppermute | solution.py:191
  34.6 2.0 %collective-permute-start.15 = (bf16[24,2560]{1,0:T(8,128)(2,1)S(1)}, bf16[24,2560]{1,0:T(8,128)(2,1)S(1)}, u32[]{:S(2)}, u32[]{:S(2)}) collective-permute-start(bf16[24,2560]{1,0:T(8,128)(2,1)S(1)} %get-tuple-element.74), channel_id=1, source_target_pairs={{0,4},{4,0},{8,12},{12,8},{1,5},{5,1},{9,13},{13,9},{2,6},{6,2},{1... | collective-permute-start | bytes 368648 | tf_op jit(solution)/shard_map/ppermute | solution.py:191
  35.4 6.7 %collective-permute-start.14 = (bf16[24,2688]{1,0:T(8,128)(2,1)S(1)}, bf16[24,2688]{1,0:T(8,128)(2,1)S(1)}, u32[]{:S(2)}, u32[]{:S(2)}) collective-permute-start(bf16[24,2688]{1,0:T(8,128)(2,1)S(1)} %get-tuple-element.71.earlier), channel_id=1, source_target_pairs={{0,12},{4,8},{8,4},{12,0},{1,13},{5,9},{9,5},{13,1},{2,14},{6,10},... | collective-permute-start | bytes 387080 | tf_op jit(solution)/shard_map/ppermute | solution.py:191
  36.6 6.9 %collective-permute-start.19 = (bf16[24,2560]{1,0:T(8,128)(2,1)S(1)}, bf16[24,2560]{1,0:T(8,128)(2,1)S(1)}, u32[]{:S(2)}, u32[]{:S(2)}) collective-permute-start(bf16[24,2560]{1,0:T(8,128)(2,1)S(1)} %get-tuple-element.75.earlier), channel_id=1, source_target_pairs={{0,12},{4,8},{8,4},{12,0},{1,13},{5,9},{9,5},{13,1},{2,14},{6,10},... | collective-permute-start | bytes 368648 | tf_op jit(solution)/shard_map/ppermute | solution.py:191
  38.5 5.7 %slice-start.6 = ((s8[10485760]{0:T(1024)(128)(4,1)}), s8[4194304]{0:T(1024)(128)(4,1)S(1)}, s32[]{:S(2)}) async-start(s8[10485760]{0:T(1024)(128)(4,1)} %bitcast.5), calls=%async_computation.6 | async-start | bytes 8388608
  38.6 5.7 %slice-start.7 = ((s8[10485760]{0:T(1024)(128)(4,1)}), s8[4194304]{0:T(1024)(128)(4,1)S(1)}, s32[]{:S(2)}) async-start(s8[10485760]{0:T(1024)(128)(4,1)} %bitcast.5), calls=%async_computation.7 | async-start | bytes 8388608
  38.6 5.7 %slice-start.8 = ((s8[10485760]{0:T(1024)(128)(4,1)}), s8[2097152]{0:T(1024)(128)(4,1)S(1)}, s32[]{:S(2)}) async-start(s8[10485760]{0:T(1024)(128)(4,1)} %bitcast.5), calls=%async_computation.8 | async-start | bytes 4194304
  38.6 1.4 %collective-permute-start.17 = (bf16[24,1536]{1,0:T(8,128)(2,1)S(1)}, bf16[24,1536]{1,0:T(8,128)(2,1)S(1)}, u32[]{:S(2)}, u32[]{:S(2)}) collective-permute-start(bf16[24,1536]{1,0:T(8,128)(2,1)S(1)} %get-tuple-element.76.earlier), channel_id=1, source_target_pairs={{0,4},{4,0},{8,12},{12,8},{1,5},{5,1},{9,13},{13,9},{2,6},{6,2},{1... | collective-permute-start | bytes 221192 | tf_op jit(solution)/shard_map/ppermute | solution.py:191
  39.6 1.3 %collective-permute-start.16 = (bf16[24,1536]{1,0:T(8,128)(2,1)S(1)}, bf16[24,1536]{1,0:T(8,128)(2,1)S(1)}, u32[]{:S(2)}, u32[]{:S(2)}) collective-permute-start(bf16[24,1536]{1,0:T(8,128)(2,1)S(1)} %get-tuple-element.78.earlier), channel_id=1, source_target_pairs={{0,4},{4,0},{8,12},{12,8},{1,5},{5,1},{9,13},{13,9},{2,6},{6,2},{1... | collective-permute-start | bytes 221192 | tf_op jit(solution)/shard_map/ppermute | solution.py:191
  40.0 5.1 %collective-permute-start.21 = (bf16[24,1536]{1,0:T(8,128)(2,1)S(1)}, bf16[24,1536]{1,0:T(8,128)(2,1)S(1)}, u32[]{:S(2)}, u32[]{:S(2)}) collective-permute-start(bf16[24,1536]{1,0:T(8,128)(2,1)S(1)} %get-tuple-element.80.earlier), channel_id=1, source_target_pairs={{0,12},{4,8},{8,4},{12,0},{1,13},{5,9},{9,5},{13,1},{2,14},{6,10},... | collective-permute-start | bytes 221192 | tf_op jit(solution)/shard_map/ppermute | solution.py:191
  40.9 5.8 %collective-permute-start.23 = (bf16[24,1536]{1,0:T(8,128)(2,1)S(1)}, bf16[24,1536]{1,0:T(8,128)(2,1)S(1)}, u32[]{:S(2)}, u32[]{:S(2)}) collective-permute-start(bf16[24,1536]{1,0:T(8,128)(2,1)S(1)} %get-tuple-element.81.earlier), channel_id=1, source_target_pairs={{0,12},{4,8},{8,4},{12,0},{1,13},{5,9},{9,5},{13,1},{2,14},{6,10},... | collective-permute-start | bytes 221192 | tf_op jit(solution)/shard_map/ppermute | solution.py:191
  42.2 2.0 %collective-permute-start.18 = (bf16[24,1280]{1,0:T(8,128)(2,1)S(1)}, bf16[24,1280]{1,0:T(8,128)(2,1)S(1)}, u32[]{:S(2)}, u32[]{:S(2)}) collective-permute-start(bf16[24,1280]{1,0:T(8,128)(2,1)S(1)} %get-tuple-element.82.mine.earlier), channel_id=1, source_target_pairs={{0,4},{4,0},{8,12},{12,8},{1,5},{5,1},{9,13},{13,9},{2,6},{6,2},{1... | collective-permute-start | bytes 184328 | tf_op jit(solution)/shard_map/ppermute | solution.py:191
  43.7 2.1 %collective-permute-start.20 = (bf16[24,1280]{1,0:T(8,128)(2,1)S(1)}, bf16[24,1280]{1,0:T(8,128)(2,1)S(1)}, u32[]{:S(2)}, u32[]{:S(2)}) collective-permute-start(bf16[24,1280]{1,0:T(8,128)(2,1)S(1)} %shard_map.138.mine), channel_id=1, source_target_pairs={{0,4},{4,0},{8,12},{12,8},{1,5},{5,1},{9,13},{13,9},{2,6},{6,2},{1... | collective-permute-start | bytes 184328 | tf_op jit(solution)/shard_map/ppermute | solution.py:191
  45.2 1.8 %collective-permute-start.22 = (bf16[24,768]{1,0:T(8,128)(2,1)S(1)}, bf16[24,768]{1,0:T(8,128)(2,1)S(1)}, u32[]{:S(2)}, u32[]{:S(2)}) collective-permute-start(bf16[24,768]{1,0:T(8,128)(2,1)S(1)} %shard_map.140.mine), channel_id=1, source_target_pairs={{0,4},{4,0},{8,12},{12,8},{1,5},{5,1},{9,13},{13,9},{2,6},{6,2},{1... | collective-permute-start | bytes 110600 | tf_op jit(solution)/shard_map/ppermute | solution.py:191
  46.8 1.3 %collective-permute-start.24 = (bf16[24,768]{1,0:T(8,128)(2,1)S(1)}, bf16[24,768]{1,0:T(8,128)(2,1)S(1)}, u32[]{:S(2)}, u32[]{:S(2)}) collective-permute-start(bf16[24,768]{1,0:T(8,128)(2,1)S(1)} %shard_map.142.mine), channel_id=1, source_target_pairs={{0,4},{4,0},{8,12},{12,8},{1,5},{5,1},{9,13},{13,9},{2,6},{6,2},{1... | collective-permute-start | bytes 110600 | tf_op jit(solution)/shard_map/ppermute | solution.py:191
  48.6 6.0 %collective-permute-start.25 = (bf16[12,1280]{1,0:T(8,128)(2,1)S(1)}, bf16[12,1280]{1,0:T(8,128)(2,1)S(1)}, u32[]{:S(2)}, u32[]{:S(2)}) collective-permute-start(bf16[12,1280]{1,0:T(8,128)(2,1)S(1)} %get-tuple-element.87), channel_id=1, source_target_pairs={{0,3},{1,2},{2,1},{3,0},{4,7},{5,6},{6,5},{7,4},{8,11},{9,10},{10,... | collective-permute-start | bytes 92168 | tf_op jit(solution)/shard_map/ppermute | solution.py:191
  50.1 5.7 %collective-permute-start.26 = (bf16[12,1280]{1,0:T(8,128)(2,1)S(1)}, bf16[12,1280]{1,0:T(8,128)(2,1)S(1)}, u32[]{:S(2)}, u32[]{:S(2)}) collective-permute-start(bf16[12,1280]{1,0:T(8,128)(2,1)S(1)} %get-tuple-element.88), channel_id=1, source_target_pairs={{0,2},{1,3},{2,0},{3,1},{4,6},{5,7},{6,4},{7,5},{8,10},{9,11},{10,... | collective-permute-start | bytes 92168 | tf_op jit(solution)/shard_map/ppermute | solution.py:191
  50.2 5.6 %collective-permute-start.27 = (bf16[12,1280]{1,0:T(8,128)(2,1)S(1)}, bf16[12,1280]{1,0:T(8,128)(2,1)S(1)}, u32[]{:S(2)}, u32[]{:S(2)}) collective-permute-start(bf16[12,1280]{1,0:T(8,128)(2,1)S(1)} %get-tuple-element.89), channel_id=1, source_target_pairs={{0,1},{1,0},{2,3},{3,2},{4,5},{5,4},{6,7},{7,6},{8,9},{9,8},{10,11... | collective-permute-start | bytes 92168 | tf_op jit(solution)/shard_map/ppermute | solution.py:191

commit v12 on v10

--- a/solution.py
+++ b/solution.py
@@ -295,11 +295,13 @@
 
 
 def attend_near_kernel(per_device, heads, lengths, source, keys, values, assign, out, order):
-    shape = order.shape
-    slots = jnp.broadcast_to(group_slots(shape[0], assign), shape)
-    line = lax.broadcasted_iota(jnp.int32, shape, 0)
+    group = order.shape[0]
+    slots = jnp.broadcast_to(group_slots(group, assign), (group, group))
+    line = lax.broadcasted_iota(jnp.int32, (group, group), 0)
     match = jnp.where(line == slots, 1.0, 0.0).astype(jnp.bfloat16)
-    same = jnp.where(line == lax.broadcasted_iota(jnp.int32, shape, 1), 1.0, 0.0).astype(jnp.bfloat16)
+    line = lax.broadcasted_iota(jnp.int32, order.shape, 0)
+    same = line == (lax.broadcasted_iota(jnp.int32, order.shape, 1) & 15)
+    same = jnp.where(same, 1.0, 0.0).astype(jnp.bfloat16)
     order[...] = lax.dot_general(
         match, same, (((0,), (0,)), ((), ())), preferred_element_type=jnp.float32
     ).astype(jnp.bfloat16)
@@ -324,28 +326,47 @@
     out[...] = rows[...].astype(jnp.bfloat16)
 
 
-def project_kernel(far, per_device, first, second, assign, resid, weight, keep, send):
+def slot_rows(far, per_device, count):
     sec, tp = lax.axis_index("sec"), lax.axis_index("tp")
-    base = sec ^ (3 * far)
     share = 2 * per_device
-    count = keep.shape[0]
-    lines = jnp.concatenate([first[...], second[...]], axis=0)
-    shape = (count, lines.shape[0])
+    shape = (count, 32)
     line = lax.broadcasted_iota(jnp.int32, shape, 1)
     place, index = (line >> 2) & 3, line & 3
-    from_sec = base ^ (line >> 4) ^ jnp.where(place > 0, 1, 0)
+    from_sec = sec ^ (3 * far) ^ (line >> 4) ^ jnp.where(place > 0, 1, 0)
     row = (tp ^ place) * share + (from_sec & 1) * per_device + index
     match = (lax.broadcasted_iota(jnp.int32, shape, 0) == row) & (index < per_device)
-    match = jnp.where(match, 1.0, 0.0).astype(jnp.bfloat16)
-    ordered = jnp.dot(match, lines, preferred_element_type=jnp.float32).astype(jnp.bfloat16)
-    total = jnp.dot(ordered, weight[...], preferred_element_type=jnp.float32)
+    return jnp.where(match, 1.0, 0.0).astype(jnp.bfloat16)
+
+
+def resid_rows(far, per_device, count, assign, resid):
+    sec, tp = lax.axis_index("sec"), lax.axis_index("tp")
+    share = 2 * per_device
     group = resid.shape[0]
-    slots = jnp.broadcast_to(group_slots(group, assign), (count, group)) - share * (base >> 1)
+    chip = (sec ^ (3 * far)) >> 1
+    slots = jnp.broadcast_to(group_slots(group, assign), (count, group)) - share * chip
     match = lax.broadcasted_iota(jnp.int32, (count, group), 0) == slots + tp * share
     match = jnp.where(match & (slots >= 0) & (slots < share), 1.0, 0.0).astype(jnp.bfloat16)
-    total = total + jnp.dot(match, resid[...], preferred_element_type=jnp.float32)
+    return jnp.dot(match, resid[...], preferred_element_type=jnp.float32)
+
+
+def project(match, first, second, resid, weight, keep, send):
+    lines = jnp.concatenate([first[...], second[...]], axis=0)
+    ordered = jnp.dot(match, lines, preferred_element_type=jnp.float32).astype(jnp.bfloat16)
+    total = resid + jnp.dot(ordered, weight[...], preferred_element_type=jnp.float32)
     keep[...] = total
     send[...] = total.astype(jnp.bfloat16)
+
+
+def project_near_kernel(per_device, first, second, assign, resid, weight, keep, send, far_match, far_resid):
+    count = keep.shape[0]
+    near = resid_rows(0, per_device, count, assign, resid)
+    project(slot_rows(0, per_device, count), first, second, near, weight, keep, send)
+    far_match[...] = slot_rows(1, per_device, count)
+    far_resid[...] = resid_rows(1, per_device, count, assign, resid)
+
+
+def project_far_kernel(first, second, match, resid, weight, keep, send):
+    project(match[...], first, second, resid[...], weight, keep, send)
 
 
 def add_kernel(mine, other, keep, send):
@@ -474,17 +495,23 @@
     to_groups(jnp.where(swapped, upper, lower), jnp.where(swapped, lower, upper), groups)
     keep[...] = groups[tp, 0:group]
     for step, target in enumerate((first, second, third)):
-        target[...] = groups[tp ^ (step + 1), 0:group].astype(jnp.bfloat16)
-
-
-def finish_kernel(third, second, first, stream, mine, order, out):
+        part = groups[tp ^ (step + 1), 0:group]
+        columns = target.shape[1]
+        target[...] = jnp.concatenate([part[:, :columns], part[:, columns:]], axis=0).astype(jnp.bfloat16)
+
+
+def finish_kernel(third, second, first, stream, mine, order, out, terms):
     total = stream[...] + mine[...]
+    group = out.shape[0]
     for other in (first, second, third):
-        total = total + other[...].astype(jnp.float32)
-    coarse = total.astype(jnp.bfloat16)
-    fine = (total - coarse.astype(jnp.float32)).astype(jnp.bfloat16)
-    ordered = [jnp.dot(order[...], term, preferred_element_type=jnp.float32) for term in (coarse, fine)]
-    out[...] = (ordered[0] + ordered[1]).astype(jnp.bfloat16)
+        halves = other[...].astype(jnp.float32)
+        total = total + jnp.concatenate([halves[:group], halves[group:]], axis=1)
+    coarse = total.astype(jnp.bfloat16).astype(jnp.float32)
+    terms[...] = jnp.zeros_like(terms)
+    terms[0:group] = coarse
+    terms[16 : 16 + group] = total - coarse
+    ordered = jnp.dot(order[...], terms[...].astype(jnp.bfloat16), preferred_element_type=jnp.float32)
+    out[...] = ordered.astype(jnp.bfloat16)
 
 
 def local_pairs(
@@ -536,7 +563,7 @@
     caches = (key_cache, cached_value_rows)
     near, order = call(
         functools.partial(attend_near_kernel, per_device, heads),
-        [((2, 4, head_block), f32), ((group, group), bf16)],
+        [((2, 4, head_block), f32), ((group, 32), bf16)],
         (cache_len, mine, *caches, assign),
         smem=(0,),
         resident=(2, 3),
@@ -557,18 +584,18 @@
 
     pair = [((half, features), f32), ((half, features), bf16)]
 
-    def project(far, *lines):
-        return call(
-            functools.partial(project_kernel, far, per_device), pair, (*lines, assign, resid, out_weight), resident=(4,), nanos=0 if far else 2000
-        )
-
     def tp_sum(mine, away):
         mine, away = call(add_kernel, pair, (mine, swap(away, "tp", 1)))
         return mine, swap(away, "tp", 2)
 
-    near = project(0, own, beside)
+    *near, match, rows = call(
+        functools.partial(project_near_kernel, per_device),
+        pair + [((half, 32), bf16), ((half, features), f32)],
+        (own, beside, assign, resid, out_weight),
+        resident=(4,),
+    )
     corner = swap(after(across, near[1]), "sec", 1)
-    far = project(1, across, corner)
+    far = call(project_far_kernel, pair, (across, corner, match, rows, out_weight), resident=(4,), nanos=0)
     sums = tp_sum(*near) + tp_sum(*far)
 
     sizes = [width * sixteenths // 16 for sixteenths in (5, 5, 3, 3)]
@@ -648,13 +675,18 @@
         else:
             mine, *parts = call(
                 functools.partial(down_last_kernel, starts[index]),
-                [((group, features), f32)] + [((group, features), bf16)] * 3,
+                [((group, features), f32)] + [((half, features // 2), bf16)] * 3,
                 (before, hidden, beside, down_weight),
                 [pltpu.VMEM((4, 16, features), f32)],
                 resident=(3,),
             )
     parts = [swap(parts[step - 1], "tp", step) for step in (3, 2, 1)]
-    (out,) = call(finish_kernel, [((group, features), bf16)], (*parts, stream, mine, order))
+    (out,) = call(
+        finish_kernel,
+        [((group, features), bf16)],
+        (*parts, stream, mine, order),
+        [pltpu.VMEM((32, features), f32)],
+    )
     return out
 
 

time: 57 us -> 56.1 us (0.984)
  no operation moved by 1% of the time
where the time goes in v12:
time: 56.1 us; the launch traced here: 55.9 us
  starting transfers between devices  26 us (46%)
  waiting for transfers between devices  15.7 us (28%)
  Pallas kernels  13.8 us (25%)
    ppermute x28, starting transfers between devices, swap(): return lax.ppermute(value, axis, [(i, i ^ step) for i in range(total)])  26 us
    ppermute x28, waiting for transfers between devices, swap(): return lax.ppermute(value, axis, [(i, i ^ step) for i in range(total)])  15.7 us
    pallas_call x27, Pallas kernels, call(): pl.pallas_call(kernel, out_shape=[jax.ShapeDtypeStruct(shape, dtype) for...  13.8 us
  transfers between devices with their start and end apart: 28, of which 15 were waited for; matrix products, arithmetic and copies ran while one was open for 0% of the time, Pallas kernels for 18%

profile of v12, /device:TPU:0, one launch (start us, length us, event | category | flops | bytes accessed | tf_op | source)
XLA Modules:
  0.0 55.9 jit_solution(7055584555803761687)
XLA Ops:
  0.0 0.5 collective-permute-start
  0.5 0.1 collective-permute-start.1
  0.6 1.4 %shard_map.118 = (bf16[2,48,128]{2,1,0:T(8,128)(2,1)S(1)}, bf16[16,12]{1,0:T(8,128)(2,1)S(1)}) custom-call(bf16[12,1280]{1,0:T(8,128)(2,1)} %query.1, bf16[12,512]{1,0:T(8,128)(2,1)} %pairs.1, s32[1,48]{1,0:T(1,128)} %bitcast.7), custom_call_target="tpu_custom_call" | custom-call | flops 2000000000 | tf_op jit(solution)/shard_map/pallas_call | solution.py:160
  2.0 0.1 shard_map.119
  2.2 2.6 %collective-permute-start.2 = (bf16[2,48,128]{2,1,0:T(8,128)(2,1)S(1)}, bf16[2,48,128]{2,1,0:T(8,128)(2,1)S(1)}, u32[]{:S(2)}, u32[]{:S(2)}) collective-permute-start(bf16[2,48,128]{2,1,0:T(8,128)(2,1)S(1)} %get-tuple-element.51), channel_id=1, source_target_pairs={{0,12},{4,8},{8,4},{12,0},{1,13},{5,9},{9,5},{13,1},{2,14},{6,10},... | collective-permute-start | bytes 73736 | tf_op jit(solution)/shard_map/ppermute | solution.py:191
  4.8 1.5 %shard_map.120 = (f32[2,4,1280]{2,1,0:T(4,128)S(1)}, bf16[12,32]{1,0:T(8,128)(2,1)S(1)}) custom-call(s32[3]{0:T(128)S(1)} %copy-done.4, bf16[2,48,128]{2,1,0:T(8,128)(2,1)S(1)} %get-tuple-element.52.source, bf16[3,224,1024]{2,1,0:T(8,128)(2,1)S(1)} %copy-done.1, bf16[3,224,1024]{2,1,0:T(8,128)(2,1)S(1)} %copy-done.2, s32[1,48]{1,0:T(1,128)S(1)} %bitcast.8), custom_call_target="tpu_custom_call" | custom-call | flops 2000000000 | tf_op jit(solution)/shard_map/pallas_call | solution.py:160
  6.3 0.0 collective-permute-done.2.source
  6.3 1.2 %shard_map.121 = (bf16[4,1280]{1,0:T(4,128)(2,1)S(1)}, bf16[4,1280]{1,0:T(4,128)(2,1)S(1)}, bf16[4,1280]{1,0:T(4,128)(2,1)S(1)}, bf16[4,1280]{1,0:T(4,128)(2,1)S(1)}) custom-call(s32[3]{0:T(128)S(1)} %copy-done.4, bf16[2,48,128]{2,1,0:T(8,128)(2,1)S(1)} %collective-permute-done.2.source, f32[2,4,1280]{2,1,0:T(4,128)S(1)} %get-tuple-element.53.near, ...), custom_call_target="tpu_custom_call" | custom-call | flops 2000000000 | tf_op jit(solution)/shard_map/pallas_call | solution.py:160
  7.4 4.2 %collective-permute-start.3 = (bf16[4,1280]{1,0:T(4,128)(2,1)S(1)}, bf16[4,1280]{1,0:T(4,128)(2,1)S(1)}, u32[]{:S(2)}, u32[]{:S(2)}) collective-permute-start(bf16[4,1280]{1,0:T(4,128)(2,1)S(1)} %get-tuple-element.54), channel_id=1, source_target_pairs={{0,7},{1,6},{2,5},{3,4},{4,3},{5,2},{6,1},{7,0},{8,15},{9,14},{10,... | collective-permute-start | bytes 30728 | tf_op jit(solution)/shard_map/ppermute | solution.py:191
  11.6 0.7 %collective-permute-start.5 = (bf16[4,1280]{1,0:T(4,128)(2,1)S(1)}, bf16[4,1280]{1,0:T(4,128)(2,1)S(1)}, u32[]{:S(2)}, u32[]{:S(2)}) collective-permute-start(bf16[4,1280]{1,0:T(4,128)(2,1)S(1)} %get-tuple-element.56), channel_id=1, source_target_pairs={{0,5},{1,4},{2,7},{3,6},{4,1},{5,0},{6,3},{7,2},{8,13},{9,12},{10,... | collective-permute-start | bytes 30728 | tf_op jit(solution)/shard_map/ppermute | solution.py:191
  12.3 0.7 %collective-permute-done.3.third = bf16[4,1280]{1,0:T(4,128)(2,1)S(1)} collective-permute-done((bf16[4,1280]{1,0:T(4,128)(2,1)S(1)}, bf16[4,1280]{1,0:T(4,128)(2,1)S(1)}, u32[]{:S(2)}, u32[]{:S(2)}) %collective-permute-start.3) | collective-permute-done | bytes 10272 | tf_op jit(solution)/shard_map/ppermute | solution.py:191
  13.0 2.6 %collective-permute-done.4.second = bf16[4,1280]{1,0:T(4,128)(2,1)S(1)} collective-permute-done((bf16[4,1280]{1,0:T(4,128)(2,1)S(1)}, bf16[4,1280]{1,0:T(4,128)(2,1)S(1)}, u32[]{:S(2)}, u32[]{:S(2)}) %collective-permute-start.4) | collective-permute-done | bytes 10272 | tf_op jit(solution)/shard_map/ppermute | solution.py:191
  15.7 0.5 collective-permute-start.6
  16.2 1.2 %collective-permute-start.9 = (bf16[16,1280]{1,0:T(8,128)(2,1)S(1)}, bf16[16,1280]{1,0:T(8,128)(2,1)S(1)}, u32[]{:S(2)}, u32[]{:S(2)}) collective-permute-start(bf16[16,1280]{1,0:T(8,128)(2,1)S(1)} %shard_map.122.first), channel_id=1, source_target_pairs={{0,12},{4,8},{8,4},{12,0},{1,13},{5,9},{9,5},{13,1},{2,14},{6,10},... | collective-permute-start | bytes 122888 | tf_op jit(solution)/shard_map/ppermute | solution.py:191
  17.4 0.8 %shard_map.123 = (f32[24,1280]{1,0:T(8,128)S(1)}, bf16[24,1280]{1,0:T(8,128)(2,1)S(1)}, bf16[24,32]{1,0:T(8,128)(2,1)S(1)}, f32[24,1280]{1,0:T(8,128)S(1)}) custom-call(bf16[16,1280]{1,0:T(8,128)(2,1)S(1)} %shard_map.122.first, bf16[16,1280]{1,0:T(8,128)(2,1)S(1)} %collective-permute-done.6.second, s32[1,48]{1,0:T(1,128)S(1)} %bitcast.9, ...), custom_call_target="tpu_custom_call" | custom-call | flops 2000000000 | tf_op jit(solution)/shard_map/pallas_call | solution.py:160
  18.2 0.1 collective-permute-start.7
  18.3 1.5 %collective-permute-done.9.value.first = bf16[16,1280]{1,0:T(8,128)(2,1)S(1)} collective-permute-done((bf16[16,1280]{1,0:T(8,128)(2,1)S(1)}, bf16[16,1280]{1,0:T(8,128)(2,1)S(1)}, u32[]{:S(2)}, u32[]{:S(2)}) %collective-permute-start.9) | collective-permute-done | bytes 40992 | tf_op jit(solution)/shard_map/ppermute | solution.py:191
  19.8 0.1 collective-permute-start.10
  19.9 1.1 %collective-permute-done.10.second = bf16[16,1280]{1,0:T(8,128)(2,1)S(1)} collective-permute-done((bf16[16,1280]{1,0:T(8,128)(2,1)S(1)}, bf16[16,1280]{1,0:T(8,128)(2,1)S(1)}, u32[]{:S(2)}, u32[]{:S(2)}) %collective-permute-start.10) | collective-permute-done | bytes 40992 | tf_op jit(solution)/shard_map/ppermute | solution.py:191
  21.0 0.7 %shard_map.126 = (f32[24,1280]{1,0:T(8,128)S(1)}, bf16[24,1280]{1,0:T(8,128)(2,1)S(1)}) custom-call(bf16[16,1280]{1,0:T(8,128)(2,1)S(1)} %collective-permute-done.9.value.first, bf16[16,1280]{1,0:T(8,128)(2,1)S(1)} %collective-permute-done.10.second, bf16[24,32]{1,0:T(8,128)(2,1)S(1)} %get-tuple-element.62.match, f32[24,1280]{1,0:T(8,128)S(1)} %get-tuple-element.63.resid, ...), custom_call_target="tpu_custom_call" | custom-call | tf_op jit(solution)/shard_map/pallas_call | solution.py:160
  21.7 0.6 %collective-permute-start.11 = (bf16[24,1280]{1,0:T(8,128)(2,1)S(1)}, bf16[24,1280]{1,0:T(8,128)(2,1)S(1)}, u32[]{:S(2)}, u32[]{:S(2)}) collective-permute-start(bf16[24,1280]{1,0:T(8,128)(2,1)S(1)} %get-tuple-element.65), channel_id=1, source_target_pairs={{0,1},{1,0},{2,3},{3,2},{4,5},{5,4},{6,7},{7,6},{8,9},{9,8},{10,11... | collective-permute-start | bytes 184328 | tf_op jit(solution)/shard_map/ppermute | solution.py:191
  22.2 0.4 collective-permute-done.7.other
  22.6 2.0 %collective-permute-start.8 = (bf16[24,1280]{1,0:T(8,128)(2,1)S(1)}, bf16[24,1280]{1,0:T(8,128)(2,1)S(1)}, u32[]{:S(2)}, u32[]{:S(2)}) collective-permute-start(bf16[24,1280]{1,0:T(8,128)(2,1)S(1)} %get-tuple-element.61), channel_id=1, source_target_pairs={{0,2},{1,3},{2,0},{3,1},{4,6},{5,7},{6,4},{7,5},{8,10},{9,11},{10,... | collective-permute-start | bytes 184328 | tf_op jit(solution)/shard_map/ppermute | solution.py:191
  24.6 1.3 %collective-permute-done.11.other = bf16[24,1280]{1,0:T(8,128)(2,1)S(1)} collective-permute-done((bf16[24,1280]{1,0:T(8,128)(2,1)S(1)}, bf16[24,1280]{1,0:T(8,128)(2,1)S(1)}, u32[]{:S(2)}, u32[]{:S(2)}) %collective-permute-start.11) | collective-permute-done | bytes 61472 | tf_op jit(solution)/shard_map/ppermute | solution.py:191
  26.0 2.1 %collective-permute-start.12 = (bf16[24,1280]{1,0:T(8,128)(2,1)S(1)}, bf16[24,1280]{1,0:T(8,128)(2,1)S(1)}, u32[]{:S(2)}, u32[]{:S(2)}) collective-permute-start(bf16[24,1280]{1,0:T(8,128)(2,1)S(1)} %get-tuple-element.67), channel_id=1, source_target_pairs={{0,2},{1,3},{2,0},{3,1},{4,6},{5,7},{6,4},{7,5},{8,10},{9,11},{10,... | collective-permute-start | bytes 184328 | tf_op jit(solution)/shard_map/ppermute | solution.py:191
  28.1 1.9 %collective-permute-done.8.near_other = bf16[24,1280]{1,0:T(8,128)(2,1)S(1)} collective-permute-done((bf16[24,1280]{1,0:T(8,128)(2,1)S(1)}, bf16[24,1280]{1,0:T(8,128)(2,1)S(1)}, u32[]{:S(2)}, u32[]{:S(2)}) %collective-permute-start.8) | collective-permute-done | bytes 61472 | tf_op jit(solution)/shard_map/ppermute | solution.py:191
  29.9 1.8 %collective-permute-done.12.far_other = bf16[24,1280]{1,0:T(8,128)(2,1)S(1)} collective-permute-done((bf16[24,1280]{1,0:T(8,128)(2,1)S(1)}, bf16[24,1280]{1,0:T(8,128)(2,1)S(1)}, u32[]{:S(2)}, u32[]{:S(2)}) %collective-permute-start.12) | collective-permute-done | bytes 61472 | tf_op jit(solution)/shard_map/ppermute | solution.py:191
  31.8 1.3 %shard_map.128 = (f32[24,2688]{1,0:T(8,128)S(1)}, bf16[24,2688]{1,0:T(8,128)(2,1)S(1)}, bf16[48,1280]{1,0:T(8,128)(2,1)S(1)}, f32[12,1280]{1,0:T(8,128)S(1)}) custom-call(f32[24,1280]{1,0:T(8,128)S(1)} %get-tuple-element.60.near, bf16[24,1280]{1,0:T(8,128)(2,1)S(1)} %collective-permute-done.8.near_other, f32[24,1280]{1,0:T(8,128)S(1)} %get-tuple-element.66.far, ...), custom_call_target="tpu_custom_call" | custom-call | flops 2000000000 | tf_op jit(solution)/shard_map/pallas_call | solution.py:160
  33.1 0.1 collective-permute-start.13
  33.2 1.3 %shard_map.130 = (f32[24,2560]{1,0:T(8,128)S(1)}, bf16[24,2560]{1,0:T(8,128)(2,1)S(1)}) custom-call(bf16[48,1280]{1,0:T(8,128)(2,1)S(1)} %get-tuple-element.72.features, bf16[1280,4096]{1,0:T(8,128)(2,1)S(1)} %bitcast.2, bf16[1280,4096]{1,0:T(8,128)(2,1)S(1)} %bitcast.4, bf16[24,2688]{1,0:T(8,128)(2,1)S(1)} %get-tuple-element.69.earlier), custom_call_target="tpu_custom_call" | custom-call | tf_op jit(solution)/shard_map/pallas_call | solution.py:160
  34.5 0.5 collective-permute-start.15
  35.0 0.2 shard_map.129
  35.3 1.2 %collective-permute-start.14 = (bf16[24,2688]{1,0:T(8,128)(2,1)S(1)}, bf16[24,2688]{1,0:T(8,128)(2,1)S(1)}, u32[]{:S(2)}, u32[]{:S(2)}) collective-permute-start(bf16[24,2688]{1,0:T(8,128)(2,1)S(1)} %get-tuple-element.71.earlier), channel_id=1, source_target_pairs={{0,12},{4,8},{8,4},{12,0},{1,13},{5,9},{9,5},{13,1},{2,14},{6,10},... | collective-permute-start | bytes 387080 | tf_op jit(solution)/shard_map/ppermute | solution.py:191
  36.5 1.1 %collective-permute-start.19 = (bf16[24,2560]{1,0:T(8,128)(2,1)S(1)}, bf16[24,2560]{1,0:T(8,128)(2,1)S(1)}, u32[]{:S(2)}, u32[]{:S(2)}) collective-permute-start(bf16[24,2560]{1,0:T(8,128)(2,1)S(1)} %get-tuple-element.75.earlier), channel_id=1, source_target_pairs={{0,12},{4,8},{8,4},{12,0},{1,13},{5,9},{9,5},{13,1},{2,14},{6,10},... | collective-permute-start | bytes 368648 | tf_op jit(solution)/shard_map/ppermute | solution.py:191
  37.6 0.8 %shard_map.132 = (f32[24,1536]{1,0:T(8,128)S(1)}, bf16[24,1536]{1,0:T(8,128)(2,1)S(1)}) custom-call(bf16[48,1280]{1,0:T(8,128)(2,1)S(1)} %get-tuple-element.72.features, bf16[1280,4096]{1,0:T(8,128)(2,1)S(1)} %bitcast.2, bf16[1280,4096]{1,0:T(8,128)(2,1)S(1)} %bitcast.4, bf16[24,2560]{1,0:T(8,128)(2,1)S(1)} %get-tuple-element.75.earlier), custom_call_target="tpu_custom_call" | custom-call | tf_op jit(solution)/shard_map/pallas_call | solution.py:160
  38.4 0.2 collective-permute-start.17
  38.7 0.8 %shard_map.133 = (f32[24,1536]{1,0:T(8,128)S(1)}, bf16[24,1536]{1,0:T(8,128)(2,1)S(1)}) custom-call(bf16[48,1280]{1,0:T(8,128)(2,1)S(1)} %get-tuple-element.72.features, bf16[1280,4096]{1,0:T(8,128)(2,1)S(1)} %bitcast.2, bf16[1280,4096]{1,0:T(8,128)(2,1)S(1)} %bitcast.4, bf16[24,1536]{1,0:T(8,128)(2,1)S(1)} %get-tuple-element.76.earlier), custom_call_target="tpu_custom_call" | custom-call | tf_op jit(solution)/shard_map/pallas_call | solution.py:160
  39.5 0.4 collective-permute-start.16
  39.9 0.8 %collective-permute-start.21 = (bf16[24,1536]{1,0:T(8,128)(2,1)S(1)}, bf16[24,1536]{1,0:T(8,128)(2,1)S(1)}, u32[]{:S(2)}, u32[]{:S(2)}) collective-permute-start(bf16[24,1536]{1,0:T(8,128)(2,1)S(1)} %get-tuple-element.80.earlier), channel_id=1, source_target_pairs={{0,12},{4,8},{8,4},{12,0},{1,13},{5,9},{9,5},{13,1},{2,14},{6,10},... | collective-permute-start | bytes 221192 | tf_op jit(solution)/shard_map/ppermute | solution.py:191
  40.7 0.1 collective-permute-done.16.other
  40.8 1.1 %collective-permute-start.23 = (bf16[24,1536]{1,0:T(8,128)(2,1)S(1)}, bf16[24,1536]{1,0:T(8,128)(2,1)S(1)}, u32[]{:S(2)}, u32[]{:S(2)}) collective-permute-start(bf16[24,1536]{1,0:T(8,128)(2,1)S(1)} %get-tuple-element.81.earlier), channel_id=1, source_target_pairs={{0,12},{4,8},{8,4},{12,0},{1,13},{5,9},{9,5},{13,1},{2,14},{6,10},... | collective-permute-start | bytes 221192 | tf_op jit(solution)/shard_map/ppermute | solution.py:191
  41.9 0.2 shard_map.136
  42.1 0.2 collective-permute-start.18
  42.3 1.1 %collective-permute-done.19.other = bf16[24,2560]{1,0:T(8,128)(2,1)S(1)} collective-permute-done((bf16[24,2560]{1,0:T(8,128)(2,1)S(1)}, bf16[24,2560]{1,0:T(8,128)(2,1)S(1)}, u32[]{:S(2)}, u32[]{:S(2)}) %collective-permute-start.19) | collective-permute-done | bytes 122912 | tf_op jit(solution)/shard_map/ppermute | solution.py:191
  43.4 0.1 shard_map.138.mine
  43.6 0.6 %collective-permute-start.20 = (bf16[24,1280]{1,0:T(8,128)(2,1)S(1)}, bf16[24,1280]{1,0:T(8,128)(2,1)S(1)}, u32[]{:S(2)}, u32[]{:S(2)}) collective-permute-start(bf16[24,1280]{1,0:T(8,128)(2,1)S(1)} %shard_map.138.mine), channel_id=1, source_target_pairs={{0,4},{4,0},{8,12},{12,8},{1,5},{5,1},{9,13},{13,9},{2,6},{6,2},{1... | collective-permute-start | bytes 184328 | tf_op jit(solution)/shard_map/ppermute | solution.py:191
  44.2 0.7 %shard_map.137.before.earlier = f32[48,1280]{1,0:T(8,128)S(1)} custom-call(bf16[24,1280]{1,0:T(8,128)(2,1)S(1)} %get-tuple-element.82.mine.earlier, bf16[24,1280]{1,0:T(8,128)(2,1)S(1)} %collective-permute-done.18.other, bf16[4096,1280]{1,0:T(8,128)(2,1)S(1)} %bitcast.6), custom_call_target="tpu_custom_call" | custom-call | flops 1000000000 | tf_op jit(solution)/shard_map/pallas_call | solution.py:160
  44.9 0.2 collective-permute-done.21.other
  45.0 0.1 shard_map.140.mine
  45.1 0.6 %collective-permute-start.22 = (bf16[24,768]{1,0:T(8,128)(2,1)S(1)}, bf16[24,768]{1,0:T(8,128)(2,1)S(1)}, u32[]{:S(2)}, u32[]{:S(2)}) collective-permute-start(bf16[24,768]{1,0:T(8,128)(2,1)S(1)} %shard_map.140.mine), channel_id=1, source_target_pairs={{0,4},{4,0},{8,12},{12,8},{1,5},{5,1},{9,13},{13,9},{2,6},{6,2},{1... | collective-permute-start | bytes 110600 | tf_op jit(solution)/shard_map/ppermute | solution.py:191
  45.7 0.7 %shard_map.139.before.earlier = f32[48,1280]{1,0:T(8,128)S(1)} custom-call(f32[48,1280]{1,0:T(8,128)S(1)} %shard_map.137.before.earlier, bf16[24,1280]{1,0:T(8,128)(2,1)S(1)} %shard_map.138.mine, bf16[24,1280]{1,0:T(8,128)(2,1)S(1)} %collective-permute-done.20.other, bf16[4096,1280]{1,0:T(8,128)(2,1)S(1)} %bitcast.6), custom_call_target="tpu_custom_call" | custom-call | flops 1000000000 | tf_op jit(solution)/shard_map/pallas_call | solution.py:160
  46.4 0.2 collective-permute-done.23.other
  46.6 0.1 shard_map.142.mine
  46.7 0.2 collective-permute-start.24
  46.9 0.5 shard_map.141.before
  47.4 0.6 %collective-permute-done.24.other = bf16[24,768]{1,0:T(8,128)(2,1)S(1)} collective-permute-done((bf16[24,768]{1,0:T(8,128)(2,1)S(1)}, bf16[24,768]{1,0:T(8,128)(2,1)S(1)}, u32[]{:S(2)}, u32[]{:S(2)}) %collective-permute-start.24) | collective-permute-done | bytes 36896 | tf_op jit(solution)/shard_map/ppermute | solution.py:191
  48.0 0.5 shard_map.143
  48.5 1.5 %collective-permute-start.25 = (bf16[24,640]{1,0:T(8,128)(2,1)S(1)}, bf16[24,640]{1,0:T(8,128)(2,1)S(1)}, u32[]{:S(2)}, u32[]{:S(2)}) collective-permute-start(bf16[24,640]{1,0:T(8,128)(2,1)S(1)} %get-tuple-element.87), channel_id=1, source_target_pairs={{0,3},{1,2},{2,1},{3,0},{4,7},{5,6},{6,5},{7,4},{8,11},{9,10},{10,... | collective-permute-start | bytes 92168 | tf_op jit(solution)/shard_map/ppermute | solution.py:191
  50.0 0.1 collective-permute-start.26
  50.1 2.9 %collective-permute-start.27 = (bf16[24,640]{1,0:T(8,128)(2,1)S(1)}, bf16[24,640]{1,0:T(8,128)(2,1)S(1)}, u32[]{:S(2)}, u32[]{:S(2)}) collective-permute-start(bf16[24,640]{1,0:T(8,128)(2,1)S(1)} %get-tuple-element.89), channel_id=1, source_target_pairs={{0,1},{1,0},{2,3},{3,2},{4,5},{5,4},{6,7},{7,6},{8,9},{9,8},{10,11... | collective-permute-start | bytes 92168 | tf_op jit(solution)/shard_map/ppermute | solution.py:191
  52.9 1.3 %collective-permute-done.25.third = bf16[24,640]{1,0:T(8,128)(2,1)S(1)} collective-permute-done((bf16[24,640]{1,0:T(8,128)(2,1)S(1)}, bf16[24,640]{1,0:T(8,128)(2,1)S(1)}, u32[]{:S(2)}, u32[]{:S(2)}) %collective-permute-start.25) | collective-permute-done | bytes 30752 | tf_op jit(solution)/shard_map/ppermute | solution.py:191
  54.3 0.8 %collective-permute-done.26.second = bf16[24,640]{1,0:T(8,128)(2,1)S(1)} collective-permute-done((bf16[24,640]{1,0:T(8,128)(2,1)S(1)}, bf16[24,640]{1,0:T(8,128)(2,1)S(1)}, u32[]{:S(2)}, u32[]{:S(2)}) %collective-permute-start.26) | collective-permute-done | bytes 30752 | tf_op jit(solution)/shard_map/ppermute | solution.py:191
  55.1 0.0 collective-permute-done.27.first
  55.1 0.8 %shard_map.144 = bf16[12,1280]{1,0:T(8,128)(2,1)} custom-call(bf16[24,640]{1,0:T(8,128)(2,1)S(1)} %collective-permute-done.25.third, bf16[24,640]{1,0:T(8,128)(2,1)S(1)} %collective-permute-done.26.second, bf16[24,640]{1,0:T(8,128)(2,1)S(1)} %collective-permute-done.27.first, f32[12,1280]{1,0:T(8,128)S(1)} %get-tuple-element.90.stream, ...), custom_call_target="tpu_custom_call" | custom-call | flops 2000000000 | tf_op jit(solution)/shard_map/pallas_call | solution.py:160
  (55 shorter events, 0.3 us)
Async XLA Ops:
  0.0 4.8 %copy-start.5 = (s32[48]{0:T(128)S(1)}, s32[48]{0:T(128)}, u32[]{:S(2)}) copy-start(s32[48]{0:T(128)} %param.18) | copy-start | bytes 580
  0.0 4.8 %copy-start.1 = (bf16[3,224,1024]{2,1,0:T(8,128)(2,1)S(1)}, bf16[3,224,1024]{2,1,0:T(8,128)(2,1)}, u32[]{:S(2)}) copy-start(bf16[3,224,1024]{2,1,0:T(8,128)(2,1)} %keys.3) | copy-start | bytes 4128772
  0.0 4.8 %copy-start.2 = (bf16[3,224,1024]{2,1,0:T(8,128)(2,1)S(1)}, bf16[3,224,1024]{2,1,0:T(8,128)(2,1)}, u32[]{:S(2)}) copy-start(bf16[3,224,1024]{2,1,0:T(8,128)(2,1)} %values.3) | copy-start | bytes 4128772
  0.0 4.8 %copy-start.4 = (s32[3]{0:T(128)S(1)}, s32[3]{0:T(128)}, u32[]{:S(2)}) copy-start(s32[3]{0:T(128)} %lengths.3) | copy-start | bytes 40
  0.0 2.0 %collective-permute-start = (bf16[12,1280]{1,0:T(8,128)(2,1)}, bf16[12,1280]{1,0:T(8,128)(2,1)S(1)}, u32[]{:S(2)}, u32[]{:S(2)}) collective-permute-start(bf16[12,1280]{1,0:T(8,128)(2,1)} %query.1), channel_id=1, source_target_pairs={{0,4},{4,0},{8,12},{12,8},{1,5},{5,1},{9,13},{13,9},{2,6},{6,2},{1... | collective-permute-start | bytes 92168 | tf_op jit(solution)/shard_map/ppermute | solution.py:191
  0.5 1.5 %collective-permute-start.1 = (bf16[12,512]{1,0:T(8,128)(2,1)}, bf16[12,512]{1,0:T(8,128)(2,1)S(1)}, u32[]{:S(2)}, u32[]{:S(2)}) collective-permute-start(bf16[12,512]{1,0:T(8,128)(2,1)} %pairs.1), channel_id=1, source_target_pairs={{0,4},{4,0},{8,12},{12,8},{1,5},{5,1},{9,13},{13,9},{2,6},{6,2},{1... | collective-permute-start | bytes 36872 | tf_op jit(solution)/shard_map/ppermute | solution.py:191
  2.2 4.1 %collective-permute-start.2 = (bf16[2,48,128]{2,1,0:T(8,128)(2,1)S(1)}, bf16[2,48,128]{2,1,0:T(8,128)(2,1)S(1)}, u32[]{:S(2)}, u32[]{:S(2)}) collective-permute-start(bf16[2,48,128]{2,1,0:T(8,128)(2,1)S(1)} %get-tuple-element.51), channel_id=1, source_target_pairs={{0,12},{4,8},{8,4},{12,0},{1,13},{5,9},{9,5},{13,1},{2,14},{6,10},... | collective-permute-start | bytes 73736 | tf_op jit(solution)/shard_map/ppermute | solution.py:191
  4.8 12.6 %copy-start = (bf16[1280,1280]{1,0:T(8,128)(2,1)S(1)}, bf16[1280,1280]{1,0:T(8,128)(2,1)}, u32[]{:S(2)}) copy-start(bf16[1280,1280]{1,0:T(8,128)(2,1)} %weight.7) | copy-start | bytes 9830404
  4.8 12.6 %copy-start.3 = (bf16[12,1280]{1,0:T(8,128)(2,1)S(1)}, bf16[12,1280]{1,0:T(8,128)(2,1)}, u32[]{:S(2)}) copy-start(bf16[12,1280]{1,0:T(8,128)(2,1)} %resid.1) | copy-start | bytes 92164
  7.4 5.6 %collective-permute-start.3 = (bf16[4,1280]{1,0:T(4,128)(2,1)S(1)}, bf16[4,1280]{1,0:T(4,128)(2,1)S(1)}, u32[]{:S(2)}, u32[]{:S(2)}) collective-permute-start(bf16[4,1280]{1,0:T(4,128)(2,1)S(1)} %get-tuple-element.54), channel_id=1, source_target_pairs={{0,7},{1,6},{2,5},{3,4},{4,3},{5,2},{6,1},{7,0},{8,15},{9,14},{10,... | collective-permute-start | bytes 30728 | tf_op jit(solution)/shard_map/ppermute | solution.py:191
  11.6 4.0 %collective-permute-start.4 = (bf16[4,1280]{1,0:T(4,128)(2,1)S(1)}, bf16[4,1280]{1,0:T(4,128)(2,1)S(1)}, u32[]{:S(2)}, u32[]{:S(2)}) collective-permute-start(bf16[4,1280]{1,0:T(4,128)(2,1)S(1)} %get-tuple-element.55), channel_id=1, source_target_pairs={{0,6},{1,7},{2,4},{3,5},{4,2},{5,3},{6,0},{7,1},{8,14},{9,15},{10,... | collective-permute-start | bytes 30728 | tf_op jit(solution)/shard_map/ppermute | solution.py:191
  11.6 4.0 %collective-permute-start.5 = (bf16[4,1280]{1,0:T(4,128)(2,1)S(1)}, bf16[4,1280]{1,0:T(4,128)(2,1)S(1)}, u32[]{:S(2)}, u32[]{:S(2)}) collective-permute-start(bf16[4,1280]{1,0:T(4,128)(2,1)S(1)} %get-tuple-element.56), channel_id=1, source_target_pairs={{0,5},{1,4},{2,7},{3,6},{4,1},{5,0},{6,3},{7,2},{8,13},{9,12},{10,... | collective-permute-start | bytes 30728 | tf_op jit(solution)/shard_map/ppermute | solution.py:191
  15.6 16.1 %slice-start.3 = ((s8[10485760]{0:T(1024)(128)(4,1)}), s8[4194304]{0:T(1024)(128)(4,1)S(1)}, s32[]{:S(2)}) async-start(s8[10485760]{0:T(1024)(128)(4,1)} %bitcast.3), calls=%async_computation.3 | async-start | bytes 8388608
  15.7 16.1 %slice-start.4 = ((s8[10485760]{0:T(1024)(128)(4,1)}), s8[4194304]{0:T(1024)(128)(4,1)S(1)}, s32[]{:S(2)}) async-start(s8[10485760]{0:T(1024)(128)(4,1)} %bitcast.3), calls=%async_computation.4 | async-start | bytes 8388608
  15.7 1.7 %collective-permute-start.6 = (bf16[16,1280]{1,0:T(8,128)(2,1)S(1)}, bf16[16,1280]{1,0:T(8,128)(2,1)S(1)}, u32[]{:S(2)}, u32[]{:S(2)}) collective-permute-start(bf16[16,1280]{1,0:T(8,128)(2,1)S(1)} %shard_map.122.first), channel_id=1, source_target_pairs={{0,4},{4,0},{8,12},{12,8},{1,5},{5,1},{9,13},{13,9},{2,6},{6,2},{1... | collective-permute-start | bytes 122888 | tf_op jit(solution)/shard_map/ppermute | solution.py:191
  16.2 3.6 %collective-permute-start.9 = (bf16[16,1280]{1,0:T(8,128)(2,1)S(1)}, bf16[16,1280]{1,0:T(8,128)(2,1)S(1)}, u32[]{:S(2)}, u32[]{:S(2)}) collective-permute-start(bf16[16,1280]{1,0:T(8,128)(2,1)S(1)} %shard_map.122.first), channel_id=1, source_target_pairs={{0,12},{4,8},{8,4},{12,0},{1,13},{5,9},{9,5},{13,1},{2,14},{6,10},... | collective-permute-start | bytes 122888 | tf_op jit(solution)/shard_map/ppermute | solution.py:191
  17.4 14.4 %slice-start = ((s8[10485760]{0:T(1024)(128)(4,1)}), s8[4194304]{0:T(1024)(128)(4,1)S(1)}, s32[]{:S(2)}) async-start(s8[10485760]{0:T(1024)(128)(4,1)} %bitcast.1), calls=%async_computation | async-start | bytes 8388608
  18.2 9.9 %copy-start.6 = (bf16[1280]{0:T(1024)(128)(2,1)S(1)}, bf16[1280]{0:T(1024)(128)(2,1)}, u32[]{:S(2)}) copy-start(bf16[1280]{0:T(1024)(128)(2,1)} %param.20) | copy-start | bytes 7684
  18.2 4.4 %collective-permute-start.7 = (bf16[24,1280]{1,0:T(8,128)(2,1)S(1)}, bf16[24,1280]{1,0:T(8,128)(2,1)S(1)}, u32[]{:S(2)}, u32[]{:S(2)}) collective-permute-start(bf16[24,1280]{1,0:T(8,128)(2,1)S(1)} %get-tuple-element.59.earlier), channel_id=1, source_target_pairs={{0,1},{1,0},{2,3},{3,2},{4,5},{5,4},{6,7},{7,6},{8,9},{9,8},{10,11... | collective-permute-start | bytes 184328 | tf_op jit(solution)/shard_map/ppermute | solution.py:191
  19.8 1.2 %collective-permute-start.10 = (bf16[16,1280]{1,0:T(8,128)(2,1)S(1)}, bf16[16,1280]{1,0:T(8,128)(2,1)S(1)}, u32[]{:S(2)}, u32[]{:S(2)}) collective-permute-start(bf16[16,1280]{1,0:T(8,128)(2,1)S(1)} %shard_map.125), channel_id=1, source_target_pairs={{0,4},{4,0},{8,12},{12,8},{1,5},{5,1},{9,13},{13,9},{2,6},{6,2},{1... | collective-permute-start | bytes 122888 | tf_op jit(solution)/shard_map/ppermute | solution.py:191
  21.0 10.8 %slice-start.1 = ((s8[10485760]{0:T(1024)(128)(4,1)}), s8[4194304]{0:T(1024)(128)(4,1)S(1)}, s32[]{:S(2)}) async-start(s8[10485760]{0:T(1024)(128)(4,1)} %bitcast.1), calls=%async_computation.1 | async-start | bytes 8388608
  21.7 4.3 %collective-permute-start.11 = (bf16[24,1280]{1,0:T(8,128)(2,1)S(1)}, bf16[24,1280]{1,0:T(8,128)(2,1)S(1)}, u32[]{:S(2)}, u32[]{:S(2)}) collective-permute-start(bf16[24,1280]{1,0:T(8,128)(2,1)S(1)} %get-tuple-element.65), channel_id=1, source_target_pairs={{0,1},{1,0},{2,3},{3,2},{4,5},{5,4},{6,7},{7,6},{8,9},{9,8},{10,11... | collective-permute-start | bytes 184328 | tf_op jit(solution)/shard_map/ppermute | solution.py:191
  22.6 9.2 %slice-start.2 = ((s8[10485760]{0:T(1024)(128)(4,1)}), s8[2097152]{0:T(1024)(128)(4,1)S(1)}, s32[]{:S(2)}) async-start(s8[10485760]{0:T(1024)(128)(4,1)} %bitcast.1), calls=%async_computation.2 | async-start | bytes 4194304
  22.6 9.2 %slice-start.5 = ((s8[10485760]{0:T(1024)(128)(4,1)}), s8[2097152]{0:T(1024)(128)(4,1)S(1)}, s32[]{:S(2)}) async-start(s8[10485760]{0:T(1024)(128)(4,1)} %bitcast.3), calls=%async_computation.5 | async-start | bytes 4194304
  22.6 7.3 %collective-permute-start.8 = (bf16[24,1280]{1,0:T(8,128)(2,1)S(1)}, bf16[24,1280]{1,0:T(8,128)(2,1)S(1)}, u32[]{:S(2)}, u32[]{:S(2)}) collective-permute-start(bf16[24,1280]{1,0:T(8,128)(2,1)S(1)} %get-tuple-element.61), channel_id=1, source_target_pairs={{0,2},{1,3},{2,0},{3,1},{4,6},{5,7},{6,4},{7,5},{8,10},{9,11},{10,... | collective-permute-start | bytes 184328 | tf_op jit(solution)/shard_map/ppermute | solution.py:191
  26.0 5.8 %collective-permute-start.12 = (bf16[24,1280]{1,0:T(8,128)(2,1)S(1)}, bf16[24,1280]{1,0:T(8,128)(2,1)S(1)}, u32[]{:S(2)}, u32[]{:S(2)}) collective-permute-start(bf16[24,1280]{1,0:T(8,128)(2,1)S(1)} %get-tuple-element.67), channel_id=1, source_target_pairs={{0,2},{1,3},{2,0},{3,1},{4,6},{5,7},{6,4},{7,5},{8,10},{9,11},{10,... | collective-permute-start | bytes 184328 | tf_op jit(solution)/shard_map/ppermute | solution.py:191
  33.1 1.9 %collective-permute-start.13 = (bf16[24,2688]{1,0:T(8,128)(2,1)S(1)}, bf16[24,2688]{1,0:T(8,128)(2,1)S(1)}, u32[]{:S(2)}, u32[]{:S(2)}) collective-permute-start(bf16[24,2688]{1,0:T(8,128)(2,1)S(1)} %get-tuple-element.69.earlier), channel_id=1, source_target_pairs={{0,4},{4,0},{8,12},{12,8},{1,5},{5,1},{9,13},{13,9},{2,6},{6,2},{1... | collective-permute-start | bytes 387080 | tf_op jit(solution)/shard_map/ppermute | solution.py:191
  34.5 2.0 %collective-permute-start.15 = (bf16[24,2560]{1,0:T(8,128)(2,1)S(1)}, bf16[24,2560]{1,0:T(8,128)(2,1)S(1)}, u32[]{:S(2)}, u32[]{:S(2)}) collective-permute-start(bf16[24,2560]{1,0:T(8,128)(2,1)S(1)} %get-tuple-element.74), channel_id=1, source_target_pairs={{0,4},{4,0},{8,12},{12,8},{1,5},{5,1},{9,13},{13,9},{2,6},{6,2},{1... | collective-permute-start | bytes 368648 | tf_op jit(solution)/shard_map/ppermute | solution.py:191
  35.3 6.6 %collective-permute-start.14 = (bf16[24,2688]{1,0:T(8,128)(2,1)S(1)}, bf16[24,2688]{1,0:T(8,128)(2,1)S(1)}, u32[]{:S(2)}, u32[]{:S(2)}) collective-permute-start(bf16[24,2688]{1,0:T(8,128)(2,1)S(1)} %get-tuple-element.71.earlier), channel_id=1, source_target_pairs={{0,12},{4,8},{8,4},{12,0},{1,13},{5,9},{9,5},{13,1},{2,14},{6,10},... | collective-permute-start | bytes 387080 | tf_op jit(solution)/shard_map/ppermute | solution.py:191
  36.5 7.0 %collective-permute-start.19 = (bf16[24,2560]{1,0:T(8,128)(2,1)S(1)}, bf16[24,2560]{1,0:T(8,128)(2,1)S(1)}, u32[]{:S(2)}, u32[]{:S(2)}) collective-permute-start(bf16[24,2560]{1,0:T(8,128)(2,1)S(1)} %get-tuple-element.75.earlier), channel_id=1, source_target_pairs={{0,12},{4,8},{8,4},{12,0},{1,13},{5,9},{9,5},{13,1},{2,14},{6,10},... | collective-permute-start | bytes 368648 | tf_op jit(solution)/shard_map/ppermute | solution.py:191
  38.4 5.8 %slice-start.6 = ((s8[10485760]{0:T(1024)(128)(4,1)}), s8[4194304]{0:T(1024)(128)(4,1)S(1)}, s32[]{:S(2)}) async-start(s8[10485760]{0:T(1024)(128)(4,1)} %bitcast.5), calls=%async_computation.6 | async-start | bytes 8388608
  38.4 5.7 %slice-start.7 = ((s8[10485760]{0:T(1024)(128)(4,1)}), s8[4194304]{0:T(1024)(128)(4,1)S(1)}, s32[]{:S(2)}) async-start(s8[10485760]{0:T(1024)(128)(4,1)} %bitcast.5), calls=%async_computation.7 | async-start | bytes 8388608
  38.4 5.7 %slice-start.8 = ((s8[10485760]{0:T(1024)(128)(4,1)}), s8[2097152]{0:T(1024)(128)(4,1)S(1)}, s32[]{:S(2)}) async-start(s8[10485760]{0:T(1024)(128)(4,1)} %bitcast.5), calls=%async_computation.8 | async-start | bytes 4194304
  38.4 1.4 %collective-permute-start.17 = (bf16[24,1536]{1,0:T(8,128)(2,1)S(1)}, bf16[24,1536]{1,0:T(8,128)(2,1)S(1)}, u32[]{:S(2)}, u32[]{:S(2)}) collective-permute-start(bf16[24,1536]{1,0:T(8,128)(2,1)S(1)} %get-tuple-element.76.earlier), channel_id=1, source_target_pairs={{0,4},{4,0},{8,12},{12,8},{1,5},{5,1},{9,13},{13,9},{2,6},{6,2},{1... | collective-permute-start | bytes 221192 | tf_op jit(solution)/shard_map/ppermute | solution.py:191
  39.5 1.3 %collective-permute-start.16 = (bf16[24,1536]{1,0:T(8,128)(2,1)S(1)}, bf16[24,1536]{1,0:T(8,128)(2,1)S(1)}, u32[]{:S(2)}, u32[]{:S(2)}) collective-permute-start(bf16[24,1536]{1,0:T(8,128)(2,1)S(1)} %get-tuple-element.78.earlier), channel_id=1, source_target_pairs={{0,4},{4,0},{8,12},{12,8},{1,5},{5,1},{9,13},{13,9},{2,6},{6,2},{1... | collective-permute-start | bytes 221192 | tf_op jit(solution)/shard_map/ppermute | solution.py:191
  39.9 5.1 %collective-permute-start.21 = (bf16[24,1536]{1,0:T(8,128)(2,1)S(1)}, bf16[24,1536]{1,0:T(8,128)(2,1)S(1)}, u32[]{:S(2)}, u32[]{:S(2)}) collective-permute-start(bf16[24,1536]{1,0:T(8,128)(2,1)S(1)} %get-tuple-element.80.earlier), channel_id=1, source_target_pairs={{0,12},{4,8},{8,4},{12,0},{1,13},{5,9},{9,5},{13,1},{2,14},{6,10},... | collective-permute-start | bytes 221192 | tf_op jit(solution)/shard_map/ppermute | solution.py:191
  40.8 5.8 %collective-permute-start.23 = (bf16[24,1536]{1,0:T(8,128)(2,1)S(1)}, bf16[24,1536]{1,0:T(8,128)(2,1)S(1)}, u32[]{:S(2)}, u32[]{:S(2)}) collective-permute-start(bf16[24,1536]{1,0:T(8,128)(2,1)S(1)} %get-tuple-element.81.earlier), channel_id=1, source_target_pairs={{0,12},{4,8},{8,4},{12,0},{1,13},{5,9},{9,5},{13,1},{2,14},{6,10},... | collective-permute-start | bytes 221192 | tf_op jit(solution)/shard_map/ppermute | solution.py:191
  42.1 2.1 %collective-permute-start.18 = (bf16[24,1280]{1,0:T(8,128)(2,1)S(1)}, bf16[24,1280]{1,0:T(8,128)(2,1)S(1)}, u32[]{:S(2)}, u32[]{:S(2)}) collective-permute-start(bf16[24,1280]{1,0:T(8,128)(2,1)S(1)} %get-tuple-element.82.mine.earlier), channel_id=1, source_target_pairs={{0,4},{4,0},{8,12},{12,8},{1,5},{5,1},{9,13},{13,9},{2,6},{6,2},{1... | collective-permute-start | bytes 184328 | tf_op jit(solution)/shard_map/ppermute | solution.py:191
  43.6 2.1 %collective-permute-start.20 = (bf16[24,1280]{1,0:T(8,128)(2,1)S(1)}, bf16[24,1280]{1,0:T(8,128)(2,1)S(1)}, u32[]{:S(2)}, u32[]{:S(2)}) collective-permute-start(bf16[24,1280]{1,0:T(8,128)(2,1)S(1)} %shard_map.138.mine), channel_id=1, source_target_pairs={{0,4},{4,0},{8,12},{12,8},{1,5},{5,1},{9,13},{13,9},{2,6},{6,2},{1... | collective-permute-start | bytes 184328 | tf_op jit(solution)/shard_map/ppermute | solution.py:191
  45.1 1.8 %collective-permute-start.22 = (bf16[24,768]{1,0:T(8,128)(2,1)S(1)}, bf16[24,768]{1,0:T(8,128)(2,1)S(1)}, u32[]{:S(2)}, u32[]{:S(2)}) collective-permute-start(bf16[24,768]{1,0:T(8,128)(2,1)S(1)} %shard_map.140.mine), channel_id=1, source_target_pairs={{0,4},{4,0},{8,12},{12,8},{1,5},{5,1},{9,13},{13,9},{2,6},{6,2},{1... | collective-permute-start | bytes 110600 | tf_op jit(solution)/shard_map/ppermute | solution.py:191
  46.7 1.3 %collective-permute-start.24 = (bf16[24,768]{1,0:T(8,128)(2,1)S(1)}, bf16[24,768]{1,0:T(8,128)(2,1)S(1)}, u32[]{:S(2)}, u32[]{:S(2)}) collective-permute-start(bf16[24,768]{1,0:T(8,128)(2,1)S(1)} %shard_map.142.mine), channel_id=1, source_target_pairs={{0,4},{4,0},{8,12},{12,8},{1,5},{5,1},{9,13},{13,9},{2,6},{6,2},{1... | collective-permute-start | bytes 110600 | tf_op jit(solution)/shard_map/ppermute | solution.py:191
  48.5 5.8 %collective-permute-start.25 = (bf16[24,640]{1,0:T(8,128)(2,1)S(1)}, bf16[24,640]{1,0:T(8,128)(2,1)S(1)}, u32[]{:S(2)}, u32[]{:S(2)}) collective-permute-start(bf16[24,640]{1,0:T(8,128)(2,1)S(1)} %get-tuple-element.87), channel_id=1, source_target_pairs={{0,3},{1,2},{2,1},{3,0},{4,7},{5,6},{6,5},{7,4},{8,11},{9,10},{10,... | collective-permute-start | bytes 92168 | tf_op jit(solution)/shard_map/ppermute | solution.py:191
  50.0 5.1 %collective-permute-start.26 = (bf16[24,640]{1,0:T(8,128)(2,1)S(1)}, bf16[24,640]{1,0:T(8,128)(2,1)S(1)}, u32[]{:S(2)}, u32[]{:S(2)}) collective-permute-start(bf16[24,640]{1,0:T(8,128)(2,1)S(1)} %get-tuple-element.88), channel_id=1, source_target_pairs={{0,2},{1,3},{2,0},{3,1},{4,6},{5,7},{6,4},{7,5},{8,10},{9,11},{10,... | collective-permute-start | bytes 92168 | tf_op jit(solution)/shard_map/ppermute | solution.py:191
  50.1 5.0 %collective-permute-start.27 = (bf16[24,640]{1,0:T(8,128)(2,1)S(1)}, bf16[24,640]{1,0:T(8,128)(2,1)S(1)}, u32[]{:S(2)}, u32[]{:S(2)}) collective-permute-start(bf16[24,640]{1,0:T(8,128)(2,1)S(1)} %get-tuple-element.89), channel_id=1, source_target_pairs={{0,1},{1,0},{2,3},{3,2},{4,5},{5,4},{6,7},{7,6},{8,9},{9,8},{10,11... | collective-permute-start | bytes 92168 | tf_op jit(solution)/shard_map/ppermute | solution.py:191

commit v13 on v12

--- a/solution.py
+++ b/solution.py
@@ -295,16 +295,22 @@
 
 
 def attend_near_kernel(per_device, heads, lengths, source, keys, values, assign, out, order):
-    group = order.shape[0]
+    group = order.shape[0] // 2
     slots = jnp.broadcast_to(group_slots(group, assign), (group, group))
     line = lax.broadcasted_iota(jnp.int32, (group, group), 0)
     match = jnp.where(line == slots, 1.0, 0.0).astype(jnp.bfloat16)
-    line = lax.broadcasted_iota(jnp.int32, order.shape, 0)
-    same = line == (lax.broadcasted_iota(jnp.int32, order.shape, 1) & 15)
-    same = jnp.where(same, 1.0, 0.0).astype(jnp.bfloat16)
-    order[...] = lax.dot_general(
-        match, same, (((0,), (0,)), ((), ())), preferred_element_type=jnp.float32
-    ).astype(jnp.bfloat16)
+    shape = (group, order.shape[1])
+    column = lax.broadcasted_iota(jnp.int32, shape, 1) & 31
+    column = jnp.where(column < group, column, jnp.where(column < 2 * group, column - group, group))
+    same = jnp.where(lax.broadcasted_iota(jnp.int32, shape, 0) == column, 1.0, 0.0).astype(jnp.bfloat16)
+    ordered = lax.dot_general(match, same, (((0,), (0,)), ((), ())), preferred_element_type=jnp.float32)
+    line = lax.broadcasted_iota(jnp.int32, (2 * group, group), 0)
+    line = jnp.where(line < group, line, line - group)
+    twice = jnp.where(line == lax.broadcasted_iota(jnp.int32, (2 * group, group), 1), 1.0, 0.0).astype(jnp.bfloat16)
+    ordered = jnp.dot(twice, ordered.astype(jnp.bfloat16), preferred_element_type=jnp.float32)
+    lower = lax.broadcasted_iota(jnp.int32, order.shape, 0) < group
+    first = (lax.broadcasted_iota(jnp.int32, order.shape, 1) & 31) < group
+    order[...] = jnp.where(lower == first, ordered, 0.0).astype(jnp.bfloat16)
     out[...] = jnp.zeros_like(out)
     attend_blocks(per_device, heads, lengths, lax.axis_index("sec") >> 1, source, keys, values, out, 0)
 
@@ -477,8 +483,14 @@
     return jnp.dot(lines.astype(jnp.bfloat16), rows, preferred_element_type=jnp.float32)
 
 
-def down_first_kernel(mine, other, weight, out):
+def column_halves(rows):
+    columns = rows.shape[1] // 2
+    return jnp.concatenate([rows[:, :columns], rows[:, columns:]], axis=0)
+
+
+def down_first_kernel(mine, other, weight, stream, out, stream_halves):
     out[...] = down_product(0, mine, other, weight)
+    stream_halves[...] = column_halves(stream[...])
 
 
 def down_more_kernel(unit, before, mine, other, weight, out):
@@ -488,30 +500,28 @@
 def down_last_kernel(unit, before, mine, other, weight, keep, first, second, third, groups):
     tp = lax.axis_index("tp")
     product = before[...] + down_product(unit, mine, other, weight)
-    group = keep.shape[0]
+    group = keep.shape[0] // 2
     half = product.shape[0] // 2
     swapped = row_half() == 1
     lower, upper = product[:half], product[half:]
     to_groups(jnp.where(swapped, upper, lower), jnp.where(swapped, lower, upper), groups)
-    keep[...] = groups[tp, 0:group]
-    for step, target in enumerate((first, second, third)):
-        part = groups[tp ^ (step + 1), 0:group]
-        columns = target.shape[1]
-        target[...] = jnp.concatenate([part[:, :columns], part[:, columns:]], axis=0).astype(jnp.bfloat16)
+    for step, target in enumerate((keep, first, second, third)):
+        target[...] = column_halves(groups[tp ^ step, 0:group]).astype(target.dtype)
 
 
 def finish_kernel(third, second, first, stream, mine, order, out, terms):
     total = stream[...] + mine[...]
-    group = out.shape[0]
     for other in (first, second, third):
-        halves = other[...].astype(jnp.float32)
-        total = total + jnp.concatenate([halves[:group], halves[group:]], axis=1)
+        total = total + other[...].astype(jnp.float32)
+    lines, columns = total.shape
     coarse = total.astype(jnp.bfloat16).astype(jnp.float32)
     terms[...] = jnp.zeros_like(terms)
-    terms[0:group] = coarse
-    terms[16 : 16 + group] = total - coarse
+    terms[0:lines] = coarse
+    terms[32 : 32 + lines] = total - coarse
     ordered = jnp.dot(order[...], terms[...].astype(jnp.bfloat16), preferred_element_type=jnp.float32)
-    out[...] = ordered.astype(jnp.bfloat16)
+    group = lines // 2
+    out[:, :columns] = ordered[:group].astype(jnp.bfloat16)
+    out[:, columns:] = ordered[group:].astype(jnp.bfloat16)
 
 
 def local_pairs(
@@ -563,7 +573,7 @@
     caches = (key_cache, cached_value_rows)
     near, order = call(
         functools.partial(attend_near_kernel, per_device, heads),
-        [((2, 4, head_block), f32), ((group, 32), bf16)],
+        [((2, 4, head_block), f32), ((half, 64), bf16)],
         (cache_len, mine, *caches, assign),
         smem=(0,),
         resident=(2, 3),
@@ -598,7 +608,7 @@
     far = call(project_far_kernel, pair, (across, corner, match, rows, out_weight), resident=(4,), nanos=0)
     sums = tp_sum(*near) + tp_sum(*far)
 
-    sizes = [width * sixteenths // 16 for sixteenths in (5, 5, 3, 3)]
+    sizes = [width * sixteenths // 16 for sixteenths in (5, 5, 4, 2)]
     starts = [sum(sizes[:index]) for index in range(len(sizes))]
     chunk = width // 16
     weights = (gate_weight, up_weight)
@@ -661,7 +671,13 @@
             )
         beside = swap(hidden, "sec", 1)
         if index == 0:
-            (before,) = call(down_first_kernel, total, (hidden, beside, down_weight), resident=(2,), nanos=1000)
+            before, stream = call(
+                down_first_kernel,
+                total + [((half, features // 2), f32)],
+                (hidden, beside, down_weight, stream),
+                resident=(2,),
+                nanos=1000,
+            )
             parts_done.append(before)
         elif index < len(sizes) - 1:
             (before,) = call(
@@ -675,7 +691,7 @@
         else:
             mine, *parts = call(
                 functools.partial(down_last_kernel, starts[index]),
-                [((group, features), f32)] + [((half, features // 2), bf16)] * 3,
+                [((half, features // 2), f32)] + [((half, features // 2), bf16)] * 3,
                 (before, hidden, beside, down_weight),
                 [pltpu.VMEM((4, 16, features), f32)],
                 resident=(3,),
@@ -685,7 +701,7 @@
         finish_kernel,
         [((group, features), bf16)],
         (*parts, stream, mine, order),
-        [pltpu.VMEM((32, features), f32)],
+        [pltpu.VMEM((64, features // 2), f32)],
     )
     return out
 

time: 56.1 us -> 55.9 us (level)
  transfers between devices with their start and end apart: 28 -> 28, of which waited for: 15 -> 16; matrix products, arithmetic and copies ran while one was open for 0% -> 0% of each run, Pallas kernels for 18% -> 18%
where the time goes in v13:
time: 55.9 us; the launch traced here: 55.8 us
  starting transfers between devices  25.7 us (46%)
  waiting for transfers between devices  15.8 us (28%)
  Pallas kernels  13.9 us (25%)
    ppermute x28, starting transfers between devices, swap(): return lax.ppermute(value, axis, [(i, i ^ step) for i in range(total)])  25.7 us
    ppermute x28, waiting for transfers between devices, swap(): return lax.ppermute(value, axis, [(i, i ^ step) for i in range(total)])  15.8 us
    pallas_call x27, Pallas kernels, call(): pl.pallas_call(kernel, out_shape=[jax.ShapeDtypeStruct(shape, dtype) for...  13.9 us
  transfers between devices with their start and end apart: 28, of which 16 were waited for; matrix products, arithmetic and copies ran while one was open for 0% of the time, Pallas kernels for 18%

profile of v13, /device:TPU:0, one launch (start us, length us, event | category | flops | bytes accessed | tf_op | source)
XLA Modules:
  0.0 55.8 jit_solution(10929356232375269823)
XLA Ops:
  0.0 0.5 collective-permute-start
  0.5 0.1 collective-permute-start.1
  0.6 1.4 %shard_map.118 = (bf16[2,48,128]{2,1,0:T(8,128)(2,1)S(1)}, bf16[16,12]{1,0:T(8,128)(2,1)S(1)}) custom-call(bf16[12,1280]{1,0:T(8,128)(2,1)} %query.1, bf16[12,512]{1,0:T(8,128)(2,1)} %pairs.1, s32[1,48]{1,0:T(1,128)} %bitcast.7), custom_call_target="tpu_custom_call" | custom-call | flops 2000000000 | tf_op jit(solution)/shard_map/pallas_call | solution.py:160
  2.0 0.1 shard_map.119
  2.2 2.6 %collective-permute-start.2 = (bf16[2,48,128]{2,1,0:T(8,128)(2,1)S(1)}, bf16[2,48,128]{2,1,0:T(8,128)(2,1)S(1)}, u32[]{:S(2)}, u32[]{:S(2)}) collective-permute-start(bf16[2,48,128]{2,1,0:T(8,128)(2,1)S(1)} %get-tuple-element.53), channel_id=1, source_target_pairs={{0,12},{4,8},{8,4},{12,0},{1,13},{5,9},{9,5},{13,1},{2,14},{6,10},... | collective-permute-start | bytes 73736 | tf_op jit(solution)/shard_map/ppermute | solution.py:191
  4.8 1.6 %shard_map.120 = (f32[2,4,1280]{2,1,0:T(4,128)S(1)}, bf16[24,64]{1,0:T(8,128)(2,1)S(1)}) custom-call(s32[3]{0:T(128)S(1)} %copy-done.4, bf16[2,48,128]{2,1,0:T(8,128)(2,1)S(1)} %get-tuple-element.54.source, bf16[3,224,1024]{2,1,0:T(8,128)(2,1)S(1)} %copy-done.1, bf16[3,224,1024]{2,1,0:T(8,128)(2,1)S(1)} %copy-done.2, s32[1,48]{1,0:T(1,128)S(1)} %bitcast.8), custom_call_target="tpu_custom_call" | custom-call | flops 2000000000 | tf_op jit(solution)/shard_map/pallas_call | solution.py:160
  6.4 1.2 %shard_map.121 = (bf16[4,1280]{1,0:T(4,128)(2,1)S(1)}, bf16[4,1280]{1,0:T(4,128)(2,1)S(1)}, bf16[4,1280]{1,0:T(4,128)(2,1)S(1)}, bf16[4,1280]{1,0:T(4,128)(2,1)S(1)}) custom-call(s32[3]{0:T(128)S(1)} %copy-done.4, bf16[2,48,128]{2,1,0:T(8,128)(2,1)S(1)} %collective-permute-done.2.source, f32[2,4,1280]{2,1,0:T(4,128)S(1)} %get-tuple-element.55.near, ...), custom_call_target="tpu_custom_call" | custom-call | flops 2000000000 | tf_op jit(solution)/shard_map/pallas_call | solution.py:160
  7.5 4.1 %collective-permute-start.3 = (bf16[4,1280]{1,0:T(4,128)(2,1)S(1)}, bf16[4,1280]{1,0:T(4,128)(2,1)S(1)}, u32[]{:S(2)}, u32[]{:S(2)}) collective-permute-start(bf16[4,1280]{1,0:T(4,128)(2,1)S(1)} %get-tuple-element.56), channel_id=1, source_target_pairs={{0,7},{1,6},{2,5},{3,4},{4,3},{5,2},{6,1},{7,0},{8,15},{9,14},{10,... | collective-permute-start | bytes 30728 | tf_op jit(solution)/shard_map/ppermute | solution.py:191
  11.6 0.7 %collective-permute-start.5 = (bf16[4,1280]{1,0:T(4,128)(2,1)S(1)}, bf16[4,1280]{1,0:T(4,128)(2,1)S(1)}, u32[]{:S(2)}, u32[]{:S(2)}) collective-permute-start(bf16[4,1280]{1,0:T(4,128)(2,1)S(1)} %get-tuple-element.58), channel_id=1, source_target_pairs={{0,5},{1,4},{2,7},{3,6},{4,1},{5,0},{6,3},{7,2},{8,13},{9,12},{10,... | collective-permute-start | bytes 30728 | tf_op jit(solution)/shard_map/ppermute | solution.py:191
  12.3 0.7 %collective-permute-done.3.third = bf16[4,1280]{1,0:T(4,128)(2,1)S(1)} collective-permute-done((bf16[4,1280]{1,0:T(4,128)(2,1)S(1)}, bf16[4,1280]{1,0:T(4,128)(2,1)S(1)}, u32[]{:S(2)}, u32[]{:S(2)}) %collective-permute-start.3) | collective-permute-done | bytes 10272 | tf_op jit(solution)/shard_map/ppermute | solution.py:191
  13.0 2.6 %collective-permute-done.4.second = bf16[4,1280]{1,0:T(4,128)(2,1)S(1)} collective-permute-done((bf16[4,1280]{1,0:T(4,128)(2,1)S(1)}, bf16[4,1280]{1,0:T(4,128)(2,1)S(1)}, u32[]{:S(2)}, u32[]{:S(2)}) %collective-permute-start.4) | collective-permute-done | bytes 10272 | tf_op jit(solution)/shard_map/ppermute | solution.py:191
  15.7 0.5 collective-permute-start.6
  16.2 1.2 %collective-permute-start.9 = (bf16[16,1280]{1,0:T(8,128)(2,1)S(1)}, bf16[16,1280]{1,0:T(8,128)(2,1)S(1)}, u32[]{:S(2)}, u32[]{:S(2)}) collective-permute-start(bf16[16,1280]{1,0:T(8,128)(2,1)S(1)} %shard_map.122.first), channel_id=1, source_target_pairs={{0,12},{4,8},{8,4},{12,0},{1,13},{5,9},{9,5},{13,1},{2,14},{6,10},... | collective-permute-start | bytes 122888 | tf_op jit(solution)/shard_map/ppermute | solution.py:191
  17.4 0.8 %shard_map.123 = (f32[24,1280]{1,0:T(8,128)S(1)}, bf16[24,1280]{1,0:T(8,128)(2,1)S(1)}, bf16[24,32]{1,0:T(8,128)(2,1)S(1)}, f32[24,1280]{1,0:T(8,128)S(1)}) custom-call(bf16[16,1280]{1,0:T(8,128)(2,1)S(1)} %shard_map.122.first, bf16[16,1280]{1,0:T(8,128)(2,1)S(1)} %collective-permute-done.6.second, s32[1,48]{1,0:T(1,128)S(1)} %bitcast.9, ...), custom_call_target="tpu_custom_call" | custom-call | flops 2000000000 | tf_op jit(solution)/shard_map/pallas_call | solution.py:160
  18.2 0.1 collective-permute-start.7
  18.3 1.5 %collective-permute-done.9.value.first = bf16[16,1280]{1,0:T(8,128)(2,1)S(1)} collective-permute-done((bf16[16,1280]{1,0:T(8,128)(2,1)S(1)}, bf16[16,1280]{1,0:T(8,128)(2,1)S(1)}, u32[]{:S(2)}, u32[]{:S(2)}) %collective-permute-start.9) | collective-permute-done | bytes 40992 | tf_op jit(solution)/shard_map/ppermute | solution.py:191
  19.8 0.1 collective-permute-start.10
  19.9 1.1 %collective-permute-done.10.second = bf16[16,1280]{1,0:T(8,128)(2,1)S(1)} collective-permute-done((bf16[16,1280]{1,0:T(8,128)(2,1)S(1)}, bf16[16,1280]{1,0:T(8,128)(2,1)S(1)}, u32[]{:S(2)}, u32[]{:S(2)}) %collective-permute-start.10) | collective-permute-done | bytes 40992 | tf_op jit(solution)/shard_map/ppermute | solution.py:191
  21.0 0.7 %shard_map.126 = (f32[24,1280]{1,0:T(8,128)S(1)}, bf16[24,1280]{1,0:T(8,128)(2,1)S(1)}) custom-call(bf16[16,1280]{1,0:T(8,128)(2,1)S(1)} %collective-permute-done.9.value.first, bf16[16,1280]{1,0:T(8,128)(2,1)S(1)} %collective-permute-done.10.second, bf16[24,32]{1,0:T(8,128)(2,1)S(1)} %get-tuple-element.64.match, f32[24,1280]{1,0:T(8,128)S(1)} %get-tuple-element.65.resid, ...), custom_call_target="tpu_custom_call" | custom-call | tf_op jit(solution)/shard_map/pallas_call | solution.py:160
  21.7 0.6 %collective-permute-start.11 = (bf16[24,1280]{1,0:T(8,128)(2,1)S(1)}, bf16[24,1280]{1,0:T(8,128)(2,1)S(1)}, u32[]{:S(2)}, u32[]{:S(2)}) collective-permute-start(bf16[24,1280]{1,0:T(8,128)(2,1)S(1)} %get-tuple-element.67), channel_id=1, source_target_pairs={{0,1},{1,0},{2,3},{3,2},{4,5},{5,4},{6,7},{7,6},{8,9},{9,8},{10,11... | collective-permute-start | bytes 184328 | tf_op jit(solution)/shard_map/ppermute | solution.py:191
  22.2 0.4 collective-permute-done.7.other
  22.6 2.0 %collective-permute-start.8 = (bf16[24,1280]{1,0:T(8,128)(2,1)S(1)}, bf16[24,1280]{1,0:T(8,128)(2,1)S(1)}, u32[]{:S(2)}, u32[]{:S(2)}) collective-permute-start(bf16[24,1280]{1,0:T(8,128)(2,1)S(1)} %get-tuple-element.63), channel_id=1, source_target_pairs={{0,2},{1,3},{2,0},{3,1},{4,6},{5,7},{6,4},{7,5},{8,10},{9,11},{10,... | collective-permute-start | bytes 184328 | tf_op jit(solution)/shard_map/ppermute | solution.py:191
  24.6 1.3 %collective-permute-done.11.other = bf16[24,1280]{1,0:T(8,128)(2,1)S(1)} collective-permute-done((bf16[24,1280]{1,0:T(8,128)(2,1)S(1)}, bf16[24,1280]{1,0:T(8,128)(2,1)S(1)}, u32[]{:S(2)}, u32[]{:S(2)}) %collective-permute-start.11) | collective-permute-done | bytes 61472 | tf_op jit(solution)/shard_map/ppermute | solution.py:191
  26.0 2.1 %collective-permute-start.12 = (bf16[24,1280]{1,0:T(8,128)(2,1)S(1)}, bf16[24,1280]{1,0:T(8,128)(2,1)S(1)}, u32[]{:S(2)}, u32[]{:S(2)}) collective-permute-start(bf16[24,1280]{1,0:T(8,128)(2,1)S(1)} %get-tuple-element.69), channel_id=1, source_target_pairs={{0,2},{1,3},{2,0},{3,1},{4,6},{5,7},{6,4},{7,5},{8,10},{9,11},{10,... | collective-permute-start | bytes 184328 | tf_op jit(solution)/shard_map/ppermute | solution.py:191
  28.1 1.9 %collective-permute-done.8.near_other = bf16[24,1280]{1,0:T(8,128)(2,1)S(1)} collective-permute-done((bf16[24,1280]{1,0:T(8,128)(2,1)S(1)}, bf16[24,1280]{1,0:T(8,128)(2,1)S(1)}, u32[]{:S(2)}, u32[]{:S(2)}) %collective-permute-start.8) | collective-permute-done | bytes 61472 | tf_op jit(solution)/shard_map/ppermute | solution.py:191
  29.9 1.8 %collective-permute-done.12.far_other = bf16[24,1280]{1,0:T(8,128)(2,1)S(1)} collective-permute-done((bf16[24,1280]{1,0:T(8,128)(2,1)S(1)}, bf16[24,1280]{1,0:T(8,128)(2,1)S(1)}, u32[]{:S(2)}, u32[]{:S(2)}) %collective-permute-start.12) | collective-permute-done | bytes 61472 | tf_op jit(solution)/shard_map/ppermute | solution.py:191
  31.8 1.3 %shard_map.128 = (f32[24,2688]{1,0:T(8,128)S(1)}, bf16[24,2688]{1,0:T(8,128)(2,1)S(1)}, bf16[48,1280]{1,0:T(8,128)(2,1)S(1)}, f32[12,1280]{1,0:T(8,128)S(1)}) custom-call(f32[24,1280]{1,0:T(8,128)S(1)} %get-tuple-element.62.near, bf16[24,1280]{1,0:T(8,128)(2,1)S(1)} %collective-permute-done.8.near_other, f32[24,1280]{1,0:T(8,128)S(1)} %get-tuple-element.68.far, ...), custom_call_target="tpu_custom_call" | custom-call | flops 2000000000 | tf_op jit(solution)/shard_map/pallas_call | solution.py:160
  33.1 0.1 collective-permute-start.13
  33.2 1.3 %shard_map.130 = (f32[24,2560]{1,0:T(8,128)S(1)}, bf16[24,2560]{1,0:T(8,128)(2,1)S(1)}) custom-call(bf16[48,1280]{1,0:T(8,128)(2,1)S(1)} %get-tuple-element.74.features, bf16[1280,4096]{1,0:T(8,128)(2,1)S(1)} %bitcast.2, bf16[1280,4096]{1,0:T(8,128)(2,1)S(1)} %bitcast.4, bf16[24,2688]{1,0:T(8,128)(2,1)S(1)} %get-tuple-element.71.earlier), custom_call_target="tpu_custom_call" | custom-call | tf_op jit(solution)/shard_map/pallas_call | solution.py:160
  34.5 0.5 collective-permute-start.15
  35.0 0.2 shard_map.129
  35.3 1.2 %collective-permute-start.14 = (bf16[24,2688]{1,0:T(8,128)(2,1)S(1)}, bf16[24,2688]{1,0:T(8,128)(2,1)S(1)}, u32[]{:S(2)}, u32[]{:S(2)}) collective-permute-start(bf16[24,2688]{1,0:T(8,128)(2,1)S(1)} %get-tuple-element.73.earlier), channel_id=1, source_target_pairs={{0,12},{4,8},{8,4},{12,0},{1,13},{5,9},{9,5},{13,1},{2,14},{6,10},... | collective-permute-start | bytes 387080 | tf_op jit(solution)/shard_map/ppermute | solution.py:191
  36.5 1.1 %collective-permute-start.19 = (bf16[24,2560]{1,0:T(8,128)(2,1)S(1)}, bf16[24,2560]{1,0:T(8,128)(2,1)S(1)}, u32[]{:S(2)}, u32[]{:S(2)}) collective-permute-start(bf16[24,2560]{1,0:T(8,128)(2,1)S(1)} %get-tuple-element.77.earlier), channel_id=1, source_target_pairs={{0,12},{4,8},{8,4},{12,0},{1,13},{5,9},{9,5},{13,1},{2,14},{6,10},... | collective-permute-start | bytes 368648 | tf_op jit(solution)/shard_map/ppermute | solution.py:191
  37.6 1.0 %shard_map.132 = (f32[24,2048]{1,0:T(8,128)S(1)}, bf16[24,2048]{1,0:T(8,128)(2,1)S(1)}) custom-call(bf16[48,1280]{1,0:T(8,128)(2,1)S(1)} %get-tuple-element.74.features, bf16[1280,4096]{1,0:T(8,128)(2,1)S(1)} %bitcast.2, bf16[1280,4096]{1,0:T(8,128)(2,1)S(1)} %bitcast.4, bf16[24,2560]{1,0:T(8,128)(2,1)S(1)} %get-tuple-element.77.earlier), custom_call_target="tpu_custom_call" | custom-call | tf_op jit(solution)/shard_map/pallas_call | solution.py:160
  38.7 0.2 collective-permute-start.17
  38.9 0.6 shard_map.133
  39.5 0.4 collective-permute-start.16
  39.9 0.2 collective-permute-done.17.other
  40.1 0.9 %collective-permute-start.21 = (bf16[24,2048]{1,0:T(8,128)(2,1)S(1)}, bf16[24,2048]{1,0:T(8,128)(2,1)S(1)}, u32[]{:S(2)}, u32[]{:S(2)}) collective-permute-start(bf16[24,2048]{1,0:T(8,128)(2,1)S(1)} %get-tuple-element.82.earlier), channel_id=1, source_target_pairs={{0,12},{4,8},{8,4},{12,0},{1,13},{5,9},{9,5},{13,1},{2,14},{6,10},... | collective-permute-start | bytes 294920 | tf_op jit(solution)/shard_map/ppermute | solution.py:191
  41.0 1.0 %collective-permute-start.23 = (bf16[24,1024]{1,0:T(8,128)(2,1)S(1)}, bf16[24,1024]{1,0:T(8,128)(2,1)S(1)}, u32[]{:S(2)}, u32[]{:S(2)}) collective-permute-start(bf16[24,1024]{1,0:T(8,128)(2,1)S(1)} %get-tuple-element.83.earlier), channel_id=1, source_target_pairs={{0,12},{4,8},{8,4},{12,0},{1,13},{5,9},{9,5},{13,1},{2,14},{6,10},... | collective-permute-start | bytes 147464 | tf_op jit(solution)/shard_map/ppermute | solution.py:191
  42.0 0.2 shard_map.136
  42.2 0.2 collective-permute-start.18
  42.4 1.0 %collective-permute-done.19.other = bf16[24,2560]{1,0:T(8,128)(2,1)S(1)} collective-permute-done((bf16[24,2560]{1,0:T(8,128)(2,1)S(1)}, bf16[24,2560]{1,0:T(8,128)(2,1)S(1)}, u32[]{:S(2)}, u32[]{:S(2)}) %collective-permute-start.19) | collective-permute-done | bytes 122912 | tf_op jit(solution)/shard_map/ppermute | solution.py:191
  43.4 0.1 shard_map.138.mine
  43.6 0.6 %collective-permute-start.20 = (bf16[24,1280]{1,0:T(8,128)(2,1)S(1)}, bf16[24,1280]{1,0:T(8,128)(2,1)S(1)}, u32[]{:S(2)}, u32[]{:S(2)}) collective-permute-start(bf16[24,1280]{1,0:T(8,128)(2,1)S(1)} %shard_map.138.mine), channel_id=1, source_target_pairs={{0,4},{4,0},{8,12},{12,8},{1,5},{5,1},{9,13},{13,9},{2,6},{6,2},{1... | collective-permute-start | bytes 184328 | tf_op jit(solution)/shard_map/ppermute | solution.py:191
  44.2 0.7 %shard_map.137 = (f32[48,1280]{1,0:T(8,128)S(1)}, f32[24,640]{1,0:T(8,128)S(1)}) custom-call(bf16[24,1280]{1,0:T(8,128)(2,1)S(1)} %get-tuple-element.84.mine.earlier, bf16[24,1280]{1,0:T(8,128)(2,1)S(1)} %collective-permute-done.18.other, bf16[4096,1280]{1,0:T(8,128)(2,1)S(1)} %bitcast.6, f32[12,1280]{1,0:T(8,128)S(1)} %get-tuple-element.85.stream), custom_call_target="tpu_custom_call" | custom-call | flops 1000000000 | tf_op jit(solution)/shard_map/pallas_call | solution.py:160
  44.9 0.2 collective-permute-done.20.other
  45.0 0.7 %shard_map.139.before.earlier = f32[48,1280]{1,0:T(8,128)S(1)} custom-call(f32[48,1280]{1,0:T(8,128)S(1)} %get-tuple-element.86.before.earlier, bf16[24,1280]{1,0:T(8,128)(2,1)S(1)} %shard_map.138.mine, bf16[24,1280]{1,0:T(8,128)(2,1)S(1)} %collective-permute-done.20.other, bf16[4096,1280]{1,0:T(8,128)(2,1)S(1)} %bitcast.6), custom_call_target="tpu_custom_call" | custom-call | flops 1000000000 | tf_op jit(solution)/shard_map/pallas_call | solution.py:160
  45.8 0.1 shard_map.140.mine
  45.9 0.4 collective-permute-start.22
  46.3 0.3 collective-permute-done.23.other
  46.6 0.1 shard_map.142.mine
  46.7 0.2 collective-permute-start.24
  46.9 0.3 collective-permute-done.22.other
  47.2 0.6 %shard_map.141.before = f32[48,1280]{1,0:T(8,128)S(1)} custom-call(f32[48,1280]{1,0:T(8,128)S(1)} %shard_map.139.before.earlier, bf16[24,1024]{1,0:T(8,128)(2,1)S(1)} %shard_map.140.mine, bf16[24,1024]{1,0:T(8,128)(2,1)S(1)} %collective-permute-done.22.other, bf16[4096,1280]{1,0:T(8,128)(2,1)S(1)} %bitcast.6), custom_call_target="tpu_custom_call" | custom-call | flops 1000000000 | tf_op jit(solution)/shard_map/pallas_call | solution.py:160
  47.7 0.2 collective-permute-done.24.other
  48.0 0.4 shard_map.143
  48.3 1.5 %collective-permute-start.25 = (bf16[24,640]{1,0:T(8,128)(2,1)S(1)}, bf16[24,640]{1,0:T(8,128)(2,1)S(1)}, u32[]{:S(2)}, u32[]{:S(2)}) collective-permute-start(bf16[24,640]{1,0:T(8,128)(2,1)S(1)} %get-tuple-element.91), channel_id=1, source_target_pairs={{0,3},{1,2},{2,1},{3,0},{4,7},{5,6},{6,5},{7,4},{8,11},{9,10},{10,... | collective-permute-start | bytes 92168 | tf_op jit(solution)/shard_map/ppermute | solution.py:191
  49.8 0.1 collective-permute-start.26
  49.9 2.9 %collective-permute-start.27 = (bf16[24,640]{1,0:T(8,128)(2,1)S(1)}, bf16[24,640]{1,0:T(8,128)(2,1)S(1)}, u32[]{:S(2)}, u32[]{:S(2)}) collective-permute-start(bf16[24,640]{1,0:T(8,128)(2,1)S(1)} %get-tuple-element.93), channel_id=1, source_target_pairs={{0,1},{1,0},{2,3},{3,2},{4,5},{5,4},{6,7},{7,6},{8,9},{9,8},{10,11... | collective-permute-start | bytes 92168 | tf_op jit(solution)/shard_map/ppermute | solution.py:191
  52.8 1.3 %collective-permute-done.25.third = bf16[24,640]{1,0:T(8,128)(2,1)S(1)} collective-permute-done((bf16[24,640]{1,0:T(8,128)(2,1)S(1)}, bf16[24,640]{1,0:T(8,128)(2,1)S(1)}, u32[]{:S(2)}, u32[]{:S(2)}) %collective-permute-start.25) | collective-permute-done | bytes 30752 | tf_op jit(solution)/shard_map/ppermute | solution.py:191
  54.1 0.8 %collective-permute-done.26.second = bf16[24,640]{1,0:T(8,128)(2,1)S(1)} collective-permute-done((bf16[24,640]{1,0:T(8,128)(2,1)S(1)}, bf16[24,640]{1,0:T(8,128)(2,1)S(1)}, u32[]{:S(2)}, u32[]{:S(2)}) %collective-permute-start.26) | collective-permute-done | bytes 30752 | tf_op jit(solution)/shard_map/ppermute | solution.py:191
  55.0 0.0 collective-permute-done.27.first
  55.0 0.8 %shard_map.144 = bf16[12,1280]{1,0:T(8,128)(2,1)} custom-call(bf16[24,640]{1,0:T(8,128)(2,1)S(1)} %collective-permute-done.25.third, bf16[24,640]{1,0:T(8,128)(2,1)S(1)} %collective-permute-done.26.second, bf16[24,640]{1,0:T(8,128)(2,1)S(1)} %collective-permute-done.27.first, f32[24,640]{1,0:T(8,128)S(1)} %get-tuple-element.94.stream, ...), custom_call_target="tpu_custom_call" | custom-call | flops 2000000000 | tf_op jit(solution)/shard_map/pallas_call | solution.py:160
  (55 shorter events, 0.3 us)
Async XLA Ops:
  0.0 4.8 %copy-start.5 = (s32[48]{0:T(128)S(1)}, s32[48]{0:T(128)}, u32[]{:S(2)}) copy-start(s32[48]{0:T(128)} %param.18) | copy-start | bytes 580
  0.0 4.8 %copy-start.1 = (bf16[3,224,1024]{2,1,0:T(8,128)(2,1)S(1)}, bf16[3,224,1024]{2,1,0:T(8,128)(2,1)}, u32[]{:S(2)}) copy-start(bf16[3,224,1024]{2,1,0:T(8,128)(2,1)} %keys.3) | copy-start | bytes 4128772
  0.0 4.8 %copy-start.2 = (bf16[3,224,1024]{2,1,0:T(8,128)(2,1)S(1)}, bf16[3,224,1024]{2,1,0:T(8,128)(2,1)}, u32[]{:S(2)}) copy-start(bf16[3,224,1024]{2,1,0:T(8,128)(2,1)} %values.3) | copy-start | bytes 4128772
  0.0 4.8 %copy-start.4 = (s32[3]{0:T(128)S(1)}, s32[3]{0:T(128)}, u32[]{:S(2)}) copy-start(s32[3]{0:T(128)} %lengths.3) | copy-start | bytes 40
  0.0 2.0 %collective-permute-start = (bf16[12,1280]{1,0:T(8,128)(2,1)}, bf16[12,1280]{1,0:T(8,128)(2,1)S(1)}, u32[]{:S(2)}, u32[]{:S(2)}) collective-permute-start(bf16[12,1280]{1,0:T(8,128)(2,1)} %query.1), channel_id=1, source_target_pairs={{0,4},{4,0},{8,12},{12,8},{1,5},{5,1},{9,13},{13,9},{2,6},{6,2},{1... | collective-permute-start | bytes 92168 | tf_op jit(solution)/shard_map/ppermute | solution.py:191
  0.5 1.5 %collective-permute-start.1 = (bf16[12,512]{1,0:T(8,128)(2,1)}, bf16[12,512]{1,0:T(8,128)(2,1)S(1)}, u32[]{:S(2)}, u32[]{:S(2)}) collective-permute-start(bf16[12,512]{1,0:T(8,128)(2,1)} %pairs.1), channel_id=1, source_target_pairs={{0,4},{4,0},{8,12},{12,8},{1,5},{5,1},{9,13},{13,9},{2,6},{6,2},{1... | collective-permute-start | bytes 36872 | tf_op jit(solution)/shard_map/ppermute | solution.py:191
  2.2 4.2 %collective-permute-start.2 = (bf16[2,48,128]{2,1,0:T(8,128)(2,1)S(1)}, bf16[2,48,128]{2,1,0:T(8,128)(2,1)S(1)}, u32[]{:S(2)}, u32[]{:S(2)}) collective-permute-start(bf16[2,48,128]{2,1,0:T(8,128)(2,1)S(1)} %get-tuple-element.53), channel_id=1, source_target_pairs={{0,12},{4,8},{8,4},{12,0},{1,13},{5,9},{9,5},{13,1},{2,14},{6,10},... | collective-permute-start | bytes 73736 | tf_op jit(solution)/shard_map/ppermute | solution.py:191
  4.8 12.6 %copy-start = (bf16[1280,1280]{1,0:T(8,128)(2,1)S(1)}, bf16[1280,1280]{1,0:T(8,128)(2,1)}, u32[]{:S(2)}) copy-start(bf16[1280,1280]{1,0:T(8,128)(2,1)} %weight.7) | copy-start | bytes 9830404
  4.8 12.6 %copy-start.3 = (bf16[12,1280]{1,0:T(8,128)(2,1)S(1)}, bf16[12,1280]{1,0:T(8,128)(2,1)}, u32[]{:S(2)}) copy-start(bf16[12,1280]{1,0:T(8,128)(2,1)} %resid.1) | copy-start | bytes 92164
  7.5 5.5 %collective-permute-start.3 = (bf16[4,1280]{1,0:T(4,128)(2,1)S(1)}, bf16[4,1280]{1,0:T(4,128)(2,1)S(1)}, u32[]{:S(2)}, u32[]{:S(2)}) collective-permute-start(bf16[4,1280]{1,0:T(4,128)(2,1)S(1)} %get-tuple-element.56), channel_id=1, source_target_pairs={{0,7},{1,6},{2,5},{3,4},{4,3},{5,2},{6,1},{7,0},{8,15},{9,14},{10,... | collective-permute-start | bytes 30728 | tf_op jit(solution)/shard_map/ppermute | solution.py:191
  11.6 4.0 %collective-permute-start.4 = (bf16[4,1280]{1,0:T(4,128)(2,1)S(1)}, bf16[4,1280]{1,0:T(4,128)(2,1)S(1)}, u32[]{:S(2)}, u32[]{:S(2)}) collective-permute-start(bf16[4,1280]{1,0:T(4,128)(2,1)S(1)} %get-tuple-element.57), channel_id=1, source_target_pairs={{0,6},{1,7},{2,4},{3,5},{4,2},{5,3},{6,0},{7,1},{8,14},{9,15},{10,... | collective-permute-start | bytes 30728 | tf_op jit(solution)/shard_map/ppermute | solution.py:191
  11.6 4.0 %collective-permute-start.5 = (bf16[4,1280]{1,0:T(4,128)(2,1)S(1)}, bf16[4,1280]{1,0:T(4,128)(2,1)S(1)}, u32[]{:S(2)}, u32[]{:S(2)}) collective-permute-start(bf16[4,1280]{1,0:T(4,128)(2,1)S(1)} %get-tuple-element.58), channel_id=1, source_target_pairs={{0,5},{1,4},{2,7},{3,6},{4,1},{5,0},{6,3},{7,2},{8,13},{9,12},{10,... | collective-permute-start | bytes 30728 | tf_op jit(solution)/shard_map/ppermute | solution.py:191
  15.6 16.1 %slice-start.3 = ((s8[10485760]{0:T(1024)(128)(4,1)}), s8[4194304]{0:T(1024)(128)(4,1)S(1)}, s32[]{:S(2)}) async-start(s8[10485760]{0:T(1024)(128)(4,1)} %bitcast.3), calls=%async_computation.3 | async-start | bytes 8388608
  15.7 16.1 %slice-start.4 = ((s8[10485760]{0:T(1024)(128)(4,1)}), s8[4194304]{0:T(1024)(128)(4,1)S(1)}, s32[]{:S(2)}) async-start(s8[10485760]{0:T(1024)(128)(4,1)} %bitcast.3), calls=%async_computation.4 | async-start | bytes 8388608
  15.7 1.7 %collective-permute-start.6 = (bf16[16,1280]{1,0:T(8,128)(2,1)S(1)}, bf16[16,1280]{1,0:T(8,128)(2,1)S(1)}, u32[]{:S(2)}, u32[]{:S(2)}) collective-permute-start(bf16[16,1280]{1,0:T(8,128)(2,1)S(1)} %shard_map.122.first), channel_id=1, source_target_pairs={{0,4},{4,0},{8,12},{12,8},{1,5},{5,1},{9,13},{13,9},{2,6},{6,2},{1... | collective-permute-start | bytes 122888 | tf_op jit(solution)/shard_map/ppermute | solution.py:191
  16.2 3.6 %collective-permute-start.9 = (bf16[16,1280]{1,0:T(8,128)(2,1)S(1)}, bf16[16,1280]{1,0:T(8,128)(2,1)S(1)}, u32[]{:S(2)}, u32[]{:S(2)}) collective-permute-start(bf16[16,1280]{1,0:T(8,128)(2,1)S(1)} %shard_map.122.first), channel_id=1, source_target_pairs={{0,12},{4,8},{8,4},{12,0},{1,13},{5,9},{9,5},{13,1},{2,14},{6,10},... | collective-permute-start | bytes 122888 | tf_op jit(solution)/shard_map/ppermute | solution.py:191
  17.4 14.4 %slice-start = ((s8[10485760]{0:T(1024)(128)(4,1)}), s8[4194304]{0:T(1024)(128)(4,1)S(1)}, s32[]{:S(2)}) async-start(s8[10485760]{0:T(1024)(128)(4,1)} %bitcast.1), calls=%async_computation | async-start | bytes 8388608
  18.2 9.9 %copy-start.6 = (bf16[1280]{0:T(1024)(128)(2,1)S(1)}, bf16[1280]{0:T(1024)(128)(2,1)}, u32[]{:S(2)}) copy-start(bf16[1280]{0:T(1024)(128)(2,1)} %param.20) | copy-start | bytes 7684
  18.2 4.4 %collective-permute-start.7 = (bf16[24,1280]{1,0:T(8,128)(2,1)S(1)}, bf16[24,1280]{1,0:T(8,128)(2,1)S(1)}, u32[]{:S(2)}, u32[]{:S(2)}) collective-permute-start(bf16[24,1280]{1,0:T(8,128)(2,1)S(1)} %get-tuple-element.61.earlier), channel_id=1, source_target_pairs={{0,1},{1,0},{2,3},{3,2},{4,5},{5,4},{6,7},{7,6},{8,9},{9,8},{10,11... | collective-permute-start | bytes 184328 | tf_op jit(solution)/shard_map/ppermute | solution.py:191
  19.8 1.2 %collective-permute-start.10 = (bf16[16,1280]{1,0:T(8,128)(2,1)S(1)}, bf16[16,1280]{1,0:T(8,128)(2,1)S(1)}, u32[]{:S(2)}, u32[]{:S(2)}) collective-permute-start(bf16[16,1280]{1,0:T(8,128)(2,1)S(1)} %shard_map.125), channel_id=1, source_target_pairs={{0,4},{4,0},{8,12},{12,8},{1,5},{5,1},{9,13},{13,9},{2,6},{6,2},{1... | collective-permute-start | bytes 122888 | tf_op jit(solution)/shard_map/ppermute | solution.py:191
  21.0 10.8 %slice-start.1 = ((s8[10485760]{0:T(1024)(128)(4,1)}), s8[4194304]{0:T(1024)(128)(4,1)S(1)}, s32[]{:S(2)}) async-start(s8[10485760]{0:T(1024)(128)(4,1)} %bitcast.1), calls=%async_computation.1 | async-start | bytes 8388608
  21.7 4.3 %collective-permute-start.11 = (bf16[24,1280]{1,0:T(8,128)(2,1)S(1)}, bf16[24,1280]{1,0:T(8,128)(2,1)S(1)}, u32[]{:S(2)}, u32[]{:S(2)}) collective-permute-start(bf16[24,1280]{1,0:T(8,128)(2,1)S(1)} %get-tuple-element.67), channel_id=1, source_target_pairs={{0,1},{1,0},{2,3},{3,2},{4,5},{5,4},{6,7},{7,6},{8,9},{9,8},{10,11... | collective-permute-start | bytes 184328 | tf_op jit(solution)/shard_map/ppermute | solution.py:191
  22.6 9.2 %slice-start.2 = ((s8[10485760]{0:T(1024)(128)(4,1)}), s8[2097152]{0:T(1024)(128)(4,1)S(1)}, s32[]{:S(2)}) async-start(s8[10485760]{0:T(1024)(128)(4,1)} %bitcast.1), calls=%async_computation.2 | async-start | bytes 4194304
  22.6 9.2 %slice-start.5 = ((s8[10485760]{0:T(1024)(128)(4,1)}), s8[2097152]{0:T(1024)(128)(4,1)S(1)}, s32[]{:S(2)}) async-start(s8[10485760]{0:T(1024)(128)(4,1)} %bitcast.3), calls=%async_computation.5 | async-start | bytes 4194304
  22.6 7.3 %collective-permute-start.8 = (bf16[24,1280]{1,0:T(8,128)(2,1)S(1)}, bf16[24,1280]{1,0:T(8,128)(2,1)S(1)}, u32[]{:S(2)}, u32[]{:S(2)}) collective-permute-start(bf16[24,1280]{1,0:T(8,128)(2,1)S(1)} %get-tuple-element.63), channel_id=1, source_target_pairs={{0,2},{1,3},{2,0},{3,1},{4,6},{5,7},{6,4},{7,5},{8,10},{9,11},{10,... | collective-permute-start | bytes 184328 | tf_op jit(solution)/shard_map/ppermute | solution.py:191
  26.0 5.8 %collective-permute-start.12 = (bf16[24,1280]{1,0:T(8,128)(2,1)S(1)}, bf16[24,1280]{1,0:T(8,128)(2,1)S(1)}, u32[]{:S(2)}, u32[]{:S(2)}) collective-permute-start(bf16[24,1280]{1,0:T(8,128)(2,1)S(1)} %get-tuple-element.69), channel_id=1, source_target_pairs={{0,2},{1,3},{2,0},{3,1},{4,6},{5,7},{6,4},{7,5},{8,10},{9,11},{10,... | collective-permute-start | bytes 184328 | tf_op jit(solution)/shard_map/ppermute | solution.py:191
  33.1 1.9 %collective-permute-start.13 = (bf16[24,2688]{1,0:T(8,128)(2,1)S(1)}, bf16[24,2688]{1,0:T(8,128)(2,1)S(1)}, u32[]{:S(2)}, u32[]{:S(2)}) collective-permute-start(bf16[24,2688]{1,0:T(8,128)(2,1)S(1)} %get-tuple-element.71.earlier), channel_id=1, source_target_pairs={{0,4},{4,0},{8,12},{12,8},{1,5},{5,1},{9,13},{13,9},{2,6},{6,2},{1... | collective-permute-start | bytes 387080 | tf_op jit(solution)/shard_map/ppermute | solution.py:191
  34.5 2.0 %collective-permute-start.15 = (bf16[24,2560]{1,0:T(8,128)(2,1)S(1)}, bf16[24,2560]{1,0:T(8,128)(2,1)S(1)}, u32[]{:S(2)}, u32[]{:S(2)}) collective-permute-start(bf16[24,2560]{1,0:T(8,128)(2,1)S(1)} %get-tuple-element.76), channel_id=1, source_target_pairs={{0,4},{4,0},{8,12},{12,8},{1,5},{5,1},{9,13},{13,9},{2,6},{6,2},{1... | collective-permute-start | bytes 368648 | tf_op jit(solution)/shard_map/ppermute | solution.py:191
  35.3 6.7 %collective-permute-start.14 = (bf16[24,2688]{1,0:T(8,128)(2,1)S(1)}, bf16[24,2688]{1,0:T(8,128)(2,1)S(1)}, u32[]{:S(2)}, u32[]{:S(2)}) collective-permute-start(bf16[24,2688]{1,0:T(8,128)(2,1)S(1)} %get-tuple-element.73.earlier), channel_id=1, source_target_pairs={{0,12},{4,8},{8,4},{12,0},{1,13},{5,9},{9,5},{13,1},{2,14},{6,10},... | collective-permute-start | bytes 387080 | tf_op jit(solution)/shard_map/ppermute | solution.py:191
  36.5 7.0 %collective-permute-start.19 = (bf16[24,2560]{1,0:T(8,128)(2,1)S(1)}, bf16[24,2560]{1,0:T(8,128)(2,1)S(1)}, u32[]{:S(2)}, u32[]{:S(2)}) collective-permute-start(bf16[24,2560]{1,0:T(8,128)(2,1)S(1)} %get-tuple-element.77.earlier), channel_id=1, source_target_pairs={{0,12},{4,8},{8,4},{12,0},{1,13},{5,9},{9,5},{13,1},{2,14},{6,10},... | collective-permute-start | bytes 368648 | tf_op jit(solution)/shard_map/ppermute | solution.py:191
  38.6 5.5 %slice-start.6 = ((s8[10485760]{0:T(1024)(128)(4,1)}), s8[4194304]{0:T(1024)(128)(4,1)S(1)}, s32[]{:S(2)}) async-start(s8[10485760]{0:T(1024)(128)(4,1)} %bitcast.5), calls=%async_computation.6 | async-start | bytes 8388608
  38.7 5.5 %slice-start.7 = ((s8[10485760]{0:T(1024)(128)(4,1)}), s8[4194304]{0:T(1024)(128)(4,1)S(1)}, s32[]{:S(2)}) async-start(s8[10485760]{0:T(1024)(128)(4,1)} %bitcast.5), calls=%async_computation.7 | async-start | bytes 8388608
  38.7 5.5 %slice-start.8 = ((s8[10485760]{0:T(1024)(128)(4,1)}), s8[2097152]{0:T(1024)(128)(4,1)S(1)}, s32[]{:S(2)}) async-start(s8[10485760]{0:T(1024)(128)(4,1)} %bitcast.5), calls=%async_computation.8 | async-start | bytes 4194304
  38.7 1.4 %collective-permute-start.17 = (bf16[24,2048]{1,0:T(8,128)(2,1)S(1)}, bf16[24,2048]{1,0:T(8,128)(2,1)S(1)}, u32[]{:S(2)}, u32[]{:S(2)}) collective-permute-start(bf16[24,2048]{1,0:T(8,128)(2,1)S(1)} %get-tuple-element.78.earlier), channel_id=1, source_target_pairs={{0,4},{4,0},{8,12},{12,8},{1,5},{5,1},{9,13},{13,9},{2,6},{6,2},{1... | collective-permute-start | bytes 294920 | tf_op jit(solution)/shard_map/ppermute | solution.py:191
  39.5 1.5 %collective-permute-start.16 = (bf16[24,1024]{1,0:T(8,128)(2,1)S(1)}, bf16[24,1024]{1,0:T(8,128)(2,1)S(1)}, u32[]{:S(2)}, u32[]{:S(2)}) collective-permute-start(bf16[24,1024]{1,0:T(8,128)(2,1)S(1)} %get-tuple-element.80.earlier), channel_id=1, source_target_pairs={{0,4},{4,0},{8,12},{12,8},{1,5},{5,1},{9,13},{13,9},{2,6},{6,2},{1... | collective-permute-start | bytes 147464 | tf_op jit(solution)/shard_map/ppermute | solution.py:191
  40.1 5.7 %collective-permute-start.21 = (bf16[24,2048]{1,0:T(8,128)(2,1)S(1)}, bf16[24,2048]{1,0:T(8,128)(2,1)S(1)}, u32[]{:S(2)}, u32[]{:S(2)}) collective-permute-start(bf16[24,2048]{1,0:T(8,128)(2,1)S(1)} %get-tuple-element.82.earlier), channel_id=1, source_target_pairs={{0,12},{4,8},{8,4},{12,0},{1,13},{5,9},{9,5},{13,1},{2,14},{6,10},... | collective-permute-start | bytes 294920 | tf_op jit(solution)/shard_map/ppermute | solution.py:191
  41.0 5.6 %collective-permute-start.23 = (bf16[24,1024]{1,0:T(8,128)(2,1)S(1)}, bf16[24,1024]{1,0:T(8,128)(2,1)S(1)}, u32[]{:S(2)}, u32[]{:S(2)}) collective-permute-start(bf16[24,1024]{1,0:T(8,128)(2,1)S(1)} %get-tuple-element.83.earlier), channel_id=1, source_target_pairs={{0,12},{4,8},{8,4},{12,0},{1,13},{5,9},{9,5},{13,1},{2,14},{6,10},... | collective-permute-start | bytes 147464 | tf_op jit(solution)/shard_map/ppermute | solution.py:191
  42.2 2.0 %collective-permute-start.18 = (bf16[24,1280]{1,0:T(8,128)(2,1)S(1)}, bf16[24,1280]{1,0:T(8,128)(2,1)S(1)}, u32[]{:S(2)}, u32[]{:S(2)}) collective-permute-start(bf16[24,1280]{1,0:T(8,128)(2,1)S(1)} %get-tuple-element.84.mine.earlier), channel_id=1, source_target_pairs={{0,4},{4,0},{8,12},{12,8},{1,5},{5,1},{9,13},{13,9},{2,6},{6,2},{1... | collective-permute-start | bytes 184328 | tf_op jit(solution)/shard_map/ppermute | solution.py:191
  43.6 1.5 %collective-permute-start.20 = (bf16[24,1280]{1,0:T(8,128)(2,1)S(1)}, bf16[24,1280]{1,0:T(8,128)(2,1)S(1)}, u32[]{:S(2)}, u32[]{:S(2)}) collective-permute-start(bf16[24,1280]{1,0:T(8,128)(2,1)S(1)} %shard_map.138.mine), channel_id=1, source_target_pairs={{0,4},{4,0},{8,12},{12,8},{1,5},{5,1},{9,13},{13,9},{2,6},{6,2},{1... | collective-permute-start | bytes 184328 | tf_op jit(solution)/shard_map/ppermute | solution.py:191
  45.9 1.3 %collective-permute-start.22 = (bf16[24,1024]{1,0:T(8,128)(2,1)S(1)}, bf16[24,1024]{1,0:T(8,128)(2,1)S(1)}, u32[]{:S(2)}, u32[]{:S(2)}) collective-permute-start(bf16[24,1024]{1,0:T(8,128)(2,1)S(1)} %shard_map.140.mine), channel_id=1, source_target_pairs={{0,4},{4,0},{8,12},{12,8},{1,5},{5,1},{9,13},{13,9},{2,6},{6,2},{1... | collective-permute-start | bytes 147464 | tf_op jit(solution)/shard_map/ppermute | solution.py:191
  46.7 1.3 %collective-permute-start.24 = (bf16[24,512]{1,0:T(8,128)(2,1)S(1)}, bf16[24,512]{1,0:T(8,128)(2,1)S(1)}, u32[]{:S(2)}, u32[]{:S(2)}) collective-permute-start(bf16[24,512]{1,0:T(8,128)(2,1)S(1)} %shard_map.142.mine), channel_id=1, source_target_pairs={{0,4},{4,0},{8,12},{12,8},{1,5},{5,1},{9,13},{13,9},{2,6},{6,2},{1... | collective-permute-start | bytes 73736 | tf_op jit(solution)/shard_map/ppermute | solution.py:191
  48.3 5.8 %collective-permute-start.25 = (bf16[24,640]{1,0:T(8,128)(2,1)S(1)}, bf16[24,640]{1,0:T(8,128)(2,1)S(1)}, u32[]{:S(2)}, u32[]{:S(2)}) collective-permute-start(bf16[24,640]{1,0:T(8,128)(2,1)S(1)} %get-tuple-element.91), channel_id=1, source_target_pairs={{0,3},{1,2},{2,1},{3,0},{4,7},{5,6},{6,5},{7,4},{8,11},{9,10},{10,... | collective-permute-start | bytes 92168 | tf_op jit(solution)/shard_map/ppermute | solution.py:191
  49.8 5.1 %collective-permute-start.26 = (bf16[24,640]{1,0:T(8,128)(2,1)S(1)}, bf16[24,640]{1,0:T(8,128)(2,1)S(1)}, u32[]{:S(2)}, u32[]{:S(2)}) collective-permute-start(bf16[24,640]{1,0:T(8,128)(2,1)S(1)} %get-tuple-element.92), channel_id=1, source_target_pairs={{0,2},{1,3},{2,0},{3,1},{4,6},{5,7},{6,4},{7,5},{8,10},{9,11},{10,... | collective-permute-start | bytes 92168 | tf_op jit(solution)/shard_map/ppermute | solution.py:191
  49.9 5.1 %collective-permute-start.27 = (bf16[24,640]{1,0:T(8,128)(2,1)S(1)}, bf16[24,640]{1,0:T(8,128)(2,1)S(1)}, u32[]{:S(2)}, u32[]{:S(2)}) collective-permute-start(bf16[24,640]{1,0:T(8,128)(2,1)S(1)} %get-tuple-element.93), channel_id=1, source_target_pairs={{0,1},{1,0},{2,3},{3,2},{4,5},{5,4},{6,7},{7,6},{8,9},{9,8},{10,11... | collective-permute-start | bytes 92168 | tf_op jit(solution)/shard_map/ppermute | solution.py:191

commit v14 on v13

--- a/solution.py
+++ b/solution.py
@@ -594,9 +594,9 @@
 
     pair = [((half, features), f32), ((half, features), bf16)]
 
-    def tp_sum(mine, away):
-        mine, away = call(add_kernel, pair, (mine, swap(away, "tp", 1)))
-        return mine, swap(away, "tp", 2)
+    def tp_sum(mine, away, first, second):
+        mine, away = call(add_kernel, pair, (mine, swap(away, "tp", first)))
+        return mine, swap(away, "tp", second)
 
     *near, match, rows = call(
         functools.partial(project_near_kernel, per_device),
@@ -606,7 +606,7 @@
     )
     corner = swap(after(across, near[1]), "sec", 1)
     far = call(project_far_kernel, pair, (across, corner, match, rows, out_weight), resident=(4,), nanos=0)
-    sums = tp_sum(*near) + tp_sum(*far)
+    sums = tp_sum(*near, 2, 1) + tp_sum(*far, 1, 2)
 
     sizes = [width * sixteenths // 16 for sixteenths in (5, 5, 4, 2)]
     starts = [sum(sizes[:index]) for index in range(len(sizes))]

time: 55.9 us -> 55.9 us (level)
  starting transfers between devices: 25.7 us -> 24.5 us
  waiting for transfers between devices: 15.8 us -> 17 us
    ppermute x28, waiting for transfers between devices: 15.8 us -> 17 us  [swap(): return lax.ppermute(value, axis, [(i, i ^ step) for i in range(total)])]
    ppermute x28, starting transfers between devices: 25.7 us -> 24.5 us  [swap(): return lax.ppermute(value, axis, [(i, i ^ step) for i in range(total)])]
where the time goes in v14:
time: 55.9 us; the launch traced here: 55.8 us
  starting transfers between devices  24.5 us (44%)
  waiting for transfers between devices  17 us (30%)
  Pallas kernels  13.9 us (25%)
    ppermute x28, starting transfers between devices, swap(): return lax.ppermute(value, axis, [(i, i ^ step) for i in range(total)])  24.5 us
    ppermute x28, waiting for transfers between devices, swap(): return lax.ppermute(value, axis, [(i, i ^ step) for i in range(total)])  17 us
    pallas_call x27, Pallas kernels, call(): pl.pallas_call(kernel, out_shape=[jax.ShapeDtypeStruct(shape, dtype) for...  13.9 us
  transfers between devices with their start and end apart: 28, of which 16 were waited for; matrix products, arithmetic and copies ran while one was open for 0% of the time, Pallas kernels for 18%

profile of v14, /device:TPU:0, one launch (start us, length us, event | category | flops | bytes accessed | tf_op | source)
XLA Modules:
  0.0 55.8 jit_solution(8967266630611253940)
XLA Ops:
  0.0 0.5 collective-permute-start
  0.5 0.1 collective-permute-start.1
  0.6 1.4 %shard_map.118 = (bf16[2,48,128]{2,1,0:T(8,128)(2,1)S(1)}, bf16[16,12]{1,0:T(8,128)(2,1)S(1)}) custom-call(bf16[12,1280]{1,0:T(8,128)(2,1)} %query.1, bf16[12,512]{1,0:T(8,128)(2,1)} %pairs.1, s32[1,48]{1,0:T(1,128)} %bitcast.7), custom_call_target="tpu_custom_call" | custom-call | flops 2000000000 | tf_op jit(solution)/shard_map/pallas_call | solution.py:160
  2.0 0.1 shard_map.119
  2.2 2.6 %collective-permute-start.2 = (bf16[2,48,128]{2,1,0:T(8,128)(2,1)S(1)}, bf16[2,48,128]{2,1,0:T(8,128)(2,1)S(1)}, u32[]{:S(2)}, u32[]{:S(2)}) collective-permute-start(bf16[2,48,128]{2,1,0:T(8,128)(2,1)S(1)} %get-tuple-element.53), channel_id=1, source_target_pairs={{0,12},{4,8},{8,4},{12,0},{1,13},{5,9},{9,5},{13,1},{2,14},{6,10},... | collective-permute-start | bytes 73736 | tf_op jit(solution)/shard_map/ppermute | solution.py:191
  4.8 1.6 %shard_map.120 = (f32[2,4,1280]{2,1,0:T(4,128)S(1)}, bf16[24,64]{1,0:T(8,128)(2,1)S(1)}) custom-call(s32[3]{0:T(128)S(1)} %copy-done.4, bf16[2,48,128]{2,1,0:T(8,128)(2,1)S(1)} %get-tuple-element.54.source, bf16[3,224,1024]{2,1,0:T(8,128)(2,1)S(1)} %copy-done.1, bf16[3,224,1024]{2,1,0:T(8,128)(2,1)S(1)} %copy-done.2, s32[1,48]{1,0:T(1,128)S(1)} %bitcast.8), custom_call_target="tpu_custom_call" | custom-call | flops 2000000000 | tf_op jit(solution)/shard_map/pallas_call | solution.py:160
  6.4 1.2 %shard_map.121 = (bf16[4,1280]{1,0:T(4,128)(2,1)S(1)}, bf16[4,1280]{1,0:T(4,128)(2,1)S(1)}, bf16[4,1280]{1,0:T(4,128)(2,1)S(1)}, bf16[4,1280]{1,0:T(4,128)(2,1)S(1)}) custom-call(s32[3]{0:T(128)S(1)} %copy-done.4, bf16[2,48,128]{2,1,0:T(8,128)(2,1)S(1)} %collective-permute-done.2.source, f32[2,4,1280]{2,1,0:T(4,128)S(1)} %get-tuple-element.55.near, ...), custom_call_target="tpu_custom_call" | custom-call | flops 2000000000 | tf_op jit(solution)/shard_map/pallas_call | solution.py:160
  7.5 4.1 %collective-permute-start.3 = (bf16[4,1280]{1,0:T(4,128)(2,1)S(1)}, bf16[4,1280]{1,0:T(4,128)(2,1)S(1)}, u32[]{:S(2)}, u32[]{:S(2)}) collective-permute-start(bf16[4,1280]{1,0:T(4,128)(2,1)S(1)} %get-tuple-element.56), channel_id=1, source_target_pairs={{0,7},{1,6},{2,5},{3,4},{4,3},{5,2},{6,1},{7,0},{8,15},{9,14},{10,... | collective-permute-start | bytes 30728 | tf_op jit(solution)/shard_map/ppermute | solution.py:191
  11.6 0.7 %collective-permute-start.5 = (bf16[4,1280]{1,0:T(4,128)(2,1)S(1)}, bf16[4,1280]{1,0:T(4,128)(2,1)S(1)}, u32[]{:S(2)}, u32[]{:S(2)}) collective-permute-start(bf16[4,1280]{1,0:T(4,128)(2,1)S(1)} %get-tuple-element.58), channel_id=1, source_target_pairs={{0,5},{1,4},{2,7},{3,6},{4,1},{5,0},{6,3},{7,2},{8,13},{9,12},{10,... | collective-permute-start | bytes 30728 | tf_op jit(solution)/shard_map/ppermute | solution.py:191
  12.3 0.7 %collective-permute-done.3.third = bf16[4,1280]{1,0:T(4,128)(2,1)S(1)} collective-permute-done((bf16[4,1280]{1,0:T(4,128)(2,1)S(1)}, bf16[4,1280]{1,0:T(4,128)(2,1)S(1)}, u32[]{:S(2)}, u32[]{:S(2)}) %collective-permute-start.3) | collective-permute-done | bytes 10272 | tf_op jit(solution)/shard_map/ppermute | solution.py:191
  13.0 2.6 %collective-permute-done.4.second = bf16[4,1280]{1,0:T(4,128)(2,1)S(1)} collective-permute-done((bf16[4,1280]{1,0:T(4,128)(2,1)S(1)}, bf16[4,1280]{1,0:T(4,128)(2,1)S(1)}, u32[]{:S(2)}, u32[]{:S(2)}) %collective-permute-start.4) | collective-permute-done | bytes 10272 | tf_op jit(solution)/shard_map/ppermute | solution.py:191
  15.7 0.5 collective-permute-start.6
  16.2 1.2 %collective-permute-start.9 = (bf16[16,1280]{1,0:T(8,128)(2,1)S(1)}, bf16[16,1280]{1,0:T(8,128)(2,1)S(1)}, u32[]{:S(2)}, u32[]{:S(2)}) collective-permute-start(bf16[16,1280]{1,0:T(8,128)(2,1)S(1)} %shard_map.122.first), channel_id=1, source_target_pairs={{0,12},{4,8},{8,4},{12,0},{1,13},{5,9},{9,5},{13,1},{2,14},{6,10},... | collective-permute-start | bytes 122888 | tf_op jit(solution)/shard_map/ppermute | solution.py:191
  17.4 0.8 %shard_map.123 = (f32[24,1280]{1,0:T(8,128)S(1)}, bf16[24,1280]{1,0:T(8,128)(2,1)S(1)}, bf16[24,32]{1,0:T(8,128)(2,1)S(1)}, f32[24,1280]{1,0:T(8,128)S(1)}) custom-call(bf16[16,1280]{1,0:T(8,128)(2,1)S(1)} %shard_map.122.first, bf16[16,1280]{1,0:T(8,128)(2,1)S(1)} %collective-permute-done.6.second, s32[1,48]{1,0:T(1,128)S(1)} %bitcast.9, ...), custom_call_target="tpu_custom_call" | custom-call | flops 2000000000 | tf_op jit(solution)/shard_map/pallas_call | solution.py:160
  18.2 2.1 %collective-permute-start.7 = (bf16[24,1280]{1,0:T(8,128)(2,1)S(1)}, bf16[24,1280]{1,0:T(8,128)(2,1)S(1)}, u32[]{:S(2)}, u32[]{:S(2)}) collective-permute-start(bf16[24,1280]{1,0:T(8,128)(2,1)S(1)} %get-tuple-element.61.earlier), channel_id=1, source_target_pairs={{0,2},{1,3},{2,0},{3,1},{4,6},{5,7},{6,4},{7,5},{8,10},{9,11},{10,... | collective-permute-start | bytes 184328 | tf_op jit(solution)/shard_map/ppermute | solution.py:191
  20.3 1.2 %collective-permute-done.10.second = bf16[16,1280]{1,0:T(8,128)(2,1)S(1)} collective-permute-done((bf16[16,1280]{1,0:T(8,128)(2,1)S(1)}, bf16[16,1280]{1,0:T(8,128)(2,1)S(1)}, u32[]{:S(2)}, u32[]{:S(2)}) %collective-permute-start.10) | collective-permute-done | bytes 40992 | tf_op jit(solution)/shard_map/ppermute | solution.py:191
  21.5 0.7 %shard_map.126 = (f32[24,1280]{1,0:T(8,128)S(1)}, bf16[24,1280]{1,0:T(8,128)(2,1)S(1)}) custom-call(bf16[16,1280]{1,0:T(8,128)(2,1)S(1)} %collective-permute-done.9.value.first, bf16[16,1280]{1,0:T(8,128)(2,1)S(1)} %collective-permute-done.10.second, bf16[24,32]{1,0:T(8,128)(2,1)S(1)} %get-tuple-element.64.match, f32[24,1280]{1,0:T(8,128)S(1)} %get-tuple-element.65.resid, ...), custom_call_target="tpu_custom_call" | custom-call | tf_op jit(solution)/shard_map/pallas_call | solution.py:160
  22.2 0.1 collective-permute-start.11
  22.3 1.7 %collective-permute-done.7.other = bf16[24,1280]{1,0:T(8,128)(2,1)S(1)} collective-permute-done((bf16[24,1280]{1,0:T(8,128)(2,1)S(1)}, bf16[24,1280]{1,0:T(8,128)(2,1)S(1)}, u32[]{:S(2)}, u32[]{:S(2)}) %collective-permute-start.7) | collective-permute-done | bytes 61472 | tf_op jit(solution)/shard_map/ppermute | solution.py:191
  24.0 0.3 collective-permute-start.8
  24.4 2.1 %collective-permute-done.11.other = bf16[24,1280]{1,0:T(8,128)(2,1)S(1)} collective-permute-done((bf16[24,1280]{1,0:T(8,128)(2,1)S(1)}, bf16[24,1280]{1,0:T(8,128)(2,1)S(1)}, u32[]{:S(2)}, u32[]{:S(2)}) %collective-permute-start.11) | collective-permute-done | bytes 61472 | tf_op jit(solution)/shard_map/ppermute | solution.py:191
  26.5 1.6 %collective-permute-start.12 = (bf16[24,1280]{1,0:T(8,128)(2,1)S(1)}, bf16[24,1280]{1,0:T(8,128)(2,1)S(1)}, u32[]{:S(2)}, u32[]{:S(2)}) collective-permute-start(bf16[24,1280]{1,0:T(8,128)(2,1)S(1)} %get-tuple-element.69), channel_id=1, source_target_pairs={{0,2},{1,3},{2,0},{3,1},{4,6},{5,7},{6,4},{7,5},{8,10},{9,11},{10,... | collective-permute-start | bytes 184328 | tf_op jit(solution)/shard_map/ppermute | solution.py:191
  28.1 0.3 collective-permute-done.8.near_other
  28.3 3.6 %collective-permute-done.12.far_other = bf16[24,1280]{1,0:T(8,128)(2,1)S(1)} collective-permute-done((bf16[24,1280]{1,0:T(8,128)(2,1)S(1)}, bf16[24,1280]{1,0:T(8,128)(2,1)S(1)}, u32[]{:S(2)}, u32[]{:S(2)}) %collective-permute-start.12) | collective-permute-done | bytes 61472 | tf_op jit(solution)/shard_map/ppermute | solution.py:191
  32.0 1.3 %shard_map.128 = (f32[24,2688]{1,0:T(8,128)S(1)}, bf16[24,2688]{1,0:T(8,128)(2,1)S(1)}, bf16[48,1280]{1,0:T(8,128)(2,1)S(1)}, f32[12,1280]{1,0:T(8,128)S(1)}) custom-call(f32[24,1280]{1,0:T(8,128)S(1)} %get-tuple-element.62.near, bf16[24,1280]{1,0:T(8,128)(2,1)S(1)} %collective-permute-done.8.near_other, f32[24,1280]{1,0:T(8,128)S(1)} %get-tuple-element.68.far, ...), custom_call_target="tpu_custom_call" | custom-call | flops 2000000000 | tf_op jit(solution)/shard_map/pallas_call | solution.py:160
  33.3 0.1 collective-permute-start.13
  33.4 1.3 %shard_map.130 = (f32[24,2560]{1,0:T(8,128)S(1)}, bf16[24,2560]{1,0:T(8,128)(2,1)S(1)}) custom-call(bf16[48,1280]{1,0:T(8,128)(2,1)S(1)} %get-tuple-element.74.features, bf16[1280,4096]{1,0:T(8,128)(2,1)S(1)} %bitcast.2, bf16[1280,4096]{1,0:T(8,128)(2,1)S(1)} %bitcast.4, bf16[24,2688]{1,0:T(8,128)(2,1)S(1)} %get-tuple-element.71.earlier), custom_call_target="tpu_custom_call" | custom-call | tf_op jit(solution)/shard_map/pallas_call | solution.py:160
  34.6 0.5 collective-permute-start.15
  35.2 0.2 shard_map.129
  35.4 0.7 %collective-permute-start.14 = (bf16[24,2688]{1,0:T(8,128)(2,1)S(1)}, bf16[24,2688]{1,0:T(8,128)(2,1)S(1)}, u32[]{:S(2)}, u32[]{:S(2)}) collective-permute-start(bf16[24,2688]{1,0:T(8,128)(2,1)S(1)} %get-tuple-element.73.earlier), channel_id=1, source_target_pairs={{0,12},{4,8},{8,4},{12,0},{1,13},{5,9},{9,5},{13,1},{2,14},{6,10},... | collective-permute-start | bytes 387080 | tf_op jit(solution)/shard_map/ppermute | solution.py:191
  36.1 0.0 collective-permute-done.15.other
  36.2 1.1 %collective-permute-start.19 = (bf16[24,2560]{1,0:T(8,128)(2,1)S(1)}, bf16[24,2560]{1,0:T(8,128)(2,1)S(1)}, u32[]{:S(2)}, u32[]{:S(2)}) collective-permute-start(bf16[24,2560]{1,0:T(8,128)(2,1)S(1)} %get-tuple-element.77.earlier), channel_id=1, source_target_pairs={{0,12},{4,8},{8,4},{12,0},{1,13},{5,9},{9,5},{13,1},{2,14},{6,10},... | collective-permute-start | bytes 368648 | tf_op jit(solution)/shard_map/ppermute | solution.py:191
  37.3 1.0 %shard_map.132 = (f32[24,2048]{1,0:T(8,128)S(1)}, bf16[24,2048]{1,0:T(8,128)(2,1)S(1)}) custom-call(bf16[48,1280]{1,0:T(8,128)(2,1)S(1)} %get-tuple-element.74.features, bf16[1280,4096]{1,0:T(8,128)(2,1)S(1)} %bitcast.2, bf16[1280,4096]{1,0:T(8,128)(2,1)S(1)} %bitcast.4, bf16[24,2560]{1,0:T(8,128)(2,1)S(1)} %get-tuple-element.77.earlier), custom_call_target="tpu_custom_call" | custom-call | tf_op jit(solution)/shard_map/pallas_call | solution.py:160
  38.3 0.0 slice-start.6
  38.4 0.2 collective-permute-start.17
  38.6 0.6 shard_map.133
  39.2 0.4 collective-permute-start.16
  39.6 0.2 collective-permute-done.17.other
  39.8 0.9 %collective-permute-start.21 = (bf16[24,2048]{1,0:T(8,128)(2,1)S(1)}, bf16[24,2048]{1,0:T(8,128)(2,1)S(1)}, u32[]{:S(2)}, u32[]{:S(2)}) collective-permute-start(bf16[24,2048]{1,0:T(8,128)(2,1)S(1)} %get-tuple-element.82.earlier), channel_id=1, source_target_pairs={{0,12},{4,8},{8,4},{12,0},{1,13},{5,9},{9,5},{13,1},{2,14},{6,10},... | collective-permute-start | bytes 294920 | tf_op jit(solution)/shard_map/ppermute | solution.py:191
  40.7 1.0 %collective-permute-start.23 = (bf16[24,1024]{1,0:T(8,128)(2,1)S(1)}, bf16[24,1024]{1,0:T(8,128)(2,1)S(1)}, u32[]{:S(2)}, u32[]{:S(2)}) collective-permute-start(bf16[24,1024]{1,0:T(8,128)(2,1)S(1)} %get-tuple-element.83.earlier), channel_id=1, source_target_pairs={{0,12},{4,8},{8,4},{12,0},{1,13},{5,9},{9,5},{13,1},{2,14},{6,10},... | collective-permute-start | bytes 147464 | tf_op jit(solution)/shard_map/ppermute | solution.py:191
  41.7 0.2 shard_map.136
  41.9 0.2 collective-permute-start.18
  42.1 1.5 %collective-permute-done.19.other = bf16[24,2560]{1,0:T(8,128)(2,1)S(1)} collective-permute-done((bf16[24,2560]{1,0:T(8,128)(2,1)S(1)}, bf16[24,2560]{1,0:T(8,128)(2,1)S(1)}, u32[]{:S(2)}, u32[]{:S(2)}) %collective-permute-start.19) | collective-permute-done | bytes 122912 | tf_op jit(solution)/shard_map/ppermute | solution.py:191
  43.6 0.1 shard_map.138.mine
  43.7 0.6 %collective-permute-start.20 = (bf16[24,1280]{1,0:T(8,128)(2,1)S(1)}, bf16[24,1280]{1,0:T(8,128)(2,1)S(1)}, u32[]{:S(2)}, u32[]{:S(2)}) collective-permute-start(bf16[24,1280]{1,0:T(8,128)(2,1)S(1)} %shard_map.138.mine), channel_id=1, source_target_pairs={{0,4},{4,0},{8,12},{12,8},{1,5},{5,1},{9,13},{13,9},{2,6},{6,2},{1... | collective-permute-start | bytes 184328 | tf_op jit(solution)/shard_map/ppermute | solution.py:191
  44.3 0.7 %shard_map.137 = (f32[48,1280]{1,0:T(8,128)S(1)}, f32[24,640]{1,0:T(8,128)S(1)}) custom-call(bf16[24,1280]{1,0:T(8,128)(2,1)S(1)} %get-tuple-element.84.mine.earlier, bf16[24,1280]{1,0:T(8,128)(2,1)S(1)} %collective-permute-done.18.other, bf16[4096,1280]{1,0:T(8,128)(2,1)S(1)} %bitcast.6, f32[12,1280]{1,0:T(8,128)S(1)} %get-tuple-element.85.stream), custom_call_target="tpu_custom_call" | custom-call | flops 1000000000 | tf_op jit(solution)/shard_map/pallas_call | solution.py:160
  45.0 0.2 collective-permute-done.20.other
  45.2 0.7 %shard_map.139.before.earlier = f32[48,1280]{1,0:T(8,128)S(1)} custom-call(f32[48,1280]{1,0:T(8,128)S(1)} %get-tuple-element.86.before.earlier, bf16[24,1280]{1,0:T(8,128)(2,1)S(1)} %shard_map.138.mine, bf16[24,1280]{1,0:T(8,128)(2,1)S(1)} %collective-permute-done.20.other, bf16[4096,1280]{1,0:T(8,128)(2,1)S(1)} %bitcast.6), custom_call_target="tpu_custom_call" | custom-call | flops 1000000000 | tf_op jit(solution)/shard_map/pallas_call | solution.py:160
  45.9 0.1 shard_map.140.mine
  46.0 0.4 collective-permute-start.22
  46.5 0.3 collective-permute-done.23.other
  46.8 0.1 shard_map.142.mine
  46.9 0.2 collective-permute-start.24
  47.1 0.3 collective-permute-done.22.other
  47.3 0.6 %shard_map.141.before = f32[48,1280]{1,0:T(8,128)S(1)} custom-call(f32[48,1280]{1,0:T(8,128)S(1)} %shard_map.139.before.earlier, bf16[24,1024]{1,0:T(8,128)(2,1)S(1)} %shard_map.140.mine, bf16[24,1024]{1,0:T(8,128)(2,1)S(1)} %collective-permute-done.22.other, bf16[4096,1280]{1,0:T(8,128)(2,1)S(1)} %bitcast.6), custom_call_target="tpu_custom_call" | custom-call | flops 1000000000 | tf_op jit(solution)/shard_map/pallas_call | solution.py:160
  47.9 0.2 collective-permute-done.24.other
  48.1 0.4 shard_map.143
  48.5 1.1 %collective-permute-start.25 = (bf16[24,640]{1,0:T(8,128)(2,1)S(1)}, bf16[24,640]{1,0:T(8,128)(2,1)S(1)}, u32[]{:S(2)}, u32[]{:S(2)}) collective-permute-start(bf16[24,640]{1,0:T(8,128)(2,1)S(1)} %get-tuple-element.91), channel_id=1, source_target_pairs={{0,3},{1,2},{2,1},{3,0},{4,7},{5,6},{6,5},{7,4},{8,11},{9,10},{10,... | collective-permute-start | bytes 92168 | tf_op jit(solution)/shard_map/ppermute | solution.py:191
  49.6 0.4 collective-permute-start.26
  50.0 3.0 %collective-permute-start.27 = (bf16[24,640]{1,0:T(8,128)(2,1)S(1)}, bf16[24,640]{1,0:T(8,128)(2,1)S(1)}, u32[]{:S(2)}, u32[]{:S(2)}) collective-permute-start(bf16[24,640]{1,0:T(8,128)(2,1)S(1)} %get-tuple-element.93), channel_id=1, source_target_pairs={{0,1},{1,0},{2,3},{3,2},{4,5},{5,4},{6,7},{7,6},{8,9},{9,8},{10,11... | collective-permute-start | bytes 92168 | tf_op jit(solution)/shard_map/ppermute | solution.py:191
  53.0 1.4 %collective-permute-done.25.third = bf16[24,640]{1,0:T(8,128)(2,1)S(1)} collective-permute-done((bf16[24,640]{1,0:T(8,128)(2,1)S(1)}, bf16[24,640]{1,0:T(8,128)(2,1)S(1)}, u32[]{:S(2)}, u32[]{:S(2)}) %collective-permute-start.25) | collective-permute-done | bytes 30752 | tf_op jit(solution)/shard_map/ppermute | solution.py:191
  54.4 0.6 %collective-permute-done.26.second = bf16[24,640]{1,0:T(8,128)(2,1)S(1)} collective-permute-done((bf16[24,640]{1,0:T(8,128)(2,1)S(1)}, bf16[24,640]{1,0:T(8,128)(2,1)S(1)}, u32[]{:S(2)}, u32[]{:S(2)}) %collective-permute-start.26) | collective-permute-done | bytes 30752 | tf_op jit(solution)/shard_map/ppermute | solution.py:191
  55.0 0.1 collective-permute-done.27.first
  55.0 0.8 %shard_map.144 = bf16[12,1280]{1,0:T(8,128)(2,1)} custom-call(bf16[24,640]{1,0:T(8,128)(2,1)S(1)} %collective-permute-done.25.third, bf16[24,640]{1,0:T(8,128)(2,1)S(1)} %collective-permute-done.26.second, bf16[24,640]{1,0:T(8,128)(2,1)S(1)} %collective-permute-done.27.first, f32[24,640]{1,0:T(8,128)S(1)} %get-tuple-element.94.stream, ...), custom_call_target="tpu_custom_call" | custom-call | flops 2000000000 | tf_op jit(solution)/shard_map/pallas_call | solution.py:160
  (55 shorter events, 0.3 us)
Async XLA Ops:
  0.0 4.8 %copy-start.5 = (s32[48]{0:T(128)S(1)}, s32[48]{0:T(128)}, u32[]{:S(2)}) copy-start(s32[48]{0:T(128)} %param.18) | copy-start | bytes 580
  0.0 4.8 %copy-start.1 = (bf16[3,224,1024]{2,1,0:T(8,128)(2,1)S(1)}, bf16[3,224,1024]{2,1,0:T(8,128)(2,1)}, u32[]{:S(2)}) copy-start(bf16[3,224,1024]{2,1,0:T(8,128)(2,1)} %keys.3) | copy-start | bytes 4128772
  0.0 4.8 %copy-start.2 = (bf16[3,224,1024]{2,1,0:T(8,128)(2,1)S(1)}, bf16[3,224,1024]{2,1,0:T(8,128)(2,1)}, u32[]{:S(2)}) copy-start(bf16[3,224,1024]{2,1,0:T(8,128)(2,1)} %values.3) | copy-start | bytes 4128772
  0.0 4.8 %copy-start.4 = (s32[3]{0:T(128)S(1)}, s32[3]{0:T(128)}, u32[]{:S(2)}) copy-start(s32[3]{0:T(128)} %lengths.3) | copy-start | bytes 40
  0.0 2.0 %collective-permute-start = (bf16[12,1280]{1,0:T(8,128)(2,1)}, bf16[12,1280]{1,0:T(8,128)(2,1)S(1)}, u32[]{:S(2)}, u32[]{:S(2)}) collective-permute-start(bf16[12,1280]{1,0:T(8,128)(2,1)} %query.1), channel_id=1, source_target_pairs={{0,4},{4,0},{8,12},{12,8},{1,5},{5,1},{9,13},{13,9},{2,6},{6,2},{1... | collective-permute-start | bytes 92168 | tf_op jit(solution)/shard_map/ppermute | solution.py:191
  0.5 1.5 %collective-permute-start.1 = (bf16[12,512]{1,0:T(8,128)(2,1)}, bf16[12,512]{1,0:T(8,128)(2,1)S(1)}, u32[]{:S(2)}, u32[]{:S(2)}) collective-permute-start(bf16[12,512]{1,0:T(8,128)(2,1)} %pairs.1), channel_id=1, source_target_pairs={{0,4},{4,0},{8,12},{12,8},{1,5},{5,1},{9,13},{13,9},{2,6},{6,2},{1... | collective-permute-start | bytes 36872 | tf_op jit(solution)/shard_map/ppermute | solution.py:191
  2.2 4.2 %collective-permute-start.2 = (bf16[2,48,128]{2,1,0:T(8,128)(2,1)S(1)}, bf16[2,48,128]{2,1,0:T(8,128)(2,1)S(1)}, u32[]{:S(2)}, u32[]{:S(2)}) collective-permute-start(bf16[2,48,128]{2,1,0:T(8,128)(2,1)S(1)} %get-tuple-element.53), channel_id=1, source_target_pairs={{0,12},{4,8},{8,4},{12,0},{1,13},{5,9},{9,5},{13,1},{2,14},{6,10},... | collective-permute-start | bytes 73736 | tf_op jit(solution)/shard_map/ppermute | solution.py:191
  4.8 12.6 %copy-start = (bf16[1280,1280]{1,0:T(8,128)(2,1)S(1)}, bf16[1280,1280]{1,0:T(8,128)(2,1)}, u32[]{:S(2)}) copy-start(bf16[1280,1280]{1,0:T(8,128)(2,1)} %weight.7) | copy-start | bytes 9830404
  4.8 12.6 %copy-start.3 = (bf16[12,1280]{1,0:T(8,128)(2,1)S(1)}, bf16[12,1280]{1,0:T(8,128)(2,1)}, u32[]{:S(2)}) copy-start(bf16[12,1280]{1,0:T(8,128)(2,1)} %resid.1) | copy-start | bytes 92164
  7.5 5.5 %collective-permute-start.3 = (bf16[4,1280]{1,0:T(4,128)(2,1)S(1)}, bf16[4,1280]{1,0:T(4,128)(2,1)S(1)}, u32[]{:S(2)}, u32[]{:S(2)}) collective-permute-start(bf16[4,1280]{1,0:T(4,128)(2,1)S(1)} %get-tuple-element.56), channel_id=1, source_target_pairs={{0,7},{1,6},{2,5},{3,4},{4,3},{5,2},{6,1},{7,0},{8,15},{9,14},{10,... | collective-permute-start | bytes 30728 | tf_op jit(solution)/shard_map/ppermute | solution.py:191
  11.6 4.0 %collective-permute-start.4 = (bf16[4,1280]{1,0:T(4,128)(2,1)S(1)}, bf16[4,1280]{1,0:T(4,128)(2,1)S(1)}, u32[]{:S(2)}, u32[]{:S(2)}) collective-permute-start(bf16[4,1280]{1,0:T(4,128)(2,1)S(1)} %get-tuple-element.57), channel_id=1, source_target_pairs={{0,6},{1,7},{2,4},{3,5},{4,2},{5,3},{6,0},{7,1},{8,14},{9,15},{10,... | collective-permute-start | bytes 30728 | tf_op jit(solution)/shard_map/ppermute | solution.py:191
  11.6 4.0 %collective-permute-start.5 = (bf16[4,1280]{1,0:T(4,128)(2,1)S(1)}, bf16[4,1280]{1,0:T(4,128)(2,1)S(1)}, u32[]{:S(2)}, u32[]{:S(2)}) collective-permute-start(bf16[4,1280]{1,0:T(4,128)(2,1)S(1)} %get-tuple-element.58), channel_id=1, source_target_pairs={{0,5},{1,4},{2,7},{3,6},{4,1},{5,0},{6,3},{7,2},{8,13},{9,12},{10,... | collective-permute-start | bytes 30728 | tf_op jit(solution)/shard_map/ppermute | solution.py:191
  15.6 16.3 %slice-start.3 = ((s8[10485760]{0:T(1024)(128)(4,1)}), s8[4194304]{0:T(1024)(128)(4,1)S(1)}, s32[]{:S(2)}) async-start(s8[10485760]{0:T(1024)(128)(4,1)} %bitcast.3), calls=%async_computation.3 | async-start | bytes 8388608
  15.7 16.3 %slice-start.4 = ((s8[10485760]{0:T(1024)(128)(4,1)}), s8[4194304]{0:T(1024)(128)(4,1)S(1)}, s32[]{:S(2)}) async-start(s8[10485760]{0:T(1024)(128)(4,1)} %bitcast.3), calls=%async_computation.4 | async-start | bytes 8388608
  15.7 1.7 %collective-permute-start.6 = (bf16[16,1280]{1,0:T(8,128)(2,1)S(1)}, bf16[16,1280]{1,0:T(8,128)(2,1)S(1)}, u32[]{:S(2)}, u32[]{:S(2)}) collective-permute-start(bf16[16,1280]{1,0:T(8,128)(2,1)S(1)} %shard_map.122.first), channel_id=1, source_target_pairs={{0,4},{4,0},{8,12},{12,8},{1,5},{5,1},{9,13},{13,9},{2,6},{6,2},{1... | collective-permute-start | bytes 122888 | tf_op jit(solution)/shard_map/ppermute | solution.py:191
  16.2 4.1 %collective-permute-start.9 = (bf16[16,1280]{1,0:T(8,128)(2,1)S(1)}, bf16[16,1280]{1,0:T(8,128)(2,1)S(1)}, u32[]{:S(2)}, u32[]{:S(2)}) collective-permute-start(bf16[16,1280]{1,0:T(8,128)(2,1)S(1)} %shard_map.122.first), channel_id=1, source_target_pairs={{0,12},{4,8},{8,4},{12,0},{1,13},{5,9},{9,5},{13,1},{2,14},{6,10},... | collective-permute-start | bytes 122888 | tf_op jit(solution)/shard_map/ppermute | solution.py:191
  17.4 14.6 %slice-start = ((s8[10485760]{0:T(1024)(128)(4,1)}), s8[4194304]{0:T(1024)(128)(4,1)S(1)}, s32[]{:S(2)}) async-start(s8[10485760]{0:T(1024)(128)(4,1)} %bitcast.1), calls=%async_computation | async-start | bytes 8388608
  18.2 9.9 %copy-start.6 = (bf16[1280]{0:T(1024)(128)(2,1)S(1)}, bf16[1280]{0:T(1024)(128)(2,1)}, u32[]{:S(2)}) copy-start(bf16[1280]{0:T(1024)(128)(2,1)} %param.20) | copy-start | bytes 7684
  18.2 5.8 %collective-permute-start.7 = (bf16[24,1280]{1,0:T(8,128)(2,1)S(1)}, bf16[24,1280]{1,0:T(8,128)(2,1)S(1)}, u32[]{:S(2)}, u32[]{:S(2)}) collective-permute-start(bf16[24,1280]{1,0:T(8,128)(2,1)S(1)} %get-tuple-element.61.earlier), channel_id=1, source_target_pairs={{0,2},{1,3},{2,0},{3,1},{4,6},{5,7},{6,4},{7,5},{8,10},{9,11},{10,... | collective-permute-start | bytes 184328 | tf_op jit(solution)/shard_map/ppermute | solution.py:191
  20.3 1.2 %collective-permute-start.10 = (bf16[16,1280]{1,0:T(8,128)(2,1)S(1)}, bf16[16,1280]{1,0:T(8,128)(2,1)S(1)}, u32[]{:S(2)}, u32[]{:S(2)}) collective-permute-start(bf16[16,1280]{1,0:T(8,128)(2,1)S(1)} %shard_map.125), channel_id=1, source_target_pairs={{0,4},{4,0},{8,12},{12,8},{1,5},{5,1},{9,13},{13,9},{2,6},{6,2},{1... | collective-permute-start | bytes 122888 | tf_op jit(solution)/shard_map/ppermute | solution.py:191
  21.5 10.4 %slice-start.1 = ((s8[10485760]{0:T(1024)(128)(4,1)}), s8[4194304]{0:T(1024)(128)(4,1)S(1)}, s32[]{:S(2)}) async-start(s8[10485760]{0:T(1024)(128)(4,1)} %bitcast.1), calls=%async_computation.1 | async-start | bytes 8388608
  22.2 4.3 %collective-permute-start.11 = (bf16[24,1280]{1,0:T(8,128)(2,1)S(1)}, bf16[24,1280]{1,0:T(8,128)(2,1)S(1)}, u32[]{:S(2)}, u32[]{:S(2)}) collective-permute-start(bf16[24,1280]{1,0:T(8,128)(2,1)S(1)} %get-tuple-element.67), channel_id=1, source_target_pairs={{0,1},{1,0},{2,3},{3,2},{4,5},{5,4},{6,7},{7,6},{8,9},{9,8},{10,11... | collective-permute-start | bytes 184328 | tf_op jit(solution)/shard_map/ppermute | solution.py:191
  24.0 7.9 %slice-start.2 = ((s8[10485760]{0:T(1024)(128)(4,1)}), s8[2097152]{0:T(1024)(128)(4,1)S(1)}, s32[]{:S(2)}) async-start(s8[10485760]{0:T(1024)(128)(4,1)} %bitcast.1), calls=%async_computation.2 | async-start | bytes 4194304
  24.0 7.9 %slice-start.5 = ((s8[10485760]{0:T(1024)(128)(4,1)}), s8[2097152]{0:T(1024)(128)(4,1)S(1)}, s32[]{:S(2)}) async-start(s8[10485760]{0:T(1024)(128)(4,1)} %bitcast.3), calls=%async_computation.5 | async-start | bytes 4194304
  24.0 4.3 %collective-permute-start.8 = (bf16[24,1280]{1,0:T(8,128)(2,1)S(1)}, bf16[24,1280]{1,0:T(8,128)(2,1)S(1)}, u32[]{:S(2)}, u32[]{:S(2)}) collective-permute-start(bf16[24,1280]{1,0:T(8,128)(2,1)S(1)} %get-tuple-element.63), channel_id=1, source_target_pairs={{0,1},{1,0},{2,3},{3,2},{4,5},{5,4},{6,7},{7,6},{8,9},{9,8},{10,11... | collective-permute-start | bytes 184328 | tf_op jit(solution)/shard_map/ppermute | solution.py:191
  26.5 5.4 %collective-permute-start.12 = (bf16[24,1280]{1,0:T(8,128)(2,1)S(1)}, bf16[24,1280]{1,0:T(8,128)(2,1)S(1)}, u32[]{:S(2)}, u32[]{:S(2)}) collective-permute-start(bf16[24,1280]{1,0:T(8,128)(2,1)S(1)} %get-tuple-element.69), channel_id=1, source_target_pairs={{0,2},{1,3},{2,0},{3,1},{4,6},{5,7},{6,4},{7,5},{8,10},{9,11},{10,... | collective-permute-start | bytes 184328 | tf_op jit(solution)/shard_map/ppermute | solution.py:191
  33.3 1.9 %collective-permute-start.13 = (bf16[24,2688]{1,0:T(8,128)(2,1)S(1)}, bf16[24,2688]{1,0:T(8,128)(2,1)S(1)}, u32[]{:S(2)}, u32[]{:S(2)}) collective-permute-start(bf16[24,2688]{1,0:T(8,128)(2,1)S(1)} %get-tuple-element.71.earlier), channel_id=1, source_target_pairs={{0,4},{4,0},{8,12},{12,8},{1,5},{5,1},{9,13},{13,9},{2,6},{6,2},{1... | collective-permute-start | bytes 387080 | tf_op jit(solution)/shard_map/ppermute | solution.py:191
  34.6 1.5 %collective-permute-start.15 = (bf16[24,2560]{1,0:T(8,128)(2,1)S(1)}, bf16[24,2560]{1,0:T(8,128)(2,1)S(1)}, u32[]{:S(2)}, u32[]{:S(2)}) collective-permute-start(bf16[24,2560]{1,0:T(8,128)(2,1)S(1)} %get-tuple-element.76), channel_id=1, source_target_pairs={{0,4},{4,0},{8,12},{12,8},{1,5},{5,1},{9,13},{13,9},{2,6},{6,2},{1... | collective-permute-start | bytes 368648 | tf_op jit(solution)/shard_map/ppermute | solution.py:191
  35.4 6.2 %collective-permute-start.14 = (bf16[24,2688]{1,0:T(8,128)(2,1)S(1)}, bf16[24,2688]{1,0:T(8,128)(2,1)S(1)}, u32[]{:S(2)}, u32[]{:S(2)}) collective-permute-start(bf16[24,2688]{1,0:T(8,128)(2,1)S(1)} %get-tuple-element.73.earlier), channel_id=1, source_target_pairs={{0,12},{4,8},{8,4},{12,0},{1,13},{5,9},{9,5},{13,1},{2,14},{6,10},... | collective-permute-start | bytes 387080 | tf_op jit(solution)/shard_map/ppermute | solution.py:191
  36.2 7.4 %collective-permute-start.19 = (bf16[24,2560]{1,0:T(8,128)(2,1)S(1)}, bf16[24,2560]{1,0:T(8,128)(2,1)S(1)}, u32[]{:S(2)}, u32[]{:S(2)}) collective-permute-start(bf16[24,2560]{1,0:T(8,128)(2,1)S(1)} %get-tuple-element.77.earlier), channel_id=1, source_target_pairs={{0,12},{4,8},{8,4},{12,0},{1,13},{5,9},{9,5},{13,1},{2,14},{6,10},... | collective-permute-start | bytes 368648 | tf_op jit(solution)/shard_map/ppermute | solution.py:191
  38.3 6.0 %slice-start.6 = ((s8[10485760]{0:T(1024)(128)(4,1)}), s8[4194304]{0:T(1024)(128)(4,1)S(1)}, s32[]{:S(2)}) async-start(s8[10485760]{0:T(1024)(128)(4,1)} %bitcast.5), calls=%async_computation.6 | async-start | bytes 8388608
  38.3 6.0 %slice-start.7 = ((s8[10485760]{0:T(1024)(128)(4,1)}), s8[4194304]{0:T(1024)(128)(4,1)S(1)}, s32[]{:S(2)}) async-start(s8[10485760]{0:T(1024)(128)(4,1)} %bitcast.5), calls=%async_computation.7 | async-start | bytes 8388608
  38.4 6.0 %slice-start.8 = ((s8[10485760]{0:T(1024)(128)(4,1)}), s8[2097152]{0:T(1024)(128)(4,1)S(1)}, s32[]{:S(2)}) async-start(s8[10485760]{0:T(1024)(128)(4,1)} %bitcast.5), calls=%async_computation.8 | async-start | bytes 4194304
  38.4 1.4 %collective-permute-start.17 = (bf16[24,2048]{1,0:T(8,128)(2,1)S(1)}, bf16[24,2048]{1,0:T(8,128)(2,1)S(1)}, u32[]{:S(2)}, u32[]{:S(2)}) collective-permute-start(bf16[24,2048]{1,0:T(8,128)(2,1)S(1)} %get-tuple-element.78.earlier), channel_id=1, source_target_pairs={{0,4},{4,0},{8,12},{12,8},{1,5},{5,1},{9,13},{13,9},{2,6},{6,2},{1... | collective-permute-start | bytes 294920 | tf_op jit(solution)/shard_map/ppermute | solution.py:191
  39.2 1.5 %collective-permute-start.16 = (bf16[24,1024]{1,0:T(8,128)(2,1)S(1)}, bf16[24,1024]{1,0:T(8,128)(2,1)S(1)}, u32[]{:S(2)}, u32[]{:S(2)}) collective-permute-start(bf16[24,1024]{1,0:T(8,128)(2,1)S(1)} %get-tuple-element.80.earlier), channel_id=1, source_target_pairs={{0,4},{4,0},{8,12},{12,8},{1,5},{5,1},{9,13},{13,9},{2,6},{6,2},{1... | collective-permute-start | bytes 147464 | tf_op jit(solution)/shard_map/ppermute | solution.py:191
  39.8 6.1 %collective-permute-start.21 = (bf16[24,2048]{1,0:T(8,128)(2,1)S(1)}, bf16[24,2048]{1,0:T(8,128)(2,1)S(1)}, u32[]{:S(2)}, u32[]{:S(2)}) collective-permute-start(bf16[24,2048]{1,0:T(8,128)(2,1)S(1)} %get-tuple-element.82.earlier), channel_id=1, source_target_pairs={{0,12},{4,8},{8,4},{12,0},{1,13},{5,9},{9,5},{13,1},{2,14},{6,10},... | collective-permute-start | bytes 294920 | tf_op jit(solution)/shard_map/ppermute | solution.py:191
  40.7 6.1 %collective-permute-start.23 = (bf16[24,1024]{1,0:T(8,128)(2,1)S(1)}, bf16[24,1024]{1,0:T(8,128)(2,1)S(1)}, u32[]{:S(2)}, u32[]{:S(2)}) collective-permute-start(bf16[24,1024]{1,0:T(8,128)(2,1)S(1)} %get-tuple-element.83.earlier), channel_id=1, source_target_pairs={{0,12},{4,8},{8,4},{12,0},{1,13},{5,9},{9,5},{13,1},{2,14},{6,10},... | collective-permute-start | bytes 147464 | tf_op jit(solution)/shard_map/ppermute | solution.py:191
  41.9 2.5 %collective-permute-start.18 = (bf16[24,1280]{1,0:T(8,128)(2,1)S(1)}, bf16[24,1280]{1,0:T(8,128)(2,1)S(1)}, u32[]{:S(2)}, u32[]{:S(2)}) collective-permute-start(bf16[24,1280]{1,0:T(8,128)(2,1)S(1)} %get-tuple-element.84.mine.earlier), channel_id=1, source_target_pairs={{0,4},{4,0},{8,12},{12,8},{1,5},{5,1},{9,13},{13,9},{2,6},{6,2},{1... | collective-permute-start | bytes 184328 | tf_op jit(solution)/shard_map/ppermute | solution.py:191
  43.7 1.5 %collective-permute-start.20 = (bf16[24,1280]{1,0:T(8,128)(2,1)S(1)}, bf16[24,1280]{1,0:T(8,128)(2,1)S(1)}, u32[]{:S(2)}, u32[]{:S(2)}) collective-permute-start(bf16[24,1280]{1,0:T(8,128)(2,1)S(1)} %shard_map.138.mine), channel_id=1, source_target_pairs={{0,4},{4,0},{8,12},{12,8},{1,5},{5,1},{9,13},{13,9},{2,6},{6,2},{1... | collective-permute-start | bytes 184328 | tf_op jit(solution)/shard_map/ppermute | solution.py:191
  46.0 1.3 %collective-permute-start.22 = (bf16[24,1024]{1,0:T(8,128)(2,1)S(1)}, bf16[24,1024]{1,0:T(8,128)(2,1)S(1)}, u32[]{:S(2)}, u32[]{:S(2)}) collective-permute-start(bf16[24,1024]{1,0:T(8,128)(2,1)S(1)} %shard_map.140.mine), channel_id=1, source_target_pairs={{0,4},{4,0},{8,12},{12,8},{1,5},{5,1},{9,13},{13,9},{2,6},{6,2},{1... | collective-permute-start | bytes 147464 | tf_op jit(solution)/shard_map/ppermute | solution.py:191
  46.9 1.3 %collective-permute-start.24 = (bf16[24,512]{1,0:T(8,128)(2,1)S(1)}, bf16[24,512]{1,0:T(8,128)(2,1)S(1)}, u32[]{:S(2)}, u32[]{:S(2)}) collective-permute-start(bf16[24,512]{1,0:T(8,128)(2,1)S(1)} %shard_map.142.mine), channel_id=1, source_target_pairs={{0,4},{4,0},{8,12},{12,8},{1,5},{5,1},{9,13},{13,9},{2,6},{6,2},{1... | collective-permute-start | bytes 73736 | tf_op jit(solution)/shard_map/ppermute | solution.py:191
  48.5 5.9 %collective-permute-start.25 = (bf16[24,640]{1,0:T(8,128)(2,1)S(1)}, bf16[24,640]{1,0:T(8,128)(2,1)S(1)}, u32[]{:S(2)}, u32[]{:S(2)}) collective-permute-start(bf16[24,640]{1,0:T(8,128)(2,1)S(1)} %get-tuple-element.91), channel_id=1, source_target_pairs={{0,3},{1,2},{2,1},{3,0},{4,7},{5,6},{6,5},{7,4},{8,11},{9,10},{10,... | collective-permute-start | bytes 92168 | tf_op jit(solution)/shard_map/ppermute | solution.py:191
  49.6 5.4 %collective-permute-start.26 = (bf16[24,640]{1,0:T(8,128)(2,1)S(1)}, bf16[24,640]{1,0:T(8,128)(2,1)S(1)}, u32[]{:S(2)}, u32[]{:S(2)}) collective-permute-start(bf16[24,640]{1,0:T(8,128)(2,1)S(1)} %get-tuple-element.92), channel_id=1, source_target_pairs={{0,2},{1,3},{2,0},{3,1},{4,6},{5,7},{6,4},{7,5},{8,10},{9,11},{10,... | collective-permute-start | bytes 92168 | tf_op jit(solution)/shard_map/ppermute | solution.py:191
  50.0 5.0 %collective-permute-start.27 = (bf16[24,640]{1,0:T(8,128)(2,1)S(1)}, bf16[24,640]{1,0:T(8,128)(2,1)S(1)}, u32[]{:S(2)}, u32[]{:S(2)}) collective-permute-start(bf16[24,640]{1,0:T(8,128)(2,1)S(1)} %get-tuple-element.93), channel_id=1, source_target_pairs={{0,1},{1,0},{2,3},{3,2},{4,5},{5,4},{6,7},{7,6},{8,9},{9,8},{10,11... | collective-permute-start | bytes 92168 | tf_op jit(solution)/shard_map/ppermute | solution.py:191

commit v15 on v14

--- a/solution.py
+++ b/solution.py
@@ -166,15 +166,6 @@
         compiler_params=pltpu.CompilerParams(vmem_limit_bytes=limit * MIB),
         cost_estimate=pl.CostEstimate(flops=nanos * 10**6, bytes_accessed=0, transcendentals=0),
     )(*placed)
-
-
-def copy_kernel(value, earlier, out):
-    out[...] = value[...]
-
-
-def after(value, earlier):
-    (value,) = call(copy_kernel, [(value.shape, value.dtype)], (value, earlier), free=(1,), nanos=0)
-    return value
 
 
 def constrained(operand, space):
@@ -604,7 +595,7 @@
         (own, beside, assign, resid, out_weight),
         resident=(4,),
     )
-    corner = swap(after(across, near[1]), "sec", 1)
+    corner = swap(own, "sec", 2)
     far = call(project_far_kernel, pair, (across, corner, match, rows, out_weight), resident=(4,), nanos=0)
     sums = tp_sum(*near, 2, 1) + tp_sum(*far, 1, 2)
 

time: 55.9 us -> 59 us (1.055)
  waiting for transfers between devices: 17 us -> 20.4 us
    ppermute x28, waiting for transfers between devices: 17 us -> 20.4 us  [swap(): return lax.ppermute(value, axis, [(i, i ^ step) for i in range(total)])]
    pallas_call x27 -> x26, Pallas kernels: 13.9 us -> 13.9 us  [call(): pl.pallas_call(kernel, out_shape=[jax.ShapeDtypeStruct(shape, dtype) for...]
  transfers between devices with their start and end apart: 28 -> 28, of which waited for: 16 -> 16; matrix products, arithmetic and copies ran while one was open for 0% -> 0% of each run, Pallas kernels for 18% -> 16%
where the time goes in v15:
time: 59 us; the launch traced here: 58.9 us
  starting transfers between devices  24.2 us (41%)
  waiting for transfers between devices  20.4 us (35%)
  Pallas kernels  13.9 us (24%)
    ppermute x28, starting transfers between devices, swap(): return lax.ppermute(value, axis, [(i, i ^ step) for i in range(total)])  24.2 us
    ppermute x28, waiting for transfers between devices, swap(): return lax.ppermute(value, axis, [(i, i ^ step) for i in range(total)])  20.4 us
    pallas_call x26, Pallas kernels, call(): pl.pallas_call(kernel, out_shape=[jax.ShapeDtypeStruct(shape, dtype) for...  13.9 us
  transfers between devices with their start and end apart: 28, of which 16 were waited for; matrix products, arithmetic and copies ran while one was open for 0% of the time, Pallas kernels for 16%

profile of v15, /device:TPU:0, one launch (start us, length us, event | category | flops | bytes accessed | tf_op | source)
XLA Modules:
  0.0 58.9 jit_solution(2805771238560399405)
XLA Ops:
  0.0 0.5 collective-permute-start
  0.5 0.1 collective-permute-start.1
  0.6 1.4 %shard_map.118 = (bf16[2,48,128]{2,1,0:T(8,128)(2,1)S(1)}, bf16[16,12]{1,0:T(8,128)(2,1)S(1)}) custom-call(bf16[12,1280]{1,0:T(8,128)(2,1)} %query.1, bf16[12,512]{1,0:T(8,128)(2,1)} %pairs.1, s32[1,48]{1,0:T(1,128)} %bitcast.7), custom_call_target="tpu_custom_call" | custom-call | flops 2000000000 | tf_op jit(solution)/shard_map/pallas_call | solution.py:160
  2.0 0.1 shard_map.119
  2.2 2.6 %collective-permute-start.2 = (bf16[2,48,128]{2,1,0:T(8,128)(2,1)S(1)}, bf16[2,48,128]{2,1,0:T(8,128)(2,1)S(1)}, u32[]{:S(2)}, u32[]{:S(2)}) collective-permute-start(bf16[2,48,128]{2,1,0:T(8,128)(2,1)S(1)} %get-tuple-element.53), channel_id=1, source_target_pairs={{0,12},{4,8},{8,4},{12,0},{1,13},{5,9},{9,5},{13,1},{2,14},{6,10},... | collective-permute-start | bytes 73736 | tf_op jit(solution)/shard_map/ppermute | solution.py:182
  4.8 1.6 %shard_map.120 = (f32[2,4,1280]{2,1,0:T(4,128)S(1)}, bf16[24,64]{1,0:T(8,128)(2,1)S(1)}) custom-call(s32[3]{0:T(128)S(1)} %copy-done.4, bf16[2,48,128]{2,1,0:T(8,128)(2,1)S(1)} %get-tuple-element.54.source, bf16[3,224,1024]{2,1,0:T(8,128)(2,1)S(1)} %copy-done.1, bf16[3,224,1024]{2,1,0:T(8,128)(2,1)S(1)} %copy-done.2, s32[1,48]{1,0:T(1,128)S(1)} %bitcast.8), custom_call_target="tpu_custom_call" | custom-call | flops 2000000000 | tf_op jit(solution)/shard_map/pallas_call | solution.py:160
  6.4 1.2 %shard_map.121 = (bf16[4,1280]{1,0:T(4,128)(2,1)S(1)}, bf16[4,1280]{1,0:T(4,128)(2,1)S(1)}, bf16[4,1280]{1,0:T(4,128)(2,1)S(1)}, bf16[4,1280]{1,0:T(4,128)(2,1)S(1)}) custom-call(s32[3]{0:T(128)S(1)} %copy-done.4, bf16[2,48,128]{2,1,0:T(8,128)(2,1)S(1)} %collective-permute-done.2.source, f32[2,4,1280]{2,1,0:T(4,128)S(1)} %get-tuple-element.55.near, ...), custom_call_target="tpu_custom_call" | custom-call | flops 2000000000 | tf_op jit(solution)/shard_map/pallas_call | solution.py:160
  7.5 4.1 %collective-permute-start.3 = (bf16[4,1280]{1,0:T(4,128)(2,1)S(1)}, bf16[4,1280]{1,0:T(4,128)(2,1)S(1)}, u32[]{:S(2)}, u32[]{:S(2)}) collective-permute-start(bf16[4,1280]{1,0:T(4,128)(2,1)S(1)} %get-tuple-element.56), channel_id=1, source_target_pairs={{0,7},{1,6},{2,5},{3,4},{4,3},{5,2},{6,1},{7,0},{8,15},{9,14},{10,... | collective-permute-start | bytes 30728 | tf_op jit(solution)/shard_map/ppermute | solution.py:182
  11.6 0.7 %collective-permute-start.5 = (bf16[4,1280]{1,0:T(4,128)(2,1)S(1)}, bf16[4,1280]{1,0:T(4,128)(2,1)S(1)}, u32[]{:S(2)}, u32[]{:S(2)}) collective-permute-start(bf16[4,1280]{1,0:T(4,128)(2,1)S(1)} %get-tuple-element.58), channel_id=1, source_target_pairs={{0,5},{1,4},{2,7},{3,6},{4,1},{5,0},{6,3},{7,2},{8,13},{9,12},{10,... | collective-permute-start | bytes 30728 | tf_op jit(solution)/shard_map/ppermute | solution.py:182
  12.3 0.7 %collective-permute-done.3.third = bf16[4,1280]{1,0:T(4,128)(2,1)S(1)} collective-permute-done((bf16[4,1280]{1,0:T(4,128)(2,1)S(1)}, bf16[4,1280]{1,0:T(4,128)(2,1)S(1)}, u32[]{:S(2)}, u32[]{:S(2)}) %collective-permute-start.3) | collective-permute-done | bytes 10272 | tf_op jit(solution)/shard_map/ppermute | solution.py:182
  13.0 2.6 %collective-permute-done.4.second = bf16[4,1280]{1,0:T(4,128)(2,1)S(1)} collective-permute-done((bf16[4,1280]{1,0:T(4,128)(2,1)S(1)}, bf16[4,1280]{1,0:T(4,128)(2,1)S(1)}, u32[]{:S(2)}, u32[]{:S(2)}) %collective-permute-start.4) | collective-permute-done | bytes 10272 | tf_op jit(solution)/shard_map/ppermute | solution.py:182
  15.7 0.0 slice-start.4
  15.7 0.5 collective-permute-start.6
  16.2 1.5 %collective-permute-start.10 = (bf16[16,1280]{1,0:T(8,128)(2,1)S(1)}, bf16[16,1280]{1,0:T(8,128)(2,1)S(1)}, u32[]{:S(2)}, u32[]{:S(2)}) collective-permute-start(bf16[16,1280]{1,0:T(8,128)(2,1)S(1)} %shard_map.122.first), channel_id=1, source_target_pairs={{0,8},{4,12},{8,0},{12,4},{1,9},{5,13},{9,1},{13,5},{2,10},{6,14},... | collective-permute-start | bytes 122888 | tf_op jit(solution)/shard_map/ppermute | solution.py:182
  17.7 0.0 slice-start
  17.7 0.8 %shard_map.123 = (f32[24,1280]{1,0:T(8,128)S(1)}, bf16[24,1280]{1,0:T(8,128)(2,1)S(1)}, bf16[24,32]{1,0:T(8,128)(2,1)S(1)}, f32[24,1280]{1,0:T(8,128)S(1)}) custom-call(bf16[16,1280]{1,0:T(8,128)(2,1)S(1)} %shard_map.122.first, bf16[16,1280]{1,0:T(8,128)(2,1)S(1)} %collective-permute-done.6.second, s32[1,48]{1,0:T(1,128)S(1)} %bitcast.9, ...), custom_call_target="tpu_custom_call" | custom-call | flops 2000000000 | tf_op jit(solution)/shard_map/pallas_call | solution.py:160
  18.5 1.7 %collective-permute-done.10.second = bf16[16,1280]{1,0:T(8,128)(2,1)S(1)} collective-permute-done((bf16[16,1280]{1,0:T(8,128)(2,1)S(1)}, bf16[16,1280]{1,0:T(8,128)(2,1)S(1)}, u32[]{:S(2)}, u32[]{:S(2)}) %collective-permute-start.10) | collective-permute-done | bytes 40992 | tf_op jit(solution)/shard_map/ppermute | solution.py:182
  20.2 1.3 %collective-permute-done.9.first = bf16[16,1280]{1,0:T(8,128)(2,1)S(1)} collective-permute-done((bf16[16,1280]{1,0:T(8,128)(2,1)S(1)}, bf16[16,1280]{1,0:T(8,128)(2,1)S(1)}, u32[]{:S(2)}, u32[]{:S(2)}) %collective-permute-start.9) | collective-permute-done | bytes 40992 | tf_op jit(solution)/shard_map/ppermute | solution.py:182
  21.5 0.7 %shard_map.125 = (f32[24,1280]{1,0:T(8,128)S(1)}, bf16[24,1280]{1,0:T(8,128)(2,1)S(1)}) custom-call(bf16[16,1280]{1,0:T(8,128)(2,1)S(1)} %collective-permute-done.9.first, bf16[16,1280]{1,0:T(8,128)(2,1)S(1)} %collective-permute-done.10.second, bf16[24,32]{1,0:T(8,128)(2,1)S(1)} %get-tuple-element.64.match, f32[24,1280]{1,0:T(8,128)S(1)} %get-tuple-element.65.resid, ...), custom_call_target="tpu_custom_call" | custom-call | tf_op jit(solution)/shard_map/pallas_call | solution.py:160
  22.2 0.1 collective-permute-start.11
  22.3 2.0 %collective-permute-start.7 = (bf16[24,1280]{1,0:T(8,128)(2,1)S(1)}, bf16[24,1280]{1,0:T(8,128)(2,1)S(1)}, u32[]{:S(2)}, u32[]{:S(2)}) collective-permute-start(bf16[24,1280]{1,0:T(8,128)(2,1)S(1)} %get-tuple-element.61), channel_id=1, source_target_pairs={{0,2},{1,3},{2,0},{3,1},{4,6},{5,7},{6,4},{7,5},{8,10},{9,11},{10,... | collective-permute-start | bytes 184328 | tf_op jit(solution)/shard_map/ppermute | solution.py:182
  24.3 3.4 %collective-permute-done.11.other = bf16[24,1280]{1,0:T(8,128)(2,1)S(1)} collective-permute-done((bf16[24,1280]{1,0:T(8,128)(2,1)S(1)}, bf16[24,1280]{1,0:T(8,128)(2,1)S(1)}, u32[]{:S(2)}, u32[]{:S(2)}) %collective-permute-start.11) | collective-permute-done | bytes 61472 | tf_op jit(solution)/shard_map/ppermute | solution.py:182
  27.7 0.8 %collective-permute-start.12 = (bf16[24,1280]{1,0:T(8,128)(2,1)S(1)}, bf16[24,1280]{1,0:T(8,128)(2,1)S(1)}, u32[]{:S(2)}, u32[]{:S(2)}) collective-permute-start(bf16[24,1280]{1,0:T(8,128)(2,1)S(1)} %get-tuple-element.69), channel_id=1, source_target_pairs={{0,2},{1,3},{2,0},{3,1},{4,6},{5,7},{6,4},{7,5},{8,10},{9,11},{10,... | collective-permute-start | bytes 184328 | tf_op jit(solution)/shard_map/ppermute | solution.py:182
  28.5 0.9 %collective-permute-start.8 = (bf16[24,1280]{1,0:T(8,128)(2,1)S(1)}, bf16[24,1280]{1,0:T(8,128)(2,1)S(1)}, u32[]{:S(2)}, u32[]{:S(2)}) collective-permute-start(bf16[24,1280]{1,0:T(8,128)(2,1)S(1)} %get-tuple-element.63), channel_id=1, source_target_pairs={{0,1},{1,0},{2,3},{3,2},{4,5},{5,4},{6,7},{7,6},{8,9},{9,8},{10,11... | collective-permute-start | bytes 184328 | tf_op jit(solution)/shard_map/ppermute | solution.py:182
  29.5 3.5 %collective-permute-done.12.far_other = bf16[24,1280]{1,0:T(8,128)(2,1)S(1)} collective-permute-done((bf16[24,1280]{1,0:T(8,128)(2,1)S(1)}, bf16[24,1280]{1,0:T(8,128)(2,1)S(1)}, u32[]{:S(2)}, u32[]{:S(2)}) %collective-permute-start.12) | collective-permute-done | bytes 61472 | tf_op jit(solution)/shard_map/ppermute | solution.py:182
  33.0 0.5 collective-permute-done.8.near_other
  33.5 1.3 %shard_map.127 = (f32[24,2688]{1,0:T(8,128)S(1)}, bf16[24,2688]{1,0:T(8,128)(2,1)S(1)}, bf16[48,1280]{1,0:T(8,128)(2,1)S(1)}, f32[12,1280]{1,0:T(8,128)S(1)}) custom-call(f32[24,1280]{1,0:T(8,128)S(1)} %get-tuple-element.62.near, bf16[24,1280]{1,0:T(8,128)(2,1)S(1)} %collective-permute-done.8.near_other, f32[24,1280]{1,0:T(8,128)S(1)} %get-tuple-element.68.far, ...), custom_call_target="tpu_custom_call" | custom-call | flops 2000000000 | tf_op jit(solution)/shard_map/pallas_call | solution.py:160
  34.9 0.1 collective-permute-start.13
  34.9 1.3 %shard_map.129 = (f32[24,2560]{1,0:T(8,128)S(1)}, bf16[24,2560]{1,0:T(8,128)(2,1)S(1)}) custom-call(bf16[48,1280]{1,0:T(8,128)(2,1)S(1)} %get-tuple-element.74.features, bf16[1280,4096]{1,0:T(8,128)(2,1)S(1)} %bitcast.2, bf16[1280,4096]{1,0:T(8,128)(2,1)S(1)} %bitcast.4, bf16[24,2688]{1,0:T(8,128)(2,1)S(1)} %get-tuple-element.71.earlier), custom_call_target="tpu_custom_call" | custom-call | tf_op jit(solution)/shard_map/pallas_call | solution.py:160
  36.2 0.5 collective-permute-start.15
  36.7 0.2 shard_map.128
  37.0 0.4 collective-permute-start.14
  37.3 0.4 collective-permute-done.15.other
  37.7 1.1 %collective-permute-start.19 = (bf16[24,2560]{1,0:T(8,128)(2,1)S(1)}, bf16[24,2560]{1,0:T(8,128)(2,1)S(1)}, u32[]{:S(2)}, u32[]{:S(2)}) collective-permute-start(bf16[24,2560]{1,0:T(8,128)(2,1)S(1)} %get-tuple-element.77.earlier), channel_id=1, source_target_pairs={{0,12},{4,8},{8,4},{12,0},{1,13},{5,9},{9,5},{13,1},{2,14},{6,10},... | collective-permute-start | bytes 368648 | tf_op jit(solution)/shard_map/ppermute | solution.py:182
  38.8 1.0 %shard_map.131 = (f32[24,2048]{1,0:T(8,128)S(1)}, bf16[24,2048]{1,0:T(8,128)(2,1)S(1)}) custom-call(bf16[48,1280]{1,0:T(8,128)(2,1)S(1)} %get-tuple-element.74.features, bf16[1280,4096]{1,0:T(8,128)(2,1)S(1)} %bitcast.2, bf16[1280,4096]{1,0:T(8,128)(2,1)S(1)} %bitcast.4, bf16[24,2560]{1,0:T(8,128)(2,1)S(1)} %get-tuple-element.77.earlier), custom_call_target="tpu_custom_call" | custom-call | tf_op jit(solution)/shard_map/pallas_call | solution.py:160
  39.9 0.0 slice-start.6
  39.9 0.1 collective-permute-start.17
  40.0 0.6 shard_map.132
  40.5 0.5 collective-permute-start.16
  41.1 0.2 collective-permute-done.17.other
  41.3 0.8 %collective-permute-start.21 = (bf16[24,2048]{1,0:T(8,128)(2,1)S(1)}, bf16[24,2048]{1,0:T(8,128)(2,1)S(1)}, u32[]{:S(2)}, u32[]{:S(2)}) collective-permute-start(bf16[24,2048]{1,0:T(8,128)(2,1)S(1)} %get-tuple-element.82.earlier), channel_id=1, source_target_pairs={{0,12},{4,8},{8,4},{12,0},{1,13},{5,9},{9,5},{13,1},{2,14},{6,10},... | collective-permute-start | bytes 294920 | tf_op jit(solution)/shard_map/ppermute | solution.py:182
  42.1 1.1 %collective-permute-start.23 = (bf16[24,1024]{1,0:T(8,128)(2,1)S(1)}, bf16[24,1024]{1,0:T(8,128)(2,1)S(1)}, u32[]{:S(2)}, u32[]{:S(2)}) collective-permute-start(bf16[24,1024]{1,0:T(8,128)(2,1)S(1)} %get-tuple-element.83.earlier), channel_id=1, source_target_pairs={{0,12},{4,8},{8,4},{12,0},{1,13},{5,9},{9,5},{13,1},{2,14},{6,10},... | collective-permute-start | bytes 147464 | tf_op jit(solution)/shard_map/ppermute | solution.py:182
  43.2 0.2 shard_map.135
  43.4 0.2 collective-permute-start.18
  43.6 1.5 %collective-permute-done.19.other = bf16[24,2560]{1,0:T(8,128)(2,1)S(1)} collective-permute-done((bf16[24,2560]{1,0:T(8,128)(2,1)S(1)}, bf16[24,2560]{1,0:T(8,128)(2,1)S(1)}, u32[]{:S(2)}, u32[]{:S(2)}) %collective-permute-start.19) | collective-permute-done | bytes 122912 | tf_op jit(solution)/shard_map/ppermute | solution.py:182
  45.2 0.1 shard_map.137.mine
  45.3 0.6 collective-permute-start.20
  45.9 0.7 %shard_map.136 = (f32[48,1280]{1,0:T(8,128)S(1)}, f32[24,640]{1,0:T(8,128)S(1)}) custom-call(bf16[24,1280]{1,0:T(8,128)(2,1)S(1)} %get-tuple-element.84.mine.earlier, bf16[24,1280]{1,0:T(8,128)(2,1)S(1)} %collective-permute-done.18.other, bf16[4096,1280]{1,0:T(8,128)(2,1)S(1)} %bitcast.6, f32[12,1280]{1,0:T(8,128)S(1)} %get-tuple-element.85.stream), custom_call_target="tpu_custom_call" | custom-call | flops 1000000000 | tf_op jit(solution)/shard_map/pallas_call | solution.py:160
  46.6 0.2 collective-permute-done.20.other
  46.8 0.7 %shard_map.138.before.earlier = f32[48,1280]{1,0:T(8,128)S(1)} custom-call(f32[48,1280]{1,0:T(8,128)S(1)} %get-tuple-element.86.before.earlier, bf16[24,1280]{1,0:T(8,128)(2,1)S(1)} %shard_map.137.mine, bf16[24,1280]{1,0:T(8,128)(2,1)S(1)} %collective-permute-done.20.other, bf16[4096,1280]{1,0:T(8,128)(2,1)S(1)} %bitcast.6), custom_call_target="tpu_custom_call" | custom-call | flops 1000000000 | tf_op jit(solution)/shard_map/pallas_call | solution.py:160
  47.5 0.1 shard_map.139.mine
  47.6 0.4 collective-permute-start.22
  48.0 0.3 collective-permute-done.23.other
  48.3 0.1 shard_map.141.mine
  48.4 0.2 collective-permute-start.24
  48.6 0.3 collective-permute-done.22.other
  48.9 0.6 shard_map.140.before
  49.5 0.2 collective-permute-done.24.other
  49.7 0.4 shard_map.142
  50.1 3.2 %collective-permute-start.25 = (bf16[24,640]{1,0:T(8,128)(2,1)S(1)}, bf16[24,640]{1,0:T(8,128)(2,1)S(1)}, u32[]{:S(2)}, u32[]{:S(2)}) collective-permute-start(bf16[24,640]{1,0:T(8,128)(2,1)S(1)} %get-tuple-element.91), channel_id=1, source_target_pairs={{0,3},{1,2},{2,1},{3,0},{4,7},{5,6},{6,5},{7,4},{8,11},{9,10},{10,... | collective-permute-start | bytes 92168 | tf_op jit(solution)/shard_map/ppermute | solution.py:182
  53.3 1.2 %collective-permute-start.27 = (bf16[24,640]{1,0:T(8,128)(2,1)S(1)}, bf16[24,640]{1,0:T(8,128)(2,1)S(1)}, u32[]{:S(2)}, u32[]{:S(2)}) collective-permute-start(bf16[24,640]{1,0:T(8,128)(2,1)S(1)} %get-tuple-element.93), channel_id=1, source_target_pairs={{0,1},{1,0},{2,3},{3,2},{4,5},{5,4},{6,7},{7,6},{8,9},{9,8},{10,11... | collective-permute-start | bytes 92168 | tf_op jit(solution)/shard_map/ppermute | solution.py:182
  54.5 1.3 %collective-permute-done.25.third = bf16[24,640]{1,0:T(8,128)(2,1)S(1)} collective-permute-done((bf16[24,640]{1,0:T(8,128)(2,1)S(1)}, bf16[24,640]{1,0:T(8,128)(2,1)S(1)}, u32[]{:S(2)}, u32[]{:S(2)}) %collective-permute-start.25) | collective-permute-done | bytes 30752 | tf_op jit(solution)/shard_map/ppermute | solution.py:182
  55.9 2.2 %collective-permute-done.26.second = bf16[24,640]{1,0:T(8,128)(2,1)S(1)} collective-permute-done((bf16[24,640]{1,0:T(8,128)(2,1)S(1)}, bf16[24,640]{1,0:T(8,128)(2,1)S(1)}, u32[]{:S(2)}, u32[]{:S(2)}) %collective-permute-start.26) | collective-permute-done | bytes 30752 | tf_op jit(solution)/shard_map/ppermute | solution.py:182
  58.1 0.8 %shard_map.143 = bf16[12,1280]{1,0:T(8,128)(2,1)} custom-call(bf16[24,640]{1,0:T(8,128)(2,1)S(1)} %collective-permute-done.25.third, bf16[24,640]{1,0:T(8,128)(2,1)S(1)} %collective-permute-done.26.second, bf16[24,640]{1,0:T(8,128)(2,1)S(1)} %collective-permute-done.27.first, f32[24,640]{1,0:T(8,128)S(1)} %get-tuple-element.94.stream, ...), custom_call_target="tpu_custom_call" | custom-call | flops 2000000000 | tf_op jit(solution)/shard_map/pallas_call | solution.py:160
  (54 shorter events, 0.2 us)
Async XLA Ops:
  0.0 4.8 %copy-start.5 = (s32[48]{0:T(128)S(1)}, s32[48]{0:T(128)}, u32[]{:S(2)}) copy-start(s32[48]{0:T(128)} %param.18) | copy-start | bytes 580
  0.0 4.8 %copy-start.1 = (bf16[3,224,1024]{2,1,0:T(8,128)(2,1)S(1)}, bf16[3,224,1024]{2,1,0:T(8,128)(2,1)}, u32[]{:S(2)}) copy-start(bf16[3,224,1024]{2,1,0:T(8,128)(2,1)} %keys.3) | copy-start | bytes 4128772
  0.0 4.8 %copy-start.2 = (bf16[3,224,1024]{2,1,0:T(8,128)(2,1)S(1)}, bf16[3,224,1024]{2,1,0:T(8,128)(2,1)}, u32[]{:S(2)}) copy-start(bf16[3,224,1024]{2,1,0:T(8,128)(2,1)} %values.3) | copy-start | bytes 4128772
  0.0 4.8 %copy-start.4 = (s32[3]{0:T(128)S(1)}, s32[3]{0:T(128)}, u32[]{:S(2)}) copy-start(s32[3]{0:T(128)} %lengths.3) | copy-start | bytes 40
  0.0 2.0 %collective-permute-start = (bf16[12,1280]{1,0:T(8,128)(2,1)}, bf16[12,1280]{1,0:T(8,128)(2,1)S(1)}, u32[]{:S(2)}, u32[]{:S(2)}) collective-permute-start(bf16[12,1280]{1,0:T(8,128)(2,1)} %query.1), channel_id=1, source_target_pairs={{0,4},{4,0},{8,12},{12,8},{1,5},{5,1},{9,13},{13,9},{2,6},{6,2},{1... | collective-permute-start | bytes 92168 | tf_op jit(solution)/shard_map/ppermute | solution.py:182
  0.5 1.5 %collective-permute-start.1 = (bf16[12,512]{1,0:T(8,128)(2,1)}, bf16[12,512]{1,0:T(8,128)(2,1)S(1)}, u32[]{:S(2)}, u32[]{:S(2)}) collective-permute-start(bf16[12,512]{1,0:T(8,128)(2,1)} %pairs.1), channel_id=1, source_target_pairs={{0,4},{4,0},{8,12},{12,8},{1,5},{5,1},{9,13},{13,9},{2,6},{6,2},{1... | collective-permute-start | bytes 36872 | tf_op jit(solution)/shard_map/ppermute | solution.py:182
  2.2 4.2 %collective-permute-start.2 = (bf16[2,48,128]{2,1,0:T(8,128)(2,1)S(1)}, bf16[2,48,128]{2,1,0:T(8,128)(2,1)S(1)}, u32[]{:S(2)}, u32[]{:S(2)}) collective-permute-start(bf16[2,48,128]{2,1,0:T(8,128)(2,1)S(1)} %get-tuple-element.53), channel_id=1, source_target_pairs={{0,12},{4,8},{8,4},{12,0},{1,13},{5,9},{9,5},{13,1},{2,14},{6,10},... | collective-permute-start | bytes 73736 | tf_op jit(solution)/shard_map/ppermute | solution.py:182
  4.8 12.9 %copy-start = (bf16[1280,1280]{1,0:T(8,128)(2,1)S(1)}, bf16[1280,1280]{1,0:T(8,128)(2,1)}, u32[]{:S(2)}) copy-start(bf16[1280,1280]{1,0:T(8,128)(2,1)} %weight.7) | copy-start | bytes 9830404
  4.8 12.9 %copy-start.3 = (bf16[12,1280]{1,0:T(8,128)(2,1)S(1)}, bf16[12,1280]{1,0:T(8,128)(2,1)}, u32[]{:S(2)}) copy-start(bf16[12,1280]{1,0:T(8,128)(2,1)} %resid.1) | copy-start | bytes 92164
  7.5 5.5 %collective-permute-start.3 = (bf16[4,1280]{1,0:T(4,128)(2,1)S(1)}, bf16[4,1280]{1,0:T(4,128)(2,1)S(1)}, u32[]{:S(2)}, u32[]{:S(2)}) collective-permute-start(bf16[4,1280]{1,0:T(4,128)(2,1)S(1)} %get-tuple-element.56), channel_id=1, source_target_pairs={{0,7},{1,6},{2,5},{3,4},{4,3},{5,2},{6,1},{7,0},{8,15},{9,14},{10,... | collective-permute-start | bytes 30728 | tf_op jit(solution)/shard_map/ppermute | solution.py:182
  11.6 4.0 %collective-permute-start.4 = (bf16[4,1280]{1,0:T(4,128)(2,1)S(1)}, bf16[4,1280]{1,0:T(4,128)(2,1)S(1)}, u32[]{:S(2)}, u32[]{:S(2)}) collective-permute-start(bf16[4,1280]{1,0:T(4,128)(2,1)S(1)} %get-tuple-element.57), channel_id=1, source_target_pairs={{0,6},{1,7},{2,4},{3,5},{4,2},{5,3},{6,0},{7,1},{8,14},{9,15},{10,... | collective-permute-start | bytes 30728 | tf_op jit(solution)/shard_map/ppermute | solution.py:182
  11.6 4.0 %collective-permute-start.5 = (bf16[4,1280]{1,0:T(4,128)(2,1)S(1)}, bf16[4,1280]{1,0:T(4,128)(2,1)S(1)}, u32[]{:S(2)}, u32[]{:S(2)}) collective-permute-start(bf16[4,1280]{1,0:T(4,128)(2,1)S(1)} %get-tuple-element.58), channel_id=1, source_target_pairs={{0,5},{1,4},{2,7},{3,6},{4,1},{5,0},{6,3},{7,2},{8,13},{9,12},{10,... | collective-permute-start | bytes 30728 | tf_op jit(solution)/shard_map/ppermute | solution.py:182
  15.6 17.8 %slice-start.3 = ((s8[10485760]{0:T(1024)(128)(4,1)}), s8[4194304]{0:T(1024)(128)(4,1)S(1)}, s32[]{:S(2)}) async-start(s8[10485760]{0:T(1024)(128)(4,1)} %bitcast.3), calls=%async_computation.3 | async-start | bytes 8388608
  15.7 17.8 %slice-start.4 = ((s8[10485760]{0:T(1024)(128)(4,1)}), s8[4194304]{0:T(1024)(128)(4,1)S(1)}, s32[]{:S(2)}) async-start(s8[10485760]{0:T(1024)(128)(4,1)} %bitcast.3), calls=%async_computation.4 | async-start | bytes 8388608
  15.7 2.0 %collective-permute-start.6 = (bf16[16,1280]{1,0:T(8,128)(2,1)S(1)}, bf16[16,1280]{1,0:T(8,128)(2,1)S(1)}, u32[]{:S(2)}, u32[]{:S(2)}) collective-permute-start(bf16[16,1280]{1,0:T(8,128)(2,1)S(1)} %shard_map.122.first), channel_id=1, source_target_pairs={{0,4},{4,0},{8,12},{12,8},{1,5},{5,1},{9,13},{13,9},{2,6},{6,2},{1... | collective-permute-start | bytes 122888 | tf_op jit(solution)/shard_map/ppermute | solution.py:182
  16.2 4.0 %collective-permute-start.10 = (bf16[16,1280]{1,0:T(8,128)(2,1)S(1)}, bf16[16,1280]{1,0:T(8,128)(2,1)S(1)}, u32[]{:S(2)}, u32[]{:S(2)}) collective-permute-start(bf16[16,1280]{1,0:T(8,128)(2,1)S(1)} %shard_map.122.first), channel_id=1, source_target_pairs={{0,8},{4,12},{8,0},{12,4},{1,9},{5,13},{9,1},{13,5},{2,10},{6,14},... | collective-permute-start | bytes 122888 | tf_op jit(solution)/shard_map/ppermute | solution.py:182
  17.7 3.8 %collective-permute-start.9 = (bf16[16,1280]{1,0:T(8,128)(2,1)S(1)}, bf16[16,1280]{1,0:T(8,128)(2,1)S(1)}, u32[]{:S(2)}, u32[]{:S(2)}) collective-permute-start(bf16[16,1280]{1,0:T(8,128)(2,1)S(1)} %shard_map.122.first), channel_id=1, source_target_pairs={{0,12},{4,8},{8,4},{12,0},{1,13},{5,9},{9,5},{13,1},{2,14},{6,10},... | collective-permute-start | bytes 122888 | tf_op jit(solution)/shard_map/ppermute | solution.py:182
  17.7 15.8 %slice-start = ((s8[10485760]{0:T(1024)(128)(4,1)}), s8[4194304]{0:T(1024)(128)(4,1)S(1)}, s32[]{:S(2)}) async-start(s8[10485760]{0:T(1024)(128)(4,1)} %bitcast.1), calls=%async_computation | async-start | bytes 8388608
  18.5 11.0 %copy-start.6 = (bf16[1280]{0:T(1024)(128)(2,1)S(1)}, bf16[1280]{0:T(1024)(128)(2,1)}, u32[]{:S(2)}) copy-start(bf16[1280]{0:T(1024)(128)(2,1)} %param.20) | copy-start | bytes 7684
  21.5 12.0 %slice-start.1 = ((s8[10485760]{0:T(1024)(128)(4,1)}), s8[4194304]{0:T(1024)(128)(4,1)S(1)}, s32[]{:S(2)}) async-start(s8[10485760]{0:T(1024)(128)(4,1)} %bitcast.1), calls=%async_computation.1 | async-start | bytes 8388608
  22.2 5.5 %collective-permute-start.11 = (bf16[24,1280]{1,0:T(8,128)(2,1)S(1)}, bf16[24,1280]{1,0:T(8,128)(2,1)S(1)}, u32[]{:S(2)}, u32[]{:S(2)}) collective-permute-start(bf16[24,1280]{1,0:T(8,128)(2,1)S(1)} %get-tuple-element.67), channel_id=1, source_target_pairs={{0,1},{1,0},{2,3},{3,2},{4,5},{5,4},{6,7},{7,6},{8,9},{9,8},{10,11... | collective-permute-start | bytes 184328 | tf_op jit(solution)/shard_map/ppermute | solution.py:182
  22.3 6.3 %collective-permute-start.7 = (bf16[24,1280]{1,0:T(8,128)(2,1)S(1)}, bf16[24,1280]{1,0:T(8,128)(2,1)S(1)}, u32[]{:S(2)}, u32[]{:S(2)}) collective-permute-start(bf16[24,1280]{1,0:T(8,128)(2,1)S(1)} %get-tuple-element.61), channel_id=1, source_target_pairs={{0,2},{1,3},{2,0},{3,1},{4,6},{5,7},{6,4},{7,5},{8,10},{9,11},{10,... | collective-permute-start | bytes 184328 | tf_op jit(solution)/shard_map/ppermute | solution.py:182
  27.7 5.8 %slice-start.2 = ((s8[10485760]{0:T(1024)(128)(4,1)}), s8[2097152]{0:T(1024)(128)(4,1)S(1)}, s32[]{:S(2)}) async-start(s8[10485760]{0:T(1024)(128)(4,1)} %bitcast.1), calls=%async_computation.2 | async-start | bytes 4194304
  27.7 5.8 %slice-start.5 = ((s8[10485760]{0:T(1024)(128)(4,1)}), s8[2097152]{0:T(1024)(128)(4,1)S(1)}, s32[]{:S(2)}) async-start(s8[10485760]{0:T(1024)(128)(4,1)} %bitcast.3), calls=%async_computation.5 | async-start | bytes 4194304
  27.7 5.3 %collective-permute-start.12 = (bf16[24,1280]{1,0:T(8,128)(2,1)S(1)}, bf16[24,1280]{1,0:T(8,128)(2,1)S(1)}, u32[]{:S(2)}, u32[]{:S(2)}) collective-permute-start(bf16[24,1280]{1,0:T(8,128)(2,1)S(1)} %get-tuple-element.69), channel_id=1, source_target_pairs={{0,2},{1,3},{2,0},{3,1},{4,6},{5,7},{6,4},{7,5},{8,10},{9,11},{10,... | collective-permute-start | bytes 184328 | tf_op jit(solution)/shard_map/ppermute | solution.py:182
  28.5 4.9 %collective-permute-start.8 = (bf16[24,1280]{1,0:T(8,128)(2,1)S(1)}, bf16[24,1280]{1,0:T(8,128)(2,1)S(1)}, u32[]{:S(2)}, u32[]{:S(2)}) collective-permute-start(bf16[24,1280]{1,0:T(8,128)(2,1)S(1)} %get-tuple-element.63), channel_id=1, source_target_pairs={{0,1},{1,0},{2,3},{3,2},{4,5},{5,4},{6,7},{7,6},{8,9},{9,8},{10,11... | collective-permute-start | bytes 184328 | tf_op jit(solution)/shard_map/ppermute | solution.py:182
  34.9 1.9 %collective-permute-start.13 = (bf16[24,2688]{1,0:T(8,128)(2,1)S(1)}, bf16[24,2688]{1,0:T(8,128)(2,1)S(1)}, u32[]{:S(2)}, u32[]{:S(2)}) collective-permute-start(bf16[24,2688]{1,0:T(8,128)(2,1)S(1)} %get-tuple-element.71.earlier), channel_id=1, source_target_pairs={{0,4},{4,0},{8,12},{12,8},{1,5},{5,1},{9,13},{13,9},{2,6},{6,2},{1... | collective-permute-start | bytes 387080 | tf_op jit(solution)/shard_map/ppermute | solution.py:182
  36.2 1.5 %collective-permute-start.15 = (bf16[24,2560]{1,0:T(8,128)(2,1)S(1)}, bf16[24,2560]{1,0:T(8,128)(2,1)S(1)}, u32[]{:S(2)}, u32[]{:S(2)}) collective-permute-start(bf16[24,2560]{1,0:T(8,128)(2,1)S(1)} %get-tuple-element.76), channel_id=1, source_target_pairs={{0,4},{4,0},{8,12},{12,8},{1,5},{5,1},{9,13},{13,9},{2,6},{6,2},{1... | collective-permute-start | bytes 368648 | tf_op jit(solution)/shard_map/ppermute | solution.py:182
  37.0 6.2 %collective-permute-start.14 = (bf16[24,2688]{1,0:T(8,128)(2,1)S(1)}, bf16[24,2688]{1,0:T(8,128)(2,1)S(1)}, u32[]{:S(2)}, u32[]{:S(2)}) collective-permute-start(bf16[24,2688]{1,0:T(8,128)(2,1)S(1)} %get-tuple-element.73.earlier), channel_id=1, source_target_pairs={{0,12},{4,8},{8,4},{12,0},{1,13},{5,9},{9,5},{13,1},{2,14},{6,10},... | collective-permute-start | bytes 387080 | tf_op jit(solution)/shard_map/ppermute | solution.py:182
  37.7 7.4 %collective-permute-start.19 = (bf16[24,2560]{1,0:T(8,128)(2,1)S(1)}, bf16[24,2560]{1,0:T(8,128)(2,1)S(1)}, u32[]{:S(2)}, u32[]{:S(2)}) collective-permute-start(bf16[24,2560]{1,0:T(8,128)(2,1)S(1)} %get-tuple-element.77.earlier), channel_id=1, source_target_pairs={{0,12},{4,8},{8,4},{12,0},{1,13},{5,9},{9,5},{13,1},{2,14},{6,10},... | collective-permute-start | bytes 368648 | tf_op jit(solution)/shard_map/ppermute | solution.py:182
  39.9 6.0 %slice-start.6 = ((s8[10485760]{0:T(1024)(128)(4,1)}), s8[4194304]{0:T(1024)(128)(4,1)S(1)}, s32[]{:S(2)}) async-start(s8[10485760]{0:T(1024)(128)(4,1)} %bitcast.5), calls=%async_computation.6 | async-start | bytes 8388608
  39.9 6.0 %slice-start.7 = ((s8[10485760]{0:T(1024)(128)(4,1)}), s8[4194304]{0:T(1024)(128)(4,1)S(1)}, s32[]{:S(2)}) async-start(s8[10485760]{0:T(1024)(128)(4,1)} %bitcast.5), calls=%async_computation.7 | async-start | bytes 8388608
  39.9 6.0 %slice-start.8 = ((s8[10485760]{0:T(1024)(128)(4,1)}), s8[2097152]{0:T(1024)(128)(4,1)S(1)}, s32[]{:S(2)}) async-start(s8[10485760]{0:T(1024)(128)(4,1)} %bitcast.5), calls=%async_computation.8 | async-start | bytes 4194304
  39.9 1.4 %collective-permute-start.17 = (bf16[24,2048]{1,0:T(8,128)(2,1)S(1)}, bf16[24,2048]{1,0:T(8,128)(2,1)S(1)}, u32[]{:S(2)}, u32[]{:S(2)}) collective-permute-start(bf16[24,2048]{1,0:T(8,128)(2,1)S(1)} %get-tuple-element.78.earlier), channel_id=1, source_target_pairs={{0,4},{4,0},{8,12},{12,8},{1,5},{5,1},{9,13},{13,9},{2,6},{6,2},{1... | collective-permute-start | bytes 294920 | tf_op jit(solution)/shard_map/ppermute | solution.py:182
  40.5 1.6 %collective-permute-start.16 = (bf16[24,1024]{1,0:T(8,128)(2,1)S(1)}, bf16[24,1024]{1,0:T(8,128)(2,1)S(1)}, u32[]{:S(2)}, u32[]{:S(2)}) collective-permute-start(bf16[24,1024]{1,0:T(8,128)(2,1)S(1)} %get-tuple-element.80.earlier), channel_id=1, source_target_pairs={{0,4},{4,0},{8,12},{12,8},{1,5},{5,1},{9,13},{13,9},{2,6},{6,2},{1... | collective-permute-start | bytes 147464 | tf_op jit(solution)/shard_map/ppermute | solution.py:182
  41.3 6.2 %collective-permute-start.21 = (bf16[24,2048]{1,0:T(8,128)(2,1)S(1)}, bf16[24,2048]{1,0:T(8,128)(2,1)S(1)}, u32[]{:S(2)}, u32[]{:S(2)}) collective-permute-start(bf16[24,2048]{1,0:T(8,128)(2,1)S(1)} %get-tuple-element.82.earlier), channel_id=1, source_target_pairs={{0,12},{4,8},{8,4},{12,0},{1,13},{5,9},{9,5},{13,1},{2,14},{6,10},... | collective-permute-start | bytes 294920 | tf_op jit(solution)/shard_map/ppermute | solution.py:182
  42.1 6.2 %collective-permute-start.23 = (bf16[24,1024]{1,0:T(8,128)(2,1)S(1)}, bf16[24,1024]{1,0:T(8,128)(2,1)S(1)}, u32[]{:S(2)}, u32[]{:S(2)}) collective-permute-start(bf16[24,1024]{1,0:T(8,128)(2,1)S(1)} %get-tuple-element.83.earlier), channel_id=1, source_target_pairs={{0,12},{4,8},{8,4},{12,0},{1,13},{5,9},{9,5},{13,1},{2,14},{6,10},... | collective-permute-start | bytes 147464 | tf_op jit(solution)/shard_map/ppermute | solution.py:182
  43.4 2.5 %collective-permute-start.18 = (bf16[24,1280]{1,0:T(8,128)(2,1)S(1)}, bf16[24,1280]{1,0:T(8,128)(2,1)S(1)}, u32[]{:S(2)}, u32[]{:S(2)}) collective-permute-start(bf16[24,1280]{1,0:T(8,128)(2,1)S(1)} %get-tuple-element.84.mine.earlier), channel_id=1, source_target_pairs={{0,4},{4,0},{8,12},{12,8},{1,5},{5,1},{9,13},{13,9},{2,6},{6,2},{1... | collective-permute-start | bytes 184328 | tf_op jit(solution)/shard_map/ppermute | solution.py:182
  45.3 1.5 %collective-permute-start.20 = (bf16[24,1280]{1,0:T(8,128)(2,1)S(1)}, bf16[24,1280]{1,0:T(8,128)(2,1)S(1)}, u32[]{:S(2)}, u32[]{:S(2)}) collective-permute-start(bf16[24,1280]{1,0:T(8,128)(2,1)S(1)} %shard_map.137.mine), channel_id=1, source_target_pairs={{0,4},{4,0},{8,12},{12,8},{1,5},{5,1},{9,13},{13,9},{2,6},{6,2},{1... | collective-permute-start | bytes 184328 | tf_op jit(solution)/shard_map/ppermute | solution.py:182
  47.6 1.3 %collective-permute-start.22 = (bf16[24,1024]{1,0:T(8,128)(2,1)S(1)}, bf16[24,1024]{1,0:T(8,128)(2,1)S(1)}, u32[]{:S(2)}, u32[]{:S(2)}) collective-permute-start(bf16[24,1024]{1,0:T(8,128)(2,1)S(1)} %shard_map.139.mine), channel_id=1, source_target_pairs={{0,4},{4,0},{8,12},{12,8},{1,5},{5,1},{9,13},{13,9},{2,6},{6,2},{1... | collective-permute-start | bytes 147464 | tf_op jit(solution)/shard_map/ppermute | solution.py:182
  48.4 1.3 %collective-permute-start.24 = (bf16[24,512]{1,0:T(8,128)(2,1)S(1)}, bf16[24,512]{1,0:T(8,128)(2,1)S(1)}, u32[]{:S(2)}, u32[]{:S(2)}) collective-permute-start(bf16[24,512]{1,0:T(8,128)(2,1)S(1)} %shard_map.141.mine), channel_id=1, source_target_pairs={{0,4},{4,0},{8,12},{12,8},{1,5},{5,1},{9,13},{13,9},{2,6},{6,2},{1... | collective-permute-start | bytes 73736 | tf_op jit(solution)/shard_map/ppermute | solution.py:182
  50.1 5.8 %collective-permute-start.25 = (bf16[24,640]{1,0:T(8,128)(2,1)S(1)}, bf16[24,640]{1,0:T(8,128)(2,1)S(1)}, u32[]{:S(2)}, u32[]{:S(2)}) collective-permute-start(bf16[24,640]{1,0:T(8,128)(2,1)S(1)} %get-tuple-element.91), channel_id=1, source_target_pairs={{0,3},{1,2},{2,1},{3,0},{4,7},{5,6},{6,5},{7,4},{8,11},{9,10},{10,... | collective-permute-start | bytes 92168 | tf_op jit(solution)/shard_map/ppermute | solution.py:182
  53.3 4.8 %collective-permute-start.26 = (bf16[24,640]{1,0:T(8,128)(2,1)S(1)}, bf16[24,640]{1,0:T(8,128)(2,1)S(1)}, u32[]{:S(2)}, u32[]{:S(2)}) collective-permute-start(bf16[24,640]{1,0:T(8,128)(2,1)S(1)} %get-tuple-element.92), channel_id=1, source_target_pairs={{0,2},{1,3},{2,0},{3,1},{4,6},{5,7},{6,4},{7,5},{8,10},{9,11},{10,... | collective-permute-start | bytes 92168 | tf_op jit(solution)/shard_map/ppermute | solution.py:182
  53.3 4.8 %collective-permute-start.27 = (bf16[24,640]{1,0:T(8,128)(2,1)S(1)}, bf16[24,640]{1,0:T(8,128)(2,1)S(1)}, u32[]{:S(2)}, u32[]{:S(2)}) collective-permute-start(bf16[24,640]{1,0:T(8,128)(2,1)S(1)} %get-tuple-element.93), channel_id=1, source_target_pairs={{0,1},{1,0},{2,3},{3,2},{4,5},{5,4},{6,7},{7,6},{8,9},{9,8},{10,11... | collective-permute-start | bytes 92168 | tf_op jit(solution)/shard_map/ppermute | solution.py:182
